TPU v7x, 32 devices: a whole 2x2x4 slice. The times are simulated.
32 devices in a mesh: occi: 4 (over z), occj: 8 (over y, x, core).
Axes of the slice: x: 2, y: 2, z: 4, core: 2. Of those that a mesh axis runs over, the one named last changes fastest.
Arguments:
- amplitudes: float32 [8, 8, 512, 512], P('occi', 'occj'), may hold values from -6 to 6
- vectors: bfloat16 [3, 512, 512], P(None, 'occj'), may hold values from -0.25 to 0.25
- occupied_fock_block: bfloat16 [8, 8], replicated, may hold values from -2 to 2
- occ_energy: float32 [8], replicated, may hold values from -3 to -0.3
- vir_energy: float32 [512], replicated, may hold values from 0.2 to 4
Outputs:
- updated: float32 [8, 8, 512, 512], P('occi', 'occj')
All inputs are finite; a program needn't handle non-finite values.
Results may differ from a plain program's by a relative error of at most 0.0028.
Values may be sent and summed in bfloat16 or wider, within the bound.
No kernel may reach another device: no remote copies, remote signals or barrier semaphores. Data moves between devices by JAX's collectives and lax.ppermute only.
A program may use at most 64 MiB of HBM per device.

v0:
```python
import jax
import jax.numpy as jnp
from jax import lax
from jax.sharding import PartitionSpec as P

ITERS = 2


def ladder_term(reduced_precision_copy, gathered):
    running = jnp.zeros(reduced_precision_copy.shape, jnp.float32)
    for vector_id in range(gathered.shape[0]):
        single = gathered[vector_id]
        inner = jnp.einsum(
            "pjcd,bd->pjcb", reduced_precision_copy, single, preferred_element_type=jnp.float32
        ).astype(jnp.bfloat16)
        running = running + jnp.einsum(
            "ac,pjcb->pjab", single, inner, preferred_element_type=jnp.float32
        )
    return running.astype(jnp.bfloat16)


def occupied_fock_blend(slab_partitioned, occupied_fock_block):
    flattened_row_list = slab_partitioned.reshape(slab_partitioned.shape[0], -1)
    contracted_result = lax.dot_general(
        occupied_fock_block,
        flattened_row_list,
        (((0,), (0,)), ((), ())),
        preferred_element_type=jnp.float32,
    )
    return -contracted_result.reshape(slab_partitioned.shape)


def to_mirror(half_slab):
    moved = lax.all_to_all(
        lax.all_to_all(half_slab, "occj", split_axis=0, concat_axis=1, tiled=True),
        "occi",
        split_axis=1,
        concat_axis=2,
        tiled=True,
    )
    return jnp.transpose(moved, (1, 0, 3, 2))


def local(amplitudes, vectors, occupied_fock_block, occ_energy, vir_energy):
    gathered = lax.all_gather(vectors, "occj", axis=1, tiled=True)
    rows_first = amplitudes.shape[0]
    rows_second = amplitudes.shape[1]
    occ_first = lax.dynamic_slice_in_dim(
        occ_energy, lax.axis_index("occi") * rows_first, rows_first
    )
    occ_second = lax.dynamic_slice_in_dim(
        occ_energy, lax.axis_index("occj") * rows_second, rows_second
    )
    denominator = (
        occ_first[:, None, None, None]
        + occ_second[None, :, None, None]
        - vir_energy[None, None, :, None]
        - vir_energy[None, None, None, :]
    )
    current = amplitudes
    for iteration in range(ITERS):
        reduced_precision_copy = current.astype(jnp.bfloat16)
        slab_partitioned = lax.all_to_all(
            reduced_precision_copy, "occi", split_axis=2, concat_axis=0, tiled=True
        )
        ladder = ladder_term(reduced_precision_copy, gathered)
        blended_amplitude = occupied_fock_blend(slab_partitioned, occupied_fock_block)
        ladder_slab = lax.all_to_all(ladder, "occi", split_axis=2, concat_axis=0, tiled=True)
        half_slab = (ladder_slab.astype(jnp.float32) + blended_amplitude).astype(jnp.bfloat16)
        halfway = lax.all_to_all(half_slab, "occi", split_axis=0, concat_axis=2, tiled=True)
        mirrored = to_mirror(half_slab)
        residual = halfway.astype(jnp.float32) + mirrored.astype(jnp.float32)
        current = current + residual / denominator
    return current


def solution(mesh):
    return jax.shard_map(
        local,
        mesh=mesh,
        in_specs=(P("occi", "occj", None, None), P(None, "occj", None), P(), P(), P()),
        out_specs=P("occi", "occj", None, None),
        check_vma=False,
    )
```

profile of v0, /device:TPU:0, one launch (start us, length us, event | category | flops | bytes accessed | tf_op | source)
XLA Modules:
  0.0 334.8 jit_solution(4919480147053598620)
XLA Ops:
  6.5 0.0 copy-start
  6.5 0.0 all-gather.2.cloned.1.call-start
  6.5 0.7 all-gather.2.cloned.1.call-update
  7.3 1.7 bitcast_convert_fusion
  9.0 2.1 copy.124
  11.0 6.3 %all-to-all-start.1 = ((bf16[2,1,512,512]{3,0,1,2:T(2,128)(2,1)}), bf16[2,1,512,512]{3,0,1,2:T(2,128)(2,1)S(1)}, u32[]{:S(2)}, u32[]{:S(2)}) async-start(bf16[2,1,512,512]{3,0,1,2:T(2,128)(2,1)} %copy.124), calls=%async_computation.1 | async-start | bytes 2097152 | tf_op jit(solution)/shard_map/all_to_all | solution.py:63
  17.4 20.3 %all-gather.2.cloned.1.call-done = bf16[3,512,512]{2,1,0:T(8,128)(2,1)} async-done(((bf16[3,64,512]{2,1,0:T(8,128)(2,1)}), bf16[3,512,512]{2,1,0:T(8,128)(2,1)}) %all-gather.2.cloned.1.call-update) | async-done | bytes 1572880 | tf_op jit(solution)/shard_map/all_gather | solution.py:45
  37.7 3.8 %fusion.4 = f32[2,512,512]{2,1,0:T(8,128)} fusion(bf16[2,1,512,512]{3,2,0,1:T(8,128)(2,1)S(1)} %bitcast_convert_fusion, bf16[3,512,512]{2,1,0:T(8,128)(2,1)} %all-gather.2.cloned.1.call-done), kind=kOutput, calls=%fused_computation.24 | convolution fusion | flops 1074266112 | bytes 4194304 | tf_op jit(solution)/shard_map/ac,pjcb->pjab/dot_general | solution.py:16
  41.5 3.8 %fusion.5 = f32[2,512,512]{2,1,0:T(8,128)} fusion(bf16[2,1,512,512]{3,2,0,1:T(8,128)(2,1)S(1)} %bitcast_convert_fusion, bf16[3,512,512]{2,1,0:T(8,128)(2,1)} %all-gather.2.cloned.1.call-done), kind=kOutput, calls=%fused_computation.25 | convolution fusion | flops 1074266112 | bytes 4194304 | tf_op jit(solution)/shard_map/ac,pjcb->pjab/dot_general | solution.py:16
  45.3 3.8 %fusion.8 = bf16[2,1,512,512]{2,3,0,1:T(8,128)(2,1)S(1)} fusion(f32[2,512,512]{2,1,0:T(8,128)} %fusion.4, f32[2,512,512]{2,1,0:T(8,128)} %fusion.5, bf16[2,1,512,512]{3,2,0,1:T(8,128)(2,1)S(1)} %bitcast_convert_fusion, bf16[3,512,512]{2,1,0:T(8,128)(2,1)} %all-gather.2.cloned.1.call-done), kind=kOutput, calls=%fused_computation.28 | convolution fusion | flops 1075838976 | bytes 7340032 | tf_op jit(solution)/shard_map/ac,pjcb->pjab/dot_general | solution.py:16
  49.2 2.1 copy.122
  51.3 0.0 all-to-all-done.1
  51.3 4.6 %all-to-all-start = ((bf16[2,1,512,512]{3,0,1,2:T(2,128)(2,1)}), bf16[2,1,512,512]{3,0,1,2:T(2,128)(2,1)S(1)}, u32[]{:S(2)}, u32[]{:S(2)}) async-start(bf16[2,1,512,512]{3,0,1,2:T(2,128)(2,1)} %copy.122), calls=%async_computation | async-start | bytes 2097152 | tf_op jit(solution)/shard_map/all_to_all | solution.py:68
  55.9 0.2 copy.125
  56.0 0.1 copy.126
  56.1 25.9 %all-to-all-done = bf16[2,1,512,512]{3,0,1,2:T(2,128)(2,1)S(1)} async-done(((bf16[2,1,512,512]{3,0,1,2:T(2,128)(2,1)}), bf16[2,1,512,512]{3,0,1,2:T(2,128)(2,1)S(1)}, u32[]{:S(2)}, u32[]{:S(2)}) %all-to-all-start) | async-done | bytes 1048608 | tf_op jit(solution)/shard_map/all_to_all | solution.py:68
  82.0 2.5 copy_bitcast_fusion
  84.5 2.7 reshape.198
  87.2 0.0 copy-done
  87.2 0.8 fusion.9
  88.0 0.3 copy.128
  88.3 18.5 %all_to_all.108 = bf16[8,1,128,512]{3,2,1,0:T(8,128)(2,1)} all-to-all(bf16[8,1,128,512]{3,2,1,0:T(8,128)(2,1)S(1)} %copy.128), channel_id=1, replica_groups=mesh['occi'=4,'occj'=8] {'occj'}, dimensions={0} | all-to-all | bytes 2097152 | tf_op jit(solution)/shard_map/all_to_all | solution.py:35
  106.8 27.9 %all_to_all.109 = bf16[8,1,128,512]{3,2,1,0:T(8,128)(2,1)S(1)} all-to-all(bf16[8,1,128,512]{3,2,1,0:T(8,128)(2,1)S(1)} %copy.128), channel_id=1, replica_groups=mesh['occi'=4,'occj'=8] {'occi'}, dimensions={0} | all-to-all | bytes 2097152 | tf_op jit(solution)/shard_map/all_to_all | solution.py:70
  134.7 3.7 %all-to-all-start.4 = ((bf16[1,8,128,512]{3,2,0,1:T(8,128)(2,1)}), bf16[1,8,128,512]{3,2,0,1:T(8,128)(2,1)S(1)}, u32[]{:S(2)}, u32[]{:S(2)}) async-start(bf16[1,8,128,512]{3,2,0,1:T(8,128)(2,1)} %bitcast.24), calls=%async_computation.4 | async-start | bytes 2097152 | tf_op jit(solution)/shard_map/all_to_all | solution.py:34
  138.4 0.0 copy-done.4
  138.4 0.6 dynamic_slice.7
  139.0 0.7 dynamic-slice_add_fusion
  139.7 0.0 copy-done.3
  139.7 0.1 broadcast_subtract_fusion
  139.8 0.3 convert_bitcast_fusion.2
  140.1 1.6 copy.130
  141.7 21.3 %all-to-all-done.4 = bf16[1,8,128,512]{3,2,0,1:T(8,128)(2,1)S(1)} async-done(((bf16[1,8,128,512]{3,2,0,1:T(8,128)(2,1)}), bf16[1,8,128,512]{3,2,0,1:T(8,128)(2,1)S(1)}, u32[]{:S(2)}, u32[]{:S(2)}) %all-to-all-start.4) | async-done | bytes 1048608 | tf_op jit(solution)/shard_map/all_to_all | solution.py:34
  163.0 1.6 copy.133
  164.6 3.2 reshape.202
  167.8 0.0 copy-done.1
  167.8 4.1 %fusion.27 = (bf16[2,1,512,512]{3,2,0,1:T(8,128)(2,1)S(1)}, f32[2,1,512,512]{3,2,0,1:T(8,128)}) fusion(f32[512]{0:T(512)S(1)} %copy-done.3, f32[2,512]{1,0:T(2,128)S(1)} %broadcast_subtract_fusion, f32[1,2,512,512]{2,3,1,0:T(8,128)} %reshape.202, f32[2,1,4,128,512]{4,3,2,0,1:T(8,128)} %copy.130, f32[2,1,512,512]{3,2,1,0:T(8,128)S(1)} %copy-done.1), kind=kLoop, calls=%fused_computation.44 | loop fusion | flops 2621440 | bytes 9443328 | tf_op jit(solution)/shard_map/convert_element_type | solution.py:62
  171.9 3.9 %fusion.6 = f32[2,512,512]{2,1,0:T(8,128)} fusion(bf16[2,1,512,512]{3,2,0,1:T(8,128)(2,1)S(1)} %get-tuple-element.5, bf16[3,512,512]{2,1,0:T(8,128)(2,1)} %all-gather.2.cloned.1.call-done), kind=kOutput, calls=%fused_computation.26 | convolution fusion | flops 1074266112 | bytes 4194304 | tf_op jit(solution)/shard_map/ac,pjcb->pjab/dot_general | solution.py:16
  175.9 0.0 copy-done.5
  175.9 2.6 fusion.7
  178.4 3.8 %fusion.10 = bf16[2,1,512,512]{2,3,0,1:T(8,128)(2,1)S(1)} fusion(f32[2,512,512]{2,1,0:T(8,128)} %fusion.6, f32[2,512,512]{2,1,0:T(8,128)} %fusion.7, bf16[2,1,512,512]{3,2,0,1:T(8,128)(2,1)S(1)} %get-tuple-element.5, bf16[3,512,512]{2,1,0:T(8,128)(2,1)} %all-gather.2.cloned.1.call-done), kind=kOutput, calls=%fused_computation.30 | convolution fusion | flops 1075838976 | bytes 7340032 | tf_op jit(solution)/shard_map/ac,pjcb->pjab/dot_general | solution.py:16
  182.3 2.1 copy.138
  184.4 3.5 %all-to-all-start.5 = ((bf16[2,1,512,512]{3,0,1,2:T(2,128)(2,1)}), bf16[2,1,512,512]{3,0,1,2:T(2,128)(2,1)S(1)}, u32[]{:S(2)}, u32[]{:S(2)}) async-start(bf16[2,1,512,512]{3,0,1,2:T(2,128)(2,1)} %copy.138), calls=%async_computation.5 | async-start | bytes 2097152 | tf_op jit(solution)/shard_map/all_to_all | solution.py:68
  187.9 2.1 copy.141
  190.0 23.1 %all-to-all-done.5 = bf16[2,1,512,512]{3,0,1,2:T(2,128)(2,1)S(1)} async-done(((bf16[2,1,512,512]{3,0,1,2:T(2,128)(2,1)}), bf16[2,1,512,512]{3,0,1,2:T(2,128)(2,1)S(1)}, u32[]{:S(2)}, u32[]{:S(2)}) %all-to-all-start.5) | async-done | bytes 1048608 | tf_op jit(solution)/shard_map/all_to_all | solution.py:68
  213.1 3.5 %all-to-all-start.6 = ((bf16[2,1,512,512]{3,0,1,2:T(2,128)(2,1)}), bf16[2,1,512,512]{3,0,1,2:T(2,128)(2,1)S(1)}, u32[]{:S(2)}, u32[]{:S(2)}) async-start(bf16[2,1,512,512]{3,0,1,2:T(2,128)(2,1)} %copy.141), calls=%async_computation.6 | async-start | bytes 2097152 | tf_op jit(solution)/shard_map/all_to_all | solution.py:63
  216.6 0.2 copy.139
  216.8 0.3 convert_bitcast_fusion.1
  217.1 0.2 copy.140
  217.2 24.5 %all-to-all-done.6 = bf16[2,1,512,512]{3,0,1,2:T(2,128)(2,1)S(1)} async-done(((bf16[2,1,512,512]{3,0,1,2:T(2,128)(2,1)}), bf16[2,1,512,512]{3,0,1,2:T(2,128)(2,1)S(1)}, u32[]{:S(2)}, u32[]{:S(2)}) %all-to-all-start.6) | async-done | bytes 1048608 | tf_op jit(solution)/shard_map/all_to_all | solution.py:63
  241.8 0.2 copy.142
  242.0 0.1 copy.143
  242.0 0.6 copy.161
  242.6 0.5 convolution_negate_fusion
  243.1 1.5 fusion.11
  244.6 18.5 %all_to_all.110 = bf16[8,1,128,512]{3,2,1,0:T(8,128)(2,1)} all-to-all(bf16[8,1,128,512]{3,2,1,0:T(8,128)(2,1)S(1)} %fusion.11), channel_id=1, replica_groups=mesh['occi'=4,'occj'=8] {'occj'}, dimensions={0} | all-to-all | bytes 2097152 | tf_op jit(solution)/shard_map/all_to_all | solution.py:35
  263.0 27.8 %all_to_all.111 = bf16[8,1,128,512]{3,2,1,0:T(8,128)(2,1)S(1)} all-to-all(bf16[8,1,128,512]{3,2,1,0:T(8,128)(2,1)S(1)} %fusion.11), channel_id=1, replica_groups=mesh['occi'=4,'occj'=8] {'occi'}, dimensions={0} | all-to-all | bytes 2097152 | tf_op jit(solution)/shard_map/all_to_all | solution.py:70
  290.8 3.5 %all-to-all-start.9 = ((bf16[1,8,128,512]{3,2,0,1:T(8,128)(2,1)}), bf16[1,8,128,512]{3,2,0,1:T(8,128)(2,1)S(1)}, u32[]{:S(2)}, u32[]{:S(2)}) async-start(bf16[1,8,128,512]{3,2,0,1:T(8,128)(2,1)} %bitcast.46), calls=%async_computation.9 | async-start | bytes 2097152 | tf_op jit(solution)/shard_map/all_to_all | solution.py:34
  294.3 0.3 convert_bitcast_fusion
  294.6 1.6 copy.147
  296.2 22.9 %all-to-all-done.9 = bf16[1,8,128,512]{3,2,0,1:T(8,128)(2,1)S(1)} async-done(((bf16[1,8,128,512]{3,2,0,1:T(8,128)(2,1)}), bf16[1,8,128,512]{3,2,0,1:T(8,128)(2,1)S(1)}, u32[]{:S(2)}, u32[]{:S(2)}) %all-to-all-start.9) | async-done | bytes 1048608 | tf_op jit(solution)/shard_map/all_to_all | solution.py:34
  319.1 1.7 copy.150
  320.8 3.2 reshape.203
  324.0 0.0 copy-done.2
  324.0 4.0 %fusion.2 = f32[2,1,512,512]{3,2,1,0:T(8,128)} fusion(f32[2,1,512,512]{3,2,0,1:T(8,128)S(1)} %copy-done.2, f32[1,2,512,512]{2,3,1,0:T(8,128)} %reshape.203, f32[2,1,4,128,512]{4,3,2,0,1:T(8,128)} %copy.147, f32[512]{0:T(512)S(1)} %copy-done.3, f32[2,512]{1,0:T(2,128)S(1)} %broadcast_subtract_fusion), kind=kLoop, calls=%fused_computation.5 | loop fusion | flops 2097152 | bytes 8394752 | tf_op jit(solution)/shard_map/add | solution.py:73
  (5 shorter events, 0.0 us)
Async XLA Ops:
  6.5 80.7 %copy-start = (bf16[8,8]{1,0:T(8,128)(2,1)S(1)}, bf16[8,8]{1,0:T(8,128)(2,1)}, u32[]{:S(2)}) copy-start(bf16[8,8]{1,0:T(8,128)(2,1)} %param.7) | copy-start | bytes 388
  6.5 31.2 %all-gather.2.cloned.1.call-start = ((), (), s32[]{:S(2)}) async-start(), calls=%async_computation.10 | async-start | bytes 1769472 | tf_op jit(solution)/shard_map/all_gather | solution.py:45
  11.0 40.2 %all-to-all-start.1 = ((bf16[2,1,512,512]{3,0,1,2:T(2,128)(2,1)}), bf16[2,1,512,512]{3,0,1,2:T(2,128)(2,1)S(1)}, u32[]{:S(2)}, u32[]{:S(2)}) async-start(bf16[2,1,512,512]{3,0,1,2:T(2,128)(2,1)} %copy.124), calls=%async_computation.1 | async-start | bytes 2097152 | tf_op jit(solution)/shard_map/all_to_all | solution.py:63
  51.3 30.8 %all-to-all-start = ((bf16[2,1,512,512]{3,0,1,2:T(2,128)(2,1)}), bf16[2,1,512,512]{3,0,1,2:T(2,128)(2,1)S(1)}, u32[]{:S(2)}, u32[]{:S(2)}) async-start(bf16[2,1,512,512]{3,0,1,2:T(2,128)(2,1)} %copy.122), calls=%async_computation | async-start | bytes 2097152 | tf_op jit(solution)/shard_map/all_to_all | solution.py:68
  106.8 31.6 %copy-start.4 = (f32[8]{0:T(128)S(1)}, f32[8]{0:T(128)}, u32[]{:S(2)}) copy-start(f32[8]{0:T(128)} %param.8) | copy-start | bytes 100
  106.8 32.9 %copy-start.3 = (f32[512]{0:T(512)S(1)}, f32[512]{0:T(512)}, u32[]{:S(2)}) copy-start(f32[512]{0:T(512)} %param.9) | copy-start | bytes 6148
  134.7 28.3 %all-to-all-start.4 = ((bf16[1,8,128,512]{3,2,0,1:T(8,128)(2,1)}), bf16[1,8,128,512]{3,2,0,1:T(8,128)(2,1)S(1)}, u32[]{:S(2)}, u32[]{:S(2)}) async-start(bf16[1,8,128,512]{3,2,0,1:T(8,128)(2,1)} %bitcast.24), calls=%async_computation.4 | async-start | bytes 2097152 | tf_op jit(solution)/shard_map/all_to_all | solution.py:34
  164.6 3.2 copy-start.1
  171.9 3.9 %copy-start.5 = (bf16[3,512,512]{2,1,0:T(8,128)(2,1)S(1)}, bf16[3,512,512]{2,1,0:T(8,128)(2,1)}, u32[]{:S(2)}) copy-start(bf16[3,512,512]{2,1,0:T(8,128)(2,1)} %all-gather.2.cloned.1.call-done) | copy-start | bytes 4718596
  184.4 28.7 %all-to-all-start.5 = ((bf16[2,1,512,512]{3,0,1,2:T(2,128)(2,1)}), bf16[2,1,512,512]{3,0,1,2:T(2,128)(2,1)S(1)}, u32[]{:S(2)}, u32[]{:S(2)}) async-start(bf16[2,1,512,512]{3,0,1,2:T(2,128)(2,1)} %copy.138), calls=%async_computation.5 | async-start | bytes 2097152 | tf_op jit(solution)/shard_map/all_to_all | solution.py:68
  213.1 28.7 %all-to-all-start.6 = ((bf16[2,1,512,512]{3,0,1,2:T(2,128)(2,1)}), bf16[2,1,512,512]{3,0,1,2:T(2,128)(2,1)S(1)}, u32[]{:S(2)}, u32[]{:S(2)}) async-start(bf16[2,1,512,512]{3,0,1,2:T(2,128)(2,1)} %copy.141), calls=%async_computation.6 | async-start | bytes 2097152 | tf_op jit(solution)/shard_map/all_to_all | solution.py:63
  290.8 28.3 %all-to-all-start.9 = ((bf16[1,8,128,512]{3,2,0,1:T(8,128)(2,1)}), bf16[1,8,128,512]{3,2,0,1:T(8,128)(2,1)S(1)}, u32[]{:S(2)}, u32[]{:S(2)}) async-start(bf16[1,8,128,512]{3,2,0,1:T(8,128)(2,1)} %bitcast.46), calls=%async_computation.9 | async-start | bytes 2097152 | tf_op jit(solution)/shard_map/all_to_all | solution.py:34
  320.8 3.2 copy-start.2
Sparse Core Ops, SparseCore 0:
  9.3 28.3 all-gather.1
where the time goes:
time: 336 us; the launch traced here: 335 us
  waiting for transfers between devices  139 us (41%)
  blocking collectives  92.6 us (28%)
  local copies, waits for them, and re-layouts  26.1 us (8%)
  starting transfers between devices  25.2 us (8%)
  matrix products  23.1 us (7%)
  other arithmetic  15.4 us (5%)
  between operations  13.6 us (4%)
    all_to_all x2, blocking collectives, local(): lax.all_to_all(half_slab, 'occi', split_axis=0, concat_axis=2, tiled=True)  55.7 us
    all_to_all x2, waiting for transfers between devices, local(): lax.all_to_all(ladder, 'occi', split_axis=2, concat_axis=0, tiled=True)  49 us
    all_to_all x2, waiting for transfers between devices, to_mirror(): lax.all_to_all(lax.all_to_all(half_slab, 'occj', split_axis=0, concat_axi...  44.2 us
    all_to_all x2, blocking collectives, to_mirror(): lax.all_to_all(half_slab, 'occj', split_axis=0, concat_axis=1, tiled=True)  36.9 us
    all_to_all x2, waiting for transfers between devices, local(): lax.all_to_all(reduced_precision_copy, 'occi', split_axis=2, concat_axis=...  24.5 us
    dot_general x6, matrix products, ladder_term(): jnp.einsum('ac,pjcb->pjab', single, inner, preferred_element_type=jnp.flo...  21.8 us
    all_gather x1, waiting for transfers between devices, local(): gathered = lax.all_gather(vectors, 'occj', axis=1, tiled=True)  20.3 us
    convert_element_type x6, local copies, waits for them, and re-layouts, local(): residual = halfway.astype(jnp.float32) + mirrored.astype(jnp.float32)  12.9 us
  transfers between devices with their start and end apart: 7, of which 6 were waited for; matrix products, arithmetic and copies ran while one was open for 8% of the time, Pallas kernels for 0%

commit v1 on v0

v1 whole, which is shorter than its diff:
```python
import functools
import math

import jax
import jax.numpy as jnp
from jax import lax
from jax.experimental import pallas as pl
from jax.experimental.pallas import tpu as pltpu
from jax.sharding import PartitionSpec as P

VMEM = pl.BlockSpec(memory_space=pltpu.VMEM)
SMEM = pl.BlockSpec(memory_space=pltpu.SMEM)
PARAMS = pltpu.CompilerParams(vmem_limit_bytes=50 * 2**20)
WIDE = jnp.float32
NARROW = jnp.bfloat16


class Tiles:
    def __init__(self, devices, virtual):
        n = math.isqrt(2 * devices)
        assert n * n == 2 * devices and n % 2 == 0 and virtual % n == 0
        self.n = n
        self.edge = virtual // n
        self.rows = self.edge // 2
        self.above = [(a, b) for a in range(n) for b in range(a + 1, n)]
        self.diagonal = [(len(self.above) + k // 2, k % 2, k) for k in range(n)]

    def span(self, k):
        return slice(k * self.edge, (k + 1) * self.edge)

    def mirror_within(self, x):
        e, g = self.edge, self.rows
        parts = []
        for c in range(2):
            tile = jnp.concatenate([x[c * g:(c + 1) * g, :e], x[c * g:(c + 1) * g, e:]], axis=0).T
            parts.append(jnp.concatenate([tile[:g], tile[g:]], axis=1))
        return jnp.concatenate(parts, axis=0)

    def mirror_across(self, x):
        return jnp.concatenate([x[:, self.edge:], x[:, :self.edge]], axis=1)


def call(body, outs, scratch, flops, moved, *operands, specs, aliases=None):
    return pl.pallas_call(
        body,
        out_shape=outs,
        in_specs=specs,
        out_specs=jax.tree.map(lambda _: VMEM, outs),
        scratch_shapes=scratch,
        compiler_params=PARAMS,
        input_output_aliases=aliases or {},
        cost_estimate=pl.CostEstimate(flops=flops, bytes_accessed=moved, transcendentals=0),
    )(*operands)


def pack_pair(tiles, source, out, pair, mirrored=False):
    e, g = tiles.edge, tiles.rows
    straight, turned = (slice(e, None), slice(0, e)) if mirrored else (slice(0, e), slice(e, None))
    for d, (a, b) in enumerate(tiles.above):
        out[d, pair, :, straight] = source[tiles.span(a), tiles.span(b)].astype(NARROW)
        out[d, pair, :, turned] = source[tiles.span(b), tiles.span(a)].astype(WIDE).T.astype(NARROW)
    for d, c, k in tiles.diagonal:
        tile = source[tiles.span(k), tiles.span(k)]
        tile = tile.astype(WIDE).T.astype(NARROW) if mirrored else tile.astype(NARROW)
        out[d, pair, c * g:(c + 1) * g, :e] = tile[:g]
        out[d, pair, c * g:(c + 1) * g, e:] = tile[g:]


def unpack_pair(tiles, blocks, pair, put):
    e, g = tiles.edge, tiles.rows
    for d, (a, b) in enumerate(tiles.above):
        put(a, b, blocks[d, pair, :, :e].astype(WIDE))
        put(b, a, blocks[d, pair, :, e:].astype(WIDE).T)
    for d, c, k in tiles.diagonal:
        upper = blocks[d, pair, c * g:(c + 1) * g, :e]
        lower = blocks[d, pair, c * g:(c + 1) * g, e:]
        put(k, k, jnp.concatenate([upper, lower], axis=0).astype(WIDE))


def pack_kernel(tiles, source, out):
    for pair in range(source.shape[0]):
        pack_pair(tiles, source.at[pair], out, pair, mirrored=True)


def pack(tiles, devices, amplitudes):
    count = amplitudes.shape[0]
    out = jax.ShapeDtypeStruct((devices, count, tiles.edge, 2 * tiles.edge), NARROW)
    return call(functools.partial(pack_kernel, tiles), out, [], amplitudes.size, amplitudes.size * 6,
                amplitudes, specs=[VMEM])


def assemble(place, order, pieces, whole):
    k = 0
    for piece in pieces:
        rows = piece.shape[2]
        for block in range(piece.shape[0]):
            start = pl.multiple_of((place[1] ^ order[k]) * rows, rows)
            for single in range(piece.shape[1]):
                whole[single, pl.ds(start, rows), :] = piece[block, single]
            k += 1


def ladder_pair(matrix, whole, total):
    def one(single, carry):
        vector = whole[single]
        inner = lax.dot_general(matrix, vector, (((1,), (1,)), ((), ())), preferred_element_type=WIDE)
        term = jnp.dot(vector, inner.astype(NARROW), preferred_element_type=WIDE)
        total[...] += term
        return carry

    total[...] = jnp.zeros_like(total)
    lax.fori_loop(0, whole.shape[0], one, 0)


def first_ladder_kernel(tiles, order, place, source, low, high, out, whole, total):
    assemble(place, order, (low, high), whole)
    for pair in range(source.shape[0]):
        ladder_pair(source[pair].astype(NARROW), whole, total)
        pack_pair(tiles, total, out, pair)


def second_ladder_kernel(tiles, order, count, place, occ, source, blocks, row, column, low, high, out,
                         whole, total, matrix):
    assemble(place, order, (low, high), whole)
    for pair in range(count):
        def put(a, b, tile):
            matrix[tiles.span(a), tiles.span(b)] = tile.astype(NARROW)

        unpack_pair(tiles, blocks, pair, put)
        ladder_pair(matrix[...], whole, total)
        base = occ[place[0] * count + pair] + occ[place[1]]

        def finish(step, carry):
            at = pl.ds(pl.multiple_of(step * 16, 16), 16)
            own = base - row[at, :1] - column[...]
            out[pair, at, :] = (
                source[pair, at, :] + 2.0 * matrix[at, :].astype(WIDE) + (2.0 * total[at, :]) / own
            )
            return carry

        lax.fori_loop(0, total.shape[0] // 16, finish, 0)


def add_kernel(tiles, source, blocks, out):
    for pair in range(source.shape[0]):
        def put(a, b, tile):
            here = (pair, tiles.span(a), tiles.span(b))
            out[here] = source[here] + tile

        unpack_pair(tiles, blocks, pair, put)


def mix(place, fock, first, load, store, rows, width):
    total = fock.shape[0]
    strips = rows // 16

    def strip(step, carry):
        u = step // strips
        at = pl.ds(pl.multiple_of(lax.rem(step, strips) * 16, 16), 16)
        taken = [load(k // first, u, k % first, at) for k in range(total)]
        for k in range(total):
            column = (place[0] ^ (k // first)) * first + k % first
            result = None
            for m in range(total):
                line = (place[0] ^ (m // first)) * first + m % first
                term = (-fock[line, column]) * taken[m]
                result = term if result is None else result + term
            store(k // first, u, k % first, column, at, result)
        return carry

    lax.fori_loop(0, first * strips, strip, 0)


def half_kernel(tiles, groups, first, place, fock, ladder, *refs):
    held, out = refs[:groups], refs[groups:]

    def load(s, u, r, at):
        return held[s][u, r, at, :].astype(WIDE)

    def store(s, u, w, column, at, result):
        out[s][u, w, at, :] = (ladder[column, u, at, :].astype(WIDE) + result).astype(NARROW)

    mix(place, fock, first, load, store, tiles.edge, 2 * tiles.edge)


def with_mirror(tiles, place, x, finish):
    across = place[1] < len(tiles.above)

    @pl.when(across)
    def _():
        finish(tiles.mirror_across(x))

    @pl.when(jnp.logical_not(across))
    def _():
        finish(tiles.mirror_within(x))


def update_kernel(tiles, groups, first, place, fock, occ, sums, *refs):
    own, other = refs[:groups], refs[groups:2 * groups]
    sent, rest = refs[2 * groups:2 * groups + 2]
    out = refs[2 * groups + 2:3 * groups + 2]
    update = refs[3 * groups + 2]

    def one(step, carry):
        u, w = step // first, lax.rem(step, first)
        for s in range(groups):
            column = (place[0] ^ s) * first + w
            base = occ[place[0] * first + u] + occ[column]

            def finish(mirrored):
                value = (own[s][u, w].astype(WIDE) + mirrored) / (base - sums[...])
                narrow = value.astype(NARROW)
                update[u, s * first + w] = value
                sent[column, u] = narrow
                rest[u, s * first + w] = (2.0 * (value - narrow.astype(WIDE))).astype(NARROW)

            with_mirror(tiles, place, other[s][w, u].astype(WIDE), finish)
        return carry

    lax.fori_loop(0, first * first, one, 0)

    def load(s, u, r, at):
        return update[u, s * first + r, at, :]

    def store(s, u, w, column, at, result):
        out[s][u, w, at, :] = result.astype(NARROW)

    mix(place, fock, first, load, store, tiles.edge, 2 * tiles.edge)


def rest_kernel(tiles, groups, first, place, occ, sums, rest, *refs):
    own, other, out = refs[:groups], refs[groups:2 * groups], refs[2 * groups]

    def one(step, carry):
        u, w = step // first, lax.rem(step, first)
        for s in range(groups):
            column = (place[0] ^ s) * first + w
            base = occ[place[0] * first + u] + occ[column]

            def finish(mirrored):
                value = (own[s][u, w].astype(WIDE) + mirrored) / (base - sums[...])
                out[column, u] = (rest[u, s * first + w].astype(WIDE) + value).astype(NARROW)

            with_mirror(tiles, place, other[s][w, u].astype(WIDE), finish)
        return carry

    lax.fori_loop(0, first * first, one, 0)


def exchange(blocks):
    return lax.all_to_all(blocks, "occj", split_axis=0, concat_axis=0, tiled=True)


def across_first(parts, groups):
    return [parts[0]] + [
        lax.ppermute(parts[s], "occi", [(k, k ^ s) for k in range(groups)]) for s in range(1, groups)
    ]


def gather_vectors(vectors, devices):
    held, order = vectors[None], [0]
    step = devices // 2
    while True:
        other = lax.ppermute(held, "occj", [(k, k ^ step) for k in range(devices)])
        order = order + [k ^ step for k in order]
        if step == 1:
            return held, other, order
        held = jnp.concatenate([held, other], axis=0)
        step //= 2


def virtual_sums(tiles, vir_energy, q):
    e, g = tiles.edge, tiles.rows
    n_above = len(tiles.above)
    first = jnp.array([a for a, _ in tiles.above] + list(range(0, tiles.n, 2)), jnp.int32)[q]
    second = jnp.array([b for _, b in tiles.above] + list(range(1, tiles.n, 2)), jnp.int32)[q]
    a = lax.dynamic_slice_in_dim(vir_energy, first * e, e)
    b = lax.dynamic_slice_in_dim(vir_energy, second * e, e)
    pair = a[:, None] + b[None, :]
    across = jnp.concatenate([pair, pair], axis=1)
    halves = [
        jnp.concatenate([t[:g, None] + t[None, :], t[g:, None] + t[None, :]], axis=1) for t in (a, b)
    ]
    return jnp.where(q < n_above, across, jnp.concatenate(halves, axis=0))


def local(groups, devices, amplitudes, vectors, occupied_fock_block, occ_energy, vir_energy):
    first, second, virtual = amplitudes.shape[:3]
    assert second == 1 and groups * first == devices
    assert groups & (groups - 1) == 0 and devices & (devices - 1) == 0
    tiles = Tiles(devices, virtual)
    edge = tiles.edge
    current = amplitudes.reshape(first, virtual, virtual)
    count = current.size
    fock = occupied_fock_block.astype(WIDE)
    p, q = lax.axis_index("occi"), lax.axis_index("occj")
    place = jnp.stack([p, q]).astype(jnp.int32)
    part = jax.ShapeDtypeStruct((first, first, edge, 2 * edge), NARROW)
    packed = jax.ShapeDtypeStruct((devices, first, edge, 2 * edge), NARROW)
    vector_rows = virtual // devices

    low, high, order = gather_vectors(vectors, devices)
    held = exchange(pack(tiles, devices, current)).reshape(groups, first, first, edge, 2 * edge)
    mirror = across_first([held[p ^ s] for s in range(groups)], groups)
    sums = virtual_sums(tiles, vir_energy, q)

    ladder_flops = first * vectors.shape[0] * 4 * virtual**3
    ladder = exchange(call(
        functools.partial(first_ladder_kernel, tiles, order), packed,
        [pltpu.VMEM((vectors.shape[0], virtual, virtual), NARROW), pltpu.VMEM((virtual, virtual), WIDE)],
        ladder_flops, 8 * count, place, current, low, high, specs=[SMEM, VMEM, VMEM, VMEM],
    ))
    half = call(
        functools.partial(half_kernel, tiles, groups, first), [part] * groups, [],
        2 * devices * count, 6 * count, place, fock, ladder, *mirror, specs=[SMEM] * 2 + [VMEM] * (groups + 1),
    )
    other = across_first(half, groups)
    sent, rest, *mixed = call(
        functools.partial(update_kernel, tiles, groups, first),
        [packed, jax.ShapeDtypeStruct((first, devices, edge, 2 * edge), NARROW)] + [part] * groups,
        [pltpu.VMEM((first, devices, edge, 2 * edge), WIDE)],
        2 * devices * count, 10 * count, place, fock, occ_energy, sums, *half, *other,
        specs=[SMEM] * 3 + [VMEM] * (2 * groups + 1),
    )
    other = across_first(mixed, groups)
    back = exchange(sent)
    base = call(
        functools.partial(second_ladder_kernel, tiles, order, first),
        jax.ShapeDtypeStruct(current.shape, WIDE),
        [pltpu.VMEM((vectors.shape[0], virtual, virtual), NARROW), pltpu.VMEM((virtual, virtual), WIDE),
         pltpu.VMEM((virtual, virtual), NARROW)],
        ladder_flops, 12 * count, place, occ_energy, current, back,
        jnp.broadcast_to(vir_energy[:, None], (virtual, 128)), vir_energy[None, :], low, high,
        specs=[SMEM] * 2 + [VMEM] * 6,
    )
    rest = exchange(call(
        functools.partial(rest_kernel, tiles, groups, first), packed, [],
        4 * count, 8 * count, place, occ_energy, sums, rest, *mixed, *other,
        specs=[SMEM] * 2 + [VMEM] * (2 * groups + 2),
    ))
    done = call(
        functools.partial(add_kernel, tiles), jax.ShapeDtypeStruct(current.shape, WIDE), [],
        count, 10 * count, base, rest, specs=[VMEM, VMEM], aliases={0: 0},
    )
    return done.reshape(amplitudes.shape)


def solution(mesh):
    sizes = (mesh.shape["occi"], mesh.shape["occj"])
    return jax.shard_map(
        functools.partial(local, *sizes),
        mesh=mesh,
        in_specs=(P("occi", "occj", None, None), P(None, "occj", None), P(), P(), P()),
        out_specs=P("occi", "occj", None, None),
        check_vma=False,
    )
```

time: 336 us -> 160 us (0.48)
  blocking collectives: 92.6 us -> 0 us
  waiting for transfers between devices: 139 us -> 74.8 us
  Pallas kernels: 0 us -> 36.2 us
  local copies, waits for them, and re-layouts: 26.1 us -> 1.78 us
  matrix products: 23.1 us -> 0 us
  starting transfers between devices: 25.2 us -> 40.7 us
  other arithmetic: 15.4 us -> 2.24 us
  between operations: 13.6 us -> 1.54 us
    all_to_all x6 -> x4, waiting for transfers between devices: 118 us -> 5.77 us  [exchange(): lax.all_to_all(blocks, 'occj', split_axis=0, concat_axis=0, tiled=True)]
    all_to_all x4 -> x0, blocking collectives: 92.6 us -> none  [the longest x2 55.7 us: local(): lax.all_to_all(half_slab, 'occi', split_axis=0, concat_axis=2, tiled=True)]
    ppermute x0 -> x12, waiting for transfers between devices: none -> 69.1 us  [the longest x9 55.4 us: across_first(): lax.ppermute(parts[s], 'occi', [(k, k ^ s) for k in range(groups)])]
    pallas_call x0 -> x7, Pallas kernels: none -> 36.2 us  [call(): pl.pallas_call(body, out_shape=outs, in_specs=specs, out_specs=jax.tree.m...]
    convert_element_type x13 -> x0, local copies, waits for them, and re-layouts: 24.3 us -> none  [the longest x6 12.9 us: local(): residual = halfway.astype(jnp.float32) + mirrored.astype(jnp.float32)]
    ppermute x0 -> x12, starting transfers between devices: none -> 23.5 us  [the longest x9 18.6 us: across_first(): lax.ppermute(parts[s], 'occi', [(k, k ^ s) for k in range(groups)])]
    dot_general x8 -> x0, matrix products: 23.1 us -> none  [the longest x6 21.8 us: ladder_term(): jnp.einsum('ac,pjcb->pjab', single, inner, preferred_element_type=jnp.flo...]
    all_gather x1 -> x0, waiting for transfers between devices: 20.3 us -> none  [local(): gathered = lax.all_gather(vectors, 'occj', axis=1, tiled=True)]
  transfers between devices with their start and end apart: 7 -> 16, of which waited for: 6 -> 10; matrix products, arithmetic and copies ran while one was open for 8% -> 1% of each run, Pallas kernels for 0% -> 16%
where the time goes in v1:
time: 160 us; the launch traced here: 157 us
  waiting for transfers between devices  74.8 us (47%)
  starting transfers between devices  40.7 us (25%)
  Pallas kernels  36.2 us (23%)
  other arithmetic  2.24 us (1%)
  local copies, waits for them, and re-layouts  1.78 us (1%)
    ppermute x9, waiting for transfers between devices, across_first(): lax.ppermute(parts[s], 'occi', [(k, k ^ s) for k in range(groups)])  55.4 us
    pallas_call x7, Pallas kernels, call(): pl.pallas_call(body, out_shape=outs, in_specs=specs, out_specs=jax.tree.m...  36.2 us
    ppermute x9, starting transfers between devices, across_first(): lax.ppermute(parts[s], 'occi', [(k, k ^ s) for k in range(groups)])  18.6 us
    all_to_all x4, starting transfers between devices, exchange(): lax.all_to_all(blocks, 'occj', split_axis=0, concat_axis=0, tiled=True)  17.2 us
    ppermute x3, waiting for transfers between devices, gather_vectors(): other = lax.ppermute(held, 'occj', [(k, k ^ step) for k in range(devices)])  13.7 us
    all_to_all x4, waiting for transfers between devices, exchange(): lax.all_to_all(blocks, 'occj', split_axis=0, concat_axis=0, tiled=True)  5.77 us
    ppermute x3, starting transfers between devices, gather_vectors(): other = lax.ppermute(held, 'occj', [(k, k ^ step) for k in range(devices)])  4.82 us
  transfers between devices with their start and end apart: 16, of which 10 were waited for; matrix products, arithmetic and copies ran while one was open for 1% of the time, Pallas kernels for 16%

profile of v1, /device:TPU:0, one launch (start us, length us, event | category | flops | bytes accessed | tf_op | source)
XLA Modules:
  0.0 157.3 jit_solution(11387952182776343982)
XLA Ops:
  0.0 0.0 copy-start
  0.0 3.0 %collective-permute-start = (bf16[1,3,64,512]{3,2,1,0:T(8,128)(2,1)}, bf16[1,3,64,512]{3,2,1,0:T(8,128)(2,1)S(1)}, u32[]{:S(2)}, u32[]{:S(2)}) collective-permute-start(bf16[1,3,64,512]{3,2,1,0:T(8,128)(2,1)} %bitcast.24), channel_id=1, source_target_pairs={{0,4},{1,5},{2,6},{3,7},{4,0},{5,1},{6,2},{7,3},{8,12},{9,13},{10,... | collective-permute-start | bytes 589832 | tf_op jit(solution)/shard_map/ppermute | solution.py:264
  3.0 5.1 %collective-permute-done = bf16[1,3,64,512]{3,2,1,0:T(8,128)(2,1)S(1)} collective-permute-done((bf16[1,3,64,512]{3,2,1,0:T(8,128)(2,1)}, bf16[1,3,64,512]{3,2,1,0:T(8,128)(2,1)S(1)}, u32[]{:S(2)}, u32[]{:S(2)}) %collective-permute-start) | collective-permute-done | bytes 196640 | tf_op jit(solution)/shard_map/ppermute | solution.py:264
  8.1 1.0 pad_maximum_fusion.1
  9.0 1.8 %collective-permute-start.1 = (bf16[2,3,64,512]{3,2,1,0:T(8,128)(2,1)S(1)}, bf16[2,3,64,512]{3,2,1,0:T(8,128)(2,1)S(1)}, u32[]{:S(2)}, u32[]{:S(2)}) collective-permute-start(bf16[2,3,64,512]{3,2,1,0:T(8,128)(2,1)S(1)} %pad_maximum_fusion.1), channel_id=1, source_target_pairs={{0,2},{1,3},{2,0},{3,1},{4,6},{5,7},{6,4},{7,5},{8,10},{9,11},{10,... | collective-permute-start | bytes 1179656 | tf_op jit(solution)/shard_map/ppermute | solution.py:264
  10.8 8.6 %collective-permute-done.1 = bf16[2,3,64,512]{3,2,1,0:T(8,128)(2,1)S(1)} collective-permute-done((bf16[2,3,64,512]{3,2,1,0:T(8,128)(2,1)S(1)}, bf16[2,3,64,512]{3,2,1,0:T(8,128)(2,1)S(1)}, u32[]{:S(2)}, u32[]{:S(2)}) %collective-permute-start.1) | collective-permute-done | bytes 393248 | tf_op jit(solution)/shard_map/ppermute | solution.py:264
  19.4 1.0 pad_maximum_fusion.low
  20.4 0.0 copy-start.2
  20.4 0.1 collective-permute-start.2
  20.5 0.0 copy-done
  20.5 0.0 copy-start.8
  20.5 0.0 copy-start.7
  20.5 1.2 shard_map.74
  21.8 3.7 %all-to-all-start.1 = ((bf16[8,2,128,256]{3,2,1,0:T(8,128)(2,1)}), bf16[8,2,128,256]{3,2,1,0:T(8,128)(2,1)S(1)}, u32[]{:S(2)}, u32[]{:S(2)}) async-start(bf16[8,2,128,256]{3,2,1,0:T(8,128)(2,1)} %shard_map.74), calls=%async_computation.1 | async-start | bytes 2097152 | tf_op jit(solution)/shard_map/all_to_all | solution.py:251
  25.5 0.0 copy-done.8
  25.5 0.7 dynamic_slice.26
  26.8 0.0 copy-done.7
  26.8 0.7 dynamic_slice.24
  28.2 0.1 pad_add_fusion.place
  28.3 0.0 collective-permute-done.2.high
  28.3 0.0 copy-done.2
  28.3 8.3 %shard_map.73 = bf16[8,2,128,256]{3,2,1,0:T(8,128)(2,1)} custom-call(s32[2]{0:T(128)S(1)} %pad_add_fusion.place, f32[2,512,512]{2,1,0:T(8,128)} %bitcast.19, bf16[4,3,64,512]{3,2,1,0:T(8,128)(2,1)S(1)} %pad_maximum_fusion.low, bf16[4,3,64,512]{3,2,1,0:T(8,128)(2,1)} %collective-permute-done.2.high), custom_call_target="tpu_custom_call" | custom-call | flops 3221225472 | bytes 4194304 | tf_op jit(solution)/shard_map/pallas_call | solution.py:44
  36.6 4.3 %all-to-all-done.1 = bf16[8,2,128,256]{3,2,1,0:T(8,128)(2,1)S(1)} async-done(((bf16[8,2,128,256]{3,2,1,0:T(8,128)(2,1)}), bf16[8,2,128,256]{3,2,1,0:T(8,128)(2,1)S(1)}, u32[]{:S(2)}, u32[]{:S(2)}) %all-to-all-start.1) | async-done | bytes 1048608 | tf_op jit(solution)/shard_map/all_to_all | solution.py:251
  40.9 3.6 %all-to-all-start = ((bf16[8,2,128,256]{3,2,1,0:T(8,128)(2,1)}), bf16[8,2,128,256]{3,2,1,0:T(8,128)(2,1)S(1)}, u32[]{:S(2)}, u32[]{:S(2)}) async-start(bf16[8,2,128,256]{3,2,1,0:T(8,128)(2,1)} %shard_map.73), calls=%async_computation | async-start | bytes 2097152 | tf_op jit(solution)/shard_map/all_to_all | solution.py:251
  44.5 0.0 copy-done.4
  44.5 0.1 fusion
  44.6 0.1 fusion.1
  44.6 0.1 dynamic-slice_bitcast_fusion
  44.7 1.7 %collective-permute-start.3 = (bf16[2,2,128,256]{3,2,1,0:T(8,128)(2,1)S(1)}, bf16[2,2,128,256]{3,2,1,0:T(8,128)(2,1)S(1)}, u32[]{:S(2)}, u32[]{:S(2)}) collective-permute-start(bf16[2,2,128,256]{3,2,1,0:T(8,128)(2,1)S(1)} %get-tuple-element.27), channel_id=1, source_target_pairs={{0,8},{8,0},{16,24},{24,16},{1,9},{9,1},{17,25},{25,17},{2,10},{10... | collective-permute-start | bytes 786440 | tf_op jit(solution)/shard_map/ppermute | solution.py:256
  46.4 2.6 %collective-permute-start.4 = (bf16[2,2,128,256]{3,2,1,0:T(8,128)(2,1)S(1)}, bf16[2,2,128,256]{3,2,1,0:T(8,128)(2,1)S(1)}, u32[]{:S(2)}, u32[]{:S(2)}) collective-permute-start(bf16[2,2,128,256]{3,2,1,0:T(8,128)(2,1)S(1)} %get-tuple-element.26), channel_id=1, source_target_pairs={{0,16},{8,24},{16,0},{24,8},{1,17},{9,25},{17,1},{25,9},{2,18},{10... | collective-permute-start | bytes 786440 | tf_op jit(solution)/shard_map/ppermute | solution.py:256
  49.0 0.2 collective-permute-start.5
  49.2 0.1 fusion.2
  49.3 0.0 copy-done.6
  49.3 0.1 broadcast_add_fusion.2
  49.4 9.1 %collective-permute-done.3.refs_1_ = bf16[2,2,128,256]{3,2,1,0:T(8,128)(2,1)S(1)} collective-permute-done((bf16[2,2,128,256]{3,2,1,0:T(8,128)(2,1)S(1)}, bf16[2,2,128,256]{3,2,1,0:T(8,128)(2,1)S(1)}, u32[]{:S(2)}, u32[]{:S(2)}) %collective-permute-start.3) | collective-permute-done | bytes 262176 | tf_op jit(solution)/shard_map/ppermute | solution.py:256
  58.5 9.2 %collective-permute-done.4.refs_2_ = bf16[2,2,128,256]{3,2,1,0:T(8,128)(2,1)S(1)} collective-permute-done((bf16[2,2,128,256]{3,2,1,0:T(8,128)(2,1)S(1)}, bf16[2,2,128,256]{3,2,1,0:T(8,128)(2,1)S(1)}, u32[]{:S(2)}, u32[]{:S(2)}) %collective-permute-start.4) | collective-permute-done | bytes 262176 | tf_op jit(solution)/shard_map/ppermute | solution.py:256
  67.7 0.0 collective-permute-done.5.refs_3_
  67.7 0.0 all-to-all-done.ladder
  67.7 2.6 %shard_map.75 = (bf16[2,2,128,256]{3,2,1,0:T(8,128)(2,1)S(1)}, bf16[2,2,128,256]{3,2,1,0:T(8,128)(2,1)S(1)}, bf16[2,2,128,256]{3,2,1,0:T(8,128)(2,1)S(1)}, bf16[2,2,128,256]{3,2,1,0:T(8,128)(2,1)S(1)}) custom-call(s32[2]{0:T(128)S(1)} %pad_add_fusion.place, f32[8,8]{1,0:T(8,128)S(1)} %convert_element_type.3.fock, ...), custom_call_target="tpu_custom_call" | custom-call | flops 8388608 | bytes 3145728 | tf_op jit(solution)/shard_map/pallas_call | solution.py:44
  70.3 5.4 %collective-permute-start.6 = (bf16[2,2,128,256]{3,2,1,0:T(8,128)(2,1)S(1)}, bf16[2,2,128,256]{3,2,1,0:T(8,128)(2,1)S(1)}, u32[]{:S(2)}, u32[]{:S(2)}) collective-permute-start(bf16[2,2,128,256]{3,2,1,0:T(8,128)(2,1)S(1)} %get-tuple-element.16.refs_1_), channel_id=1, source_target_pairs={{0,8},{8,0},{16,24},{24,16},{1,9},{9,1},{17,25},{25,17},{2,10},{10... | collective-permute-start | bytes 786440 | tf_op jit(solution)/shard_map/ppermute | solution.py:256
  75.7 1.1 collective-permute-start.7
  76.8 1.4 collective-permute-start.8
  78.2 0.1 broadcast_add_fusion
  78.3 7.7 %collective-permute-done.6.refs_5_ = bf16[2,2,128,256]{3,2,1,0:T(8,128)(2,1)S(1)} collective-permute-done((bf16[2,2,128,256]{3,2,1,0:T(8,128)(2,1)S(1)}, bf16[2,2,128,256]{3,2,1,0:T(8,128)(2,1)S(1)}, u32[]{:S(2)}, u32[]{:S(2)}) %collective-permute-start.6) | collective-permute-done | bytes 262176 | tf_op jit(solution)/shard_map/ppermute | solution.py:256
  85.9 11.1 %collective-permute-done.7.refs_6_ = bf16[2,2,128,256]{3,2,1,0:T(8,128)(2,1)S(1)} collective-permute-done((bf16[2,2,128,256]{3,2,1,0:T(8,128)(2,1)S(1)}, bf16[2,2,128,256]{3,2,1,0:T(8,128)(2,1)S(1)}, u32[]{:S(2)}, u32[]{:S(2)}) %collective-permute-start.7) | collective-permute-done | bytes 262176 | tf_op jit(solution)/shard_map/ppermute | solution.py:256
  97.1 0.0 collective-permute-done.8.refs_7_
  97.1 0.0 copy-done.5
  97.1 4.7 %shard_map.76 = (bf16[8,2,128,256]{3,2,1,0:T(8,128)(2,1)}, bf16[2,8,128,256]{3,2,1,0:T(8,128)(2,1)}, bf16[2,2,128,256]{3,2,1,0:T(8,128)(2,1)S(1)}, bf16[2,2,128,...) custom-call(s32[2]{0:T(128)S(1)} %pad_add_fusion.place, ...), custom_call_target="tpu_custom_call" | custom-call | flops 8388608 | bytes 5242880 | tf_op jit(solution)/shard_map/pallas_call | solution.py:44
  101.8 5.0 %all-to-all-start.2 = ((bf16[8,2,128,256]{3,2,1,0:T(8,128)(2,1)}), bf16[8,2,128,256]{3,2,1,0:T(8,128)(2,1)S(1)}, u32[]{:S(2)}, u32[]{:S(2)}) async-start(bf16[8,2,128,256]{3,2,1,0:T(8,128)(2,1)} %get-tuple-element.19), calls=%async_computation.2 | async-start | bytes 2097152 | tf_op jit(solution)/shard_map/all_to_all | solution.py:251
  106.7 5.0 %collective-permute-start.10 = (bf16[2,2,128,256]{3,2,1,0:T(8,128)(2,1)S(1)}, bf16[2,2,128,256]{3,2,1,0:T(8,128)(2,1)S(1)}, u32[]{:S(2)}, u32[]{:S(2)}) collective-permute-start(bf16[2,2,128,256]{3,2,1,0:T(8,128)(2,1)S(1)} %get-tuple-element.23.refs_2_), channel_id=1, source_target_pairs={{0,16},{8,24},{16,0},{24,8},{1,17},{9,25},{17,1},{25,9},{2,18},{10... | collective-permute-start | bytes 786440 | tf_op jit(solution)/shard_map/ppermute | solution.py:256
  111.7 1.4 collective-permute-start.11
  113.1 0.0 collective-permute-start.9
  113.1 17.1 %collective-permute-done.10.refs_6_ = bf16[2,2,128,256]{3,2,1,0:T(8,128)(2,1)S(1)} collective-permute-done((bf16[2,2,128,256]{3,2,1,0:T(8,128)(2,1)S(1)}, bf16[2,2,128,256]{3,2,1,0:T(8,128)(2,1)S(1)}, u32[]{:S(2)}, u32[]{:S(2)}) %collective-permute-start.10) | collective-permute-done | bytes 262176 | tf_op jit(solution)/shard_map/ppermute | solution.py:256
  130.1 0.0 collective-permute-done.11.refs_7_
  130.1 1.1 collective-permute-done.9.refs_5_
  131.3 0.0 copy-done.1
  131.3 2.4 %shard_map.78 = bf16[8,2,128,256]{3,2,1,0:T(8,128)(2,1)} custom-call(s32[2]{0:T(128)S(1)} %pad_add_fusion.place, f32[8]{0:T(128)S(1)} %copy-done.5, f32[128,256]{1,0:T(8,128)S(1)} %maximum_select_fusion.sums, bf16[2,8,128,256]{3,2,1,0:T(8,128)(2,1)S(1)} %copy-done.1, bf16[2,2,128,256]{3,2,1,0:T(8,128)(2,1)S(1)} %get-tuple-element.21.refs_0_.refs_4_, ...), custom_call_target="tpu_custom_call" | custom-call | flops 2097152 | bytes 4194304 | tf_op jit(solution)/shard_map/pallas_call | solution.py:44
  133.7 0.0 all-to-all-done.2.blocks
  133.7 5.0 %all-to-all-start.3 = ((bf16[8,2,128,256]{3,2,1,0:T(8,128)(2,1)}), bf16[8,2,128,256]{3,2,1,0:T(8,128)(2,1)S(1)}, u32[]{:S(2)}, u32[]{:S(2)}) async-start(bf16[8,2,128,256]{3,2,1,0:T(8,128)(2,1)} %shard_map.78), calls=%async_computation.3 | async-start | bytes 2097152 | tf_op jit(solution)/shard_map/all_to_all | solution.py:251
  138.7 0.1 broadcast_in_dim.7.row
  138.8 0.0 copy-done.3
  138.8 13.8 %shard_map.77.source = f32[2,512,512]{2,1,0:T(8,128)} custom-call(s32[2]{0:T(128)S(1)} %pad_add_fusion.place, f32[8]{0:T(128)S(1)} %copy-done.5, f32[2,512,512]{2,1,0:T(8,128)} %bitcast.20, bf16[8,2,128,256]{3,2,1,0:T(8,128)(2,1)S(1)} %all-to-all-done.2.blocks, f32[512,128]{1,0:T(8,128)S(1)} %broadcast_in_dim.7.row, f32[1,512]{1,0:T(1,128)S(1)} %bitcast.22, ...), custom_call_target="tpu_custom_call" | custom-call | flops 3221225472 | bytes 6291456 | tf_op jit(solution)/shard_map/pallas_call | solution.py:44
  152.7 1.4 all-to-all-done.3.blocks
  154.1 3.2 %shard_map.79 = f32[2,512,512]{2,1,0:T(8,128)} custom-call(f32[2,512,512]{2,1,0:T(8,128)} %shard_map.77.source, bf16[8,2,128,256]{3,2,1,0:T(8,128)(2,1)S(1)} %all-to-all-done.3.blocks), custom_call_target="tpu_custom_call", output_to_operand_aliasing={{}: (0, {})} | custom-call | flops 524288 | bytes 5242880 | tf_op jit(solution)/shard_map/pallas_call | solution.py:44
  (7 shorter events, 0.0 us)
Async XLA Ops:
  0.0 20.5 %copy-start = (f32[2,1,512,512]{3,2,1,0:T(8,128)S(1)}, f32[2,1,512,512]{3,2,1,0:T(8,128)}, u32[]{:S(2)}) copy-start(f32[2,1,512,512]{3,2,1,0:T(8,128)} %param.7) | copy-start | bytes 6291460
  0.0 8.1 %collective-permute-start = (bf16[1,3,64,512]{3,2,1,0:T(8,128)(2,1)}, bf16[1,3,64,512]{3,2,1,0:T(8,128)(2,1)S(1)}, u32[]{:S(2)}, u32[]{:S(2)}) collective-permute-start(bf16[1,3,64,512]{3,2,1,0:T(8,128)(2,1)} %bitcast.24), channel_id=1, source_target_pairs={{0,4},{1,5},{2,6},{3,7},{4,0},{5,1},{6,2},{7,3},{8,12},{9,13},{10,... | collective-permute-start | bytes 589832 | tf_op jit(solution)/shard_map/ppermute | solution.py:264
  9.0 10.4 %collective-permute-start.1 = (bf16[2,3,64,512]{3,2,1,0:T(8,128)(2,1)S(1)}, bf16[2,3,64,512]{3,2,1,0:T(8,128)(2,1)S(1)}, u32[]{:S(2)}, u32[]{:S(2)}) collective-permute-start(bf16[2,3,64,512]{3,2,1,0:T(8,128)(2,1)S(1)} %pad_maximum_fusion.1), channel_id=1, source_target_pairs={{0,2},{1,3},{2,0},{3,1},{4,6},{5,7},{6,4},{7,5},{8,10},{9,11},{10,... | collective-permute-start | bytes 1179656 | tf_op jit(solution)/shard_map/ppermute | solution.py:264
  20.4 7.9 %copy-start.2 = (bf16[4,3,64,512]{3,2,1,0:T(8,128)(2,1)}, bf16[4,3,64,512]{3,2,1,0:T(8,128)(2,1)S(1)}, u32[]{:S(2)}) copy-start(bf16[4,3,64,512]{3,2,1,0:T(8,128)(2,1)S(1)} %pad_maximum_fusion.low) | copy-start | bytes 2359300
  20.4 7.8 %collective-permute-start.2 = (bf16[4,3,64,512]{3,2,1,0:T(8,128)(2,1)S(1)}, bf16[4,3,64,512]{3,2,1,0:T(8,128)(2,1)}, u32[]{:S(2)}, u32[]{:S(2)}) collective-permute-start(bf16[4,3,64,512]{3,2,1,0:T(8,128)(2,1)S(1)} %pad_maximum_fusion.low), channel_id=1, source_target_pairs={{0,1},{1,0},{2,3},{3,2},{4,5},{5,4},{6,7},{7,6},{8,9},{9,8},{10,11... | collective-permute-start | bytes 2359304 | tf_op jit(solution)/shard_map/ppermute | solution.py:264
  20.5 5.0 %copy-start.8 = (s32[8]{0:T(128)S(1)}, s32[8]{0:T(128)}, u32[]{:S(2)}) copy-start(s32[8]{0:T(128)} %constant.33.clone) | copy-start | bytes 100
  20.5 6.3 %copy-start.7 = (s32[8]{0:T(128)S(1)}, s32[8]{0:T(128)}, u32[]{:S(2)}) copy-start(s32[8]{0:T(128)} %constant.32.clone) | copy-start | bytes 100
  21.8 19.1 %all-to-all-start.1 = ((bf16[8,2,128,256]{3,2,1,0:T(8,128)(2,1)}), bf16[8,2,128,256]{3,2,1,0:T(8,128)(2,1)S(1)}, u32[]{:S(2)}, u32[]{:S(2)}) async-start(bf16[8,2,128,256]{3,2,1,0:T(8,128)(2,1)} %shard_map.74), calls=%async_computation.1 | async-start | bytes 2097152 | tf_op jit(solution)/shard_map/all_to_all | solution.py:251
  36.6 7.9 %copy-start.4 = (f32[512]{0:T(512)S(1)}, f32[512]{0:T(512)}, u32[]{:S(2)}) copy-start(f32[512]{0:T(512)} %param.11) | copy-start | bytes 6148
  36.6 12.7 %copy-start.6 = (bf16[8,8]{1,0:T(8,128)(2,1)S(1)}, bf16[8,8]{1,0:T(8,128)(2,1)}, u32[]{:S(2)}) copy-start(bf16[8,8]{1,0:T(8,128)(2,1)} %param.9) | copy-start | bytes 388
  40.9 26.8 %all-to-all-start = ((bf16[8,2,128,256]{3,2,1,0:T(8,128)(2,1)}), bf16[8,2,128,256]{3,2,1,0:T(8,128)(2,1)S(1)}, u32[]{:S(2)}, u32[]{:S(2)}) async-start(bf16[8,2,128,256]{3,2,1,0:T(8,128)(2,1)} %shard_map.73), calls=%async_computation | async-start | bytes 2097152 | tf_op jit(solution)/shard_map/all_to_all | solution.py:251
  44.6 52.4 %copy-start.5 = (f32[8]{0:T(128)S(1)}, f32[8]{0:T(128)}, u32[]{:S(2)}) copy-start(f32[8]{0:T(128)} %occ.5) | copy-start | bytes 100
  44.7 13.8 %collective-permute-start.3 = (bf16[2,2,128,256]{3,2,1,0:T(8,128)(2,1)S(1)}, bf16[2,2,128,256]{3,2,1,0:T(8,128)(2,1)S(1)}, u32[]{:S(2)}, u32[]{:S(2)}) collective-permute-start(bf16[2,2,128,256]{3,2,1,0:T(8,128)(2,1)S(1)} %get-tuple-element.27), channel_id=1, source_target_pairs={{0,8},{8,0},{16,24},{24,16},{1,9},{9,1},{17,25},{25,17},{2,10},{10... | collective-permute-start | bytes 786440 | tf_op jit(solution)/shard_map/ppermute | solution.py:256
  46.4 21.3 %collective-permute-start.4 = (bf16[2,2,128,256]{3,2,1,0:T(8,128)(2,1)S(1)}, bf16[2,2,128,256]{3,2,1,0:T(8,128)(2,1)S(1)}, u32[]{:S(2)}, u32[]{:S(2)}) collective-permute-start(bf16[2,2,128,256]{3,2,1,0:T(8,128)(2,1)S(1)} %get-tuple-element.26), channel_id=1, source_target_pairs={{0,16},{8,24},{16,0},{24,8},{1,17},{9,25},{17,1},{25,9},{2,18},{10... | collective-permute-start | bytes 786440 | tf_op jit(solution)/shard_map/ppermute | solution.py:256
  49.0 18.8 %collective-permute-start.5 = (bf16[2,2,128,256]{3,2,1,0:T(8,128)(2,1)S(1)}, bf16[2,2,128,256]{3,2,1,0:T(8,128)(2,1)S(1)}, u32[]{:S(2)}, u32[]{:S(2)}) collective-permute-start(bf16[2,2,128,256]{3,2,1,0:T(8,128)(2,1)S(1)} %get-tuple-element.25), channel_id=1, source_target_pairs={{0,24},{8,16},{16,8},{24,0},{1,25},{9,17},{17,9},{25,1},{2,26},{10... | collective-permute-start | bytes 786440 | tf_op jit(solution)/shard_map/ppermute | solution.py:256
  70.3 15.6 %collective-permute-start.6 = (bf16[2,2,128,256]{3,2,1,0:T(8,128)(2,1)S(1)}, bf16[2,2,128,256]{3,2,1,0:T(8,128)(2,1)S(1)}, u32[]{:S(2)}, u32[]{:S(2)}) collective-permute-start(bf16[2,2,128,256]{3,2,1,0:T(8,128)(2,1)S(1)} %get-tuple-element.16.refs_1_), channel_id=1, source_target_pairs={{0,8},{8,0},{16,24},{24,16},{1,9},{9,1},{17,25},{25,17},{2,10},{10... | collective-permute-start | bytes 786440 | tf_op jit(solution)/shard_map/ppermute | solution.py:256
  75.7 21.4 %collective-permute-start.7 = (bf16[2,2,128,256]{3,2,1,0:T(8,128)(2,1)S(1)}, bf16[2,2,128,256]{3,2,1,0:T(8,128)(2,1)S(1)}, u32[]{:S(2)}, u32[]{:S(2)}) collective-permute-start(bf16[2,2,128,256]{3,2,1,0:T(8,128)(2,1)S(1)} %get-tuple-element.17.refs_2_), channel_id=1, source_target_pairs={{0,16},{8,24},{16,0},{24,8},{1,17},{9,25},{17,1},{25,9},{2,18},{10... | collective-permute-start | bytes 786440 | tf_op jit(solution)/shard_map/ppermute | solution.py:256
  76.8 20.3 %collective-permute-start.8 = (bf16[2,2,128,256]{3,2,1,0:T(8,128)(2,1)S(1)}, bf16[2,2,128,256]{3,2,1,0:T(8,128)(2,1)S(1)}, u32[]{:S(2)}, u32[]{:S(2)}) collective-permute-start(bf16[2,2,128,256]{3,2,1,0:T(8,128)(2,1)S(1)} %get-tuple-element.18.refs_3_), channel_id=1, source_target_pairs={{0,24},{8,16},{16,8},{24,0},{1,25},{9,17},{17,9},{25,1},{2,26},{10... | collective-permute-start | bytes 786440 | tf_op jit(solution)/shard_map/ppermute | solution.py:256
  101.8 29.5 %copy-start.1 = (bf16[2,8,128,256]{3,2,1,0:T(8,128)(2,1)S(1)}, bf16[2,8,128,256]{3,2,1,0:T(8,128)(2,1)}, u32[]{:S(2)}) copy-start(bf16[2,8,128,256]{3,2,1,0:T(8,128)(2,1)} %get-tuple-element.20.rest) | copy-start | bytes 3145732
  101.8 31.9 %all-to-all-start.2 = ((bf16[8,2,128,256]{3,2,1,0:T(8,128)(2,1)}), bf16[8,2,128,256]{3,2,1,0:T(8,128)(2,1)S(1)}, u32[]{:S(2)}, u32[]{:S(2)}) async-start(bf16[8,2,128,256]{3,2,1,0:T(8,128)(2,1)} %get-tuple-element.19), calls=%async_computation.2 | async-start | bytes 2097152 | tf_op jit(solution)/shard_map/all_to_all | solution.py:251
  106.7 23.4 %collective-permute-start.10 = (bf16[2,2,128,256]{3,2,1,0:T(8,128)(2,1)S(1)}, bf16[2,2,128,256]{3,2,1,0:T(8,128)(2,1)S(1)}, u32[]{:S(2)}, u32[]{:S(2)}) collective-permute-start(bf16[2,2,128,256]{3,2,1,0:T(8,128)(2,1)S(1)} %get-tuple-element.23.refs_2_), channel_id=1, source_target_pairs={{0,16},{8,24},{16,0},{24,8},{1,17},{9,25},{17,1},{25,9},{2,18},{10... | collective-permute-start | bytes 786440 | tf_op jit(solution)/shard_map/ppermute | solution.py:256
  111.7 18.4 %collective-permute-start.11 = (bf16[2,2,128,256]{3,2,1,0:T(8,128)(2,1)S(1)}, bf16[2,2,128,256]{3,2,1,0:T(8,128)(2,1)S(1)}, u32[]{:S(2)}, u32[]{:S(2)}) collective-permute-start(bf16[2,2,128,256]{3,2,1,0:T(8,128)(2,1)S(1)} %get-tuple-element.24.refs_3_), channel_id=1, source_target_pairs={{0,24},{8,16},{16,8},{24,0},{1,25},{9,17},{17,9},{25,1},{2,26},{10... | collective-permute-start | bytes 786440 | tf_op jit(solution)/shard_map/ppermute | solution.py:256
  113.1 18.2 %collective-permute-start.9 = (bf16[2,2,128,256]{3,2,1,0:T(8,128)(2,1)S(1)}, bf16[2,2,128,256]{3,2,1,0:T(8,128)(2,1)S(1)}, u32[]{:S(2)}, u32[]{:S(2)}) collective-permute-start(bf16[2,2,128,256]{3,2,1,0:T(8,128)(2,1)S(1)} %get-tuple-element.22.refs_1_), channel_id=1, source_target_pairs={{0,8},{8,0},{16,24},{24,16},{1,9},{9,1},{17,25},{25,17},{2,10},{10... | collective-permute-start | bytes 786440 | tf_op jit(solution)/shard_map/ppermute | solution.py:256
  133.7 5.1 %copy-start.3 = (bf16[4,3,64,512]{3,2,1,0:T(8,128)(2,1)S(1)}, bf16[4,3,64,512]{3,2,1,0:T(8,128)(2,1)}, u32[]{:S(2)}) copy-start(bf16[4,3,64,512]{3,2,1,0:T(8,128)(2,1)} %copy-done.2) | copy-start | bytes 2359300
  133.7 20.4 %all-to-all-start.3 = ((bf16[8,2,128,256]{3,2,1,0:T(8,128)(2,1)}), bf16[8,2,128,256]{3,2,1,0:T(8,128)(2,1)S(1)}, u32[]{:S(2)}, u32[]{:S(2)}) async-start(bf16[8,2,128,256]{3,2,1,0:T(8,128)(2,1)} %shard_map.78), calls=%async_computation.3 | async-start | bytes 2097152 | tf_op jit(solution)/shard_map/all_to_all | solution.py:251

commit v2 on v1

--- a/solution.py
+++ b/solution.py
@@ -30,11 +30,8 @@
 
     def mirror_within(self, x):
         e, g = self.edge, self.rows
-        parts = []
-        for c in range(2):
-            tile = jnp.concatenate([x[c * g:(c + 1) * g, :e], x[c * g:(c + 1) * g, e:]], axis=0).T
-            parts.append(jnp.concatenate([tile[:g], tile[g:]], axis=1))
-        return jnp.concatenate(parts, axis=0)
+        tile = jnp.concatenate([x[:, :e], x[:, e:]], axis=0).T
+        return jnp.concatenate([tile[:g], tile[g:]], axis=1)
 
     def mirror_across(self, x):
         return jnp.concatenate([x[:, self.edge:], x[:, :self.edge]], axis=1)
@@ -53,40 +50,37 @@
     )(*operands)
 
 
-def pack_pair(tiles, source, out, pair, mirrored=False):
+def pack_pair(tiles, source, outs, pair, mirrored=False):
     e, g = tiles.edge, tiles.rows
     straight, turned = (slice(e, None), slice(0, e)) if mirrored else (slice(0, e), slice(e, None))
     for d, (a, b) in enumerate(tiles.above):
-        out[d, pair, :, straight] = source[tiles.span(a), tiles.span(b)].astype(NARROW)
-        out[d, pair, :, turned] = source[tiles.span(b), tiles.span(a)].astype(WIDE).T.astype(NARROW)
+        tile = source[tiles.span(a), tiles.span(b)].astype(NARROW)
+        other = source[tiles.span(b), tiles.span(a)].astype(WIDE).T.astype(NARROW)
+        for c, out in enumerate(outs):
+            out[d, pair, :, straight] = tile[c * g:(c + 1) * g]
+            out[d, pair, :, turned] = other[c * g:(c + 1) * g]
     for d, c, k in tiles.diagonal:
         tile = source[tiles.span(k), tiles.span(k)]
         tile = tile.astype(WIDE).T.astype(NARROW) if mirrored else tile.astype(NARROW)
-        out[d, pair, c * g:(c + 1) * g, :e] = tile[:g]
-        out[d, pair, c * g:(c + 1) * g, e:] = tile[g:]
-
-
-def unpack_pair(tiles, blocks, pair, put):
+        outs[c][d, pair, :, :e] = tile[:g]
+        outs[c][d, pair, :, e:] = tile[g:]
+
+
+def unpack_pair(tiles, blocks, c, pair, put):
     e, g = tiles.edge, tiles.rows
     for d, (a, b) in enumerate(tiles.above):
-        put(a, b, blocks[d, pair, :, :e].astype(WIDE))
-        put(b, a, blocks[d, pair, :, e:].astype(WIDE).T)
-    for d, c, k in tiles.diagonal:
-        upper = blocks[d, pair, c * g:(c + 1) * g, :e]
-        lower = blocks[d, pair, c * g:(c + 1) * g, e:]
-        put(k, k, jnp.concatenate([upper, lower], axis=0).astype(WIDE))
-
-
-def pack_kernel(tiles, source, out):
+        strip = slice(a * e + c * g, a * e + (c + 1) * g)
+        put(strip, tiles.span(b), blocks[d, pair, :, :e].astype(WIDE))
+        put(tiles.span(b), strip, blocks[d, pair, :, e:].astype(WIDE).T)
+    for d, chunk, k in tiles.diagonal:
+        if chunk == c:
+            put(slice(k * e, k * e + g), tiles.span(k), blocks[d, pair, :, :e].astype(WIDE))
+            put(slice(k * e + g, (k + 1) * e), tiles.span(k), blocks[d, pair, :, e:].astype(WIDE))
+
+
+def pack_kernel(tiles, source, *outs):
     for pair in range(source.shape[0]):
-        pack_pair(tiles, source.at[pair], out, pair, mirrored=True)
-
-
-def pack(tiles, devices, amplitudes):
-    count = amplitudes.shape[0]
-    out = jax.ShapeDtypeStruct((devices, count, tiles.edge, 2 * tiles.edge), NARROW)
-    return call(functools.partial(pack_kernel, tiles), out, [], amplitudes.size, amplitudes.size * 6,
-                amplitudes, specs=[VMEM])
+        pack_pair(tiles, source.at[pair], outs, pair, mirrored=True)
 
 
 def assemble(place, order, pieces, whole):
@@ -112,21 +106,24 @@
     lax.fori_loop(0, whole.shape[0], one, 0)
 
 
-def first_ladder_kernel(tiles, order, place, source, low, high, out, whole, total):
+def first_ladder_kernel(tiles, order, place, source, low, high, *refs):
+    outs, (whole, total) = refs[:2], refs[2:]
     assemble(place, order, (low, high), whole)
     for pair in range(source.shape[0]):
         ladder_pair(source[pair].astype(NARROW), whole, total)
-        pack_pair(tiles, total, out, pair)
-
-
-def second_ladder_kernel(tiles, order, count, place, occ, source, blocks, row, column, low, high, out,
+        pack_pair(tiles, total, outs, pair)
+
+
+def second_ladder_kernel(tiles, order, place, occ, source, upper, lower, row, column, low, high, out,
                          whole, total, matrix):
     assemble(place, order, (low, high), whole)
+    count = source.shape[0]
     for pair in range(count):
-        def put(a, b, tile):
-            matrix[tiles.span(a), tiles.span(b)] = tile.astype(NARROW)
-
-        unpack_pair(tiles, blocks, pair, put)
+        def put(rows, columns, values):
+            matrix[rows, columns] = values.astype(NARROW)
+
+        unpack_pair(tiles, upper, 0, pair, put)
+        unpack_pair(tiles, lower, 1, pair, put)
         ladder_pair(matrix[...], whole, total)
         base = occ[place[0] * count + pair] + occ[place[1]]
 
@@ -141,16 +138,16 @@
         lax.fori_loop(0, total.shape[0] // 16, finish, 0)
 
 
-def add_kernel(tiles, source, blocks, out):
+def add_kernel(tiles, source, upper, lower, out):
     for pair in range(source.shape[0]):
-        def put(a, b, tile):
-            here = (pair, tiles.span(a), tiles.span(b))
-            out[here] = source[here] + tile
-
-        unpack_pair(tiles, blocks, pair, put)
-
-
-def mix(place, fock, first, load, store, rows, width):
+        def put(rows, columns, values):
+            out[pair, rows, columns] = source[pair, rows, columns] + values
+
+        unpack_pair(tiles, upper, 0, pair, put)
+        unpack_pair(tiles, lower, 1, pair, put)
+
+
+def mix(place, fock, first, load, store, rows):
     total = fock.shape[0]
     strips = rows // 16
 
@@ -180,7 +177,7 @@
     def store(s, u, w, column, at, result):
         out[s][u, w, at, :] = (ladder[column, u, at, :].astype(WIDE) + result).astype(NARROW)
 
-    mix(place, fock, first, load, store, tiles.edge, 2 * tiles.edge)
+    mix(place, fock, first, load, store, tiles.rows)
 
 
 def with_mirror(tiles, place, x, finish):
@@ -225,7 +222,7 @@
     def store(s, u, w, column, at, result):
         out[s][u, w, at, :] = result.astype(NARROW)
 
-    mix(place, fock, first, load, store, tiles.edge, 2 * tiles.edge)
+    mix(place, fock, first, load, store, tiles.rows)
 
 
 def rest_kernel(tiles, groups, first, place, occ, sums, rest, *refs):
@@ -257,10 +254,16 @@
     ]
 
 
-def gather_vectors(vectors, devices):
+def tie(x, *others):
+    return lax.optimization_barrier((x, *others))[0]
+
+
+def gather_vectors(vectors, devices, late):
     held, order = vectors[None], [0]
     step = devices // 2
     while True:
+        if step == 1:
+            held = tie(held, late)
         other = lax.ppermute(held, "occj", [(k, k ^ step) for k in range(devices)])
         order = order + [k ^ step for k in order]
         if step == 1:
@@ -276,12 +279,13 @@
     second = jnp.array([b for _, b in tiles.above] + list(range(1, tiles.n, 2)), jnp.int32)[q]
     a = lax.dynamic_slice_in_dim(vir_energy, first * e, e)
     b = lax.dynamic_slice_in_dim(vir_energy, second * e, e)
-    pair = a[:, None] + b[None, :]
-    across = jnp.concatenate([pair, pair], axis=1)
-    halves = [
-        jnp.concatenate([t[:g, None] + t[None, :], t[g:, None] + t[None, :]], axis=1) for t in (a, b)
-    ]
-    return jnp.where(q < n_above, across, jnp.concatenate(halves, axis=0))
+    sums = []
+    for c, own in enumerate((a, b)):
+        pair = a[c * g:(c + 1) * g, None] + b[None, :]
+        across = jnp.concatenate([pair, pair], axis=1)
+        within = jnp.concatenate([own[:g, None] + own[None, :], own[g:, None] + own[None, :]], axis=1)
+        sums.append(jnp.where(q < n_above, across, within))
+    return sums
 
 
 def local(groups, devices, amplitudes, vectors, occupied_fock_block, occ_energy, vir_energy):
@@ -289,58 +293,67 @@
     assert second == 1 and groups * first == devices
     assert groups & (groups - 1) == 0 and devices & (devices - 1) == 0
     tiles = Tiles(devices, virtual)
-    edge = tiles.edge
+    block = (tiles.rows, 2 * tiles.edge)
     current = amplitudes.reshape(first, virtual, virtual)
     count = current.size
     fock = occupied_fock_block.astype(WIDE)
     p, q = lax.axis_index("occi"), lax.axis_index("occj")
     place = jnp.stack([p, q]).astype(jnp.int32)
-    part = jax.ShapeDtypeStruct((first, first, edge, 2 * edge), NARROW)
-    packed = jax.ShapeDtypeStruct((devices, first, edge, 2 * edge), NARROW)
-    vector_rows = virtual // devices
-
-    low, high, order = gather_vectors(vectors, devices)
-    held = exchange(pack(tiles, devices, current)).reshape(groups, first, first, edge, 2 * edge)
-    mirror = across_first([held[p ^ s] for s in range(groups)], groups)
+    part = jax.ShapeDtypeStruct((first, first, *block), NARROW)
+    packed = jax.ShapeDtypeStruct((devices, first, *block), NARROW)
+    whole = pltpu.VMEM((vectors.shape[0], virtual, virtual), NARROW)
+    square = pltpu.VMEM((virtual, virtual), WIDE)
+    chunks = range(2)
+
+    started = call(functools.partial(pack_kernel, tiles), [packed] * 2, [], count, 6 * count,
+                   current, specs=[VMEM])
+    held = [exchange(x).reshape(groups, first, first, *block) for x in started]
+    mirror = [across_first([x[p ^ s] for s in range(groups)], groups) for x in held]
+
+    low, high, order = gather_vectors(tie(vectors, *started), devices, held[0])
+    ladder_flops = first * vectors.shape[0] * 4 * virtual**3
+    ladder = [exchange(x) for x in call(
+        functools.partial(first_ladder_kernel, tiles, order), [packed] * 2, [whole, square],
+        ladder_flops, 8 * count, place, current, low, high, specs=[SMEM] + [VMEM] * 3,
+    )]
     sums = virtual_sums(tiles, vir_energy, q)
 
-    ladder_flops = first * vectors.shape[0] * 4 * virtual**3
-    ladder = exchange(call(
-        functools.partial(first_ladder_kernel, tiles, order), packed,
-        [pltpu.VMEM((vectors.shape[0], virtual, virtual), NARROW), pltpu.VMEM((virtual, virtual), WIDE)],
-        ladder_flops, 8 * count, place, current, low, high, specs=[SMEM, VMEM, VMEM, VMEM],
-    ))
-    half = call(
-        functools.partial(half_kernel, tiles, groups, first), [part] * groups, [],
-        2 * devices * count, 6 * count, place, fock, ladder, *mirror, specs=[SMEM] * 2 + [VMEM] * (groups + 1),
+    sent, rest, mixed = [], [], []
+    for c in chunks:
+        half = call(
+            functools.partial(half_kernel, tiles, groups, first), [part] * groups, [],
+            devices * count, 3 * count, place, fock, ladder[c], *mirror[c],
+            specs=[SMEM] * 2 + [VMEM] * (groups + 1),
+        )
+        other = across_first(half, groups)
+        sent_one, rest_one, *mixed_one = call(
+            functools.partial(update_kernel, tiles, groups, first),
+            [packed, jax.ShapeDtypeStruct((first, devices, *block), NARROW)] + [part] * groups,
+            [pltpu.VMEM((first, devices, *block), WIDE)],
+            devices * count, 5 * count, place, fock, occ_energy, sums[c], *half, *other,
+            specs=[SMEM] * 3 + [VMEM] * (2 * groups + 1),
+        )
+        sent.append(exchange(sent_one))
+        rest.append(rest_one)
+        mixed.append(mixed_one)
+
+    base = call(
+        functools.partial(second_ladder_kernel, tiles, order), jax.ShapeDtypeStruct(current.shape, WIDE),
+        [whole, square, pltpu.VMEM((virtual, virtual), NARROW)],
+        ladder_flops, 12 * count, place, occ_energy, current, *sent,
+        jnp.broadcast_to(vir_energy[:, None], (virtual, 128)), vir_energy[None, :], low, high,
+        specs=[SMEM] * 2 + [VMEM] * 7,
     )
-    other = across_first(half, groups)
-    sent, rest, *mixed = call(
-        functools.partial(update_kernel, tiles, groups, first),
-        [packed, jax.ShapeDtypeStruct((first, devices, edge, 2 * edge), NARROW)] + [part] * groups,
-        [pltpu.VMEM((first, devices, edge, 2 * edge), WIDE)],
-        2 * devices * count, 10 * count, place, fock, occ_energy, sums, *half, *other,
-        specs=[SMEM] * 3 + [VMEM] * (2 * groups + 1),
-    )
-    other = across_first(mixed, groups)
-    back = exchange(sent)
-    base = call(
-        functools.partial(second_ladder_kernel, tiles, order, first),
-        jax.ShapeDtypeStruct(current.shape, WIDE),
-        [pltpu.VMEM((vectors.shape[0], virtual, virtual), NARROW), pltpu.VMEM((virtual, virtual), WIDE),
-         pltpu.VMEM((virtual, virtual), NARROW)],
-        ladder_flops, 12 * count, place, occ_energy, current, back,
-        jnp.broadcast_to(vir_energy[:, None], (virtual, 128)), vir_energy[None, :], low, high,
-        specs=[SMEM] * 2 + [VMEM] * 6,
-    )
-    rest = exchange(call(
-        functools.partial(rest_kernel, tiles, groups, first), packed, [],
-        4 * count, 8 * count, place, occ_energy, sums, rest, *mixed, *other,
-        specs=[SMEM] * 2 + [VMEM] * (2 * groups + 2),
-    ))
+    last = [
+        exchange(call(
+            functools.partial(rest_kernel, tiles, groups, first), packed, [],
+            2 * count, 4 * count, place, occ_energy, sums[c], rest[c], *mixed[c],
+            *across_first(mixed[c], groups), specs=[SMEM] * 2 + [VMEM] * (2 * groups + 2),
+        )) for c in chunks
+    ]
     done = call(
         functools.partial(add_kernel, tiles), jax.ShapeDtypeStruct(current.shape, WIDE), [],
-        count, 10 * count, base, rest, specs=[VMEM, VMEM], aliases={0: 0},
+        count, 10 * count, base, *last, specs=[VMEM] * 3, aliases={0: 0},
     )
     return done.reshape(amplitudes.shape)
 

time: 160 us -> 197 us (1.23)
  starting transfers between devices: 40.7 us -> 71.3 us
  local copies, waits for them, and re-layouts: 1.78 us -> 9.92 us
  Pallas kernels: 36.2 us -> 40 us
  waiting for transfers between devices: 74.8 us -> 71.5 us
    all_to_all x4 -> x8, starting transfers between devices: 17.2 us -> 34.9 us  [exchange(): lax.all_to_all(blocks, 'occj', split_axis=0, concat_axis=0, tiled=True)]
    ppermute x9 -> x18, starting transfers between devices: 18.6 us -> 31.6 us  [across_first(): lax.ppermute(parts[s], 'occi', [(k, k ^ s) for k in range(groups)])]
    unnamed x18 -> x34, local copies, waits for them, and re-layouts: 0.04 us -> 7.23 us
    ppermute x9 -> x18, waiting for transfers between devices: 55.4 us -> 51.2 us  [across_first(): lax.ppermute(parts[s], 'occi', [(k, k ^ s) for k in range(groups)])]
    pallas_call x7 -> x10, Pallas kernels: 36.2 us -> 40 us  [call(): pl.pallas_call(body, out_shape=outs, in_specs=specs, out_specs=jax.tree.m...]
    all_to_all x4 -> x8, waiting for transfers between devices: 5.77 us -> 8.54 us  [exchange(): lax.all_to_all(blocks, 'occj', split_axis=0, concat_axis=0, tiled=True)]
  transfers between devices with their start and end apart: 16 -> 29, of which waited for: 10 -> 18; matrix products, arithmetic and copies ran while one was open for 1% -> 2% of each run, Pallas kernels for 16% -> 18%
where the time goes in v2:
time: 197 us; the launch traced here: 195 us
  waiting for transfers between devices  71.5 us (36%)
  starting transfers between devices  71.3 us (36%)
  Pallas kernels  40 us (20%)
  local copies, waits for them, and re-layouts  9.92 us (5%)
    ppermute x18, waiting for transfers between devices, across_first(): lax.ppermute(parts[s], 'occi', [(k, k ^ s) for k in range(groups)])  51.2 us
    pallas_call x10, Pallas kernels, call(): pl.pallas_call(body, out_shape=outs, in_specs=specs, out_specs=jax.tree.m...  40 us
    all_to_all x8, starting transfers between devices, exchange(): lax.all_to_all(blocks, 'occj', split_axis=0, concat_axis=0, tiled=True)  34.9 us
    ppermute x18, starting transfers between devices, across_first(): lax.ppermute(parts[s], 'occi', [(k, k ^ s) for k in range(groups)])  31.6 us
    ppermute x3, waiting for transfers between devices, gather_vectors(): other = lax.ppermute(held, 'occj', [(k, k ^ step) for k in range(devices)])  11.7 us
    all_to_all x8, waiting for transfers between devices, exchange(): lax.all_to_all(blocks, 'occj', split_axis=0, concat_axis=0, tiled=True)  8.54 us
    unnamed x34, local copies, waits for them, and re-layouts  7.23 us
    ppermute x3, starting transfers between devices, gather_vectors(): other = lax.ppermute(held, 'occj', [(k, k ^ step) for k in range(devices)])  4.75 us
  transfers between devices with their start and end apart: 29, of which 18 were waited for; matrix products, arithmetic and copies ran while one was open for 2% of the time, Pallas kernels for 18%

profile of v2, /device:TPU:0, one launch (start us, length us, event | category | flops | bytes accessed | tf_op | source)
XLA Modules:
  0.0 195.1 jit_solution(8741156482846640066)
XLA Ops:
  0.0 1.6 copy-done
  1.6 1.2 shard_map.73
  2.8 3.0 %collective-permute-start = (bf16[1,3,64,512]{3,2,1,0:T(8,128)(2,1)S(1)}, bf16[1,3,64,512]{3,2,1,0:T(8,128)(2,1)S(1)}, u32[]{:S(2)}, u32[]{:S(2)}) collective-permute-start(bf16[1,3,64,512]{3,2,1,0:T(8,128)(2,1)S(1)} %bitcast.34), channel_id=1, source_target_pairs={{0,4},{1,5},{2,6},{3,7},{4,0},{5,1},{6,2},{7,3},{8,12},{9,13},{10,... | collective-permute-start | bytes 589832 | tf_op jit(solution)/shard_map/ppermute | solution.py:267
  5.8 4.9 %collective-permute-done = bf16[1,3,64,512]{3,2,1,0:T(8,128)(2,1)S(1)} collective-permute-done((bf16[1,3,64,512]{3,2,1,0:T(8,128)(2,1)S(1)}, bf16[1,3,64,512]{3,2,1,0:T(8,128)(2,1)S(1)}, u32[]{:S(2)}, u32[]{:S(2)}) %collective-permute-start) | collective-permute-done | bytes 196640 | tf_op jit(solution)/shard_map/ppermute | solution.py:267
  10.7 1.8 collective-permute-start.1
  12.5 3.5 %all-to-all-start = ((bf16[8,2,64,256]{3,2,1,0:T(8,128)(2,1)}), bf16[8,2,64,256]{3,2,1,0:T(8,128)(2,1)S(1)}, u32[]{:S(2)}, u32[]{:S(2)}) async-start(bf16[8,2,64,256]{3,2,1,0:T(8,128)(2,1)} %get-tuple-element.31), calls=%async_computation | async-start | bytes 1048576 | tf_op jit(solution)/shard_map/all_to_all | solution.py:248
  16.0 6.8 %collective-permute-done.1 = bf16[2,3,64,512]{3,2,1,0:T(8,128)(2,1)S(1)} collective-permute-done((bf16[2,3,64,512]{3,2,1,0:T(8,128)(2,1)S(1)}, bf16[2,3,64,512]{3,2,1,0:T(8,128)(2,1)S(1)}, u32[]{:S(2)}, u32[]{:S(2)}) %collective-permute-start.1) | collective-permute-done | bytes 393248 | tf_op jit(solution)/shard_map/ppermute | solution.py:267
  22.9 4.6 %all-to-all-done = bf16[8,2,64,256]{3,2,1,0:T(8,128)(2,1)S(1)} async-done(((bf16[8,2,64,256]{3,2,1,0:T(8,128)(2,1)}), bf16[8,2,64,256]{3,2,1,0:T(8,128)(2,1)S(1)}, u32[]{:S(2)}, u32[]{:S(2)}) %all-to-all-start) | async-done | bytes 524320 | tf_op jit(solution)/shard_map/all_to_all | solution.py:248
  27.6 0.8 copy-done.11
  28.4 3.5 %all-to-all-start.4 = ((bf16[8,2,64,256]{3,2,1,0:T(8,128)(2,1)}), bf16[8,2,64,256]{3,2,1,0:T(8,128)(2,1)S(1)}, u32[]{:S(2)}, u32[]{:S(2)}) async-start(bf16[8,2,64,256]{3,2,1,0:T(8,128)(2,1)} %get-tuple-element.32), calls=%async_computation.4 | async-start | bytes 1048576 | tf_op jit(solution)/shard_map/all_to_all | solution.py:248
  32.0 8.4 %shard_map.74 = (bf16[8,2,64,256]{3,2,1,0:T(8,128)(2,1)}, bf16[8,2,64,256]{3,2,1,0:T(8,128)(2,1)}) custom-call(s32[2]{0:T(128)S(1)} %pad_add_fusion.place, f32[2,512,512]{2,1,0:T(8,128)} %bitcast.28, bf16[4,3,64,512]{3,2,1,0:T(8,128)(2,1)S(1)} %pad_maximum_fusion.low, bf16[4,3,64,512]{3,2,1,0:T(8,128)(2,1)S(1)} %collective-permute-done.2.high), custom_call_target="tpu_custom_call" | custom-call | flops 3221225472 | bytes 4194304 | tf_op jit(solution)/shard_map/pallas_call | solution.py:41
  40.4 1.1 all-to-all-done.4
  41.6 3.6 %all-to-all-start.3 = ((bf16[8,2,64,256]{3,2,1,0:T(8,128)(2,1)}), bf16[8,2,64,256]{3,2,1,0:T(8,128)(2,1)S(1)}, u32[]{:S(2)}, u32[]{:S(2)}) async-start(bf16[8,2,64,256]{3,2,1,0:T(8,128)(2,1)} %get-tuple-element.41), calls=%async_computation.3 | async-start | bytes 1048576 | tf_op jit(solution)/shard_map/all_to_all | solution.py:248
  47.9 2.7 %collective-permute-start.10 = (bf16[2,2,64,256]{3,2,1,0:T(8,128)(2,1)S(1)}, bf16[2,2,64,256]{3,2,1,0:T(8,128)(2,1)S(1)}, u32[]{:S(2)}, u32[]{:S(2)}) collective-permute-start(bf16[2,2,64,256]{3,2,1,0:T(8,128)(2,1)S(1)} %get-tuple-element.58), channel_id=1, source_target_pairs={{0,16},{8,24},{16,0},{24,8},{1,17},{9,25},{17,1},{25,9},{2,18},{10... | collective-permute-start | bytes 393224 | tf_op jit(solution)/shard_map/ppermute | solution.py:253
  50.5 1.3 collective-permute-start.11
  52.1 2.8 %all-to-all-done.3.ladder = bf16[8,2,64,256]{3,2,1,0:T(8,128)(2,1)S(1)} async-done(((bf16[8,2,64,256]{3,2,1,0:T(8,128)(2,1)}), bf16[8,2,64,256]{3,2,1,0:T(8,128)(2,1)S(1)}, u32[]{:S(2)}, u32[]{:S(2)}) %all-to-all-start.3) | async-done | bytes 524320 | tf_op jit(solution)/shard_map/all_to_all | solution.py:248
  54.9 3.5 %all-to-all-start.1 = ((bf16[8,2,64,256]{3,2,1,0:T(8,128)(2,1)}), bf16[8,2,64,256]{3,2,1,0:T(8,128)(2,1)S(1)}, u32[]{:S(2)}, u32[]{:S(2)}) async-start(bf16[8,2,64,256]{3,2,1,0:T(8,128)(2,1)} %get-tuple-element.35), calls=%async_computation.1 | async-start | bytes 1048576 | tf_op jit(solution)/shard_map/all_to_all | solution.py:248
  58.4 2.4 %collective-permute-done.10.refs_2_ = bf16[2,2,64,256]{3,2,1,0:T(8,128)(2,1)S(1)} collective-permute-done((bf16[2,2,64,256]{3,2,1,0:T(8,128)(2,1)S(1)}, bf16[2,2,64,256]{3,2,1,0:T(8,128)(2,1)S(1)}, u32[]{:S(2)}, u32[]{:S(2)}) %collective-permute-start.10) | collective-permute-done | bytes 131104 | tf_op jit(solution)/shard_map/ppermute | solution.py:253
  60.8 0.8 collective-permute-done.9.refs_1_
  61.6 1.6 shard_map.77
  63.2 2.2 %collective-permute-start.12 = (bf16[2,2,64,256]{3,2,1,0:T(8,128)(2,1)S(1)}, bf16[2,2,64,256]{3,2,1,0:T(8,128)(2,1)S(1)}, u32[]{:S(2)}, u32[]{:S(2)}) collective-permute-start(bf16[2,2,64,256]{3,2,1,0:T(8,128)(2,1)S(1)} %get-tuple-element.43.refs_1_), channel_id=1, source_target_pairs={{0,8},{8,0},{16,24},{24,16},{1,9},{9,1},{17,25},{25,17},{2,10},{10... | collective-permute-start | bytes 393224 | tf_op jit(solution)/shard_map/ppermute | solution.py:253
  65.4 2.0 %collective-permute-start.13 = (bf16[2,2,64,256]{3,2,1,0:T(8,128)(2,1)S(1)}, bf16[2,2,64,256]{3,2,1,0:T(8,128)(2,1)S(1)}, u32[]{:S(2)}, u32[]{:S(2)}) collective-permute-start(bf16[2,2,64,256]{3,2,1,0:T(8,128)(2,1)S(1)} %get-tuple-element.44.refs_2_), channel_id=1, source_target_pairs={{0,16},{8,24},{16,0},{24,8},{1,17},{9,25},{17,1},{25,9},{2,18},{10... | collective-permute-start | bytes 393224 | tf_op jit(solution)/shard_map/ppermute | solution.py:253
  67.4 1.4 collective-permute-start.14
  68.8 0.7 broadcast_add_fusion.1
  69.5 2.1 %collective-permute-done.12.refs_5_ = bf16[2,2,64,256]{3,2,1,0:T(8,128)(2,1)S(1)} collective-permute-done((bf16[2,2,64,256]{3,2,1,0:T(8,128)(2,1)S(1)}, bf16[2,2,64,256]{3,2,1,0:T(8,128)(2,1)S(1)}, u32[]{:S(2)}, u32[]{:S(2)}) %collective-permute-start.12) | collective-permute-done | bytes 131104 | tf_op jit(solution)/shard_map/ppermute | solution.py:253
  71.6 1.5 collective-permute-done.13.refs_6_
  73.1 4.9 %collective-permute-done.14.refs_7_ = bf16[2,2,64,256]{3,2,1,0:T(8,128)(2,1)S(1)} collective-permute-done((bf16[2,2,64,256]{3,2,1,0:T(8,128)(2,1)S(1)}, bf16[2,2,64,256]{3,2,1,0:T(8,128)(2,1)S(1)}, u32[]{:S(2)}, u32[]{:S(2)}) %collective-permute-start.14) | collective-permute-done | bytes 131104 | tf_op jit(solution)/shard_map/ppermute | solution.py:253
  78.0 3.0 %shard_map.78 = (bf16[8,2,64,256]{3,2,1,0:T(8,128)(2,1)}, bf16[2,8,64,256]{3,2,1,0:T(8,128)(2,1)S(1)}, bf16[2,2,64,256]{3,2,1,0:T(8,128)(2,1)S(1)}, bf16[2,2,64,...) custom-call(s32[2]{0:T(128)S(1)} %pad_add_fusion.place, ...), custom_call_target="tpu_custom_call" | custom-call | flops 4194304 | bytes 2621440 | tf_op jit(solution)/shard_map/pallas_call | solution.py:41
  80.9 5.0 %all-to-all-start.5 = ((bf16[8,2,64,256]{3,2,1,0:T(8,128)(2,1)}), bf16[8,2,64,256]{3,2,1,0:T(8,128)(2,1)S(1)}, u32[]{:S(2)}, u32[]{:S(2)}) async-start(bf16[8,2,64,256]{3,2,1,0:T(8,128)(2,1)} %get-tuple-element.46), calls=%async_computation.5 | async-start | bytes 1048576 | tf_op jit(solution)/shard_map/all_to_all | solution.py:248
  86.0 1.1 dynamic-slice_bitcast_fusion.4
  87.1 2.6 %collective-permute-start.3 = (bf16[2,2,64,256]{3,2,1,0:T(8,128)(2,1)S(1)}, bf16[2,2,64,256]{3,2,1,0:T(8,128)(2,1)S(1)}, u32[]{:S(2)}, u32[]{:S(2)}) collective-permute-start(bf16[2,2,64,256]{3,2,1,0:T(8,128)(2,1)S(1)} %get-tuple-element.63), channel_id=1, source_target_pairs={{0,8},{8,0},{16,24},{24,16},{1,9},{9,1},{17,25},{25,17},{2,10},{10... | collective-permute-start | bytes 393224 | tf_op jit(solution)/shard_map/ppermute | solution.py:253
  89.7 1.8 collective-permute-start.4
  91.6 1.4 collective-permute-start.5
  93.0 3.4 %collective-permute-done.3.refs_1_ = bf16[2,2,64,256]{3,2,1,0:T(8,128)(2,1)S(1)} collective-permute-done((bf16[2,2,64,256]{3,2,1,0:T(8,128)(2,1)S(1)}, bf16[2,2,64,256]{3,2,1,0:T(8,128)(2,1)S(1)}, u32[]{:S(2)}, u32[]{:S(2)}) %collective-permute-start.3) | collective-permute-done | bytes 131104 | tf_op jit(solution)/shard_map/ppermute | solution.py:253
  96.4 6.2 %collective-permute-done.4.refs_2_ = bf16[2,2,64,256]{3,2,1,0:T(8,128)(2,1)S(1)} collective-permute-done((bf16[2,2,64,256]{3,2,1,0:T(8,128)(2,1)S(1)}, bf16[2,2,64,256]{3,2,1,0:T(8,128)(2,1)S(1)}, u32[]{:S(2)}, u32[]{:S(2)}) %collective-permute-start.4) | collective-permute-done | bytes 131104 | tf_op jit(solution)/shard_map/ppermute | solution.py:253
  102.6 1.6 shard_map.75
  104.2 2.7 %collective-permute-start.6 = (bf16[2,2,64,256]{3,2,1,0:T(8,128)(2,1)S(1)}, bf16[2,2,64,256]{3,2,1,0:T(8,128)(2,1)S(1)}, u32[]{:S(2)}, u32[]{:S(2)}) collective-permute-start(bf16[2,2,64,256]{3,2,1,0:T(8,128)(2,1)S(1)} %get-tuple-element.37.refs_1_), channel_id=1, source_target_pairs={{0,8},{8,0},{16,24},{24,16},{1,9},{9,1},{17,25},{25,17},{2,10},{10... | collective-permute-start | bytes 393224 | tf_op jit(solution)/shard_map/ppermute | solution.py:253
  107.0 1.8 collective-permute-start.7
  108.8 1.4 collective-permute-start.8
  110.2 1.4 collective-permute-done.6.refs_5_
  111.5 8.0 %collective-permute-done.7.refs_6_ = bf16[2,2,64,256]{3,2,1,0:T(8,128)(2,1)S(1)} collective-permute-done((bf16[2,2,64,256]{3,2,1,0:T(8,128)(2,1)S(1)}, bf16[2,2,64,256]{3,2,1,0:T(8,128)(2,1)S(1)}, u32[]{:S(2)}, u32[]{:S(2)}) %collective-permute-start.7) | collective-permute-done | bytes 131104 | tf_op jit(solution)/shard_map/ppermute | solution.py:253
  119.5 3.0 %shard_map.76 = (bf16[8,2,64,256]{3,2,1,0:T(8,128)(2,1)}, bf16[2,8,64,256]{3,2,1,0:T(8,128)(2,1)S(1)}, bf16[2,2,64,256]{3,2,1,0:T(8,128)(2,1)S(1)}, bf16[2,2,64,...) custom-call(s32[2]{0:T(128)S(1)} %pad_add_fusion.place, ...), custom_call_target="tpu_custom_call" | custom-call | flops 4194304 | bytes 2621440 | tf_op jit(solution)/shard_map/pallas_call | solution.py:41
  122.5 0.8 copy-done.1
  123.3 5.1 %all-to-all-start.2 = ((bf16[8,2,64,256]{3,2,1,0:T(8,128)(2,1)}), bf16[8,2,64,256]{3,2,1,0:T(8,128)(2,1)S(1)}, u32[]{:S(2)}, u32[]{:S(2)}) async-start(bf16[8,2,64,256]{3,2,1,0:T(8,128)(2,1)} %get-tuple-element.40), calls=%async_computation.2 | async-start | bytes 1048576 | tf_op jit(solution)/shard_map/all_to_all | solution.py:248
  128.4 2.2 %collective-permute-start.18 = (bf16[2,2,64,256]{3,2,1,0:T(8,128)(2,1)S(1)}, bf16[2,2,64,256]{3,2,1,0:T(8,128)(2,1)S(1)}, u32[]{:S(2)}, u32[]{:S(2)}) collective-permute-start(bf16[2,2,64,256]{3,2,1,0:T(8,128)(2,1)S(1)} %get-tuple-element.54.refs_1_), channel_id=1, source_target_pairs={{0,8},{8,0},{16,24},{24,16},{1,9},{9,1},{17,25},{25,17},{2,10},{10... | collective-permute-start | bytes 393224 | tf_op jit(solution)/shard_map/ppermute | solution.py:253
  130.6 1.3 collective-permute-start.19
  132.0 1.4 collective-permute-start.20
  133.3 3.6 %collective-permute-done.18.refs_5_ = bf16[2,2,64,256]{3,2,1,0:T(8,128)(2,1)S(1)} collective-permute-done((bf16[2,2,64,256]{3,2,1,0:T(8,128)(2,1)S(1)}, bf16[2,2,64,256]{3,2,1,0:T(8,128)(2,1)S(1)}, u32[]{:S(2)}, u32[]{:S(2)}) %collective-permute-start.18) | collective-permute-done | bytes 131104 | tf_op jit(solution)/shard_map/ppermute | solution.py:253
  137.0 6.7 %collective-permute-done.19.refs_6_ = bf16[2,2,64,256]{3,2,1,0:T(8,128)(2,1)S(1)} collective-permute-done((bf16[2,2,64,256]{3,2,1,0:T(8,128)(2,1)}, bf16[2,2,64,256]{3,2,1,0:T(8,128)(2,1)S(1)}, u32[]{:S(2)}, u32[]{:S(2)}) %collective-permute-start.19) | collective-permute-done | bytes 131104 | tf_op jit(solution)/shard_map/ppermute | solution.py:253
  143.7 0.9 copy-done.4
  144.6 0.9 copy-done.6
  145.5 2.0 %shard_map.81 = bf16[8,2,64,256]{3,2,1,0:T(8,128)(2,1)} custom-call(s32[2]{0:T(128)S(1)} %pad_add_fusion.place, f32[8]{0:T(128)S(1)} %copy-done.7, f32[64,256]{1,0:T(8,128)S(1)} %maximum_select_fusion.1.sums, bf16[2,8,64,256]{3,2,1,0:T(8,128)(2,1)S(1)} %get-tuple-element.52.rest, bf16[2,2,64,256]{3,2,1,0:T(8,128)(2,1)S(1)} %get-tuple-element.53.refs_0_.refs_4_, ...), custom_call_target="tpu_custom_call" | custom-call | flops 1048576 | bytes 2097152 | tf_op jit(solution)/shard_map/pallas_call | solution.py:41
  147.5 5.4 %all-to-all-start.7 = ((bf16[8,2,64,256]{3,2,1,0:T(8,128)(2,1)}), bf16[8,2,64,256]{3,2,1,0:T(8,128)(2,1)S(1)}, u32[]{:S(2)}, u32[]{:S(2)}) async-start(bf16[8,2,64,256]{3,2,1,0:T(8,128)(2,1)} %shard_map.81), calls=%async_computation.7 | async-start | bytes 1048576 | tf_op jit(solution)/shard_map/all_to_all | solution.py:248
  152.8 2.3 %collective-permute-start.15 = (bf16[2,2,64,256]{3,2,1,0:T(8,128)(2,1)S(1)}, bf16[2,2,64,256]{3,2,1,0:T(8,128)(2,1)S(1)}, u32[]{:S(2)}, u32[]{:S(2)}) collective-permute-start(bf16[2,2,64,256]{3,2,1,0:T(8,128)(2,1)S(1)} %get-tuple-element.49.refs_1_), channel_id=1, source_target_pairs={{0,8},{8,0},{16,24},{24,16},{1,9},{9,1},{17,25},{25,17},{2,10},{10... | collective-permute-start | bytes 393224 | tf_op jit(solution)/shard_map/ppermute | solution.py:253
  155.2 1.3 collective-permute-start.16
  156.4 1.4 collective-permute-start.17
  157.8 3.8 %collective-permute-done.15.refs_5_ = bf16[2,2,64,256]{3,2,1,0:T(8,128)(2,1)S(1)} collective-permute-done((bf16[2,2,64,256]{3,2,1,0:T(8,128)(2,1)S(1)}, bf16[2,2,64,256]{3,2,1,0:T(8,128)(2,1)S(1)}, u32[]{:S(2)}, u32[]{:S(2)}) %collective-permute-start.15) | collective-permute-done | bytes 131104 | tf_op jit(solution)/shard_map/ppermute | solution.py:253
  161.7 6.4 %collective-permute-done.16.refs_6_ = bf16[2,2,64,256]{3,2,1,0:T(8,128)(2,1)S(1)} collective-permute-done((bf16[2,2,64,256]{3,2,1,0:T(8,128)(2,1)S(1)}, bf16[2,2,64,256]{3,2,1,0:T(8,128)(2,1)S(1)}, u32[]{:S(2)}, u32[]{:S(2)}) %collective-permute-start.16) | collective-permute-done | bytes 131104 | tf_op jit(solution)/shard_map/ppermute | solution.py:253
  168.1 1.0 copy-done.2
  169.1 2.0 %shard_map.80 = bf16[8,2,64,256]{3,2,1,0:T(8,128)(2,1)} custom-call(s32[2]{0:T(128)S(1)} %pad_add_fusion.place, f32[8]{0:T(128)S(1)} %copy-done.7, f32[64,256]{1,0:T(8,128)S(1)} %maximum_select_fusion.sums, bf16[2,8,64,256]{3,2,1,0:T(8,128)(2,1)S(1)} %copy-done.2, bf16[2,2,64,256]{3,2,1,0:T(8,128)(2,1)S(1)} %get-tuple-element.48.refs_0_.refs_4_, ...), custom_call_target="tpu_custom_call" | custom-call | flops 1048576 | bytes 2097152 | tf_op jit(solution)/shard_map/pallas_call | solution.py:41
  171.1 5.4 %all-to-all-start.6 = ((bf16[8,2,64,256]{3,2,1,0:T(8,128)(2,1)}), bf16[8,2,64,256]{3,2,1,0:T(8,128)(2,1)S(1)}, u32[]{:S(2)}, u32[]{:S(2)}) async-start(bf16[8,2,64,256]{3,2,1,0:T(8,128)(2,1)} %shard_map.80), calls=%async_computation.6 | async-start | bytes 1048576 | tf_op jit(solution)/shard_map/all_to_all | solution.py:248
  176.6 1.1 copy-done.10
  177.7 14.0 %shard_map.79.source = f32[2,512,512]{2,1,0:T(8,128)} custom-call(s32[2]{0:T(128)S(1)} %pad_add_fusion.place, f32[8]{0:T(128)S(1)} %copy-done.7, f32[2,512,512]{2,1,0:T(8,128)} %bitcast.29, bf16[8,2,64,256]{3,2,1,0:T(8,128)(2,1)S(1)} %all-to-all-done.2.upper, bf16[8,2,64,256]{3,2,1,0:T(8,128)(2,1)S(1)} %all-to-all-done.5.lower, ...), custom_call_target="tpu_custom_call" | custom-call | flops 3221225472 | bytes 6291456 | tf_op jit(solution)/shard_map/pallas_call | solution.py:41
  191.7 3.4 %shard_map.82 = f32[2,512,512]{2,1,0:T(8,128)} custom-call(f32[2,512,512]{2,1,0:T(8,128)} %shard_map.79.source, bf16[8,2,64,256]{3,2,1,0:T(8,128)(2,1)S(1)} %all-to-all-done.6.upper, bf16[8,2,64,256]{3,2,1,0:T(8,128)(2,1)S(1)} %all-to-all-done.7.lower), custom_call_target="tpu_custom_call", output_to_operand_aliasing={{}: (0, {})} | custom-call | flops 524288 | bytes 5242880 | tf_op jit(solution)/shard_map/pallas_call | solution.py:41
  (52 shorter events, 2.1 us)
Async XLA Ops:
  0.0 1.6 copy-start
  1.6 1.2 copy-start.12
  2.8 7.9 %collective-permute-start = (bf16[1,3,64,512]{3,2,1,0:T(8,128)(2,1)S(1)}, bf16[1,3,64,512]{3,2,1,0:T(8,128)(2,1)S(1)}, u32[]{:S(2)}, u32[]{:S(2)}) collective-permute-start(bf16[1,3,64,512]{3,2,1,0:T(8,128)(2,1)S(1)} %bitcast.34), channel_id=1, source_target_pairs={{0,4},{1,5},{2,6},{3,7},{4,0},{5,1},{6,2},{7,3},{8,12},{9,13},{10,... | collective-permute-start | bytes 589832 | tf_op jit(solution)/shard_map/ppermute | solution.py:267
  10.7 12.1 %collective-permute-start.1 = (bf16[2,3,64,512]{3,2,1,0:T(8,128)(2,1)S(1)}, bf16[2,3,64,512]{3,2,1,0:T(8,128)(2,1)S(1)}, u32[]{:S(2)}, u32[]{:S(2)}) collective-permute-start(bf16[2,3,64,512]{3,2,1,0:T(8,128)(2,1)S(1)} %pad_maximum_fusion.1), channel_id=1, source_target_pairs={{0,2},{1,3},{2,0},{3,1},{4,6},{5,7},{6,4},{7,5},{8,10},{9,11},{10,... | collective-permute-start | bytes 1179656 | tf_op jit(solution)/shard_map/ppermute | solution.py:267
  12.5 15.1 %all-to-all-start = ((bf16[8,2,64,256]{3,2,1,0:T(8,128)(2,1)}), bf16[8,2,64,256]{3,2,1,0:T(8,128)(2,1)S(1)}, u32[]{:S(2)}, u32[]{:S(2)}) async-start(bf16[8,2,64,256]{3,2,1,0:T(8,128)(2,1)} %get-tuple-element.31), calls=%async_computation | async-start | bytes 1048576 | tf_op jit(solution)/shard_map/all_to_all | solution.py:248
  27.6 0.8 copy-start.11
  28.4 3.6 %collective-permute-start.2 = (bf16[4,3,64,512]{3,2,1,0:T(8,128)(2,1)S(1)}, bf16[4,3,64,512]{3,2,1,0:T(8,128)(2,1)S(1)}, u32[]{:S(2)}, u32[]{:S(2)}) collective-permute-start(bf16[4,3,64,512]{3,2,1,0:T(8,128)(2,1)S(1)} %pad_maximum_fusion.low), channel_id=1, source_target_pairs={{0,1},{1,0},{2,3},{3,2},{4,5},{5,4},{6,7},{7,6},{8,9},{9,8},{10,11... | collective-permute-start | bytes 2359304 | tf_op jit(solution)/shard_map/ppermute | solution.py:267
  28.4 13.2 %all-to-all-start.4 = ((bf16[8,2,64,256]{3,2,1,0:T(8,128)(2,1)}), bf16[8,2,64,256]{3,2,1,0:T(8,128)(2,1)S(1)}, u32[]{:S(2)}, u32[]{:S(2)}) async-start(bf16[8,2,64,256]{3,2,1,0:T(8,128)(2,1)} %get-tuple-element.32), calls=%async_computation.4 | async-start | bytes 1048576 | tf_op jit(solution)/shard_map/all_to_all | solution.py:248
  32.0 13.2 %copy-start.16 = (s32[8]{0:T(128)S(1)}, s32[8]{0:T(128)}, u32[]{:S(2)}) copy-start(s32[8]{0:T(128)} %constant.33.clone) | copy-start | bytes 100
  32.0 14.4 %copy-start.15 = (s32[8]{0:T(128)S(1)}, s32[8]{0:T(128)}, u32[]{:S(2)}) copy-start(s32[8]{0:T(128)} %constant.32.clone) | copy-start | bytes 100
  32.0 15.7 %copy-start.14 = (bf16[8,8]{1,0:T(8,128)(2,1)S(1)}, bf16[8,8]{1,0:T(8,128)(2,1)}, u32[]{:S(2)}) copy-start(bf16[8,8]{1,0:T(8,128)(2,1)} %param.9) | copy-start | bytes 388
  32.0 15.8 %copy-start.8 = (f32[512]{0:T(512)S(1)}, f32[512]{0:T(512)}, u32[]{:S(2)}) copy-start(f32[512]{0:T(512)} %param.11) | copy-start | bytes 6148
  32.0 8.4 %copy-start.9 = (bf16[4,3,64,512]{3,2,1,0:T(8,128)(2,1)}, bf16[4,3,64,512]{3,2,1,0:T(8,128)(2,1)S(1)}, u32[]{:S(2)}) copy-start(bf16[4,3,64,512]{3,2,1,0:T(8,128)(2,1)S(1)} %collective-permute-done.2.high) | copy-start | bytes 2359300
  41.6 36.4 %copy-start.7 = (f32[8]{0:T(128)S(1)}, f32[8]{0:T(128)}, u32[]{:S(2)}) copy-start(f32[8]{0:T(128)} %occ.9) | copy-start | bytes 100
  41.6 13.3 %all-to-all-start.3 = ((bf16[8,2,64,256]{3,2,1,0:T(8,128)(2,1)}), bf16[8,2,64,256]{3,2,1,0:T(8,128)(2,1)S(1)}, u32[]{:S(2)}, u32[]{:S(2)}) async-start(bf16[8,2,64,256]{3,2,1,0:T(8,128)(2,1)} %get-tuple-element.41), calls=%async_computation.3 | async-start | bytes 1048576 | tf_op jit(solution)/shard_map/all_to_all | solution.py:248
  47.9 13.0 %collective-permute-start.10 = (bf16[2,2,64,256]{3,2,1,0:T(8,128)(2,1)S(1)}, bf16[2,2,64,256]{3,2,1,0:T(8,128)(2,1)S(1)}, u32[]{:S(2)}, u32[]{:S(2)}) collective-permute-start(bf16[2,2,64,256]{3,2,1,0:T(8,128)(2,1)S(1)} %get-tuple-element.58), channel_id=1, source_target_pairs={{0,16},{8,24},{16,0},{24,8},{1,17},{9,25},{17,1},{25,9},{2,18},{10... | collective-permute-start | bytes 393224 | tf_op jit(solution)/shard_map/ppermute | solution.py:253
  50.5 10.3 %collective-permute-start.11 = (bf16[2,2,64,256]{3,2,1,0:T(8,128)(2,1)S(1)}, bf16[2,2,64,256]{3,2,1,0:T(8,128)(2,1)S(1)}, u32[]{:S(2)}, u32[]{:S(2)}) collective-permute-start(bf16[2,2,64,256]{3,2,1,0:T(8,128)(2,1)S(1)} %get-tuple-element.57), channel_id=1, source_target_pairs={{0,24},{8,16},{16,8},{24,0},{1,25},{9,17},{17,9},{25,1},{2,26},{10... | collective-permute-start | bytes 393224 | tf_op jit(solution)/shard_map/ppermute | solution.py:253
  51.9 9.7 %collective-permute-start.9 = (bf16[2,2,64,256]{3,2,1,0:T(8,128)(2,1)S(1)}, bf16[2,2,64,256]{3,2,1,0:T(8,128)(2,1)S(1)}, u32[]{:S(2)}, u32[]{:S(2)}) collective-permute-start(bf16[2,2,64,256]{3,2,1,0:T(8,128)(2,1)S(1)} %get-tuple-element.59), channel_id=1, source_target_pairs={{0,8},{8,0},{16,24},{24,16},{1,9},{9,1},{17,25},{25,17},{2,10},{10... | collective-permute-start | bytes 393224 | tf_op jit(solution)/shard_map/ppermute | solution.py:253
  54.9 26.0 %all-to-all-start.1 = ((bf16[8,2,64,256]{3,2,1,0:T(8,128)(2,1)}), bf16[8,2,64,256]{3,2,1,0:T(8,128)(2,1)S(1)}, u32[]{:S(2)}, u32[]{:S(2)}) async-start(bf16[8,2,64,256]{3,2,1,0:T(8,128)(2,1)} %get-tuple-element.35), calls=%async_computation.1 | async-start | bytes 1048576 | tf_op jit(solution)/shard_map/all_to_all | solution.py:248
  63.2 8.4 %collective-permute-start.12 = (bf16[2,2,64,256]{3,2,1,0:T(8,128)(2,1)S(1)}, bf16[2,2,64,256]{3,2,1,0:T(8,128)(2,1)S(1)}, u32[]{:S(2)}, u32[]{:S(2)}) collective-permute-start(bf16[2,2,64,256]{3,2,1,0:T(8,128)(2,1)S(1)} %get-tuple-element.43.refs_1_), channel_id=1, source_target_pairs={{0,8},{8,0},{16,24},{24,16},{1,9},{9,1},{17,25},{25,17},{2,10},{10... | collective-permute-start | bytes 393224 | tf_op jit(solution)/shard_map/ppermute | solution.py:253
  65.4 7.6 %collective-permute-start.13 = (bf16[2,2,64,256]{3,2,1,0:T(8,128)(2,1)S(1)}, bf16[2,2,64,256]{3,2,1,0:T(8,128)(2,1)S(1)}, u32[]{:S(2)}, u32[]{:S(2)}) collective-permute-start(bf16[2,2,64,256]{3,2,1,0:T(8,128)(2,1)S(1)} %get-tuple-element.44.refs_2_), channel_id=1, source_target_pairs={{0,16},{8,24},{16,0},{24,8},{1,17},{9,25},{17,1},{25,9},{2,18},{10... | collective-permute-start | bytes 393224 | tf_op jit(solution)/shard_map/ppermute | solution.py:253
  67.4 10.5 %collective-permute-start.14 = (bf16[2,2,64,256]{3,2,1,0:T(8,128)(2,1)S(1)}, bf16[2,2,64,256]{3,2,1,0:T(8,128)(2,1)S(1)}, u32[]{:S(2)}, u32[]{:S(2)}) collective-permute-start(bf16[2,2,64,256]{3,2,1,0:T(8,128)(2,1)S(1)} %get-tuple-element.45.refs_3_), channel_id=1, source_target_pairs={{0,24},{8,16},{16,8},{24,0},{1,25},{9,17},{17,9},{25,1},{2,26},{10... | collective-permute-start | bytes 393224 | tf_op jit(solution)/shard_map/ppermute | solution.py:253
  80.9 41.6 %copy-start.3 = (bf16[2,2,64,256]{3,2,1,0:T(8,128)(2,1)}, bf16[2,2,64,256]{3,2,1,0:T(8,128)(2,1)S(1)}, u32[]{:S(2)}) copy-start(bf16[2,2,64,256]{3,2,1,0:T(8,128)(2,1)S(1)} %get-tuple-element.55.refs_2_) | copy-start | bytes 393220
  80.9 41.6 %copy-start.5 = (bf16[2,2,64,256]{3,2,1,0:T(8,128)(2,1)}, bf16[2,2,64,256]{3,2,1,0:T(8,128)(2,1)S(1)}, u32[]{:S(2)}) copy-start(bf16[2,2,64,256]{3,2,1,0:T(8,128)(2,1)S(1)} %get-tuple-element.56.refs_3_) | copy-start | bytes 393220
  80.9 29.2 %copy-start.13 = (f32[64,128]{1,0:T(8,128)S(1)}, f32[64,128]{1,0:T(8,128)}, u32[]{:S(2)}) copy-start(f32[64,128]{1,0:T(8,128)} %get-tuple-element.71) | copy-start | bytes 98308
  80.9 42.4 %all-to-all-start.5 = ((bf16[8,2,64,256]{3,2,1,0:T(8,128)(2,1)}), bf16[8,2,64,256]{3,2,1,0:T(8,128)(2,1)S(1)}, u32[]{:S(2)}, u32[]{:S(2)}) async-start(bf16[8,2,64,256]{3,2,1,0:T(8,128)(2,1)} %get-tuple-element.46), calls=%async_computation.5 | async-start | bytes 1048576 | tf_op jit(solution)/shard_map/all_to_all | solution.py:248
  87.1 9.3 %collective-permute-start.3 = (bf16[2,2,64,256]{3,2,1,0:T(8,128)(2,1)S(1)}, bf16[2,2,64,256]{3,2,1,0:T(8,128)(2,1)S(1)}, u32[]{:S(2)}, u32[]{:S(2)}) collective-permute-start(bf16[2,2,64,256]{3,2,1,0:T(8,128)(2,1)S(1)} %get-tuple-element.63), channel_id=1, source_target_pairs={{0,8},{8,0},{16,24},{24,16},{1,9},{9,1},{17,25},{25,17},{2,10},{10... | collective-permute-start | bytes 393224 | tf_op jit(solution)/shard_map/ppermute | solution.py:253
  89.7 12.9 %collective-permute-start.4 = (bf16[2,2,64,256]{3,2,1,0:T(8,128)(2,1)S(1)}, bf16[2,2,64,256]{3,2,1,0:T(8,128)(2,1)S(1)}, u32[]{:S(2)}, u32[]{:S(2)}) collective-permute-start(bf16[2,2,64,256]{3,2,1,0:T(8,128)(2,1)S(1)} %get-tuple-element.62), channel_id=1, source_target_pairs={{0,16},{8,24},{16,0},{24,8},{1,17},{9,25},{17,1},{25,9},{2,18},{10... | collective-permute-start | bytes 393224 | tf_op jit(solution)/shard_map/ppermute | solution.py:253
  91.6 11.0 %collective-permute-start.5 = (bf16[2,2,64,256]{3,2,1,0:T(8,128)(2,1)S(1)}, bf16[2,2,64,256]{3,2,1,0:T(8,128)(2,1)S(1)}, u32[]{:S(2)}, u32[]{:S(2)}) collective-permute-start(bf16[2,2,64,256]{3,2,1,0:T(8,128)(2,1)S(1)} %get-tuple-element.61), channel_id=1, source_target_pairs={{0,24},{8,16},{16,8},{24,0},{1,25},{9,17},{17,9},{25,1},{2,26},{10... | collective-permute-start | bytes 393224 | tf_op jit(solution)/shard_map/ppermute | solution.py:253
  104.2 7.3 %collective-permute-start.6 = (bf16[2,2,64,256]{3,2,1,0:T(8,128)(2,1)S(1)}, bf16[2,2,64,256]{3,2,1,0:T(8,128)(2,1)S(1)}, u32[]{:S(2)}, u32[]{:S(2)}) collective-permute-start(bf16[2,2,64,256]{3,2,1,0:T(8,128)(2,1)S(1)} %get-tuple-element.37.refs_1_), channel_id=1, source_target_pairs={{0,8},{8,0},{16,24},{24,16},{1,9},{9,1},{17,25},{25,17},{2,10},{10... | collective-permute-start | bytes 393224 | tf_op jit(solution)/shard_map/ppermute | solution.py:253
  107.0 12.5 %collective-permute-start.7 = (bf16[2,2,64,256]{3,2,1,0:T(8,128)(2,1)S(1)}, bf16[2,2,64,256]{3,2,1,0:T(8,128)(2,1)S(1)}, u32[]{:S(2)}, u32[]{:S(2)}) collective-permute-start(bf16[2,2,64,256]{3,2,1,0:T(8,128)(2,1)S(1)} %get-tuple-element.38.refs_2_), channel_id=1, source_target_pairs={{0,16},{8,24},{16,0},{24,8},{1,17},{9,25},{17,1},{25,9},{2,18},{10... | collective-permute-start | bytes 393224 | tf_op jit(solution)/shard_map/ppermute | solution.py:253
  108.8 10.8 %collective-permute-start.8 = (bf16[2,2,64,256]{3,2,1,0:T(8,128)(2,1)S(1)}, bf16[2,2,64,256]{3,2,1,0:T(8,128)(2,1)S(1)}, u32[]{:S(2)}, u32[]{:S(2)}) collective-permute-start(bf16[2,2,64,256]{3,2,1,0:T(8,128)(2,1)S(1)} %get-tuple-element.39.refs_3_), channel_id=1, source_target_pairs={{0,24},{8,16},{16,8},{24,0},{1,25},{9,17},{17,9},{25,1},{2,26},{10... | collective-permute-start | bytes 393224 | tf_op jit(solution)/shard_map/ppermute | solution.py:253
  122.5 0.8 copy-start.1
  123.3 24.2 %all-to-all-start.2 = ((bf16[8,2,64,256]{3,2,1,0:T(8,128)(2,1)}), bf16[8,2,64,256]{3,2,1,0:T(8,128)(2,1)S(1)}, u32[]{:S(2)}, u32[]{:S(2)}) async-start(bf16[8,2,64,256]{3,2,1,0:T(8,128)(2,1)} %get-tuple-element.40), calls=%async_computation.2 | async-start | bytes 1048576 | tf_op jit(solution)/shard_map/all_to_all | solution.py:248
  128.4 8.6 %collective-permute-start.18 = (bf16[2,2,64,256]{3,2,1,0:T(8,128)(2,1)S(1)}, bf16[2,2,64,256]{3,2,1,0:T(8,128)(2,1)S(1)}, u32[]{:S(2)}, u32[]{:S(2)}) collective-permute-start(bf16[2,2,64,256]{3,2,1,0:T(8,128)(2,1)S(1)} %get-tuple-element.54.refs_1_), channel_id=1, source_target_pairs={{0,8},{8,0},{16,24},{24,16},{1,9},{9,1},{17,25},{25,17},{2,10},{10... | collective-permute-start | bytes 393224 | tf_op jit(solution)/shard_map/ppermute | solution.py:253
  130.6 13.1 %collective-permute-start.19 = (bf16[2,2,64,256]{3,2,1,0:T(8,128)(2,1)}, bf16[2,2,64,256]{3,2,1,0:T(8,128)(2,1)S(1)}, u32[]{:S(2)}, u32[]{:S(2)}) collective-permute-start(bf16[2,2,64,256]{3,2,1,0:T(8,128)(2,1)} %copy-done.3), channel_id=1, source_target_pairs={{0,16},{8,24},{16,0},{24,8},{1,17},{9,25},{17,1},{25,9},{2,18},{10... | collective-permute-start | bytes 393224 | tf_op jit(solution)/shard_map/ppermute | solution.py:253
  132.0 11.8 %collective-permute-start.20 = (bf16[2,2,64,256]{3,2,1,0:T(8,128)(2,1)}, bf16[2,2,64,256]{3,2,1,0:T(8,128)(2,1)S(1)}, u32[]{:S(2)}, u32[]{:S(2)}) collective-permute-start(bf16[2,2,64,256]{3,2,1,0:T(8,128)(2,1)} %copy-done.5), channel_id=1, source_target_pairs={{0,24},{8,16},{16,8},{24,0},{1,25},{9,17},{17,9},{25,1},{2,26},{10... | collective-permute-start | bytes 393224 | tf_op jit(solution)/shard_map/ppermute | solution.py:253
  143.7 0.9 copy-start.4
  144.6 0.9 copy-start.6
  147.5 23.6 %all-to-all-start.7 = ((bf16[8,2,64,256]{3,2,1,0:T(8,128)(2,1)}), bf16[8,2,64,256]{3,2,1,0:T(8,128)(2,1)S(1)}, u32[]{:S(2)}, u32[]{:S(2)}) async-start(bf16[8,2,64,256]{3,2,1,0:T(8,128)(2,1)} %shard_map.81), calls=%async_computation.7 | async-start | bytes 1048576 | tf_op jit(solution)/shard_map/all_to_all | solution.py:248
  152.8 8.8 %collective-permute-start.15 = (bf16[2,2,64,256]{3,2,1,0:T(8,128)(2,1)S(1)}, bf16[2,2,64,256]{3,2,1,0:T(8,128)(2,1)S(1)}, u32[]{:S(2)}, u32[]{:S(2)}) collective-permute-start(bf16[2,2,64,256]{3,2,1,0:T(8,128)(2,1)S(1)} %get-tuple-element.49.refs_1_), channel_id=1, source_target_pairs={{0,8},{8,0},{16,24},{24,16},{1,9},{9,1},{17,25},{25,17},{2,10},{10... | collective-permute-start | bytes 393224 | tf_op jit(solution)/shard_map/ppermute | solution.py:253
  155.2 12.9 %collective-permute-start.16 = (bf16[2,2,64,256]{3,2,1,0:T(8,128)(2,1)S(1)}, bf16[2,2,64,256]{3,2,1,0:T(8,128)(2,1)S(1)}, u32[]{:S(2)}, u32[]{:S(2)}) collective-permute-start(bf16[2,2,64,256]{3,2,1,0:T(8,128)(2,1)S(1)} %get-tuple-element.50.refs_2_), channel_id=1, source_target_pairs={{0,16},{8,24},{16,0},{24,8},{1,17},{9,25},{17,1},{25,9},{2,18},{10... | collective-permute-start | bytes 393224 | tf_op jit(solution)/shard_map/ppermute | solution.py:253
  156.4 11.6 %collective-permute-start.17 = (bf16[2,2,64,256]{3,2,1,0:T(8,128)(2,1)S(1)}, bf16[2,2,64,256]{3,2,1,0:T(8,128)(2,1)S(1)}, u32[]{:S(2)}, u32[]{:S(2)}) collective-permute-start(bf16[2,2,64,256]{3,2,1,0:T(8,128)(2,1)S(1)} %get-tuple-element.51.refs_3_), channel_id=1, source_target_pairs={{0,24},{8,16},{16,8},{24,0},{1,25},{9,17},{17,9},{25,1},{2,26},{10... | collective-permute-start | bytes 393224 | tf_op jit(solution)/shard_map/ppermute | solution.py:253
  168.1 1.0 copy-start.2
  171.1 20.6 %all-to-all-start.6 = ((bf16[8,2,64,256]{3,2,1,0:T(8,128)(2,1)}), bf16[8,2,64,256]{3,2,1,0:T(8,128)(2,1)S(1)}, u32[]{:S(2)}, u32[]{:S(2)}) async-start(bf16[8,2,64,256]{3,2,1,0:T(8,128)(2,1)} %shard_map.80), calls=%async_computation.6 | async-start | bytes 1048576 | tf_op jit(solution)/shard_map/all_to_all | solution.py:248
  176.6 1.1 copy-start.10

commit v3 on v1

--- a/solution.py
+++ b/solution.py
@@ -92,49 +92,55 @@
 def assemble(place, order, pieces, whole):
     k = 0
     for piece in pieces:
-        rows = piece.shape[2]
-        for block in range(piece.shape[0]):
+        count, rows, virtual = piece.shape[-3:]
+        for block in range(piece.shape[0] if len(piece.shape) == 4 else 1):
             start = pl.multiple_of((place[1] ^ order[k]) * rows, rows)
-            for single in range(piece.shape[1]):
-                whole[single, pl.ds(start, rows), :] = piece[block, single]
+            for single in range(count):
+                values = piece[block, single] if len(piece.shape) == 4 else piece[single]
+                whole[pl.ds(start, rows), single * virtual:(single + 1) * virtual] = values
             k += 1
 
 
-def ladder_pair(matrix, whole, total):
-    def one(single, carry):
-        vector = whole[single]
-        inner = lax.dot_general(matrix, vector, (((1,), (1,)), ((), ())), preferred_element_type=WIDE)
-        term = jnp.dot(vector, inner.astype(NARROW), preferred_element_type=WIDE)
-        total[...] += term
-        return carry
-
-    total[...] = jnp.zeros_like(total)
-    lax.fori_loop(0, whole.shape[0], one, 0)
-
-
-def first_ladder_kernel(tiles, order, place, source, low, high, out, whole, total):
-    assemble(place, order, (low, high), whole)
+def ladder_pair(matrix, whole, inner, total):
+    virtual = matrix.shape[0]
+    for single in range(whole.shape[1] // virtual):
+        at = slice(single * virtual, (single + 1) * virtual)
+        inner[at, :] = lax.dot_general(
+            matrix, whole[:, at], (((1,), (1,)), ((), ())), preferred_element_type=WIDE
+        ).astype(NARROW)
+    total[...] = jnp.dot(whole[...], inner[...], preferred_element_type=WIDE)
+
+
+def inverse(x):
+    guess = pl.reciprocal(x, approx=True)
+    return guess * (2.0 - x * guess)
+
+
+def first_ladder_kernel(tiles, order, place, source, *refs):
+    pieces, (out, whole, inner, total) = refs[:-4], refs[-4:]
+    assemble(place, order, pieces, whole)
     for pair in range(source.shape[0]):
-        ladder_pair(source[pair].astype(NARROW), whole, total)
+        ladder_pair(source[pair].astype(NARROW), whole, inner, total)
         pack_pair(tiles, total, out, pair)
 
 
-def second_ladder_kernel(tiles, order, count, place, occ, source, blocks, row, column, low, high, out,
-                         whole, total, matrix):
-    assemble(place, order, (low, high), whole)
+def second_ladder_kernel(tiles, order, place, occ, source, blocks, row, column, *refs):
+    pieces, (out, whole, inner, total, matrix) = refs[:-5], refs[-5:]
+    assemble(place, order, pieces, whole)
+    count = source.shape[0]
     for pair in range(count):
         def put(a, b, tile):
             matrix[tiles.span(a), tiles.span(b)] = tile.astype(NARROW)
 
         unpack_pair(tiles, blocks, pair, put)
-        ladder_pair(matrix[...], whole, total)
+        ladder_pair(matrix[...], whole, inner, total)
         base = occ[place[0] * count + pair] + occ[place[1]]
 
         def finish(step, carry):
             at = pl.ds(pl.multiple_of(step * 16, 16), 16)
             own = base - row[at, :1] - column[...]
             out[pair, at, :] = (
-                source[pair, at, :] + 2.0 * matrix[at, :].astype(WIDE) + (2.0 * total[at, :]) / own
+                source[pair, at, :] + 2.0 * (matrix[at, :].astype(WIDE) + total[at, :] * inverse(own))
             )
             return carry
 
@@ -208,7 +214,7 @@
             base = occ[place[0] * first + u] + occ[column]
 
             def finish(mirrored):
-                value = (own[s][u, w].astype(WIDE) + mirrored) / (base - sums[...])
+                value = (own[s][u, w].astype(WIDE) + mirrored) * inverse(base - sums[...])
                 narrow = value.astype(NARROW)
                 update[u, s * first + w] = value
                 sent[column, u] = narrow
@@ -238,7 +244,7 @@
             base = occ[place[0] * first + u] + occ[column]
 
             def finish(mirrored):
-                value = (own[s][u, w].astype(WIDE) + mirrored) / (base - sums[...])
+                value = (own[s][u, w].astype(WIDE) + mirrored) * inverse(base - sums[...])
                 out[column, u] = (rest[u, s * first + w].astype(WIDE) + value).astype(NARROW)
 
             with_mirror(tiles, place, other[s][w, u].astype(WIDE), finish)
@@ -253,20 +259,23 @@
 
 def across_first(parts, groups):
     return [parts[0]] + [
-        lax.ppermute(parts[s], "occi", [(k, k ^ s) for k in range(groups)]) for s in range(1, groups)
-    ]
+        lax.ppermute(parts[s], "occi", [(k, k ^ s) for k in range(groups)])
+        for s in range(groups - 1, 0, -1)
+    ][::-1]
+
+
+def tie(x, *others):
+    return lax.optimization_barrier((x, *others))[0]
 
 
 def gather_vectors(vectors, devices):
-    held, order = vectors[None], [0]
-    step = devices // 2
-    while True:
-        other = lax.ppermute(held, "occj", [(k, k ^ step) for k in range(devices)])
-        order = order + [k ^ step for k in order]
-        if step == 1:
-            return held, other, order
-        held = jnp.concatenate([held, other], axis=0)
-        step //= 2
+    def turn(x, k):
+        return lax.ppermute(x, "occj", [(d, d ^ k) for d in range(devices)])
+
+    even = list(range(0, devices, 2))
+    held = [vectors] + [turn(vectors, k) for k in even[1:]]
+    other = turn(jnp.stack(held), 1)
+    return [*held, other], even + [k ^ 1 for k in even]
 
 
 def virtual_sums(tiles, vir_energy, q):
@@ -297,18 +306,23 @@
     place = jnp.stack([p, q]).astype(jnp.int32)
     part = jax.ShapeDtypeStruct((first, first, edge, 2 * edge), NARROW)
     packed = jax.ShapeDtypeStruct((devices, first, edge, 2 * edge), NARROW)
-    vector_rows = virtual // devices
-
-    low, high, order = gather_vectors(vectors, devices)
-    held = exchange(pack(tiles, devices, current)).reshape(groups, first, first, edge, 2 * edge)
-    mirror = across_first([held[p ^ s] for s in range(groups)], groups)
+    singles = vectors.shape[0]
+    whole = pltpu.VMEM((virtual, singles * virtual), NARROW)
+    inner = pltpu.VMEM((singles * virtual, virtual), NARROW)
+    square = pltpu.VMEM((virtual, virtual), WIDE)
+
+    started = pack(tiles, devices, current)
+    held = exchange(started)
+    pieces, order = gather_vectors(tie(vectors, started), devices)
+    parts = held.reshape(groups, first, first, edge, 2 * edge)
+    mirror = across_first([parts[p ^ s] for s in range(groups)], groups)
     sums = virtual_sums(tiles, vir_energy, q)
 
-    ladder_flops = first * vectors.shape[0] * 4 * virtual**3
+    ladder_flops = first * singles * 4 * virtual**3
     ladder = exchange(call(
-        functools.partial(first_ladder_kernel, tiles, order), packed,
-        [pltpu.VMEM((vectors.shape[0], virtual, virtual), NARROW), pltpu.VMEM((virtual, virtual), WIDE)],
-        ladder_flops, 8 * count, place, current, low, high, specs=[SMEM, VMEM, VMEM, VMEM],
+        functools.partial(first_ladder_kernel, tiles, order), packed, [whole, inner, square],
+        ladder_flops, 8 * count, tie(place, held), current, *pieces,
+        specs=[SMEM] + [VMEM] * (1 + len(pieces)),
     ))
     half = call(
         functools.partial(half_kernel, tiles, groups, first), [part] * groups, [],
@@ -323,15 +337,13 @@
         specs=[SMEM] * 3 + [VMEM] * (2 * groups + 1),
     )
     other = across_first(mixed, groups)
-    back = exchange(sent)
+    back = exchange(tie(sent, other[1]))
     base = call(
-        functools.partial(second_ladder_kernel, tiles, order, first),
-        jax.ShapeDtypeStruct(current.shape, WIDE),
-        [pltpu.VMEM((vectors.shape[0], virtual, virtual), NARROW), pltpu.VMEM((virtual, virtual), WIDE),
-         pltpu.VMEM((virtual, virtual), NARROW)],
+        functools.partial(second_ladder_kernel, tiles, order), jax.ShapeDtypeStruct(current.shape, WIDE),
+        [whole, inner, square, pltpu.VMEM((virtual, virtual), NARROW)],
         ladder_flops, 12 * count, place, occ_energy, current, back,
-        jnp.broadcast_to(vir_energy[:, None], (virtual, 128)), vir_energy[None, :], low, high,
-        specs=[SMEM] * 2 + [VMEM] * 6,
+        jnp.broadcast_to(vir_energy[:, None], (virtual, 128)), vir_energy[None, :], *pieces,
+        specs=[SMEM] * 2 + [VMEM] * (4 + len(pieces)),
     )
     rest = exchange(call(
         functools.partial(rest_kernel, tiles, groups, first), packed, [],

time: 160 us -> 159 us (level)
  the two profiles are of different devices: /device:TPU:0 before, /device:TPU:8 now
where the time goes in v3:
time: 159 us
  waiting for transfers between devices  90.1 us (57%)
  Pallas kernels  33.4 us (21%)
  starting transfers between devices  28.8 us (18%)
  local copies, waits for them, and re-layouts  4.42 us (3%)
    ppermute x9, waiting for transfers between devices, across_first(): lax.ppermute(parts[s], 'occi', [(k, k ^ s) for k in range(groups)])  75 us
    pallas_call x7, Pallas kernels, call(): pl.pallas_call(body, out_shape=outs, in_specs=specs, out_specs=jax.tree.m...  33.4 us
    all_to_all x4, starting transfers between devices, exchange(): lax.all_to_all(blocks, 'occj', split_axis=0, concat_axis=0, tiled=True)  16.4 us
    all_to_all x4, waiting for transfers between devices, exchange(): lax.all_to_all(blocks, 'occj', split_axis=0, concat_axis=0, tiled=True)  10 us
    ppermute x9, starting transfers between devices, across_first(): lax.ppermute(parts[s], 'occi', [(k, k ^ s) for k in range(groups)])  8.78 us
    ppermute x4, waiting for transfers between devices, turn(): return lax.ppermute(x, 'occj', [(d, d ^ k) for d in range(devices)])  5.09 us
    ppermute x4, starting transfers between devices, turn(): return lax.ppermute(x, 'occj', [(d, d ^ k) for d in range(devices)])  3.56 us
  transfers between devices with their start and end apart: 17, of which 14 were waited for; matrix products, arithmetic and copies ran while one was open for 1% of the time, Pallas kernels for 9%

profile of v3, /device:TPU:8, one launch (start us, length us, event | category | flops | bytes accessed | tf_op | source)
XLA Modules:
  0.0 158.6 jit_solution(13283691546737342735)
XLA Ops:
  0.0 1.6 %copy-done = f32[2,1,512,512]{3,2,1,0:T(8,128)S(1)} copy-done((f32[2,1,512,512]{3,2,1,0:T(8,128)S(1)}, f32[2,1,512,512]{3,2,1,0:T(8,128)}, u32[]{:S(2)}) %copy-start) | copy-done | bytes 2097176
  1.6 1.2 shard_map.73
  2.8 0.0 copy-done.2
  2.8 1.5 collective-permute-start
  4.3 1.5 collective-permute-start.1
  5.8 0.5 collective-permute-start.2
  6.3 3.7 %all-to-all-start = ((bf16[8,2,128,256]{3,2,1,0:T(8,128)(2,1)}), bf16[8,2,128,256]{3,2,1,0:T(8,128)(2,1)S(1)}, u32[]{:S(2)}, u32[]{:S(2)}) async-start(bf16[8,2,128,256]{3,2,1,0:T(8,128)(2,1)} %shard_map.73), calls=%async_computation | async-start | bytes 2097152 | tf_op jit(solution)/shard_map/all_to_all | solution.py:257
  10.0 0.6 collective-permute-done.refs_1_
  10.6 4.4 %collective-permute-done.1.refs_2_ = bf16[3,64,512]{2,1,0:T(8,128)(2,1)S(1)} collective-permute-done((bf16[3,64,512]{2,1,0:T(8,128)(2,1)S(1)}, bf16[3,64,512]{2,1,0:T(8,128)(2,1)S(1)}, u32[]{:S(2)}, u32[]{:S(2)}) %collective-permute-start.1) | collective-permute-done | bytes 196640 | tf_op jit(solution)/shard_map/ppermute | solution.py:273
  15.0 0.1 collective-permute-done.2.refs_3_
  15.1 0.1 pad_maximum_fusion
  15.2 0.1 collective-permute-start.3
  15.3 0.0 copy-done.16
  15.3 0.7 dynamic_slice.26
  16.6 0.0 copy-done.15
  16.6 0.6 dynamic_slice.24
  17.8 0.1 pad_add_fusion.place
  17.9 8.3 %all-to-all-done = bf16[8,2,128,256]{3,2,1,0:T(8,128)(2,1)S(1)} async-done(((bf16[8,2,128,256]{3,2,1,0:T(8,128)(2,1)}), bf16[8,2,128,256]{3,2,1,0:T(8,128)(2,1)S(1)}, u32[]{:S(2)}, u32[]{:S(2)}) %all-to-all-start) | async-done | bytes 1048608 | tf_op jit(solution)/shard_map/all_to_all | solution.py:257
  26.1 0.0 collective-permute-done.3.refs_4_
  26.1 6.5 %shard_map.74 = bf16[8,2,128,256]{3,2,1,0:T(8,128)(2,1)} custom-call(s32[2]{0:T(128)S(1)} %pad_add_fusion.place, f32[2,512,512]{2,1,0:T(8,128)} %bitcast.22, bf16[3,64,512]{2,1,0:T(8,128)(2,1)S(1)} %copy-done.2, bf16[3,64,512]{2,1,0:T(8,128)(2,1)S(1)} %collective-permute-done.refs_1_, bf16[3,64,512]{2,1,0:T(8,128)(2,1)S(1)} %collective-permute-done.1.refs_2_, ...), custom_call_target="tpu_custom_call" | custom-call | flops 3221225472 | bytes 4194304 | tf_op jit(solution)/shard_map/pallas_call | solution.py:44
  32.6 0.0 copy-done.4
  32.6 0.0 copy-done.6
  32.6 0.0 copy-done.8
  32.6 0.0 copy-done.12
  32.6 0.0 copy-start.10
  32.7 0.0 copy-start.14
  32.7 3.6 %all-to-all-start.1 = ((bf16[8,2,128,256]{3,2,1,0:T(8,128)(2,1)}), bf16[8,2,128,256]{3,2,1,0:T(8,128)(2,1)S(1)}, u32[]{:S(2)}, u32[]{:S(2)}) async-start(bf16[8,2,128,256]{3,2,1,0:T(8,128)(2,1)} %shard_map.74), calls=%async_computation.1 | async-start | bytes 2097152 | tf_op jit(solution)/shard_map/all_to_all | solution.py:257
  36.3 0.1 fusion
  36.3 0.1 fusion.1
  36.4 0.1 dynamic-slice_bitcast_fusion
  36.5 0.5 collective-permute-start.4
  37.1 2.6 %collective-permute-start.5 = (bf16[2,2,128,256]{3,2,1,0:T(8,128)(2,1)S(1)}, bf16[2,2,128,256]{3,2,1,0:T(8,128)(2,1)S(1)}, u32[]{:S(2)}, u32[]{:S(2)}) collective-permute-start(bf16[2,2,128,256]{3,2,1,0:T(8,128)(2,1)S(1)} %get-tuple-element.32), channel_id=1, source_target_pairs={{0,16},{8,24},{16,0},{24,8},{1,17},{9,25},{17,1},{25,9},{2,18},{10... | collective-permute-start | bytes 786440 | tf_op jit(solution)/shard_map/ppermute | solution.py:262
  39.6 0.5 collective-permute-start.6
  40.1 0.1 fusion.2
  40.2 0.1 broadcast_add_fusion.2
  40.3 8.0 %collective-permute-done.4.refs_1_ = bf16[2,2,128,256]{3,2,1,0:T(8,128)(2,1)S(1)} collective-permute-done((bf16[2,2,128,256]{3,2,1,0:T(8,128)(2,1)S(1)}, bf16[2,2,128,256]{3,2,1,0:T(8,128)(2,1)S(1)}, u32[]{:S(2)}, u32[]{:S(2)}) %collective-permute-start.4) | collective-permute-done | bytes 262176 | tf_op jit(solution)/shard_map/ppermute | solution.py:262
  48.3 9.3 %collective-permute-done.5.refs_2_ = bf16[2,2,128,256]{3,2,1,0:T(8,128)(2,1)S(1)} collective-permute-done((bf16[2,2,128,256]{3,2,1,0:T(8,128)(2,1)S(1)}, bf16[2,2,128,256]{3,2,1,0:T(8,128)(2,1)S(1)}, u32[]{:S(2)}, u32[]{:S(2)}) %collective-permute-start.5) | collective-permute-done | bytes 262176 | tf_op jit(solution)/shard_map/ppermute | solution.py:262
  57.6 5.7 %collective-permute-done.6.refs_3_ = bf16[2,2,128,256]{3,2,1,0:T(8,128)(2,1)S(1)} collective-permute-done((bf16[2,2,128,256]{3,2,1,0:T(8,128)(2,1)S(1)}, bf16[2,2,128,256]{3,2,1,0:T(8,128)(2,1)S(1)}, u32[]{:S(2)}, u32[]{:S(2)}) %collective-permute-start.6) | collective-permute-done | bytes 262176 | tf_op jit(solution)/shard_map/ppermute | solution.py:262
  63.3 0.0 all-to-all-done.1.ladder
  63.3 2.6 %shard_map.75 = (bf16[2,2,128,256]{3,2,1,0:T(8,128)(2,1)S(1)}, bf16[2,2,128,256]{3,2,1,0:T(8,128)(2,1)S(1)}, bf16[2,2,128,256]{3,2,1,0:T(8,128)(2,1)S(1)}, bf16[2,2,128,256]{3,2,1,0:T(8,128)(2,1)S(1)}) custom-call(s32[2]{0:T(128)S(1)} %pad_add_fusion.place, f32[8,8]{1,0:T(8,128)S(1)} %convert_element_type.3.fock, ...), custom_call_target="tpu_custom_call" | custom-call | flops 8388608 | bytes 3145728 | tf_op jit(solution)/shard_map/pallas_call | solution.py:44
  65.8 0.1 collective-permute-start.7
  65.9 3.0 %collective-permute-start.8 = (bf16[2,2,128,256]{3,2,1,0:T(8,128)(2,1)S(1)}, bf16[2,2,128,256]{3,2,1,0:T(8,128)(2,1)S(1)}, u32[]{:S(2)}, u32[]{:S(2)}) collective-permute-start(bf16[2,2,128,256]{3,2,1,0:T(8,128)(2,1)S(1)} %get-tuple-element.22.refs_2_), channel_id=1, source_target_pairs={{0,16},{8,24},{16,0},{24,8},{1,17},{9,25},{17,1},{25,9},{2,18},{10... | collective-permute-start | bytes 786440 | tf_op jit(solution)/shard_map/ppermute | solution.py:262
  68.9 0.5 collective-permute-start.9
  69.4 0.1 broadcast_add_fusion
  69.5 6.2 %collective-permute-done.7.refs_5_ = bf16[2,2,128,256]{3,2,1,0:T(8,128)(2,1)S(1)} collective-permute-done((bf16[2,2,128,256]{3,2,1,0:T(8,128)(2,1)S(1)}, bf16[2,2,128,256]{3,2,1,0:T(8,128)(2,1)S(1)}, u32[]{:S(2)}, u32[]{:S(2)}) %collective-permute-start.7) | collective-permute-done | bytes 262176 | tf_op jit(solution)/shard_map/ppermute | solution.py:262
  75.7 11.2 %collective-permute-done.8.refs_6_ = bf16[2,2,128,256]{3,2,1,0:T(8,128)(2,1)S(1)} collective-permute-done((bf16[2,2,128,256]{3,2,1,0:T(8,128)(2,1)S(1)}, bf16[2,2,128,256]{3,2,1,0:T(8,128)(2,1)S(1)}, u32[]{:S(2)}, u32[]{:S(2)}) %collective-permute-start.8) | collective-permute-done | bytes 262176 | tf_op jit(solution)/shard_map/ppermute | solution.py:262
  86.9 4.5 %collective-permute-done.9.refs_7_ = bf16[2,2,128,256]{3,2,1,0:T(8,128)(2,1)S(1)} collective-permute-done((bf16[2,2,128,256]{3,2,1,0:T(8,128)(2,1)S(1)}, bf16[2,2,128,256]{3,2,1,0:T(8,128)(2,1)S(1)}, u32[]{:S(2)}, u32[]{:S(2)}) %collective-permute-start.9) | collective-permute-done | bytes 262176 | tf_op jit(solution)/shard_map/ppermute | solution.py:262
  91.4 4.9 %shard_map.76 = (bf16[8,2,128,256]{3,2,1,0:T(8,128)(2,1)}, bf16[2,8,128,256]{3,2,1,0:T(8,128)(2,1)}, bf16[2,2,128,256]{3,2,1,0:T(8,128)(2,1)S(1)}, bf16[2,2,128,...) custom-call(s32[2]{0:T(128)S(1)} %pad_add_fusion.place, ...), custom_call_target="tpu_custom_call" | custom-call | flops 8388608 | bytes 5242880 | tf_op jit(solution)/shard_map/pallas_call | solution.py:44
  96.4 0.0 collective-permute-start.10
  96.4 6.4 %collective-permute-done.10.refs_5_ = bf16[2,2,128,256]{3,2,1,0:T(8,128)(2,1)S(1)} collective-permute-done((bf16[2,2,128,256]{3,2,1,0:T(8,128)(2,1)S(1)}, bf16[2,2,128,256]{3,2,1,0:T(8,128)(2,1)S(1)}, u32[]{:S(2)}, u32[]{:S(2)}) %collective-permute-start.10) | collective-permute-done | bytes 262176 | tf_op jit(solution)/shard_map/ppermute | solution.py:262
  102.7 4.4 %all-to-all-start.2 = ((bf16[8,2,128,256]{3,2,1,0:T(8,128)(2,1)}), bf16[8,2,128,256]{3,2,1,0:T(8,128)(2,1)S(1)}, u32[]{:S(2)}, u32[]{:S(2)}) async-start(bf16[8,2,128,256]{3,2,1,0:T(8,128)(2,1)} %get-tuple-element.26), calls=%async_computation.2 | async-start | bytes 2097152 | tf_op jit(solution)/shard_map/all_to_all | solution.py:257
  107.1 1.0 collective-permute-start.11
  108.2 0.6 collective-permute-start.12
  108.8 17.2 %collective-permute-done.11.refs_6_ = bf16[2,2,128,256]{3,2,1,0:T(8,128)(2,1)S(1)} collective-permute-done((bf16[2,2,128,256]{3,2,1,0:T(8,128)(2,1)S(1)}, bf16[2,2,128,256]{3,2,1,0:T(8,128)(2,1)S(1)}, u32[]{:S(2)}, u32[]{:S(2)}) %collective-permute-start.11) | collective-permute-done | bytes 262176 | tf_op jit(solution)/shard_map/ppermute | solution.py:262
  126.0 6.5 %collective-permute-done.12.refs_7_ = bf16[2,2,128,256]{3,2,1,0:T(8,128)(2,1)S(1)} collective-permute-done((bf16[2,2,128,256]{3,2,1,0:T(8,128)(2,1)S(1)}, bf16[2,2,128,256]{3,2,1,0:T(8,128)(2,1)S(1)}, u32[]{:S(2)}, u32[]{:S(2)}) %collective-permute-start.12) | collective-permute-done | bytes 262176 | tf_op jit(solution)/shard_map/ppermute | solution.py:262
  132.5 0.0 copy-done.1
  132.6 2.6 %shard_map.78 = bf16[8,2,128,256]{3,2,1,0:T(8,128)(2,1)} custom-call(s32[2]{0:T(128)S(1)} %pad_add_fusion.place, f32[8]{0:T(128)S(1)} %copy-done.11, f32[128,256]{1,0:T(8,128)S(1)} %maximum_select_fusion.sums, bf16[2,8,128,256]{3,2,1,0:T(8,128)(2,1)S(1)} %copy-done.1, bf16[2,2,128,256]{3,2,1,0:T(8,128)(2,1)S(1)} %get-tuple-element.28.refs_0_.refs_4_, ...), custom_call_target="tpu_custom_call" | custom-call | flops 2097152 | bytes 4194304 | tf_op jit(solution)/shard_map/pallas_call | solution.py:44
  135.2 0.0 all-to-all-done.2.blocks
  135.2 4.7 %all-to-all-start.3 = ((bf16[8,2,128,256]{3,2,1,0:T(8,128)(2,1)}), bf16[8,2,128,256]{3,2,1,0:T(8,128)(2,1)S(1)}, u32[]{:S(2)}, u32[]{:S(2)}) async-start(bf16[8,2,128,256]{3,2,1,0:T(8,128)(2,1)} %shard_map.78), calls=%async_computation.3 | async-start | bytes 2097152 | tf_op jit(solution)/shard_map/all_to_all | solution.py:257
  139.9 0.1 broadcast_in_dim.4.row
  140.1 1.1 copy-done.13
  141.2 12.4 %shard_map.77.source = f32[2,512,512]{2,1,0:T(8,128)} custom-call(s32[2]{0:T(128)S(1)} %pad_add_fusion.place, f32[8]{0:T(128)S(1)} %copy-done.11, f32[2,512,512]{2,1,0:T(8,128)} %bitcast.23, bf16[8,2,128,256]{3,2,1,0:T(8,128)(2,1)S(1)} %all-to-all-done.2.blocks, f32[512,128]{1,0:T(8,128)S(1)} %broadcast_in_dim.4.row, f32[1,512]{1,0:T(1,128)S(1)} %bitcast.29, ...), custom_call_target="tpu_custom_call" | custom-call | flops 3221225472 | bytes 6291456 | tf_op jit(solution)/shard_map/pallas_call | solution.py:44
  153.6 1.7 %all-to-all-done.3.blocks = bf16[8,2,128,256]{3,2,1,0:T(8,128)(2,1)S(1)} async-done(((bf16[8,2,128,256]{3,2,1,0:T(8,128)(2,1)}), bf16[8,2,128,256]{3,2,1,0:T(8,128)(2,1)S(1)}, u32[]{:S(2)}, u32[]{:S(2)}) %all-to-all-start.3) | async-done | bytes 1048608 | tf_op jit(solution)/shard_map/all_to_all | solution.py:257
  155.3 3.2 %shard_map.79 = f32[2,512,512]{2,1,0:T(8,128)} custom-call(f32[2,512,512]{2,1,0:T(8,128)} %shard_map.77.source, bf16[8,2,128,256]{3,2,1,0:T(8,128)(2,1)S(1)} %all-to-all-done.3.blocks), custom_call_target="tpu_custom_call", output_to_operand_aliasing={{}: (0, {})} | custom-call | flops 524288 | bytes 5242880 | tf_op jit(solution)/shard_map/pallas_call | solution.py:44
  (24 shorter events, 0.1 us)
Async XLA Ops:
  0.0 1.6 %copy-start = (f32[2,1,512,512]{3,2,1,0:T(8,128)S(1)}, f32[2,1,512,512]{3,2,1,0:T(8,128)}, u32[]{:S(2)}) copy-start(f32[2,1,512,512]{3,2,1,0:T(8,128)} %param.7) | copy-start | bytes 6291460
  1.6 1.2 copy-start.2
  2.8 12.5 %copy-start.16 = (s32[8]{0:T(128)S(1)}, s32[8]{0:T(128)}, u32[]{:S(2)}) copy-start(s32[8]{0:T(128)} %constant.33.clone) | copy-start | bytes 100
  2.8 13.8 %copy-start.15 = (s32[8]{0:T(128)S(1)}, s32[8]{0:T(128)}, u32[]{:S(2)}) copy-start(s32[8]{0:T(128)} %constant.32.clone) | copy-start | bytes 100
  2.8 7.8 %collective-permute-start = (bf16[3,64,512]{2,1,0:T(8,128)(2,1)S(1)}, bf16[3,64,512]{2,1,0:T(8,128)(2,1)S(1)}, u32[]{:S(2)}, u32[]{:S(2)}) collective-permute-start(bf16[3,64,512]{2,1,0:T(8,128)(2,1)S(1)} %copy-done.2), channel_id=1, source_target_pairs={{0,2},{1,3},{2,0},{3,1},{4,6},{5,7},{6,4},{7,5},{8,10},{9,11},{10,... | collective-permute-start | bytes 589832 | tf_op jit(solution)/shard_map/ppermute | solution.py:273
  4.3 10.7 %collective-permute-start.1 = (bf16[3,64,512]{2,1,0:T(8,128)(2,1)S(1)}, bf16[3,64,512]{2,1,0:T(8,128)(2,1)S(1)}, u32[]{:S(2)}, u32[]{:S(2)}) collective-permute-start(bf16[3,64,512]{2,1,0:T(8,128)(2,1)S(1)} %copy-done.2), channel_id=1, source_target_pairs={{0,4},{1,5},{2,6},{3,7},{4,0},{5,1},{6,2},{7,3},{8,12},{9,13},{10,... | collective-permute-start | bytes 589832 | tf_op jit(solution)/shard_map/ppermute | solution.py:273
  5.8 9.3 %collective-permute-start.2 = (bf16[3,64,512]{2,1,0:T(8,128)(2,1)S(1)}, bf16[3,64,512]{2,1,0:T(8,128)(2,1)S(1)}, u32[]{:S(2)}, u32[]{:S(2)}) collective-permute-start(bf16[3,64,512]{2,1,0:T(8,128)(2,1)S(1)} %copy-done.2), channel_id=1, source_target_pairs={{0,6},{1,7},{2,4},{3,5},{4,2},{5,3},{6,0},{7,1},{8,14},{9,15},{10,... | collective-permute-start | bytes 589832 | tf_op jit(solution)/shard_map/ppermute | solution.py:273
  6.3 19.8 %all-to-all-start = ((bf16[8,2,128,256]{3,2,1,0:T(8,128)(2,1)}), bf16[8,2,128,256]{3,2,1,0:T(8,128)(2,1)S(1)}, u32[]{:S(2)}, u32[]{:S(2)}) async-start(bf16[8,2,128,256]{3,2,1,0:T(8,128)(2,1)} %shard_map.73), calls=%async_computation | async-start | bytes 2097152 | tf_op jit(solution)/shard_map/all_to_all | solution.py:257
  10.6 22.0 %copy-start.4 = (bf16[3,64,512]{2,1,0:T(8,128)(2,1)}, bf16[3,64,512]{2,1,0:T(8,128)(2,1)S(1)}, u32[]{:S(2)}) copy-start(bf16[3,64,512]{2,1,0:T(8,128)(2,1)S(1)} %collective-permute-done.refs_1_) | copy-start | bytes 589828
  15.0 17.6 %copy-start.6 = (bf16[3,64,512]{2,1,0:T(8,128)(2,1)}, bf16[3,64,512]{2,1,0:T(8,128)(2,1)S(1)}, u32[]{:S(2)}) copy-start(bf16[3,64,512]{2,1,0:T(8,128)(2,1)S(1)} %collective-permute-done.1.refs_2_) | copy-start | bytes 589828
  15.1 17.5 %copy-start.8 = (bf16[3,64,512]{2,1,0:T(8,128)(2,1)}, bf16[3,64,512]{2,1,0:T(8,128)(2,1)S(1)}, u32[]{:S(2)}) copy-start(bf16[3,64,512]{2,1,0:T(8,128)(2,1)S(1)} %collective-permute-done.2.refs_3_) | copy-start | bytes 589828
  15.2 10.9 %collective-permute-start.3 = (bf16[4,3,64,512]{3,2,1,0:T(8,128)(2,1)S(1)}, bf16[4,3,64,512]{3,2,1,0:T(8,128)(2,1)S(1)}, u32[]{:S(2)}, u32[]{:S(2)}) collective-permute-start(bf16[4,3,64,512]{3,2,1,0:T(8,128)(2,1)S(1)} %pad_maximum_fusion), channel_id=1, source_target_pairs={{0,1},{1,0},{2,3},{3,2},{4,5},{5,4},{6,7},{7,6},{8,9},{9,8},{10,11... | collective-permute-start | bytes 2359304 | tf_op jit(solution)/shard_map/ppermute | solution.py:273
  26.1 6.5 %copy-start.12 = (bf16[4,3,64,512]{3,2,1,0:T(8,128)(2,1)}, bf16[4,3,64,512]{3,2,1,0:T(8,128)(2,1)S(1)}, u32[]{:S(2)}) copy-start(bf16[4,3,64,512]{3,2,1,0:T(8,128)(2,1)S(1)} %collective-permute-done.3.refs_4_) | copy-start | bytes 2359300
  32.6 3.6 %copy-start.10 = (f32[512]{0:T(512)S(1)}, f32[512]{0:T(512)}, u32[]{:S(2)}) copy-start(f32[512]{0:T(512)} %param.11) | copy-start | bytes 6148
  32.7 7.5 %copy-start.14 = (bf16[8,8]{1,0:T(8,128)(2,1)S(1)}, bf16[8,8]{1,0:T(8,128)(2,1)}, u32[]{:S(2)}) copy-start(bf16[8,8]{1,0:T(8,128)(2,1)} %param.9) | copy-start | bytes 388
  32.7 30.6 %all-to-all-start.1 = ((bf16[8,2,128,256]{3,2,1,0:T(8,128)(2,1)}), bf16[8,2,128,256]{3,2,1,0:T(8,128)(2,1)S(1)}, u32[]{:S(2)}, u32[]{:S(2)}) async-start(bf16[8,2,128,256]{3,2,1,0:T(8,128)(2,1)} %shard_map.74), calls=%async_computation.1 | async-start | bytes 2097152 | tf_op jit(solution)/shard_map/all_to_all | solution.py:257
  36.4 55.0 %copy-start.11 = (f32[8]{0:T(128)S(1)}, f32[8]{0:T(128)}, u32[]{:S(2)}) copy-start(f32[8]{0:T(128)} %occ.5) | copy-start | bytes 100
  36.5 11.8 %collective-permute-start.4 = (bf16[2,2,128,256]{3,2,1,0:T(8,128)(2,1)S(1)}, bf16[2,2,128,256]{3,2,1,0:T(8,128)(2,1)S(1)}, u32[]{:S(2)}, u32[]{:S(2)}) collective-permute-start(bf16[2,2,128,256]{3,2,1,0:T(8,128)(2,1)S(1)} %get-tuple-element.33), channel_id=1, source_target_pairs={{0,8},{8,0},{16,24},{24,16},{1,9},{9,1},{17,25},{25,17},{2,10},{10... | collective-permute-start | bytes 786440 | tf_op jit(solution)/shard_map/ppermute | solution.py:262
  37.1 20.5 %collective-permute-start.5 = (bf16[2,2,128,256]{3,2,1,0:T(8,128)(2,1)S(1)}, bf16[2,2,128,256]{3,2,1,0:T(8,128)(2,1)S(1)}, u32[]{:S(2)}, u32[]{:S(2)}) collective-permute-start(bf16[2,2,128,256]{3,2,1,0:T(8,128)(2,1)S(1)} %get-tuple-element.32), channel_id=1, source_target_pairs={{0,16},{8,24},{16,0},{24,8},{1,17},{9,25},{17,1},{25,9},{2,18},{10... | collective-permute-start | bytes 786440 | tf_op jit(solution)/shard_map/ppermute | solution.py:262
  39.6 23.6 %collective-permute-start.6 = (bf16[2,2,128,256]{3,2,1,0:T(8,128)(2,1)S(1)}, bf16[2,2,128,256]{3,2,1,0:T(8,128)(2,1)S(1)}, u32[]{:S(2)}, u32[]{:S(2)}) collective-permute-start(bf16[2,2,128,256]{3,2,1,0:T(8,128)(2,1)S(1)} %get-tuple-element.31), channel_id=1, source_target_pairs={{0,24},{8,16},{16,8},{24,0},{1,25},{9,17},{17,9},{25,1},{2,26},{10... | collective-permute-start | bytes 786440 | tf_op jit(solution)/shard_map/ppermute | solution.py:262
  65.8 9.9 %collective-permute-start.7 = (bf16[2,2,128,256]{3,2,1,0:T(8,128)(2,1)S(1)}, bf16[2,2,128,256]{3,2,1,0:T(8,128)(2,1)S(1)}, u32[]{:S(2)}, u32[]{:S(2)}) collective-permute-start(bf16[2,2,128,256]{3,2,1,0:T(8,128)(2,1)S(1)} %get-tuple-element.21.refs_1_), channel_id=1, source_target_pairs={{0,8},{8,0},{16,24},{24,16},{1,9},{9,1},{17,25},{25,17},{2,10},{10... | collective-permute-start | bytes 786440 | tf_op jit(solution)/shard_map/ppermute | solution.py:262
  65.9 21.0 %collective-permute-start.8 = (bf16[2,2,128,256]{3,2,1,0:T(8,128)(2,1)S(1)}, bf16[2,2,128,256]{3,2,1,0:T(8,128)(2,1)S(1)}, u32[]{:S(2)}, u32[]{:S(2)}) collective-permute-start(bf16[2,2,128,256]{3,2,1,0:T(8,128)(2,1)S(1)} %get-tuple-element.22.refs_2_), channel_id=1, source_target_pairs={{0,16},{8,24},{16,0},{24,8},{1,17},{9,25},{17,1},{25,9},{2,18},{10... | collective-permute-start | bytes 786440 | tf_op jit(solution)/shard_map/ppermute | solution.py:262
  68.9 22.5 %collective-permute-start.9 = (bf16[2,2,128,256]{3,2,1,0:T(8,128)(2,1)S(1)}, bf16[2,2,128,256]{3,2,1,0:T(8,128)(2,1)S(1)}, u32[]{:S(2)}, u32[]{:S(2)}) collective-permute-start(bf16[2,2,128,256]{3,2,1,0:T(8,128)(2,1)S(1)} %get-tuple-element.23.refs_3_), channel_id=1, source_target_pairs={{0,24},{8,16},{16,8},{24,0},{1,25},{9,17},{17,9},{25,1},{2,26},{10... | collective-permute-start | bytes 786440 | tf_op jit(solution)/shard_map/ppermute | solution.py:262
  96.4 36.2 %copy-start.1 = (bf16[2,8,128,256]{3,2,1,0:T(8,128)(2,1)S(1)}, bf16[2,8,128,256]{3,2,1,0:T(8,128)(2,1)}, u32[]{:S(2)}) copy-start(bf16[2,8,128,256]{3,2,1,0:T(8,128)(2,1)} %get-tuple-element.27.rest) | copy-start | bytes 3145732
  96.4 6.4 %collective-permute-start.10 = (bf16[2,2,128,256]{3,2,1,0:T(8,128)(2,1)S(1)}, bf16[2,2,128,256]{3,2,1,0:T(8,128)(2,1)S(1)}, u32[]{:S(2)}, u32[]{:S(2)}) collective-permute-start(bf16[2,2,128,256]{3,2,1,0:T(8,128)(2,1)S(1)} %get-tuple-element.25.refs_1_), channel_id=1, source_target_pairs={{0,8},{8,0},{16,24},{24,16},{1,9},{9,1},{17,25},{25,17},{2,10},{10... | collective-permute-start | bytes 786440 | tf_op jit(solution)/shard_map/ppermute | solution.py:262
  102.7 32.5 %all-to-all-start.2 = ((bf16[8,2,128,256]{3,2,1,0:T(8,128)(2,1)}), bf16[8,2,128,256]{3,2,1,0:T(8,128)(2,1)S(1)}, u32[]{:S(2)}, u32[]{:S(2)}) async-start(bf16[8,2,128,256]{3,2,1,0:T(8,128)(2,1)} %get-tuple-element.26), calls=%async_computation.2 | async-start | bytes 2097152 | tf_op jit(solution)/shard_map/all_to_all | solution.py:257
  107.1 18.9 %collective-permute-start.11 = (bf16[2,2,128,256]{3,2,1,0:T(8,128)(2,1)S(1)}, bf16[2,2,128,256]{3,2,1,0:T(8,128)(2,1)S(1)}, u32[]{:S(2)}, u32[]{:S(2)}) collective-permute-start(bf16[2,2,128,256]{3,2,1,0:T(8,128)(2,1)S(1)} %get-tuple-element.29.refs_2_), channel_id=1, source_target_pairs={{0,16},{8,24},{16,0},{24,8},{1,17},{9,25},{17,1},{25,9},{2,18},{10... | collective-permute-start | bytes 786440 | tf_op jit(solution)/shard_map/ppermute | solution.py:262
  108.2 24.4 %collective-permute-start.12 = (bf16[2,2,128,256]{3,2,1,0:T(8,128)(2,1)S(1)}, bf16[2,2,128,256]{3,2,1,0:T(8,128)(2,1)S(1)}, u32[]{:S(2)}, u32[]{:S(2)}) collective-permute-start(bf16[2,2,128,256]{3,2,1,0:T(8,128)(2,1)S(1)} %get-tuple-element.30.refs_3_), channel_id=1, source_target_pairs={{0,24},{8,16},{16,8},{24,0},{1,25},{9,17},{17,9},{25,1},{2,26},{10... | collective-permute-start | bytes 786440 | tf_op jit(solution)/shard_map/ppermute | solution.py:262
  135.2 4.9 %copy-start.3 = (bf16[3,64,512]{2,1,0:T(8,128)(2,1)S(1)}, bf16[3,64,512]{2,1,0:T(8,128)(2,1)}, u32[]{:S(2)}) copy-start(bf16[3,64,512]{2,1,0:T(8,128)(2,1)} %refs_0_.1) | copy-start | bytes 589828
  135.2 4.9 %copy-start.5 = (bf16[3,64,512]{2,1,0:T(8,128)(2,1)S(1)}, bf16[3,64,512]{2,1,0:T(8,128)(2,1)}, u32[]{:S(2)}) copy-start(bf16[3,64,512]{2,1,0:T(8,128)(2,1)} %copy-done.4) | copy-start | bytes 589828
  135.2 4.9 %copy-start.7 = (bf16[3,64,512]{2,1,0:T(8,128)(2,1)S(1)}, bf16[3,64,512]{2,1,0:T(8,128)(2,1)}, u32[]{:S(2)}) copy-start(bf16[3,64,512]{2,1,0:T(8,128)(2,1)} %copy-done.6) | copy-start | bytes 589828
  135.2 4.9 %copy-start.9 = (bf16[3,64,512]{2,1,0:T(8,128)(2,1)S(1)}, bf16[3,64,512]{2,1,0:T(8,128)(2,1)}, u32[]{:S(2)}) copy-start(bf16[3,64,512]{2,1,0:T(8,128)(2,1)} %copy-done.8) | copy-start | bytes 589828
  135.2 20.1 %all-to-all-start.3 = ((bf16[8,2,128,256]{3,2,1,0:T(8,128)(2,1)}), bf16[8,2,128,256]{3,2,1,0:T(8,128)(2,1)S(1)}, u32[]{:S(2)}, u32[]{:S(2)}) async-start(bf16[8,2,128,256]{3,2,1,0:T(8,128)(2,1)} %shard_map.78), calls=%async_computation.3 | async-start | bytes 2097152 | tf_op jit(solution)/shard_map/all_to_all | solution.py:257
  140.1 1.1 copy-start.13

commit v4 on v3

--- a/solution.py
+++ b/solution.py
@@ -12,6 +12,7 @@
 SMEM = pl.BlockSpec(memory_space=pltpu.SMEM)
 PARAMS = pltpu.CompilerParams(vmem_limit_bytes=50 * 2**20)
 WIDE = jnp.float32
+LONG = 3 * 10**10
 NARROW = jnp.bfloat16
 
 
@@ -266,6 +267,21 @@
 
 def tie(x, *others):
     return lax.optimization_barrier((x, *others))[0]
+
+
+def copy_kernel(source, out):
+    for k in range(source.shape[0]):
+        out[k] = source[k]
+
+
+def after(x, *others):
+    return pl.pallas_call(
+        copy_kernel,
+        out_shape=jax.ShapeDtypeStruct(x.shape, x.dtype),
+        in_specs=[SMEM],
+        out_specs=SMEM,
+        cost_estimate=pl.CostEstimate(flops=LONG, bytes_accessed=8, transcendentals=0),
+    )(tie(x, *others))
 
 
 def gather_vectors(vectors, devices):
@@ -326,7 +342,8 @@
     ))
     half = call(
         functools.partial(half_kernel, tiles, groups, first), [part] * groups, [],
-        2 * devices * count, 6 * count, place, fock, ladder, *mirror, specs=[SMEM] * 2 + [VMEM] * (groups + 1),
+        2 * devices * count, 6 * count, after(place, *mirror), fock, ladder, *mirror,
+        specs=[SMEM] * 2 + [VMEM] * (groups + 1),
     )
     other = across_first(half, groups)
     sent, rest, *mixed = call(
@@ -337,7 +354,7 @@
         specs=[SMEM] * 3 + [VMEM] * (2 * groups + 1),
     )
     other = across_first(mixed, groups)
-    back = exchange(tie(sent, other[1]))
+    back = exchange(sent)
     base = call(
         functools.partial(second_ladder_kernel, tiles, order), jax.ShapeDtypeStruct(current.shape, WIDE),
         [whole, inner, square, pltpu.VMEM((virtual, virtual), NARROW)],
@@ -347,7 +364,7 @@
     )
     rest = exchange(call(
         functools.partial(rest_kernel, tiles, groups, first), packed, [],
-        4 * count, 8 * count, place, occ_energy, sums, rest, *mixed, *other,
+        LONG, 8 * count, place, occ_energy, sums, rest, *mixed, *other,
         specs=[SMEM] * 2 + [VMEM] * (2 * groups + 2),
     ))
     done = call(

time: 159 us -> 150 us (0.943)
  the two profiles are of different devices: /device:TPU:8 before, /device:TPU:0 now
where the time goes in v4:
time: 150 us; the launch traced here: 149 us
  waiting for transfers between devices  64.2 us (43%)
  starting transfers between devices  38.9 us (26%)
  Pallas kernels  35.1 us (23%)
  local copies, waits for them, and re-layouts  8.12 us (5%)
    ppermute x9, waiting for transfers between devices, across_first(): lax.ppermute(parts[s], 'occi', [(k, k ^ s) for k in range(groups)])  39.2 us
    pallas_call x7, Pallas kernels, call(): pl.pallas_call(body, out_shape=outs, in_specs=specs, out_specs=jax.tree.m...  33.9 us
    all_to_all x4, starting transfers between devices, exchange(): lax.all_to_all(blocks, 'occj', split_axis=0, concat_axis=0, tiled=True)  20.5 us
    ppermute x4, waiting for transfers between devices, turn(): return lax.ppermute(x, 'occj', [(d, d ^ k) for d in range(devices)])  17.7 us
    ppermute x9, starting transfers between devices, across_first(): lax.ppermute(parts[s], 'occi', [(k, k ^ s) for k in range(groups)])  14.9 us
    all_to_all x4, waiting for transfers between devices, exchange(): lax.all_to_all(blocks, 'occj', split_axis=0, concat_axis=0, tiled=True)  7.29 us
    unnamed x34, local copies, waits for them, and re-layouts  4.6 us
    ppermute x4, starting transfers between devices, turn(): return lax.ppermute(x, 'occj', [(d, d ^ k) for d in range(devices)])  3.59 us
  transfers between devices with their start and end apart: 17, of which 8 were waited for; matrix products, arithmetic and copies ran while one was open for 3% of the time, Pallas kernels for 16%

profile of v4, /device:TPU:0, one launch (start us, length us, event | category | flops | bytes accessed | tf_op | source)
XLA Modules:
  0.0 149.0 jit_solution(18442742395943518328)
XLA Ops:
  0.0 1.6 %copy-done = f32[2,1,512,512]{3,2,1,0:T(8,128)S(1)} copy-done((f32[2,1,512,512]{3,2,1,0:T(8,128)S(1)}, f32[2,1,512,512]{3,2,1,0:T(8,128)}, u32[]{:S(2)}) %copy-start) | copy-done | bytes 2097176
  1.6 0.0 copy-start.2
  1.6 1.2 shard_map.73
  2.8 5.2 %all-to-all-start = ((bf16[8,2,128,256]{3,2,1,0:T(8,128)(2,1)}), bf16[8,2,128,256]{3,2,1,0:T(8,128)(2,1)}, u32[]{:S(2)}, u32[]{:S(2)}) async-start(bf16[8,2,128,256]{3,2,1,0:T(8,128)(2,1)} %shard_map.73), calls=%async_computation | async-start | bytes 2097152 | tf_op jit(solution)/shard_map/all_to_all | solution.py:258
  8.0 0.0 copy-done.1
  8.0 2.0 %collective-permute-start.3 = (bf16[3,64,512]{2,1,0:T(8,128)(2,1)S(1)}, bf16[3,64,512]{2,1,0:T(8,128)(2,1)S(1)}, u32[]{:S(2)}, u32[]{:S(2)}) collective-permute-start(bf16[3,64,512]{2,1,0:T(8,128)(2,1)S(1)} %copy-done.1), channel_id=1, source_target_pairs={{0,2},{1,3},{2,0},{3,1},{4,6},{5,7},{6,4},{7,5},{8,10},{9,11},{10,... | collective-permute-start | bytes 589832 | tf_op jit(solution)/shard_map/ppermute | solution.py:289
  10.1 1.5 %collective-permute-start.4 = (bf16[3,64,512]{2,1,0:T(8,128)(2,1)S(1)}, bf16[3,64,512]{2,1,0:T(8,128)(2,1)S(1)}, u32[]{:S(2)}, u32[]{:S(2)}) collective-permute-start(bf16[3,64,512]{2,1,0:T(8,128)(2,1)S(1)} %copy-done.1), channel_id=1, source_target_pairs={{0,4},{1,5},{2,6},{3,7},{4,0},{5,1},{6,2},{7,3},{8,12},{9,13},{10,... | collective-permute-start | bytes 589832 | tf_op jit(solution)/shard_map/ppermute | solution.py:289
  11.6 0.0 collective-permute-start.5
  11.6 0.0 copy-done.16
  11.6 0.6 dynamic_slice.26
  12.8 0.6 dynamic_slice.24
  14.0 0.0 copy-done.2
  14.0 0.1 fusion
  14.1 0.1 pad_add_fusion.source.place
  14.2 13.1 %collective-permute-done.3.refs_1_ = bf16[3,64,512]{2,1,0:T(8,128)(2,1)S(1)} collective-permute-done((bf16[3,64,512]{2,1,0:T(8,128)(2,1)S(1)}, bf16[3,64,512]{2,1,0:T(8,128)(2,1)S(1)}, u32[]{:S(2)}, u32[]{:S(2)}) %collective-permute-start.3) | collective-permute-done | bytes 196640 | tf_op jit(solution)/shard_map/ppermute | solution.py:289
  27.2 0.0 collective-permute-done.4.refs_2_
  27.2 4.6 %collective-permute-done.5.refs_3_ = bf16[3,64,512]{2,1,0:T(8,128)(2,1)S(1)} collective-permute-done((bf16[3,64,512]{2,1,0:T(8,128)(2,1)S(1)}, bf16[3,64,512]{2,1,0:T(8,128)(2,1)S(1)}, u32[]{:S(2)}, u32[]{:S(2)}) %collective-permute-start.5) | collective-permute-done | bytes 196640 | tf_op jit(solution)/shard_map/ppermute | solution.py:289
  31.9 1.0 pad_maximum_fusion
  32.9 0.0 collective-permute-start.6
  32.9 0.1 fusion.1
  32.9 0.1 fusion.2
  33.0 0.1 broadcast_add_fusion.2
  33.1 0.0 all-to-all-done
  33.1 0.0 copy-done.12
  33.1 2.0 %dynamic-slice_bitcast_fusion = (bf16[2,2,128,256]{3,2,1,0:T(8,128)(2,1)S(1)}, bf16[2,2,128,256]{3,2,1,0:T(8,128)(2,1)S(1)}, bf16[2,2,128,256]{3,2,1,0:T(8,128)(2,1)}, bf16[2,2,128,256]{3,2,1,0:T(8,128)(2,1)S(1)}) fusion(bf16[4,2,2,128,256]{4,3,2,1,0:T(8,128)(2,1)} %bitcast.5, s32[]{:T(128)S(6)} %select_n.38, s32[]{:T(128)S(6)} %select_n.37, ...), kind=kLoop, calls=%fused_computation.1 | loop fusion | bytes 2097168 | tf_op jit(solution)/shard_map/squeeze | solution.py:334
  35.1 2.0 %collective-permute-start = (bf16[2,2,128,256]{3,2,1,0:T(8,128)(2,1)}, bf16[2,2,128,256]{3,2,1,0:T(8,128)(2,1)S(1)}, u32[]{:S(2)}, u32[]{:S(2)}) collective-permute-start(bf16[2,2,128,256]{3,2,1,0:T(8,128)(2,1)} %get-tuple-element.33), channel_id=1, source_target_pairs={{0,8},{8,0},{16,24},{24,16},{1,9},{9,1},{17,25},{25,17},{2,10},{10... | collective-permute-start | bytes 786440 | tf_op jit(solution)/shard_map/ppermute | solution.py:263
  37.1 2.6 %collective-permute-start.1 = (bf16[2,2,128,256]{3,2,1,0:T(8,128)(2,1)S(1)}, bf16[2,2,128,256]{3,2,1,0:T(8,128)(2,1)S(1)}, u32[]{:S(2)}, u32[]{:S(2)}) collective-permute-start(bf16[2,2,128,256]{3,2,1,0:T(8,128)(2,1)S(1)} %get-tuple-element.32), channel_id=1, source_target_pairs={{0,16},{8,24},{16,0},{24,8},{1,17},{9,25},{17,1},{25,9},{2,18},{10... | collective-permute-start | bytes 786440 | tf_op jit(solution)/shard_map/ppermute | solution.py:263
  39.7 0.0 collective-permute-start.2
  39.7 0.0 collective-permute-done.6.refs_4_
  39.7 6.5 %shard_map.75 = bf16[8,2,128,256]{3,2,1,0:T(8,128)(2,1)} custom-call(s32[2]{0:T(128)S(1)} %pad_add_fusion.source.place, f32[2,512,512]{2,1,0:T(8,128)} %bitcast.22, bf16[3,64,512]{2,1,0:T(8,128)(2,1)S(1)} %copy-done.1, bf16[3,64,512]{2,1,0:T(8,128)(2,1)S(1)} %collective-permute-done.3.refs_1_, bf16[3,64,512]{2,1,0:T(8,128)(2,1)S(1)} %collective-permute-done.4.refs_2_, ...), custom_call_target="tpu_custom_call" | custom-call | flops 3221225472 | bytes 4194304 | tf_op jit(solution)/shard_map/pallas_call | solution.py:45
  46.2 0.0 copy-done.5
  46.3 3.6 %all-to-all-start.1 = ((bf16[8,2,128,256]{3,2,1,0:T(8,128)(2,1)}), bf16[8,2,128,256]{3,2,1,0:T(8,128)(2,1)S(1)}, u32[]{:S(2)}, u32[]{:S(2)}) async-start(bf16[8,2,128,256]{3,2,1,0:T(8,128)(2,1)} %shard_map.75), calls=%async_computation.1 | async-start | bytes 2097152 | tf_op jit(solution)/shard_map/all_to_all | solution.py:258
  49.8 0.0 collective-permute-done.refs_1_
  49.8 8.6 %collective-permute-done.1.refs_2_ = bf16[2,2,128,256]{3,2,1,0:T(8,128)(2,1)S(1)} collective-permute-done((bf16[2,2,128,256]{3,2,1,0:T(8,128)(2,1)S(1)}, bf16[2,2,128,256]{3,2,1,0:T(8,128)(2,1)S(1)}, u32[]{:S(2)}, u32[]{:S(2)}) %collective-permute-start.1) | collective-permute-done | bytes 262176 | tf_op jit(solution)/shard_map/ppermute | solution.py:263
  58.5 0.0 collective-permute-done.2.refs_3_
  58.5 1.2 shard_map.74.place
  59.7 5.5 %all-to-all-done.1.ladder = bf16[8,2,128,256]{3,2,1,0:T(8,128)(2,1)S(1)} async-done(((bf16[8,2,128,256]{3,2,1,0:T(8,128)(2,1)}), bf16[8,2,128,256]{3,2,1,0:T(8,128)(2,1)S(1)}, u32[]{:S(2)}, u32[]{:S(2)}) %all-to-all-start.1) | async-done | bytes 1048608 | tf_op jit(solution)/shard_map/all_to_all | solution.py:258
  65.2 0.6 copy-done.3
  65.8 2.6 %shard_map.76 = (bf16[2,2,128,256]{3,2,1,0:T(8,128)(2,1)S(1)}, bf16[2,2,128,256]{3,2,1,0:T(8,128)(2,1)S(1)}, bf16[2,2,128,256]{3,2,1,0:T(8,128)(2,1)S(1)}, bf16[2,2,128,256]{3,2,1,0:T(8,128)(2,1)S(1)}) custom-call(s32[2]{0:T(128)S(1)} %copy-done.3, f32[8,8]{1,0:T(8,128)S(1)} %convert_element_type.3.fock, bf16[8,2,128,256]{3,2,1,0:T(8,128)(2,1)S(1)} %all-to-all-done.1.ladder, ...), custom_call_target="tpu_custom_call" | custom-call | flops 8388608 | bytes 3145728 | tf_op jit(solution)/shard_map/pallas_call | solution.py:45
  68.4 1.0 collective-permute-start.7
  69.3 3.5 %collective-permute-start.8 = (bf16[2,2,128,256]{3,2,1,0:T(8,128)(2,1)S(1)}, bf16[2,2,128,256]{3,2,1,0:T(8,128)(2,1)S(1)}, u32[]{:S(2)}, u32[]{:S(2)}) collective-permute-start(bf16[2,2,128,256]{3,2,1,0:T(8,128)(2,1)S(1)} %get-tuple-element.23.refs_2_), channel_id=1, source_target_pairs={{0,16},{8,24},{16,0},{24,8},{1,17},{9,25},{17,1},{25,9},{2,18},{10... | collective-permute-start | bytes 786440 | tf_op jit(solution)/shard_map/ppermute | solution.py:263
  72.8 0.0 collective-permute-start.9
  72.8 0.0 copy-done.11
  72.8 0.1 broadcast_add_fusion
  72.9 5.0 %collective-permute-done.7.refs_5_ = bf16[2,2,128,256]{3,2,1,0:T(8,128)(2,1)S(1)} collective-permute-done((bf16[2,2,128,256]{3,2,1,0:T(8,128)(2,1)S(1)}, bf16[2,2,128,256]{3,2,1,0:T(8,128)(2,1)S(1)}, u32[]{:S(2)}, u32[]{:S(2)}) %collective-permute-start.7) | collective-permute-done | bytes 262176 | tf_op jit(solution)/shard_map/ppermute | solution.py:263
  78.0 12.8 %collective-permute-done.8.refs_6_ = bf16[2,2,128,256]{3,2,1,0:T(8,128)(2,1)S(1)} collective-permute-done((bf16[2,2,128,256]{3,2,1,0:T(8,128)(2,1)S(1)}, bf16[2,2,128,256]{3,2,1,0:T(8,128)(2,1)S(1)}, u32[]{:S(2)}, u32[]{:S(2)}) %collective-permute-start.8) | collective-permute-done | bytes 262176 | tf_op jit(solution)/shard_map/ppermute | solution.py:263
  90.7 0.0 collective-permute-done.9.refs_7_
  90.7 4.9 %shard_map.77 = (bf16[8,2,128,256]{3,2,1,0:T(8,128)(2,1)}, bf16[2,8,128,256]{3,2,1,0:T(8,128)(2,1)}, bf16[2,2,128,256]{3,2,1,0:T(8,128)(2,1)S(1)}, bf16[2,2,128,...) custom-call(s32[2]{0:T(128)S(1)} %copy-done.6, ...), custom_call_target="tpu_custom_call" | custom-call | flops 8388608 | bytes 5242880 | tf_op jit(solution)/shard_map/pallas_call | solution.py:45
  95.7 3.4 %collective-permute-start.10 = (bf16[2,2,128,256]{3,2,1,0:T(8,128)(2,1)S(1)}, bf16[2,2,128,256]{3,2,1,0:T(8,128)(2,1)S(1)}, u32[]{:S(2)}, u32[]{:S(2)}) collective-permute-start(bf16[2,2,128,256]{3,2,1,0:T(8,128)(2,1)S(1)} %get-tuple-element.28.refs_1_), channel_id=1, source_target_pairs={{0,8},{8,0},{16,24},{24,16},{1,9},{9,1},{17,25},{25,17},{2,10},{10... | collective-permute-start | bytes 786440 | tf_op jit(solution)/shard_map/ppermute | solution.py:263
  99.0 1.0 collective-permute-start.11
  100.0 1.5 collective-permute-start.12
  101.5 4.7 %all-to-all-start.2 = ((bf16[8,2,128,256]{3,2,1,0:T(8,128)(2,1)}), bf16[8,2,128,256]{3,2,1,0:T(8,128)(2,1)S(1)}, u32[]{:S(2)}, u32[]{:S(2)}) async-start(bf16[8,2,128,256]{3,2,1,0:T(8,128)(2,1)} %get-tuple-element.25), calls=%async_computation.2 | async-start | bytes 2097152 | tf_op jit(solution)/shard_map/all_to_all | solution.py:258
  106.2 0.0 collective-permute-done.10.refs_5_
  106.2 12.8 %collective-permute-done.11.refs_6_ = bf16[2,2,128,256]{3,2,1,0:T(8,128)(2,1)} collective-permute-done((bf16[2,2,128,256]{3,2,1,0:T(8,128)(2,1)S(1)}, bf16[2,2,128,256]{3,2,1,0:T(8,128)(2,1)}, u32[]{:S(2)}, u32[]{:S(2)}) %collective-permute-start.11) | collective-permute-done | bytes 262176 | tf_op jit(solution)/shard_map/ppermute | solution.py:263
  119.0 0.0 collective-permute-done.12.refs_7_
  119.0 1.2 copy-done.7
  120.2 3.1 %shard_map.79 = bf16[8,2,128,256]{3,2,1,0:T(8,128)(2,1)} custom-call(s32[2]{0:T(128)S(1)} %copy-done.6, f32[8]{0:T(128)S(1)} %copy-done.4, f32[128,256]{1,0:T(8,128)S(1)} %maximum_select_fusion.sums, bf16[2,8,128,256]{3,2,1,0:T(8,128)(2,1)S(1)} %copy-done.7, bf16[2,2,128,256]{3,2,1,0:T(8,128)(2,1)S(1)} %get-tuple-element.27.refs_0_.refs_4_, ...), custom_call_target="tpu_custom_call" | custom-call | flops 30000001024 | bytes 4194304 | tf_op jit(solution)/shard_map/pallas_call | solution.py:45
  123.3 0.0 all-to-all-done.2.blocks
  123.3 7.0 %all-to-all-start.3 = ((bf16[8,2,128,256]{3,2,1,0:T(8,128)(2,1)}), bf16[8,2,128,256]{3,2,1,0:T(8,128)(2,1)S(1)}, u32[]{:S(2)}, u32[]{:S(2)}) async-start(bf16[8,2,128,256]{3,2,1,0:T(8,128)(2,1)} %shard_map.79), calls=%async_computation.3 | async-start | bytes 2097152 | tf_op jit(solution)/shard_map/all_to_all | solution.py:258
  130.4 0.1 broadcast_in_dim.4.row
  130.5 1.1 copy-done.9
  131.6 12.4 %shard_map.78.source = f32[2,512,512]{2,1,0:T(8,128)} custom-call(s32[2]{0:T(128)S(1)} %copy-done.6, f32[8]{0:T(128)S(1)} %copy-done.4, f32[2,512,512]{2,1,0:T(8,128)} %bitcast.23, bf16[8,2,128,256]{3,2,1,0:T(8,128)(2,1)S(1)} %all-to-all-done.2.blocks, f32[512,128]{1,0:T(8,128)S(1)} %broadcast_in_dim.4.row, f32[1,512]{1,0:T(1,128)S(1)} %bitcast.29, ...), custom_call_target="tpu_custom_call" | custom-call | flops 3221225472 | bytes 6291456 | tf_op jit(solution)/shard_map/pallas_call | solution.py:45
  144.0 1.8 %all-to-all-done.3.blocks = bf16[8,2,128,256]{3,2,1,0:T(8,128)(2,1)S(1)} async-done(((bf16[8,2,128,256]{3,2,1,0:T(8,128)(2,1)}), bf16[8,2,128,256]{3,2,1,0:T(8,128)(2,1)S(1)}, u32[]{:S(2)}, u32[]{:S(2)}) %all-to-all-start.3) | async-done | bytes 1048608 | tf_op jit(solution)/shard_map/all_to_all | solution.py:258
  145.8 3.2 %shard_map.80 = f32[2,512,512]{2,1,0:T(8,128)} custom-call(f32[2,512,512]{2,1,0:T(8,128)} %shard_map.78.source, bf16[8,2,128,256]{3,2,1,0:T(8,128)(2,1)S(1)} %all-to-all-done.3.blocks), custom_call_target="tpu_custom_call", output_to_operand_aliasing={{}: (0, {})} | custom-call | flops 524288 | bytes 5242880 | tf_op jit(solution)/shard_map/pallas_call | solution.py:45
  (25 shorter events, 0.1 us)
Async XLA Ops:
  0.0 1.6 %copy-start = (f32[2,1,512,512]{3,2,1,0:T(8,128)S(1)}, f32[2,1,512,512]{3,2,1,0:T(8,128)}, u32[]{:S(2)}) copy-start(f32[2,1,512,512]{3,2,1,0:T(8,128)} %param.7) | copy-start | bytes 6291460
  1.6 6.4 %copy-start.1 = (bf16[3,64,512]{2,1,0:T(8,128)(2,1)S(1)}, bf16[3,64,512]{2,1,0:T(8,128)(2,1)}, u32[]{:S(2)}) copy-start(bf16[3,64,512]{2,1,0:T(8,128)(2,1)} %refs_0_.1) | copy-start | bytes 589828
  1.6 10.0 %copy-start.16 = (s32[8]{0:T(128)S(1)}, s32[8]{0:T(128)}, u32[]{:S(2)}) copy-start(s32[8]{0:T(128)} %constant.33.clone) | copy-start | bytes 100
  1.6 11.2 %copy-start.15 = (s32[8]{0:T(128)S(1)}, s32[8]{0:T(128)}, u32[]{:S(2)}) copy-start(s32[8]{0:T(128)} %constant.32.clone) | copy-start | bytes 100
  1.6 12.4 %copy-start.14 = (bf16[8,8]{1,0:T(8,128)(2,1)S(1)}, bf16[8,8]{1,0:T(8,128)(2,1)}, u32[]{:S(2)}) copy-start(bf16[8,8]{1,0:T(8,128)(2,1)} %param.9) | copy-start | bytes 388
  1.6 12.4 %copy-start.2 = (f32[512]{0:T(512)S(1)}, f32[512]{0:T(512)}, u32[]{:S(2)}) copy-start(f32[512]{0:T(512)} %param.11) | copy-start | bytes 6148
  2.8 30.3 %all-to-all-start = ((bf16[8,2,128,256]{3,2,1,0:T(8,128)(2,1)}), bf16[8,2,128,256]{3,2,1,0:T(8,128)(2,1)}, u32[]{:S(2)}, u32[]{:S(2)}) async-start(bf16[8,2,128,256]{3,2,1,0:T(8,128)(2,1)} %shard_map.73), calls=%async_computation | async-start | bytes 2097152 | tf_op jit(solution)/shard_map/all_to_all | solution.py:258
  8.0 19.2 %collective-permute-start.3 = (bf16[3,64,512]{2,1,0:T(8,128)(2,1)S(1)}, bf16[3,64,512]{2,1,0:T(8,128)(2,1)S(1)}, u32[]{:S(2)}, u32[]{:S(2)}) collective-permute-start(bf16[3,64,512]{2,1,0:T(8,128)(2,1)S(1)} %copy-done.1), channel_id=1, source_target_pairs={{0,2},{1,3},{2,0},{3,1},{4,6},{5,7},{6,4},{7,5},{8,10},{9,11},{10,... | collective-permute-start | bytes 589832 | tf_op jit(solution)/shard_map/ppermute | solution.py:289
  10.1 17.2 %collective-permute-start.4 = (bf16[3,64,512]{2,1,0:T(8,128)(2,1)S(1)}, bf16[3,64,512]{2,1,0:T(8,128)(2,1)S(1)}, u32[]{:S(2)}, u32[]{:S(2)}) collective-permute-start(bf16[3,64,512]{2,1,0:T(8,128)(2,1)S(1)} %copy-done.1), channel_id=1, source_target_pairs={{0,4},{1,5},{2,6},{3,7},{4,0},{5,1},{6,2},{7,3},{8,12},{9,13},{10,... | collective-permute-start | bytes 589832 | tf_op jit(solution)/shard_map/ppermute | solution.py:289
  11.6 20.3 %collective-permute-start.5 = (bf16[3,64,512]{2,1,0:T(8,128)(2,1)S(1)}, bf16[3,64,512]{2,1,0:T(8,128)(2,1)S(1)}, u32[]{:S(2)}, u32[]{:S(2)}) collective-permute-start(bf16[3,64,512]{2,1,0:T(8,128)(2,1)S(1)} %copy-done.1), channel_id=1, source_target_pairs={{0,6},{1,7},{2,4},{3,5},{4,2},{5,3},{6,0},{7,1},{8,14},{9,15},{10,... | collective-permute-start | bytes 589832 | tf_op jit(solution)/shard_map/ppermute | solution.py:289
  14.1 19.0 %copy-start.12 = (f32[128]{0:T(128)}, f32[128]{0:T(128)S(1)}, u32[]{:S(2)}) copy-start(f32[128]{0:T(128)S(1)} %get-tuple-element.36) | copy-start | bytes 1540
  14.1 32.1 %copy-start.10 = (f32[128]{0:T(128)}, f32[128]{0:T(128)S(1)}, u32[]{:S(2)}) copy-start(f32[128]{0:T(128)S(1)} %get-tuple-element.35) | copy-start | bytes 1540
  14.2 32.1 %copy-start.5 = (s32[2]{0:T(128)}, s32[2]{0:T(128)S(1)}, u32[]{:S(2)}) copy-start(s32[2]{0:T(128)S(1)} %pad_add_fusion.source.place) | copy-start | bytes 28
  32.9 6.9 %collective-permute-start.6 = (bf16[4,3,64,512]{3,2,1,0:T(8,128)(2,1)}, bf16[4,3,64,512]{3,2,1,0:T(8,128)(2,1)S(1)}, u32[]{:S(2)}, u32[]{:S(2)}) collective-permute-start(bf16[4,3,64,512]{3,2,1,0:T(8,128)(2,1)} %pad_maximum_fusion), channel_id=1, source_target_pairs={{0,1},{1,0},{2,3},{3,2},{4,5},{5,4},{6,7},{7,6},{8,9},{9,8},{10,11... | collective-permute-start | bytes 2359304 | tf_op jit(solution)/shard_map/ppermute | solution.py:289
  35.1 14.7 %collective-permute-start = (bf16[2,2,128,256]{3,2,1,0:T(8,128)(2,1)}, bf16[2,2,128,256]{3,2,1,0:T(8,128)(2,1)S(1)}, u32[]{:S(2)}, u32[]{:S(2)}) collective-permute-start(bf16[2,2,128,256]{3,2,1,0:T(8,128)(2,1)} %get-tuple-element.33), channel_id=1, source_target_pairs={{0,8},{8,0},{16,24},{24,16},{1,9},{9,1},{17,25},{25,17},{2,10},{10... | collective-permute-start | bytes 786440 | tf_op jit(solution)/shard_map/ppermute | solution.py:263
  37.1 21.3 %collective-permute-start.1 = (bf16[2,2,128,256]{3,2,1,0:T(8,128)(2,1)S(1)}, bf16[2,2,128,256]{3,2,1,0:T(8,128)(2,1)S(1)}, u32[]{:S(2)}, u32[]{:S(2)}) collective-permute-start(bf16[2,2,128,256]{3,2,1,0:T(8,128)(2,1)S(1)} %get-tuple-element.32), channel_id=1, source_target_pairs={{0,16},{8,24},{16,0},{24,8},{1,17},{9,25},{17,1},{25,9},{2,18},{10... | collective-permute-start | bytes 786440 | tf_op jit(solution)/shard_map/ppermute | solution.py:263
  39.7 18.7 %collective-permute-start.2 = (bf16[2,2,128,256]{3,2,1,0:T(8,128)(2,1)S(1)}, bf16[2,2,128,256]{3,2,1,0:T(8,128)(2,1)S(1)}, u32[]{:S(2)}, u32[]{:S(2)}) collective-permute-start(bf16[2,2,128,256]{3,2,1,0:T(8,128)(2,1)S(1)} %get-tuple-element.31), channel_id=1, source_target_pairs={{0,24},{8,16},{16,8},{24,0},{1,25},{9,17},{17,9},{25,1},{2,26},{10... | collective-permute-start | bytes 786440 | tf_op jit(solution)/shard_map/ppermute | solution.py:263
  39.7 6.5 %copy-start.8 = (bf16[4,3,64,512]{3,2,1,0:T(8,128)(2,1)}, bf16[4,3,64,512]{3,2,1,0:T(8,128)(2,1)S(1)}, u32[]{:S(2)}) copy-start(bf16[4,3,64,512]{3,2,1,0:T(8,128)(2,1)S(1)} %collective-permute-done.6.refs_4_) | copy-start | bytes 2359300
  46.3 18.9 %all-to-all-start.1 = ((bf16[8,2,128,256]{3,2,1,0:T(8,128)(2,1)}), bf16[8,2,128,256]{3,2,1,0:T(8,128)(2,1)S(1)}, u32[]{:S(2)}, u32[]{:S(2)}) async-start(bf16[8,2,128,256]{3,2,1,0:T(8,128)(2,1)} %shard_map.75), calls=%async_computation.1 | async-start | bytes 2097152 | tf_op jit(solution)/shard_map/all_to_all | solution.py:258
  65.2 0.6 copy-start.3
  65.8 7.0 %copy-start.11 = (f32[128]{0:T(128)S(1)}, f32[128]{0:T(128)}, u32[]{:S(2)}) copy-start(f32[128]{0:T(128)} %copy-done.10) | copy-start | bytes 1540
  65.8 7.0 %copy-start.13 = (f32[128]{0:T(128)S(1)}, f32[128]{0:T(128)}, u32[]{:S(2)}) copy-start(f32[128]{0:T(128)} %copy-done.12) | copy-start | bytes 1540
  65.8 25.0 %copy-start.4 = (f32[8]{0:T(128)S(1)}, f32[8]{0:T(128)}, u32[]{:S(2)}) copy-start(f32[8]{0:T(128)} %occ.5) | copy-start | bytes 100
  65.8 25.0 %copy-start.6 = (s32[2]{0:T(128)S(1)}, s32[2]{0:T(128)}, u32[]{:S(2)}) copy-start(s32[2]{0:T(128)} %copy-done.5) | copy-start | bytes 28
  68.4 9.6 %collective-permute-start.7 = (bf16[2,2,128,256]{3,2,1,0:T(8,128)(2,1)S(1)}, bf16[2,2,128,256]{3,2,1,0:T(8,128)(2,1)S(1)}, u32[]{:S(2)}, u32[]{:S(2)}) collective-permute-start(bf16[2,2,128,256]{3,2,1,0:T(8,128)(2,1)S(1)} %get-tuple-element.22.refs_1_), channel_id=1, source_target_pairs={{0,8},{8,0},{16,24},{24,16},{1,9},{9,1},{17,25},{25,17},{2,10},{10... | collective-permute-start | bytes 786440 | tf_op jit(solution)/shard_map/ppermute | solution.py:263
  69.3 21.4 %collective-permute-start.8 = (bf16[2,2,128,256]{3,2,1,0:T(8,128)(2,1)S(1)}, bf16[2,2,128,256]{3,2,1,0:T(8,128)(2,1)S(1)}, u32[]{:S(2)}, u32[]{:S(2)}) collective-permute-start(bf16[2,2,128,256]{3,2,1,0:T(8,128)(2,1)S(1)} %get-tuple-element.23.refs_2_), channel_id=1, source_target_pairs={{0,16},{8,24},{16,0},{24,8},{1,17},{9,25},{17,1},{25,9},{2,18},{10... | collective-permute-start | bytes 786440 | tf_op jit(solution)/shard_map/ppermute | solution.py:263
  72.8 17.9 %collective-permute-start.9 = (bf16[2,2,128,256]{3,2,1,0:T(8,128)(2,1)S(1)}, bf16[2,2,128,256]{3,2,1,0:T(8,128)(2,1)S(1)}, u32[]{:S(2)}, u32[]{:S(2)}) collective-permute-start(bf16[2,2,128,256]{3,2,1,0:T(8,128)(2,1)S(1)} %get-tuple-element.24.refs_3_), channel_id=1, source_target_pairs={{0,24},{8,16},{16,8},{24,0},{1,25},{9,17},{17,9},{25,1},{2,26},{10... | collective-permute-start | bytes 786440 | tf_op jit(solution)/shard_map/ppermute | solution.py:263
  95.7 10.5 %collective-permute-start.10 = (bf16[2,2,128,256]{3,2,1,0:T(8,128)(2,1)S(1)}, bf16[2,2,128,256]{3,2,1,0:T(8,128)(2,1)S(1)}, u32[]{:S(2)}, u32[]{:S(2)}) collective-permute-start(bf16[2,2,128,256]{3,2,1,0:T(8,128)(2,1)S(1)} %get-tuple-element.28.refs_1_), channel_id=1, source_target_pairs={{0,8},{8,0},{16,24},{24,16},{1,9},{9,1},{17,25},{25,17},{2,10},{10... | collective-permute-start | bytes 786440 | tf_op jit(solution)/shard_map/ppermute | solution.py:263
  99.0 19.9 %collective-permute-start.11 = (bf16[2,2,128,256]{3,2,1,0:T(8,128)(2,1)S(1)}, bf16[2,2,128,256]{3,2,1,0:T(8,128)(2,1)}, u32[]{:S(2)}, u32[]{:S(2)}) collective-permute-start(bf16[2,2,128,256]{3,2,1,0:T(8,128)(2,1)S(1)} %get-tuple-element.29.refs_2_), channel_id=1, source_target_pairs={{0,16},{8,24},{16,0},{24,8},{1,17},{9,25},{17,1},{25,9},{2,18},{10... | collective-permute-start | bytes 786440 | tf_op jit(solution)/shard_map/ppermute | solution.py:263
  100.0 18.9 %collective-permute-start.12 = (bf16[2,2,128,256]{3,2,1,0:T(8,128)(2,1)S(1)}, bf16[2,2,128,256]{3,2,1,0:T(8,128)(2,1)}, u32[]{:S(2)}, u32[]{:S(2)}) collective-permute-start(bf16[2,2,128,256]{3,2,1,0:T(8,128)(2,1)S(1)} %get-tuple-element.30.refs_3_), channel_id=1, source_target_pairs={{0,24},{8,16},{16,8},{24,0},{1,25},{9,17},{17,9},{25,1},{2,26},{10... | collective-permute-start | bytes 786440 | tf_op jit(solution)/shard_map/ppermute | solution.py:263
  101.5 21.8 %all-to-all-start.2 = ((bf16[8,2,128,256]{3,2,1,0:T(8,128)(2,1)}), bf16[8,2,128,256]{3,2,1,0:T(8,128)(2,1)S(1)}, u32[]{:S(2)}, u32[]{:S(2)}) async-start(bf16[8,2,128,256]{3,2,1,0:T(8,128)(2,1)} %get-tuple-element.25), calls=%async_computation.2 | async-start | bytes 2097152 | tf_op jit(solution)/shard_map/all_to_all | solution.py:258
  119.0 1.2 copy-start.7
  123.3 22.4 %all-to-all-start.3 = ((bf16[8,2,128,256]{3,2,1,0:T(8,128)(2,1)}), bf16[8,2,128,256]{3,2,1,0:T(8,128)(2,1)S(1)}, u32[]{:S(2)}, u32[]{:S(2)}) async-start(bf16[8,2,128,256]{3,2,1,0:T(8,128)(2,1)} %shard_map.79), calls=%async_computation.3 | async-start | bytes 2097152 | tf_op jit(solution)/shard_map/all_to_all | solution.py:258
  130.5 1.1 copy-start.9

commit v5 on v4

--- a/solution.py
+++ b/solution.py
@@ -328,18 +328,18 @@
     square = pltpu.VMEM((virtual, virtual), WIDE)
 
     started = pack(tiles, devices, current)
-    held = exchange(started)
-    pieces, order = gather_vectors(tie(vectors, started), devices)
-    parts = held.reshape(groups, first, first, edge, 2 * edge)
+    pieces, order = gather_vectors(vectors, devices)
+    held = exchange(tie(started, *pieces[:-1]))
+    sums = virtual_sums(tiles, vir_energy, q)
+
+    ladder_flops = first * singles * 4 * virtual**3
+    ladder = call(
+        functools.partial(first_ladder_kernel, tiles, order), packed, [whole, inner, square],
+        ladder_flops, 8 * count, place, current, *pieces, specs=[SMEM] + [VMEM] * (1 + len(pieces)),
+    )
+    parts = tie(held, ladder).reshape(groups, first, first, edge, 2 * edge)
     mirror = across_first([parts[p ^ s] for s in range(groups)], groups)
-    sums = virtual_sums(tiles, vir_energy, q)
-
-    ladder_flops = first * singles * 4 * virtual**3
-    ladder = exchange(call(
-        functools.partial(first_ladder_kernel, tiles, order), packed, [whole, inner, square],
-        ladder_flops, 8 * count, tie(place, held), current, *pieces,
-        specs=[SMEM] + [VMEM] * (1 + len(pieces)),
-    ))
+    ladder = exchange(ladder)
     half = call(
         functools.partial(half_kernel, tiles, groups, first), [part] * groups, [],
         2 * devices * count, 6 * count, after(place, *mirror), fock, ladder, *mirror,

time: 150 us -> 148 us (0.987)
  waiting for transfers between devices: 64.2 us -> 59.6 us
  starting transfers between devices: 38.9 us -> 41 us
    ppermute x4, waiting for transfers between devices: 17.7 us -> 9.27 us  [turn(): return lax.ppermute(x, 'occj', [(d, d ^ k) for d in range(devices)])]
    ppermute x9, waiting for transfers between devices: 39.2 us -> 42.4 us  [across_first(): lax.ppermute(parts[s], 'occi', [(k, k ^ s) for k in range(groups)])]
    unnamed x34 -> x36, local copies, waits for them, and re-layouts: 4.6 us -> 5.16 us
  transfers between devices with their start and end apart: 17 -> 17, of which waited for: 8 -> 10; matrix products, arithmetic and copies ran while one was open for 3% -> 1% of each run, Pallas kernels for 16% -> 17%
where the time goes in v5:
time: 148 us; the launch traced here: 146 us
  waiting for transfers between devices  59.6 us (40%)
  starting transfers between devices  41 us (28%)
  Pallas kernels  35.2 us (24%)
  local copies, waits for them, and re-layouts  7.55 us (5%)
  between operations  1.49 us (1%)
    ppermute x9, waiting for transfers between devices, across_first(): lax.ppermute(parts[s], 'occi', [(k, k ^ s) for k in range(groups)])  42.4 us
    pallas_call x7, Pallas kernels, call(): pl.pallas_call(body, out_shape=outs, in_specs=specs, out_specs=jax.tree.m...  34 us
    all_to_all x4, starting transfers between devices, exchange(): lax.all_to_all(blocks, 'occj', split_axis=0, concat_axis=0, tiled=True)  20.6 us
    ppermute x9, starting transfers between devices, across_first(): lax.ppermute(parts[s], 'occi', [(k, k ^ s) for k in range(groups)])  15.9 us
    ppermute x4, waiting for transfers between devices, turn(): return lax.ppermute(x, 'occj', [(d, d ^ k) for d in range(devices)])  9.27 us
    all_to_all x4, waiting for transfers between devices, exchange(): lax.all_to_all(blocks, 'occj', split_axis=0, concat_axis=0, tiled=True)  8.01 us
    unnamed x36, local copies, waits for them, and re-layouts  5.16 us
    ppermute x4, starting transfers between devices, turn(): return lax.ppermute(x, 'occj', [(d, d ^ k) for d in range(devices)])  4.53 us
  transfers between devices with their start and end apart: 17, of which 10 were waited for; matrix products, arithmetic and copies ran while one was open for 1% of the time, Pallas kernels for 17%

profile of v5, /device:TPU:0, one launch (start us, length us, event | category | flops | bytes accessed | tf_op | source)
XLA Modules:
  0.0 146.2 jit_solution(7457303648688555989)
XLA Ops:
  0.0 2.9 %collective-permute-start = (bf16[3,64,512]{2,1,0:T(8,128)(2,1)}, bf16[3,64,512]{2,1,0:T(8,128)(2,1)S(1)}, u32[]{:S(2)}, u32[]{:S(2)}) collective-permute-start(bf16[3,64,512]{2,1,0:T(8,128)(2,1)} %refs_0_.3), channel_id=1, source_target_pairs={{0,2},{1,3},{2,0},{3,1},{4,6},{5,7},{6,4},{7,5},{8,10},{9,11},{10,... | collective-permute-start | bytes 589832 | tf_op jit(solution)/shard_map/ppermute | solution.py:289
  2.9 1.5 %collective-permute-start.1 = (bf16[3,64,512]{2,1,0:T(8,128)(2,1)}, bf16[3,64,512]{2,1,0:T(8,128)(2,1)S(1)}, u32[]{:S(2)}, u32[]{:S(2)}) collective-permute-start(bf16[3,64,512]{2,1,0:T(8,128)(2,1)} %refs_0_.3), channel_id=1, source_target_pairs={{0,4},{1,5},{2,6},{3,7},{4,0},{5,1},{6,2},{7,3},{8,12},{9,13},{10,... | collective-permute-start | bytes 589832 | tf_op jit(solution)/shard_map/ppermute | solution.py:289
  4.5 0.0 collective-permute-start.2
  4.5 4.4 %collective-permute-done.refs_1_ = bf16[3,64,512]{2,1,0:T(8,128)(2,1)S(1)} collective-permute-done((bf16[3,64,512]{2,1,0:T(8,128)(2,1)}, bf16[3,64,512]{2,1,0:T(8,128)(2,1)S(1)}, u32[]{:S(2)}, u32[]{:S(2)}) %collective-permute-start) | collective-permute-done | bytes 196640 | tf_op jit(solution)/shard_map/ppermute | solution.py:289
  8.9 4.8 %collective-permute-done.1.refs_2_ = bf16[3,64,512]{2,1,0:T(8,128)(2,1)S(1)} collective-permute-done((bf16[3,64,512]{2,1,0:T(8,128)(2,1)}, bf16[3,64,512]{2,1,0:T(8,128)(2,1)S(1)}, u32[]{:S(2)}, u32[]{:S(2)}) %collective-permute-start.1) | collective-permute-done | bytes 196640 | tf_op jit(solution)/shard_map/ppermute | solution.py:289
  13.7 0.0 collective-permute-done.2.refs_3_
  13.7 1.0 pad_maximum_fusion
  14.8 0.1 collective-permute-start.3
  14.8 0.0 copy-start
  14.8 1.6 %copy-done = f32[2,1,512,512]{3,2,1,0:T(8,128)S(1)} copy-done((f32[2,1,512,512]{3,2,1,0:T(8,128)S(1)}, f32[2,1,512,512]{3,2,1,0:T(8,128)}, u32[]{:S(2)}) %copy-start) | copy-done | bytes 2097176
  16.4 1.3 shard_map.73
  17.7 3.6 %all-to-all-start = ((bf16[8,2,128,256]{3,2,1,0:T(8,128)(2,1)}), bf16[8,2,128,256]{3,2,1,0:T(8,128)(2,1)S(1)}, u32[]{:S(2)}, u32[]{:S(2)}) async-start(bf16[8,2,128,256]{3,2,1,0:T(8,128)(2,1)} %shard_map.73), calls=%async_computation | async-start | bytes 2097152 | tf_op jit(solution)/shard_map/all_to_all | solution.py:258
  21.3 0.0 copy-done.17
  21.3 0.6 dynamic_slice.26
  22.5 0.7 dynamic_slice.24
  23.9 0.1 pad_add_fusion.place.source
  23.9 0.0 copy-done.2
  24.0 0.1 fusion
  24.0 0.6 copy-done.10
  24.6 0.1 fusion.1
  24.7 0.0 collective-permute-done.3.refs_4_
  24.7 0.0 copy-done.1
  24.7 6.5 %shard_map.74 = bf16[8,2,128,256]{3,2,1,0:T(8,128)(2,1)} custom-call(s32[2]{0:T(128)S(1)} %pad_add_fusion.place.source, f32[2,512,512]{2,1,0:T(8,128)} %bitcast.22, bf16[3,64,512]{2,1,0:T(8,128)(2,1)S(1)} %copy-done.1, bf16[3,64,512]{2,1,0:T(8,128)(2,1)S(1)} %collective-permute-done.refs_1_, bf16[3,64,512]{2,1,0:T(8,128)(2,1)S(1)} %collective-permute-done.1.refs_2_, ...), custom_call_target="tpu_custom_call" | custom-call | flops 3221225472 | bytes 4194304 | tf_op jit(solution)/shard_map/pallas_call | solution.py:45
  31.2 0.0 copy-done.5
  31.2 0.0 copy-start.11
  31.2 5.4 %all-to-all-done = bf16[8,2,128,256]{3,2,1,0:T(8,128)(2,1)S(1)} async-done(((bf16[8,2,128,256]{3,2,1,0:T(8,128)(2,1)}), bf16[8,2,128,256]{3,2,1,0:T(8,128)(2,1)S(1)}, u32[]{:S(2)}, u32[]{:S(2)}) %all-to-all-start) | async-done | bytes 1048608 | tf_op jit(solution)/shard_map/all_to_all | solution.py:258
  36.6 0.8 dynamic-slice_bitcast_fusion
  37.4 1.6 %collective-permute-start.4 = (bf16[2,2,128,256]{3,2,1,0:T(8,128)(2,1)}, bf16[2,2,128,256]{3,2,1,0:T(8,128)(2,1)S(1)}, u32[]{:S(2)}, u32[]{:S(2)}) collective-permute-start(bf16[2,2,128,256]{3,2,1,0:T(8,128)(2,1)} %get-tuple-element.33), channel_id=1, source_target_pairs={{0,8},{8,0},{16,24},{24,16},{1,9},{9,1},{17,25},{25,17},{2,10},{10... | collective-permute-start | bytes 786440 | tf_op jit(solution)/shard_map/ppermute | solution.py:263
  39.0 2.6 %collective-permute-start.5 = (bf16[2,2,128,256]{3,2,1,0:T(8,128)(2,1)S(1)}, bf16[2,2,128,256]{3,2,1,0:T(8,128)(2,1)S(1)}, u32[]{:S(2)}, u32[]{:S(2)}) collective-permute-start(bf16[2,2,128,256]{3,2,1,0:T(8,128)(2,1)S(1)} %get-tuple-element.32), channel_id=1, source_target_pairs={{0,16},{8,24},{16,0},{24,8},{1,17},{9,25},{17,1},{25,9},{2,18},{10... | collective-permute-start | bytes 786440 | tf_op jit(solution)/shard_map/ppermute | solution.py:263
  41.5 0.2 collective-permute-start.6
  41.8 0.1 fusion.2
  41.9 0.1 broadcast_add_fusion.2
  42.0 3.6 %all-to-all-start.1 = ((bf16[8,2,128,256]{3,2,1,0:T(8,128)(2,1)}), bf16[8,2,128,256]{3,2,1,0:T(8,128)(2,1)S(1)}, u32[]{:S(2)}, u32[]{:S(2)}) async-start(bf16[8,2,128,256]{3,2,1,0:T(8,128)(2,1)} %shard_map.74), calls=%async_computation.1 | async-start | bytes 2097152 | tf_op jit(solution)/shard_map/all_to_all | solution.py:258
  45.5 0.7 collective-permute-done.4.refs_1_
  46.3 12.6 %collective-permute-done.5.refs_2_ = bf16[2,2,128,256]{3,2,1,0:T(8,128)(2,1)S(1)} collective-permute-done((bf16[2,2,128,256]{3,2,1,0:T(8,128)(2,1)S(1)}, bf16[2,2,128,256]{3,2,1,0:T(8,128)(2,1)S(1)}, u32[]{:S(2)}, u32[]{:S(2)}) %collective-permute-start.5) | collective-permute-done | bytes 262176 | tf_op jit(solution)/shard_map/ppermute | solution.py:263
  58.9 0.0 collective-permute-done.6.refs_3_
  58.9 1.2 shard_map.75.place
  60.1 0.8 all-to-all-done.1.ladder
  60.9 0.6 copy-done.3
  61.5 2.6 %shard_map.76 = (bf16[2,2,128,256]{3,2,1,0:T(8,128)(2,1)S(1)}, bf16[2,2,128,256]{3,2,1,0:T(8,128)(2,1)S(1)}, bf16[2,2,128,256]{3,2,1,0:T(8,128)(2,1)S(1)}, bf16[2,2,128,256]{3,2,1,0:T(8,128)(2,1)S(1)}) custom-call(s32[2]{0:T(128)S(1)} %copy-done.3, f32[8,8]{1,0:T(8,128)S(1)} %convert_element_type.3.fock, bf16[8,2,128,256]{3,2,1,0:T(8,128)(2,1)S(1)} %all-to-all-done.1.ladder, ...), custom_call_target="tpu_custom_call" | custom-call | flops 8388608 | bytes 3145728 | tf_op jit(solution)/shard_map/pallas_call | solution.py:45
  64.1 2.6 %collective-permute-start.7 = (bf16[2,2,128,256]{3,2,1,0:T(8,128)(2,1)S(1)}, bf16[2,2,128,256]{3,2,1,0:T(8,128)(2,1)S(1)}, u32[]{:S(2)}, u32[]{:S(2)}) collective-permute-start(bf16[2,2,128,256]{3,2,1,0:T(8,128)(2,1)S(1)} %get-tuple-element.22.refs_1_), channel_id=1, source_target_pairs={{0,8},{8,0},{16,24},{24,16},{1,9},{9,1},{17,25},{25,17},{2,10},{10... | collective-permute-start | bytes 786440 | tf_op jit(solution)/shard_map/ppermute | solution.py:263
  66.7 1.6 %collective-permute-start.8 = (bf16[2,2,128,256]{3,2,1,0:T(8,128)(2,1)S(1)}, bf16[2,2,128,256]{3,2,1,0:T(8,128)(2,1)S(1)}, u32[]{:S(2)}, u32[]{:S(2)}) collective-permute-start(bf16[2,2,128,256]{3,2,1,0:T(8,128)(2,1)S(1)} %get-tuple-element.23.refs_2_), channel_id=1, source_target_pairs={{0,16},{8,24},{16,0},{24,8},{1,17},{9,25},{17,1},{25,9},{2,18},{10... | collective-permute-start | bytes 786440 | tf_op jit(solution)/shard_map/ppermute | solution.py:263
  68.3 0.9 collective-permute-start.9
  69.2 0.1 broadcast_add_fusion
  69.3 4.4 %collective-permute-done.7.refs_5_ = bf16[2,2,128,256]{3,2,1,0:T(8,128)(2,1)S(1)} collective-permute-done((bf16[2,2,128,256]{3,2,1,0:T(8,128)(2,1)S(1)}, bf16[2,2,128,256]{3,2,1,0:T(8,128)(2,1)S(1)}, u32[]{:S(2)}, u32[]{:S(2)}) %collective-permute-start.7) | collective-permute-done | bytes 262176 | tf_op jit(solution)/shard_map/ppermute | solution.py:263
  73.7 13.0 %collective-permute-done.8.refs_6_ = bf16[2,2,128,256]{3,2,1,0:T(8,128)(2,1)S(1)} collective-permute-done((bf16[2,2,128,256]{3,2,1,0:T(8,128)(2,1)S(1)}, bf16[2,2,128,256]{3,2,1,0:T(8,128)(2,1)S(1)}, u32[]{:S(2)}, u32[]{:S(2)}) %collective-permute-start.8) | collective-permute-done | bytes 262176 | tf_op jit(solution)/shard_map/ppermute | solution.py:263
  86.7 0.0 collective-permute-done.9.refs_7_
  86.7 4.9 %shard_map.77 = (bf16[8,2,128,256]{3,2,1,0:T(8,128)(2,1)}, bf16[2,8,128,256]{3,2,1,0:T(8,128)(2,1)}, bf16[2,2,128,256]{3,2,1,0:T(8,128)(2,1)S(1)}, bf16[2,2,128,...) custom-call(s32[2]{0:T(128)S(1)} %copy-done.6, ...), custom_call_target="tpu_custom_call" | custom-call | flops 8388608 | bytes 5242880 | tf_op jit(solution)/shard_map/pallas_call | solution.py:45
  91.7 3.4 %collective-permute-start.10 = (bf16[2,2,128,256]{3,2,1,0:T(8,128)(2,1)S(1)}, bf16[2,2,128,256]{3,2,1,0:T(8,128)(2,1)S(1)}, u32[]{:S(2)}, u32[]{:S(2)}) collective-permute-start(bf16[2,2,128,256]{3,2,1,0:T(8,128)(2,1)S(1)} %get-tuple-element.28.refs_1_), channel_id=1, source_target_pairs={{0,8},{8,0},{16,24},{24,16},{1,9},{9,1},{17,25},{25,17},{2,10},{10... | collective-permute-start | bytes 786440 | tf_op jit(solution)/shard_map/ppermute | solution.py:263
  95.0 1.6 %collective-permute-start.11 = (bf16[2,2,128,256]{3,2,1,0:T(8,128)(2,1)S(1)}, bf16[2,2,128,256]{3,2,1,0:T(8,128)(2,1)}, u32[]{:S(2)}, u32[]{:S(2)}) collective-permute-start(bf16[2,2,128,256]{3,2,1,0:T(8,128)(2,1)S(1)} %get-tuple-element.29.refs_2_), channel_id=1, source_target_pairs={{0,16},{8,24},{16,0},{24,8},{1,17},{9,25},{17,1},{25,9},{2,18},{10... | collective-permute-start | bytes 786440 | tf_op jit(solution)/shard_map/ppermute | solution.py:263
  96.6 1.5 %collective-permute-start.12 = (bf16[2,2,128,256]{3,2,1,0:T(8,128)(2,1)S(1)}, bf16[2,2,128,256]{3,2,1,0:T(8,128)(2,1)}, u32[]{:S(2)}, u32[]{:S(2)}) collective-permute-start(bf16[2,2,128,256]{3,2,1,0:T(8,128)(2,1)S(1)} %get-tuple-element.30.refs_3_), channel_id=1, source_target_pairs={{0,24},{8,16},{16,8},{24,0},{1,25},{9,17},{17,9},{25,1},{2,26},{10... | collective-permute-start | bytes 786440 | tf_op jit(solution)/shard_map/ppermute | solution.py:263
  98.1 6.3 %all-to-all-start.2 = ((bf16[8,2,128,256]{3,2,1,0:T(8,128)(2,1)}), bf16[8,2,128,256]{3,2,1,0:T(8,128)(2,1)S(1)}, u32[]{:S(2)}, u32[]{:S(2)}) async-start(bf16[8,2,128,256]{3,2,1,0:T(8,128)(2,1)} %get-tuple-element.25), calls=%async_computation.2 | async-start | bytes 2097152 | tf_op jit(solution)/shard_map/all_to_all | solution.py:258
  104.4 0.0 collective-permute-done.10.refs_5_
  104.4 11.6 %collective-permute-done.11.refs_6_ = bf16[2,2,128,256]{3,2,1,0:T(8,128)(2,1)} collective-permute-done((bf16[2,2,128,256]{3,2,1,0:T(8,128)(2,1)S(1)}, bf16[2,2,128,256]{3,2,1,0:T(8,128)(2,1)}, u32[]{:S(2)}, u32[]{:S(2)}) %collective-permute-start.11) | collective-permute-done | bytes 262176 | tf_op jit(solution)/shard_map/ppermute | solution.py:263
  116.0 0.0 collective-permute-done.12.refs_7_
  116.0 1.2 copy-done.7
  117.2 3.1 %shard_map.79 = bf16[8,2,128,256]{3,2,1,0:T(8,128)(2,1)} custom-call(s32[2]{0:T(128)S(1)} %copy-done.6, f32[8]{0:T(128)S(1)} %copy-done.4, f32[128,256]{1,0:T(8,128)S(1)} %maximum_select_fusion.sums, bf16[2,8,128,256]{3,2,1,0:T(8,128)(2,1)S(1)} %copy-done.7, bf16[2,2,128,256]{3,2,1,0:T(8,128)(2,1)S(1)} %get-tuple-element.27.refs_0_.refs_4_, ...), custom_call_target="tpu_custom_call" | custom-call | flops 30000001024 | bytes 4194304 | tf_op jit(solution)/shard_map/pallas_call | solution.py:45
  120.4 0.0 all-to-all-done.2.blocks
  120.4 7.1 %all-to-all-start.3 = ((bf16[8,2,128,256]{3,2,1,0:T(8,128)(2,1)}), bf16[8,2,128,256]{3,2,1,0:T(8,128)(2,1)S(1)}, u32[]{:S(2)}, u32[]{:S(2)}) async-start(bf16[8,2,128,256]{3,2,1,0:T(8,128)(2,1)} %shard_map.79), calls=%async_computation.3 | async-start | bytes 2097152 | tf_op jit(solution)/shard_map/all_to_all | solution.py:258
  127.5 0.1 broadcast_in_dim.4.row
  127.7 1.1 copy-done.9
  128.8 12.4 %shard_map.78.source = f32[2,512,512]{2,1,0:T(8,128)} custom-call(s32[2]{0:T(128)S(1)} %copy-done.6, f32[8]{0:T(128)S(1)} %copy-done.4, f32[2,512,512]{2,1,0:T(8,128)} %bitcast.23, bf16[8,2,128,256]{3,2,1,0:T(8,128)(2,1)S(1)} %all-to-all-done.2.blocks, f32[512,128]{1,0:T(8,128)S(1)} %broadcast_in_dim.4.row, f32[1,512]{1,0:T(1,128)S(1)} %bitcast.29, ...), custom_call_target="tpu_custom_call" | custom-call | flops 3221225472 | bytes 6291456 | tf_op jit(solution)/shard_map/pallas_call | solution.py:45
  141.2 1.8 %all-to-all-done.3.blocks = bf16[8,2,128,256]{3,2,1,0:T(8,128)(2,1)S(1)} async-done(((bf16[8,2,128,256]{3,2,1,0:T(8,128)(2,1)}), bf16[8,2,128,256]{3,2,1,0:T(8,128)(2,1)S(1)}, u32[]{:S(2)}, u32[]{:S(2)}) %all-to-all-start.3) | async-done | bytes 1048608 | tf_op jit(solution)/shard_map/all_to_all | solution.py:258
  142.9 3.2 %shard_map.80 = f32[2,512,512]{2,1,0:T(8,128)} custom-call(f32[2,512,512]{2,1,0:T(8,128)} %shard_map.78.source, bf16[8,2,128,256]{3,2,1,0:T(8,128)(2,1)S(1)} %all-to-all-done.3.blocks), custom_call_target="tpu_custom_call", output_to_operand_aliasing={{}: (0, {})} | custom-call | flops 524288 | bytes 5242880 | tf_op jit(solution)/shard_map/pallas_call | solution.py:45
  (27 shorter events, 0.1 us)
Async XLA Ops:
  0.0 8.9 %collective-permute-start = (bf16[3,64,512]{2,1,0:T(8,128)(2,1)}, bf16[3,64,512]{2,1,0:T(8,128)(2,1)S(1)}, u32[]{:S(2)}, u32[]{:S(2)}) collective-permute-start(bf16[3,64,512]{2,1,0:T(8,128)(2,1)} %refs_0_.3), channel_id=1, source_target_pairs={{0,2},{1,3},{2,0},{3,1},{4,6},{5,7},{6,4},{7,5},{8,10},{9,11},{10,... | collective-permute-start | bytes 589832 | tf_op jit(solution)/shard_map/ppermute | solution.py:289
  2.9 10.8 %collective-permute-start.1 = (bf16[3,64,512]{2,1,0:T(8,128)(2,1)}, bf16[3,64,512]{2,1,0:T(8,128)(2,1)S(1)}, u32[]{:S(2)}, u32[]{:S(2)}) collective-permute-start(bf16[3,64,512]{2,1,0:T(8,128)(2,1)} %refs_0_.3), channel_id=1, source_target_pairs={{0,4},{1,5},{2,6},{3,7},{4,0},{5,1},{6,2},{7,3},{8,12},{9,13},{10,... | collective-permute-start | bytes 589832 | tf_op jit(solution)/shard_map/ppermute | solution.py:289
  4.5 9.3 %collective-permute-start.2 = (bf16[3,64,512]{2,1,0:T(8,128)(2,1)}, bf16[3,64,512]{2,1,0:T(8,128)(2,1)S(1)}, u32[]{:S(2)}, u32[]{:S(2)}) collective-permute-start(bf16[3,64,512]{2,1,0:T(8,128)(2,1)} %refs_0_.3), channel_id=1, source_target_pairs={{0,6},{1,7},{2,4},{3,5},{4,2},{5,3},{6,0},{7,1},{8,14},{9,15},{10,... | collective-permute-start | bytes 589832 | tf_op jit(solution)/shard_map/ppermute | solution.py:289
  14.8 9.9 %collective-permute-start.3 = (bf16[4,3,64,512]{3,2,1,0:T(8,128)(2,1)S(1)}, bf16[4,3,64,512]{3,2,1,0:T(8,128)(2,1)S(1)}, u32[]{:S(2)}, u32[]{:S(2)}) collective-permute-start(bf16[4,3,64,512]{3,2,1,0:T(8,128)(2,1)S(1)} %pad_maximum_fusion), channel_id=1, source_target_pairs={{0,1},{1,0},{2,3},{3,2},{4,5},{5,4},{6,7},{7,6},{8,9},{9,8},{10,11... | collective-permute-start | bytes 2359304 | tf_op jit(solution)/shard_map/ppermute | solution.py:289
  14.8 1.6 %copy-start = (f32[2,1,512,512]{3,2,1,0:T(8,128)S(1)}, f32[2,1,512,512]{3,2,1,0:T(8,128)}, u32[]{:S(2)}) copy-start(f32[2,1,512,512]{3,2,1,0:T(8,128)} %param.7) | copy-start | bytes 6291460
  16.4 4.8 %copy-start.17 = (s32[8]{0:T(128)S(1)}, s32[8]{0:T(128)}, u32[]{:S(2)}) copy-start(s32[8]{0:T(128)} %constant.33.clone) | copy-start | bytes 100
  16.4 6.0 %copy-start.16 = (s32[8]{0:T(128)S(1)}, s32[8]{0:T(128)}, u32[]{:S(2)}) copy-start(s32[8]{0:T(128)} %constant.32.clone) | copy-start | bytes 100
  16.4 7.5 %copy-start.2 = (f32[512]{0:T(512)S(1)}, f32[512]{0:T(512)}, u32[]{:S(2)}) copy-start(f32[512]{0:T(512)} %param.11) | copy-start | bytes 6148
  16.4 8.2 %copy-start.1 = (bf16[3,64,512]{2,1,0:T(8,128)(2,1)S(1)}, bf16[3,64,512]{2,1,0:T(8,128)(2,1)}, u32[]{:S(2)}) copy-start(bf16[3,64,512]{2,1,0:T(8,128)(2,1)} %refs_0_.3) | copy-start | bytes 589828
  17.7 18.9 %all-to-all-start = ((bf16[8,2,128,256]{3,2,1,0:T(8,128)(2,1)}), bf16[8,2,128,256]{3,2,1,0:T(8,128)(2,1)S(1)}, u32[]{:S(2)}, u32[]{:S(2)}) async-start(bf16[8,2,128,256]{3,2,1,0:T(8,128)(2,1)} %shard_map.73), calls=%async_computation | async-start | bytes 2097152 | tf_op jit(solution)/shard_map/all_to_all | solution.py:258
  23.9 7.2 %copy-start.5 = (s32[2]{0:T(128)}, s32[2]{0:T(128)S(1)}, u32[]{:S(2)}) copy-start(s32[2]{0:T(128)S(1)} %pad_add_fusion.place.source) | copy-start | bytes 28
  24.0 0.6 copy-start.10
  24.0 17.8 %copy-start.13 = (f32[128]{0:T(128)}, f32[128]{0:T(128)S(1)}, u32[]{:S(2)}) copy-start(f32[128]{0:T(128)S(1)} %get-tuple-element.36) | copy-start | bytes 1540
  24.7 6.5 %copy-start.8 = (bf16[4,3,64,512]{3,2,1,0:T(8,128)(2,1)}, bf16[4,3,64,512]{3,2,1,0:T(8,128)(2,1)S(1)}, u32[]{:S(2)}) copy-start(bf16[4,3,64,512]{3,2,1,0:T(8,128)(2,1)S(1)} %collective-permute-done.3.refs_4_) | copy-start | bytes 2359300
  31.2 10.7 %copy-start.15 = (bf16[8,8]{1,0:T(8,128)(2,1)S(1)}, bf16[8,8]{1,0:T(8,128)(2,1)}, u32[]{:S(2)}) copy-start(bf16[8,8]{1,0:T(8,128)(2,1)} %param.9) | copy-start | bytes 388
  31.2 10.7 %copy-start.11 = (f32[128]{0:T(128)S(1)}, f32[128]{0:T(128)}, u32[]{:S(2)}) copy-start(f32[128]{0:T(128)} %copy-done.10) | copy-start | bytes 1540
  37.4 8.9 %collective-permute-start.4 = (bf16[2,2,128,256]{3,2,1,0:T(8,128)(2,1)}, bf16[2,2,128,256]{3,2,1,0:T(8,128)(2,1)S(1)}, u32[]{:S(2)}, u32[]{:S(2)}) collective-permute-start(bf16[2,2,128,256]{3,2,1,0:T(8,128)(2,1)} %get-tuple-element.33), channel_id=1, source_target_pairs={{0,8},{8,0},{16,24},{24,16},{1,9},{9,1},{17,25},{25,17},{2,10},{10... | collective-permute-start | bytes 786440 | tf_op jit(solution)/shard_map/ppermute | solution.py:263
  39.0 19.9 %collective-permute-start.5 = (bf16[2,2,128,256]{3,2,1,0:T(8,128)(2,1)S(1)}, bf16[2,2,128,256]{3,2,1,0:T(8,128)(2,1)S(1)}, u32[]{:S(2)}, u32[]{:S(2)}) collective-permute-start(bf16[2,2,128,256]{3,2,1,0:T(8,128)(2,1)S(1)} %get-tuple-element.32), channel_id=1, source_target_pairs={{0,16},{8,24},{16,0},{24,8},{1,17},{9,25},{17,1},{25,9},{2,18},{10... | collective-permute-start | bytes 786440 | tf_op jit(solution)/shard_map/ppermute | solution.py:263
  41.5 17.3 %collective-permute-start.6 = (bf16[2,2,128,256]{3,2,1,0:T(8,128)(2,1)S(1)}, bf16[2,2,128,256]{3,2,1,0:T(8,128)(2,1)S(1)}, u32[]{:S(2)}, u32[]{:S(2)}) collective-permute-start(bf16[2,2,128,256]{3,2,1,0:T(8,128)(2,1)S(1)} %get-tuple-element.31), channel_id=1, source_target_pairs={{0,24},{8,16},{16,8},{24,0},{1,25},{9,17},{17,9},{25,1},{2,26},{10... | collective-permute-start | bytes 786440 | tf_op jit(solution)/shard_map/ppermute | solution.py:263
  42.0 18.9 %all-to-all-start.1 = ((bf16[8,2,128,256]{3,2,1,0:T(8,128)(2,1)}), bf16[8,2,128,256]{3,2,1,0:T(8,128)(2,1)S(1)}, u32[]{:S(2)}, u32[]{:S(2)}) async-start(bf16[8,2,128,256]{3,2,1,0:T(8,128)(2,1)} %shard_map.74), calls=%async_computation.1 | async-start | bytes 2097152 | tf_op jit(solution)/shard_map/all_to_all | solution.py:258
  60.9 0.6 copy-start.3
  61.5 7.7 %copy-start.12 = (f32[128]{0:T(128)S(1)}, f32[128]{0:T(128)}, u32[]{:S(2)}) copy-start(f32[128]{0:T(128)} %copy-done.10) | copy-start | bytes 1540
  61.5 7.7 %copy-start.14 = (f32[128]{0:T(128)S(1)}, f32[128]{0:T(128)}, u32[]{:S(2)}) copy-start(f32[128]{0:T(128)} %copy-done.13) | copy-start | bytes 1540
  61.5 25.2 %copy-start.4 = (f32[8]{0:T(128)S(1)}, f32[8]{0:T(128)}, u32[]{:S(2)}) copy-start(f32[8]{0:T(128)} %occ.5) | copy-start | bytes 100
  61.5 25.2 %copy-start.6 = (s32[2]{0:T(128)S(1)}, s32[2]{0:T(128)}, u32[]{:S(2)}) copy-start(s32[2]{0:T(128)} %copy-done.5) | copy-start | bytes 28
  64.1 9.6 %collective-permute-start.7 = (bf16[2,2,128,256]{3,2,1,0:T(8,128)(2,1)S(1)}, bf16[2,2,128,256]{3,2,1,0:T(8,128)(2,1)S(1)}, u32[]{:S(2)}, u32[]{:S(2)}) collective-permute-start(bf16[2,2,128,256]{3,2,1,0:T(8,128)(2,1)S(1)} %get-tuple-element.22.refs_1_), channel_id=1, source_target_pairs={{0,8},{8,0},{16,24},{24,16},{1,9},{9,1},{17,25},{25,17},{2,10},{10... | collective-permute-start | bytes 786440 | tf_op jit(solution)/shard_map/ppermute | solution.py:263
  66.7 20.0 %collective-permute-start.8 = (bf16[2,2,128,256]{3,2,1,0:T(8,128)(2,1)S(1)}, bf16[2,2,128,256]{3,2,1,0:T(8,128)(2,1)S(1)}, u32[]{:S(2)}, u32[]{:S(2)}) collective-permute-start(bf16[2,2,128,256]{3,2,1,0:T(8,128)(2,1)S(1)} %get-tuple-element.23.refs_2_), channel_id=1, source_target_pairs={{0,16},{8,24},{16,0},{24,8},{1,17},{9,25},{17,1},{25,9},{2,18},{10... | collective-permute-start | bytes 786440 | tf_op jit(solution)/shard_map/ppermute | solution.py:263
  68.3 18.4 %collective-permute-start.9 = (bf16[2,2,128,256]{3,2,1,0:T(8,128)(2,1)S(1)}, bf16[2,2,128,256]{3,2,1,0:T(8,128)(2,1)S(1)}, u32[]{:S(2)}, u32[]{:S(2)}) collective-permute-start(bf16[2,2,128,256]{3,2,1,0:T(8,128)(2,1)S(1)} %get-tuple-element.24.refs_3_), channel_id=1, source_target_pairs={{0,24},{8,16},{16,8},{24,0},{1,25},{9,17},{17,9},{25,1},{2,26},{10... | collective-permute-start | bytes 786440 | tf_op jit(solution)/shard_map/ppermute | solution.py:263
  91.7 12.7 %collective-permute-start.10 = (bf16[2,2,128,256]{3,2,1,0:T(8,128)(2,1)S(1)}, bf16[2,2,128,256]{3,2,1,0:T(8,128)(2,1)S(1)}, u32[]{:S(2)}, u32[]{:S(2)}) collective-permute-start(bf16[2,2,128,256]{3,2,1,0:T(8,128)(2,1)S(1)} %get-tuple-element.28.refs_1_), channel_id=1, source_target_pairs={{0,8},{8,0},{16,24},{24,16},{1,9},{9,1},{17,25},{25,17},{2,10},{10... | collective-permute-start | bytes 786440 | tf_op jit(solution)/shard_map/ppermute | solution.py:263
  95.0 21.0 %collective-permute-start.11 = (bf16[2,2,128,256]{3,2,1,0:T(8,128)(2,1)S(1)}, bf16[2,2,128,256]{3,2,1,0:T(8,128)(2,1)}, u32[]{:S(2)}, u32[]{:S(2)}) collective-permute-start(bf16[2,2,128,256]{3,2,1,0:T(8,128)(2,1)S(1)} %get-tuple-element.29.refs_2_), channel_id=1, source_target_pairs={{0,16},{8,24},{16,0},{24,8},{1,17},{9,25},{17,1},{25,9},{2,18},{10... | collective-permute-start | bytes 786440 | tf_op jit(solution)/shard_map/ppermute | solution.py:263
  96.6 19.4 %collective-permute-start.12 = (bf16[2,2,128,256]{3,2,1,0:T(8,128)(2,1)S(1)}, bf16[2,2,128,256]{3,2,1,0:T(8,128)(2,1)}, u32[]{:S(2)}, u32[]{:S(2)}) collective-permute-start(bf16[2,2,128,256]{3,2,1,0:T(8,128)(2,1)S(1)} %get-tuple-element.30.refs_3_), channel_id=1, source_target_pairs={{0,24},{8,16},{16,8},{24,0},{1,25},{9,17},{17,9},{25,1},{2,26},{10... | collective-permute-start | bytes 786440 | tf_op jit(solution)/shard_map/ppermute | solution.py:263
  98.1 22.3 %all-to-all-start.2 = ((bf16[8,2,128,256]{3,2,1,0:T(8,128)(2,1)}), bf16[8,2,128,256]{3,2,1,0:T(8,128)(2,1)S(1)}, u32[]{:S(2)}, u32[]{:S(2)}) async-start(bf16[8,2,128,256]{3,2,1,0:T(8,128)(2,1)} %get-tuple-element.25), calls=%async_computation.2 | async-start | bytes 2097152 | tf_op jit(solution)/shard_map/all_to_all | solution.py:258
  116.0 1.2 copy-start.7
  120.4 22.5 %all-to-all-start.3 = ((bf16[8,2,128,256]{3,2,1,0:T(8,128)(2,1)}), bf16[8,2,128,256]{3,2,1,0:T(8,128)(2,1)S(1)}, u32[]{:S(2)}, u32[]{:S(2)}) async-start(bf16[8,2,128,256]{3,2,1,0:T(8,128)(2,1)} %shard_map.79), calls=%async_computation.3 | async-start | bytes 2097152 | tf_op jit(solution)/shard_map/all_to_all | solution.py:258
  127.6 1.1 copy-start.9

commit v6 on v5

--- a/solution.py
+++ b/solution.py
@@ -31,11 +31,8 @@
 
     def mirror_within(self, x):
         e, g = self.edge, self.rows
-        parts = []
-        for c in range(2):
-            tile = jnp.concatenate([x[c * g:(c + 1) * g, :e], x[c * g:(c + 1) * g, e:]], axis=0).T
-            parts.append(jnp.concatenate([tile[:g], tile[g:]], axis=1))
-        return jnp.concatenate(parts, axis=0)
+        tile = jnp.concatenate([x[:, :e], x[:, e:]], axis=0).T
+        return jnp.concatenate([tile[:g], tile[g:]], axis=1)
 
     def mirror_across(self, x):
         return jnp.concatenate([x[:, self.edge:], x[:, :self.edge]], axis=1)
@@ -54,40 +51,36 @@
     )(*operands)
 
 
-def pack_pair(tiles, source, out, pair, mirrored=False):
+def pack_pair(tiles, source, outs, pair, mirrored=False):
     e, g = tiles.edge, tiles.rows
     straight, turned = (slice(e, None), slice(0, e)) if mirrored else (slice(0, e), slice(e, None))
     for d, (a, b) in enumerate(tiles.above):
-        out[d, pair, :, straight] = source[tiles.span(a), tiles.span(b)].astype(NARROW)
-        out[d, pair, :, turned] = source[tiles.span(b), tiles.span(a)].astype(WIDE).T.astype(NARROW)
+        tile = source[tiles.span(a), tiles.span(b)].astype(NARROW)
+        other = source[tiles.span(b), tiles.span(a)].astype(WIDE).T.astype(NARROW)
+        for c, out in enumerate(outs):
+            out[d, pair, :, straight] = tile[c * g:(c + 1) * g]
+            out[d, pair, :, turned] = other[c * g:(c + 1) * g]
     for d, c, k in tiles.diagonal:
         tile = source[tiles.span(k), tiles.span(k)]
         tile = tile.astype(WIDE).T.astype(NARROW) if mirrored else tile.astype(NARROW)
-        out[d, pair, c * g:(c + 1) * g, :e] = tile[:g]
-        out[d, pair, c * g:(c + 1) * g, e:] = tile[g:]
-
-
-def unpack_pair(tiles, blocks, pair, put):
-    e, g = tiles.edge, tiles.rows
+        outs[c][d, pair, :, :e] = tile[:g]
+        outs[c][d, pair, :, e:] = tile[g:]
+
+
+def unpack_pair(tiles, chunks, pair, put):
+    e = tiles.edge
     for d, (a, b) in enumerate(tiles.above):
-        put(a, b, blocks[d, pair, :, :e].astype(WIDE))
-        put(b, a, blocks[d, pair, :, e:].astype(WIDE).T)
+        block = jnp.concatenate([chunk[d, pair] for chunk in chunks], axis=0).astype(WIDE)
+        put(a, b, block[:, :e])
+        put(b, a, block[:, e:].T)
     for d, c, k in tiles.diagonal:
-        upper = blocks[d, pair, c * g:(c + 1) * g, :e]
-        lower = blocks[d, pair, c * g:(c + 1) * g, e:]
-        put(k, k, jnp.concatenate([upper, lower], axis=0).astype(WIDE))
-
-
-def pack_kernel(tiles, source, out):
+        block = chunks[c][d, pair].astype(WIDE)
+        put(k, k, jnp.concatenate([block[:, :e], block[:, e:]], axis=0))
+
+
+def pack_kernel(tiles, source, *outs):
     for pair in range(source.shape[0]):
-        pack_pair(tiles, source.at[pair], out, pair, mirrored=True)
-
-
-def pack(tiles, devices, amplitudes):
-    count = amplitudes.shape[0]
-    out = jax.ShapeDtypeStruct((devices, count, tiles.edge, 2 * tiles.edge), NARROW)
-    return call(functools.partial(pack_kernel, tiles), out, [], amplitudes.size, amplitudes.size * 6,
-                amplitudes, specs=[VMEM])
+        pack_pair(tiles, source.at[pair], outs, pair, mirrored=True)
 
 
 def assemble(place, order, pieces, whole):
@@ -118,14 +111,14 @@
 
 
 def first_ladder_kernel(tiles, order, place, source, *refs):
-    pieces, (out, whole, inner, total) = refs[:-4], refs[-4:]
+    pieces, outs, (whole, inner, total) = refs[:-5], refs[-5:-3], refs[-3:]
     assemble(place, order, pieces, whole)
     for pair in range(source.shape[0]):
         ladder_pair(source[pair].astype(NARROW), whole, inner, total)
-        pack_pair(tiles, total, out, pair)
-
-
-def second_ladder_kernel(tiles, order, place, occ, source, blocks, row, column, *refs):
+        pack_pair(tiles, total, outs, pair)
+
+
+def second_ladder_kernel(tiles, order, place, occ, source, upper, lower, row, column, *refs):
     pieces, (out, whole, inner, total, matrix) = refs[:-5], refs[-5:]
     assemble(place, order, pieces, whole)
     count = source.shape[0]
@@ -133,7 +126,7 @@
         def put(a, b, tile):
             matrix[tiles.span(a), tiles.span(b)] = tile.astype(NARROW)
 
-        unpack_pair(tiles, blocks, pair, put)
+        unpack_pair(tiles, (upper, lower), pair, put)
         ladder_pair(matrix[...], whole, inner, total)
         base = occ[place[0] * count + pair] + occ[place[1]]
 
@@ -149,15 +142,16 @@
 
 
 def add_kernel(tiles, source, blocks, out):
+    chunks = [blocks.at[:, :, :tiles.rows], blocks.at[:, :, tiles.rows:]]
     for pair in range(source.shape[0]):
         def put(a, b, tile):
             here = (pair, tiles.span(a), tiles.span(b))
             out[here] = source[here] + tile
 
-        unpack_pair(tiles, blocks, pair, put)
-
-
-def mix(place, fock, first, load, store, rows, width):
+        unpack_pair(tiles, chunks, pair, put)
+
+
+def mix(place, fock, first, load, store, rows):
     total = fock.shape[0]
     strips = rows // 16
 
@@ -187,7 +181,7 @@
     def store(s, u, w, column, at, result):
         out[s][u, w, at, :] = (ladder[column, u, at, :].astype(WIDE) + result).astype(NARROW)
 
-    mix(place, fock, first, load, store, tiles.edge, 2 * tiles.edge)
+    mix(place, fock, first, load, store, tiles.rows)
 
 
 def with_mirror(tiles, place, x, finish):
@@ -202,11 +196,12 @@
         finish(tiles.mirror_within(x))
 
 
-def update_kernel(tiles, groups, first, place, fock, occ, sums, *refs):
+def update_kernel(tiles, groups, first, chunk, place, fock, occ, sums, *refs):
     own, other = refs[:groups], refs[groups:2 * groups]
     sent, rest = refs[2 * groups:2 * groups + 2]
     out = refs[2 * groups + 2:3 * groups + 2]
     update = refs[3 * groups + 2]
+    here = slice(chunk * tiles.rows, (chunk + 1) * tiles.rows)
 
     def one(step, carry):
         u, w = step // first, lax.rem(step, first)
@@ -215,7 +210,7 @@
             base = occ[place[0] * first + u] + occ[column]
 
             def finish(mirrored):
-                value = (own[s][u, w].astype(WIDE) + mirrored) * inverse(base - sums[...])
+                value = (own[s][u, w].astype(WIDE) + mirrored) * inverse(base - sums[here])
                 narrow = value.astype(NARROW)
                 update[u, s * first + w] = value
                 sent[column, u] = narrow
@@ -232,11 +227,15 @@
     def store(s, u, w, column, at, result):
         out[s][u, w, at, :] = result.astype(NARROW)
 
-    mix(place, fock, first, load, store, tiles.edge, 2 * tiles.edge)
-
-
-def rest_kernel(tiles, groups, first, place, occ, sums, rest, *refs):
+    mix(place, fock, first, load, store, tiles.rows)
+
+
+def rest_kernel(tiles, groups, first, chunk, place, occ, sums, rest, *refs):
+    before, refs = refs[:chunk], refs[chunk:]
     own, other, out = refs[:groups], refs[groups:2 * groups], refs[2 * groups]
+    here = slice(chunk * tiles.rows, (chunk + 1) * tiles.rows)
+    for ref in before:
+        out[:, :, :tiles.rows, :] = ref[...]
 
     def one(step, carry):
         u, w = step // first, lax.rem(step, first)
@@ -245,8 +244,8 @@
             base = occ[place[0] * first + u] + occ[column]
 
             def finish(mirrored):
-                value = (own[s][u, w].astype(WIDE) + mirrored) * inverse(base - sums[...])
-                out[column, u] = (rest[u, s * first + w].astype(WIDE) + value).astype(NARROW)
+                value = (own[s][u, w].astype(WIDE) + mirrored) * inverse(base - sums[here])
+                out[column, u, here] = (rest[u, s * first + w].astype(WIDE) + value).astype(NARROW)
 
             with_mirror(tiles, place, other[s][w, u].astype(WIDE), finish)
         return carry
@@ -284,13 +283,13 @@
     )(tie(x, *others))
 
 
-def gather_vectors(vectors, devices):
+def gather_vectors(vectors, devices, packed):
     def turn(x, k):
         return lax.ppermute(x, "occj", [(d, d ^ k) for d in range(devices)])
 
     even = list(range(0, devices, 2))
     held = [vectors] + [turn(vectors, k) for k in even[1:]]
-    other = turn(jnp.stack(held), 1)
+    other = turn(tie(jnp.stack(held), packed), 1)
     return [*held, other], even + [k ^ 1 for k in even]
 
 
@@ -320,53 +319,65 @@
     fock = occupied_fock_block.astype(WIDE)
     p, q = lax.axis_index("occi"), lax.axis_index("occj")
     place = jnp.stack([p, q]).astype(jnp.int32)
-    part = jax.ShapeDtypeStruct((first, first, edge, 2 * edge), NARROW)
     packed = jax.ShapeDtypeStruct((devices, first, edge, 2 * edge), NARROW)
+    upper = jax.ShapeDtypeStruct((devices, first, tiles.rows, 2 * edge), NARROW)
+    part = jax.ShapeDtypeStruct((first, first, tiles.rows, 2 * edge), NARROW)
     singles = vectors.shape[0]
     whole = pltpu.VMEM((virtual, singles * virtual), NARROW)
     inner = pltpu.VMEM((singles * virtual, virtual), NARROW)
     square = pltpu.VMEM((virtual, virtual), WIDE)
-
-    started = pack(tiles, devices, current)
-    pieces, order = gather_vectors(vectors, devices)
-    held = exchange(tie(started, *pieces[:-1]))
+    chunks = range(2)
+
+    started = call(functools.partial(pack_kernel, tiles), [upper] * 2, [], count, 6 * count, current, specs=[VMEM])
+    pieces, order = gather_vectors(vectors, devices, started[0])
+    held = [exchange(tie(started[0], *pieces[:-1])), exchange(started[1])]
     sums = virtual_sums(tiles, vir_energy, q)
 
     ladder_flops = first * singles * 4 * virtual**3
     ladder = call(
-        functools.partial(first_ladder_kernel, tiles, order), packed, [whole, inner, square],
+        functools.partial(first_ladder_kernel, tiles, order), [upper] * 2, [whole, inner, square],
         ladder_flops, 8 * count, place, current, *pieces, specs=[SMEM] + [VMEM] * (1 + len(pieces)),
     )
-    parts = tie(held, ladder).reshape(groups, first, first, edge, 2 * edge)
-    mirror = across_first([parts[p ^ s] for s in range(groups)], groups)
-    ladder = exchange(ladder)
-    half = call(
-        functools.partial(half_kernel, tiles, groups, first), [part] * groups, [],
-        2 * devices * count, 6 * count, after(place, *mirror), fock, ladder, *mirror,
-        specs=[SMEM] * 2 + [VMEM] * (groups + 1),
-    )
-    other = across_first(half, groups)
-    sent, rest, *mixed = call(
-        functools.partial(update_kernel, tiles, groups, first),
-        [packed, jax.ShapeDtypeStruct((first, devices, edge, 2 * edge), NARROW)] + [part] * groups,
-        [pltpu.VMEM((first, devices, edge, 2 * edge), WIDE)],
-        2 * devices * count, 10 * count, place, fock, occ_energy, sums, *half, *other,
-        specs=[SMEM] * 3 + [VMEM] * (2 * groups + 1),
-    )
-    other = across_first(mixed, groups)
-    back = exchange(sent)
+    mirror = []
+    for c in chunks:
+        parts = tie(held[c], *ladder).reshape(groups, first, *part.shape[1:])
+        mirror.append(across_first([parts[p ^ s] for s in range(groups)], groups))
+    ladder = [exchange(x) for x in ladder]
+
+    half, other = [], []
+    for c in chunks:
+        half.append(call(
+            functools.partial(half_kernel, tiles, groups, first), [part] * groups, [],
+            LONG, 6 * count, after(place, *mirror[c]) if c == 0 else place, fock, ladder[c], *mirror[c],
+            specs=[SMEM] * 2 + [VMEM] * (groups + 1),
+        ))
+        other.append(across_first(half[c], groups))
+    back, rest, mixed = [], [], []
+    for c in chunks:
+        sent, rest_one, *mixed_one = call(
+            functools.partial(update_kernel, tiles, groups, first, c),
+            [upper, jax.ShapeDtypeStruct((first, devices, *part.shape[2:]), NARROW)] + [part] * groups,
+            [pltpu.VMEM((first, devices, *part.shape[2:]), WIDE)],
+            LONG, 10 * count, place, fock, occ_energy, sums, *half[c], *other[c],
+            specs=[SMEM] * 3 + [VMEM] * (2 * groups + 1),
+        )
+        back, rest, mixed = back + [exchange(sent)], rest + [rest_one], mixed + [mixed_one]
+    other = [across_first(x, groups) for x in mixed]
     base = call(
         functools.partial(second_ladder_kernel, tiles, order), jax.ShapeDtypeStruct(current.shape, WIDE),
         [whole, inner, square, pltpu.VMEM((virtual, virtual), NARROW)],
-        ladder_flops, 12 * count, place, occ_energy, current, back,
+        ladder_flops, 12 * count, place, occ_energy, current, *back,
         jnp.broadcast_to(vir_energy[:, None], (virtual, 128)), vir_energy[None, :], *pieces,
-        specs=[SMEM] * 2 + [VMEM] * (4 + len(pieces)),
+        specs=[SMEM] * 2 + [VMEM] * (5 + len(pieces)),
     )
-    rest = exchange(call(
-        functools.partial(rest_kernel, tiles, groups, first), packed, [],
-        LONG, 8 * count, place, occ_energy, sums, rest, *mixed, *other,
-        specs=[SMEM] * 2 + [VMEM] * (2 * groups + 2),
-    ))
+    last = []
+    for c in chunks:
+        last = [call(
+            functools.partial(rest_kernel, tiles, groups, first, c), (upper, packed)[c], [],
+            LONG, 8 * count, place, occ_energy, sums, rest[c], *last, *mixed[c], *other[c],
+            specs=[SMEM] * 2 + [VMEM] * (2 * groups + 2 + c),
+        )]
+    rest = exchange(last[0])
     done = call(
         functools.partial(add_kernel, tiles), jax.ShapeDtypeStruct(current.shape, WIDE), [],
         count, 10 * count, base, rest, specs=[VMEM, VMEM], aliases={0: 0},

time: 148 us -> 154 us (1.041)
  starting transfers between devices: 41 us -> 74.4 us
  waiting for transfers between devices: 59.6 us -> 28.8 us
  local copies, waits for them, and re-layouts: 7.55 us -> 9.94 us
  Pallas kernels: 35.2 us -> 37.2 us
    ppermute x9 -> x18, waiting for transfers between devices: 42.4 us -> 2.19 us  [across_first(): lax.ppermute(parts[s], 'occi', [(k, k ^ s) for k in range(groups)])]
    ppermute x9 -> x18, starting transfers between devices: 15.9 us -> 41.8 us  [across_first(): lax.ppermute(parts[s], 'occi', [(k, k ^ s) for k in range(groups)])]
    all_to_all x4 -> x7, waiting for transfers between devices: 8.01 us -> 24.1 us  [exchange(): lax.all_to_all(blocks, 'occj', split_axis=0, concat_axis=0, tiled=True)]
    all_to_all x4 -> x7, starting transfers between devices: 20.6 us -> 28 us  [exchange(): lax.all_to_all(blocks, 'occj', split_axis=0, concat_axis=0, tiled=True)]
    ppermute x4, waiting for transfers between devices: 9.27 us -> 2.49 us  [turn(): return lax.ppermute(x, 'occj', [(d, d ^ k) for d in range(devices)])]
    pallas_call x7 -> x10, Pallas kernels: 34 us -> 36.1 us  [call(): pl.pallas_call(body, out_shape=outs, in_specs=specs, out_specs=jax.tree.m...]
    unnamed x36 -> x48, local copies, waits for them, and re-layouts: 5.16 us -> 6.31 us
  transfers between devices with their start and end apart: 17 -> 29, of which waited for: 10 -> 8; matrix products, arithmetic and copies ran while one was open for 1% -> 3% of each run, Pallas kernels for 17% -> 22%
where the time goes in v6:
time: 154 us; the launch traced here: 153 us
  starting transfers between devices  74.4 us (48%)
  Pallas kernels  37.2 us (24%)
  waiting for transfers between devices  28.8 us (19%)
  local copies, waits for them, and re-layouts  9.94 us (6%)
  between operations  1.7 us (1%)
    ppermute x18, starting transfers between devices, across_first(): lax.ppermute(parts[s], 'occi', [(k, k ^ s) for k in range(groups)])  41.8 us
    pallas_call x10, Pallas kernels, call(): pl.pallas_call(body, out_shape=outs, in_specs=specs, out_specs=jax.tree.m...  36.1 us
    all_to_all x7, starting transfers between devices, exchange(): lax.all_to_all(blocks, 'occj', split_axis=0, concat_axis=0, tiled=True)  28 us
    all_to_all x7, waiting for transfers between devices, exchange(): lax.all_to_all(blocks, 'occj', split_axis=0, concat_axis=0, tiled=True)  24.1 us
    unnamed x48, local copies, waits for them, and re-layouts  6.31 us
    ppermute x4, starting transfers between devices, turn(): return lax.ppermute(x, 'occj', [(d, d ^ k) for d in range(devices)])  4.53 us
  transfers between devices with their start and end apart: 29, of which 8 were waited for; matrix products, arithmetic and copies ran while one was open for 3% of the time, Pallas kernels for 22%

profile of v6, /device:TPU:0, one launch (start us, length us, event | category | flops | bytes accessed | tf_op | source)
XLA Modules:
  0.0 153.1 jit_solution(3219570719243685061)
XLA Ops:
  0.0 2.9 %collective-permute-start = (bf16[3,64,512]{2,1,0:T(8,128)(2,1)}, bf16[3,64,512]{2,1,0:T(8,128)(2,1)S(1)}, u32[]{:S(2)}, u32[]{:S(2)}) collective-permute-start(bf16[3,64,512]{2,1,0:T(8,128)(2,1)} %refs_0_.3), channel_id=1, source_target_pairs={{0,2},{1,3},{2,0},{3,1},{4,6},{5,7},{6,4},{7,5},{8,10},{9,11},{10,... | collective-permute-start | bytes 589832 | tf_op jit(solution)/shard_map/ppermute | solution.py:288
  2.9 1.5 collective-permute-start.1
  4.5 1.2 dynamic_slice.38
  6.4 1.2 dynamic_slice.36
  8.3 1.6 %copy-done = f32[2,1,512,512]{3,2,1,0:T(8,128)S(1)} copy-done((f32[2,1,512,512]{3,2,1,0:T(8,128)S(1)}, f32[2,1,512,512]{3,2,1,0:T(8,128)}, u32[]{:S(2)}) %copy-start) | copy-done | bytes 2097176
  9.9 1.2 shard_map.73
  11.1 0.1 fusion
  11.2 0.1 fusion.1
  11.2 2.5 %collective-permute-done.1.refs_2_ = bf16[3,64,512]{2,1,0:T(8,128)(2,1)S(1)} collective-permute-done((bf16[3,64,512]{2,1,0:T(8,128)(2,1)}, bf16[3,64,512]{2,1,0:T(8,128)(2,1)S(1)}, u32[]{:S(2)}, u32[]{:S(2)}) %collective-permute-start.1) | collective-permute-done | bytes 196640 | tf_op jit(solution)/shard_map/ppermute | solution.py:288
  13.7 0.1 pad_maximum_fusion
  13.9 0.1 collective-permute-start.3
  13.9 0.1 fusion.2
  14.0 3.5 %all-to-all-start = ((bf16[8,2,64,256]{3,2,1,0:T(8,128)(2,1)}), bf16[8,2,64,256]{3,2,1,0:T(8,128)(2,1)S(1)}, u32[]{:S(2)}, u32[]{:S(2)}) async-start(bf16[8,2,64,256]{3,2,1,0:T(8,128)(2,1)} %get-tuple-element.35), calls=%async_computation | async-start | bytes 1048576 | tf_op jit(solution)/shard_map/all_to_all | solution.py:257
  17.5 0.1 pad_add_fusion.place.source
  17.6 0.1 broadcast_add_fusion
  17.7 0.7 broadcast_add_fusion.2
  18.4 8.8 %all-to-all-done = bf16[8,2,64,256]{3,2,1,0:T(8,128)(2,1)S(1)} async-done(((bf16[8,2,64,256]{3,2,1,0:T(8,128)(2,1)}), bf16[8,2,64,256]{3,2,1,0:T(8,128)(2,1)S(1)}, u32[]{:S(2)}, u32[]{:S(2)}) %all-to-all-start) | async-done | bytes 524320 | tf_op jit(solution)/shard_map/all_to_all | solution.py:257
  27.2 3.5 %all-to-all-start.4 = ((bf16[8,2,64,256]{3,2,1,0:T(8,128)(2,1)}), bf16[8,2,64,256]{3,2,1,0:T(8,128)(2,1)S(1)}, u32[]{:S(2)}, u32[]{:S(2)}) async-start(bf16[8,2,64,256]{3,2,1,0:T(8,128)(2,1)} %get-tuple-element.46), calls=%async_computation.4 | async-start | bytes 1048576 | tf_op jit(solution)/shard_map/all_to_all | solution.py:257
  30.7 6.5 %shard_map.74 = (bf16[8,2,64,256]{3,2,1,0:T(8,128)(2,1)}, bf16[8,2,64,256]{3,2,1,0:T(8,128)(2,1)}) custom-call(s32[2]{0:T(128)S(1)} %pad_add_fusion.place.source, f32[2,512,512]{2,1,0:T(8,128)} %bitcast.31, bf16[3,64,512]{2,1,0:T(8,128)(2,1)S(1)} %copy-done.1, bf16[3,64,512]{2,1,0:T(8,128)(2,1)S(1)} %collective-permute-done.refs_1_, ...), custom_call_target="tpu_custom_call" | custom-call | flops 3221225472 | bytes 4194304 | tf_op jit(solution)/shard_map/pallas_call | solution.py:42
  37.3 1.7 %collective-permute-start.4 = (bf16[2,2,64,256]{3,2,1,0:T(8,128)(2,1)S(1)}, bf16[2,2,64,256]{3,2,1,0:T(8,128)(2,1)S(1)}, u32[]{:S(2)}, u32[]{:S(2)}) collective-permute-start(bf16[2,2,64,256]{3,2,1,0:T(8,128)(2,1)S(1)} %get-tuple-element.69), channel_id=1, source_target_pairs={{0,8},{8,0},{16,24},{24,16},{1,9},{9,1},{17,25},{25,17},{2,10},{10... | collective-permute-start | bytes 393224 | tf_op jit(solution)/shard_map/ppermute | solution.py:262
  39.0 2.6 %collective-permute-start.5 = (bf16[2,2,64,256]{3,2,1,0:T(8,128)(2,1)S(1)}, bf16[2,2,64,256]{3,2,1,0:T(8,128)(2,1)S(1)}, u32[]{:S(2)}, u32[]{:S(2)}) collective-permute-start(bf16[2,2,64,256]{3,2,1,0:T(8,128)(2,1)S(1)} %get-tuple-element.68), channel_id=1, source_target_pairs={{0,16},{8,24},{16,0},{24,8},{1,17},{9,25},{17,1},{25,9},{2,18},{10... | collective-permute-start | bytes 393224 | tf_op jit(solution)/shard_map/ppermute | solution.py:262
  41.6 0.2 collective-permute-start.6
  41.8 4.1 %all-to-all-start.1 = ((bf16[8,2,64,256]{3,2,1,0:T(8,128)(2,1)}), bf16[8,2,64,256]{3,2,1,0:T(8,128)(2,1)S(1)}, u32[]{:S(2)}, u32[]{:S(2)}) async-start(bf16[8,2,64,256]{3,2,1,0:T(8,128)(2,1)} %get-tuple-element.37), calls=%async_computation.1 | async-start | bytes 1048576 | tf_op jit(solution)/shard_map/all_to_all | solution.py:257
  45.9 0.7 dynamic-slice_bitcast_fusion
  46.7 0.7 collective-permute-start.10
  47.4 3.5 %collective-permute-start.11 = (bf16[2,2,64,256]{3,2,1,0:T(8,128)(2,1)}, bf16[2,2,64,256]{3,2,1,0:T(8,128)(2,1)S(1)}, u32[]{:S(2)}, u32[]{:S(2)}) collective-permute-start(bf16[2,2,64,256]{3,2,1,0:T(8,128)(2,1)} %get-tuple-element.64), channel_id=1, source_target_pairs={{0,16},{8,24},{16,0},{24,8},{1,17},{9,25},{17,1},{25,9},{2,18},{10... | collective-permute-start | bytes 393224 | tf_op jit(solution)/shard_map/ppermute | solution.py:262
  50.9 0.2 collective-permute-start.12
  51.1 0.8 collective-permute-done.5.refs_2_
  51.9 1.2 shard_map.75.place
  53.1 2.6 %all-to-all-done.1.ladder = bf16[8,2,64,256]{3,2,1,0:T(8,128)(2,1)S(1)} async-done(((bf16[8,2,64,256]{3,2,1,0:T(8,128)(2,1)}), bf16[8,2,64,256]{3,2,1,0:T(8,128)(2,1)S(1)}, u32[]{:S(2)}, u32[]{:S(2)}) %all-to-all-start.1) | async-done | bytes 524320 | tf_op jit(solution)/shard_map/all_to_all | solution.py:257
  55.7 3.5 %all-to-all-start.3 = ((bf16[8,2,64,256]{3,2,1,0:T(8,128)(2,1)}), bf16[8,2,64,256]{3,2,1,0:T(8,128)(2,1)S(1)}, u32[]{:S(2)}, u32[]{:S(2)}) async-start(bf16[8,2,64,256]{3,2,1,0:T(8,128)(2,1)} %get-tuple-element.38), calls=%async_computation.3 | async-start | bytes 1048576 | tf_op jit(solution)/shard_map/all_to_all | solution.py:257
  59.2 0.7 copy-done.20
  59.9 1.6 %shard_map.76 = (bf16[2,2,64,256]{3,2,1,0:T(8,128)(2,1)S(1)}, bf16[2,2,64,256]{3,2,1,0:T(8,128)(2,1)S(1)}, bf16[2,2,64,256]{3,2,1,0:T(8,128)(2,1)S(1)}, bf16[2,2,64,256]{3,2,1,0:T(8,128)(2,1)S(1)}) custom-call(s32[2]{0:T(128)S(1)} %copy-done.20, f32[8,8]{1,0:T(8,128)S(1)} %convert_element_type.3.fock, bf16[8,2,64,256]{3,2,1,0:T(8,128)(2,1)S(1)} %all-to-all-done.1.ladder, ...), custom_call_target="tpu_custom_call" | custom-call | flops 30000001024 | bytes 3145728 | tf_op jit(solution)/shard_map/pallas_call | solution.py:42
  61.4 7.0 %collective-permute-start.7 = (bf16[2,2,64,256]{3,2,1,0:T(8,128)(2,1)S(1)}, bf16[2,2,64,256]{3,2,1,0:T(8,128)(2,1)S(1)}, u32[]{:S(2)}, u32[]{:S(2)}) collective-permute-start(bf16[2,2,64,256]{3,2,1,0:T(8,128)(2,1)S(1)} %get-tuple-element.42.refs_1_), channel_id=1, source_target_pairs={{0,8},{8,0},{16,24},{24,16},{1,9},{9,1},{17,25},{25,17},{2,10},{10... | collective-permute-start | bytes 393224 | tf_op jit(solution)/shard_map/ppermute | solution.py:262
  68.5 1.1 collective-permute-start.8
  69.6 1.4 collective-permute-start.9
  71.0 1.6 %shard_map.78 = (bf16[2,2,64,256]{3,2,1,0:T(8,128)(2,1)S(1)}, bf16[2,2,64,256]{3,2,1,0:T(8,128)(2,1)S(1)}, bf16[2,2,64,256]{3,2,1,0:T(8,128)(2,1)S(1)}, bf16[2,2,64,256]{3,2,1,0:T(8,128)(2,1)S(1)}) custom-call(s32[2]{0:T(128)S(1)} %copy-done.15, f32[8,8]{1,0:T(8,128)S(1)} %convert_element_type.3.fock, bf16[8,2,64,256]{3,2,1,0:T(8,128)(2,1)S(1)} %all-to-all-done.3.ladder, ...), custom_call_target="tpu_custom_call" | custom-call | flops 30000001024 | bytes 3145728 | tf_op jit(solution)/shard_map/pallas_call | solution.py:42
  72.6 5.0 %collective-permute-start.13 = (bf16[2,2,64,256]{3,2,1,0:T(8,128)(2,1)S(1)}, bf16[2,2,64,256]{3,2,1,0:T(8,128)(2,1)S(1)}, u32[]{:S(2)}, u32[]{:S(2)}) collective-permute-start(bf16[2,2,64,256]{3,2,1,0:T(8,128)(2,1)S(1)} %get-tuple-element.49.refs_1_), channel_id=1, source_target_pairs={{0,8},{8,0},{16,24},{24,16},{1,9},{9,1},{17,25},{25,17},{2,10},{10... | collective-permute-start | bytes 393224 | tf_op jit(solution)/shard_map/ppermute | solution.py:262
  77.6 1.1 collective-permute-start.14
  78.7 1.4 collective-permute-start.15
  80.0 1.3 collective-permute-done.8.refs_6_
  81.4 3.0 %shard_map.77 = (bf16[8,2,64,256]{3,2,1,0:T(8,128)(2,1)}, bf16[2,8,64,256]{3,2,1,0:T(8,128)(2,1)S(1)}, bf16[2,2,64,256]{3,2,1,0:T(8,128)(2,1)S(1)}, bf16[2,2,64,...) custom-call(s32[2]{0:T(128)S(1)} %copy-done.15, ...), custom_call_target="tpu_custom_call" | custom-call | flops 30000001024 | bytes 5242880 | tf_op jit(solution)/shard_map/pallas_call | solution.py:42
  84.4 9.0 %collective-permute-start.16 = (bf16[2,2,64,256]{3,2,1,0:T(8,128)(2,1)S(1)}, bf16[2,2,64,256]{3,2,1,0:T(8,128)(2,1)S(1)}, u32[]{:S(2)}, u32[]{:S(2)}) collective-permute-start(bf16[2,2,64,256]{3,2,1,0:T(8,128)(2,1)S(1)} %get-tuple-element.56.refs_1_), channel_id=1, source_target_pairs={{0,8},{8,0},{16,24},{24,16},{1,9},{9,1},{17,25},{25,17},{2,10},{10... | collective-permute-start | bytes 393224 | tf_op jit(solution)/shard_map/ppermute | solution.py:262
  93.4 1.1 collective-permute-start.17
  94.5 1.5 collective-permute-start.18
  95.9 3.1 %shard_map.79 = (bf16[8,2,64,256]{3,2,1,0:T(8,128)(2,1)}, bf16[2,8,64,256]{3,2,1,0:T(8,128)(2,1)S(1)}, bf16[2,2,64,256]{3,2,1,0:T(8,128)(2,1)S(1)}, bf16[2,2,64,...) custom-call(s32[2]{0:T(128)S(1)} %copy-done.15, ...), custom_call_target="tpu_custom_call" | custom-call | flops 30000001024 | bytes 5242880 | tf_op jit(solution)/shard_map/pallas_call | solution.py:42
  99.0 1.0 collective-permute-start.19
  100.0 2.0 %collective-permute-start.20 = (bf16[2,2,64,256]{3,2,1,0:T(8,128)(2,1)S(1)}, bf16[2,2,64,256]{3,2,1,0:T(8,128)(2,1)S(1)}, u32[]{:S(2)}, u32[]{:S(2)}) collective-permute-start(bf16[2,2,64,256]{3,2,1,0:T(8,128)(2,1)S(1)} %get-tuple-element.61.refs_3_), channel_id=1, source_target_pairs={{0,16},{8,24},{16,0},{24,8},{1,17},{9,25},{17,1},{25,9},{2,18},{10... | collective-permute-start | bytes 393224 | tf_op jit(solution)/shard_map/ppermute | solution.py:262
  101.9 6.2 %all-to-all-start.5 = ((bf16[8,2,64,256]{3,2,1,0:T(8,128)(2,1)}), bf16[8,2,64,256]{3,2,1,0:T(8,128)(2,1)S(1)}, u32[]{:S(2)}, u32[]{:S(2)}) async-start(bf16[8,2,64,256]{3,2,1,0:T(8,128)(2,1)} %get-tuple-element.52), calls=%async_computation.5 | async-start | bytes 1048576 | tf_op jit(solution)/shard_map/all_to_all | solution.py:257
  108.1 1.6 %collective-permute-start.21 = (bf16[2,2,64,256]{3,2,1,0:T(8,128)(2,1)S(1)}, bf16[2,2,64,256]{3,2,1,0:T(8,128)(2,1)S(1)}, u32[]{:S(2)}, u32[]{:S(2)}) collective-permute-start(bf16[2,2,64,256]{3,2,1,0:T(8,128)(2,1)S(1)} %get-tuple-element.62.refs_4_), channel_id=1, source_target_pairs={{0,24},{8,16},{16,8},{24,0},{1,25},{9,17},{17,9},{25,1},{2,26},{10... | collective-permute-start | bytes 393224 | tf_op jit(solution)/shard_map/ppermute | solution.py:262
  109.7 1.0 copy-done.19
  110.8 1.3 shard_map.81.refs_0_
  112.0 0.8 copy-done.16
  112.8 5.0 %all-to-all-done.5.lower = bf16[8,2,64,256]{3,2,1,0:T(8,128)(2,1)S(1)} async-done(((bf16[8,2,64,256]{3,2,1,0:T(8,128)(2,1)}), bf16[8,2,64,256]{3,2,1,0:T(8,128)(2,1)S(1)}, u32[]{:S(2)}, u32[]{:S(2)}) %all-to-all-start.5) | async-done | bytes 524320 | tf_op jit(solution)/shard_map/all_to_all | solution.py:257
  117.8 3.5 %all-to-all-start.2 = ((bf16[8,2,64,256]{3,2,1,0:T(8,128)(2,1)}), bf16[8,2,64,256]{3,2,1,0:T(8,128)(2,1)S(1)}, u32[]{:S(2)}, u32[]{:S(2)}) async-start(bf16[8,2,64,256]{3,2,1,0:T(8,128)(2,1)} %get-tuple-element.45), calls=%async_computation.2 | async-start | bytes 1048576 | tf_op jit(solution)/shard_map/all_to_all | solution.py:257
  121.4 1.0 copy-done.17
  122.4 2.3 %shard_map.82 = bf16[8,2,128,256]{3,2,1,0:T(8,128)(2,1)} custom-call(s32[2]{0:T(128)S(1)} %copy-done.15, f32[8]{0:T(128)S(1)} %copy-done.13, f32[128,256]{1,0:T(8,128)S(1)} %maximum_select_fusion.sums, bf16[2,8,64,256]{3,2,1,0:T(8,128)(2,1)S(1)} %get-tuple-element.53.rest, bf16[8,2,64,256]{3,2,1,0:T(8,128)(2,1)S(1)} %copy-done.17, ...), custom_call_target="tpu_custom_call" | custom-call | flops 30000001024 | bytes 4194304 | tf_op jit(solution)/shard_map/pallas_call | solution.py:42
  124.8 6.2 %all-to-all-done.2.upper = bf16[8,2,64,256]{3,2,1,0:T(8,128)(2,1)S(1)} async-done(((bf16[8,2,64,256]{3,2,1,0:T(8,128)(2,1)}), bf16[8,2,64,256]{3,2,1,0:T(8,128)(2,1)S(1)}, u32[]{:S(2)}, u32[]{:S(2)}) %all-to-all-start.2) | async-done | bytes 524320 | tf_op jit(solution)/shard_map/all_to_all | solution.py:257
  131.0 3.7 %all-to-all-start.6 = ((bf16[8,2,128,256]{3,2,1,0:T(8,128)(2,1)}), bf16[8,2,128,256]{3,2,1,0:T(8,128)(2,1)S(1)}, u32[]{:S(2)}, u32[]{:S(2)}) async-start(bf16[8,2,128,256]{3,2,1,0:T(8,128)(2,1)} %shard_map.82), calls=%async_computation.6 | async-start | bytes 2097152 | tf_op jit(solution)/shard_map/all_to_all | solution.py:257
  134.8 0.1 broadcast_in_dim.4.row
  135.0 1.1 copy-done.12
  136.1 12.4 %shard_map.80.source = f32[2,512,512]{2,1,0:T(8,128)} custom-call(s32[2]{0:T(128)S(1)} %copy-done.15, f32[8]{0:T(128)S(1)} %copy-done.13, f32[2,512,512]{2,1,0:T(8,128)} %bitcast.32, bf16[8,2,64,256]{3,2,1,0:T(8,128)(2,1)S(1)} %all-to-all-done.2.upper, bf16[8,2,64,256]{3,2,1,0:T(8,128)(2,1)S(1)} %all-to-all-done.5.lower, ...), custom_call_target="tpu_custom_call" | custom-call | flops 3221225472 | bytes 6291456 | tf_op jit(solution)/shard_map/pallas_call | solution.py:42
  148.4 1.5 all-to-all-done.6.blocks
  149.9 3.1 %shard_map.83 = f32[2,512,512]{2,1,0:T(8,128)} custom-call(f32[2,512,512]{2,1,0:T(8,128)} %shard_map.80.source, bf16[8,2,128,256]{3,2,1,0:T(8,128)(2,1)S(1)} %all-to-all-done.6.blocks), custom_call_target="tpu_custom_call", output_to_operand_aliasing={{}: (0, {})} | custom-call | flops 524288 | bytes 5242880 | tf_op jit(solution)/shard_map/pallas_call | solution.py:42
  (67 shorter events, 0.2 us)
Async XLA Ops:
  0.0 11.1 %copy-start.9 = (f32[512]{0:T(512)S(1)}, f32[512]{0:T(512)}, u32[]{:S(2)}) copy-start(f32[512]{0:T(512)} %param.11) | copy-start | bytes 6148
  0.0 11.2 %collective-permute-start = (bf16[3,64,512]{2,1,0:T(8,128)(2,1)}, bf16[3,64,512]{2,1,0:T(8,128)(2,1)S(1)}, u32[]{:S(2)}, u32[]{:S(2)}) collective-permute-start(bf16[3,64,512]{2,1,0:T(8,128)(2,1)} %refs_0_.3), channel_id=1, source_target_pairs={{0,2},{1,3},{2,0},{3,1},{4,6},{5,7},{6,4},{7,5},{8,10},{9,11},{10,... | collective-permute-start | bytes 589832 | tf_op jit(solution)/shard_map/ppermute | solution.py:288
  2.9 10.8 %collective-permute-start.1 = (bf16[3,64,512]{2,1,0:T(8,128)(2,1)}, bf16[3,64,512]{2,1,0:T(8,128)(2,1)S(1)}, u32[]{:S(2)}, u32[]{:S(2)}) collective-permute-start(bf16[3,64,512]{2,1,0:T(8,128)(2,1)} %refs_0_.3), channel_id=1, source_target_pairs={{0,4},{1,5},{2,6},{3,7},{4,0},{5,1},{6,2},{7,3},{8,12},{9,13},{10,... | collective-permute-start | bytes 589832 | tf_op jit(solution)/shard_map/ppermute | solution.py:288
  4.5 9.3 %collective-permute-start.2 = (bf16[3,64,512]{2,1,0:T(8,128)(2,1)}, bf16[3,64,512]{2,1,0:T(8,128)(2,1)S(1)}, u32[]{:S(2)}, u32[]{:S(2)}) collective-permute-start(bf16[3,64,512]{2,1,0:T(8,128)(2,1)} %refs_0_.3), channel_id=1, source_target_pairs={{0,6},{1,7},{2,4},{3,5},{4,2},{5,3},{6,0},{7,1},{8,14},{9,15},{10,... | collective-permute-start | bytes 589832 | tf_op jit(solution)/shard_map/ppermute | solution.py:288
  8.3 1.6 %copy-start = (f32[2,1,512,512]{3,2,1,0:T(8,128)S(1)}, f32[2,1,512,512]{3,2,1,0:T(8,128)}, u32[]{:S(2)}) copy-start(f32[2,1,512,512]{3,2,1,0:T(8,128)} %param.7) | copy-start | bytes 6291460
  9.9 3.9 %copy-start.1 = (bf16[3,64,512]{2,1,0:T(8,128)(2,1)S(1)}, bf16[3,64,512]{2,1,0:T(8,128)(2,1)}, u32[]{:S(2)}) copy-start(bf16[3,64,512]{2,1,0:T(8,128)(2,1)} %refs_0_.3) | copy-start | bytes 589828
  11.2 26.0 %copy-start.3 = (bf16[3,64,512]{2,1,0:T(8,128)(2,1)}, bf16[3,64,512]{2,1,0:T(8,128)(2,1)S(1)}, u32[]{:S(2)}) copy-start(bf16[3,64,512]{2,1,0:T(8,128)(2,1)S(1)} %collective-permute-done.refs_1_) | copy-start | bytes 589828
  13.7 23.5 %copy-start.5 = (bf16[3,64,512]{2,1,0:T(8,128)(2,1)}, bf16[3,64,512]{2,1,0:T(8,128)(2,1)S(1)}, u32[]{:S(2)}) copy-start(bf16[3,64,512]{2,1,0:T(8,128)(2,1)S(1)} %collective-permute-done.1.refs_2_) | copy-start | bytes 589828
  13.7 23.5 %copy-start.7 = (bf16[3,64,512]{2,1,0:T(8,128)(2,1)}, bf16[3,64,512]{2,1,0:T(8,128)(2,1)S(1)}, u32[]{:S(2)}) copy-start(bf16[3,64,512]{2,1,0:T(8,128)(2,1)S(1)} %collective-permute-done.2.refs_3_) | copy-start | bytes 589828
  13.9 16.9 %collective-permute-start.3 = (bf16[4,3,64,512]{3,2,1,0:T(8,128)(2,1)S(1)}, bf16[4,3,64,512]{3,2,1,0:T(8,128)(2,1)S(1)}, u32[]{:S(2)}, u32[]{:S(2)}) collective-permute-start(bf16[4,3,64,512]{3,2,1,0:T(8,128)(2,1)S(1)} %pad_maximum_fusion), channel_id=1, source_target_pairs={{0,1},{1,0},{2,3},{3,2},{4,5},{5,4},{6,7},{7,6},{8,9},{9,8},{10,11... | collective-permute-start | bytes 2359304 | tf_op jit(solution)/shard_map/ppermute | solution.py:288
  14.0 13.2 %all-to-all-start = ((bf16[8,2,64,256]{3,2,1,0:T(8,128)(2,1)}), bf16[8,2,64,256]{3,2,1,0:T(8,128)(2,1)S(1)}, u32[]{:S(2)}, u32[]{:S(2)}) async-start(bf16[8,2,64,256]{3,2,1,0:T(8,128)(2,1)} %get-tuple-element.35), calls=%async_computation | async-start | bytes 1048576 | tf_op jit(solution)/shard_map/all_to_all | solution.py:257
  17.6 19.6 %copy-start.14 = (s32[2]{0:T(128)}, s32[2]{0:T(128)S(1)}, u32[]{:S(2)}) copy-start(s32[2]{0:T(128)S(1)} %pad_add_fusion.place.source) | copy-start | bytes 28
  27.2 14.6 %all-to-all-start.4 = ((bf16[8,2,64,256]{3,2,1,0:T(8,128)(2,1)}), bf16[8,2,64,256]{3,2,1,0:T(8,128)(2,1)S(1)}, u32[]{:S(2)}, u32[]{:S(2)}) async-start(bf16[8,2,64,256]{3,2,1,0:T(8,128)(2,1)} %get-tuple-element.46), calls=%async_computation.4 | async-start | bytes 1048576 | tf_op jit(solution)/shard_map/all_to_all | solution.py:257
  30.7 11.1 %copy-start.21 = (f32[64,128]{1,0:T(8,128)S(1)}, f32[64,128]{1,0:T(8,128)}, u32[]{:S(2)}) copy-start(f32[64,128]{1,0:T(8,128)} %get-tuple-element.81) | copy-start | bytes 98308
  30.7 11.1 %copy-start.22 = (f32[64,128]{1,0:T(8,128)S(1)}, f32[64,128]{1,0:T(8,128)}, u32[]{:S(2)}) copy-start(f32[64,128]{1,0:T(8,128)} %get-tuple-element.82) | copy-start | bytes 98308
  30.7 11.1 %copy-start.23 = (bf16[8,8]{1,0:T(8,128)(2,1)S(1)}, bf16[8,8]{1,0:T(8,128)(2,1)}, u32[]{:S(2)}) copy-start(bf16[8,8]{1,0:T(8,128)(2,1)} %param.9) | copy-start | bytes 388
  30.7 6.5 %copy-start.11 = (bf16[4,3,64,512]{3,2,1,0:T(8,128)(2,1)}, bf16[4,3,64,512]{3,2,1,0:T(8,128)(2,1)S(1)}, u32[]{:S(2)}) copy-start(bf16[4,3,64,512]{3,2,1,0:T(8,128)(2,1)S(1)} %collective-permute-done.3.refs_4_) | copy-start | bytes 2359300
  37.3 13.6 %collective-permute-start.4 = (bf16[2,2,64,256]{3,2,1,0:T(8,128)(2,1)S(1)}, bf16[2,2,64,256]{3,2,1,0:T(8,128)(2,1)S(1)}, u32[]{:S(2)}, u32[]{:S(2)}) collective-permute-start(bf16[2,2,64,256]{3,2,1,0:T(8,128)(2,1)S(1)} %get-tuple-element.69), channel_id=1, source_target_pairs={{0,8},{8,0},{16,24},{24,16},{1,9},{9,1},{17,25},{25,17},{2,10},{10... | collective-permute-start | bytes 393224 | tf_op jit(solution)/shard_map/ppermute | solution.py:262
  39.0 12.9 %collective-permute-start.5 = (bf16[2,2,64,256]{3,2,1,0:T(8,128)(2,1)S(1)}, bf16[2,2,64,256]{3,2,1,0:T(8,128)(2,1)S(1)}, u32[]{:S(2)}, u32[]{:S(2)}) collective-permute-start(bf16[2,2,64,256]{3,2,1,0:T(8,128)(2,1)S(1)} %get-tuple-element.68), channel_id=1, source_target_pairs={{0,16},{8,24},{16,0},{24,8},{1,17},{9,25},{17,1},{25,9},{2,18},{10... | collective-permute-start | bytes 393224 | tf_op jit(solution)/shard_map/ppermute | solution.py:262
  41.6 10.3 %collective-permute-start.6 = (bf16[2,2,64,256]{3,2,1,0:T(8,128)(2,1)S(1)}, bf16[2,2,64,256]{3,2,1,0:T(8,128)(2,1)S(1)}, u32[]{:S(2)}, u32[]{:S(2)}) collective-permute-start(bf16[2,2,64,256]{3,2,1,0:T(8,128)(2,1)S(1)} %get-tuple-element.67), channel_id=1, source_target_pairs={{0,24},{8,16},{16,8},{24,0},{1,25},{9,17},{17,9},{25,1},{2,26},{10... | collective-permute-start | bytes 393224 | tf_op jit(solution)/shard_map/ppermute | solution.py:262
  41.8 13.9 %all-to-all-start.1 = ((bf16[8,2,64,256]{3,2,1,0:T(8,128)(2,1)}), bf16[8,2,64,256]{3,2,1,0:T(8,128)(2,1)S(1)}, u32[]{:S(2)}, u32[]{:S(2)}) async-start(bf16[8,2,64,256]{3,2,1,0:T(8,128)(2,1)} %get-tuple-element.37), calls=%async_computation.1 | async-start | bytes 1048576 | tf_op jit(solution)/shard_map/all_to_all | solution.py:257
  46.7 22.9 %collective-permute-start.10 = (bf16[2,2,64,256]{3,2,1,0:T(8,128)(2,1)}, bf16[2,2,64,256]{3,2,1,0:T(8,128)(2,1)S(1)}, u32[]{:S(2)}, u32[]{:S(2)}) collective-permute-start(bf16[2,2,64,256]{3,2,1,0:T(8,128)(2,1)} %get-tuple-element.65), channel_id=1, source_target_pairs={{0,8},{8,0},{16,24},{24,16},{1,9},{9,1},{17,25},{25,17},{2,10},{10... | collective-permute-start | bytes 393224 | tf_op jit(solution)/shard_map/ppermute | solution.py:262
  47.4 23.6 %collective-permute-start.11 = (bf16[2,2,64,256]{3,2,1,0:T(8,128)(2,1)}, bf16[2,2,64,256]{3,2,1,0:T(8,128)(2,1)S(1)}, u32[]{:S(2)}, u32[]{:S(2)}) collective-permute-start(bf16[2,2,64,256]{3,2,1,0:T(8,128)(2,1)} %get-tuple-element.64), channel_id=1, source_target_pairs={{0,16},{8,24},{16,0},{24,8},{1,17},{9,25},{17,1},{25,9},{2,18},{10... | collective-permute-start | bytes 393224 | tf_op jit(solution)/shard_map/ppermute | solution.py:262
  50.9 20.1 %collective-permute-start.12 = (bf16[2,2,64,256]{3,2,1,0:T(8,128)(2,1)S(1)}, bf16[2,2,64,256]{3,2,1,0:T(8,128)(2,1)S(1)}, u32[]{:S(2)}, u32[]{:S(2)}) collective-permute-start(bf16[2,2,64,256]{3,2,1,0:T(8,128)(2,1)S(1)} %get-tuple-element.63), channel_id=1, source_target_pairs={{0,24},{8,16},{16,8},{24,0},{1,25},{9,17},{17,9},{25,1},{2,26},{10... | collective-permute-start | bytes 393224 | tf_op jit(solution)/shard_map/ppermute | solution.py:262
  55.7 15.3 %all-to-all-start.3 = ((bf16[8,2,64,256]{3,2,1,0:T(8,128)(2,1)}), bf16[8,2,64,256]{3,2,1,0:T(8,128)(2,1)S(1)}, u32[]{:S(2)}, u32[]{:S(2)}) async-start(bf16[8,2,64,256]{3,2,1,0:T(8,128)(2,1)} %get-tuple-element.38), calls=%async_computation.3 | async-start | bytes 1048576 | tf_op jit(solution)/shard_map/all_to_all | solution.py:257
  59.2 0.7 copy-start.20
  59.9 11.1 %copy-start.15 = (s32[2]{0:T(128)S(1)}, s32[2]{0:T(128)}, u32[]{:S(2)}) copy-start(s32[2]{0:T(128)} %copy-done.14) | copy-start | bytes 28
  61.4 17.2 %collective-permute-start.7 = (bf16[2,2,64,256]{3,2,1,0:T(8,128)(2,1)S(1)}, bf16[2,2,64,256]{3,2,1,0:T(8,128)(2,1)S(1)}, u32[]{:S(2)}, u32[]{:S(2)}) collective-permute-start(bf16[2,2,64,256]{3,2,1,0:T(8,128)(2,1)S(1)} %get-tuple-element.42.refs_1_), channel_id=1, source_target_pairs={{0,8},{8,0},{16,24},{24,16},{1,9},{9,1},{17,25},{25,17},{2,10},{10... | collective-permute-start | bytes 393224 | tf_op jit(solution)/shard_map/ppermute | solution.py:262
  68.5 12.9 %collective-permute-start.8 = (bf16[2,2,64,256]{3,2,1,0:T(8,128)(2,1)S(1)}, bf16[2,2,64,256]{3,2,1,0:T(8,128)(2,1)S(1)}, u32[]{:S(2)}, u32[]{:S(2)}) collective-permute-start(bf16[2,2,64,256]{3,2,1,0:T(8,128)(2,1)S(1)} %get-tuple-element.43.refs_2_), channel_id=1, source_target_pairs={{0,16},{8,24},{16,0},{24,8},{1,17},{9,25},{17,1},{25,9},{2,18},{10... | collective-permute-start | bytes 393224 | tf_op jit(solution)/shard_map/ppermute | solution.py:262
  69.6 11.8 %collective-permute-start.9 = (bf16[2,2,64,256]{3,2,1,0:T(8,128)(2,1)S(1)}, bf16[2,2,64,256]{3,2,1,0:T(8,128)(2,1)S(1)}, u32[]{:S(2)}, u32[]{:S(2)}) collective-permute-start(bf16[2,2,64,256]{3,2,1,0:T(8,128)(2,1)S(1)} %get-tuple-element.44.refs_3_), channel_id=1, source_target_pairs={{0,24},{8,16},{16,8},{24,0},{1,25},{9,17},{17,9},{25,1},{2,26},{10... | collective-permute-start | bytes 393224 | tf_op jit(solution)/shard_map/ppermute | solution.py:262
  71.0 10.4 %copy-start.13 = (f32[8]{0:T(128)S(1)}, f32[8]{0:T(128)}, u32[]{:S(2)}) copy-start(f32[8]{0:T(128)} %occ.9) | copy-start | bytes 100
  72.6 21.9 %collective-permute-start.13 = (bf16[2,2,64,256]{3,2,1,0:T(8,128)(2,1)S(1)}, bf16[2,2,64,256]{3,2,1,0:T(8,128)(2,1)S(1)}, u32[]{:S(2)}, u32[]{:S(2)}) collective-permute-start(bf16[2,2,64,256]{3,2,1,0:T(8,128)(2,1)S(1)} %get-tuple-element.49.refs_1_), channel_id=1, source_target_pairs={{0,8},{8,0},{16,24},{24,16},{1,9},{9,1},{17,25},{25,17},{2,10},{10... | collective-permute-start | bytes 393224 | tf_op jit(solution)/shard_map/ppermute | solution.py:262
  77.6 18.4 %collective-permute-start.14 = (bf16[2,2,64,256]{3,2,1,0:T(8,128)(2,1)S(1)}, bf16[2,2,64,256]{3,2,1,0:T(8,128)(2,1)S(1)}, u32[]{:S(2)}, u32[]{:S(2)}) collective-permute-start(bf16[2,2,64,256]{3,2,1,0:T(8,128)(2,1)S(1)} %get-tuple-element.50.refs_2_), channel_id=1, source_target_pairs={{0,16},{8,24},{16,0},{24,8},{1,17},{9,25},{17,1},{25,9},{2,18},{10... | collective-permute-start | bytes 393224 | tf_op jit(solution)/shard_map/ppermute | solution.py:262
  78.7 17.3 %collective-permute-start.15 = (bf16[2,2,64,256]{3,2,1,0:T(8,128)(2,1)S(1)}, bf16[2,2,64,256]{3,2,1,0:T(8,128)(2,1)S(1)}, u32[]{:S(2)}, u32[]{:S(2)}) collective-permute-start(bf16[2,2,64,256]{3,2,1,0:T(8,128)(2,1)S(1)} %get-tuple-element.51.refs_3_), channel_id=1, source_target_pairs={{0,24},{8,16},{16,8},{24,0},{1,25},{9,17},{17,9},{25,1},{2,26},{10... | collective-permute-start | bytes 393224 | tf_op jit(solution)/shard_map/ppermute | solution.py:262
  84.4 14.6 %copy-start.18 = (bf16[2,8,64,256]{3,2,1,0:T(8,128)(2,1)}, bf16[2,8,64,256]{3,2,1,0:T(8,128)(2,1)S(1)}, u32[]{:S(2)}) copy-start(bf16[2,8,64,256]{3,2,1,0:T(8,128)(2,1)S(1)} %get-tuple-element.54.rest) | copy-start | bytes 1572868
  84.4 23.7 %collective-permute-start.16 = (bf16[2,2,64,256]{3,2,1,0:T(8,128)(2,1)S(1)}, bf16[2,2,64,256]{3,2,1,0:T(8,128)(2,1)S(1)}, u32[]{:S(2)}, u32[]{:S(2)}) collective-permute-start(bf16[2,2,64,256]{3,2,1,0:T(8,128)(2,1)S(1)} %get-tuple-element.56.refs_1_), channel_id=1, source_target_pairs={{0,8},{8,0},{16,24},{24,16},{1,9},{9,1},{17,25},{25,17},{2,10},{10... | collective-permute-start | bytes 393224 | tf_op jit(solution)/shard_map/ppermute | solution.py:262
  93.4 16.3 %collective-permute-start.17 = (bf16[2,2,64,256]{3,2,1,0:T(8,128)(2,1)S(1)}, bf16[2,2,64,256]{3,2,1,0:T(8,128)(2,1)S(1)}, u32[]{:S(2)}, u32[]{:S(2)}) collective-permute-start(bf16[2,2,64,256]{3,2,1,0:T(8,128)(2,1)S(1)} %get-tuple-element.57.refs_2_), channel_id=1, source_target_pairs={{0,16},{8,24},{16,0},{24,8},{1,17},{9,25},{17,1},{25,9},{2,18},{10... | collective-permute-start | bytes 393224 | tf_op jit(solution)/shard_map/ppermute | solution.py:262
  94.5 15.2 %collective-permute-start.18 = (bf16[2,2,64,256]{3,2,1,0:T(8,128)(2,1)S(1)}, bf16[2,2,64,256]{3,2,1,0:T(8,128)(2,1)S(1)}, u32[]{:S(2)}, u32[]{:S(2)}) collective-permute-start(bf16[2,2,64,256]{3,2,1,0:T(8,128)(2,1)S(1)} %get-tuple-element.58.refs_3_), channel_id=1, source_target_pairs={{0,24},{8,16},{16,8},{24,0},{1,25},{9,17},{17,9},{25,1},{2,26},{10... | collective-permute-start | bytes 393224 | tf_op jit(solution)/shard_map/ppermute | solution.py:262
  99.0 22.3 %collective-permute-start.19 = (bf16[2,2,64,256]{3,2,1,0:T(8,128)(2,1)S(1)}, bf16[2,2,64,256]{3,2,1,0:T(8,128)(2,1)S(1)}, u32[]{:S(2)}, u32[]{:S(2)}) collective-permute-start(bf16[2,2,64,256]{3,2,1,0:T(8,128)(2,1)S(1)} %get-tuple-element.60.refs_2_), channel_id=1, source_target_pairs={{0,8},{8,0},{16,24},{24,16},{1,9},{9,1},{17,25},{25,17},{2,10},{10... | collective-permute-start | bytes 393224 | tf_op jit(solution)/shard_map/ppermute | solution.py:262
  100.0 21.4 %collective-permute-start.20 = (bf16[2,2,64,256]{3,2,1,0:T(8,128)(2,1)S(1)}, bf16[2,2,64,256]{3,2,1,0:T(8,128)(2,1)S(1)}, u32[]{:S(2)}, u32[]{:S(2)}) collective-permute-start(bf16[2,2,64,256]{3,2,1,0:T(8,128)(2,1)S(1)} %get-tuple-element.61.refs_3_), channel_id=1, source_target_pairs={{0,16},{8,24},{16,0},{24,8},{1,17},{9,25},{17,1},{25,9},{2,18},{10... | collective-permute-start | bytes 393224 | tf_op jit(solution)/shard_map/ppermute | solution.py:262
  101.9 15.9 %all-to-all-start.5 = ((bf16[8,2,64,256]{3,2,1,0:T(8,128)(2,1)}), bf16[8,2,64,256]{3,2,1,0:T(8,128)(2,1)S(1)}, u32[]{:S(2)}, u32[]{:S(2)}) async-start(bf16[8,2,64,256]{3,2,1,0:T(8,128)(2,1)} %get-tuple-element.52), calls=%async_computation.5 | async-start | bytes 1048576 | tf_op jit(solution)/shard_map/all_to_all | solution.py:257
  108.1 13.3 %collective-permute-start.21 = (bf16[2,2,64,256]{3,2,1,0:T(8,128)(2,1)S(1)}, bf16[2,2,64,256]{3,2,1,0:T(8,128)(2,1)S(1)}, u32[]{:S(2)}, u32[]{:S(2)}) collective-permute-start(bf16[2,2,64,256]{3,2,1,0:T(8,128)(2,1)S(1)} %get-tuple-element.62.refs_4_), channel_id=1, source_target_pairs={{0,24},{8,16},{16,8},{24,0},{1,25},{9,17},{17,9},{25,1},{2,26},{10... | collective-permute-start | bytes 393224 | tf_op jit(solution)/shard_map/ppermute | solution.py:262
  109.7 1.0 copy-start.19
  112.0 0.8 copy-start.16
  117.8 13.2 %all-to-all-start.2 = ((bf16[8,2,64,256]{3,2,1,0:T(8,128)(2,1)}), bf16[8,2,64,256]{3,2,1,0:T(8,128)(2,1)S(1)}, u32[]{:S(2)}, u32[]{:S(2)}) async-start(bf16[8,2,64,256]{3,2,1,0:T(8,128)(2,1)} %get-tuple-element.45), calls=%async_computation.2 | async-start | bytes 1048576 | tf_op jit(solution)/shard_map/all_to_all | solution.py:257
  121.4 1.0 copy-start.17
  124.8 10.0 %copy-start.10 = (f32[512]{0:T(512)S(1)}, f32[512]{0:T(512)}, u32[]{:S(2)}) copy-start(f32[512]{0:T(512)} %param.11) | copy-start | bytes 6148
  124.8 10.1 %copy-start.2 = (bf16[3,64,512]{2,1,0:T(8,128)(2,1)S(1)}, bf16[3,64,512]{2,1,0:T(8,128)(2,1)}, u32[]{:S(2)}) copy-start(bf16[3,64,512]{2,1,0:T(8,128)(2,1)} %refs_0_.3) | copy-start | bytes 589828
  124.8 10.2 %copy-start.4 = (bf16[3,64,512]{2,1,0:T(8,128)(2,1)S(1)}, bf16[3,64,512]{2,1,0:T(8,128)(2,1)}, u32[]{:S(2)}) copy-start(bf16[3,64,512]{2,1,0:T(8,128)(2,1)} %copy-done.3) | copy-start | bytes 589828
  124.8 10.2 %copy-start.6 = (bf16[3,64,512]{2,1,0:T(8,128)(2,1)S(1)}, bf16[3,64,512]{2,1,0:T(8,128)(2,1)}, u32[]{:S(2)}) copy-start(bf16[3,64,512]{2,1,0:T(8,128)(2,1)} %copy-done.5) | copy-start | bytes 589828
  124.8 10.2 %copy-start.8 = (bf16[3,64,512]{2,1,0:T(8,128)(2,1)S(1)}, bf16[3,64,512]{2,1,0:T(8,128)(2,1)}, u32[]{:S(2)}) copy-start(bf16[3,64,512]{2,1,0:T(8,128)(2,1)} %copy-done.7) | copy-start | bytes 589828
  131.0 18.9 %all-to-all-start.6 = ((bf16[8,2,128,256]{3,2,1,0:T(8,128)(2,1)}), bf16[8,2,128,256]{3,2,1,0:T(8,128)(2,1)S(1)}, u32[]{:S(2)}, u32[]{:S(2)}) async-start(bf16[8,2,128,256]{3,2,1,0:T(8,128)(2,1)} %shard_map.82), calls=%async_computation.6 | async-start | bytes 2097152 | tf_op jit(solution)/shard_map/all_to_all | solution.py:257
  134.9 1.1 copy-start.12

commit v7 on v6

--- a/solution.py
+++ b/solution.py
@@ -51,36 +51,56 @@
     )(*operands)
 
 
-def pack_pair(tiles, source, outs, pair, mirrored=False):
+def pack_pair(tiles, source, out, pair, mirrored=False):
     e, g = tiles.edge, tiles.rows
     straight, turned = (slice(e, None), slice(0, e)) if mirrored else (slice(0, e), slice(e, None))
     for d, (a, b) in enumerate(tiles.above):
-        tile = source[tiles.span(a), tiles.span(b)].astype(NARROW)
-        other = source[tiles.span(b), tiles.span(a)].astype(WIDE).T.astype(NARROW)
-        for c, out in enumerate(outs):
-            out[d, pair, :, straight] = tile[c * g:(c + 1) * g]
-            out[d, pair, :, turned] = other[c * g:(c + 1) * g]
+        out[d, pair, :, straight] = source[tiles.span(a), tiles.span(b)].astype(NARROW)
+        out[d, pair, :, turned] = source[tiles.span(b), tiles.span(a)].astype(WIDE).T.astype(NARROW)
     for d, c, k in tiles.diagonal:
         tile = source[tiles.span(k), tiles.span(k)]
         tile = tile.astype(WIDE).T.astype(NARROW) if mirrored else tile.astype(NARROW)
-        outs[c][d, pair, :, :e] = tile[:g]
-        outs[c][d, pair, :, e:] = tile[g:]
-
-
-def unpack_pair(tiles, chunks, pair, put):
-    e = tiles.edge
+        out[d, pair, c * g:(c + 1) * g, :e] = tile[:g]
+        out[d, pair, c * g:(c + 1) * g, e:] = tile[g:]
+
+
+def unpack_pair(tiles, blocks, pair, put):
+    e, g = tiles.edge, tiles.rows
     for d, (a, b) in enumerate(tiles.above):
-        block = jnp.concatenate([chunk[d, pair] for chunk in chunks], axis=0).astype(WIDE)
-        put(a, b, block[:, :e])
-        put(b, a, block[:, e:].T)
+        put(a, b, blocks[d, pair, :, :e].astype(WIDE))
+        put(b, a, blocks[d, pair, :, e:].astype(WIDE).T)
     for d, c, k in tiles.diagonal:
-        block = chunks[c][d, pair].astype(WIDE)
-        put(k, k, jnp.concatenate([block[:, :e], block[:, e:]], axis=0))
-
-
-def pack_kernel(tiles, source, *outs):
+        upper = blocks[d, pair, c * g:(c + 1) * g, :e]
+        lower = blocks[d, pair, c * g:(c + 1) * g, e:]
+        put(k, k, jnp.concatenate([upper, lower], axis=0).astype(WIDE))
+
+
+def to_distances(place, whole, outs):
+    for k, out in enumerate(outs):
+        out[...] = whole[place[1] ^ k]
+
+
+def from_distances(place, pieces, whole):
+    for k, piece in enumerate(pieces):
+        whole[place[1] ^ k] = piece[...]
+
+
+def pack_kernel(tiles, place, source, *refs):
+    outs, whole = refs[:-1], refs[-1]
     for pair in range(source.shape[0]):
-        pack_pair(tiles, source.at[pair], outs, pair, mirrored=True)
+        pack_pair(tiles, source.at[pair], whole, pair, mirrored=True)
+    to_distances(place, whole, outs)
+
+
+def sort_kernel(tiles, groups, place, *refs):
+    pieces, outs, whole = refs[:-2 * groups - 1], refs[-2 * groups - 1:-1], refs[-1]
+    first = whole.shape[1]
+    from_distances(place, pieces, whole)
+    for s in range(groups):
+        for u in range(first):
+            block = whole[(place[0] ^ s) * first + u]
+            for c in range(2):
+                outs[c * groups + s][u] = block[:, c * tiles.rows:(c + 1) * tiles.rows]
 
 
 def assemble(place, order, pieces, whole):
@@ -111,14 +131,14 @@
 
 
 def first_ladder_kernel(tiles, order, place, source, *refs):
-    pieces, outs, (whole, inner, total) = refs[:-5], refs[-5:-3], refs[-3:]
+    pieces, (out, whole, inner, total) = refs[:-4], refs[-4:]
     assemble(place, order, pieces, whole)
     for pair in range(source.shape[0]):
         ladder_pair(source[pair].astype(NARROW), whole, inner, total)
-        pack_pair(tiles, total, outs, pair)
-
-
-def second_ladder_kernel(tiles, order, place, occ, source, upper, lower, row, column, *refs):
+        pack_pair(tiles, total, out, pair)
+
+
+def second_ladder_kernel(tiles, order, place, occ, source, blocks, row, column, *refs):
     pieces, (out, whole, inner, total, matrix) = refs[:-5], refs[-5:]
     assemble(place, order, pieces, whole)
     count = source.shape[0]
@@ -126,29 +146,31 @@
         def put(a, b, tile):
             matrix[tiles.span(a), tiles.span(b)] = tile.astype(NARROW)
 
-        unpack_pair(tiles, (upper, lower), pair, put)
+        unpack_pair(tiles, blocks, pair, put)
         ladder_pair(matrix[...], whole, inner, total)
         base = occ[place[0] * count + pair] + occ[place[1]]
+        strip = math.gcd(64, total.shape[0])
 
         def finish(step, carry):
-            at = pl.ds(pl.multiple_of(step * 16, 16), 16)
+            at = pl.ds(pl.multiple_of(step * strip, strip), strip)
             own = base - row[at, :1] - column[...]
             out[pair, at, :] = (
                 source[pair, at, :] + 2.0 * (matrix[at, :].astype(WIDE) + total[at, :] * inverse(own))
             )
             return carry
 
-        lax.fori_loop(0, total.shape[0] // 16, finish, 0)
-
-
-def add_kernel(tiles, source, blocks, out):
-    chunks = [blocks.at[:, :, :tiles.rows], blocks.at[:, :, tiles.rows:]]
+        lax.fori_loop(0, total.shape[0] // strip, finish, 0)
+
+
+def add_kernel(tiles, place, source, *refs):
+    pieces, (out, whole) = refs[:-2], refs[-2:]
+    from_distances(place, pieces, whole)
     for pair in range(source.shape[0]):
         def put(a, b, tile):
             here = (pair, tiles.span(a), tiles.span(b))
             out[here] = source[here] + tile
 
-        unpack_pair(tiles, chunks, pair, put)
+        unpack_pair(tiles, whole, pair, put)
 
 
 def mix(place, fock, first, load, store, rows):
@@ -172,14 +194,15 @@
     lax.fori_loop(0, first * strips, strip, 0)
 
 
-def half_kernel(tiles, groups, first, place, fock, ladder, *refs):
+def half_kernel(tiles, groups, first, chunk, place, fock, ladder, *refs):
     held, out = refs[:groups], refs[groups:]
 
     def load(s, u, r, at):
         return held[s][u, r, at, :].astype(WIDE)
 
     def store(s, u, w, column, at, result):
-        out[s][u, w, at, :] = (ladder[column, u, at, :].astype(WIDE) + result).astype(NARROW)
+        rows = pl.ds(pl.multiple_of(chunk * tiles.rows + at.start, 16), at.size)
+        out[s][u, w, at, :] = (ladder[column, u, rows, :].astype(WIDE) + result).astype(NARROW)
 
     mix(place, fock, first, load, store, tiles.rows)
 
@@ -197,11 +220,14 @@
 
 
 def update_kernel(tiles, groups, first, chunk, place, fock, occ, sums, *refs):
+    before, refs = refs[:chunk], refs[chunk:]
     own, other = refs[:groups], refs[groups:2 * groups]
     sent, rest = refs[2 * groups:2 * groups + 2]
     out = refs[2 * groups + 2:3 * groups + 2]
     update = refs[3 * groups + 2]
     here = slice(chunk * tiles.rows, (chunk + 1) * tiles.rows)
+    for ref in before:
+        sent[:, :, :tiles.rows, :] = ref[...]
 
     def one(step, carry):
         u, w = step // first, lax.rem(step, first)
@@ -213,7 +239,7 @@
                 value = (own[s][u, w].astype(WIDE) + mirrored) * inverse(base - sums[here])
                 narrow = value.astype(NARROW)
                 update[u, s * first + w] = value
-                sent[column, u] = narrow
+                sent[column, u, here] = narrow
                 rest[u, s * first + w] = (2.0 * (value - narrow.astype(WIDE))).astype(NARROW)
 
             with_mirror(tiles, place, other[s][w, u].astype(WIDE), finish)
@@ -231,11 +257,12 @@
 
 
 def rest_kernel(tiles, groups, first, chunk, place, occ, sums, rest, *refs):
-    before, refs = refs[:chunk], refs[chunk:]
-    own, other, out = refs[:groups], refs[groups:2 * groups], refs[2 * groups]
+    own, other, refs = refs[:groups], refs[groups:2 * groups], refs[2 * groups:]
+    out = refs[-1]
     here = slice(chunk * tiles.rows, (chunk + 1) * tiles.rows)
-    for ref in before:
-        out[:, :, :tiles.rows, :] = ref[...]
+    there = here if chunk else slice(None)
+    if chunk:
+        out[:, :, :tiles.rows, :] = refs[0][...]
 
     def one(step, carry):
         u, w = step // first, lax.rem(step, first)
@@ -245,16 +272,26 @@
 
             def finish(mirrored):
                 value = (own[s][u, w].astype(WIDE) + mirrored) * inverse(base - sums[here])
-                out[column, u, here] = (rest[u, s * first + w].astype(WIDE) + value).astype(NARROW)
+                out[column, u, there] = (rest[u, s * first + w].astype(WIDE) + value).astype(NARROW)
 
             with_mirror(tiles, place, other[s][w, u].astype(WIDE), finish)
         return carry
 
     lax.fori_loop(0, first * first, one, 0)
+    if chunk:
+        to_distances(place, out, refs[1:-1])
 
 
 def exchange(blocks):
     return lax.all_to_all(blocks, "occj", split_axis=0, concat_axis=0, tiled=True)
+
+
+def by_distance(parts):
+    devices = len(parts)
+    return [parts[0]] + [
+        lax.ppermute(parts[k], "occj", [(d, d ^ k) for d in range(devices)])
+        for k in range(devices - 1, 0, -1)
+    ][::-1]
 
 
 def across_first(parts, groups):
@@ -328,59 +365,65 @@
     square = pltpu.VMEM((virtual, virtual), WIDE)
     chunks = range(2)
 
-    started = call(functools.partial(pack_kernel, tiles), [upper] * 2, [], count, 6 * count, current, specs=[VMEM])
+    distant = jax.ShapeDtypeStruct((first, edge, 2 * edge), NARROW)
+    blocks = pltpu.VMEM(packed.shape, NARROW)
+    started = call(functools.partial(pack_kernel, tiles), [distant] * devices, [blocks], count, 6 * count,
+                   place, current, specs=[SMEM, VMEM])
     pieces, order = gather_vectors(vectors, devices, started[0])
-    held = [exchange(tie(started[0], *pieces[:-1])), exchange(started[1])]
+    held = by_distance(started)
     sums = virtual_sums(tiles, vir_energy, q)
 
     ladder_flops = first * singles * 4 * virtual**3
     ladder = call(
-        functools.partial(first_ladder_kernel, tiles, order), [upper] * 2, [whole, inner, square],
+        functools.partial(first_ladder_kernel, tiles, order), packed, [whole, inner, square],
         ladder_flops, 8 * count, place, current, *pieces, specs=[SMEM] + [VMEM] * (1 + len(pieces)),
     )
-    mirror = []
-    for c in chunks:
-        parts = tie(held[c], *ladder).reshape(groups, first, *part.shape[1:])
-        mirror.append(across_first([parts[p ^ s] for s in range(groups)], groups))
-    ladder = [exchange(x) for x in ladder]
+    parts = call(
+        functools.partial(sort_kernel, tiles, groups), [part] * (2 * groups), [blocks], count, 4 * count,
+        tie(place, ladder), *held, specs=[SMEM] + [VMEM] * devices,
+    )
+    mirror = [across_first(parts[c * groups:(c + 1) * groups], groups) for c in chunks]
+    ladder = exchange(ladder)
 
     half, other = [], []
     for c in chunks:
         half.append(call(
-            functools.partial(half_kernel, tiles, groups, first), [part] * groups, [],
-            LONG, 6 * count, after(place, *mirror[c]) if c == 0 else place, fock, ladder[c], *mirror[c],
+            functools.partial(half_kernel, tiles, groups, first, c), [part] * groups, [],
+            LONG, 6 * count, after(place, *mirror[c]) if c == 0 else place, fock, ladder, *mirror[c],
             specs=[SMEM] * 2 + [VMEM] * (groups + 1),
         ))
         other.append(across_first(half[c], groups))
-    back, rest, mixed = [], [], []
+    sent, rest, mixed = [], [], []
     for c in chunks:
-        sent, rest_one, *mixed_one = call(
+        sent_one, rest_one, *mixed_one = call(
             functools.partial(update_kernel, tiles, groups, first, c),
-            [upper, jax.ShapeDtypeStruct((first, devices, *part.shape[2:]), NARROW)] + [part] * groups,
+            [(upper, packed)[c], jax.ShapeDtypeStruct((first, devices, *part.shape[2:]), NARROW)] + [part] * groups,
             [pltpu.VMEM((first, devices, *part.shape[2:]), WIDE)],
-            LONG, 10 * count, place, fock, occ_energy, sums, *half[c], *other[c],
-            specs=[SMEM] * 3 + [VMEM] * (2 * groups + 1),
+            LONG, 10 * count, place, fock, occ_energy, sums, *sent, *half[c], *other[c],
+            specs=[SMEM] * 3 + [VMEM] * (2 * groups + 1 + c),
         )
-        back, rest, mixed = back + [exchange(sent)], rest + [rest_one], mixed + [mixed_one]
+        sent, rest, mixed = [sent_one], rest + [rest_one], mixed + [mixed_one]
     other = [across_first(x, groups) for x in mixed]
+    back = exchange(sent[0])
     base = call(
         functools.partial(second_ladder_kernel, tiles, order), jax.ShapeDtypeStruct(current.shape, WIDE),
         [whole, inner, square, pltpu.VMEM((virtual, virtual), NARROW)],
-        ladder_flops, 12 * count, place, occ_energy, current, *back,
+        ladder_flops, 12 * count, place, occ_energy, current, back,
         jnp.broadcast_to(vir_energy[:, None], (virtual, 128)), vir_energy[None, :], *pieces,
-        specs=[SMEM] * 2 + [VMEM] * (5 + len(pieces)),
+        specs=[SMEM] * 2 + [VMEM] * (4 + len(pieces)),
     )
     last = []
     for c in chunks:
-        last = [call(
-            functools.partial(rest_kernel, tiles, groups, first, c), (upper, packed)[c], [],
-            LONG, 8 * count, place, occ_energy, sums, rest[c], *last, *mixed[c], *other[c],
+        last = call(
+            functools.partial(rest_kernel, tiles, groups, first, c),
+            [distant] * devices if c else [upper], [blocks] if c else [],
+            LONG, 8 * count, place, occ_energy, sums, rest[c], *mixed[c], *other[c], *last,
             specs=[SMEM] * 2 + [VMEM] * (2 * groups + 2 + c),
-        )]
-    rest = exchange(last[0])
+        )
     done = call(
-        functools.partial(add_kernel, tiles), jax.ShapeDtypeStruct(current.shape, WIDE), [],
-        count, 10 * count, base, rest, specs=[VMEM, VMEM], aliases={0: 0},
+        functools.partial(add_kernel, tiles), jax.ShapeDtypeStruct(current.shape, WIDE), [blocks],
+        count, 10 * count, place, base, *by_distance(last), specs=[SMEM] + [VMEM] * (1 + devices),
+        aliases={1: 0},
     )
     return done.reshape(amplitudes.shape)
 

time: 154 us -> 130 us (0.84)
  waiting for transfers between devices: 28.8 us -> 17.9 us
  starting transfers between devices: 74.4 us -> 67.8 us
  Pallas kernels: 37.2 us -> 32.1 us
    all_to_all x7 -> x2, starting transfers between devices: 28 us -> 7.31 us  [exchange(): lax.all_to_all(blocks, 'occj', split_axis=0, concat_axis=0, tiled=True)]
    ppermute x0 -> x14, starting transfers between devices: none -> 17.5 us  [by_distance(): lax.ppermute(parts[k], 'occj', [(d, d ^ k) for d in range(devices)])]
    all_to_all x7 -> x2, waiting for transfers between devices: 24.1 us -> 7.72 us  [exchange(): lax.all_to_all(blocks, 'occj', split_axis=0, concat_axis=0, tiled=True)]
    pallas_call x10 -> x11, Pallas kernels: 36.1 us -> 30.9 us  [call(): pl.pallas_call(body, out_shape=outs, in_specs=specs, out_specs=jax.tree.m...]
    ppermute x18, waiting for transfers between devices: 2.19 us -> 6.91 us  [across_first(): lax.ppermute(parts[s], 'occi', [(k, k ^ s) for k in range(groups)])]
    ppermute x18, starting transfers between devices: 41.8 us -> 38.4 us  [across_first(): lax.ppermute(parts[s], 'occi', [(k, k ^ s) for k in range(groups)])]
    unnamed x48 -> x56, local copies, waits for them, and re-layouts: 6.31 us -> 7.05 us
  transfers between devices with their start and end apart: 29 -> 38, of which waited for: 8 -> 7; matrix products, arithmetic and copies ran while one was open for 3% -> 1% of each run, Pallas kernels for 22% -> 22%
where the time goes in v7:
time: 130 us; the launch traced here: 128 us
  starting transfers between devices  67.8 us (52%)
  Pallas kernels  32.1 us (25%)
  waiting for transfers between devices  17.9 us (14%)
  local copies, waits for them, and re-layouts  8.56 us (7%)
  between operations  1.76 us (1%)
    ppermute x18, starting transfers between devices, across_first(): lax.ppermute(parts[s], 'occi', [(k, k ^ s) for k in range(groups)])  38.4 us
    pallas_call x11, Pallas kernels, call(): pl.pallas_call(body, out_shape=outs, in_specs=specs, out_specs=jax.tree.m...  30.9 us
    ppermute x14, starting transfers between devices, by_distance(): lax.ppermute(parts[k], 'occj', [(d, d ^ k) for d in range(devices)])  17.5 us
    all_to_all x2, waiting for transfers between devices, exchange(): lax.all_to_all(blocks, 'occj', split_axis=0, concat_axis=0, tiled=True)  7.72 us
    all_to_all x2, starting transfers between devices, exchange(): lax.all_to_all(blocks, 'occj', split_axis=0, concat_axis=0, tiled=True)  7.31 us
    unnamed x56, local copies, waits for them, and re-layouts  7.05 us
    ppermute x18, waiting for transfers between devices, across_first(): lax.ppermute(parts[s], 'occi', [(k, k ^ s) for k in range(groups)])  6.91 us
    ppermute x4, starting transfers between devices, turn(): return lax.ppermute(x, 'occj', [(d, d ^ k) for d in range(devices)])  4.62 us
  transfers between devices with their start and end apart: 38, of which 7 were waited for; matrix products, arithmetic and copies ran while one was open for 1% of the time, Pallas kernels for 22%

profile of v7, /device:TPU:0, one launch (start us, length us, event | category | flops | bytes accessed | tf_op | source)
XLA Modules:
  0.0 128.5 jit_solution(15044833746041198809)
XLA Ops:
  0.0 3.0 %collective-permute-start = (bf16[3,64,512]{2,1,0:T(8,128)(2,1)}, bf16[3,64,512]{2,1,0:T(8,128)(2,1)S(1)}, u32[]{:S(2)}, u32[]{:S(2)}) collective-permute-start(bf16[3,64,512]{2,1,0:T(8,128)(2,1)} %refs_0_.3), channel_id=1, source_target_pairs={{0,2},{1,3},{2,0},{3,1},{4,6},{5,7},{6,4},{7,5},{8,10},{9,11},{10,... | collective-permute-start | bytes 589832 | tf_op jit(solution)/shard_map/ppermute | solution.py:325
  3.0 1.5 %collective-permute-start.1 = (bf16[3,64,512]{2,1,0:T(8,128)(2,1)}, bf16[3,64,512]{2,1,0:T(8,128)(2,1)S(1)}, u32[]{:S(2)}, u32[]{:S(2)}) collective-permute-start(bf16[3,64,512]{2,1,0:T(8,128)(2,1)} %refs_0_.3), channel_id=1, source_target_pairs={{0,4},{1,5},{2,6},{3,7},{4,0},{5,1},{6,2},{7,3},{8,12},{9,13},{10,... | collective-permute-start | bytes 589832 | tf_op jit(solution)/shard_map/ppermute | solution.py:325
  4.6 1.6 %copy-done = f32[2,1,512,512]{3,2,1,0:T(8,128)S(1)} copy-done((f32[2,1,512,512]{3,2,1,0:T(8,128)S(1)}, f32[2,1,512,512]{3,2,1,0:T(8,128)}, u32[]{:S(2)}) %copy-start) | copy-done | bytes 2097176
  6.2 0.9 shard_map.73
  7.1 1.6 %collective-permute-start.10 = (bf16[2,128,256]{2,1,0:T(8,128)(2,1)S(1)}, bf16[2,128,256]{2,1,0:T(8,128)(2,1)S(1)}, u32[]{:S(2)}, u32[]{:S(2)}) collective-permute-start(bf16[2,128,256]{2,1,0:T(8,128)(2,1)S(1)} %get-tuple-element.61), channel_id=1, source_target_pairs={{0,7},{1,6},{2,5},{3,4},{4,3},{5,2},{6,1},{7,0},{8,15},{9,14},{10,... | collective-permute-start | bytes 393224 | tf_op jit(solution)/shard_map/ppermute | solution.py:292
  8.7 1.5 %collective-permute-start.4 = (bf16[2,128,256]{2,1,0:T(8,128)(2,1)S(1)}, bf16[2,128,256]{2,1,0:T(8,128)(2,1)S(1)}, u32[]{:S(2)}, u32[]{:S(2)}) collective-permute-start(bf16[2,128,256]{2,1,0:T(8,128)(2,1)S(1)} %get-tuple-element.55), channel_id=1, source_target_pairs={{0,1},{1,0},{2,3},{3,2},{4,5},{5,4},{6,7},{7,6},{8,9},{9,8},{10,11... | collective-permute-start | bytes 393224 | tf_op jit(solution)/shard_map/ppermute | solution.py:292
  10.2 0.6 dynamic_slice.14
  11.4 0.6 dynamic_slice.12
  12.7 0.6 collective-permute-start.5
  13.3 2.5 %collective-permute-done.1.refs_2_ = bf16[3,64,512]{2,1,0:T(8,128)(2,1)S(1)} collective-permute-done((bf16[3,64,512]{2,1,0:T(8,128)(2,1)}, bf16[3,64,512]{2,1,0:T(8,128)(2,1)S(1)}, u32[]{:S(2)}, u32[]{:S(2)}) %collective-permute-start.1) | collective-permute-done | bytes 196640 | tf_op jit(solution)/shard_map/ppermute | solution.py:325
  15.8 0.1 pad_maximum_fusion
  16.4 2.4 %collective-permute-start.7 = (bf16[2,128,256]{2,1,0:T(8,128)(2,1)S(1)}, bf16[2,128,256]{2,1,0:T(8,128)(2,1)S(1)}, u32[]{:S(2)}, u32[]{:S(2)}) collective-permute-start(bf16[2,128,256]{2,1,0:T(8,128)(2,1)S(1)} %get-tuple-element.58), channel_id=1, source_target_pairs={{0,4},{1,5},{2,6},{3,7},{4,0},{5,1},{6,2},{7,3},{8,12},{9,13},{10,... | collective-permute-start | bytes 393224 | tf_op jit(solution)/shard_map/ppermute | solution.py:292
  18.8 0.2 collective-permute-start.8
  19.0 2.8 %collective-permute-start.9 = (bf16[2,128,256]{2,1,0:T(8,128)(2,1)S(1)}, bf16[2,128,256]{2,1,0:T(8,128)(2,1)S(1)}, u32[]{:S(2)}, u32[]{:S(2)}) collective-permute-start(bf16[2,128,256]{2,1,0:T(8,128)(2,1)S(1)} %get-tuple-element.60), channel_id=1, source_target_pairs={{0,6},{1,7},{2,4},{3,5},{4,2},{5,3},{6,0},{7,1},{8,14},{9,15},{10,... | collective-permute-start | bytes 393224 | tf_op jit(solution)/shard_map/ppermute | solution.py:292
  21.8 6.2 %shard_map.74 = bf16[8,2,128,256]{3,2,1,0:T(8,128)(2,1)} custom-call(s32[2]{0:T(128)S(1)} %pad_add_fusion.place.source, f32[2,512,512]{2,1,0:T(8,128)} %bitcast.13, bf16[3,64,512]{2,1,0:T(8,128)(2,1)S(1)} %copy-done.1, bf16[3,64,512]{2,1,0:T(8,128)(2,1)S(1)} %collective-permute-done.refs_1_, bf16[3,64,512]{2,1,0:T(8,128)(2,1)S(1)} %collective-permute-done.1.refs_2_, ...), custom_call_target="tpu_custom_call" | custom-call | flops 3221225472 | bytes 4194304 | tf_op jit(solution)/shard_map/pallas_call | solution.py:42
  28.1 0.3 collective-permute-done.8.refs_5_
  28.3 0.7 shard_map.75
  29.0 1.6 %collective-permute-start.11 = (bf16[2,2,64,256]{3,2,1,0:T(8,128)(2,1)S(1)}, bf16[2,2,64,256]{3,2,1,0:T(8,128)(2,1)S(1)}, u32[]{:S(2)}, u32[]{:S(2)}) collective-permute-start(bf16[2,2,64,256]{3,2,1,0:T(8,128)(2,1)S(1)} %get-tuple-element.63), channel_id=1, source_target_pairs={{0,8},{8,0},{16,24},{24,16},{1,9},{9,1},{17,25},{25,17},{2,10},{10... | collective-permute-start | bytes 393224 | tf_op jit(solution)/shard_map/ppermute | solution.py:299
  30.7 2.6 %collective-permute-start.12 = (bf16[2,2,64,256]{3,2,1,0:T(8,128)(2,1)S(1)}, bf16[2,2,64,256]{3,2,1,0:T(8,128)(2,1)S(1)}, u32[]{:S(2)}, u32[]{:S(2)}) collective-permute-start(bf16[2,2,64,256]{3,2,1,0:T(8,128)(2,1)S(1)} %get-tuple-element.64), channel_id=1, source_target_pairs={{0,16},{8,24},{16,0},{24,8},{1,17},{9,25},{17,1},{25,9},{2,18},{10... | collective-permute-start | bytes 393224 | tf_op jit(solution)/shard_map/ppermute | solution.py:299
  33.3 0.2 collective-permute-start.13
  33.6 3.6 %all-to-all-start = ((bf16[8,2,128,256]{3,2,1,0:T(8,128)(2,1)}), bf16[8,2,128,256]{3,2,1,0:T(8,128)(2,1)S(1)}, u32[]{:S(2)}, u32[]{:S(2)}) async-start(bf16[8,2,128,256]{3,2,1,0:T(8,128)(2,1)} %shard_map.74), calls=%async_computation | async-start | bytes 2097152 | tf_op jit(solution)/shard_map/all_to_all | solution.py:286
  37.2 0.7 collective-permute-start.17
  37.9 3.5 %collective-permute-start.18 = (bf16[2,2,64,256]{3,2,1,0:T(8,128)(2,1)S(1)}, bf16[2,2,64,256]{3,2,1,0:T(8,128)(2,1)S(1)}, u32[]{:S(2)}, u32[]{:S(2)}) collective-permute-start(bf16[2,2,64,256]{3,2,1,0:T(8,128)(2,1)S(1)} %get-tuple-element.74), channel_id=1, source_target_pairs={{0,16},{8,24},{16,0},{24,8},{1,17},{9,25},{17,1},{25,9},{2,18},{10... | collective-permute-start | bytes 393224 | tf_op jit(solution)/shard_map/ppermute | solution.py:299
  41.4 0.2 collective-permute-start.19
  41.6 2.0 %collective-permute-done.12.refs_2_ = bf16[2,2,64,256]{3,2,1,0:T(8,128)(2,1)S(1)} collective-permute-done((bf16[2,2,64,256]{3,2,1,0:T(8,128)(2,1)S(1)}, bf16[2,2,64,256]{3,2,1,0:T(8,128)(2,1)S(1)}, u32[]{:S(2)}, u32[]{:S(2)}) %collective-permute-start.12) | collective-permute-done | bytes 131104 | tf_op jit(solution)/shard_map/ppermute | solution.py:299
  43.6 1.2 shard_map.76.place
  44.8 7.7 %all-to-all-done.ladder = bf16[8,2,128,256]{3,2,1,0:T(8,128)(2,1)S(1)} async-done(((bf16[8,2,128,256]{3,2,1,0:T(8,128)(2,1)}), bf16[8,2,128,256]{3,2,1,0:T(8,128)(2,1)S(1)}, u32[]{:S(2)}, u32[]{:S(2)}) %all-to-all-start) | async-done | bytes 1048608 | tf_op jit(solution)/shard_map/all_to_all | solution.py:286
  52.5 0.6 copy-done.24
  53.1 1.6 %shard_map.77 = (bf16[2,2,64,256]{3,2,1,0:T(8,128)(2,1)S(1)}, bf16[2,2,64,256]{3,2,1,0:T(8,128)(2,1)S(1)}, bf16[2,2,64,256]{3,2,1,0:T(8,128)(2,1)S(1)}, bf16[2,2,64,256]{3,2,1,0:T(8,128)(2,1)S(1)}) custom-call(s32[2]{0:T(128)S(1)} %copy-done.24, f32[8,8]{1,0:T(8,128)S(1)} %convert_element_type.3.fock, bf16[8,2,128,256]{3,2,1,0:T(8,128)(2,1)S(1)} %all-to-all-done.ladder, ...), custom_call_target="tpu_custom_call" | custom-call | flops 30000001024 | bytes 3145728 | tf_op jit(solution)/shard_map/pallas_call | solution.py:42
  54.7 1.3 %collective-permute-start.14 = (bf16[2,2,64,256]{3,2,1,0:T(8,128)(2,1)S(1)}, bf16[2,2,64,256]{3,2,1,0:T(8,128)(2,1)S(1)}, u32[]{:S(2)}, u32[]{:S(2)}) collective-permute-start(bf16[2,2,64,256]{3,2,1,0:T(8,128)(2,1)S(1)} %get-tuple-element.68.refs_1_), channel_id=1, source_target_pairs={{0,8},{8,0},{16,24},{24,16},{1,9},{9,1},{17,25},{25,17},{2,10},{10... | collective-permute-start | bytes 393224 | tf_op jit(solution)/shard_map/ppermute | solution.py:299
  56.0 2.9 %collective-permute-start.15 = (bf16[2,2,64,256]{3,2,1,0:T(8,128)(2,1)S(1)}, bf16[2,2,64,256]{3,2,1,0:T(8,128)(2,1)S(1)}, u32[]{:S(2)}, u32[]{:S(2)}) collective-permute-start(bf16[2,2,64,256]{3,2,1,0:T(8,128)(2,1)S(1)} %get-tuple-element.69.refs_2_), channel_id=1, source_target_pairs={{0,16},{8,24},{16,0},{24,8},{1,17},{9,25},{17,1},{25,9},{2,18},{10... | collective-permute-start | bytes 393224 | tf_op jit(solution)/shard_map/ppermute | solution.py:299
  58.9 0.2 collective-permute-start.16
  59.2 1.6 %shard_map.79 = (bf16[2,2,64,256]{3,2,1,0:T(8,128)(2,1)S(1)}, bf16[2,2,64,256]{3,2,1,0:T(8,128)(2,1)S(1)}, bf16[2,2,64,256]{3,2,1,0:T(8,128)(2,1)S(1)}, bf16[2,2,64,256]{3,2,1,0:T(8,128)(2,1)S(1)}) custom-call(s32[2]{0:T(128)S(1)} %copy-done.12, f32[8,8]{1,0:T(8,128)S(1)} %convert_element_type.3.fock, bf16[8,2,128,256]{3,2,1,0:T(8,128)(2,1)S(1)} %all-to-all-done.ladder, ...), custom_call_target="tpu_custom_call" | custom-call | flops 30000001024 | bytes 3145728 | tf_op jit(solution)/shard_map/pallas_call | solution.py:42
  60.8 0.5 collective-permute-start.20
  61.2 3.8 %collective-permute-start.21 = (bf16[2,2,64,256]{3,2,1,0:T(8,128)(2,1)S(1)}, bf16[2,2,64,256]{3,2,1,0:T(8,128)(2,1)S(1)}, u32[]{:S(2)}, u32[]{:S(2)}) collective-permute-start(bf16[2,2,64,256]{3,2,1,0:T(8,128)(2,1)S(1)} %get-tuple-element.78.refs_3_), channel_id=1, source_target_pairs={{0,16},{8,24},{16,0},{24,8},{1,17},{9,25},{17,1},{25,9},{2,18},{10... | collective-permute-start | bytes 393224 | tf_op jit(solution)/shard_map/ppermute | solution.py:299
  65.0 3.0 %collective-permute-start.22 = (bf16[2,2,64,256]{3,2,1,0:T(8,128)(2,1)S(1)}, bf16[2,2,64,256]{3,2,1,0:T(8,128)(2,1)S(1)}, u32[]{:S(2)}, u32[]{:S(2)}) collective-permute-start(bf16[2,2,64,256]{3,2,1,0:T(8,128)(2,1)S(1)} %get-tuple-element.79.refs_4_), channel_id=1, source_target_pairs={{0,24},{8,16},{16,8},{24,0},{1,25},{9,17},{17,9},{25,1},{2,26},{10... | collective-permute-start | bytes 393224 | tf_op jit(solution)/shard_map/ppermute | solution.py:299
  68.0 0.9 collective-permute-done.15.refs_6_
  68.9 2.2 %shard_map.78 = (bf16[8,2,64,256]{3,2,1,0:T(8,128)(2,1)S(1)}, bf16[2,8,64,256]{3,2,1,0:T(8,128)(2,1)S(1)}, bf16[2,2,64,256]{3,2,1,0:T(8,128)(2,1)S(1)}, bf16[2,2...) custom-call(s32[2]{0:T(128)S(1)} %copy-done.12, ...), custom_call_target="tpu_custom_call" | custom-call | flops 30000001024 | bytes 5242880 | tf_op jit(solution)/shard_map/pallas_call | solution.py:42
  71.1 0.6 copy-done.20
  71.8 7.2 %collective-permute-start.26 = (bf16[2,2,64,256]{3,2,1,0:T(8,128)(2,1)S(1)}, bf16[2,2,64,256]{3,2,1,0:T(8,128)(2,1)S(1)}, u32[]{:S(2)}, u32[]{:S(2)}) collective-permute-start(bf16[2,2,64,256]{3,2,1,0:T(8,128)(2,1)S(1)} %get-tuple-element.88.refs_1_), channel_id=1, source_target_pairs={{0,8},{8,0},{16,24},{24,16},{1,9},{9,1},{17,25},{25,17},{2,10},{10... | collective-permute-start | bytes 393224 | tf_op jit(solution)/shard_map/ppermute | solution.py:299
  79.0 0.8 collective-permute-start.27
  79.8 1.6 %collective-permute-start.28 = (bf16[2,2,64,256]{3,2,1,0:T(8,128)(2,1)S(1)}, bf16[2,2,64,256]{3,2,1,0:T(8,128)(2,1)S(1)}, u32[]{:S(2)}, u32[]{:S(2)}) collective-permute-start(bf16[2,2,64,256]{3,2,1,0:T(8,128)(2,1)S(1)} %get-tuple-element.90.refs_3_), channel_id=1, source_target_pairs={{0,24},{8,16},{16,8},{24,0},{1,25},{9,17},{17,9},{25,1},{2,26},{10... | collective-permute-start | bytes 393224 | tf_op jit(solution)/shard_map/ppermute | solution.py:299
  81.3 3.2 %shard_map.80 = (bf16[8,2,128,256]{3,2,1,0:T(8,128)(2,1)}, bf16[2,8,64,256]{3,2,1,0:T(8,128)(2,1)S(1)}, bf16[2,2,64,256]{3,2,1,0:T(8,128)(2,1)S(1)}, bf16[2,2,64...) custom-call(s32[2]{0:T(128)S(1)} %copy-done.12, ...), custom_call_target="tpu_custom_call" | custom-call | flops 30000001024 | bytes 5242880 | tf_op jit(solution)/shard_map/pallas_call | solution.py:42
  84.6 0.8 copy-done.18
  85.4 0.6 copy-done.22
  86.0 3.1 %collective-permute-start.23 = (bf16[2,2,64,256]{3,2,1,0:T(8,128)(2,1)S(1)}, bf16[2,2,64,256]{3,2,1,0:T(8,128)(2,1)S(1)}, u32[]{:S(2)}, u32[]{:S(2)}) collective-permute-start(bf16[2,2,64,256]{3,2,1,0:T(8,128)(2,1)S(1)} %get-tuple-element.83.refs_1_), channel_id=1, source_target_pairs={{0,8},{8,0},{16,24},{24,16},{1,9},{9,1},{17,25},{25,17},{2,10},{10... | collective-permute-start | bytes 393224 | tf_op jit(solution)/shard_map/ppermute | solution.py:299
  89.2 3.6 %collective-permute-start.24 = (bf16[2,2,64,256]{3,2,1,0:T(8,128)(2,1)S(1)}, bf16[2,2,64,256]{3,2,1,0:T(8,128)(2,1)S(1)}, u32[]{:S(2)}, u32[]{:S(2)}) collective-permute-start(bf16[2,2,64,256]{3,2,1,0:T(8,128)(2,1)S(1)} %get-tuple-element.84.refs_2_), channel_id=1, source_target_pairs={{0,16},{8,24},{16,0},{24,8},{1,17},{9,25},{17,1},{25,9},{2,18},{10... | collective-permute-start | bytes 393224 | tf_op jit(solution)/shard_map/ppermute | solution.py:299
  92.8 3.7 %all-to-all-start.1 = ((bf16[8,2,128,256]{3,2,1,0:T(8,128)(2,1)}), bf16[8,2,128,256]{3,2,1,0:T(8,128)(2,1)S(1)}, u32[]{:S(2)}, u32[]{:S(2)}) async-start(bf16[8,2,128,256]{3,2,1,0:T(8,128)(2,1)} %get-tuple-element.80), calls=%async_computation.1 | async-start | bytes 2097152 | tf_op jit(solution)/shard_map/all_to_all | solution.py:286
  96.5 1.5 %collective-permute-start.25 = (bf16[2,2,64,256]{3,2,1,0:T(8,128)(2,1)S(1)}, bf16[2,2,64,256]{3,2,1,0:T(8,128)(2,1)S(1)}, u32[]{:S(2)}, u32[]{:S(2)}) collective-permute-start(bf16[2,2,64,256]{3,2,1,0:T(8,128)(2,1)S(1)} %get-tuple-element.85.refs_3_), channel_id=1, source_target_pairs={{0,24},{8,16},{16,8},{24,0},{1,25},{9,17},{17,9},{25,1},{2,26},{10... | collective-permute-start | bytes 393224 | tf_op jit(solution)/shard_map/ppermute | solution.py:299
  98.1 1.3 shard_map.82.refs_8_
  99.4 0.6 copy-done.15
  100.1 4.0 %collective-permute-done.25.refs_7_ = bf16[2,2,64,256]{3,2,1,0:T(8,128)(2,1)S(1)} collective-permute-done((bf16[2,2,64,256]{3,2,1,0:T(8,128)(2,1)S(1)}, bf16[2,2,64,256]{3,2,1,0:T(8,128)(2,1)S(1)}, u32[]{:S(2)}, u32[]{:S(2)}) %collective-permute-start.25) | collective-permute-done | bytes 131104 | tf_op jit(solution)/shard_map/ppermute | solution.py:299
  104.1 0.9 copy-done.16
  105.0 1.4 %shard_map.83 = (bf16[2,128,256]{2,1,0:T(8,128)(2,1)S(1)}, bf16[2,128,256]{2,1,0:T(8,128)(2,1)S(1)}, bf16[2,128,256]{2,1,0:T(8,128)(2,1)S(1)}, bf16[2,128,256]{2...) custom-call(s32[2]{0:T(128)S(1)} %copy-done.12, ...), custom_call_target="tpu_custom_call" | custom-call | flops 30000001024 | bytes 4194304 | tf_op jit(solution)/shard_map/pallas_call | solution.py:42
  106.5 1.7 %collective-permute-start.30 = (bf16[2,128,256]{2,1,0:T(8,128)(2,1)S(1)}, bf16[2,128,256]{2,1,0:T(8,128)(2,1)S(1)}, u32[]{:S(2)}, u32[]{:S(2)}) collective-permute-start(bf16[2,128,256]{2,1,0:T(8,128)(2,1)S(1)} %get-tuple-element.93), channel_id=1, source_target_pairs={{0,2},{1,3},{2,0},{3,1},{4,6},{5,7},{6,4},{7,5},{8,10},{9,11},{10,... | collective-permute-start | bytes 393224 | tf_op jit(solution)/shard_map/ppermute | solution.py:292
  108.2 0.1 collective-permute-start.31
  108.3 2.5 %collective-permute-start.32 = (bf16[2,128,256]{2,1,0:T(8,128)(2,1)S(1)}, bf16[2,128,256]{2,1,0:T(8,128)(2,1)S(1)}, u32[]{:S(2)}, u32[]{:S(2)}) collective-permute-start(bf16[2,128,256]{2,1,0:T(8,128)(2,1)S(1)} %get-tuple-element.95), channel_id=1, source_target_pairs={{0,4},{1,5},{2,6},{3,7},{4,0},{5,1},{6,2},{7,3},{8,12},{9,13},{10,... | collective-permute-start | bytes 393224 | tf_op jit(solution)/shard_map/ppermute | solution.py:292
  110.8 2.9 %collective-permute-start.34 = (bf16[2,128,256]{2,1,0:T(8,128)(2,1)S(1)}, bf16[2,128,256]{2,1,0:T(8,128)(2,1)S(1)}, u32[]{:S(2)}, u32[]{:S(2)}) collective-permute-start(bf16[2,128,256]{2,1,0:T(8,128)(2,1)S(1)} %get-tuple-element.97), channel_id=1, source_target_pairs={{0,6},{1,7},{2,4},{3,5},{4,2},{5,3},{6,0},{7,1},{8,14},{9,15},{10,... | collective-permute-start | bytes 393224 | tf_op jit(solution)/shard_map/ppermute | solution.py:292
  113.7 0.5 collective-permute-done.30.refs_2_
  114.2 1.1 collective-permute-start.35
  115.3 0.1 broadcast_in_dim.4.row
  115.5 1.1 copy-done.14
  116.6 8.6 %shard_map.81.source = f32[2,512,512]{2,1,0:T(8,128)} custom-call(s32[2]{0:T(128)S(1)} %copy-done.12, f32[8]{0:T(128)S(1)} %copy-done.17, f32[2,512,512]{2,1,0:T(8,128)} %bitcast.14, bf16[8,2,128,256]{3,2,1,0:T(8,128)(2,1)S(1)} %all-to-all-done.1.blocks, f32[512,128]{1,0:T(8,128)S(1)} %broadcast_in_dim.4.row, f32[1,512]{1,0:T(1,128)S(1)} %bitcast.20, ...), custom_call_target="tpu_custom_call" | custom-call | flops 3221225472 | bytes 6291456 | tf_op jit(solution)/shard_map/pallas_call | solution.py:42
  125.2 3.3 %shard_map.84 = f32[2,512,512]{2,1,0:T(8,128)} custom-call(s32[2]{0:T(128)S(1)} %copy-done.12, f32[2,512,512]{2,1,0:T(8,128)} %shard_map.81.source, bf16[2,128,256]{2,1,0:T(8,128)(2,1)S(1)} %get-tuple-element.91.refs_0_, bf16[2,128,256]{2,1,0:T(8,128)(2,1)S(1)} %collective-permute-done.29.refs_1_, ...), custom_call_target="tpu_custom_call", output_to_operand_aliasing={{}: (1, {})} | custom-call | flops 524288 | bytes 5242880 | tf_op jit(solution)/shard_map/pallas_call | solution.py:42
  (92 shorter events, 0.8 us)
Async XLA Ops:
  0.0 10.2 %copy-start.27 = (s32[8]{0:T(128)S(1)}, s32[8]{0:T(128)}, u32[]{:S(2)}) copy-start(s32[8]{0:T(128)} %constant.25.clone) | copy-start | bytes 100
  0.0 11.4 %copy-start.26 = (s32[8]{0:T(128)S(1)}, s32[8]{0:T(128)}, u32[]{:S(2)}) copy-start(s32[8]{0:T(128)} %constant.24.clone) | copy-start | bytes 100
  0.0 16.0 %copy-start.9 = (f32[512]{0:T(512)S(1)}, f32[512]{0:T(512)}, u32[]{:S(2)}) copy-start(f32[512]{0:T(512)} %param.11) | copy-start | bytes 6148
  0.0 12.7 %collective-permute-start = (bf16[3,64,512]{2,1,0:T(8,128)(2,1)}, bf16[3,64,512]{2,1,0:T(8,128)(2,1)S(1)}, u32[]{:S(2)}, u32[]{:S(2)}) collective-permute-start(bf16[3,64,512]{2,1,0:T(8,128)(2,1)} %refs_0_.3), channel_id=1, source_target_pairs={{0,2},{1,3},{2,0},{3,1},{4,6},{5,7},{6,4},{7,5},{8,10},{9,11},{10,... | collective-permute-start | bytes 589832 | tf_op jit(solution)/shard_map/ppermute | solution.py:325
  3.0 12.8 %collective-permute-start.1 = (bf16[3,64,512]{2,1,0:T(8,128)(2,1)}, bf16[3,64,512]{2,1,0:T(8,128)(2,1)S(1)}, u32[]{:S(2)}, u32[]{:S(2)}) collective-permute-start(bf16[3,64,512]{2,1,0:T(8,128)(2,1)} %refs_0_.3), channel_id=1, source_target_pairs={{0,4},{1,5},{2,6},{3,7},{4,0},{5,1},{6,2},{7,3},{8,12},{9,13},{10,... | collective-permute-start | bytes 589832 | tf_op jit(solution)/shard_map/ppermute | solution.py:325
  4.5 11.3 %collective-permute-start.2 = (bf16[3,64,512]{2,1,0:T(8,128)(2,1)}, bf16[3,64,512]{2,1,0:T(8,128)(2,1)S(1)}, u32[]{:S(2)}, u32[]{:S(2)}) collective-permute-start(bf16[3,64,512]{2,1,0:T(8,128)(2,1)} %refs_0_.3), channel_id=1, source_target_pairs={{0,6},{1,7},{2,4},{3,5},{4,2},{5,3},{6,0},{7,1},{8,14},{9,15},{10,... | collective-permute-start | bytes 589832 | tf_op jit(solution)/shard_map/ppermute | solution.py:325
  4.6 23.7 %copy-start.11 = (s32[2]{0:T(128)}, s32[2]{0:T(128)S(1)}, u32[]{:S(2)}) copy-start(s32[2]{0:T(128)S(1)} %pad_add_fusion.place.source) | copy-start | bytes 28
  4.6 1.6 %copy-start = (f32[2,1,512,512]{3,2,1,0:T(8,128)S(1)}, f32[2,1,512,512]{3,2,1,0:T(8,128)}, u32[]{:S(2)}) copy-start(f32[2,1,512,512]{3,2,1,0:T(8,128)} %param.7) | copy-start | bytes 6291460
  6.2 9.6 %copy-start.1 = (bf16[3,64,512]{2,1,0:T(8,128)(2,1)S(1)}, bf16[3,64,512]{2,1,0:T(8,128)(2,1)}, u32[]{:S(2)}) copy-start(bf16[3,64,512]{2,1,0:T(8,128)(2,1)} %refs_0_.3) | copy-start | bytes 589828
  7.1 9.3 %collective-permute-start.10 = (bf16[2,128,256]{2,1,0:T(8,128)(2,1)S(1)}, bf16[2,128,256]{2,1,0:T(8,128)(2,1)S(1)}, u32[]{:S(2)}, u32[]{:S(2)}) collective-permute-start(bf16[2,128,256]{2,1,0:T(8,128)(2,1)S(1)} %get-tuple-element.61), channel_id=1, source_target_pairs={{0,7},{1,6},{2,5},{3,4},{4,3},{5,2},{6,1},{7,0},{8,15},{9,14},{10,... | collective-permute-start | bytes 393224 | tf_op jit(solution)/shard_map/ppermute | solution.py:292
  8.7 10.1 %collective-permute-start.4 = (bf16[2,128,256]{2,1,0:T(8,128)(2,1)S(1)}, bf16[2,128,256]{2,1,0:T(8,128)(2,1)S(1)}, u32[]{:S(2)}, u32[]{:S(2)}) collective-permute-start(bf16[2,128,256]{2,1,0:T(8,128)(2,1)S(1)} %get-tuple-element.55), channel_id=1, source_target_pairs={{0,1},{1,0},{2,3},{3,2},{4,5},{5,4},{6,7},{7,6},{8,9},{9,8},{10,11... | collective-permute-start | bytes 393224 | tf_op jit(solution)/shard_map/ppermute | solution.py:292
  12.7 15.3 %copy-start.3 = (bf16[3,64,512]{2,1,0:T(8,128)(2,1)}, bf16[3,64,512]{2,1,0:T(8,128)(2,1)S(1)}, u32[]{:S(2)}) copy-start(bf16[3,64,512]{2,1,0:T(8,128)(2,1)S(1)} %collective-permute-done.refs_1_) | copy-start | bytes 589828
  12.7 15.3 %collective-permute-start.5 = (bf16[2,128,256]{2,1,0:T(8,128)(2,1)S(1)}, bf16[2,128,256]{2,1,0:T(8,128)(2,1)S(1)}, u32[]{:S(2)}, u32[]{:S(2)}) collective-permute-start(bf16[2,128,256]{2,1,0:T(8,128)(2,1)S(1)} %get-tuple-element.56), channel_id=1, source_target_pairs={{0,2},{1,3},{2,0},{3,1},{4,6},{5,7},{6,4},{7,5},{8,10},{9,11},{10,... | collective-permute-start | bytes 393224 | tf_op jit(solution)/shard_map/ppermute | solution.py:292
  15.8 12.2 %copy-start.5 = (bf16[3,64,512]{2,1,0:T(8,128)(2,1)}, bf16[3,64,512]{2,1,0:T(8,128)(2,1)S(1)}, u32[]{:S(2)}) copy-start(bf16[3,64,512]{2,1,0:T(8,128)(2,1)S(1)} %collective-permute-done.1.refs_2_) | copy-start | bytes 589828
  15.8 12.3 %collective-permute-start.6 = (bf16[2,128,256]{2,1,0:T(8,128)(2,1)S(1)}, bf16[2,128,256]{2,1,0:T(8,128)(2,1)S(1)}, u32[]{:S(2)}, u32[]{:S(2)}) collective-permute-start(bf16[2,128,256]{2,1,0:T(8,128)(2,1)S(1)} %get-tuple-element.57), channel_id=1, source_target_pairs={{0,3},{1,2},{2,1},{3,0},{4,7},{5,6},{6,5},{7,4},{8,11},{9,10},{10,... | collective-permute-start | bytes 393224 | tf_op jit(solution)/shard_map/ppermute | solution.py:292
  15.8 12.2 %copy-start.7 = (bf16[3,64,512]{2,1,0:T(8,128)(2,1)}, bf16[3,64,512]{2,1,0:T(8,128)(2,1)S(1)}, u32[]{:S(2)}) copy-start(bf16[3,64,512]{2,1,0:T(8,128)(2,1)S(1)} %collective-permute-done.2.refs_3_) | copy-start | bytes 589828
  15.9 3.0 %collective-permute-start.3 = (bf16[4,3,64,512]{3,2,1,0:T(8,128)(2,1)S(1)}, bf16[4,3,64,512]{3,2,1,0:T(8,128)(2,1)S(1)}, u32[]{:S(2)}, u32[]{:S(2)}) collective-permute-start(bf16[4,3,64,512]{3,2,1,0:T(8,128)(2,1)S(1)} %pad_maximum_fusion), channel_id=1, source_target_pairs={{0,1},{1,0},{2,3},{3,2},{4,5},{5,4},{6,7},{7,6},{8,9},{9,8},{10,11... | collective-permute-start | bytes 2359304 | tf_op jit(solution)/shard_map/ppermute | solution.py:325
  16.4 11.7 %collective-permute-start.7 = (bf16[2,128,256]{2,1,0:T(8,128)(2,1)S(1)}, bf16[2,128,256]{2,1,0:T(8,128)(2,1)S(1)}, u32[]{:S(2)}, u32[]{:S(2)}) collective-permute-start(bf16[2,128,256]{2,1,0:T(8,128)(2,1)S(1)} %get-tuple-element.58), channel_id=1, source_target_pairs={{0,4},{1,5},{2,6},{3,7},{4,0},{5,1},{6,2},{7,3},{8,12},{9,13},{10,... | collective-permute-start | bytes 393224 | tf_op jit(solution)/shard_map/ppermute | solution.py:292
  18.8 9.6 %collective-permute-start.8 = (bf16[2,128,256]{2,1,0:T(8,128)(2,1)S(1)}, bf16[2,128,256]{2,1,0:T(8,128)(2,1)S(1)}, u32[]{:S(2)}, u32[]{:S(2)}) collective-permute-start(bf16[2,128,256]{2,1,0:T(8,128)(2,1)S(1)} %get-tuple-element.59), channel_id=1, source_target_pairs={{0,5},{1,4},{2,7},{3,6},{4,1},{5,0},{6,3},{7,2},{8,13},{9,12},{10,... | collective-permute-start | bytes 393224 | tf_op jit(solution)/shard_map/ppermute | solution.py:292
  19.0 9.1 %copy-start.13 = (bf16[4,3,64,512]{3,2,1,0:T(8,128)(2,1)}, bf16[4,3,64,512]{3,2,1,0:T(8,128)(2,1)S(1)}, u32[]{:S(2)}) copy-start(bf16[4,3,64,512]{3,2,1,0:T(8,128)(2,1)S(1)} %collective-permute-done.3.refs_4_) | copy-start | bytes 2359300
  19.0 14.6 %copy-start.25 = (bf16[8,8]{1,0:T(8,128)(2,1)S(1)}, bf16[8,8]{1,0:T(8,128)(2,1)}, u32[]{:S(2)}) copy-start(bf16[8,8]{1,0:T(8,128)(2,1)} %param.9) | copy-start | bytes 388
  19.0 9.4 %collective-permute-start.9 = (bf16[2,128,256]{2,1,0:T(8,128)(2,1)S(1)}, bf16[2,128,256]{2,1,0:T(8,128)(2,1)S(1)}, u32[]{:S(2)}, u32[]{:S(2)}) collective-permute-start(bf16[2,128,256]{2,1,0:T(8,128)(2,1)S(1)} %get-tuple-element.60), channel_id=1, source_target_pairs={{0,6},{1,7},{2,4},{3,5},{4,2},{5,3},{6,0},{7,1},{8,14},{9,15},{10,... | collective-permute-start | bytes 393224 | tf_op jit(solution)/shard_map/ppermute | solution.py:292
  29.0 12.4 %collective-permute-start.11 = (bf16[2,2,64,256]{3,2,1,0:T(8,128)(2,1)S(1)}, bf16[2,2,64,256]{3,2,1,0:T(8,128)(2,1)S(1)}, u32[]{:S(2)}, u32[]{:S(2)}) collective-permute-start(bf16[2,2,64,256]{3,2,1,0:T(8,128)(2,1)S(1)} %get-tuple-element.63), channel_id=1, source_target_pairs={{0,8},{8,0},{16,24},{24,16},{1,9},{9,1},{17,25},{25,17},{2,10},{10... | collective-permute-start | bytes 393224 | tf_op jit(solution)/shard_map/ppermute | solution.py:299
  30.7 12.9 %collective-permute-start.12 = (bf16[2,2,64,256]{3,2,1,0:T(8,128)(2,1)S(1)}, bf16[2,2,64,256]{3,2,1,0:T(8,128)(2,1)S(1)}, u32[]{:S(2)}, u32[]{:S(2)}) collective-permute-start(bf16[2,2,64,256]{3,2,1,0:T(8,128)(2,1)S(1)} %get-tuple-element.64), channel_id=1, source_target_pairs={{0,16},{8,24},{16,0},{24,8},{1,17},{9,25},{17,1},{25,9},{2,18},{10... | collective-permute-start | bytes 393224 | tf_op jit(solution)/shard_map/ppermute | solution.py:299
  33.3 10.4 %collective-permute-start.13 = (bf16[2,2,64,256]{3,2,1,0:T(8,128)(2,1)S(1)}, bf16[2,2,64,256]{3,2,1,0:T(8,128)(2,1)S(1)}, u32[]{:S(2)}, u32[]{:S(2)}) collective-permute-start(bf16[2,2,64,256]{3,2,1,0:T(8,128)(2,1)S(1)} %get-tuple-element.65), channel_id=1, source_target_pairs={{0,24},{8,16},{16,8},{24,0},{1,25},{9,17},{17,9},{25,1},{2,26},{10... | collective-permute-start | bytes 393224 | tf_op jit(solution)/shard_map/ppermute | solution.py:299
  33.6 18.9 %all-to-all-start = ((bf16[8,2,128,256]{3,2,1,0:T(8,128)(2,1)}), bf16[8,2,128,256]{3,2,1,0:T(8,128)(2,1)S(1)}, u32[]{:S(2)}, u32[]{:S(2)}) async-start(bf16[8,2,128,256]{3,2,1,0:T(8,128)(2,1)} %shard_map.74), calls=%async_computation | async-start | bytes 2097152 | tf_op jit(solution)/shard_map/all_to_all | solution.py:286
  37.2 21.7 %collective-permute-start.17 = (bf16[2,2,64,256]{3,2,1,0:T(8,128)(2,1)S(1)}, bf16[2,2,64,256]{3,2,1,0:T(8,128)(2,1)S(1)}, u32[]{:S(2)}, u32[]{:S(2)}) collective-permute-start(bf16[2,2,64,256]{3,2,1,0:T(8,128)(2,1)S(1)} %get-tuple-element.73), channel_id=1, source_target_pairs={{0,8},{8,0},{16,24},{24,16},{1,9},{9,1},{17,25},{25,17},{2,10},{10... | collective-permute-start | bytes 393224 | tf_op jit(solution)/shard_map/ppermute | solution.py:299
  37.9 21.2 %collective-permute-start.18 = (bf16[2,2,64,256]{3,2,1,0:T(8,128)(2,1)S(1)}, bf16[2,2,64,256]{3,2,1,0:T(8,128)(2,1)S(1)}, u32[]{:S(2)}, u32[]{:S(2)}) collective-permute-start(bf16[2,2,64,256]{3,2,1,0:T(8,128)(2,1)S(1)} %get-tuple-element.74), channel_id=1, source_target_pairs={{0,16},{8,24},{16,0},{24,8},{1,17},{9,25},{17,1},{25,9},{2,18},{10... | collective-permute-start | bytes 393224 | tf_op jit(solution)/shard_map/ppermute | solution.py:299
  41.4 17.7 %collective-permute-start.19 = (bf16[2,2,64,256]{3,2,1,0:T(8,128)(2,1)S(1)}, bf16[2,2,64,256]{3,2,1,0:T(8,128)(2,1)S(1)}, u32[]{:S(2)}, u32[]{:S(2)}) collective-permute-start(bf16[2,2,64,256]{3,2,1,0:T(8,128)(2,1)S(1)} %get-tuple-element.75), channel_id=1, source_target_pairs={{0,24},{8,16},{16,8},{24,0},{1,25},{9,17},{17,9},{25,1},{2,26},{10... | collective-permute-start | bytes 393224 | tf_op jit(solution)/shard_map/ppermute | solution.py:299
  44.8 14.4 %copy-start.12 = (s32[2]{0:T(128)S(1)}, s32[2]{0:T(128)}, u32[]{:S(2)}) copy-start(s32[2]{0:T(128)} %copy-done.11) | copy-start | bytes 28
  54.7 10.3 %collective-permute-start.14 = (bf16[2,2,64,256]{3,2,1,0:T(8,128)(2,1)S(1)}, bf16[2,2,64,256]{3,2,1,0:T(8,128)(2,1)S(1)}, u32[]{:S(2)}, u32[]{:S(2)}) collective-permute-start(bf16[2,2,64,256]{3,2,1,0:T(8,128)(2,1)S(1)} %get-tuple-element.68.refs_1_), channel_id=1, source_target_pairs={{0,8},{8,0},{16,24},{24,16},{1,9},{9,1},{17,25},{25,17},{2,10},{10... | collective-permute-start | bytes 393224 | tf_op jit(solution)/shard_map/ppermute | solution.py:299
  56.0 12.8 %collective-permute-start.15 = (bf16[2,2,64,256]{3,2,1,0:T(8,128)(2,1)S(1)}, bf16[2,2,64,256]{3,2,1,0:T(8,128)(2,1)S(1)}, u32[]{:S(2)}, u32[]{:S(2)}) collective-permute-start(bf16[2,2,64,256]{3,2,1,0:T(8,128)(2,1)S(1)} %get-tuple-element.69.refs_2_), channel_id=1, source_target_pairs={{0,16},{8,24},{16,0},{24,8},{1,17},{9,25},{17,1},{25,9},{2,18},{10... | collective-permute-start | bytes 393224 | tf_op jit(solution)/shard_map/ppermute | solution.py:299
  58.9 9.9 %collective-permute-start.16 = (bf16[2,2,64,256]{3,2,1,0:T(8,128)(2,1)S(1)}, bf16[2,2,64,256]{3,2,1,0:T(8,128)(2,1)S(1)}, u32[]{:S(2)}, u32[]{:S(2)}) collective-permute-start(bf16[2,2,64,256]{3,2,1,0:T(8,128)(2,1)S(1)} %get-tuple-element.70.refs_3_), channel_id=1, source_target_pairs={{0,24},{8,16},{16,8},{24,0},{1,25},{9,17},{17,9},{25,1},{2,26},{10... | collective-permute-start | bytes 393224 | tf_op jit(solution)/shard_map/ppermute | solution.py:299
  59.2 9.7 %copy-start.17 = (f32[8]{0:T(128)S(1)}, f32[8]{0:T(128)}, u32[]{:S(2)}) copy-start(f32[8]{0:T(128)} %occ.9) | copy-start | bytes 100
  60.8 19.0 %collective-permute-start.20 = (bf16[2,2,64,256]{3,2,1,0:T(8,128)(2,1)S(1)}, bf16[2,2,64,256]{3,2,1,0:T(8,128)(2,1)S(1)}, u32[]{:S(2)}, u32[]{:S(2)}) collective-permute-start(bf16[2,2,64,256]{3,2,1,0:T(8,128)(2,1)S(1)} %get-tuple-element.77.refs_2_), channel_id=1, source_target_pairs={{0,8},{8,0},{16,24},{24,16},{1,9},{9,1},{17,25},{25,17},{2,10},{10... | collective-permute-start | bytes 393224 | tf_op jit(solution)/shard_map/ppermute | solution.py:299
  61.2 20.1 %collective-permute-start.21 = (bf16[2,2,64,256]{3,2,1,0:T(8,128)(2,1)S(1)}, bf16[2,2,64,256]{3,2,1,0:T(8,128)(2,1)S(1)}, u32[]{:S(2)}, u32[]{:S(2)}) collective-permute-start(bf16[2,2,64,256]{3,2,1,0:T(8,128)(2,1)S(1)} %get-tuple-element.78.refs_3_), channel_id=1, source_target_pairs={{0,16},{8,24},{16,0},{24,8},{1,17},{9,25},{17,1},{25,9},{2,18},{10... | collective-permute-start | bytes 393224 | tf_op jit(solution)/shard_map/ppermute | solution.py:299
  65.0 16.3 %collective-permute-start.22 = (bf16[2,2,64,256]{3,2,1,0:T(8,128)(2,1)S(1)}, bf16[2,2,64,256]{3,2,1,0:T(8,128)(2,1)S(1)}, u32[]{:S(2)}, u32[]{:S(2)}) collective-permute-start(bf16[2,2,64,256]{3,2,1,0:T(8,128)(2,1)S(1)} %get-tuple-element.79.refs_4_), channel_id=1, source_target_pairs={{0,24},{8,16},{16,8},{24,0},{1,25},{9,17},{17,9},{25,1},{2,26},{10... | collective-permute-start | bytes 393224 | tf_op jit(solution)/shard_map/ppermute | solution.py:299
  71.1 0.7 copy-start.20
  71.8 24.7 %collective-permute-start.26 = (bf16[2,2,64,256]{3,2,1,0:T(8,128)(2,1)S(1)}, bf16[2,2,64,256]{3,2,1,0:T(8,128)(2,1)S(1)}, u32[]{:S(2)}, u32[]{:S(2)}) collective-permute-start(bf16[2,2,64,256]{3,2,1,0:T(8,128)(2,1)S(1)} %get-tuple-element.88.refs_1_), channel_id=1, source_target_pairs={{0,8},{8,0},{16,24},{24,16},{1,9},{9,1},{17,25},{25,17},{2,10},{10... | collective-permute-start | bytes 393224 | tf_op jit(solution)/shard_map/ppermute | solution.py:299
  79.0 19.1 %collective-permute-start.27 = (bf16[2,2,64,256]{3,2,1,0:T(8,128)(2,1)S(1)}, bf16[2,2,64,256]{3,2,1,0:T(8,128)(2,1)S(1)}, u32[]{:S(2)}, u32[]{:S(2)}) collective-permute-start(bf16[2,2,64,256]{3,2,1,0:T(8,128)(2,1)S(1)} %get-tuple-element.89.refs_2_), channel_id=1, source_target_pairs={{0,16},{8,24},{16,0},{24,8},{1,17},{9,25},{17,1},{25,9},{2,18},{10... | collective-permute-start | bytes 393224 | tf_op jit(solution)/shard_map/ppermute | solution.py:299
  79.8 18.3 %collective-permute-start.28 = (bf16[2,2,64,256]{3,2,1,0:T(8,128)(2,1)S(1)}, bf16[2,2,64,256]{3,2,1,0:T(8,128)(2,1)S(1)}, u32[]{:S(2)}, u32[]{:S(2)}) collective-permute-start(bf16[2,2,64,256]{3,2,1,0:T(8,128)(2,1)S(1)} %get-tuple-element.90.refs_3_), channel_id=1, source_target_pairs={{0,24},{8,16},{16,8},{24,0},{1,25},{9,17},{17,9},{25,1},{2,26},{10... | collective-permute-start | bytes 393224 | tf_op jit(solution)/shard_map/ppermute | solution.py:299
  84.6 0.8 copy-start.18
  86.0 12.0 %copy-start.21 = (bf16[2,2,64,256]{3,2,1,0:T(8,128)(2,1)S(1)}, bf16[2,2,64,256]{3,2,1,0:T(8,128)(2,1)}, u32[]{:S(2)}) copy-start(bf16[2,2,64,256]{3,2,1,0:T(8,128)(2,1)} %copy-done.20) | copy-start | bytes 393220
  86.0 13.3 %collective-permute-start.23 = (bf16[2,2,64,256]{3,2,1,0:T(8,128)(2,1)S(1)}, bf16[2,2,64,256]{3,2,1,0:T(8,128)(2,1)S(1)}, u32[]{:S(2)}, u32[]{:S(2)}) collective-permute-start(bf16[2,2,64,256]{3,2,1,0:T(8,128)(2,1)S(1)} %get-tuple-element.83.refs_1_), channel_id=1, source_target_pairs={{0,8},{8,0},{16,24},{24,16},{1,9},{9,1},{17,25},{25,17},{2,10},{10... | collective-permute-start | bytes 393224 | tf_op jit(solution)/shard_map/ppermute | solution.py:299
  89.2 10.2 %collective-permute-start.24 = (bf16[2,2,64,256]{3,2,1,0:T(8,128)(2,1)S(1)}, bf16[2,2,64,256]{3,2,1,0:T(8,128)(2,1)S(1)}, u32[]{:S(2)}, u32[]{:S(2)}) collective-permute-start(bf16[2,2,64,256]{3,2,1,0:T(8,128)(2,1)S(1)} %get-tuple-element.84.refs_2_), channel_id=1, source_target_pairs={{0,16},{8,24},{16,0},{24,8},{1,17},{9,25},{17,1},{25,9},{2,18},{10... | collective-permute-start | bytes 393224 | tf_op jit(solution)/shard_map/ppermute | solution.py:299
  92.8 22.5 %all-to-all-start.1 = ((bf16[8,2,128,256]{3,2,1,0:T(8,128)(2,1)}), bf16[8,2,128,256]{3,2,1,0:T(8,128)(2,1)S(1)}, u32[]{:S(2)}, u32[]{:S(2)}) async-start(bf16[8,2,128,256]{3,2,1,0:T(8,128)(2,1)} %get-tuple-element.80), calls=%async_computation.1 | async-start | bytes 2097152 | tf_op jit(solution)/shard_map/all_to_all | solution.py:286
  96.5 7.5 %collective-permute-start.25 = (bf16[2,2,64,256]{3,2,1,0:T(8,128)(2,1)S(1)}, bf16[2,2,64,256]{3,2,1,0:T(8,128)(2,1)S(1)}, u32[]{:S(2)}, u32[]{:S(2)}) collective-permute-start(bf16[2,2,64,256]{3,2,1,0:T(8,128)(2,1)S(1)} %get-tuple-element.85.refs_3_), channel_id=1, source_target_pairs={{0,24},{8,16},{16,8},{24,0},{1,25},{9,17},{17,9},{25,1},{2,26},{10... | collective-permute-start | bytes 393224 | tf_op jit(solution)/shard_map/ppermute | solution.py:299
  98.1 6.0 %copy-start.19 = (bf16[2,8,64,256]{3,2,1,0:T(8,128)(2,1)S(1)}, bf16[2,8,64,256]{3,2,1,0:T(8,128)(2,1)}, u32[]{:S(2)}) copy-start(bf16[2,8,64,256]{3,2,1,0:T(8,128)(2,1)} %copy-done.18) | copy-start | bytes 1572868
  98.1 6.0 %copy-start.23 = (bf16[2,2,64,256]{3,2,1,0:T(8,128)(2,1)S(1)}, bf16[2,2,64,256]{3,2,1,0:T(8,128)(2,1)}, u32[]{:S(2)}) copy-start(bf16[2,2,64,256]{3,2,1,0:T(8,128)(2,1)} %copy-done.22) | copy-start | bytes 393220
  99.4 0.7 copy-start.15
  104.1 0.9 copy-start.16
  105.0 10.3 %copy-start.10 = (f32[512]{0:T(512)S(1)}, f32[512]{0:T(512)}, u32[]{:S(2)}) copy-start(f32[512]{0:T(512)} %param.11) | copy-start | bytes 6148
  105.0 10.5 %copy-start.2 = (bf16[3,64,512]{2,1,0:T(8,128)(2,1)S(1)}, bf16[3,64,512]{2,1,0:T(8,128)(2,1)}, u32[]{:S(2)}) copy-start(bf16[3,64,512]{2,1,0:T(8,128)(2,1)} %refs_0_.3) | copy-start | bytes 589828
  105.0 10.5 %copy-start.4 = (bf16[3,64,512]{2,1,0:T(8,128)(2,1)S(1)}, bf16[3,64,512]{2,1,0:T(8,128)(2,1)}, u32[]{:S(2)}) copy-start(bf16[3,64,512]{2,1,0:T(8,128)(2,1)} %copy-done.3) | copy-start | bytes 589828
  105.0 10.5 %copy-start.6 = (bf16[3,64,512]{2,1,0:T(8,128)(2,1)S(1)}, bf16[3,64,512]{2,1,0:T(8,128)(2,1)}, u32[]{:S(2)}) copy-start(bf16[3,64,512]{2,1,0:T(8,128)(2,1)} %copy-done.5) | copy-start | bytes 589828
  105.0 10.5 %copy-start.8 = (bf16[3,64,512]{2,1,0:T(8,128)(2,1)S(1)}, bf16[3,64,512]{2,1,0:T(8,128)(2,1)}, u32[]{:S(2)}) copy-start(bf16[3,64,512]{2,1,0:T(8,128)(2,1)} %copy-done.7) | copy-start | bytes 589828
  106.4 4.4 %collective-permute-start.29 = (bf16[2,128,256]{2,1,0:T(8,128)(2,1)S(1)}, bf16[2,128,256]{2,1,0:T(8,128)(2,1)S(1)}, u32[]{:S(2)}, u32[]{:S(2)}) collective-permute-start(bf16[2,128,256]{2,1,0:T(8,128)(2,1)S(1)} %get-tuple-element.92), channel_id=1, source_target_pairs={{0,1},{1,0},{2,3},{3,2},{4,5},{5,4},{6,7},{7,6},{8,9},{9,8},{10,11... | collective-permute-start | bytes 393224 | tf_op jit(solution)/shard_map/ppermute | solution.py:292
  106.5 7.7 %collective-permute-start.30 = (bf16[2,128,256]{2,1,0:T(8,128)(2,1)S(1)}, bf16[2,128,256]{2,1,0:T(8,128)(2,1)S(1)}, u32[]{:S(2)}, u32[]{:S(2)}) collective-permute-start(bf16[2,128,256]{2,1,0:T(8,128)(2,1)S(1)} %get-tuple-element.93), channel_id=1, source_target_pairs={{0,2},{1,3},{2,0},{3,1},{4,6},{5,7},{6,4},{7,5},{8,10},{9,11},{10,... | collective-permute-start | bytes 393224 | tf_op jit(solution)/shard_map/ppermute | solution.py:292
  108.2 17.0 %collective-permute-start.31 = (bf16[2,128,256]{2,1,0:T(8,128)(2,1)S(1)}, bf16[2,128,256]{2,1,0:T(8,128)(2,1)S(1)}, u32[]{:S(2)}, u32[]{:S(2)}) collective-permute-start(bf16[2,128,256]{2,1,0:T(8,128)(2,1)S(1)} %get-tuple-element.94), channel_id=1, source_target_pairs={{0,3},{1,2},{2,1},{3,0},{4,7},{5,6},{6,5},{7,4},{8,11},{9,10},{10,... | collective-permute-start | bytes 393224 | tf_op jit(solution)/shard_map/ppermute | solution.py:292
  108.3 16.8 %collective-permute-start.32 = (bf16[2,128,256]{2,1,0:T(8,128)(2,1)S(1)}, bf16[2,128,256]{2,1,0:T(8,128)(2,1)S(1)}, u32[]{:S(2)}, u32[]{:S(2)}) collective-permute-start(bf16[2,128,256]{2,1,0:T(8,128)(2,1)S(1)} %get-tuple-element.95), channel_id=1, source_target_pairs={{0,4},{1,5},{2,6},{3,7},{4,0},{5,1},{6,2},{7,3},{8,12},{9,13},{10,... | collective-permute-start | bytes 393224 | tf_op jit(solution)/shard_map/ppermute | solution.py:292
  110.8 14.4 %collective-permute-start.33 = (bf16[2,128,256]{2,1,0:T(8,128)(2,1)S(1)}, bf16[2,128,256]{2,1,0:T(8,128)(2,1)S(1)}, u32[]{:S(2)}, u32[]{:S(2)}) collective-permute-start(bf16[2,128,256]{2,1,0:T(8,128)(2,1)S(1)} %get-tuple-element.96), channel_id=1, source_target_pairs={{0,5},{1,4},{2,7},{3,6},{4,1},{5,0},{6,3},{7,2},{8,13},{9,12},{10,... | collective-permute-start | bytes 393224 | tf_op jit(solution)/shard_map/ppermute | solution.py:292
  110.8 14.4 %collective-permute-start.34 = (bf16[2,128,256]{2,1,0:T(8,128)(2,1)S(1)}, bf16[2,128,256]{2,1,0:T(8,128)(2,1)S(1)}, u32[]{:S(2)}, u32[]{:S(2)}) collective-permute-start(bf16[2,128,256]{2,1,0:T(8,128)(2,1)S(1)} %get-tuple-element.97), channel_id=1, source_target_pairs={{0,6},{1,7},{2,4},{3,5},{4,2},{5,3},{6,0},{7,1},{8,14},{9,15},{10,... | collective-permute-start | bytes 393224 | tf_op jit(solution)/shard_map/ppermute | solution.py:292
  114.2 11.0 %collective-permute-start.35 = (bf16[2,128,256]{2,1,0:T(8,128)(2,1)S(1)}, bf16[2,128,256]{2,1,0:T(8,128)(2,1)S(1)}, u32[]{:S(2)}, u32[]{:S(2)}) collective-permute-start(bf16[2,128,256]{2,1,0:T(8,128)(2,1)S(1)} %get-tuple-element.98), channel_id=1, source_target_pairs={{0,7},{1,6},{2,5},{3,4},{4,3},{5,2},{6,1},{7,0},{8,15},{9,14},{10,... | collective-permute-start | bytes 393224 | tf_op jit(solution)/shard_map/ppermute | solution.py:292
  115.5 1.1 copy-start.14
  (2 other events, 1.3 us)

commit v8 on v7

--- a/solution.py
+++ b/solution.py
@@ -38,7 +38,7 @@
         return jnp.concatenate([x[:, self.edge:], x[:, :self.edge]], axis=1)
 
 
-def call(body, outs, scratch, flops, moved, *operands, specs, aliases=None):
+def call(body, outs, scratch, flops, moved, *operands, specs):
     return pl.pallas_call(
         body,
         out_shape=outs,
@@ -46,7 +46,6 @@
         out_specs=jax.tree.map(lambda _: VMEM, outs),
         scratch_shapes=scratch,
         compiler_params=PARAMS,
-        input_output_aliases=aliases or {},
         cost_estimate=pl.CostEstimate(flops=flops, bytes_accessed=moved, transcendentals=0),
     )(*operands)
 
@@ -64,15 +63,15 @@
         out[d, pair, c * g:(c + 1) * g, e:] = tile[g:]
 
 
-def unpack_pair(tiles, blocks, pair, put):
-    e, g = tiles.edge, tiles.rows
+def unpack_pair(tiles, chunks, pair, put):
+    e = tiles.edge
     for d, (a, b) in enumerate(tiles.above):
-        put(a, b, blocks[d, pair, :, :e].astype(WIDE))
-        put(b, a, blocks[d, pair, :, e:].astype(WIDE).T)
+        block = jnp.concatenate([chunk[d, pair] for chunk in chunks], axis=0).astype(WIDE)
+        put(a, b, block[:, :e])
+        put(b, a, block[:, e:].T)
     for d, c, k in tiles.diagonal:
-        upper = blocks[d, pair, c * g:(c + 1) * g, :e]
-        lower = blocks[d, pair, c * g:(c + 1) * g, e:]
-        put(k, k, jnp.concatenate([upper, lower], axis=0).astype(WIDE))
+        block = chunks[c][d, pair].astype(WIDE)
+        put(k, k, jnp.concatenate([block[:, :e], block[:, e:]], axis=0))
 
 
 def to_distances(place, whole, outs):
@@ -138,7 +137,7 @@
         pack_pair(tiles, total, out, pair)
 
 
-def second_ladder_kernel(tiles, order, place, occ, source, blocks, row, column, *refs):
+def second_ladder_kernel(tiles, order, place, occ, source, upper, lower, row, column, *refs):
     pieces, (out, whole, inner, total, matrix) = refs[:-5], refs[-5:]
     assemble(place, order, pieces, whole)
     count = source.shape[0]
@@ -146,7 +145,7 @@
         def put(a, b, tile):
             matrix[tiles.span(a), tiles.span(b)] = tile.astype(NARROW)
 
-        unpack_pair(tiles, blocks, pair, put)
+        unpack_pair(tiles, (upper, lower), pair, put)
         ladder_pair(matrix[...], whole, inner, total)
         base = occ[place[0] * count + pair] + occ[place[1]]
         strip = math.gcd(64, total.shape[0])
@@ -165,12 +164,12 @@
 def add_kernel(tiles, place, source, *refs):
     pieces, (out, whole) = refs[:-2], refs[-2:]
     from_distances(place, pieces, whole)
-    for pair in range(source.shape[0]):
-        def put(a, b, tile):
-            here = (pair, tiles.span(a), tiles.span(b))
-            out[here] = source[here] + tile
-
-        unpack_pair(tiles, whole, pair, put)
+
+    def put(a, b, tile):
+        here = (0, tiles.span(a), tiles.span(b))
+        out[here] = source[here] + tile
+
+    unpack_pair(tiles, [whole.at[:, :, :tiles.rows], whole.at[:, :, tiles.rows:]], 0, put)
 
 
 def mix(place, fock, first, load, store, rows):
@@ -220,14 +219,11 @@
 
 
 def update_kernel(tiles, groups, first, chunk, place, fock, occ, sums, *refs):
-    before, refs = refs[:chunk], refs[chunk:]
     own, other = refs[:groups], refs[groups:2 * groups]
     sent, rest = refs[2 * groups:2 * groups + 2]
     out = refs[2 * groups + 2:3 * groups + 2]
     update = refs[3 * groups + 2]
     here = slice(chunk * tiles.rows, (chunk + 1) * tiles.rows)
-    for ref in before:
-        sent[:, :, :tiles.rows, :] = ref[...]
 
     def one(step, carry):
         u, w = step // first, lax.rem(step, first)
@@ -239,7 +235,7 @@
                 value = (own[s][u, w].astype(WIDE) + mirrored) * inverse(base - sums[here])
                 narrow = value.astype(NARROW)
                 update[u, s * first + w] = value
-                sent[column, u, here] = narrow
+                sent[column, u] = narrow
                 rest[u, s * first + w] = (2.0 * (value - narrow.astype(WIDE))).astype(NARROW)
 
             with_mirror(tiles, place, other[s][w, u].astype(WIDE), finish)
@@ -303,21 +299,6 @@
 
 def tie(x, *others):
     return lax.optimization_barrier((x, *others))[0]
-
-
-def copy_kernel(source, out):
-    for k in range(source.shape[0]):
-        out[k] = source[k]
-
-
-def after(x, *others):
-    return pl.pallas_call(
-        copy_kernel,
-        out_shape=jax.ShapeDtypeStruct(x.shape, x.dtype),
-        in_specs=[SMEM],
-        out_specs=SMEM,
-        cost_estimate=pl.CostEstimate(flops=LONG, bytes_accessed=8, transcendentals=0),
-    )(tie(x, *others))
 
 
 def gather_vectors(vectors, devices, packed):
@@ -389,28 +370,28 @@
     for c in chunks:
         half.append(call(
             functools.partial(half_kernel, tiles, groups, first, c), [part] * groups, [],
-            LONG, 6 * count, after(place, *mirror[c]) if c == 0 else place, fock, ladder, *mirror[c],
+            LONG, 6 * count, place, fock, ladder, *mirror[c],
             specs=[SMEM] * 2 + [VMEM] * (groups + 1),
         ))
         other.append(across_first(half[c], groups))
-    sent, rest, mixed = [], [], []
+    back, rest, mixed = [], [], []
     for c in chunks:
-        sent_one, rest_one, *mixed_one = call(
+        sent, rest_one, *mixed_one = call(
             functools.partial(update_kernel, tiles, groups, first, c),
-            [(upper, packed)[c], jax.ShapeDtypeStruct((first, devices, *part.shape[2:]), NARROW)] + [part] * groups,
+            [upper, jax.ShapeDtypeStruct((first, devices, *part.shape[2:]), NARROW)] + [part] * groups,
             [pltpu.VMEM((first, devices, *part.shape[2:]), WIDE)],
-            LONG, 10 * count, place, fock, occ_energy, sums, *sent, *half[c], *other[c],
-            specs=[SMEM] * 3 + [VMEM] * (2 * groups + 1 + c),
+            LONG, 10 * count, place, fock, occ_energy, sums, *half[c], *other[c],
+            specs=[SMEM] * 3 + [VMEM] * (2 * groups + 1),
         )
-        sent, rest, mixed = [sent_one], rest + [rest_one], mixed + [mixed_one]
+        back.append(exchange(tie(sent, *back)))
+        rest, mixed = rest + [rest_one], mixed + [mixed_one]
     other = [across_first(x, groups) for x in mixed]
-    back = exchange(sent[0])
     base = call(
         functools.partial(second_ladder_kernel, tiles, order), jax.ShapeDtypeStruct(current.shape, WIDE),
         [whole, inner, square, pltpu.VMEM((virtual, virtual), NARROW)],
-        ladder_flops, 12 * count, place, occ_energy, current, back,
+        ladder_flops, 12 * count, place, occ_energy, current, *back,
         jnp.broadcast_to(vir_energy[:, None], (virtual, 128)), vir_energy[None, :], *pieces,
-        specs=[SMEM] * 2 + [VMEM] * (4 + len(pieces)),
+        specs=[SMEM] * 2 + [VMEM] * (5 + len(pieces)),
     )
     last = []
     for c in chunks:
@@ -420,11 +401,20 @@
             LONG, 8 * count, place, occ_energy, sums, rest[c], *mixed[c], *other[c], *last,
             specs=[SMEM] * 2 + [VMEM] * (2 * groups + 2 + c),
         )
-    done = call(
-        functools.partial(add_kernel, tiles), jax.ShapeDtypeStruct(current.shape, WIDE), [blocks],
-        count, 10 * count, place, base, *by_distance(last), specs=[SMEM] + [VMEM] * (1 + devices),
-        aliases={1: 0},
-    )
+    def by_pair(*shape):
+        return pl.BlockSpec((1, *shape), lambda pair: (pair, 0, 0))
+
+    done = pl.pallas_call(
+        functools.partial(add_kernel, tiles),
+        grid=(first,),
+        out_shape=jax.ShapeDtypeStruct(current.shape, WIDE),
+        in_specs=[SMEM, by_pair(virtual, virtual)] + [by_pair(edge, 2 * edge)] * devices,
+        out_specs=by_pair(virtual, virtual),
+        scratch_shapes=[pltpu.VMEM((devices, 1, edge, 2 * edge), NARROW)],
+        compiler_params=PARAMS,
+        input_output_aliases={1: 0},
+        cost_estimate=pl.CostEstimate(flops=count, bytes_accessed=10 * count, transcendentals=0),
+    )(place, base, *by_distance(last))
     return done.reshape(amplitudes.shape)
 
 

time: 130 us -> 162 us (1.25)
  waiting for transfers between devices: 17.9 us -> 35.2 us
  starting transfers between devices: 67.8 us -> 79.6 us
  local copies, waits for them, and re-layouts: 8.56 us -> 11.9 us
    ppermute x14, waiting for transfers between devices: 0.81 us -> 16.1 us  [by_distance(): lax.ppermute(parts[k], 'occj', [(d, d ^ k) for d in range(devices)])]
    all_to_all x2 -> x3, starting transfers between devices: 7.31 us -> 14.1 us  [exchange(): lax.all_to_all(blocks, 'occj', split_axis=0, concat_axis=0, tiled=True)]
    ppermute x18, starting transfers between devices: 38.4 us -> 44.3 us  [across_first(): lax.ppermute(parts[s], 'occi', [(k, k ^ s) for k in range(groups)])]
    ppermute x4, waiting for transfers between devices: 2.49 us -> 6.71 us  [turn(): return lax.ppermute(x, 'occj', [(d, d ^ k) for d in range(devices)])]
    unnamed x56 -> x54, local copies, waits for them, and re-layouts: 7.05 us -> 10.3 us
    pallas_call x11 -> x10, Pallas kernels: 30.9 us -> 28.2 us  [call(): pl.pallas_call(body, out_shape=outs, in_specs=specs, out_specs=jax.tree.m...]
    all_to_all x2 -> x3, waiting for transfers between devices: 7.72 us -> 6.92 us  [exchange(): lax.all_to_all(blocks, 'occj', split_axis=0, concat_axis=0, tiled=True)]
  transfers between devices with their start and end apart: 38 -> 39, of which waited for: 7 -> 6; matrix products, arithmetic and copies ran while one was open for 1% -> 1% of each run, Pallas kernels for 22% -> 18%
where the time goes in v8:
time: 162 us; the launch traced here: 161 us
  starting transfers between devices  79.6 us (49%)
  waiting for transfers between devices  35.2 us (22%)
  Pallas kernels  31 us (19%)
  local copies, waits for them, and re-layouts  11.9 us (7%)
  between operations  1.62 us (1%)
    ppermute x18, starting transfers between devices, across_first(): lax.ppermute(parts[s], 'occi', [(k, k ^ s) for k in range(groups)])  44.3 us
    pallas_call x10, Pallas kernels, call(): pl.pallas_call(body, out_shape=outs, in_specs=specs, out_specs=jax.tree.m...  28.2 us
    ppermute x14, starting transfers between devices, by_distance(): lax.ppermute(parts[k], 'occj', [(d, d ^ k) for d in range(devices)])  16.6 us
    ppermute x14, waiting for transfers between devices, by_distance(): lax.ppermute(parts[k], 'occj', [(d, d ^ k) for d in range(devices)])  16.1 us
    all_to_all x3, starting transfers between devices, exchange(): lax.all_to_all(blocks, 'occj', split_axis=0, concat_axis=0, tiled=True)  14.1 us
    unnamed x54, local copies, waits for them, and re-layouts  10.3 us
    all_to_all x3, waiting for transfers between devices, exchange(): lax.all_to_all(blocks, 'occj', split_axis=0, concat_axis=0, tiled=True)  6.92 us
    ppermute x4, waiting for transfers between devices, turn(): return lax.ppermute(x, 'occj', [(d, d ^ k) for d in range(devices)])  6.71 us
  transfers between devices with their start and end apart: 39, of which 6 were waited for; matrix products, arithmetic and copies ran while one was open for 1% of the time, Pallas kernels for 18%

profile of v8, /device:TPU:0, one launch (start us, length us, event | category | flops | bytes accessed | tf_op | source)
XLA Modules:
  0.0 160.5 jit_solution(1035618108944916675)
XLA Ops:
  0.0 3.0 %collective-permute-start = (bf16[3,64,512]{2,1,0:T(8,128)(2,1)}, bf16[3,64,512]{2,1,0:T(8,128)(2,1)S(1)}, u32[]{:S(2)}, u32[]{:S(2)}) collective-permute-start(bf16[3,64,512]{2,1,0:T(8,128)(2,1)} %refs_0_.3), channel_id=1, source_target_pairs={{0,2},{1,3},{2,0},{3,1},{4,6},{5,7},{6,4},{7,5},{8,10},{9,11},{10,... | collective-permute-start | bytes 589832 | tf_op jit(solution)/shard_map/ppermute | solution.py:306
  3.0 1.5 collective-permute-start.1
  4.6 1.6 copy-done
  6.2 0.9 shard_map.73
  7.1 1.9 %collective-permute-done.refs_1_ = bf16[3,64,512]{2,1,0:T(8,128)(2,1)S(1)} collective-permute-done((bf16[3,64,512]{2,1,0:T(8,128)(2,1)}, bf16[3,64,512]{2,1,0:T(8,128)(2,1)S(1)}, u32[]{:S(2)}, u32[]{:S(2)}) %collective-permute-start) | collective-permute-done | bytes 196640 | tf_op jit(solution)/shard_map/ppermute | solution.py:306
  9.0 4.8 %collective-permute-done.1.refs_2_ = bf16[3,64,512]{2,1,0:T(8,128)(2,1)S(1)} collective-permute-done((bf16[3,64,512]{2,1,0:T(8,128)(2,1)}, bf16[3,64,512]{2,1,0:T(8,128)(2,1)S(1)}, u32[]{:S(2)}, u32[]{:S(2)}) %collective-permute-start.1) | collective-permute-done | bytes 196640 | tf_op jit(solution)/shard_map/ppermute | solution.py:306
  13.8 1.0 pad_maximum_fusion
  14.8 1.6 collective-permute-start.10
  16.4 1.5 collective-permute-start.5
  17.9 0.4 collective-permute-start.6
  18.3 0.6 dynamic_slice.14
  19.5 0.6 dynamic_slice.12
  20.9 1.2 collective-permute-start.7
  22.1 6.2 %shard_map.74 = bf16[8,2,128,256]{3,2,1,0:T(8,128)(2,1)} custom-call(s32[2]{0:T(128)S(1)} %pad_add_fusion.place, f32[2,512,512]{2,1,0:T(8,128)} %bitcast.13, bf16[3,64,512]{2,1,0:T(8,128)(2,1)S(1)} %copy-done.1, bf16[3,64,512]{2,1,0:T(8,128)(2,1)S(1)} %collective-permute-done.refs_1_, bf16[3,64,512]{2,1,0:T(8,128)(2,1)S(1)} %collective-permute-done.1.refs_2_, ...), custom_call_target="tpu_custom_call" | custom-call | flops 3221225472 | bytes 4194304 | tf_op jit(solution)/shard_map/pallas_call | solution.py:42
  28.3 3.6 %all-to-all-start = ((bf16[8,2,128,256]{3,2,1,0:T(8,128)(2,1)}), bf16[8,2,128,256]{3,2,1,0:T(8,128)(2,1)S(1)}, u32[]{:S(2)}, u32[]{:S(2)}) async-start(bf16[8,2,128,256]{3,2,1,0:T(8,128)(2,1)} %shard_map.74), calls=%async_computation | async-start | bytes 2097152 | tf_op jit(solution)/shard_map/all_to_all | solution.py:282
  32.1 1.7 %collective-permute-start.8 = (bf16[2,128,256]{2,1,0:T(8,128)(2,1)S(1)}, bf16[2,128,256]{2,1,0:T(8,128)(2,1)S(1)}, u32[]{:S(2)}, u32[]{:S(2)}) collective-permute-start(bf16[2,128,256]{2,1,0:T(8,128)(2,1)S(1)} %get-tuple-element.59), channel_id=1, source_target_pairs={{0,5},{1,4},{2,7},{3,6},{4,1},{5,0},{6,3},{7,2},{8,13},{9,12},{10,... | collective-permute-start | bytes 393224 | tf_op jit(solution)/shard_map/ppermute | solution.py:288
  33.8 1.5 collective-permute-start.9
  35.4 16.1 %collective-permute-done.8.refs_5_ = bf16[2,128,256]{2,1,0:T(8,128)(2,1)S(1)} collective-permute-done((bf16[2,128,256]{2,1,0:T(8,128)(2,1)S(1)}, bf16[2,128,256]{2,1,0:T(8,128)(2,1)S(1)}, u32[]{:S(2)}, u32[]{:S(2)}) %collective-permute-start.8) | collective-permute-done | bytes 131104 | tf_op jit(solution)/shard_map/ppermute | solution.py:288
  51.4 0.7 shard_map.75
  52.1 1.6 %collective-permute-start.11 = (bf16[2,2,64,256]{3,2,1,0:T(8,128)(2,1)S(1)}, bf16[2,2,64,256]{3,2,1,0:T(8,128)(2,1)S(1)}, u32[]{:S(2)}, u32[]{:S(2)}) collective-permute-start(bf16[2,2,64,256]{3,2,1,0:T(8,128)(2,1)S(1)} %get-tuple-element.63), channel_id=1, source_target_pairs={{0,8},{8,0},{16,24},{24,16},{1,9},{9,1},{17,25},{25,17},{2,10},{10... | collective-permute-start | bytes 393224 | tf_op jit(solution)/shard_map/ppermute | solution.py:295
  53.8 2.6 %collective-permute-start.12 = (bf16[2,2,64,256]{3,2,1,0:T(8,128)(2,1)S(1)}, bf16[2,2,64,256]{3,2,1,0:T(8,128)(2,1)S(1)}, u32[]{:S(2)}, u32[]{:S(2)}) collective-permute-start(bf16[2,2,64,256]{3,2,1,0:T(8,128)(2,1)S(1)} %get-tuple-element.64), channel_id=1, source_target_pairs={{0,16},{8,24},{16,0},{24,8},{1,17},{9,25},{17,1},{25,9},{2,18},{10... | collective-permute-start | bytes 393224 | tf_op jit(solution)/shard_map/ppermute | solution.py:295
  56.7 0.7 collective-permute-start.17
  57.5 3.5 %collective-permute-start.18 = (bf16[2,2,64,256]{3,2,1,0:T(8,128)(2,1)S(1)}, bf16[2,2,64,256]{3,2,1,0:T(8,128)(2,1)S(1)}, u32[]{:S(2)}, u32[]{:S(2)}) collective-permute-start(bf16[2,2,64,256]{3,2,1,0:T(8,128)(2,1)S(1)} %get-tuple-element.73), channel_id=1, source_target_pairs={{0,16},{8,24},{16,0},{24,8},{1,17},{9,25},{17,1},{25,9},{2,18},{10... | collective-permute-start | bytes 393224 | tf_op jit(solution)/shard_map/ppermute | solution.py:295
  61.0 2.7 %collective-permute-start.19 = (bf16[2,2,64,256]{3,2,1,0:T(8,128)(2,1)S(1)}, bf16[2,2,64,256]{3,2,1,0:T(8,128)(2,1)S(1)}, u32[]{:S(2)}, u32[]{:S(2)}) collective-permute-start(bf16[2,2,64,256]{3,2,1,0:T(8,128)(2,1)S(1)} %get-tuple-element.74), channel_id=1, source_target_pairs={{0,24},{8,16},{16,8},{24,0},{1,25},{9,17},{17,9},{25,1},{2,26},{10... | collective-permute-start | bytes 393224 | tf_op jit(solution)/shard_map/ppermute | solution.py:295
  63.7 3.0 %collective-permute-done.12.refs_2_ = bf16[2,2,64,256]{3,2,1,0:T(8,128)(2,1)S(1)} collective-permute-done((bf16[2,2,64,256]{3,2,1,0:T(8,128)(2,1)S(1)}, bf16[2,2,64,256]{3,2,1,0:T(8,128)(2,1)S(1)}, u32[]{:S(2)}, u32[]{:S(2)}) %collective-permute-start.12) | collective-permute-done | bytes 131104 | tf_op jit(solution)/shard_map/ppermute | solution.py:295
  66.7 1.6 shard_map.76
  68.3 9.1 %collective-permute-start.14 = (bf16[2,2,64,256]{3,2,1,0:T(8,128)(2,1)S(1)}, bf16[2,2,64,256]{3,2,1,0:T(8,128)(2,1)S(1)}, u32[]{:S(2)}, u32[]{:S(2)}) collective-permute-start(bf16[2,2,64,256]{3,2,1,0:T(8,128)(2,1)S(1)} %get-tuple-element.67.refs_1_), channel_id=1, source_target_pairs={{0,8},{8,0},{16,24},{24,16},{1,9},{9,1},{17,25},{25,17},{2,10},{10... | collective-permute-start | bytes 393224 | tf_op jit(solution)/shard_map/ppermute | solution.py:295
  77.4 1.1 collective-permute-start.15
  78.4 1.4 collective-permute-start.16
  79.8 1.6 shard_map.78
  81.4 4.4 %collective-permute-start.20 = (bf16[2,2,64,256]{3,2,1,0:T(8,128)(2,1)S(1)}, bf16[2,2,64,256]{3,2,1,0:T(8,128)(2,1)S(1)}, u32[]{:S(2)}, u32[]{:S(2)}) collective-permute-start(bf16[2,2,64,256]{3,2,1,0:T(8,128)(2,1)S(1)} %get-tuple-element.76.refs_1_), channel_id=1, source_target_pairs={{0,8},{8,0},{16,24},{24,16},{1,9},{9,1},{17,25},{25,17},{2,10},{10... | collective-permute-start | bytes 393224 | tf_op jit(solution)/shard_map/ppermute | solution.py:295
  85.8 2.5 %collective-permute-start.21 = (bf16[2,2,64,256]{3,2,1,0:T(8,128)(2,1)S(1)}, bf16[2,2,64,256]{3,2,1,0:T(8,128)(2,1)S(1)}, u32[]{:S(2)}, u32[]{:S(2)}) collective-permute-start(bf16[2,2,64,256]{3,2,1,0:T(8,128)(2,1)S(1)} %get-tuple-element.77.refs_2_), channel_id=1, source_target_pairs={{0,16},{8,24},{16,0},{24,8},{1,17},{9,25},{17,1},{25,9},{2,18},{10... | collective-permute-start | bytes 393224 | tf_op jit(solution)/shard_map/ppermute | solution.py:295
  88.3 1.4 collective-permute-start.22
  89.7 2.4 %collective-permute-done.15.refs_6_ = bf16[2,2,64,256]{3,2,1,0:T(8,128)(2,1)S(1)} collective-permute-done((bf16[2,2,64,256]{3,2,1,0:T(8,128)(2,1)S(1)}, bf16[2,2,64,256]{3,2,1,0:T(8,128)(2,1)S(1)}, u32[]{:S(2)}, u32[]{:S(2)}) %collective-permute-start.15) | collective-permute-done | bytes 131104 | tf_op jit(solution)/shard_map/ppermute | solution.py:295
  92.0 3.0 %shard_map.77 = (bf16[8,2,64,256]{3,2,1,0:T(8,128)(2,1)}, bf16[2,8,64,256]{3,2,1,0:T(8,128)(2,1)S(1)}, bf16[2,2,64,256]{3,2,1,0:T(8,128)(2,1)S(1)}, bf16[2,2,64,...) custom-call(s32[2]{0:T(128)S(1)} %pad_add_fusion.place, ...), custom_call_target="tpu_custom_call" | custom-call | flops 30000001024 | bytes 5242880 | tf_op jit(solution)/shard_map/pallas_call | solution.py:42
  95.1 6.2 %collective-permute-start.26 = (bf16[2,2,64,256]{3,2,1,0:T(8,128)(2,1)S(1)}, bf16[2,2,64,256]{3,2,1,0:T(8,128)(2,1)S(1)}, u32[]{:S(2)}, u32[]{:S(2)}) collective-permute-start(bf16[2,2,64,256]{3,2,1,0:T(8,128)(2,1)S(1)} %get-tuple-element.88.refs_1_), channel_id=1, source_target_pairs={{0,8},{8,0},{16,24},{24,16},{1,9},{9,1},{17,25},{25,17},{2,10},{10... | collective-permute-start | bytes 393224 | tf_op jit(solution)/shard_map/ppermute | solution.py:295
  101.3 1.0 collective-permute-start.27
  102.3 1.5 collective-permute-start.28
  103.8 3.0 %shard_map.79 = (bf16[8,2,64,256]{3,2,1,0:T(8,128)(2,1)}, bf16[2,8,64,256]{3,2,1,0:T(8,128)(2,1)S(1)}, bf16[2,2,64,256]{3,2,1,0:T(8,128)(2,1)S(1)}, bf16[2,2,64,...) custom-call(s32[2]{0:T(128)S(1)} %pad_add_fusion.place, ...), custom_call_target="tpu_custom_call" | custom-call | flops 30000001024 | bytes 5242880 | tf_op jit(solution)/shard_map/pallas_call | solution.py:42
  106.8 0.8 copy-done.18
  107.6 0.6 copy-done.22
  108.3 1.0 collective-permute-start.23
  109.3 1.9 %collective-permute-start.24 = (bf16[2,2,64,256]{3,2,1,0:T(8,128)(2,1)S(1)}, bf16[2,2,64,256]{3,2,1,0:T(8,128)(2,1)S(1)}, u32[]{:S(2)}, u32[]{:S(2)}) collective-permute-start(bf16[2,2,64,256]{3,2,1,0:T(8,128)(2,1)S(1)} %get-tuple-element.84.refs_2_), channel_id=1, source_target_pairs={{0,16},{8,24},{16,0},{24,8},{1,17},{9,25},{17,1},{25,9},{2,18},{10... | collective-permute-start | bytes 393224 | tf_op jit(solution)/shard_map/ppermute | solution.py:295
  111.2 6.9 %all-to-all-start.1 = ((bf16[8,2,64,256]{3,2,1,0:T(8,128)(2,1)}), bf16[8,2,64,256]{3,2,1,0:T(8,128)(2,1)S(1)}, u32[]{:S(2)}, u32[]{:S(2)}) async-start(bf16[8,2,64,256]{3,2,1,0:T(8,128)(2,1)} %get-tuple-element.70), calls=%async_computation.1 | async-start | bytes 1048576 | tf_op jit(solution)/shard_map/all_to_all | solution.py:282
  118.1 1.5 collective-permute-start.25
  119.6 1.3 shard_map.81.refs_8_
  120.9 6.9 %all-to-all-done.1.upper = bf16[8,2,64,256]{3,2,1,0:T(8,128)(2,1)S(1)} async-done(((bf16[8,2,64,256]{3,2,1,0:T(8,128)(2,1)}), bf16[8,2,64,256]{3,2,1,0:T(8,128)(2,1)S(1)}, u32[]{:S(2)}, u32[]{:S(2)}) %all-to-all-start.1) | async-done | bytes 524320 | tf_op jit(solution)/shard_map/all_to_all | solution.py:282
  127.8 3.7 %all-to-all-start.2 = ((bf16[8,2,64,256]{3,2,1,0:T(8,128)(2,1)}), bf16[8,2,64,256]{3,2,1,0:T(8,128)(2,1)S(1)}, u32[]{:S(2)}, u32[]{:S(2)}) async-start(bf16[8,2,64,256]{3,2,1,0:T(8,128)(2,1)} %get-tuple-element.80), calls=%async_computation.2 | async-start | bytes 1048576 | tf_op jit(solution)/shard_map/all_to_all | solution.py:282
  131.5 0.6 copy-done.13
  132.2 0.7 copy-done.15
  132.8 0.9 copy-done.14
  133.7 0.9 copy-done.16
  134.6 1.0 copy-done.19
  135.7 1.0 copy-done.21
  136.7 0.9 copy-done.23
  137.6 1.4 shard_map.82
  139.1 0.3 collective-permute-start.29
  139.3 1.7 %collective-permute-start.30 = (bf16[2,128,256]{2,1,0:T(8,128)(2,1)S(1)}, bf16[2,128,256]{2,1,0:T(8,128)(2,1)S(1)}, u32[]{:S(2)}, u32[]{:S(2)}) collective-permute-start(bf16[2,128,256]{2,1,0:T(8,128)(2,1)S(1)} %get-tuple-element.93), channel_id=1, source_target_pairs={{0,2},{1,3},{2,0},{3,1},{4,6},{5,7},{6,4},{7,5},{8,10},{9,11},{10,... | collective-permute-start | bytes 393224 | tf_op jit(solution)/shard_map/ppermute | solution.py:288
  141.0 2.5 %collective-permute-start.32 = (bf16[2,128,256]{2,1,0:T(8,128)(2,1)S(1)}, bf16[2,128,256]{2,1,0:T(8,128)(2,1)S(1)}, u32[]{:S(2)}, u32[]{:S(2)}) collective-permute-start(bf16[2,128,256]{2,1,0:T(8,128)(2,1)S(1)} %get-tuple-element.95), channel_id=1, source_target_pairs={{0,4},{1,5},{2,6},{3,7},{4,0},{5,1},{6,2},{7,3},{8,12},{9,13},{10,... | collective-permute-start | bytes 393224 | tf_op jit(solution)/shard_map/ppermute | solution.py:288
  143.6 2.9 %collective-permute-start.34 = (bf16[2,128,256]{2,1,0:T(8,128)(2,1)S(1)}, bf16[2,128,256]{2,1,0:T(8,128)(2,1)S(1)}, u32[]{:S(2)}, u32[]{:S(2)}) collective-permute-start(bf16[2,128,256]{2,1,0:T(8,128)(2,1)S(1)} %get-tuple-element.97), channel_id=1, source_target_pairs={{0,6},{1,7},{2,4},{3,5},{4,2},{5,3},{6,0},{7,1},{8,14},{9,15},{10,... | collective-permute-start | bytes 393224 | tf_op jit(solution)/shard_map/ppermute | solution.py:288
  146.5 1.4 collective-permute-start.35
  148.1 1.1 copy-done.12
  149.2 8.6 %shard_map.80.source = f32[2,512,512]{2,1,0:T(8,128)} custom-call(s32[2]{0:T(128)S(1)} %pad_add_fusion.place, f32[8]{0:T(128)S(1)} %copy-done.17, f32[2,512,512]{2,1,0:T(8,128)} %bitcast.14, bf16[8,2,64,256]{3,2,1,0:T(8,128)(2,1)S(1)} %all-to-all-done.1.upper, bf16[8,2,64,256]{3,2,1,0:T(8,128)(2,1)S(1)} %all-to-all-done.2.lower, ...), custom_call_target="tpu_custom_call" | custom-call | flops 3221225472 | bytes 6291456 | tf_op jit(solution)/shard_map/pallas_call | solution.py:42
  157.8 2.8 %shard_map.83 = f32[2,512,512]{2,1,0:T(8,128)} custom-call(s32[2]{0:T(128)S(1)} %pad_add_fusion.place, f32[2,512,512]{2,1,0:T(8,128)} %shard_map.80.source, bf16[2,128,256]{2,1,0:T(8,128)(2,1)S(1)} %get-tuple-element.91.refs_0_, bf16[2,128,256]{2,1,0:T(8,128)(2,1)S(1)} %collective-permute-done.29.refs_1_, ...), custom_call_target="tpu_custom_call", output_to_operand_aliasing={{}: (1, {})} | custom-call | flops 524288 | bytes 5242880 | tf_op jit(solution)/shard_map/pallas_call | solution.py:407
  (91 shorter events, 1.0 us)
Async XLA Ops:
  0.0 18.3 %copy-start.26 = (s32[8]{0:T(128)S(1)}, s32[8]{0:T(128)}, u32[]{:S(2)}) copy-start(s32[8]{0:T(128)} %constant.25.clone) | copy-start | bytes 100
  0.0 19.5 %copy-start.25 = (s32[8]{0:T(128)S(1)}, s32[8]{0:T(128)}, u32[]{:S(2)}) copy-start(s32[8]{0:T(128)} %constant.24.clone) | copy-start | bytes 100
  0.0 20.8 %copy-start.9 = (f32[512]{0:T(512)S(1)}, f32[512]{0:T(512)}, u32[]{:S(2)}) copy-start(f32[512]{0:T(512)} %param.11) | copy-start | bytes 6148
  0.0 8.9 %collective-permute-start = (bf16[3,64,512]{2,1,0:T(8,128)(2,1)}, bf16[3,64,512]{2,1,0:T(8,128)(2,1)S(1)}, u32[]{:S(2)}, u32[]{:S(2)}) collective-permute-start(bf16[3,64,512]{2,1,0:T(8,128)(2,1)} %refs_0_.3), channel_id=1, source_target_pairs={{0,2},{1,3},{2,0},{3,1},{4,6},{5,7},{6,4},{7,5},{8,10},{9,11},{10,... | collective-permute-start | bytes 589832 | tf_op jit(solution)/shard_map/ppermute | solution.py:306
  3.0 10.8 %collective-permute-start.1 = (bf16[3,64,512]{2,1,0:T(8,128)(2,1)}, bf16[3,64,512]{2,1,0:T(8,128)(2,1)S(1)}, u32[]{:S(2)}, u32[]{:S(2)}) collective-permute-start(bf16[3,64,512]{2,1,0:T(8,128)(2,1)} %refs_0_.3), channel_id=1, source_target_pairs={{0,4},{1,5},{2,6},{3,7},{4,0},{5,1},{6,2},{7,3},{8,12},{9,13},{10,... | collective-permute-start | bytes 589832 | tf_op jit(solution)/shard_map/ppermute | solution.py:306
  4.5 9.3 %collective-permute-start.2 = (bf16[3,64,512]{2,1,0:T(8,128)(2,1)}, bf16[3,64,512]{2,1,0:T(8,128)(2,1)S(1)}, u32[]{:S(2)}, u32[]{:S(2)}) collective-permute-start(bf16[3,64,512]{2,1,0:T(8,128)(2,1)} %refs_0_.3), channel_id=1, source_target_pairs={{0,6},{1,7},{2,4},{3,5},{4,2},{5,3},{6,0},{7,1},{8,14},{9,15},{10,... | collective-permute-start | bytes 589832 | tf_op jit(solution)/shard_map/ppermute | solution.py:306
  4.6 1.6 copy-start
  6.2 7.6 %copy-start.1 = (bf16[3,64,512]{2,1,0:T(8,128)(2,1)S(1)}, bf16[3,64,512]{2,1,0:T(8,128)(2,1)}, u32[]{:S(2)}) copy-start(bf16[3,64,512]{2,1,0:T(8,128)(2,1)} %refs_0_.3) | copy-start | bytes 589828
  9.0 19.3 %copy-start.3 = (bf16[3,64,512]{2,1,0:T(8,128)(2,1)}, bf16[3,64,512]{2,1,0:T(8,128)(2,1)S(1)}, u32[]{:S(2)}) copy-start(bf16[3,64,512]{2,1,0:T(8,128)(2,1)S(1)} %collective-permute-done.refs_1_) | copy-start | bytes 589828
  13.8 14.5 %copy-start.5 = (bf16[3,64,512]{2,1,0:T(8,128)(2,1)}, bf16[3,64,512]{2,1,0:T(8,128)(2,1)S(1)}, u32[]{:S(2)}) copy-start(bf16[3,64,512]{2,1,0:T(8,128)(2,1)S(1)} %collective-permute-done.1.refs_2_) | copy-start | bytes 589828
  13.8 14.5 %copy-start.7 = (bf16[3,64,512]{2,1,0:T(8,128)(2,1)}, bf16[3,64,512]{2,1,0:T(8,128)(2,1)S(1)}, u32[]{:S(2)}) copy-start(bf16[3,64,512]{2,1,0:T(8,128)(2,1)S(1)} %collective-permute-done.2.refs_3_) | copy-start | bytes 589828
  14.8 6.1 %collective-permute-start.3 = (bf16[4,3,64,512]{3,2,1,0:T(8,128)(2,1)}, bf16[4,3,64,512]{3,2,1,0:T(8,128)(2,1)S(1)}, u32[]{:S(2)}, u32[]{:S(2)}) collective-permute-start(bf16[4,3,64,512]{3,2,1,0:T(8,128)(2,1)} %pad_maximum_fusion), channel_id=1, source_target_pairs={{0,1},{1,0},{2,3},{3,2},{4,5},{5,4},{6,7},{7,6},{8,9},{9,8},{10,11... | collective-permute-start | bytes 2359304 | tf_op jit(solution)/shard_map/ppermute | solution.py:306
  14.8 17.2 %collective-permute-start.10 = (bf16[2,128,256]{2,1,0:T(8,128)(2,1)S(1)}, bf16[2,128,256]{2,1,0:T(8,128)(2,1)S(1)}, u32[]{:S(2)}, u32[]{:S(2)}) collective-permute-start(bf16[2,128,256]{2,1,0:T(8,128)(2,1)S(1)} %get-tuple-element.61), channel_id=1, source_target_pairs={{0,7},{1,6},{2,5},{3,4},{4,3},{5,2},{6,1},{7,0},{8,15},{9,14},{10,... | collective-permute-start | bytes 393224 | tf_op jit(solution)/shard_map/ppermute | solution.py:288
  16.4 17.3 %collective-permute-start.4 = (bf16[2,128,256]{2,1,0:T(8,128)(2,1)S(1)}, bf16[2,128,256]{2,1,0:T(8,128)(2,1)S(1)}, u32[]{:S(2)}, u32[]{:S(2)}) collective-permute-start(bf16[2,128,256]{2,1,0:T(8,128)(2,1)S(1)} %get-tuple-element.55), channel_id=1, source_target_pairs={{0,1},{1,0},{2,3},{3,2},{4,5},{5,4},{6,7},{7,6},{8,9},{9,8},{10,11... | collective-permute-start | bytes 393224 | tf_op jit(solution)/shard_map/ppermute | solution.py:288
  16.4 18.9 %collective-permute-start.5 = (bf16[2,128,256]{2,1,0:T(8,128)(2,1)S(1)}, bf16[2,128,256]{2,1,0:T(8,128)(2,1)S(1)}, u32[]{:S(2)}, u32[]{:S(2)}) collective-permute-start(bf16[2,128,256]{2,1,0:T(8,128)(2,1)S(1)} %get-tuple-element.56), channel_id=1, source_target_pairs={{0,2},{1,3},{2,0},{3,1},{4,6},{5,7},{6,4},{7,5},{8,10},{9,11},{10,... | collective-permute-start | bytes 393224 | tf_op jit(solution)/shard_map/ppermute | solution.py:288
  17.9 17.4 %collective-permute-start.6 = (bf16[2,128,256]{2,1,0:T(8,128)(2,1)S(1)}, bf16[2,128,256]{2,1,0:T(8,128)(2,1)S(1)}, u32[]{:S(2)}, u32[]{:S(2)}) collective-permute-start(bf16[2,128,256]{2,1,0:T(8,128)(2,1)S(1)} %get-tuple-element.57), channel_id=1, source_target_pairs={{0,3},{1,2},{2,1},{3,0},{4,7},{5,6},{6,5},{7,4},{8,11},{9,10},{10,... | collective-permute-start | bytes 393224 | tf_op jit(solution)/shard_map/ppermute | solution.py:288
  20.9 7.4 %copy-start.11 = (bf16[4,3,64,512]{3,2,1,0:T(8,128)(2,1)}, bf16[4,3,64,512]{3,2,1,0:T(8,128)(2,1)S(1)}, u32[]{:S(2)}) copy-start(bf16[4,3,64,512]{3,2,1,0:T(8,128)(2,1)S(1)} %collective-permute-done.3.refs_4_) | copy-start | bytes 2359300
  20.9 14.5 %collective-permute-start.7 = (bf16[2,128,256]{2,1,0:T(8,128)(2,1)S(1)}, bf16[2,128,256]{2,1,0:T(8,128)(2,1)S(1)}, u32[]{:S(2)}, u32[]{:S(2)}) collective-permute-start(bf16[2,128,256]{2,1,0:T(8,128)(2,1)S(1)} %get-tuple-element.58), channel_id=1, source_target_pairs={{0,4},{1,5},{2,6},{3,7},{4,0},{5,1},{6,2},{7,3},{8,12},{9,13},{10,... | collective-permute-start | bytes 393224 | tf_op jit(solution)/shard_map/ppermute | solution.py:288
  28.3 28.3 %copy-start.24 = (bf16[8,8]{1,0:T(8,128)(2,1)S(1)}, bf16[8,8]{1,0:T(8,128)(2,1)}, u32[]{:S(2)}) copy-start(bf16[8,8]{1,0:T(8,128)(2,1)} %param.9) | copy-start | bytes 388
  28.3 38.4 %all-to-all-start = ((bf16[8,2,128,256]{3,2,1,0:T(8,128)(2,1)}), bf16[8,2,128,256]{3,2,1,0:T(8,128)(2,1)S(1)}, u32[]{:S(2)}, u32[]{:S(2)}) async-start(bf16[8,2,128,256]{3,2,1,0:T(8,128)(2,1)} %shard_map.74), calls=%async_computation | async-start | bytes 2097152 | tf_op jit(solution)/shard_map/all_to_all | solution.py:282
  32.1 19.4 %collective-permute-start.8 = (bf16[2,128,256]{2,1,0:T(8,128)(2,1)S(1)}, bf16[2,128,256]{2,1,0:T(8,128)(2,1)S(1)}, u32[]{:S(2)}, u32[]{:S(2)}) collective-permute-start(bf16[2,128,256]{2,1,0:T(8,128)(2,1)S(1)} %get-tuple-element.59), channel_id=1, source_target_pairs={{0,5},{1,4},{2,7},{3,6},{4,1},{5,0},{6,3},{7,2},{8,13},{9,12},{10,... | collective-permute-start | bytes 393224 | tf_op jit(solution)/shard_map/ppermute | solution.py:288
  33.8 17.7 %collective-permute-start.9 = (bf16[2,128,256]{2,1,0:T(8,128)(2,1)S(1)}, bf16[2,128,256]{2,1,0:T(8,128)(2,1)S(1)}, u32[]{:S(2)}, u32[]{:S(2)}) collective-permute-start(bf16[2,128,256]{2,1,0:T(8,128)(2,1)S(1)} %get-tuple-element.60), channel_id=1, source_target_pairs={{0,6},{1,7},{2,4},{3,5},{4,2},{5,3},{6,0},{7,1},{8,14},{9,15},{10,... | collective-permute-start | bytes 393224 | tf_op jit(solution)/shard_map/ppermute | solution.py:288
  52.1 8.8 %collective-permute-start.11 = (bf16[2,2,64,256]{3,2,1,0:T(8,128)(2,1)S(1)}, bf16[2,2,64,256]{3,2,1,0:T(8,128)(2,1)S(1)}, u32[]{:S(2)}, u32[]{:S(2)}) collective-permute-start(bf16[2,2,64,256]{3,2,1,0:T(8,128)(2,1)S(1)} %get-tuple-element.63), channel_id=1, source_target_pairs={{0,8},{8,0},{16,24},{24,16},{1,9},{9,1},{17,25},{25,17},{2,10},{10... | collective-permute-start | bytes 393224 | tf_op jit(solution)/shard_map/ppermute | solution.py:295
  53.8 13.0 %collective-permute-start.12 = (bf16[2,2,64,256]{3,2,1,0:T(8,128)(2,1)S(1)}, bf16[2,2,64,256]{3,2,1,0:T(8,128)(2,1)S(1)}, u32[]{:S(2)}, u32[]{:S(2)}) collective-permute-start(bf16[2,2,64,256]{3,2,1,0:T(8,128)(2,1)S(1)} %get-tuple-element.64), channel_id=1, source_target_pairs={{0,16},{8,24},{16,0},{24,8},{1,17},{9,25},{17,1},{25,9},{2,18},{10... | collective-permute-start | bytes 393224 | tf_op jit(solution)/shard_map/ppermute | solution.py:295
  56.4 10.4 %collective-permute-start.13 = (bf16[2,2,64,256]{3,2,1,0:T(8,128)(2,1)S(1)}, bf16[2,2,64,256]{3,2,1,0:T(8,128)(2,1)S(1)}, u32[]{:S(2)}, u32[]{:S(2)}) collective-permute-start(bf16[2,2,64,256]{3,2,1,0:T(8,128)(2,1)S(1)} %get-tuple-element.65), channel_id=1, source_target_pairs={{0,24},{8,16},{16,8},{24,0},{1,25},{9,17},{17,9},{25,1},{2,26},{10... | collective-permute-start | bytes 393224 | tf_op jit(solution)/shard_map/ppermute | solution.py:295
  56.7 21.7 %collective-permute-start.17 = (bf16[2,2,64,256]{3,2,1,0:T(8,128)(2,1)S(1)}, bf16[2,2,64,256]{3,2,1,0:T(8,128)(2,1)S(1)}, u32[]{:S(2)}, u32[]{:S(2)}) collective-permute-start(bf16[2,2,64,256]{3,2,1,0:T(8,128)(2,1)S(1)} %get-tuple-element.72), channel_id=1, source_target_pairs={{0,8},{8,0},{16,24},{24,16},{1,9},{9,1},{17,25},{25,17},{2,10},{10... | collective-permute-start | bytes 393224 | tf_op jit(solution)/shard_map/ppermute | solution.py:295
  57.5 22.4 %collective-permute-start.18 = (bf16[2,2,64,256]{3,2,1,0:T(8,128)(2,1)S(1)}, bf16[2,2,64,256]{3,2,1,0:T(8,128)(2,1)S(1)}, u32[]{:S(2)}, u32[]{:S(2)}) collective-permute-start(bf16[2,2,64,256]{3,2,1,0:T(8,128)(2,1)S(1)} %get-tuple-element.73), channel_id=1, source_target_pairs={{0,16},{8,24},{16,0},{24,8},{1,17},{9,25},{17,1},{25,9},{2,18},{10... | collective-permute-start | bytes 393224 | tf_op jit(solution)/shard_map/ppermute | solution.py:295
  61.0 18.9 %collective-permute-start.19 = (bf16[2,2,64,256]{3,2,1,0:T(8,128)(2,1)S(1)}, bf16[2,2,64,256]{3,2,1,0:T(8,128)(2,1)S(1)}, u32[]{:S(2)}, u32[]{:S(2)}) collective-permute-start(bf16[2,2,64,256]{3,2,1,0:T(8,128)(2,1)S(1)} %get-tuple-element.74), channel_id=1, source_target_pairs={{0,24},{8,16},{16,8},{24,0},{1,25},{9,17},{17,9},{25,1},{2,26},{10... | collective-permute-start | bytes 393224 | tf_op jit(solution)/shard_map/ppermute | solution.py:295
  68.3 20.0 %collective-permute-start.14 = (bf16[2,2,64,256]{3,2,1,0:T(8,128)(2,1)S(1)}, bf16[2,2,64,256]{3,2,1,0:T(8,128)(2,1)S(1)}, u32[]{:S(2)}, u32[]{:S(2)}) collective-permute-start(bf16[2,2,64,256]{3,2,1,0:T(8,128)(2,1)S(1)} %get-tuple-element.67.refs_1_), channel_id=1, source_target_pairs={{0,8},{8,0},{16,24},{24,16},{1,9},{9,1},{17,25},{25,17},{2,10},{10... | collective-permute-start | bytes 393224 | tf_op jit(solution)/shard_map/ppermute | solution.py:295
  77.4 14.7 %collective-permute-start.15 = (bf16[2,2,64,256]{3,2,1,0:T(8,128)(2,1)S(1)}, bf16[2,2,64,256]{3,2,1,0:T(8,128)(2,1)S(1)}, u32[]{:S(2)}, u32[]{:S(2)}) collective-permute-start(bf16[2,2,64,256]{3,2,1,0:T(8,128)(2,1)S(1)} %get-tuple-element.68.refs_2_), channel_id=1, source_target_pairs={{0,16},{8,24},{16,0},{24,8},{1,17},{9,25},{17,1},{25,9},{2,18},{10... | collective-permute-start | bytes 393224 | tf_op jit(solution)/shard_map/ppermute | solution.py:295
  78.4 13.6 %collective-permute-start.16 = (bf16[2,2,64,256]{3,2,1,0:T(8,128)(2,1)S(1)}, bf16[2,2,64,256]{3,2,1,0:T(8,128)(2,1)S(1)}, u32[]{:S(2)}, u32[]{:S(2)}) collective-permute-start(bf16[2,2,64,256]{3,2,1,0:T(8,128)(2,1)S(1)} %get-tuple-element.69.refs_3_), channel_id=1, source_target_pairs={{0,24},{8,16},{16,8},{24,0},{1,25},{9,17},{17,9},{25,1},{2,26},{10... | collective-permute-start | bytes 393224 | tf_op jit(solution)/shard_map/ppermute | solution.py:295
  79.8 12.2 %copy-start.17 = (f32[8]{0:T(128)S(1)}, f32[8]{0:T(128)}, u32[]{:S(2)}) copy-start(f32[8]{0:T(128)} %occ.9) | copy-start | bytes 100
  81.4 20.8 %collective-permute-start.20 = (bf16[2,2,64,256]{3,2,1,0:T(8,128)(2,1)S(1)}, bf16[2,2,64,256]{3,2,1,0:T(8,128)(2,1)S(1)}, u32[]{:S(2)}, u32[]{:S(2)}) collective-permute-start(bf16[2,2,64,256]{3,2,1,0:T(8,128)(2,1)S(1)} %get-tuple-element.76.refs_1_), channel_id=1, source_target_pairs={{0,8},{8,0},{16,24},{24,16},{1,9},{9,1},{17,25},{25,17},{2,10},{10... | collective-permute-start | bytes 393224 | tf_op jit(solution)/shard_map/ppermute | solution.py:295
  85.8 18.0 %collective-permute-start.21 = (bf16[2,2,64,256]{3,2,1,0:T(8,128)(2,1)S(1)}, bf16[2,2,64,256]{3,2,1,0:T(8,128)(2,1)S(1)}, u32[]{:S(2)}, u32[]{:S(2)}) collective-permute-start(bf16[2,2,64,256]{3,2,1,0:T(8,128)(2,1)S(1)} %get-tuple-element.77.refs_2_), channel_id=1, source_target_pairs={{0,16},{8,24},{16,0},{24,8},{1,17},{9,25},{17,1},{25,9},{2,18},{10... | collective-permute-start | bytes 393224 | tf_op jit(solution)/shard_map/ppermute | solution.py:295
  88.3 15.5 %collective-permute-start.22 = (bf16[2,2,64,256]{3,2,1,0:T(8,128)(2,1)S(1)}, bf16[2,2,64,256]{3,2,1,0:T(8,128)(2,1)S(1)}, u32[]{:S(2)}, u32[]{:S(2)}) collective-permute-start(bf16[2,2,64,256]{3,2,1,0:T(8,128)(2,1)S(1)} %get-tuple-element.78.refs_3_), channel_id=1, source_target_pairs={{0,24},{8,16},{16,8},{24,0},{1,25},{9,17},{17,9},{25,1},{2,26},{10... | collective-permute-start | bytes 393224 | tf_op jit(solution)/shard_map/ppermute | solution.py:295
  95.1 23.0 %collective-permute-start.26 = (bf16[2,2,64,256]{3,2,1,0:T(8,128)(2,1)S(1)}, bf16[2,2,64,256]{3,2,1,0:T(8,128)(2,1)S(1)}, u32[]{:S(2)}, u32[]{:S(2)}) collective-permute-start(bf16[2,2,64,256]{3,2,1,0:T(8,128)(2,1)S(1)} %get-tuple-element.88.refs_1_), channel_id=1, source_target_pairs={{0,8},{8,0},{16,24},{24,16},{1,9},{9,1},{17,25},{25,17},{2,10},{10... | collective-permute-start | bytes 393224 | tf_op jit(solution)/shard_map/ppermute | solution.py:295
  101.3 18.3 %collective-permute-start.27 = (bf16[2,2,64,256]{3,2,1,0:T(8,128)(2,1)S(1)}, bf16[2,2,64,256]{3,2,1,0:T(8,128)(2,1)S(1)}, u32[]{:S(2)}, u32[]{:S(2)}) collective-permute-start(bf16[2,2,64,256]{3,2,1,0:T(8,128)(2,1)S(1)} %get-tuple-element.89.refs_2_), channel_id=1, source_target_pairs={{0,16},{8,24},{16,0},{24,8},{1,17},{9,25},{17,1},{25,9},{2,18},{10... | collective-permute-start | bytes 393224 | tf_op jit(solution)/shard_map/ppermute | solution.py:295
  102.3 17.3 %collective-permute-start.28 = (bf16[2,2,64,256]{3,2,1,0:T(8,128)(2,1)S(1)}, bf16[2,2,64,256]{3,2,1,0:T(8,128)(2,1)S(1)}, u32[]{:S(2)}, u32[]{:S(2)}) collective-permute-start(bf16[2,2,64,256]{3,2,1,0:T(8,128)(2,1)S(1)} %get-tuple-element.90.refs_3_), channel_id=1, source_target_pairs={{0,24},{8,16},{16,8},{24,0},{1,25},{9,17},{17,9},{25,1},{2,26},{10... | collective-permute-start | bytes 393224 | tf_op jit(solution)/shard_map/ppermute | solution.py:295
  106.8 0.8 copy-start.18
  108.3 23.2 %collective-permute-start.23 = (bf16[2,2,64,256]{3,2,1,0:T(8,128)(2,1)S(1)}, bf16[2,2,64,256]{3,2,1,0:T(8,128)(2,1)S(1)}, u32[]{:S(2)}, u32[]{:S(2)}) collective-permute-start(bf16[2,2,64,256]{3,2,1,0:T(8,128)(2,1)S(1)} %get-tuple-element.83.refs_1_), channel_id=1, source_target_pairs={{0,8},{8,0},{16,24},{24,16},{1,9},{9,1},{17,25},{25,17},{2,10},{10... | collective-permute-start | bytes 393224 | tf_op jit(solution)/shard_map/ppermute | solution.py:295
  109.3 22.2 %collective-permute-start.24 = (bf16[2,2,64,256]{3,2,1,0:T(8,128)(2,1)S(1)}, bf16[2,2,64,256]{3,2,1,0:T(8,128)(2,1)S(1)}, u32[]{:S(2)}, u32[]{:S(2)}) collective-permute-start(bf16[2,2,64,256]{3,2,1,0:T(8,128)(2,1)S(1)} %get-tuple-element.84.refs_2_), channel_id=1, source_target_pairs={{0,16},{8,24},{16,0},{24,8},{1,17},{9,25},{17,1},{25,9},{2,18},{10... | collective-permute-start | bytes 393224 | tf_op jit(solution)/shard_map/ppermute | solution.py:295
  111.2 16.6 %all-to-all-start.1 = ((bf16[8,2,64,256]{3,2,1,0:T(8,128)(2,1)}), bf16[8,2,64,256]{3,2,1,0:T(8,128)(2,1)S(1)}, u32[]{:S(2)}, u32[]{:S(2)}) async-start(bf16[8,2,64,256]{3,2,1,0:T(8,128)(2,1)} %get-tuple-element.70), calls=%async_computation.1 | async-start | bytes 1048576 | tf_op jit(solution)/shard_map/all_to_all | solution.py:282
  118.1 14.1 %collective-permute-start.25 = (bf16[2,2,64,256]{3,2,1,0:T(8,128)(2,1)S(1)}, bf16[2,2,64,256]{3,2,1,0:T(8,128)(2,1)S(1)}, u32[]{:S(2)}, u32[]{:S(2)}) collective-permute-start(bf16[2,2,64,256]{3,2,1,0:T(8,128)(2,1)S(1)} %get-tuple-element.85.refs_3_), channel_id=1, source_target_pairs={{0,24},{8,16},{16,8},{24,0},{1,25},{9,17},{17,9},{25,1},{2,26},{10... | collective-permute-start | bytes 393224 | tf_op jit(solution)/shard_map/ppermute | solution.py:295
  120.9 11.9 %copy-start.20 = (bf16[8,2,64,256]{3,2,1,0:T(8,128)(2,1)}, bf16[8,2,64,256]{3,2,1,0:T(8,128)(2,1)S(1)}, u32[]{:S(2)}) copy-start(bf16[8,2,64,256]{3,2,1,0:T(8,128)(2,1)S(1)} %shard_map.81.refs_8_) | copy-start | bytes 1572868
  127.8 20.1 %all-to-all-start.2 = ((bf16[8,2,64,256]{3,2,1,0:T(8,128)(2,1)}), bf16[8,2,64,256]{3,2,1,0:T(8,128)(2,1)S(1)}, u32[]{:S(2)}, u32[]{:S(2)}) async-start(bf16[8,2,64,256]{3,2,1,0:T(8,128)(2,1)} %get-tuple-element.80), calls=%async_computation.2 | async-start | bytes 1048576 | tf_op jit(solution)/shard_map/all_to_all | solution.py:282
  131.5 0.7 copy-start.13
  132.8 0.9 copy-start.14
  133.7 0.9 copy-start.16
  134.6 1.0 copy-start.19
  135.7 1.0 copy-start.21
  136.7 0.9 copy-start.23
  137.6 10.3 %copy-start.10 = (f32[512]{0:T(512)S(1)}, f32[512]{0:T(512)}, u32[]{:S(2)}) copy-start(f32[512]{0:T(512)} %param.11) | copy-start | bytes 6148
  137.6 10.4 %copy-start.2 = (bf16[3,64,512]{2,1,0:T(8,128)(2,1)S(1)}, bf16[3,64,512]{2,1,0:T(8,128)(2,1)}, u32[]{:S(2)}) copy-start(bf16[3,64,512]{2,1,0:T(8,128)(2,1)} %refs_0_.3) | copy-start | bytes 589828
  137.6 10.4 %copy-start.4 = (bf16[3,64,512]{2,1,0:T(8,128)(2,1)S(1)}, bf16[3,64,512]{2,1,0:T(8,128)(2,1)}, u32[]{:S(2)}) copy-start(bf16[3,64,512]{2,1,0:T(8,128)(2,1)} %copy-done.3) | copy-start | bytes 589828
  137.6 10.4 %copy-start.6 = (bf16[3,64,512]{2,1,0:T(8,128)(2,1)S(1)}, bf16[3,64,512]{2,1,0:T(8,128)(2,1)}, u32[]{:S(2)}) copy-start(bf16[3,64,512]{2,1,0:T(8,128)(2,1)} %copy-done.5) | copy-start | bytes 589828
  137.6 10.4 %copy-start.8 = (bf16[3,64,512]{2,1,0:T(8,128)(2,1)S(1)}, bf16[3,64,512]{2,1,0:T(8,128)(2,1)}, u32[]{:S(2)}) copy-start(bf16[3,64,512]{2,1,0:T(8,128)(2,1)} %copy-done.7) | copy-start | bytes 589828
  139.1 4.5 %collective-permute-start.29 = (bf16[2,128,256]{2,1,0:T(8,128)(2,1)S(1)}, bf16[2,128,256]{2,1,0:T(8,128)(2,1)S(1)}, u32[]{:S(2)}, u32[]{:S(2)}) collective-permute-start(bf16[2,128,256]{2,1,0:T(8,128)(2,1)S(1)} %get-tuple-element.92), channel_id=1, source_target_pairs={{0,1},{1,0},{2,3},{3,2},{4,5},{5,4},{6,7},{7,6},{8,9},{9,8},{10,11... | collective-permute-start | bytes 393224 | tf_op jit(solution)/shard_map/ppermute | solution.py:288
  139.3 7.2 %collective-permute-start.30 = (bf16[2,128,256]{2,1,0:T(8,128)(2,1)S(1)}, bf16[2,128,256]{2,1,0:T(8,128)(2,1)S(1)}, u32[]{:S(2)}, u32[]{:S(2)}) collective-permute-start(bf16[2,128,256]{2,1,0:T(8,128)(2,1)S(1)} %get-tuple-element.93), channel_id=1, source_target_pairs={{0,2},{1,3},{2,0},{3,1},{4,6},{5,7},{6,4},{7,5},{8,10},{9,11},{10,... | collective-permute-start | bytes 393224 | tf_op jit(solution)/shard_map/ppermute | solution.py:288
  141.0 16.7 %collective-permute-start.31 = (bf16[2,128,256]{2,1,0:T(8,128)(2,1)S(1)}, bf16[2,128,256]{2,1,0:T(8,128)(2,1)S(1)}, u32[]{:S(2)}, u32[]{:S(2)}) collective-permute-start(bf16[2,128,256]{2,1,0:T(8,128)(2,1)S(1)} %get-tuple-element.94), channel_id=1, source_target_pairs={{0,3},{1,2},{2,1},{3,0},{4,7},{5,6},{6,5},{7,4},{8,11},{9,10},{10,... | collective-permute-start | bytes 393224 | tf_op jit(solution)/shard_map/ppermute | solution.py:288
  141.0 16.7 %collective-permute-start.32 = (bf16[2,128,256]{2,1,0:T(8,128)(2,1)S(1)}, bf16[2,128,256]{2,1,0:T(8,128)(2,1)S(1)}, u32[]{:S(2)}, u32[]{:S(2)}) collective-permute-start(bf16[2,128,256]{2,1,0:T(8,128)(2,1)S(1)} %get-tuple-element.95), channel_id=1, source_target_pairs={{0,4},{1,5},{2,6},{3,7},{4,0},{5,1},{6,2},{7,3},{8,12},{9,13},{10,... | collective-permute-start | bytes 393224 | tf_op jit(solution)/shard_map/ppermute | solution.py:288
  143.6 14.2 %collective-permute-start.33 = (bf16[2,128,256]{2,1,0:T(8,128)(2,1)S(1)}, bf16[2,128,256]{2,1,0:T(8,128)(2,1)S(1)}, u32[]{:S(2)}, u32[]{:S(2)}) collective-permute-start(bf16[2,128,256]{2,1,0:T(8,128)(2,1)S(1)} %get-tuple-element.96), channel_id=1, source_target_pairs={{0,5},{1,4},{2,7},{3,6},{4,1},{5,0},{6,3},{7,2},{8,13},{9,12},{10,... | collective-permute-start | bytes 393224 | tf_op jit(solution)/shard_map/ppermute | solution.py:288
  143.6 14.2 %collective-permute-start.34 = (bf16[2,128,256]{2,1,0:T(8,128)(2,1)S(1)}, bf16[2,128,256]{2,1,0:T(8,128)(2,1)S(1)}, u32[]{:S(2)}, u32[]{:S(2)}) collective-permute-start(bf16[2,128,256]{2,1,0:T(8,128)(2,1)S(1)} %get-tuple-element.97), channel_id=1, source_target_pairs={{0,6},{1,7},{2,4},{3,5},{4,2},{5,3},{6,0},{7,1},{8,14},{9,15},{10,... | collective-permute-start | bytes 393224 | tf_op jit(solution)/shard_map/ppermute | solution.py:288
  146.5 11.3 %collective-permute-start.35 = (bf16[2,128,256]{2,1,0:T(8,128)(2,1)S(1)}, bf16[2,128,256]{2,1,0:T(8,128)(2,1)S(1)}, u32[]{:S(2)}, u32[]{:S(2)}) collective-permute-start(bf16[2,128,256]{2,1,0:T(8,128)(2,1)S(1)} %get-tuple-element.98), channel_id=1, source_target_pairs={{0,7},{1,6},{2,5},{3,4},{4,3},{5,2},{6,1},{7,0},{8,15},{9,14},{10,... | collective-permute-start | bytes 393224 | tf_op jit(solution)/shard_map/ppermute | solution.py:288
  148.1 1.1 copy-start.12
  (2 other events, 1.3 us)

commit v9 on v8

--- a/solution.py
+++ b/solution.py
@@ -10,7 +10,8 @@
 
 VMEM = pl.BlockSpec(memory_space=pltpu.VMEM)
 SMEM = pl.BlockSpec(memory_space=pltpu.SMEM)
-PARAMS = pltpu.CompilerParams(vmem_limit_bytes=50 * 2**20)
+SMALL = pltpu.CompilerParams(vmem_limit_bytes=16 * 2**20)
+LARGE = pltpu.CompilerParams(vmem_limit_bytes=24 * 2**20)
 WIDE = jnp.float32
 LONG = 3 * 10**10
 NARROW = jnp.bfloat16
@@ -38,14 +39,14 @@
         return jnp.concatenate([x[:, self.edge:], x[:, :self.edge]], axis=1)
 
 
-def call(body, outs, scratch, flops, moved, *operands, specs):
+def call(body, outs, scratch, flops, moved, *operands, specs, params=SMALL):
     return pl.pallas_call(
         body,
         out_shape=outs,
         in_specs=specs,
         out_specs=jax.tree.map(lambda _: VMEM, outs),
         scratch_shapes=scratch,
-        compiler_params=PARAMS,
+        compiler_params=params,
         cost_estimate=pl.CostEstimate(flops=flops, bytes_accessed=moved, transcendentals=0),
     )(*operands)
 
@@ -299,6 +300,21 @@
 
 def tie(x, *others):
     return lax.optimization_barrier((x, *others))[0]
+
+
+def copy_kernel(source, out):
+    for k in range(source.shape[0]):
+        out[k] = source[k]
+
+
+def after(x, *others):
+    return pl.pallas_call(
+        copy_kernel,
+        out_shape=jax.ShapeDtypeStruct(x.shape, x.dtype),
+        in_specs=[SMEM],
+        out_specs=SMEM,
+        cost_estimate=pl.CostEstimate(flops=LONG, bytes_accessed=8, transcendentals=0),
+    )(tie(x, *others))
 
 
 def gather_vectors(vectors, devices, packed):
@@ -357,7 +373,7 @@
     ladder_flops = first * singles * 4 * virtual**3
     ladder = call(
         functools.partial(first_ladder_kernel, tiles, order), packed, [whole, inner, square],
-        ladder_flops, 8 * count, place, current, *pieces, specs=[SMEM] + [VMEM] * (1 + len(pieces)),
+        ladder_flops, 8 * count, place, current, *pieces, specs=[SMEM] + [VMEM] * (1 + len(pieces)), params=LARGE,
     )
     parts = call(
         functools.partial(sort_kernel, tiles, groups), [part] * (2 * groups), [blocks], count, 4 * count,
@@ -370,7 +386,7 @@
     for c in chunks:
         half.append(call(
             functools.partial(half_kernel, tiles, groups, first, c), [part] * groups, [],
-            LONG, 6 * count, place, fock, ladder, *mirror[c],
+            LONG, 6 * count, after(place, *mirror[c]) if c == 0 else place, fock, ladder, *mirror[c],
             specs=[SMEM] * 2 + [VMEM] * (groups + 1),
         ))
         other.append(across_first(half[c], groups))
@@ -391,14 +407,14 @@
         [whole, inner, square, pltpu.VMEM((virtual, virtual), NARROW)],
         ladder_flops, 12 * count, place, occ_energy, current, *back,
         jnp.broadcast_to(vir_energy[:, None], (virtual, 128)), vir_energy[None, :], *pieces,
-        specs=[SMEM] * 2 + [VMEM] * (5 + len(pieces)),
+        specs=[SMEM] * 2 + [VMEM] * (5 + len(pieces)), params=LARGE,
     )
     last = []
     for c in chunks:
         last = call(
             functools.partial(rest_kernel, tiles, groups, first, c),
             [distant] * devices if c else [upper], [blocks] if c else [],
-            LONG, 8 * count, place, occ_energy, sums, rest[c], *mixed[c], *other[c], *last,
+            2 * count if c else LONG, 8 * count, place, occ_energy, sums, rest[c], *mixed[c], *other[c], *last,
             specs=[SMEM] * 2 + [VMEM] * (2 * groups + 2 + c),
         )
     def by_pair(*shape):
@@ -411,7 +427,7 @@
         in_specs=[SMEM, by_pair(virtual, virtual)] + [by_pair(edge, 2 * edge)] * devices,
         out_specs=by_pair(virtual, virtual),
         scratch_shapes=[pltpu.VMEM((devices, 1, edge, 2 * edge), NARROW)],
-        compiler_params=PARAMS,
+        compiler_params=SMALL,
         input_output_aliases={1: 0},
         cost_estimate=pl.CostEstimate(flops=count, bytes_accessed=10 * count, transcendentals=0),
     )(place, base, *by_distance(last))

time: 162 us -> 152 us (0.938)
  waiting for transfers between devices: 35.2 us -> 15.5 us
  local copies, waits for them, and re-layouts: 11.9 us -> 26 us
  starting transfers between devices: 79.6 us -> 68.5 us
  Pallas kernels: 31 us -> 35.8 us
    ppermute x14, waiting for transfers between devices: 16.1 us -> 1.52 us  [by_distance(): lax.ppermute(parts[k], 'occj', [(d, d ^ k) for d in range(devices)])]
    unnamed x54 -> x94, local copies, waits for them, and re-layouts: 10.3 us -> 24.4 us
    ppermute x18, starting transfers between devices: 44.3 us -> 32.2 us  [across_first(): lax.ppermute(parts[s], 'occi', [(k, k ^ s) for k in range(groups)])]
    ppermute x4, waiting for transfers between devices: 6.71 us -> 0.01 us  [turn(): return lax.ppermute(x, 'occj', [(d, d ^ k) for d in range(devices)])]
    pallas_call x10, Pallas kernels: 28.2 us -> 31.7 us  [call(): pl.pallas_call(body, out_shape=outs, in_specs=specs, out_specs=jax.tree.m...]
  transfers between devices with their start and end apart: 39 -> 39, of which waited for: 6 -> 6; matrix products, arithmetic and copies ran while one was open for 1% -> 3% of each run, Pallas kernels for 18% -> 21%
where the time goes in v9:
time: 152 us; the launch traced here: 150 us
  starting transfers between devices  68.5 us (45%)
  Pallas kernels  35.8 us (24%)
  local copies, waits for them, and re-layouts  26 us (17%)
  waiting for transfers between devices  15.5 us (10%)
  other arithmetic  2.82 us (2%)
  between operations  1.57 us (1%)
    ppermute x18, starting transfers between devices, across_first(): lax.ppermute(parts[s], 'occi', [(k, k ^ s) for k in range(groups)])  32.2 us
    pallas_call x10, Pallas kernels, call(): pl.pallas_call(body, out_shape=outs, in_specs=specs, out_specs=jax.tree.m...  31.7 us
    unnamed x94, local copies, waits for them, and re-layouts  24.4 us
    ppermute x14, starting transfers between devices, by_distance(): lax.ppermute(parts[k], 'occj', [(d, d ^ k) for d in range(devices)])  16.9 us
    all_to_all x3, starting transfers between devices, exchange(): lax.all_to_all(blocks, 'occj', split_axis=0, concat_axis=0, tiled=True)  13.9 us
    all_to_all x3, waiting for transfers between devices, exchange(): lax.all_to_all(blocks, 'occj', split_axis=0, concat_axis=0, tiled=True)  8.27 us
    ppermute x18, waiting for transfers between devices, across_first(): lax.ppermute(parts[s], 'occi', [(k, k ^ s) for k in range(groups)])  5.65 us
    ppermute x4, starting transfers between devices, turn(): return lax.ppermute(x, 'occj', [(d, d ^ k) for d in range(devices)])  5.4 us
  transfers between devices with their start and end apart: 39, of which 6 were waited for; matrix products, arithmetic and copies ran while one was open for 3% of the time, Pallas kernels for 21%

profile of v9, /device:TPU:0, one launch (start us, length us, event | category | flops | bytes accessed | tf_op | source)
XLA Modules:
  0.0 150.1 jit_solution(1494246989822196477)
XLA Ops:
  0.0 3.0 %collective-permute-start = (bf16[3,64,512]{2,1,0:T(8,128)(2,1)}, bf16[3,64,512]{2,1,0:T(8,128)(2,1)S(1)}, u32[]{:S(2)}, u32[]{:S(2)}) collective-permute-start(bf16[3,64,512]{2,1,0:T(8,128)(2,1)} %refs_0_.3), channel_id=1, source_target_pairs={{0,2},{1,3},{2,0},{3,1},{4,6},{5,7},{6,4},{7,5},{8,10},{9,11},{10,... | collective-permute-start | bytes 589832 | tf_op jit(solution)/shard_map/ppermute | solution.py:322
  3.0 1.5 %collective-permute-start.1 = (bf16[3,64,512]{2,1,0:T(8,128)(2,1)}, bf16[3,64,512]{2,1,0:T(8,128)(2,1)S(1)}, u32[]{:S(2)}, u32[]{:S(2)}) collective-permute-start(bf16[3,64,512]{2,1,0:T(8,128)(2,1)} %refs_0_.3), channel_id=1, source_target_pairs={{0,4},{1,5},{2,6},{3,7},{4,0},{5,1},{6,2},{7,3},{8,12},{9,13},{10,... | collective-permute-start | bytes 589832 | tf_op jit(solution)/shard_map/ppermute | solution.py:322
  4.6 1.6 %copy-done = f32[2,1,512,512]{3,2,1,0:T(8,128)S(1)} copy-done((f32[2,1,512,512]{3,2,1,0:T(8,128)S(1)}, f32[2,1,512,512]{3,2,1,0:T(8,128)}, u32[]{:S(2)}) %copy-start) | copy-done | bytes 2097176
  6.2 1.5 %shard_map.73 = (bf16[2,128,256]{2,1,0:T(8,128)(2,1)S(1)}, bf16[2,128,256]{2,1,0:T(8,128)(2,1)}, bf16[2,128,256]{2,1,0:T(8,128)(2,1)S(1)}, bf16[2,128,256]{2,1,0...) custom-call(s32[2]{0:T(128)S(1)} %pad_add_fusion.place.source, ...), custom_call_target="tpu_custom_call" | custom-call | flops 524288 | bytes 3145728 | tf_op jit(solution)/shard_map/pallas_call | solution.py:43
  9.7 1.5 collective-permute-start.10
  11.2 1.5 %collective-permute-start.4 = (bf16[2,128,256]{2,1,0:T(8,128)(2,1)}, bf16[2,128,256]{2,1,0:T(8,128)(2,1)S(1)}, u32[]{:S(2)}, u32[]{:S(2)}) collective-permute-start(bf16[2,128,256]{2,1,0:T(8,128)(2,1)} %get-tuple-element.56), channel_id=1, source_target_pairs={{0,1},{1,0},{2,3},{3,2},{4,5},{5,4},{6,7},{7,6},{8,9},{9,8},{10,11... | collective-permute-start | bytes 393224 | tf_op jit(solution)/shard_map/ppermute | solution.py:289
  15.9 0.8 collective-permute-start.6
  16.7 1.1 pad_maximum_fusion
  17.8 0.9 collective-permute-start.3
  18.9 0.7 broadcast_add_fusion.2
  19.6 0.8 collective-permute-start.7
  21.0 2.2 %collective-permute-start.9 = (bf16[2,128,256]{2,1,0:T(8,128)(2,1)S(1)}, bf16[2,128,256]{2,1,0:T(8,128)(2,1)S(1)}, u32[]{:S(2)}, u32[]{:S(2)}) collective-permute-start(bf16[2,128,256]{2,1,0:T(8,128)(2,1)S(1)} %get-tuple-element.61), channel_id=1, source_target_pairs={{0,6},{1,7},{2,4},{3,5},{4,2},{5,3},{6,0},{7,1},{8,14},{9,15},{10,... | collective-permute-start | bytes 393224 | tf_op jit(solution)/shard_map/ppermute | solution.py:289
  23.2 5.1 %shard_map.74 = bf16[8,2,128,256]{3,2,1,0:T(8,128)(2,1)} custom-call(s32[2]{0:T(128)S(1)} %pad_add_fusion.place.source, f32[2,512,512]{2,1,0:T(8,128)S(1)} %bitcast.14, bf16[3,64,512]{2,1,0:T(8,128)(2,1)S(1)} %copy-done.4, bf16[3,64,512]{2,1,0:T(8,128)(2,1)S(1)} %collective-permute-done.refs_1_, bf16[3,64,512]{2,1,0:T(8,128)(2,1)S(1)} %collective-permute-done.1.refs_2_, ...), custom_call_target="tpu_custom_call" | custom-call | flops 3221225472 | bytes 4194304 | tf_op jit(solution)/shard_map/pallas_call | solution.py:43
  29.0 0.9 collective-permute-done.8.refs_5_
  29.9 1.4 shard_map.75
  33.9 1.6 %collective-permute-start.11 = (bf16[2,2,64,256]{3,2,1,0:T(8,128)(2,1)}, bf16[2,2,64,256]{3,2,1,0:T(8,128)(2,1)}, u32[]{:S(2)}, u32[]{:S(2)}) collective-permute-start(bf16[2,2,64,256]{3,2,1,0:T(8,128)(2,1)} %get-tuple-element.64), channel_id=1, source_target_pairs={{0,8},{8,0},{16,24},{24,16},{1,9},{9,1},{17,25},{25,17},{2,10},{10... | collective-permute-start | bytes 393224 | tf_op jit(solution)/shard_map/ppermute | solution.py:296
  35.5 2.6 %collective-permute-start.12 = (bf16[2,2,64,256]{3,2,1,0:T(8,128)(2,1)}, bf16[2,2,64,256]{3,2,1,0:T(8,128)(2,1)}, u32[]{:S(2)}, u32[]{:S(2)}) collective-permute-start(bf16[2,2,64,256]{3,2,1,0:T(8,128)(2,1)} %get-tuple-element.65), channel_id=1, source_target_pairs={{0,16},{8,24},{16,0},{24,8},{1,17},{9,25},{17,1},{25,9},{2,18},{10... | collective-permute-start | bytes 393224 | tf_op jit(solution)/shard_map/ppermute | solution.py:296
  38.4 0.8 maximum_select_fusion.sums
  39.2 3.6 %all-to-all-start = ((bf16[8,2,128,256]{3,2,1,0:T(8,128)(2,1)}), bf16[8,2,128,256]{3,2,1,0:T(8,128)(2,1)S(1)}, u32[]{:S(2)}, u32[]{:S(2)}) async-start(bf16[8,2,128,256]{3,2,1,0:T(8,128)(2,1)} %shard_map.74), calls=%async_computation | async-start | bytes 2097152 | tf_op jit(solution)/shard_map/all_to_all | solution.py:283
  42.8 0.8 collective-permute-start.17
  43.6 3.5 %collective-permute-start.18 = (bf16[2,2,64,256]{3,2,1,0:T(8,128)(2,1)}, bf16[2,2,64,256]{3,2,1,0:T(8,128)(2,1)}, u32[]{:S(2)}, u32[]{:S(2)}) collective-permute-start(bf16[2,2,64,256]{3,2,1,0:T(8,128)(2,1)} %copy-done.27), channel_id=1, source_target_pairs={{0,16},{8,24},{16,0},{24,8},{1,17},{9,25},{17,1},{25,9},{2,18},{10... | collective-permute-start | bytes 393224 | tf_op jit(solution)/shard_map/ppermute | solution.py:296
  47.3 1.4 collective-permute-done.12.refs_2_
  48.7 1.2 shard_map.76.place
  49.9 8.3 %all-to-all-done.ladder = bf16[8,2,128,256]{3,2,1,0:T(8,128)(2,1)S(1)} async-done(((bf16[8,2,128,256]{3,2,1,0:T(8,128)(2,1)}), bf16[8,2,128,256]{3,2,1,0:T(8,128)(2,1)S(1)}, u32[]{:S(2)}, u32[]{:S(2)}) %all-to-all-start) | async-done | bytes 1048608 | tf_op jit(solution)/shard_map/all_to_all | solution.py:283
  58.2 0.9 copy-done.30
  59.7 2.0 %shard_map.77 = (bf16[2,2,64,256]{3,2,1,0:T(8,128)(2,1)S(1)}, bf16[2,2,64,256]{3,2,1,0:T(8,128)(2,1)S(1)}, bf16[2,2,64,256]{3,2,1,0:T(8,128)(2,1)S(1)}, bf16[2,2,64,256]{3,2,1,0:T(8,128)(2,1)S(1)}) custom-call(s32[2]{0:T(128)S(1)} %copy-done.43, f32[8,8]{1,0:T(8,128)S(1)} %convert_element_type.3.fock, bf16[8,2,128,256]{3,2,1,0:T(8,128)(2,1)S(1)} %all-to-all-done.ladder, ...), custom_call_target="tpu_custom_call" | custom-call | flops 30000001024 | bytes 3145728 | tf_op jit(solution)/shard_map/pallas_call | solution.py:43
  61.7 0.8 collective-permute-start.14
  62.5 3.4 %collective-permute-start.15 = (bf16[2,2,64,256]{3,2,1,0:T(8,128)(2,1)S(1)}, bf16[2,2,64,256]{3,2,1,0:T(8,128)(2,1)S(1)}, u32[]{:S(2)}, u32[]{:S(2)}) collective-permute-start(bf16[2,2,64,256]{3,2,1,0:T(8,128)(2,1)S(1)} %get-tuple-element.70.refs_2_), channel_id=1, source_target_pairs={{0,16},{8,24},{16,0},{24,8},{1,17},{9,25},{17,1},{25,9},{2,18},{10... | collective-permute-start | bytes 393224 | tf_op jit(solution)/shard_map/ppermute | solution.py:296
  66.2 2.8 %shard_map.79 = (bf16[2,2,64,256]{3,2,1,0:T(8,128)(2,1)S(1)}, bf16[2,2,64,256]{3,2,1,0:T(8,128)(2,1)}, bf16[2,2,64,256]{3,2,1,0:T(8,128)(2,1)}, bf16[2,2,64,256]{3,2,1,0:T(8,128)(2,1)}) custom-call(s32[2]{0:T(128)S(1)} %copy-done.17, f32[8,8]{1,0:T(8,128)S(1)} %convert_element_type.3.fock, bf16[8,2,128,256]{3,2,1,0:T(8,128)(2,1)S(1)} %all-to-all-done.ladder, ...), custom_call_target="tpu_custom_call" | custom-call | flops 30000001024 | bytes 3145728 | tf_op jit(solution)/shard_map/pallas_call | solution.py:43
  69.9 3.8 %collective-permute-start.21 = (bf16[2,2,64,256]{3,2,1,0:T(8,128)(2,1)}, bf16[2,2,64,256]{3,2,1,0:T(8,128)(2,1)S(1)}, u32[]{:S(2)}, u32[]{:S(2)}) collective-permute-start(bf16[2,2,64,256]{3,2,1,0:T(8,128)(2,1)} %get-tuple-element.79.refs_2_), channel_id=1, source_target_pairs={{0,16},{8,24},{16,0},{24,8},{1,17},{9,25},{17,1},{25,9},{2,18},{10... | collective-permute-start | bytes 393224 | tf_op jit(solution)/shard_map/ppermute | solution.py:296
  74.0 1.7 %collective-permute-done.15.refs_6_ = bf16[2,2,64,256]{3,2,1,0:T(8,128)(2,1)S(1)} collective-permute-done((bf16[2,2,64,256]{3,2,1,0:T(8,128)(2,1)S(1)}, bf16[2,2,64,256]{3,2,1,0:T(8,128)(2,1)S(1)}, u32[]{:S(2)}, u32[]{:S(2)}) %collective-permute-start.15) | collective-permute-done | bytes 131104 | tf_op jit(solution)/shard_map/ppermute | solution.py:296
  75.7 3.2 %shard_map.78 = (bf16[8,2,64,256]{3,2,1,0:T(8,128)(2,1)}, bf16[2,8,64,256]{3,2,1,0:T(8,128)(2,1)S(1)}, bf16[2,2,64,256]{3,2,1,0:T(8,128)(2,1)S(1)}, bf16[2,2,64,...) custom-call(s32[2]{0:T(128)S(1)} %copy-done.17, ...), custom_call_target="tpu_custom_call" | custom-call | flops 30000001024 | bytes 5242880 | tf_op jit(solution)/shard_map/pallas_call | solution.py:43
  78.9 0.8 copy-done.37
  79.7 0.7 copy-done.39
  80.3 8.1 %collective-permute-start.26 = (bf16[2,2,64,256]{3,2,1,0:T(8,128)(2,1)}, bf16[2,2,64,256]{3,2,1,0:T(8,128)(2,1)}, u32[]{:S(2)}, u32[]{:S(2)}) collective-permute-start(bf16[2,2,64,256]{3,2,1,0:T(8,128)(2,1)} %get-tuple-element.90.refs_1_), channel_id=1, source_target_pairs={{0,8},{8,0},{16,24},{24,16},{1,9},{9,1},{17,25},{25,17},{2,10},{10... | collective-permute-start | bytes 393224 | tf_op jit(solution)/shard_map/ppermute | solution.py:296
  88.9 5.1 %all-to-all-start.1 = ((bf16[8,2,64,256]{3,2,1,0:T(8,128)(2,1)}), bf16[8,2,64,256]{3,2,1,0:T(8,128)(2,1)S(1)}, u32[]{:S(2)}, u32[]{:S(2)}) async-start(bf16[8,2,64,256]{3,2,1,0:T(8,128)(2,1)} %get-tuple-element.72), calls=%async_computation.1 | async-start | bytes 1048576 | tf_op jit(solution)/shard_map/all_to_all | solution.py:283
  94.7 1.5 collective-permute-start.28
  97.4 0.9 copy-done.32
  98.3 0.9 copy-done.34
  99.2 0.9 copy-done.36
  100.1 0.9 copy-done.42
  101.0 3.5 %shard_map.80 = (bf16[8,2,64,256]{3,2,1,0:T(8,128)(2,1)}, bf16[2,8,64,256]{3,2,1,0:T(8,128)(2,1)S(1)}, bf16[2,2,64,256]{3,2,1,0:T(8,128)(2,1)S(1)}, bf16[2,2,64,...) custom-call(s32[2]{0:T(128)S(1)} %copy-done.17, ...), custom_call_target="tpu_custom_call" | custom-call | flops 30000001024 | bytes 5242880 | tf_op jit(solution)/shard_map/pallas_call | solution.py:43
  104.5 0.8 copy-done.2
  106.0 1.0 collective-permute-start.23
  107.0 1.9 %collective-permute-start.24 = (bf16[2,2,64,256]{3,2,1,0:T(8,128)(2,1)}, bf16[2,2,64,256]{3,2,1,0:T(8,128)(2,1)}, u32[]{:S(2)}, u32[]{:S(2)}) collective-permute-start(bf16[2,2,64,256]{3,2,1,0:T(8,128)(2,1)} %get-tuple-element.86.refs_2_), channel_id=1, source_target_pairs={{0,16},{8,24},{16,0},{24,8},{1,17},{9,25},{17,1},{25,9},{2,18},{10... | collective-permute-start | bytes 393224 | tf_op jit(solution)/shard_map/ppermute | solution.py:296
  108.9 5.3 %all-to-all-start.2 = ((bf16[8,2,64,256]{3,2,1,0:T(8,128)(2,1)}), bf16[8,2,64,256]{3,2,1,0:T(8,128)(2,1)S(1)}, u32[]{:S(2)}, u32[]{:S(2)}) async-start(bf16[8,2,64,256]{3,2,1,0:T(8,128)(2,1)} %get-tuple-element.82), calls=%async_computation.2 | async-start | bytes 1048576 | tf_op jit(solution)/shard_map/all_to_all | solution.py:283
  114.2 1.5 %collective-permute-start.25 = (bf16[2,2,64,256]{3,2,1,0:T(8,128)(2,1)}, bf16[2,2,64,256]{3,2,1,0:T(8,128)(2,1)S(1)}, u32[]{:S(2)}, u32[]{:S(2)}) collective-permute-start(bf16[2,2,64,256]{3,2,1,0:T(8,128)(2,1)} %copy-done.14), channel_id=1, source_target_pairs={{0,24},{8,16},{16,8},{24,0},{1,25},{9,17},{17,9},{25,1},{2,26},{10... | collective-permute-start | bytes 393224 | tf_op jit(solution)/shard_map/ppermute | solution.py:296
  115.7 1.0 copy-done.38
  116.8 0.9 copy-done.40
  117.7 2.0 %shard_map.82.refs_8_ = bf16[8,2,64,256]{3,2,1,0:T(8,128)(2,1)S(1)} custom-call(s32[2]{0:T(128)S(1)} %copy-done.17, f32[8]{0:T(128)S(1)} %copy-done.20, f32[128,256]{1,0:T(8,128)S(1)} %maximum_select_fusion.sums, bf16[2,8,64,256]{3,2,1,0:T(8,128)(2,1)S(1)} %copy-done.38, bf16[2,2,64,256]{3,2,1,0:T(8,128)(2,1)S(1)} %copy-done.40, ...), custom_call_target="tpu_custom_call" | custom-call | flops 30000001024 | bytes 4194304 | tf_op jit(solution)/shard_map/pallas_call | solution.py:43
  119.7 2.5 %collective-permute-done.25.refs_7_ = bf16[2,2,64,256]{3,2,1,0:T(8,128)(2,1)S(1)} collective-permute-done((bf16[2,2,64,256]{3,2,1,0:T(8,128)(2,1)}, bf16[2,2,64,256]{3,2,1,0:T(8,128)(2,1)S(1)}, u32[]{:S(2)}, u32[]{:S(2)}) %collective-permute-start.25) | collective-permute-done | bytes 131104 | tf_op jit(solution)/shard_map/ppermute | solution.py:296
  122.2 0.9 copy-done.13
  123.1 2.7 %shard_map.83 = (bf16[2,128,256]{2,1,0:T(8,128)(2,1)S(1)}, bf16[2,128,256]{2,1,0:T(8,128)(2,1)S(1)}, bf16[2,128,256]{2,1,0:T(8,128)(2,1)S(1)}, bf16[2,128,256]{2...) custom-call(s32[2]{0:T(128)S(1)} %copy-done.17, ...), custom_call_target="tpu_custom_call" | custom-call | flops 1048576 | bytes 4194304 | tf_op jit(solution)/shard_map/pallas_call | solution.py:43
  125.8 1.7 %collective-permute-start.30 = (bf16[2,128,256]{2,1,0:T(8,128)(2,1)S(1)}, bf16[2,128,256]{2,1,0:T(8,128)(2,1)S(1)}, u32[]{:S(2)}, u32[]{:S(2)}) collective-permute-start(bf16[2,128,256]{2,1,0:T(8,128)(2,1)S(1)} %get-tuple-element.95), channel_id=1, source_target_pairs={{0,2},{1,3},{2,0},{3,1},{4,6},{5,7},{6,4},{7,5},{8,10},{9,11},{10,... | collective-permute-start | bytes 393224 | tf_op jit(solution)/shard_map/ppermute | solution.py:289
  127.7 2.5 %collective-permute-start.32 = (bf16[2,128,256]{2,1,0:T(8,128)(2,1)}, bf16[2,128,256]{2,1,0:T(8,128)(2,1)}, u32[]{:S(2)}, u32[]{:S(2)}) collective-permute-start(bf16[2,128,256]{2,1,0:T(8,128)(2,1)} %get-tuple-element.97), channel_id=1, source_target_pairs={{0,4},{1,5},{2,6},{3,7},{4,0},{5,1},{6,2},{7,3},{8,12},{9,13},{10,... | collective-permute-start | bytes 393224 | tf_op jit(solution)/shard_map/ppermute | solution.py:289
  130.1 2.8 %collective-permute-start.34 = (bf16[2,128,256]{2,1,0:T(8,128)(2,1)}, bf16[2,128,256]{2,1,0:T(8,128)(2,1)}, u32[]{:S(2)}, u32[]{:S(2)}) collective-permute-start(bf16[2,128,256]{2,1,0:T(8,128)(2,1)} %get-tuple-element.99), channel_id=1, source_target_pairs={{0,6},{1,7},{2,4},{3,5},{4,2},{5,3},{6,0},{7,1},{8,14},{9,15},{10,... | collective-permute-start | bytes 393224 | tf_op jit(solution)/shard_map/ppermute | solution.py:289
  132.9 1.7 %collective-permute-start.35 = (bf16[2,128,256]{2,1,0:T(8,128)(2,1)}, bf16[2,128,256]{2,1,0:T(8,128)(2,1)}, u32[]{:S(2)}, u32[]{:S(2)}) collective-permute-start(bf16[2,128,256]{2,1,0:T(8,128)(2,1)} %get-tuple-element.100), channel_id=1, source_target_pairs={{0,7},{1,6},{2,5},{3,4},{4,3},{5,2},{6,1},{7,0},{8,15},{9,14},{10,... | collective-permute-start | bytes 393224 | tf_op jit(solution)/shard_map/ppermute | solution.py:289
  134.8 0.9 copy-done.5
  135.8 0.9 copy-done.7
  136.7 0.9 copy-done.9
  137.6 0.9 copy-done.11
  138.5 1.1 copy-done.22
  139.7 7.5 %shard_map.81.source = f32[2,512,512]{2,1,0:T(8,128)} custom-call(s32[2]{0:T(128)S(1)} %copy-done.17, f32[8]{0:T(128)S(1)} %copy-done.20, f32[2,512,512]{2,1,0:T(8,128)S(1)} %bitcast.15, bf16[8,2,64,256]{3,2,1,0:T(8,128)(2,1)S(1)} %all-to-all-done.1.upper, bf16[8,2,64,256]{3,2,1,0:T(8,128)(2,1)S(1)} %all-to-all-done.2.lower, ...), custom_call_target="tpu_custom_call" | custom-call | flops 3221225472 | bytes 6291456 | tf_op jit(solution)/shard_map/pallas_call | solution.py:43
  147.2 2.9 %shard_map.84 = f32[2,512,512]{2,1,0:T(8,128)} custom-call(s32[2]{0:T(128)S(1)} %copy-done.17, f32[2,512,512]{2,1,0:T(8,128)} %shard_map.81.source, bf16[2,128,256]{2,1,0:T(8,128)(2,1)S(1)} %get-tuple-element.93.refs_0_, bf16[2,128,256]{2,1,0:T(8,128)(2,1)S(1)} %collective-permute-done.29.refs_1_, ...), custom_call_target="tpu_custom_call", output_to_operand_aliasing={{}: (1, {})} | custom-call | flops 524288 | bytes 5242880 | tf_op jit(solution)/shard_map/pallas_call | solution.py:423
  (132 shorter events, 13.9 us)
Async XLA Ops:
  0.0 12.7 %copy-start.46 = (s32[8]{0:T(128)S(1)}, s32[8]{0:T(128)}, u32[]{:S(2)}) copy-start(s32[8]{0:T(128)} %constant.25.clone) | copy-start | bytes 100
  0.0 14.0 %copy-start.45 = (s32[8]{0:T(128)S(1)}, s32[8]{0:T(128)}, u32[]{:S(2)}) copy-start(s32[8]{0:T(128)} %constant.24.clone) | copy-start | bytes 100
  0.0 18.6 %copy-start.18 = (f32[512]{0:T(512)S(1)}, f32[512]{0:T(512)}, u32[]{:S(2)}) copy-start(f32[512]{0:T(512)} %param.11) | copy-start | bytes 6148
  0.0 15.2 %collective-permute-start = (bf16[3,64,512]{2,1,0:T(8,128)(2,1)}, bf16[3,64,512]{2,1,0:T(8,128)(2,1)S(1)}, u32[]{:S(2)}, u32[]{:S(2)}) collective-permute-start(bf16[3,64,512]{2,1,0:T(8,128)(2,1)} %refs_0_.3), channel_id=1, source_target_pairs={{0,2},{1,3},{2,0},{3,1},{4,6},{5,7},{6,4},{7,5},{8,10},{9,11},{10,... | collective-permute-start | bytes 589832 | tf_op jit(solution)/shard_map/ppermute | solution.py:322
  3.0 12.8 %collective-permute-start.1 = (bf16[3,64,512]{2,1,0:T(8,128)(2,1)}, bf16[3,64,512]{2,1,0:T(8,128)(2,1)S(1)}, u32[]{:S(2)}, u32[]{:S(2)}) collective-permute-start(bf16[3,64,512]{2,1,0:T(8,128)(2,1)} %refs_0_.3), channel_id=1, source_target_pairs={{0,4},{1,5},{2,6},{3,7},{4,0},{5,1},{6,2},{7,3},{8,12},{9,13},{10,... | collective-permute-start | bytes 589832 | tf_op jit(solution)/shard_map/ppermute | solution.py:322
  4.5 12.1 %collective-permute-start.2 = (bf16[3,64,512]{2,1,0:T(8,128)(2,1)}, bf16[3,64,512]{2,1,0:T(8,128)(2,1)S(1)}, u32[]{:S(2)}, u32[]{:S(2)}) collective-permute-start(bf16[3,64,512]{2,1,0:T(8,128)(2,1)} %refs_0_.3), channel_id=1, source_target_pairs={{0,6},{1,7},{2,4},{3,5},{4,2},{5,3},{6,0},{7,1},{8,14},{9,15},{10,... | collective-permute-start | bytes 589832 | tf_op jit(solution)/shard_map/ppermute | solution.py:322
  4.6 25.3 %copy-start.16 = (s32[2]{0:T(128)}, s32[2]{0:T(128)S(1)}, u32[]{:S(2)}) copy-start(s32[2]{0:T(128)S(1)} %pad_add_fusion.place.source) | copy-start | bytes 28
  4.6 1.6 %copy-start = (f32[2,1,512,512]{3,2,1,0:T(8,128)S(1)}, f32[2,1,512,512]{3,2,1,0:T(8,128)}, u32[]{:S(2)}) copy-start(f32[2,1,512,512]{3,2,1,0:T(8,128)} %param.7) | copy-start | bytes 6291460
  6.2 17.0 %copy-start.1 = (f32[2,1,512,512]{3,2,1,0:T(8,128)S(1)}, f32[2,1,512,512]{3,2,1,0:T(8,128)}, u32[]{:S(2)}) copy-start(f32[2,1,512,512]{3,2,1,0:T(8,128)} %param.7) | copy-start | bytes 6291460
  6.2 17.0 %copy-start.4 = (bf16[3,64,512]{2,1,0:T(8,128)(2,1)S(1)}, bf16[3,64,512]{2,1,0:T(8,128)(2,1)}, u32[]{:S(2)}) copy-start(bf16[3,64,512]{2,1,0:T(8,128)(2,1)} %refs_0_.3) | copy-start | bytes 589828
  9.7 9.9 %collective-permute-start.10 = (bf16[2,128,256]{2,1,0:T(8,128)(2,1)}, bf16[2,128,256]{2,1,0:T(8,128)(2,1)S(1)}, u32[]{:S(2)}, u32[]{:S(2)}) collective-permute-start(bf16[2,128,256]{2,1,0:T(8,128)(2,1)} %get-tuple-element.62), channel_id=1, source_target_pairs={{0,7},{1,6},{2,5},{3,4},{4,3},{5,2},{6,1},{7,0},{8,15},{9,14},{10,... | collective-permute-start | bytes 393224 | tf_op jit(solution)/shard_map/ppermute | solution.py:289
  11.2 9.2 %collective-permute-start.4 = (bf16[2,128,256]{2,1,0:T(8,128)(2,1)}, bf16[2,128,256]{2,1,0:T(8,128)(2,1)S(1)}, u32[]{:S(2)}, u32[]{:S(2)}) collective-permute-start(bf16[2,128,256]{2,1,0:T(8,128)(2,1)} %get-tuple-element.56), channel_id=1, source_target_pairs={{0,1},{1,0},{2,3},{3,2},{4,5},{5,4},{6,7},{7,6},{8,9},{9,8},{10,11... | collective-permute-start | bytes 393224 | tf_op jit(solution)/shard_map/ppermute | solution.py:289
  15.2 13.1 %copy-start.6 = (bf16[3,64,512]{2,1,0:T(8,128)(2,1)}, bf16[3,64,512]{2,1,0:T(8,128)(2,1)S(1)}, u32[]{:S(2)}) copy-start(bf16[3,64,512]{2,1,0:T(8,128)(2,1)S(1)} %collective-permute-done.refs_1_) | copy-start | bytes 589828
  15.3 13.2 %collective-permute-start.5 = (bf16[2,128,256]{2,1,0:T(8,128)(2,1)}, bf16[2,128,256]{2,1,0:T(8,128)(2,1)S(1)}, u32[]{:S(2)}, u32[]{:S(2)}) collective-permute-start(bf16[2,128,256]{2,1,0:T(8,128)(2,1)} %copy-done.25), channel_id=1, source_target_pairs={{0,2},{1,3},{2,0},{3,1},{4,6},{5,7},{6,4},{7,5},{8,10},{9,11},{10,... | collective-permute-start | bytes 393224 | tf_op jit(solution)/shard_map/ppermute | solution.py:289
  15.9 12.5 %copy-start.8 = (bf16[3,64,512]{2,1,0:T(8,128)(2,1)}, bf16[3,64,512]{2,1,0:T(8,128)(2,1)S(1)}, u32[]{:S(2)}) copy-start(bf16[3,64,512]{2,1,0:T(8,128)(2,1)S(1)} %collective-permute-done.1.refs_2_) | copy-start | bytes 589828
  15.9 12.6 %collective-permute-start.6 = (bf16[2,128,256]{2,1,0:T(8,128)(2,1)}, bf16[2,128,256]{2,1,0:T(8,128)(2,1)S(1)}, u32[]{:S(2)}, u32[]{:S(2)}) collective-permute-start(bf16[2,128,256]{2,1,0:T(8,128)(2,1)} %copy-done.24), channel_id=1, source_target_pairs={{0,3},{1,2},{2,1},{3,0},{4,7},{5,6},{6,5},{7,4},{8,11},{9,10},{10,... | collective-permute-start | bytes 393224 | tf_op jit(solution)/shard_map/ppermute | solution.py:289
  16.7 11.7 %copy-start.10 = (bf16[3,64,512]{2,1,0:T(8,128)(2,1)}, bf16[3,64,512]{2,1,0:T(8,128)(2,1)S(1)}, u32[]{:S(2)}) copy-start(bf16[3,64,512]{2,1,0:T(8,128)(2,1)S(1)} %collective-permute-done.2.refs_3_) | copy-start | bytes 589828
  17.8 3.2 %collective-permute-start.3 = (bf16[4,3,64,512]{3,2,1,0:T(8,128)(2,1)S(1)}, bf16[4,3,64,512]{3,2,1,0:T(8,128)(2,1)S(1)}, u32[]{:S(2)}, u32[]{:S(2)}) collective-permute-start(bf16[4,3,64,512]{3,2,1,0:T(8,128)(2,1)S(1)} %pad_maximum_fusion), channel_id=1, source_target_pairs={{0,1},{1,0},{2,3},{3,2},{4,5},{5,4},{6,7},{7,6},{8,9},{9,8},{10,11... | collective-permute-start | bytes 2359304 | tf_op jit(solution)/shard_map/ppermute | solution.py:322
  19.6 9.4 %collective-permute-start.7 = (bf16[2,128,256]{2,1,0:T(8,128)(2,1)}, bf16[2,128,256]{2,1,0:T(8,128)(2,1)S(1)}, u32[]{:S(2)}, u32[]{:S(2)}) collective-permute-start(bf16[2,128,256]{2,1,0:T(8,128)(2,1)} %copy-done.23), channel_id=1, source_target_pairs={{0,4},{1,5},{2,6},{3,7},{4,0},{5,1},{6,2},{7,3},{8,12},{9,13},{10,... | collective-permute-start | bytes 393224 | tf_op jit(solution)/shard_map/ppermute | solution.py:289
  20.4 9.5 %collective-permute-start.8 = (bf16[2,128,256]{2,1,0:T(8,128)(2,1)S(1)}, bf16[2,128,256]{2,1,0:T(8,128)(2,1)S(1)}, u32[]{:S(2)}, u32[]{:S(2)}) collective-permute-start(bf16[2,128,256]{2,1,0:T(8,128)(2,1)S(1)} %get-tuple-element.60), channel_id=1, source_target_pairs={{0,5},{1,4},{2,7},{3,6},{4,1},{5,0},{6,3},{7,2},{8,13},{9,12},{10,... | collective-permute-start | bytes 393224 | tf_op jit(solution)/shard_map/ppermute | solution.py:289
  21.0 7.4 %copy-start.21 = (bf16[4,3,64,512]{3,2,1,0:T(8,128)(2,1)}, bf16[4,3,64,512]{3,2,1,0:T(8,128)(2,1)S(1)}, u32[]{:S(2)}) copy-start(bf16[4,3,64,512]{3,2,1,0:T(8,128)(2,1)S(1)} %collective-permute-done.3.refs_4_) | copy-start | bytes 2359300
  21.0 17.4 %copy-start.44 = (bf16[8,8]{1,0:T(8,128)(2,1)S(1)}, bf16[8,8]{1,0:T(8,128)(2,1)}, u32[]{:S(2)}) copy-start(bf16[8,8]{1,0:T(8,128)(2,1)} %param.9) | copy-start | bytes 388
  21.0 8.9 %collective-permute-start.9 = (bf16[2,128,256]{2,1,0:T(8,128)(2,1)S(1)}, bf16[2,128,256]{2,1,0:T(8,128)(2,1)S(1)}, u32[]{:S(2)}, u32[]{:S(2)}) collective-permute-start(bf16[2,128,256]{2,1,0:T(8,128)(2,1)S(1)} %get-tuple-element.61), channel_id=1, source_target_pairs={{0,6},{1,7},{2,4},{3,5},{4,2},{5,3},{6,0},{7,1},{8,14},{9,15},{10,... | collective-permute-start | bytes 393224 | tf_op jit(solution)/shard_map/ppermute | solution.py:289
  33.9 13.2 %collective-permute-start.11 = (bf16[2,2,64,256]{3,2,1,0:T(8,128)(2,1)}, bf16[2,2,64,256]{3,2,1,0:T(8,128)(2,1)}, u32[]{:S(2)}, u32[]{:S(2)}) collective-permute-start(bf16[2,2,64,256]{3,2,1,0:T(8,128)(2,1)} %get-tuple-element.64), channel_id=1, source_target_pairs={{0,8},{8,0},{16,24},{24,16},{1,9},{9,1},{17,25},{25,17},{2,10},{10... | collective-permute-start | bytes 393224 | tf_op jit(solution)/shard_map/ppermute | solution.py:296
  35.5 13.2 %collective-permute-start.12 = (bf16[2,2,64,256]{3,2,1,0:T(8,128)(2,1)}, bf16[2,2,64,256]{3,2,1,0:T(8,128)(2,1)}, u32[]{:S(2)}, u32[]{:S(2)}) collective-permute-start(bf16[2,2,64,256]{3,2,1,0:T(8,128)(2,1)} %get-tuple-element.65), channel_id=1, source_target_pairs={{0,16},{8,24},{16,0},{24,8},{1,17},{9,25},{17,1},{25,9},{2,18},{10... | collective-permute-start | bytes 393224 | tf_op jit(solution)/shard_map/ppermute | solution.py:296
  38.1 10.6 %collective-permute-start.13 = (bf16[2,2,64,256]{3,2,1,0:T(8,128)(2,1)}, bf16[2,2,64,256]{3,2,1,0:T(8,128)(2,1)}, u32[]{:S(2)}, u32[]{:S(2)}) collective-permute-start(bf16[2,2,64,256]{3,2,1,0:T(8,128)(2,1)} %get-tuple-element.66), channel_id=1, source_target_pairs={{0,24},{8,16},{16,8},{24,0},{1,25},{9,17},{17,9},{25,1},{2,26},{10... | collective-permute-start | bytes 393224 | tf_op jit(solution)/shard_map/ppermute | solution.py:296
  39.2 18.9 %all-to-all-start = ((bf16[8,2,128,256]{3,2,1,0:T(8,128)(2,1)}), bf16[8,2,128,256]{3,2,1,0:T(8,128)(2,1)S(1)}, u32[]{:S(2)}, u32[]{:S(2)}) async-start(bf16[8,2,128,256]{3,2,1,0:T(8,128)(2,1)} %shard_map.74), calls=%async_computation | async-start | bytes 2097152 | tf_op jit(solution)/shard_map/all_to_all | solution.py:283
  42.8 23.1 %collective-permute-start.17 = (bf16[2,2,64,256]{3,2,1,0:T(8,128)(2,1)}, bf16[2,2,64,256]{3,2,1,0:T(8,128)(2,1)}, u32[]{:S(2)}, u32[]{:S(2)}) collective-permute-start(bf16[2,2,64,256]{3,2,1,0:T(8,128)(2,1)} %copy-done.28), channel_id=1, source_target_pairs={{0,8},{8,0},{16,24},{24,16},{1,9},{9,1},{17,25},{25,17},{2,10},{10... | collective-permute-start | bytes 393224 | tf_op jit(solution)/shard_map/ppermute | solution.py:296
  43.6 22.5 %collective-permute-start.18 = (bf16[2,2,64,256]{3,2,1,0:T(8,128)(2,1)}, bf16[2,2,64,256]{3,2,1,0:T(8,128)(2,1)}, u32[]{:S(2)}, u32[]{:S(2)}) collective-permute-start(bf16[2,2,64,256]{3,2,1,0:T(8,128)(2,1)} %copy-done.27), channel_id=1, source_target_pairs={{0,16},{8,24},{16,0},{24,8},{1,17},{9,25},{17,1},{25,9},{2,18},{10... | collective-permute-start | bytes 393224 | tf_op jit(solution)/shard_map/ppermute | solution.py:296
  47.1 19.1 %collective-permute-start.19 = (bf16[2,2,64,256]{3,2,1,0:T(8,128)(2,1)}, bf16[2,2,64,256]{3,2,1,0:T(8,128)(2,1)}, u32[]{:S(2)}, u32[]{:S(2)}) collective-permute-start(bf16[2,2,64,256]{3,2,1,0:T(8,128)(2,1)} %copy-done.26), channel_id=1, source_target_pairs={{0,24},{8,16},{16,8},{24,0},{1,25},{9,17},{17,9},{25,1},{2,26},{10... | collective-permute-start | bytes 393224 | tf_op jit(solution)/shard_map/ppermute | solution.py:296
  49.9 16.2 %copy-start.17 = (s32[2]{0:T(128)S(1)}, s32[2]{0:T(128)}, u32[]{:S(2)}) copy-start(s32[2]{0:T(128)} %copy-done.16) | copy-start | bytes 28
  61.7 12.1 %collective-permute-start.14 = (bf16[2,2,64,256]{3,2,1,0:T(8,128)(2,1)S(1)}, bf16[2,2,64,256]{3,2,1,0:T(8,128)(2,1)S(1)}, u32[]{:S(2)}, u32[]{:S(2)}) collective-permute-start(bf16[2,2,64,256]{3,2,1,0:T(8,128)(2,1)S(1)} %get-tuple-element.69.refs_1_), channel_id=1, source_target_pairs={{0,8},{8,0},{16,24},{24,16},{1,9},{9,1},{17,25},{25,17},{2,10},{10... | collective-permute-start | bytes 393224 | tf_op jit(solution)/shard_map/ppermute | solution.py:296
  62.5 13.2 %collective-permute-start.15 = (bf16[2,2,64,256]{3,2,1,0:T(8,128)(2,1)S(1)}, bf16[2,2,64,256]{3,2,1,0:T(8,128)(2,1)S(1)}, u32[]{:S(2)}, u32[]{:S(2)}) collective-permute-start(bf16[2,2,64,256]{3,2,1,0:T(8,128)(2,1)S(1)} %get-tuple-element.70.refs_2_), channel_id=1, source_target_pairs={{0,16},{8,24},{16,0},{24,8},{1,17},{9,25},{17,1},{25,9},{2,18},{10... | collective-permute-start | bytes 393224 | tf_op jit(solution)/shard_map/ppermute | solution.py:296
  65.9 9.8 %collective-permute-start.16 = (bf16[2,2,64,256]{3,2,1,0:T(8,128)(2,1)S(1)}, bf16[2,2,64,256]{3,2,1,0:T(8,128)(2,1)S(1)}, u32[]{:S(2)}, u32[]{:S(2)}) collective-permute-start(bf16[2,2,64,256]{3,2,1,0:T(8,128)(2,1)S(1)} %get-tuple-element.71.refs_3_), channel_id=1, source_target_pairs={{0,24},{8,16},{16,8},{24,0},{1,25},{9,17},{17,9},{25,1},{2,26},{10... | collective-permute-start | bytes 393224 | tf_op jit(solution)/shard_map/ppermute | solution.py:296
  66.1 9.6 %copy-start.20 = (f32[8]{0:T(128)S(1)}, f32[8]{0:T(128)}, u32[]{:S(2)}) copy-start(f32[8]{0:T(128)} %occ.9) | copy-start | bytes 100
  69.6 24.4 %collective-permute-start.20 = (bf16[2,2,64,256]{3,2,1,0:T(8,128)(2,1)}, bf16[2,2,64,256]{3,2,1,0:T(8,128)(2,1)S(1)}, u32[]{:S(2)}, u32[]{:S(2)}) collective-permute-start(bf16[2,2,64,256]{3,2,1,0:T(8,128)(2,1)} %get-tuple-element.78.refs_1_), channel_id=1, source_target_pairs={{0,8},{8,0},{16,24},{24,16},{1,9},{9,1},{17,25},{25,17},{2,10},{10... | collective-permute-start | bytes 393224 | tf_op jit(solution)/shard_map/ppermute | solution.py:296
  69.9 26.2 %collective-permute-start.21 = (bf16[2,2,64,256]{3,2,1,0:T(8,128)(2,1)}, bf16[2,2,64,256]{3,2,1,0:T(8,128)(2,1)S(1)}, u32[]{:S(2)}, u32[]{:S(2)}) collective-permute-start(bf16[2,2,64,256]{3,2,1,0:T(8,128)(2,1)} %get-tuple-element.79.refs_2_), channel_id=1, source_target_pairs={{0,16},{8,24},{16,0},{24,8},{1,17},{9,25},{17,1},{25,9},{2,18},{10... | collective-permute-start | bytes 393224 | tf_op jit(solution)/shard_map/ppermute | solution.py:296
  73.7 23.0 %collective-permute-start.22 = (bf16[2,2,64,256]{3,2,1,0:T(8,128)(2,1)}, bf16[2,2,64,256]{3,2,1,0:T(8,128)(2,1)S(1)}, u32[]{:S(2)}, u32[]{:S(2)}) collective-permute-start(bf16[2,2,64,256]{3,2,1,0:T(8,128)(2,1)} %get-tuple-element.80.refs_3_), channel_id=1, source_target_pairs={{0,24},{8,16},{16,8},{24,0},{1,25},{9,17},{17,9},{25,1},{2,26},{10... | collective-permute-start | bytes 393224 | tf_op jit(solution)/shard_map/ppermute | solution.py:296
  80.3 33.9 %collective-permute-start.26 = (bf16[2,2,64,256]{3,2,1,0:T(8,128)(2,1)}, bf16[2,2,64,256]{3,2,1,0:T(8,128)(2,1)}, u32[]{:S(2)}, u32[]{:S(2)}) collective-permute-start(bf16[2,2,64,256]{3,2,1,0:T(8,128)(2,1)} %get-tuple-element.90.refs_1_), channel_id=1, source_target_pairs={{0,8},{8,0},{16,24},{24,16},{1,9},{9,1},{17,25},{25,17},{2,10},{10... | collective-permute-start | bytes 393224 | tf_op jit(solution)/shard_map/ppermute | solution.py:296
  88.4 27.3 %collective-permute-start.27 = (bf16[2,2,64,256]{3,2,1,0:T(8,128)(2,1)}, bf16[2,2,64,256]{3,2,1,0:T(8,128)(2,1)}, u32[]{:S(2)}, u32[]{:S(2)}) collective-permute-start(bf16[2,2,64,256]{3,2,1,0:T(8,128)(2,1)} %get-tuple-element.91.refs_2_), channel_id=1, source_target_pairs={{0,16},{8,24},{16,0},{24,8},{1,17},{9,25},{17,1},{25,9},{2,18},{10... | collective-permute-start | bytes 393224 | tf_op jit(solution)/shard_map/ppermute | solution.py:296
  88.9 20.0 %all-to-all-start.1 = ((bf16[8,2,64,256]{3,2,1,0:T(8,128)(2,1)}), bf16[8,2,64,256]{3,2,1,0:T(8,128)(2,1)S(1)}, u32[]{:S(2)}, u32[]{:S(2)}) async-start(bf16[8,2,64,256]{3,2,1,0:T(8,128)(2,1)} %get-tuple-element.72), calls=%async_computation.1 | async-start | bytes 1048576 | tf_op jit(solution)/shard_map/all_to_all | solution.py:283
  94.7 21.1 %collective-permute-start.28 = (bf16[2,2,64,256]{3,2,1,0:T(8,128)(2,1)}, bf16[2,2,64,256]{3,2,1,0:T(8,128)(2,1)}, u32[]{:S(2)}, u32[]{:S(2)}) collective-permute-start(bf16[2,2,64,256]{3,2,1,0:T(8,128)(2,1)} %get-tuple-element.92.refs_3_), channel_id=1, source_target_pairs={{0,24},{8,16},{16,8},{24,0},{1,25},{9,17},{17,9},{25,1},{2,26},{10... | collective-permute-start | bytes 393224 | tf_op jit(solution)/shard_map/ppermute | solution.py:296
  106.0 13.7 %copy-start.12 = (bf16[2,2,64,256]{3,2,1,0:T(8,128)(2,1)}, bf16[2,2,64,256]{3,2,1,0:T(8,128)(2,1)S(1)}, u32[]{:S(2)}) copy-start(bf16[2,2,64,256]{3,2,1,0:T(8,128)(2,1)S(1)} %get-tuple-element.85.refs_1_) | copy-start | bytes 393220
  106.0 13.7 %collective-permute-start.23 = (bf16[2,2,64,256]{3,2,1,0:T(8,128)(2,1)S(1)}, bf16[2,2,64,256]{3,2,1,0:T(8,128)(2,1)}, u32[]{:S(2)}, u32[]{:S(2)}) collective-permute-start(bf16[2,2,64,256]{3,2,1,0:T(8,128)(2,1)S(1)} %get-tuple-element.85.refs_1_), channel_id=1, source_target_pairs={{0,8},{8,0},{16,24},{24,16},{1,9},{9,1},{17,25},{25,17},{2,10},{10... | collective-permute-start | bytes 393224 | tf_op jit(solution)/shard_map/ppermute | solution.py:296
  107.0 12.7 %collective-permute-start.24 = (bf16[2,2,64,256]{3,2,1,0:T(8,128)(2,1)}, bf16[2,2,64,256]{3,2,1,0:T(8,128)(2,1)}, u32[]{:S(2)}, u32[]{:S(2)}) collective-permute-start(bf16[2,2,64,256]{3,2,1,0:T(8,128)(2,1)} %get-tuple-element.86.refs_2_), channel_id=1, source_target_pairs={{0,16},{8,24},{16,0},{24,8},{1,17},{9,25},{17,1},{25,9},{2,18},{10... | collective-permute-start | bytes 393224 | tf_op jit(solution)/shard_map/ppermute | solution.py:296
  108.9 25.8 %all-to-all-start.2 = ((bf16[8,2,64,256]{3,2,1,0:T(8,128)(2,1)}), bf16[8,2,64,256]{3,2,1,0:T(8,128)(2,1)S(1)}, u32[]{:S(2)}, u32[]{:S(2)}) async-start(bf16[8,2,64,256]{3,2,1,0:T(8,128)(2,1)} %get-tuple-element.82), calls=%async_computation.2 | async-start | bytes 1048576 | tf_op jit(solution)/shard_map/all_to_all | solution.py:283
  114.2 8.0 %collective-permute-start.25 = (bf16[2,2,64,256]{3,2,1,0:T(8,128)(2,1)}, bf16[2,2,64,256]{3,2,1,0:T(8,128)(2,1)S(1)}, u32[]{:S(2)}, u32[]{:S(2)}) collective-permute-start(bf16[2,2,64,256]{3,2,1,0:T(8,128)(2,1)} %copy-done.14), channel_id=1, source_target_pairs={{0,24},{8,16},{16,8},{24,0},{1,25},{9,17},{17,9},{25,1},{2,26},{10... | collective-permute-start | bytes 393224 | tf_op jit(solution)/shard_map/ppermute | solution.py:296
  115.7 1.0 copy-start.38
  117.7 4.5 %copy-start.3 = (bf16[2,8,64,256]{3,2,1,0:T(8,128)(2,1)S(1)}, bf16[2,8,64,256]{3,2,1,0:T(8,128)(2,1)}, u32[]{:S(2)}) copy-start(bf16[2,8,64,256]{3,2,1,0:T(8,128)(2,1)} %copy-done.2) | copy-start | bytes 1572868
  117.7 4.5 %copy-start.15 = (bf16[2,2,64,256]{3,2,1,0:T(8,128)(2,1)S(1)}, bf16[2,2,64,256]{3,2,1,0:T(8,128)(2,1)}, u32[]{:S(2)}) copy-start(bf16[2,2,64,256]{3,2,1,0:T(8,128)(2,1)} %copy-done.14) | copy-start | bytes 393220
  119.7 15.0 %copy-start.19 = (f32[512]{0:T(512)S(1)}, f32[512]{0:T(512)}, u32[]{:S(2)}) copy-start(f32[512]{0:T(512)} %param.11) | copy-start | bytes 6148
  122.2 0.9 copy-start.13
  125.8 4.3 %collective-permute-start.29 = (bf16[2,128,256]{2,1,0:T(8,128)(2,1)S(1)}, bf16[2,128,256]{2,1,0:T(8,128)(2,1)S(1)}, u32[]{:S(2)}, u32[]{:S(2)}) collective-permute-start(bf16[2,128,256]{2,1,0:T(8,128)(2,1)S(1)} %get-tuple-element.94), channel_id=1, source_target_pairs={{0,1},{1,0},{2,3},{3,2},{4,5},{5,4},{6,7},{7,6},{8,9},{9,8},{10,11... | collective-permute-start | bytes 393224 | tf_op jit(solution)/shard_map/ppermute | solution.py:289
  125.8 7.1 %collective-permute-start.30 = (bf16[2,128,256]{2,1,0:T(8,128)(2,1)S(1)}, bf16[2,128,256]{2,1,0:T(8,128)(2,1)S(1)}, u32[]{:S(2)}, u32[]{:S(2)}) collective-permute-start(bf16[2,128,256]{2,1,0:T(8,128)(2,1)S(1)} %get-tuple-element.95), channel_id=1, source_target_pairs={{0,2},{1,3},{2,0},{3,1},{4,6},{5,7},{6,4},{7,5},{8,10},{9,11},{10,... | collective-permute-start | bytes 393224 | tf_op jit(solution)/shard_map/ppermute | solution.py:289
  127.5 19.7 %collective-permute-start.31 = (bf16[2,128,256]{2,1,0:T(8,128)(2,1)}, bf16[2,128,256]{2,1,0:T(8,128)(2,1)}, u32[]{:S(2)}, u32[]{:S(2)}) collective-permute-start(bf16[2,128,256]{2,1,0:T(8,128)(2,1)} %get-tuple-element.96), channel_id=1, source_target_pairs={{0,3},{1,2},{2,1},{3,0},{4,7},{5,6},{6,5},{7,4},{8,11},{9,10},{10,... | collective-permute-start | bytes 393224 | tf_op jit(solution)/shard_map/ppermute | solution.py:289
  127.7 19.5 %collective-permute-start.32 = (bf16[2,128,256]{2,1,0:T(8,128)(2,1)}, bf16[2,128,256]{2,1,0:T(8,128)(2,1)}, u32[]{:S(2)}, u32[]{:S(2)}) collective-permute-start(bf16[2,128,256]{2,1,0:T(8,128)(2,1)} %get-tuple-element.97), channel_id=1, source_target_pairs={{0,4},{1,5},{2,6},{3,7},{4,0},{5,1},{6,2},{7,3},{8,12},{9,13},{10,... | collective-permute-start | bytes 393224 | tf_op jit(solution)/shard_map/ppermute | solution.py:289
  130.1 17.1 %collective-permute-start.33 = (bf16[2,128,256]{2,1,0:T(8,128)(2,1)}, bf16[2,128,256]{2,1,0:T(8,128)(2,1)}, u32[]{:S(2)}, u32[]{:S(2)}) collective-permute-start(bf16[2,128,256]{2,1,0:T(8,128)(2,1)} %get-tuple-element.98), channel_id=1, source_target_pairs={{0,5},{1,4},{2,7},{3,6},{4,1},{5,0},{6,3},{7,2},{8,13},{9,12},{10,... | collective-permute-start | bytes 393224 | tf_op jit(solution)/shard_map/ppermute | solution.py:289
  130.1 17.1 %collective-permute-start.34 = (bf16[2,128,256]{2,1,0:T(8,128)(2,1)}, bf16[2,128,256]{2,1,0:T(8,128)(2,1)}, u32[]{:S(2)}, u32[]{:S(2)}) collective-permute-start(bf16[2,128,256]{2,1,0:T(8,128)(2,1)} %get-tuple-element.99), channel_id=1, source_target_pairs={{0,6},{1,7},{2,4},{3,5},{4,2},{5,3},{6,0},{7,1},{8,14},{9,15},{10,... | collective-permute-start | bytes 393224 | tf_op jit(solution)/shard_map/ppermute | solution.py:289
  132.9 14.3 %collective-permute-start.35 = (bf16[2,128,256]{2,1,0:T(8,128)(2,1)}, bf16[2,128,256]{2,1,0:T(8,128)(2,1)}, u32[]{:S(2)}, u32[]{:S(2)}) collective-permute-start(bf16[2,128,256]{2,1,0:T(8,128)(2,1)} %get-tuple-element.100), channel_id=1, source_target_pairs={{0,7},{1,6},{2,5},{3,4},{4,3},{5,2},{6,1},{7,0},{8,15},{9,14},{10,... | collective-permute-start | bytes 393224 | tf_op jit(solution)/shard_map/ppermute | solution.py:289
  134.8 0.9 copy-start.5
  135.8 0.9 copy-start.7
  136.7 0.9 copy-start.9
  137.6 0.9 copy-start.11
  138.5 1.1 copy-start.22
  (22 other events, 16.0 us)

commit v10 on v9

--- a/solution.py
+++ b/solution.py
@@ -10,8 +10,7 @@
 
 VMEM = pl.BlockSpec(memory_space=pltpu.VMEM)
 SMEM = pl.BlockSpec(memory_space=pltpu.SMEM)
-SMALL = pltpu.CompilerParams(vmem_limit_bytes=16 * 2**20)
-LARGE = pltpu.CompilerParams(vmem_limit_bytes=24 * 2**20)
+PARAMS = pltpu.CompilerParams(vmem_limit_bytes=50 * 2**20)
 WIDE = jnp.float32
 LONG = 3 * 10**10
 NARROW = jnp.bfloat16
@@ -39,14 +38,14 @@
         return jnp.concatenate([x[:, self.edge:], x[:, :self.edge]], axis=1)
 
 
-def call(body, outs, scratch, flops, moved, *operands, specs, params=SMALL):
+def call(body, outs, scratch, flops, moved, *operands, specs):
     return pl.pallas_call(
         body,
         out_shape=outs,
         in_specs=specs,
         out_specs=jax.tree.map(lambda _: VMEM, outs),
         scratch_shapes=scratch,
-        compiler_params=params,
+        compiler_params=PARAMS,
         cost_estimate=pl.CostEstimate(flops=flops, bytes_accessed=moved, transcendentals=0),
     )(*operands)
 
@@ -373,7 +372,7 @@
     ladder_flops = first * singles * 4 * virtual**3
     ladder = call(
         functools.partial(first_ladder_kernel, tiles, order), packed, [whole, inner, square],
-        ladder_flops, 8 * count, place, current, *pieces, specs=[SMEM] + [VMEM] * (1 + len(pieces)), params=LARGE,
+        ladder_flops, 8 * count, place, current, *pieces, specs=[SMEM] + [VMEM] * (1 + len(pieces)),
     )
     parts = call(
         functools.partial(sort_kernel, tiles, groups), [part] * (2 * groups), [blocks], count, 4 * count,
@@ -407,7 +406,7 @@
         [whole, inner, square, pltpu.VMEM((virtual, virtual), NARROW)],
         ladder_flops, 12 * count, place, occ_energy, current, *back,
         jnp.broadcast_to(vir_energy[:, None], (virtual, 128)), vir_energy[None, :], *pieces,
-        specs=[SMEM] * 2 + [VMEM] * (5 + len(pieces)), params=LARGE,
+        specs=[SMEM] * 2 + [VMEM] * (5 + len(pieces)),
     )
     last = []
     for c in chunks:
@@ -427,7 +426,7 @@
         in_specs=[SMEM, by_pair(virtual, virtual)] + [by_pair(edge, 2 * edge)] * devices,
         out_specs=by_pair(virtual, virtual),
         scratch_shapes=[pltpu.VMEM((devices, 1, edge, 2 * edge), NARROW)],
-        compiler_params=SMALL,
+        compiler_params=PARAMS,
         input_output_aliases={1: 0},
         cost_estimate=pl.CostEstimate(flops=count, bytes_accessed=10 * count, transcendentals=0),
     )(place, base, *by_distance(last))

time: 152 us -> 133 us (0.88)
  local copies, waits for them, and re-layouts: 26 us -> 8.39 us
  waiting for transfers between devices: 15.5 us -> 18.5 us
  Pallas kernels: 35.8 us -> 32.9 us
  other arithmetic: 2.82 us -> 0.38 us
    unnamed x94 -> x48, local copies, waits for them, and re-layouts: 24.4 us -> 6.87 us
    pallas_call x10, Pallas kernels: 31.7 us -> 28.9 us  [call(): pl.pallas_call(body, out_shape=outs, in_specs=specs, out_specs=jax.tree.m...]
    ppermute x4, waiting for transfers between devices: 0.01 us -> 2.49 us  [turn(): return lax.ppermute(x, 'occj', [(d, d ^ k) for d in range(devices)])]
    ppermute x18, starting transfers between devices: 32.2 us -> 34 us  [across_first(): lax.ppermute(parts[s], 'occi', [(k, k ^ s) for k in range(groups)])]
  transfers between devices with their start and end apart: 39 -> 39, of which waited for: 6 -> 7; matrix products, arithmetic and copies ran while one was open for 3% -> 1% of each run, Pallas kernels for 21% -> 22%
where the time goes in v10:
time: 133 us; the launch traced here: 132 us
  starting transfers between devices  69.6 us (52%)
  Pallas kernels  32.9 us (25%)
  waiting for transfers between devices  18.5 us (14%)
  local copies, waits for them, and re-layouts  8.39 us (6%)
  between operations  1.73 us (1%)
    ppermute x18, starting transfers between devices, across_first(): lax.ppermute(parts[s], 'occi', [(k, k ^ s) for k in range(groups)])  34 us
    pallas_call x10, Pallas kernels, call(): pl.pallas_call(body, out_shape=outs, in_specs=specs, out_specs=jax.tree.m...  28.9 us
    ppermute x14, starting transfers between devices, by_distance(): lax.ppermute(parts[k], 'occj', [(d, d ^ k) for d in range(devices)])  17.9 us
    all_to_all x3, starting transfers between devices, exchange(): lax.all_to_all(blocks, 'occj', split_axis=0, concat_axis=0, tiled=True)  13.1 us
    all_to_all x3, waiting for transfers between devices, exchange(): lax.all_to_all(blocks, 'occj', split_axis=0, concat_axis=0, tiled=True)  9.06 us
    unnamed x48, local copies, waits for them, and re-layouts  6.87 us
    ppermute x18, waiting for transfers between devices, across_first(): lax.ppermute(parts[s], 'occi', [(k, k ^ s) for k in range(groups)])  6.66 us
    ppermute x4, starting transfers between devices, turn(): return lax.ppermute(x, 'occj', [(d, d ^ k) for d in range(devices)])  4.62 us
  transfers between devices with their start and end apart: 39, of which 7 were waited for; matrix products, arithmetic and copies ran while one was open for 1% of the time, Pallas kernels for 22%

profile of v10, /device:TPU:0, one launch (start us, length us, event | category | flops | bytes accessed | tf_op | source)
XLA Modules:
  0.0 131.5 jit_solution(17957133958229153018)
XLA Ops:
  0.0 3.0 %collective-permute-start = (bf16[3,64,512]{2,1,0:T(8,128)(2,1)}, bf16[3,64,512]{2,1,0:T(8,128)(2,1)S(1)}, u32[]{:S(2)}, u32[]{:S(2)}) collective-permute-start(bf16[3,64,512]{2,1,0:T(8,128)(2,1)} %refs_0_.3), channel_id=1, source_target_pairs={{0,2},{1,3},{2,0},{3,1},{4,6},{5,7},{6,4},{7,5},{8,10},{9,11},{10,... | collective-permute-start | bytes 589832 | tf_op jit(solution)/shard_map/ppermute | solution.py:321
  3.0 1.5 %collective-permute-start.1 = (bf16[3,64,512]{2,1,0:T(8,128)(2,1)}, bf16[3,64,512]{2,1,0:T(8,128)(2,1)S(1)}, u32[]{:S(2)}, u32[]{:S(2)}) collective-permute-start(bf16[3,64,512]{2,1,0:T(8,128)(2,1)} %refs_0_.3), channel_id=1, source_target_pairs={{0,4},{1,5},{2,6},{3,7},{4,0},{5,1},{6,2},{7,3},{8,12},{9,13},{10,... | collective-permute-start | bytes 589832 | tf_op jit(solution)/shard_map/ppermute | solution.py:321
  4.6 1.6 %copy-done = f32[2,1,512,512]{3,2,1,0:T(8,128)S(1)} copy-done((f32[2,1,512,512]{3,2,1,0:T(8,128)S(1)}, f32[2,1,512,512]{3,2,1,0:T(8,128)}, u32[]{:S(2)}) %copy-start) | copy-done | bytes 2097176
  6.2 0.9 shard_map.73
  7.1 1.6 %collective-permute-start.10 = (bf16[2,128,256]{2,1,0:T(8,128)(2,1)S(1)}, bf16[2,128,256]{2,1,0:T(8,128)(2,1)S(1)}, u32[]{:S(2)}, u32[]{:S(2)}) collective-permute-start(bf16[2,128,256]{2,1,0:T(8,128)(2,1)S(1)} %get-tuple-element.62), channel_id=1, source_target_pairs={{0,7},{1,6},{2,5},{3,4},{4,3},{5,2},{6,1},{7,0},{8,15},{9,14},{10,... | collective-permute-start | bytes 393224 | tf_op jit(solution)/shard_map/ppermute | solution.py:288
  8.7 1.5 %collective-permute-start.4 = (bf16[2,128,256]{2,1,0:T(8,128)(2,1)S(1)}, bf16[2,128,256]{2,1,0:T(8,128)(2,1)S(1)}, u32[]{:S(2)}, u32[]{:S(2)}) collective-permute-start(bf16[2,128,256]{2,1,0:T(8,128)(2,1)S(1)} %get-tuple-element.56), channel_id=1, source_target_pairs={{0,1},{1,0},{2,3},{3,2},{4,5},{5,4},{6,7},{7,6},{8,9},{9,8},{10,11... | collective-permute-start | bytes 393224 | tf_op jit(solution)/shard_map/ppermute | solution.py:288
  10.2 0.6 dynamic_slice.14
  11.4 0.6 dynamic_slice.12
  12.7 0.6 collective-permute-start.5
  13.3 2.5 %collective-permute-done.1.refs_2_ = bf16[3,64,512]{2,1,0:T(8,128)(2,1)S(1)} collective-permute-done((bf16[3,64,512]{2,1,0:T(8,128)(2,1)}, bf16[3,64,512]{2,1,0:T(8,128)(2,1)S(1)}, u32[]{:S(2)}, u32[]{:S(2)}) %collective-permute-start.1) | collective-permute-done | bytes 196640 | tf_op jit(solution)/shard_map/ppermute | solution.py:321
  15.8 0.1 pad_maximum_fusion
  16.4 2.4 %collective-permute-start.7 = (bf16[2,128,256]{2,1,0:T(8,128)(2,1)S(1)}, bf16[2,128,256]{2,1,0:T(8,128)(2,1)S(1)}, u32[]{:S(2)}, u32[]{:S(2)}) collective-permute-start(bf16[2,128,256]{2,1,0:T(8,128)(2,1)S(1)} %get-tuple-element.59), channel_id=1, source_target_pairs={{0,4},{1,5},{2,6},{3,7},{4,0},{5,1},{6,2},{7,3},{8,12},{9,13},{10,... | collective-permute-start | bytes 393224 | tf_op jit(solution)/shard_map/ppermute | solution.py:288
  18.8 0.2 collective-permute-start.8
  19.0 2.8 %collective-permute-start.9 = (bf16[2,128,256]{2,1,0:T(8,128)(2,1)S(1)}, bf16[2,128,256]{2,1,0:T(8,128)(2,1)S(1)}, u32[]{:S(2)}, u32[]{:S(2)}) collective-permute-start(bf16[2,128,256]{2,1,0:T(8,128)(2,1)S(1)} %get-tuple-element.61), channel_id=1, source_target_pairs={{0,6},{1,7},{2,4},{3,5},{4,2},{5,3},{6,0},{7,1},{8,14},{9,15},{10,... | collective-permute-start | bytes 393224 | tf_op jit(solution)/shard_map/ppermute | solution.py:288
  21.8 6.2 %shard_map.74 = bf16[8,2,128,256]{3,2,1,0:T(8,128)(2,1)} custom-call(s32[2]{0:T(128)S(1)} %pad_add_fusion.place.source, f32[2,512,512]{2,1,0:T(8,128)} %bitcast.13, bf16[3,64,512]{2,1,0:T(8,128)(2,1)S(1)} %copy-done.1, bf16[3,64,512]{2,1,0:T(8,128)(2,1)S(1)} %collective-permute-done.refs_1_, bf16[3,64,512]{2,1,0:T(8,128)(2,1)S(1)} %collective-permute-done.1.refs_2_, ...), custom_call_target="tpu_custom_call" | custom-call | flops 3221225472 | bytes 4194304 | tf_op jit(solution)/shard_map/pallas_call | solution.py:42
  28.1 0.3 collective-permute-done.8.refs_5_
  28.3 0.7 shard_map.75
  29.0 1.6 %collective-permute-start.11 = (bf16[2,2,64,256]{3,2,1,0:T(8,128)(2,1)S(1)}, bf16[2,2,64,256]{3,2,1,0:T(8,128)(2,1)S(1)}, u32[]{:S(2)}, u32[]{:S(2)}) collective-permute-start(bf16[2,2,64,256]{3,2,1,0:T(8,128)(2,1)S(1)} %get-tuple-element.64), channel_id=1, source_target_pairs={{0,8},{8,0},{16,24},{24,16},{1,9},{9,1},{17,25},{25,17},{2,10},{10... | collective-permute-start | bytes 393224 | tf_op jit(solution)/shard_map/ppermute | solution.py:295
  30.7 2.6 %collective-permute-start.12 = (bf16[2,2,64,256]{3,2,1,0:T(8,128)(2,1)S(1)}, bf16[2,2,64,256]{3,2,1,0:T(8,128)(2,1)S(1)}, u32[]{:S(2)}, u32[]{:S(2)}) collective-permute-start(bf16[2,2,64,256]{3,2,1,0:T(8,128)(2,1)S(1)} %get-tuple-element.65), channel_id=1, source_target_pairs={{0,16},{8,24},{16,0},{24,8},{1,17},{9,25},{17,1},{25,9},{2,18},{10... | collective-permute-start | bytes 393224 | tf_op jit(solution)/shard_map/ppermute | solution.py:295
  33.3 0.2 collective-permute-start.13
  33.6 3.6 %all-to-all-start = ((bf16[8,2,128,256]{3,2,1,0:T(8,128)(2,1)}), bf16[8,2,128,256]{3,2,1,0:T(8,128)(2,1)S(1)}, u32[]{:S(2)}, u32[]{:S(2)}) async-start(bf16[8,2,128,256]{3,2,1,0:T(8,128)(2,1)} %shard_map.74), calls=%async_computation | async-start | bytes 2097152 | tf_op jit(solution)/shard_map/all_to_all | solution.py:282
  37.2 0.7 collective-permute-start.17
  37.9 3.5 %collective-permute-start.18 = (bf16[2,2,64,256]{3,2,1,0:T(8,128)(2,1)S(1)}, bf16[2,2,64,256]{3,2,1,0:T(8,128)(2,1)S(1)}, u32[]{:S(2)}, u32[]{:S(2)}) collective-permute-start(bf16[2,2,64,256]{3,2,1,0:T(8,128)(2,1)S(1)} %get-tuple-element.75), channel_id=1, source_target_pairs={{0,16},{8,24},{16,0},{24,8},{1,17},{9,25},{17,1},{25,9},{2,18},{10... | collective-permute-start | bytes 393224 | tf_op jit(solution)/shard_map/ppermute | solution.py:295
  41.4 0.2 collective-permute-start.19
  41.6 2.0 %collective-permute-done.12.refs_2_ = bf16[2,2,64,256]{3,2,1,0:T(8,128)(2,1)S(1)} collective-permute-done((bf16[2,2,64,256]{3,2,1,0:T(8,128)(2,1)S(1)}, bf16[2,2,64,256]{3,2,1,0:T(8,128)(2,1)S(1)}, u32[]{:S(2)}, u32[]{:S(2)}) %collective-permute-start.12) | collective-permute-done | bytes 131104 | tf_op jit(solution)/shard_map/ppermute | solution.py:295
  43.6 1.2 shard_map.76.place
  44.8 7.7 %all-to-all-done.ladder = bf16[8,2,128,256]{3,2,1,0:T(8,128)(2,1)S(1)} async-done(((bf16[8,2,128,256]{3,2,1,0:T(8,128)(2,1)}), bf16[8,2,128,256]{3,2,1,0:T(8,128)(2,1)S(1)}, u32[]{:S(2)}, u32[]{:S(2)}) %all-to-all-start) | async-done | bytes 1048608 | tf_op jit(solution)/shard_map/all_to_all | solution.py:282
  52.5 0.7 copy-done.20
  53.2 1.6 %shard_map.77 = (bf16[2,2,64,256]{3,2,1,0:T(8,128)(2,1)S(1)}, bf16[2,2,64,256]{3,2,1,0:T(8,128)(2,1)S(1)}, bf16[2,2,64,256]{3,2,1,0:T(8,128)(2,1)S(1)}, bf16[2,2,64,256]{3,2,1,0:T(8,128)(2,1)S(1)}) custom-call(s32[2]{0:T(128)S(1)} %copy-done.20, f32[8,8]{1,0:T(8,128)S(1)} %convert_element_type.3.fock, bf16[8,2,128,256]{3,2,1,0:T(8,128)(2,1)S(1)} %all-to-all-done.ladder, ...), custom_call_target="tpu_custom_call" | custom-call | flops 30000001024 | bytes 3145728 | tf_op jit(solution)/shard_map/pallas_call | solution.py:42
  54.8 1.3 %collective-permute-start.14 = (bf16[2,2,64,256]{3,2,1,0:T(8,128)(2,1)S(1)}, bf16[2,2,64,256]{3,2,1,0:T(8,128)(2,1)S(1)}, u32[]{:S(2)}, u32[]{:S(2)}) collective-permute-start(bf16[2,2,64,256]{3,2,1,0:T(8,128)(2,1)S(1)} %get-tuple-element.69.refs_1_), channel_id=1, source_target_pairs={{0,8},{8,0},{16,24},{24,16},{1,9},{9,1},{17,25},{25,17},{2,10},{10... | collective-permute-start | bytes 393224 | tf_op jit(solution)/shard_map/ppermute | solution.py:295
  56.1 2.9 %collective-permute-start.15 = (bf16[2,2,64,256]{3,2,1,0:T(8,128)(2,1)S(1)}, bf16[2,2,64,256]{3,2,1,0:T(8,128)(2,1)S(1)}, u32[]{:S(2)}, u32[]{:S(2)}) collective-permute-start(bf16[2,2,64,256]{3,2,1,0:T(8,128)(2,1)S(1)} %get-tuple-element.70.refs_2_), channel_id=1, source_target_pairs={{0,16},{8,24},{16,0},{24,8},{1,17},{9,25},{17,1},{25,9},{2,18},{10... | collective-permute-start | bytes 393224 | tf_op jit(solution)/shard_map/ppermute | solution.py:295
  59.0 0.2 collective-permute-start.16
  59.2 1.6 %shard_map.79 = (bf16[2,2,64,256]{3,2,1,0:T(8,128)(2,1)S(1)}, bf16[2,2,64,256]{3,2,1,0:T(8,128)(2,1)S(1)}, bf16[2,2,64,256]{3,2,1,0:T(8,128)(2,1)S(1)}, bf16[2,2,64,256]{3,2,1,0:T(8,128)(2,1)S(1)}) custom-call(s32[2]{0:T(128)S(1)} %copy-done.10, f32[8,8]{1,0:T(8,128)S(1)} %convert_element_type.3.fock, bf16[8,2,128,256]{3,2,1,0:T(8,128)(2,1)S(1)} %all-to-all-done.ladder, ...), custom_call_target="tpu_custom_call" | custom-call | flops 30000001024 | bytes 3145728 | tf_op jit(solution)/shard_map/pallas_call | solution.py:42
  60.9 0.7 copy-done.18
  61.5 0.4 collective-permute-start.20
  61.9 3.8 %collective-permute-start.21 = (bf16[2,2,64,256]{3,2,1,0:T(8,128)(2,1)S(1)}, bf16[2,2,64,256]{3,2,1,0:T(8,128)(2,1)S(1)}, u32[]{:S(2)}, u32[]{:S(2)}) collective-permute-start(bf16[2,2,64,256]{3,2,1,0:T(8,128)(2,1)S(1)} %get-tuple-element.79.refs_2_), channel_id=1, source_target_pairs={{0,16},{8,24},{16,0},{24,8},{1,17},{9,25},{17,1},{25,9},{2,18},{10... | collective-permute-start | bytes 393224 | tf_op jit(solution)/shard_map/ppermute | solution.py:295
  65.7 2.4 %collective-permute-start.22 = (bf16[2,2,64,256]{3,2,1,0:T(8,128)(2,1)S(1)}, bf16[2,2,64,256]{3,2,1,0:T(8,128)(2,1)S(1)}, u32[]{:S(2)}, u32[]{:S(2)}) collective-permute-start(bf16[2,2,64,256]{3,2,1,0:T(8,128)(2,1)S(1)} %get-tuple-element.80.refs_3_), channel_id=1, source_target_pairs={{0,24},{8,16},{16,8},{24,0},{1,25},{9,17},{17,9},{25,1},{2,26},{10... | collective-permute-start | bytes 393224 | tf_op jit(solution)/shard_map/ppermute | solution.py:295
  68.0 0.9 collective-permute-done.15.refs_6_
  69.0 3.0 %shard_map.78 = (bf16[8,2,64,256]{3,2,1,0:T(8,128)(2,1)}, bf16[2,8,64,256]{3,2,1,0:T(8,128)(2,1)S(1)}, bf16[2,2,64,256]{3,2,1,0:T(8,128)(2,1)S(1)}, bf16[2,2,64,...) custom-call(s32[2]{0:T(128)S(1)} %copy-done.10, ...), custom_call_target="tpu_custom_call" | custom-call | flops 30000001024 | bytes 5242880 | tf_op jit(solution)/shard_map/pallas_call | solution.py:42
  72.0 0.8 copy-done.16
  72.8 7.2 %collective-permute-start.26 = (bf16[2,2,64,256]{3,2,1,0:T(8,128)(2,1)S(1)}, bf16[2,2,64,256]{3,2,1,0:T(8,128)(2,1)S(1)}, u32[]{:S(2)}, u32[]{:S(2)}) collective-permute-start(bf16[2,2,64,256]{3,2,1,0:T(8,128)(2,1)S(1)} %get-tuple-element.90.refs_1_), channel_id=1, source_target_pairs={{0,8},{8,0},{16,24},{24,16},{1,9},{9,1},{17,25},{25,17},{2,10},{10... | collective-permute-start | bytes 393224 | tf_op jit(solution)/shard_map/ppermute | solution.py:295
  80.0 0.8 collective-permute-start.27
  80.8 5.7 %all-to-all-start.1 = ((bf16[8,2,64,256]{3,2,1,0:T(8,128)(2,1)}), bf16[8,2,64,256]{3,2,1,0:T(8,128)(2,1)S(1)}, u32[]{:S(2)}, u32[]{:S(2)}) async-start(bf16[8,2,64,256]{3,2,1,0:T(8,128)(2,1)} %get-tuple-element.72), calls=%async_computation.1 | async-start | bytes 1048576 | tf_op jit(solution)/shard_map/all_to_all | solution.py:282
  86.4 1.6 %collective-permute-start.28 = (bf16[2,2,64,256]{3,2,1,0:T(8,128)(2,1)S(1)}, bf16[2,2,64,256]{3,2,1,0:T(8,128)(2,1)S(1)}, u32[]{:S(2)}, u32[]{:S(2)}) collective-permute-start(bf16[2,2,64,256]{3,2,1,0:T(8,128)(2,1)S(1)} %get-tuple-element.92.refs_3_), channel_id=1, source_target_pairs={{0,24},{8,16},{16,8},{24,0},{1,25},{9,17},{17,9},{25,1},{2,26},{10... | collective-permute-start | bytes 393224 | tf_op jit(solution)/shard_map/ppermute | solution.py:295
  88.1 0.9 copy-done.19
  89.0 3.0 %shard_map.80 = (bf16[8,2,64,256]{3,2,1,0:T(8,128)(2,1)}, bf16[2,8,64,256]{3,2,1,0:T(8,128)(2,1)S(1)}, bf16[2,2,64,256]{3,2,1,0:T(8,128)(2,1)S(1)}, bf16[2,2,64,...) custom-call(s32[2]{0:T(128)S(1)} %copy-done.10, ...), custom_call_target="tpu_custom_call" | custom-call | flops 30000001024 | bytes 5242880 | tf_op jit(solution)/shard_map/pallas_call | solution.py:42
  92.0 1.1 collective-permute-start.23
  93.2 1.7 %collective-permute-start.24 = (bf16[2,2,64,256]{3,2,1,0:T(8,128)(2,1)S(1)}, bf16[2,2,64,256]{3,2,1,0:T(8,128)(2,1)S(1)}, u32[]{:S(2)}, u32[]{:S(2)}) collective-permute-start(bf16[2,2,64,256]{3,2,1,0:T(8,128)(2,1)S(1)} %get-tuple-element.86.refs_2_), channel_id=1, source_target_pairs={{0,16},{8,24},{16,0},{24,8},{1,17},{9,25},{17,1},{25,9},{2,18},{10... | collective-permute-start | bytes 393224 | tf_op jit(solution)/shard_map/ppermute | solution.py:295
  94.8 1.3 %all-to-all-done.1.upper = bf16[8,2,64,256]{3,2,1,0:T(8,128)(2,1)S(1)} async-done(((bf16[8,2,64,256]{3,2,1,0:T(8,128)(2,1)}), bf16[8,2,64,256]{3,2,1,0:T(8,128)(2,1)S(1)}, u32[]{:S(2)}, u32[]{:S(2)}) %all-to-all-start.1) | async-done | bytes 524320 | tf_op jit(solution)/shard_map/all_to_all | solution.py:282
  96.2 3.9 %all-to-all-start.2 = ((bf16[8,2,64,256]{3,2,1,0:T(8,128)(2,1)}), bf16[8,2,64,256]{3,2,1,0:T(8,128)(2,1)S(1)}, u32[]{:S(2)}, u32[]{:S(2)}) async-start(bf16[8,2,64,256]{3,2,1,0:T(8,128)(2,1)} %get-tuple-element.82), calls=%async_computation.2 | async-start | bytes 1048576 | tf_op jit(solution)/shard_map/all_to_all | solution.py:282
  100.1 1.6 %collective-permute-start.25 = (bf16[2,2,64,256]{3,2,1,0:T(8,128)(2,1)S(1)}, bf16[2,2,64,256]{3,2,1,0:T(8,128)(2,1)S(1)}, u32[]{:S(2)}, u32[]{:S(2)}) collective-permute-start(bf16[2,2,64,256]{3,2,1,0:T(8,128)(2,1)S(1)} %get-tuple-element.87.refs_3_), channel_id=1, source_target_pairs={{0,24},{8,16},{16,8},{24,0},{1,25},{9,17},{17,9},{25,1},{2,26},{10... | collective-permute-start | bytes 393224 | tf_op jit(solution)/shard_map/ppermute | solution.py:295
  101.7 1.0 copy-done.17
  102.8 1.3 shard_map.82.refs_8_
  104.1 3.8 %collective-permute-done.25.refs_7_ = bf16[2,2,64,256]{3,2,1,0:T(8,128)(2,1)S(1)} collective-permute-done((bf16[2,2,64,256]{3,2,1,0:T(8,128)(2,1)S(1)}, bf16[2,2,64,256]{3,2,1,0:T(8,128)(2,1)S(1)}, u32[]{:S(2)}, u32[]{:S(2)}) %collective-permute-start.25) | collective-permute-done | bytes 131104 | tf_op jit(solution)/shard_map/ppermute | solution.py:295
  107.9 2.1 %shard_map.83 = (bf16[2,128,256]{2,1,0:T(8,128)(2,1)S(1)}, bf16[2,128,256]{2,1,0:T(8,128)(2,1)S(1)}, bf16[2,128,256]{2,1,0:T(8,128)(2,1)S(1)}, bf16[2,128,256]{2...) custom-call(s32[2]{0:T(128)S(1)} %copy-done.10, ...), custom_call_target="tpu_custom_call" | custom-call | flops 1048576 | bytes 4194304 | tf_op jit(solution)/shard_map/pallas_call | solution.py:42
  110.0 1.7 %collective-permute-start.30 = (bf16[2,128,256]{2,1,0:T(8,128)(2,1)S(1)}, bf16[2,128,256]{2,1,0:T(8,128)(2,1)S(1)}, u32[]{:S(2)}, u32[]{:S(2)}) collective-permute-start(bf16[2,128,256]{2,1,0:T(8,128)(2,1)S(1)} %get-tuple-element.95), channel_id=1, source_target_pairs={{0,2},{1,3},{2,0},{3,1},{4,6},{5,7},{6,4},{7,5},{8,10},{9,11},{10,... | collective-permute-start | bytes 393224 | tf_op jit(solution)/shard_map/ppermute | solution.py:288
  111.7 0.2 collective-permute-start.31
  111.9 2.4 %collective-permute-start.32 = (bf16[2,128,256]{2,1,0:T(8,128)(2,1)}, bf16[2,128,256]{2,1,0:T(8,128)(2,1)S(1)}, u32[]{:S(2)}, u32[]{:S(2)}) collective-permute-start(bf16[2,128,256]{2,1,0:T(8,128)(2,1)} %get-tuple-element.97), channel_id=1, source_target_pairs={{0,4},{1,5},{2,6},{3,7},{4,0},{5,1},{6,2},{7,3},{8,12},{9,13},{10,... | collective-permute-start | bytes 393224 | tf_op jit(solution)/shard_map/ppermute | solution.py:288
  114.3 2.8 %collective-permute-start.34 = (bf16[2,128,256]{2,1,0:T(8,128)(2,1)}, bf16[2,128,256]{2,1,0:T(8,128)(2,1)S(1)}, u32[]{:S(2)}, u32[]{:S(2)}) collective-permute-start(bf16[2,128,256]{2,1,0:T(8,128)(2,1)} %get-tuple-element.99), channel_id=1, source_target_pairs={{0,6},{1,7},{2,4},{3,5},{4,2},{5,3},{6,0},{7,1},{8,14},{9,15},{10,... | collective-permute-start | bytes 393224 | tf_op jit(solution)/shard_map/ppermute | solution.py:288
  117.1 1.7 %collective-permute-start.35 = (bf16[2,128,256]{2,1,0:T(8,128)(2,1)S(1)}, bf16[2,128,256]{2,1,0:T(8,128)(2,1)S(1)}, u32[]{:S(2)}, u32[]{:S(2)}) collective-permute-start(bf16[2,128,256]{2,1,0:T(8,128)(2,1)S(1)} %get-tuple-element.100), channel_id=1, source_target_pairs={{0,7},{1,6},{2,5},{3,4},{4,3},{5,2},{6,1},{7,0},{8,15},{9,14},{10,... | collective-permute-start | bytes 393224 | tf_op jit(solution)/shard_map/ppermute | solution.py:288
  118.9 0.1 broadcast_in_dim.4.row
  119.0 1.1 copy-done.15
  120.2 8.6 %shard_map.81.source = f32[2,512,512]{2,1,0:T(8,128)} custom-call(s32[2]{0:T(128)S(1)} %copy-done.10, f32[8]{0:T(128)S(1)} %copy-done.13, f32[2,512,512]{2,1,0:T(8,128)} %bitcast.14, bf16[8,2,64,256]{3,2,1,0:T(8,128)(2,1)S(1)} %all-to-all-done.1.upper, bf16[8,2,64,256]{3,2,1,0:T(8,128)(2,1)S(1)} %all-to-all-done.2.lower, ...), custom_call_target="tpu_custom_call" | custom-call | flops 3221225472 | bytes 6291456 | tf_op jit(solution)/shard_map/pallas_call | solution.py:42
  128.7 2.8 %shard_map.84 = f32[2,512,512]{2,1,0:T(8,128)} custom-call(s32[2]{0:T(128)S(1)} %copy-done.10, f32[2,512,512]{2,1,0:T(8,128)} %shard_map.81.source, bf16[2,128,256]{2,1,0:T(8,128)(2,1)S(1)} %get-tuple-element.93.refs_0_, bf16[2,128,256]{2,1,0:T(8,128)(2,1)S(1)} %collective-permute-done.29.refs_1_, ...), custom_call_target="tpu_custom_call", output_to_operand_aliasing={{}: (1, {})} | custom-call | flops 524288 | bytes 5242880 | tf_op jit(solution)/shard_map/pallas_call | solution.py:422
  (86 shorter events, 0.8 us)
Async XLA Ops:
  0.0 10.2 %copy-start.23 = (s32[8]{0:T(128)S(1)}, s32[8]{0:T(128)}, u32[]{:S(2)}) copy-start(s32[8]{0:T(128)} %constant.25.clone) | copy-start | bytes 100
  0.0 11.4 %copy-start.22 = (s32[8]{0:T(128)S(1)}, s32[8]{0:T(128)}, u32[]{:S(2)}) copy-start(s32[8]{0:T(128)} %constant.24.clone) | copy-start | bytes 100
  0.0 16.0 %copy-start.11 = (f32[512]{0:T(512)S(1)}, f32[512]{0:T(512)}, u32[]{:S(2)}) copy-start(f32[512]{0:T(512)} %param.11) | copy-start | bytes 6148
  0.0 12.7 %collective-permute-start = (bf16[3,64,512]{2,1,0:T(8,128)(2,1)}, bf16[3,64,512]{2,1,0:T(8,128)(2,1)S(1)}, u32[]{:S(2)}, u32[]{:S(2)}) collective-permute-start(bf16[3,64,512]{2,1,0:T(8,128)(2,1)} %refs_0_.3), channel_id=1, source_target_pairs={{0,2},{1,3},{2,0},{3,1},{4,6},{5,7},{6,4},{7,5},{8,10},{9,11},{10,... | collective-permute-start | bytes 589832 | tf_op jit(solution)/shard_map/ppermute | solution.py:321
  3.0 12.8 %collective-permute-start.1 = (bf16[3,64,512]{2,1,0:T(8,128)(2,1)}, bf16[3,64,512]{2,1,0:T(8,128)(2,1)S(1)}, u32[]{:S(2)}, u32[]{:S(2)}) collective-permute-start(bf16[3,64,512]{2,1,0:T(8,128)(2,1)} %refs_0_.3), channel_id=1, source_target_pairs={{0,4},{1,5},{2,6},{3,7},{4,0},{5,1},{6,2},{7,3},{8,12},{9,13},{10,... | collective-permute-start | bytes 589832 | tf_op jit(solution)/shard_map/ppermute | solution.py:321
  4.5 11.3 %collective-permute-start.2 = (bf16[3,64,512]{2,1,0:T(8,128)(2,1)}, bf16[3,64,512]{2,1,0:T(8,128)(2,1)S(1)}, u32[]{:S(2)}, u32[]{:S(2)}) collective-permute-start(bf16[3,64,512]{2,1,0:T(8,128)(2,1)} %refs_0_.3), channel_id=1, source_target_pairs={{0,6},{1,7},{2,4},{3,5},{4,2},{5,3},{6,0},{7,1},{8,14},{9,15},{10,... | collective-permute-start | bytes 589832 | tf_op jit(solution)/shard_map/ppermute | solution.py:321
  4.6 23.7 %copy-start.9 = (s32[2]{0:T(128)}, s32[2]{0:T(128)S(1)}, u32[]{:S(2)}) copy-start(s32[2]{0:T(128)S(1)} %pad_add_fusion.place.source) | copy-start | bytes 28
  4.6 1.6 %copy-start = (f32[2,1,512,512]{3,2,1,0:T(8,128)S(1)}, f32[2,1,512,512]{3,2,1,0:T(8,128)}, u32[]{:S(2)}) copy-start(f32[2,1,512,512]{3,2,1,0:T(8,128)} %param.7) | copy-start | bytes 6291460
  6.2 9.6 %copy-start.1 = (bf16[3,64,512]{2,1,0:T(8,128)(2,1)S(1)}, bf16[3,64,512]{2,1,0:T(8,128)(2,1)}, u32[]{:S(2)}) copy-start(bf16[3,64,512]{2,1,0:T(8,128)(2,1)} %refs_0_.3) | copy-start | bytes 589828
  7.1 9.3 %collective-permute-start.10 = (bf16[2,128,256]{2,1,0:T(8,128)(2,1)S(1)}, bf16[2,128,256]{2,1,0:T(8,128)(2,1)S(1)}, u32[]{:S(2)}, u32[]{:S(2)}) collective-permute-start(bf16[2,128,256]{2,1,0:T(8,128)(2,1)S(1)} %get-tuple-element.62), channel_id=1, source_target_pairs={{0,7},{1,6},{2,5},{3,4},{4,3},{5,2},{6,1},{7,0},{8,15},{9,14},{10,... | collective-permute-start | bytes 393224 | tf_op jit(solution)/shard_map/ppermute | solution.py:288
  8.7 10.1 %collective-permute-start.4 = (bf16[2,128,256]{2,1,0:T(8,128)(2,1)S(1)}, bf16[2,128,256]{2,1,0:T(8,128)(2,1)S(1)}, u32[]{:S(2)}, u32[]{:S(2)}) collective-permute-start(bf16[2,128,256]{2,1,0:T(8,128)(2,1)S(1)} %get-tuple-element.56), channel_id=1, source_target_pairs={{0,1},{1,0},{2,3},{3,2},{4,5},{5,4},{6,7},{7,6},{8,9},{9,8},{10,11... | collective-permute-start | bytes 393224 | tf_op jit(solution)/shard_map/ppermute | solution.py:288
  12.7 15.3 %copy-start.3 = (bf16[3,64,512]{2,1,0:T(8,128)(2,1)}, bf16[3,64,512]{2,1,0:T(8,128)(2,1)S(1)}, u32[]{:S(2)}) copy-start(bf16[3,64,512]{2,1,0:T(8,128)(2,1)S(1)} %collective-permute-done.refs_1_) | copy-start | bytes 589828
  12.7 15.3 %collective-permute-start.5 = (bf16[2,128,256]{2,1,0:T(8,128)(2,1)S(1)}, bf16[2,128,256]{2,1,0:T(8,128)(2,1)S(1)}, u32[]{:S(2)}, u32[]{:S(2)}) collective-permute-start(bf16[2,128,256]{2,1,0:T(8,128)(2,1)S(1)} %get-tuple-element.57), channel_id=1, source_target_pairs={{0,2},{1,3},{2,0},{3,1},{4,6},{5,7},{6,4},{7,5},{8,10},{9,11},{10,... | collective-permute-start | bytes 393224 | tf_op jit(solution)/shard_map/ppermute | solution.py:288
  15.8 12.2 %copy-start.5 = (bf16[3,64,512]{2,1,0:T(8,128)(2,1)}, bf16[3,64,512]{2,1,0:T(8,128)(2,1)S(1)}, u32[]{:S(2)}) copy-start(bf16[3,64,512]{2,1,0:T(8,128)(2,1)S(1)} %collective-permute-done.1.refs_2_) | copy-start | bytes 589828
  15.8 12.3 %collective-permute-start.6 = (bf16[2,128,256]{2,1,0:T(8,128)(2,1)S(1)}, bf16[2,128,256]{2,1,0:T(8,128)(2,1)S(1)}, u32[]{:S(2)}, u32[]{:S(2)}) collective-permute-start(bf16[2,128,256]{2,1,0:T(8,128)(2,1)S(1)} %get-tuple-element.58), channel_id=1, source_target_pairs={{0,3},{1,2},{2,1},{3,0},{4,7},{5,6},{6,5},{7,4},{8,11},{9,10},{10,... | collective-permute-start | bytes 393224 | tf_op jit(solution)/shard_map/ppermute | solution.py:288
  15.8 12.2 %copy-start.7 = (bf16[3,64,512]{2,1,0:T(8,128)(2,1)}, bf16[3,64,512]{2,1,0:T(8,128)(2,1)S(1)}, u32[]{:S(2)}) copy-start(bf16[3,64,512]{2,1,0:T(8,128)(2,1)S(1)} %collective-permute-done.2.refs_3_) | copy-start | bytes 589828
  15.9 3.0 %collective-permute-start.3 = (bf16[4,3,64,512]{3,2,1,0:T(8,128)(2,1)S(1)}, bf16[4,3,64,512]{3,2,1,0:T(8,128)(2,1)S(1)}, u32[]{:S(2)}, u32[]{:S(2)}) collective-permute-start(bf16[4,3,64,512]{3,2,1,0:T(8,128)(2,1)S(1)} %pad_maximum_fusion), channel_id=1, source_target_pairs={{0,1},{1,0},{2,3},{3,2},{4,5},{5,4},{6,7},{7,6},{8,9},{9,8},{10,11... | collective-permute-start | bytes 2359304 | tf_op jit(solution)/shard_map/ppermute | solution.py:321
  16.4 11.7 %collective-permute-start.7 = (bf16[2,128,256]{2,1,0:T(8,128)(2,1)S(1)}, bf16[2,128,256]{2,1,0:T(8,128)(2,1)S(1)}, u32[]{:S(2)}, u32[]{:S(2)}) collective-permute-start(bf16[2,128,256]{2,1,0:T(8,128)(2,1)S(1)} %get-tuple-element.59), channel_id=1, source_target_pairs={{0,4},{1,5},{2,6},{3,7},{4,0},{5,1},{6,2},{7,3},{8,12},{9,13},{10,... | collective-permute-start | bytes 393224 | tf_op jit(solution)/shard_map/ppermute | solution.py:288
  18.8 9.6 %collective-permute-start.8 = (bf16[2,128,256]{2,1,0:T(8,128)(2,1)S(1)}, bf16[2,128,256]{2,1,0:T(8,128)(2,1)S(1)}, u32[]{:S(2)}, u32[]{:S(2)}) collective-permute-start(bf16[2,128,256]{2,1,0:T(8,128)(2,1)S(1)} %get-tuple-element.60), channel_id=1, source_target_pairs={{0,5},{1,4},{2,7},{3,6},{4,1},{5,0},{6,3},{7,2},{8,13},{9,12},{10,... | collective-permute-start | bytes 393224 | tf_op jit(solution)/shard_map/ppermute | solution.py:288
  19.0 9.1 %copy-start.14 = (bf16[4,3,64,512]{3,2,1,0:T(8,128)(2,1)}, bf16[4,3,64,512]{3,2,1,0:T(8,128)(2,1)S(1)}, u32[]{:S(2)}) copy-start(bf16[4,3,64,512]{3,2,1,0:T(8,128)(2,1)S(1)} %collective-permute-done.3.refs_4_) | copy-start | bytes 2359300
  19.0 14.6 %copy-start.21 = (bf16[8,8]{1,0:T(8,128)(2,1)S(1)}, bf16[8,8]{1,0:T(8,128)(2,1)}, u32[]{:S(2)}) copy-start(bf16[8,8]{1,0:T(8,128)(2,1)} %param.9) | copy-start | bytes 388
  19.0 9.4 %collective-permute-start.9 = (bf16[2,128,256]{2,1,0:T(8,128)(2,1)S(1)}, bf16[2,128,256]{2,1,0:T(8,128)(2,1)S(1)}, u32[]{:S(2)}, u32[]{:S(2)}) collective-permute-start(bf16[2,128,256]{2,1,0:T(8,128)(2,1)S(1)} %get-tuple-element.61), channel_id=1, source_target_pairs={{0,6},{1,7},{2,4},{3,5},{4,2},{5,3},{6,0},{7,1},{8,14},{9,15},{10,... | collective-permute-start | bytes 393224 | tf_op jit(solution)/shard_map/ppermute | solution.py:288
  29.0 12.4 %collective-permute-start.11 = (bf16[2,2,64,256]{3,2,1,0:T(8,128)(2,1)S(1)}, bf16[2,2,64,256]{3,2,1,0:T(8,128)(2,1)S(1)}, u32[]{:S(2)}, u32[]{:S(2)}) collective-permute-start(bf16[2,2,64,256]{3,2,1,0:T(8,128)(2,1)S(1)} %get-tuple-element.64), channel_id=1, source_target_pairs={{0,8},{8,0},{16,24},{24,16},{1,9},{9,1},{17,25},{25,17},{2,10},{10... | collective-permute-start | bytes 393224 | tf_op jit(solution)/shard_map/ppermute | solution.py:295
  30.7 12.9 %collective-permute-start.12 = (bf16[2,2,64,256]{3,2,1,0:T(8,128)(2,1)S(1)}, bf16[2,2,64,256]{3,2,1,0:T(8,128)(2,1)S(1)}, u32[]{:S(2)}, u32[]{:S(2)}) collective-permute-start(bf16[2,2,64,256]{3,2,1,0:T(8,128)(2,1)S(1)} %get-tuple-element.65), channel_id=1, source_target_pairs={{0,16},{8,24},{16,0},{24,8},{1,17},{9,25},{17,1},{25,9},{2,18},{10... | collective-permute-start | bytes 393224 | tf_op jit(solution)/shard_map/ppermute | solution.py:295
  33.3 10.4 %collective-permute-start.13 = (bf16[2,2,64,256]{3,2,1,0:T(8,128)(2,1)S(1)}, bf16[2,2,64,256]{3,2,1,0:T(8,128)(2,1)S(1)}, u32[]{:S(2)}, u32[]{:S(2)}) collective-permute-start(bf16[2,2,64,256]{3,2,1,0:T(8,128)(2,1)S(1)} %get-tuple-element.66), channel_id=1, source_target_pairs={{0,24},{8,16},{16,8},{24,0},{1,25},{9,17},{17,9},{25,1},{2,26},{10... | collective-permute-start | bytes 393224 | tf_op jit(solution)/shard_map/ppermute | solution.py:295
  33.6 18.9 %all-to-all-start = ((bf16[8,2,128,256]{3,2,1,0:T(8,128)(2,1)}), bf16[8,2,128,256]{3,2,1,0:T(8,128)(2,1)S(1)}, u32[]{:S(2)}, u32[]{:S(2)}) async-start(bf16[8,2,128,256]{3,2,1,0:T(8,128)(2,1)} %shard_map.74), calls=%async_computation | async-start | bytes 2097152 | tf_op jit(solution)/shard_map/all_to_all | solution.py:282
  37.2 21.8 %collective-permute-start.17 = (bf16[2,2,64,256]{3,2,1,0:T(8,128)(2,1)S(1)}, bf16[2,2,64,256]{3,2,1,0:T(8,128)(2,1)S(1)}, u32[]{:S(2)}, u32[]{:S(2)}) collective-permute-start(bf16[2,2,64,256]{3,2,1,0:T(8,128)(2,1)S(1)} %get-tuple-element.74), channel_id=1, source_target_pairs={{0,8},{8,0},{16,24},{24,16},{1,9},{9,1},{17,25},{25,17},{2,10},{10... | collective-permute-start | bytes 393224 | tf_op jit(solution)/shard_map/ppermute | solution.py:295
  37.9 21.3 %collective-permute-start.18 = (bf16[2,2,64,256]{3,2,1,0:T(8,128)(2,1)S(1)}, bf16[2,2,64,256]{3,2,1,0:T(8,128)(2,1)S(1)}, u32[]{:S(2)}, u32[]{:S(2)}) collective-permute-start(bf16[2,2,64,256]{3,2,1,0:T(8,128)(2,1)S(1)} %get-tuple-element.75), channel_id=1, source_target_pairs={{0,16},{8,24},{16,0},{24,8},{1,17},{9,25},{17,1},{25,9},{2,18},{10... | collective-permute-start | bytes 393224 | tf_op jit(solution)/shard_map/ppermute | solution.py:295
  41.4 17.8 %collective-permute-start.19 = (bf16[2,2,64,256]{3,2,1,0:T(8,128)(2,1)S(1)}, bf16[2,2,64,256]{3,2,1,0:T(8,128)(2,1)S(1)}, u32[]{:S(2)}, u32[]{:S(2)}) collective-permute-start(bf16[2,2,64,256]{3,2,1,0:T(8,128)(2,1)S(1)} %get-tuple-element.76), channel_id=1, source_target_pairs={{0,24},{8,16},{16,8},{24,0},{1,25},{9,17},{17,9},{25,1},{2,26},{10... | collective-permute-start | bytes 393224 | tf_op jit(solution)/shard_map/ppermute | solution.py:295
  44.8 14.4 %copy-start.10 = (s32[2]{0:T(128)S(1)}, s32[2]{0:T(128)}, u32[]{:S(2)}) copy-start(s32[2]{0:T(128)} %copy-done.9) | copy-start | bytes 28
  52.5 0.7 copy-start.20
  54.8 10.9 %collective-permute-start.14 = (bf16[2,2,64,256]{3,2,1,0:T(8,128)(2,1)S(1)}, bf16[2,2,64,256]{3,2,1,0:T(8,128)(2,1)S(1)}, u32[]{:S(2)}, u32[]{:S(2)}) collective-permute-start(bf16[2,2,64,256]{3,2,1,0:T(8,128)(2,1)S(1)} %get-tuple-element.69.refs_1_), channel_id=1, source_target_pairs={{0,8},{8,0},{16,24},{24,16},{1,9},{9,1},{17,25},{25,17},{2,10},{10... | collective-permute-start | bytes 393224 | tf_op jit(solution)/shard_map/ppermute | solution.py:295
  56.1 12.8 %collective-permute-start.15 = (bf16[2,2,64,256]{3,2,1,0:T(8,128)(2,1)S(1)}, bf16[2,2,64,256]{3,2,1,0:T(8,128)(2,1)S(1)}, u32[]{:S(2)}, u32[]{:S(2)}) collective-permute-start(bf16[2,2,64,256]{3,2,1,0:T(8,128)(2,1)S(1)} %get-tuple-element.70.refs_2_), channel_id=1, source_target_pairs={{0,16},{8,24},{16,0},{24,8},{1,17},{9,25},{17,1},{25,9},{2,18},{10... | collective-permute-start | bytes 393224 | tf_op jit(solution)/shard_map/ppermute | solution.py:295
  59.0 9.9 %collective-permute-start.16 = (bf16[2,2,64,256]{3,2,1,0:T(8,128)(2,1)S(1)}, bf16[2,2,64,256]{3,2,1,0:T(8,128)(2,1)S(1)}, u32[]{:S(2)}, u32[]{:S(2)}) collective-permute-start(bf16[2,2,64,256]{3,2,1,0:T(8,128)(2,1)S(1)} %get-tuple-element.71.refs_3_), channel_id=1, source_target_pairs={{0,24},{8,16},{16,8},{24,0},{1,25},{9,17},{17,9},{25,1},{2,26},{10... | collective-permute-start | bytes 393224 | tf_op jit(solution)/shard_map/ppermute | solution.py:295
  59.2 9.7 %copy-start.13 = (f32[8]{0:T(128)S(1)}, f32[8]{0:T(128)}, u32[]{:S(2)}) copy-start(f32[8]{0:T(128)} %occ.9) | copy-start | bytes 100
  60.8 0.7 copy-start.18
  61.5 24.9 %collective-permute-start.20 = (bf16[2,2,64,256]{3,2,1,0:T(8,128)(2,1)S(1)}, bf16[2,2,64,256]{3,2,1,0:T(8,128)(2,1)S(1)}, u32[]{:S(2)}, u32[]{:S(2)}) collective-permute-start(bf16[2,2,64,256]{3,2,1,0:T(8,128)(2,1)S(1)} %get-tuple-element.78.refs_1_), channel_id=1, source_target_pairs={{0,8},{8,0},{16,24},{24,16},{1,9},{9,1},{17,25},{25,17},{2,10},{10... | collective-permute-start | bytes 393224 | tf_op jit(solution)/shard_map/ppermute | solution.py:295
  61.9 26.2 %collective-permute-start.21 = (bf16[2,2,64,256]{3,2,1,0:T(8,128)(2,1)S(1)}, bf16[2,2,64,256]{3,2,1,0:T(8,128)(2,1)S(1)}, u32[]{:S(2)}, u32[]{:S(2)}) collective-permute-start(bf16[2,2,64,256]{3,2,1,0:T(8,128)(2,1)S(1)} %get-tuple-element.79.refs_2_), channel_id=1, source_target_pairs={{0,16},{8,24},{16,0},{24,8},{1,17},{9,25},{17,1},{25,9},{2,18},{10... | collective-permute-start | bytes 393224 | tf_op jit(solution)/shard_map/ppermute | solution.py:295
  65.7 22.4 %collective-permute-start.22 = (bf16[2,2,64,256]{3,2,1,0:T(8,128)(2,1)S(1)}, bf16[2,2,64,256]{3,2,1,0:T(8,128)(2,1)S(1)}, u32[]{:S(2)}, u32[]{:S(2)}) collective-permute-start(bf16[2,2,64,256]{3,2,1,0:T(8,128)(2,1)S(1)} %get-tuple-element.80.refs_3_), channel_id=1, source_target_pairs={{0,24},{8,16},{16,8},{24,0},{1,25},{9,17},{17,9},{25,1},{2,26},{10... | collective-permute-start | bytes 393224 | tf_op jit(solution)/shard_map/ppermute | solution.py:295
  72.0 0.8 copy-start.16
  72.8 27.3 %collective-permute-start.26 = (bf16[2,2,64,256]{3,2,1,0:T(8,128)(2,1)S(1)}, bf16[2,2,64,256]{3,2,1,0:T(8,128)(2,1)S(1)}, u32[]{:S(2)}, u32[]{:S(2)}) collective-permute-start(bf16[2,2,64,256]{3,2,1,0:T(8,128)(2,1)S(1)} %get-tuple-element.90.refs_1_), channel_id=1, source_target_pairs={{0,8},{8,0},{16,24},{24,16},{1,9},{9,1},{17,25},{25,17},{2,10},{10... | collective-permute-start | bytes 393224 | tf_op jit(solution)/shard_map/ppermute | solution.py:295
  80.0 21.7 %collective-permute-start.27 = (bf16[2,2,64,256]{3,2,1,0:T(8,128)(2,1)S(1)}, bf16[2,2,64,256]{3,2,1,0:T(8,128)(2,1)S(1)}, u32[]{:S(2)}, u32[]{:S(2)}) collective-permute-start(bf16[2,2,64,256]{3,2,1,0:T(8,128)(2,1)S(1)} %get-tuple-element.91.refs_2_), channel_id=1, source_target_pairs={{0,16},{8,24},{16,0},{24,8},{1,17},{9,25},{17,1},{25,9},{2,18},{10... | collective-permute-start | bytes 393224 | tf_op jit(solution)/shard_map/ppermute | solution.py:295
  80.8 15.4 %all-to-all-start.1 = ((bf16[8,2,64,256]{3,2,1,0:T(8,128)(2,1)}), bf16[8,2,64,256]{3,2,1,0:T(8,128)(2,1)S(1)}, u32[]{:S(2)}, u32[]{:S(2)}) async-start(bf16[8,2,64,256]{3,2,1,0:T(8,128)(2,1)} %get-tuple-element.72), calls=%async_computation.1 | async-start | bytes 1048576 | tf_op jit(solution)/shard_map/all_to_all | solution.py:282
  86.4 15.3 %collective-permute-start.28 = (bf16[2,2,64,256]{3,2,1,0:T(8,128)(2,1)S(1)}, bf16[2,2,64,256]{3,2,1,0:T(8,128)(2,1)S(1)}, u32[]{:S(2)}, u32[]{:S(2)}) collective-permute-start(bf16[2,2,64,256]{3,2,1,0:T(8,128)(2,1)S(1)} %get-tuple-element.92.refs_3_), channel_id=1, source_target_pairs={{0,24},{8,16},{16,8},{24,0},{1,25},{9,17},{17,9},{25,1},{2,26},{10... | collective-permute-start | bytes 393224 | tf_op jit(solution)/shard_map/ppermute | solution.py:295
  88.1 0.9 copy-start.19
  92.0 12.1 %collective-permute-start.23 = (bf16[2,2,64,256]{3,2,1,0:T(8,128)(2,1)S(1)}, bf16[2,2,64,256]{3,2,1,0:T(8,128)(2,1)S(1)}, u32[]{:S(2)}, u32[]{:S(2)}) collective-permute-start(bf16[2,2,64,256]{3,2,1,0:T(8,128)(2,1)S(1)} %get-tuple-element.85.refs_1_), channel_id=1, source_target_pairs={{0,8},{8,0},{16,24},{24,16},{1,9},{9,1},{17,25},{25,17},{2,10},{10... | collective-permute-start | bytes 393224 | tf_op jit(solution)/shard_map/ppermute | solution.py:295
  93.2 10.9 %collective-permute-start.24 = (bf16[2,2,64,256]{3,2,1,0:T(8,128)(2,1)S(1)}, bf16[2,2,64,256]{3,2,1,0:T(8,128)(2,1)S(1)}, u32[]{:S(2)}, u32[]{:S(2)}) collective-permute-start(bf16[2,2,64,256]{3,2,1,0:T(8,128)(2,1)S(1)} %get-tuple-element.86.refs_2_), channel_id=1, source_target_pairs={{0,16},{8,24},{16,0},{24,8},{1,17},{9,25},{17,1},{25,9},{2,18},{10... | collective-permute-start | bytes 393224 | tf_op jit(solution)/shard_map/ppermute | solution.py:295
  96.2 22.7 %all-to-all-start.2 = ((bf16[8,2,64,256]{3,2,1,0:T(8,128)(2,1)}), bf16[8,2,64,256]{3,2,1,0:T(8,128)(2,1)S(1)}, u32[]{:S(2)}, u32[]{:S(2)}) async-start(bf16[8,2,64,256]{3,2,1,0:T(8,128)(2,1)} %get-tuple-element.82), calls=%async_computation.2 | async-start | bytes 1048576 | tf_op jit(solution)/shard_map/all_to_all | solution.py:282
  100.1 7.8 %collective-permute-start.25 = (bf16[2,2,64,256]{3,2,1,0:T(8,128)(2,1)S(1)}, bf16[2,2,64,256]{3,2,1,0:T(8,128)(2,1)S(1)}, u32[]{:S(2)}, u32[]{:S(2)}) collective-permute-start(bf16[2,2,64,256]{3,2,1,0:T(8,128)(2,1)S(1)} %get-tuple-element.87.refs_3_), channel_id=1, source_target_pairs={{0,24},{8,16},{16,8},{24,0},{1,25},{9,17},{17,9},{25,1},{2,26},{10... | collective-permute-start | bytes 393224 | tf_op jit(solution)/shard_map/ppermute | solution.py:295
  101.7 1.0 copy-start.17
  104.0 14.8 %copy-start.12 = (f32[512]{0:T(512)S(1)}, f32[512]{0:T(512)}, u32[]{:S(2)}) copy-start(f32[512]{0:T(512)} %param.11) | copy-start | bytes 6148
  104.1 14.9 %copy-start.2 = (bf16[3,64,512]{2,1,0:T(8,128)(2,1)S(1)}, bf16[3,64,512]{2,1,0:T(8,128)(2,1)}, u32[]{:S(2)}) copy-start(bf16[3,64,512]{2,1,0:T(8,128)(2,1)} %refs_0_.3) | copy-start | bytes 589828
  104.1 14.9 %copy-start.4 = (bf16[3,64,512]{2,1,0:T(8,128)(2,1)S(1)}, bf16[3,64,512]{2,1,0:T(8,128)(2,1)}, u32[]{:S(2)}) copy-start(bf16[3,64,512]{2,1,0:T(8,128)(2,1)} %copy-done.3) | copy-start | bytes 589828
  104.1 14.9 %copy-start.6 = (bf16[3,64,512]{2,1,0:T(8,128)(2,1)S(1)}, bf16[3,64,512]{2,1,0:T(8,128)(2,1)}, u32[]{:S(2)}) copy-start(bf16[3,64,512]{2,1,0:T(8,128)(2,1)} %copy-done.5) | copy-start | bytes 589828
  104.1 14.9 %copy-start.8 = (bf16[3,64,512]{2,1,0:T(8,128)(2,1)S(1)}, bf16[3,64,512]{2,1,0:T(8,128)(2,1)}, u32[]{:S(2)}) copy-start(bf16[3,64,512]{2,1,0:T(8,128)(2,1)} %copy-done.7) | copy-start | bytes 589828
  110.0 4.3 %collective-permute-start.29 = (bf16[2,128,256]{2,1,0:T(8,128)(2,1)S(1)}, bf16[2,128,256]{2,1,0:T(8,128)(2,1)S(1)}, u32[]{:S(2)}, u32[]{:S(2)}) collective-permute-start(bf16[2,128,256]{2,1,0:T(8,128)(2,1)S(1)} %get-tuple-element.94), channel_id=1, source_target_pairs={{0,1},{1,0},{2,3},{3,2},{4,5},{5,4},{6,7},{7,6},{8,9},{9,8},{10,11... | collective-permute-start | bytes 393224 | tf_op jit(solution)/shard_map/ppermute | solution.py:288
  110.0 7.1 %collective-permute-start.30 = (bf16[2,128,256]{2,1,0:T(8,128)(2,1)S(1)}, bf16[2,128,256]{2,1,0:T(8,128)(2,1)S(1)}, u32[]{:S(2)}, u32[]{:S(2)}) collective-permute-start(bf16[2,128,256]{2,1,0:T(8,128)(2,1)S(1)} %get-tuple-element.95), channel_id=1, source_target_pairs={{0,2},{1,3},{2,0},{3,1},{4,6},{5,7},{6,4},{7,5},{8,10},{9,11},{10,... | collective-permute-start | bytes 393224 | tf_op jit(solution)/shard_map/ppermute | solution.py:288
  111.7 17.0 %collective-permute-start.31 = (bf16[2,128,256]{2,1,0:T(8,128)(2,1)}, bf16[2,128,256]{2,1,0:T(8,128)(2,1)S(1)}, u32[]{:S(2)}, u32[]{:S(2)}) collective-permute-start(bf16[2,128,256]{2,1,0:T(8,128)(2,1)} %get-tuple-element.96), channel_id=1, source_target_pairs={{0,3},{1,2},{2,1},{3,0},{4,7},{5,6},{6,5},{7,4},{8,11},{9,10},{10,... | collective-permute-start | bytes 393224 | tf_op jit(solution)/shard_map/ppermute | solution.py:288
  111.9 16.8 %collective-permute-start.32 = (bf16[2,128,256]{2,1,0:T(8,128)(2,1)}, bf16[2,128,256]{2,1,0:T(8,128)(2,1)S(1)}, u32[]{:S(2)}, u32[]{:S(2)}) collective-permute-start(bf16[2,128,256]{2,1,0:T(8,128)(2,1)} %get-tuple-element.97), channel_id=1, source_target_pairs={{0,4},{1,5},{2,6},{3,7},{4,0},{5,1},{6,2},{7,3},{8,12},{9,13},{10,... | collective-permute-start | bytes 393224 | tf_op jit(solution)/shard_map/ppermute | solution.py:288
  114.3 14.4 %collective-permute-start.33 = (bf16[2,128,256]{2,1,0:T(8,128)(2,1)}, bf16[2,128,256]{2,1,0:T(8,128)(2,1)S(1)}, u32[]{:S(2)}, u32[]{:S(2)}) collective-permute-start(bf16[2,128,256]{2,1,0:T(8,128)(2,1)} %get-tuple-element.98), channel_id=1, source_target_pairs={{0,5},{1,4},{2,7},{3,6},{4,1},{5,0},{6,3},{7,2},{8,13},{9,12},{10,... | collective-permute-start | bytes 393224 | tf_op jit(solution)/shard_map/ppermute | solution.py:288
  114.3 14.4 %collective-permute-start.34 = (bf16[2,128,256]{2,1,0:T(8,128)(2,1)}, bf16[2,128,256]{2,1,0:T(8,128)(2,1)S(1)}, u32[]{:S(2)}, u32[]{:S(2)}) collective-permute-start(bf16[2,128,256]{2,1,0:T(8,128)(2,1)} %get-tuple-element.99), channel_id=1, source_target_pairs={{0,6},{1,7},{2,4},{3,5},{4,2},{5,3},{6,0},{7,1},{8,14},{9,15},{10,... | collective-permute-start | bytes 393224 | tf_op jit(solution)/shard_map/ppermute | solution.py:288
  117.1 11.6 %collective-permute-start.35 = (bf16[2,128,256]{2,1,0:T(8,128)(2,1)S(1)}, bf16[2,128,256]{2,1,0:T(8,128)(2,1)S(1)}, u32[]{:S(2)}, u32[]{:S(2)}) collective-permute-start(bf16[2,128,256]{2,1,0:T(8,128)(2,1)S(1)} %get-tuple-element.100), channel_id=1, source_target_pairs={{0,7},{1,6},{2,5},{3,4},{4,3},{5,2},{6,1},{7,0},{8,15},{9,14},{10,... | collective-permute-start | bytes 393224 | tf_op jit(solution)/shard_map/ppermute | solution.py:288
  119.0 1.1 copy-start.15

commit v11 on v8

--- a/solution.py
+++ b/solution.py
@@ -63,15 +63,15 @@
         out[d, pair, c * g:(c + 1) * g, e:] = tile[g:]
 
 
-def unpack_pair(tiles, chunks, pair, put):
-    e = tiles.edge
+def unpack_pair(tiles, blocks, pair, put):
+    e, g = tiles.edge, tiles.rows
     for d, (a, b) in enumerate(tiles.above):
-        block = jnp.concatenate([chunk[d, pair] for chunk in chunks], axis=0).astype(WIDE)
-        put(a, b, block[:, :e])
-        put(b, a, block[:, e:].T)
+        put(a, b, blocks[d, pair, :, :e].astype(WIDE))
+        put(b, a, blocks[d, pair, :, e:].astype(WIDE).T)
     for d, c, k in tiles.diagonal:
-        block = chunks[c][d, pair].astype(WIDE)
-        put(k, k, jnp.concatenate([block[:, :e], block[:, e:]], axis=0))
+        upper = blocks[d, pair, c * g:(c + 1) * g, :e]
+        lower = blocks[d, pair, c * g:(c + 1) * g, e:]
+        put(k, k, jnp.concatenate([upper, lower], axis=0).astype(WIDE))
 
 
 def to_distances(place, whole, outs):
@@ -137,7 +137,7 @@
         pack_pair(tiles, total, out, pair)
 
 
-def second_ladder_kernel(tiles, order, place, occ, source, upper, lower, row, column, *refs):
+def second_ladder_kernel(tiles, order, place, occ, source, blocks, row, column, *refs):
     pieces, (out, whole, inner, total, matrix) = refs[:-5], refs[-5:]
     assemble(place, order, pieces, whole)
     count = source.shape[0]
@@ -145,7 +145,7 @@
         def put(a, b, tile):
             matrix[tiles.span(a), tiles.span(b)] = tile.astype(NARROW)
 
-        unpack_pair(tiles, (upper, lower), pair, put)
+        unpack_pair(tiles, blocks, pair, put)
         ladder_pair(matrix[...], whole, inner, total)
         base = occ[place[0] * count + pair] + occ[place[1]]
         strip = math.gcd(64, total.shape[0])
@@ -169,7 +169,7 @@
         here = (0, tiles.span(a), tiles.span(b))
         out[here] = source[here] + tile
 
-    unpack_pair(tiles, [whole.at[:, :, :tiles.rows], whole.at[:, :, tiles.rows:]], 0, put)
+    unpack_pair(tiles, whole, 0, put)
 
 
 def mix(place, fock, first, load, store, rows):
@@ -219,11 +219,14 @@
 
 
 def update_kernel(tiles, groups, first, chunk, place, fock, occ, sums, *refs):
+    before, refs = refs[:chunk], refs[chunk:]
     own, other = refs[:groups], refs[groups:2 * groups]
     sent, rest = refs[2 * groups:2 * groups + 2]
     out = refs[2 * groups + 2:3 * groups + 2]
     update = refs[3 * groups + 2]
     here = slice(chunk * tiles.rows, (chunk + 1) * tiles.rows)
+    for ref in before:
+        sent[:, :, :tiles.rows, :] = ref[...]
 
     def one(step, carry):
         u, w = step // first, lax.rem(step, first)
@@ -235,7 +238,7 @@
                 value = (own[s][u, w].astype(WIDE) + mirrored) * inverse(base - sums[here])
                 narrow = value.astype(NARROW)
                 update[u, s * first + w] = value
-                sent[column, u] = narrow
+                sent[column, u, here] = narrow
                 rest[u, s * first + w] = (2.0 * (value - narrow.astype(WIDE))).astype(NARROW)
 
             with_mirror(tiles, place, other[s][w, u].astype(WIDE), finish)
@@ -285,9 +288,8 @@
 def by_distance(parts):
     devices = len(parts)
     return [parts[0]] + [
-        lax.ppermute(parts[k], "occj", [(d, d ^ k) for d in range(devices)])
-        for k in range(devices - 1, 0, -1)
-    ][::-1]
+        lax.ppermute(parts[k], "occj", [(d, d ^ k) for d in range(devices)]) for k in range(1, devices)
+    ]
 
 
 def across_first(parts, groups):
@@ -364,7 +366,7 @@
         tie(place, ladder), *held, specs=[SMEM] + [VMEM] * devices,
     )
     mirror = [across_first(parts[c * groups:(c + 1) * groups], groups) for c in chunks]
-    ladder = exchange(ladder)
+    ladder = exchange(tie(ladder, *held))
 
     half, other = [], []
     for c in chunks:
@@ -374,31 +376,31 @@
             specs=[SMEM] * 2 + [VMEM] * (groups + 1),
         ))
         other.append(across_first(half[c], groups))
-    back, rest, mixed = [], [], []
+    sent, rest, mixed = [], [], []
     for c in chunks:
-        sent, rest_one, *mixed_one = call(
+        sent_one, rest_one, *mixed_one = call(
             functools.partial(update_kernel, tiles, groups, first, c),
-            [upper, jax.ShapeDtypeStruct((first, devices, *part.shape[2:]), NARROW)] + [part] * groups,
+            [(upper, packed)[c], jax.ShapeDtypeStruct((first, devices, *part.shape[2:]), NARROW)] + [part] * groups,
             [pltpu.VMEM((first, devices, *part.shape[2:]), WIDE)],
-            LONG, 10 * count, place, fock, occ_energy, sums, *half[c], *other[c],
-            specs=[SMEM] * 3 + [VMEM] * (2 * groups + 1),
+            LONG, 10 * count, place, fock, occ_energy, sums, *sent, *half[c], *other[c],
+            specs=[SMEM] * 3 + [VMEM] * (2 * groups + 1 + c),
         )
-        back.append(exchange(tie(sent, *back)))
-        rest, mixed = rest + [rest_one], mixed + [mixed_one]
+        sent, rest, mixed = [sent_one], rest + [rest_one], mixed + [mixed_one]
     other = [across_first(x, groups) for x in mixed]
+    back = exchange(sent[0])
     base = call(
         functools.partial(second_ladder_kernel, tiles, order), jax.ShapeDtypeStruct(current.shape, WIDE),
         [whole, inner, square, pltpu.VMEM((virtual, virtual), NARROW)],
-        ladder_flops, 12 * count, place, occ_energy, current, *back,
+        ladder_flops, 12 * count, place, occ_energy, current, back,
         jnp.broadcast_to(vir_energy[:, None], (virtual, 128)), vir_energy[None, :], *pieces,
-        specs=[SMEM] * 2 + [VMEM] * (5 + len(pieces)),
+        specs=[SMEM] * 2 + [VMEM] * (4 + len(pieces)),
     )
     last = []
     for c in chunks:
         last = call(
             functools.partial(rest_kernel, tiles, groups, first, c),
             [distant] * devices if c else [upper], [blocks] if c else [],
-            LONG, 8 * count, place, occ_energy, sums, rest[c], *mixed[c], *other[c], *last,
+            2 * count if c else LONG, 8 * count, place, occ_energy, sums, rest[c], *mixed[c], *other[c], *last,
             specs=[SMEM] * 2 + [VMEM] * (2 * groups + 2 + c),
         )
     def by_pair(*shape):

time: 162 us -> 134 us (0.83)
  waiting for transfers between devices: 35.2 us -> 18.4 us
  local copies, waits for them, and re-layouts: 11.9 us -> 6.24 us
  starting transfers between devices: 79.6 us -> 74 us
    ppermute x14, waiting for transfers between devices: 16.1 us -> 2.57 us  [by_distance(): lax.ppermute(parts[k], 'occj', [(d, d ^ k) for d in range(devices)])]
    all_to_all x3 -> x2, waiting for transfers between devices: 6.92 us -> 0.01 us  [exchange(): lax.all_to_all(blocks, 'occj', split_axis=0, concat_axis=0, tiled=True)]
    unnamed x54 -> x42, local copies, waits for them, and re-layouts: 10.3 us -> 4.63 us
    all_to_all x3 -> x2, starting transfers between devices: 14.1 us -> 9.82 us  [exchange(): lax.all_to_all(blocks, 'occj', split_axis=0, concat_axis=0, tiled=True)]
    ppermute x18, waiting for transfers between devices: 5.44 us -> 9.07 us  [across_first(): lax.ppermute(parts[s], 'occi', [(k, k ^ s) for k in range(groups)])]
  transfers between devices with their start and end apart: 39 -> 38, of which waited for: 6 -> 7; matrix products, arithmetic and copies ran while one was open for 1% -> 1% of each run, Pallas kernels for 18% -> 22%
where the time goes in v11:
time: 134 us; the launch traced here: 133 us
  starting transfers between devices  74 us (55%)
  Pallas kernels  31.5 us (24%)
  waiting for transfers between devices  18.4 us (14%)
  local copies, waits for them, and re-layouts  6.24 us (5%)
  between operations  1.62 us (1%)
    ppermute x18, starting transfers between devices, across_first(): lax.ppermute(parts[s], 'occi', [(k, k ^ s) for k in range(groups)])  44.1 us
    pallas_call x10, Pallas kernels, call(): pl.pallas_call(body, out_shape=outs, in_specs=specs, out_specs=jax.tree.m...  28.7 us
    ppermute x14, starting transfers between devices, by_distance(): lax.ppermute(parts[k], 'occj', [(d, d ^ k) for d in range(devices)])  15.5 us
    all_to_all x2, starting transfers between devices, exchange(): lax.all_to_all(blocks, 'occj', split_axis=0, concat_axis=0, tiled=True)  9.82 us
    ppermute x18, waiting for transfers between devices, across_first(): lax.ppermute(parts[s], 'occi', [(k, k ^ s) for k in range(groups)])  9.07 us
    ppermute x4, waiting for transfers between devices, turn(): return lax.ppermute(x, 'occj', [(d, d ^ k) for d in range(devices)])  6.71 us
    unnamed x42, local copies, waits for them, and re-layouts  4.63 us
    ppermute x4, starting transfers between devices, turn(): return lax.ppermute(x, 'occj', [(d, d ^ k) for d in range(devices)])  4.55 us
  transfers between devices with their start and end apart: 38, of which 7 were waited for; matrix products, arithmetic and copies ran while one was open for 1% of the time, Pallas kernels for 22%

profile of v11, /device:TPU:0, one launch (start us, length us, event | category | flops | bytes accessed | tf_op | source)
XLA Modules:
  0.0 133.0 jit_solution(5035900506500138467)
XLA Ops:
  0.0 3.0 %collective-permute-start = (bf16[3,64,512]{2,1,0:T(8,128)(2,1)}, bf16[3,64,512]{2,1,0:T(8,128)(2,1)S(1)}, u32[]{:S(2)}, u32[]{:S(2)}) collective-permute-start(bf16[3,64,512]{2,1,0:T(8,128)(2,1)} %refs_0_.3), channel_id=1, source_target_pairs={{0,2},{1,3},{2,0},{3,1},{4,6},{5,7},{6,4},{7,5},{8,10},{9,11},{10,... | collective-permute-start | bytes 589832 | tf_op jit(solution)/shard_map/ppermute | solution.py:308
  3.0 1.5 %collective-permute-start.1 = (bf16[3,64,512]{2,1,0:T(8,128)(2,1)}, bf16[3,64,512]{2,1,0:T(8,128)(2,1)S(1)}, u32[]{:S(2)}, u32[]{:S(2)}) collective-permute-start(bf16[3,64,512]{2,1,0:T(8,128)(2,1)} %refs_0_.3), channel_id=1, source_target_pairs={{0,4},{1,5},{2,6},{3,7},{4,0},{5,1},{6,2},{7,3},{8,12},{9,13},{10,... | collective-permute-start | bytes 589832 | tf_op jit(solution)/shard_map/ppermute | solution.py:308
  4.6 0.1 pad_add_fusion.place
  4.6 1.6 %copy-done = f32[2,1,512,512]{3,2,1,0:T(8,128)S(1)} copy-done((f32[2,1,512,512]{3,2,1,0:T(8,128)S(1)}, f32[2,1,512,512]{3,2,1,0:T(8,128)}, u32[]{:S(2)}) %copy-start) | copy-done | bytes 2097176
  6.2 0.9 shard_map.73
  7.1 1.9 %collective-permute-done.refs_1_ = bf16[3,64,512]{2,1,0:T(8,128)(2,1)S(1)} collective-permute-done((bf16[3,64,512]{2,1,0:T(8,128)(2,1)}, bf16[3,64,512]{2,1,0:T(8,128)(2,1)S(1)}, u32[]{:S(2)}, u32[]{:S(2)}) %collective-permute-start) | collective-permute-done | bytes 196640 | tf_op jit(solution)/shard_map/ppermute | solution.py:308
  9.0 4.8 %collective-permute-done.1.refs_2_ = bf16[3,64,512]{2,1,0:T(8,128)(2,1)S(1)} collective-permute-done((bf16[3,64,512]{2,1,0:T(8,128)(2,1)}, bf16[3,64,512]{2,1,0:T(8,128)(2,1)S(1)}, u32[]{:S(2)}, u32[]{:S(2)}) %collective-permute-start.1) | collective-permute-done | bytes 196640 | tf_op jit(solution)/shard_map/ppermute | solution.py:308
  13.8 1.0 pad_maximum_fusion
  14.8 1.6 %collective-permute-start.10 = (bf16[2,128,256]{2,1,0:T(8,128)(2,1)S(1)}, bf16[2,128,256]{2,1,0:T(8,128)(2,1)S(1)}, u32[]{:S(2)}, u32[]{:S(2)}) collective-permute-start(bf16[2,128,256]{2,1,0:T(8,128)(2,1)S(1)} %get-tuple-element.60), channel_id=1, source_target_pairs={{0,7},{1,6},{2,5},{3,4},{4,3},{5,2},{6,1},{7,0},{8,15},{9,14},{10,... | collective-permute-start | bytes 393224 | tf_op jit(solution)/shard_map/ppermute | solution.py:291
  16.4 1.5 %collective-permute-start.5 = (bf16[2,128,256]{2,1,0:T(8,128)(2,1)S(1)}, bf16[2,128,256]{2,1,0:T(8,128)(2,1)S(1)}, u32[]{:S(2)}, u32[]{:S(2)}) collective-permute-start(bf16[2,128,256]{2,1,0:T(8,128)(2,1)S(1)} %get-tuple-element.55), channel_id=1, source_target_pairs={{0,2},{1,3},{2,0},{3,1},{4,6},{5,7},{6,4},{7,5},{8,10},{9,11},{10,... | collective-permute-start | bytes 393224 | tf_op jit(solution)/shard_map/ppermute | solution.py:291
  17.9 0.4 collective-permute-start.6
  18.3 0.6 dynamic_slice.14
  19.5 0.7 dynamic_slice.12
  20.8 0.1 fusion
  20.9 1.5 %collective-permute-start.7 = (bf16[2,128,256]{2,1,0:T(8,128)(2,1)S(1)}, bf16[2,128,256]{2,1,0:T(8,128)(2,1)S(1)}, u32[]{:S(2)}, u32[]{:S(2)}) collective-permute-start(bf16[2,128,256]{2,1,0:T(8,128)(2,1)S(1)} %get-tuple-element.57), channel_id=1, source_target_pairs={{0,4},{1,5},{2,6},{3,7},{4,0},{5,1},{6,2},{7,3},{8,12},{9,13},{10,... | collective-permute-start | bytes 393224 | tf_op jit(solution)/shard_map/ppermute | solution.py:291
  22.4 0.9 collective-permute-start.8
  23.3 1.5 %collective-permute-start.9 = (bf16[2,128,256]{2,1,0:T(8,128)(2,1)S(1)}, bf16[2,128,256]{2,1,0:T(8,128)(2,1)S(1)}, u32[]{:S(2)}, u32[]{:S(2)}) collective-permute-start(bf16[2,128,256]{2,1,0:T(8,128)(2,1)S(1)} %get-tuple-element.59), channel_id=1, source_target_pairs={{0,6},{1,7},{2,4},{3,5},{4,2},{5,3},{6,0},{7,1},{8,14},{9,15},{10,... | collective-permute-start | bytes 393224 | tf_op jit(solution)/shard_map/ppermute | solution.py:291
  24.8 6.2 %shard_map.74 = bf16[8,2,128,256]{3,2,1,0:T(8,128)(2,1)} custom-call(s32[2]{0:T(128)S(1)} %pad_add_fusion.place, f32[2,512,512]{2,1,0:T(8,128)} %bitcast.13, bf16[3,64,512]{2,1,0:T(8,128)(2,1)S(1)} %copy-done.1, bf16[3,64,512]{2,1,0:T(8,128)(2,1)S(1)} %collective-permute-done.refs_1_, bf16[3,64,512]{2,1,0:T(8,128)(2,1)S(1)} %collective-permute-done.1.refs_2_, ...), custom_call_target="tpu_custom_call" | custom-call | flops 3221225472 | bytes 4194304 | tf_op jit(solution)/shard_map/pallas_call | solution.py:42
  31.1 1.8 %collective-permute-done.8.refs_5_ = bf16[2,128,256]{2,1,0:T(8,128)(2,1)S(1)} collective-permute-done((bf16[2,128,256]{2,1,0:T(8,128)(2,1)S(1)}, bf16[2,128,256]{2,1,0:T(8,128)(2,1)S(1)}, u32[]{:S(2)}, u32[]{:S(2)}) %collective-permute-start.8) | collective-permute-done | bytes 131104 | tf_op jit(solution)/shard_map/ppermute | solution.py:291
  32.9 3.6 %all-to-all-start = ((bf16[8,2,128,256]{3,2,1,0:T(8,128)(2,1)}), bf16[8,2,128,256]{3,2,1,0:T(8,128)(2,1)S(1)}, u32[]{:S(2)}, u32[]{:S(2)}) async-start(bf16[8,2,128,256]{3,2,1,0:T(8,128)(2,1)} %shard_map.74), calls=%async_computation | async-start | bytes 2097152 | tf_op jit(solution)/shard_map/all_to_all | solution.py:285
  36.5 0.1 fusion.1
  36.6 0.1 broadcast_add_fusion.2
  36.7 0.7 shard_map.75
  37.4 1.6 %collective-permute-start.11 = (bf16[2,2,64,256]{3,2,1,0:T(8,128)(2,1)S(1)}, bf16[2,2,64,256]{3,2,1,0:T(8,128)(2,1)S(1)}, u32[]{:S(2)}, u32[]{:S(2)}) collective-permute-start(bf16[2,2,64,256]{3,2,1,0:T(8,128)(2,1)S(1)} %get-tuple-element.64), channel_id=1, source_target_pairs={{0,8},{8,0},{16,24},{24,16},{1,9},{9,1},{17,25},{25,17},{2,10},{10... | collective-permute-start | bytes 393224 | tf_op jit(solution)/shard_map/ppermute | solution.py:297
  39.1 2.6 %collective-permute-start.12 = (bf16[2,2,64,256]{3,2,1,0:T(8,128)(2,1)S(1)}, bf16[2,2,64,256]{3,2,1,0:T(8,128)(2,1)S(1)}, u32[]{:S(2)}, u32[]{:S(2)}) collective-permute-start(bf16[2,2,64,256]{3,2,1,0:T(8,128)(2,1)S(1)} %get-tuple-element.65), channel_id=1, source_target_pairs={{0,16},{8,24},{16,0},{24,8},{1,17},{9,25},{17,1},{25,9},{2,18},{10... | collective-permute-start | bytes 393224 | tf_op jit(solution)/shard_map/ppermute | solution.py:297
  41.7 0.2 collective-permute-start.13
  41.9 0.1 broadcast_add_fusion
  42.0 0.7 collective-permute-start.17
  42.8 3.5 %collective-permute-start.18 = (bf16[2,2,64,256]{3,2,1,0:T(8,128)(2,1)S(1)}, bf16[2,2,64,256]{3,2,1,0:T(8,128)(2,1)S(1)}, u32[]{:S(2)}, u32[]{:S(2)}) collective-permute-start(bf16[2,2,64,256]{3,2,1,0:T(8,128)(2,1)S(1)} %get-tuple-element.74), channel_id=1, source_target_pairs={{0,16},{8,24},{16,0},{24,8},{1,17},{9,25},{17,1},{25,9},{2,18},{10... | collective-permute-start | bytes 393224 | tf_op jit(solution)/shard_map/ppermute | solution.py:297
  46.3 2.7 %collective-permute-start.19 = (bf16[2,2,64,256]{3,2,1,0:T(8,128)(2,1)S(1)}, bf16[2,2,64,256]{3,2,1,0:T(8,128)(2,1)S(1)}, u32[]{:S(2)}, u32[]{:S(2)}) collective-permute-start(bf16[2,2,64,256]{3,2,1,0:T(8,128)(2,1)S(1)} %get-tuple-element.75), channel_id=1, source_target_pairs={{0,24},{8,16},{16,8},{24,0},{1,25},{9,17},{17,9},{25,1},{2,26},{10... | collective-permute-start | bytes 393224 | tf_op jit(solution)/shard_map/ppermute | solution.py:297
  49.0 3.1 %collective-permute-done.12.refs_2_ = bf16[2,2,64,256]{3,2,1,0:T(8,128)(2,1)S(1)} collective-permute-done((bf16[2,2,64,256]{3,2,1,0:T(8,128)(2,1)S(1)}, bf16[2,2,64,256]{3,2,1,0:T(8,128)(2,1)S(1)}, u32[]{:S(2)}, u32[]{:S(2)}) %collective-permute-start.12) | collective-permute-done | bytes 131104 | tf_op jit(solution)/shard_map/ppermute | solution.py:297
  52.0 1.6 %shard_map.76 = (bf16[2,2,64,256]{3,2,1,0:T(8,128)(2,1)S(1)}, bf16[2,2,64,256]{3,2,1,0:T(8,128)(2,1)S(1)}, bf16[2,2,64,256]{3,2,1,0:T(8,128)(2,1)S(1)}, bf16[2,2,64,256]{3,2,1,0:T(8,128)(2,1)S(1)}) custom-call(s32[2]{0:T(128)S(1)} %pad_add_fusion.place, f32[8,8]{1,0:T(8,128)S(1)} %convert_element_type.3.fock, ...), custom_call_target="tpu_custom_call" | custom-call | flops 30000001024 | bytes 3145728 | tf_op jit(solution)/shard_map/pallas_call | solution.py:42
  53.6 9.1 %collective-permute-start.14 = (bf16[2,2,64,256]{3,2,1,0:T(8,128)(2,1)S(1)}, bf16[2,2,64,256]{3,2,1,0:T(8,128)(2,1)S(1)}, u32[]{:S(2)}, u32[]{:S(2)}) collective-permute-start(bf16[2,2,64,256]{3,2,1,0:T(8,128)(2,1)S(1)} %get-tuple-element.68.refs_1_), channel_id=1, source_target_pairs={{0,8},{8,0},{16,24},{24,16},{1,9},{9,1},{17,25},{25,17},{2,10},{10... | collective-permute-start | bytes 393224 | tf_op jit(solution)/shard_map/ppermute | solution.py:297
  62.6 1.1 collective-permute-start.15
  63.7 1.4 %collective-permute-start.16 = (bf16[2,2,64,256]{3,2,1,0:T(8,128)(2,1)S(1)}, bf16[2,2,64,256]{3,2,1,0:T(8,128)(2,1)S(1)}, u32[]{:S(2)}, u32[]{:S(2)}) collective-permute-start(bf16[2,2,64,256]{3,2,1,0:T(8,128)(2,1)S(1)} %get-tuple-element.70.refs_3_), channel_id=1, source_target_pairs={{0,24},{8,16},{16,8},{24,0},{1,25},{9,17},{17,9},{25,1},{2,26},{10... | collective-permute-start | bytes 393224 | tf_op jit(solution)/shard_map/ppermute | solution.py:297
  65.1 1.6 %shard_map.78 = (bf16[2,2,64,256]{3,2,1,0:T(8,128)(2,1)S(1)}, bf16[2,2,64,256]{3,2,1,0:T(8,128)(2,1)S(1)}, bf16[2,2,64,256]{3,2,1,0:T(8,128)(2,1)S(1)}, bf16[2,2,64,256]{3,2,1,0:T(8,128)(2,1)S(1)}) custom-call(s32[2]{0:T(128)S(1)} %pad_add_fusion.place, f32[8,8]{1,0:T(8,128)S(1)} %convert_element_type.3.fock, ...), custom_call_target="tpu_custom_call" | custom-call | flops 30000001024 | bytes 3145728 | tf_op jit(solution)/shard_map/pallas_call | solution.py:42
  66.7 3.8 %collective-permute-start.20 = (bf16[2,2,64,256]{3,2,1,0:T(8,128)(2,1)S(1)}, bf16[2,2,64,256]{3,2,1,0:T(8,128)(2,1)S(1)}, u32[]{:S(2)}, u32[]{:S(2)}) collective-permute-start(bf16[2,2,64,256]{3,2,1,0:T(8,128)(2,1)S(1)} %get-tuple-element.77.refs_2_), channel_id=1, source_target_pairs={{0,8},{8,0},{16,24},{24,16},{1,9},{9,1},{17,25},{25,17},{2,10},{10... | collective-permute-start | bytes 393224 | tf_op jit(solution)/shard_map/ppermute | solution.py:297
  70.5 2.5 %collective-permute-start.21 = (bf16[2,2,64,256]{3,2,1,0:T(8,128)(2,1)S(1)}, bf16[2,2,64,256]{3,2,1,0:T(8,128)(2,1)S(1)}, u32[]{:S(2)}, u32[]{:S(2)}) collective-permute-start(bf16[2,2,64,256]{3,2,1,0:T(8,128)(2,1)S(1)} %get-tuple-element.78.refs_3_), channel_id=1, source_target_pairs={{0,16},{8,24},{16,0},{24,8},{1,17},{9,25},{17,1},{25,9},{2,18},{10... | collective-permute-start | bytes 393224 | tf_op jit(solution)/shard_map/ppermute | solution.py:297
  73.0 1.4 %collective-permute-start.22 = (bf16[2,2,64,256]{3,2,1,0:T(8,128)(2,1)S(1)}, bf16[2,2,64,256]{3,2,1,0:T(8,128)(2,1)S(1)}, u32[]{:S(2)}, u32[]{:S(2)}) collective-permute-start(bf16[2,2,64,256]{3,2,1,0:T(8,128)(2,1)S(1)} %get-tuple-element.79.refs_4_), channel_id=1, source_target_pairs={{0,24},{8,16},{16,8},{24,0},{1,25},{9,17},{17,9},{25,1},{2,26},{10... | collective-permute-start | bytes 393224 | tf_op jit(solution)/shard_map/ppermute | solution.py:297
  74.4 2.5 %collective-permute-done.15.refs_6_ = bf16[2,2,64,256]{3,2,1,0:T(8,128)(2,1)S(1)} collective-permute-done((bf16[2,2,64,256]{3,2,1,0:T(8,128)(2,1)S(1)}, bf16[2,2,64,256]{3,2,1,0:T(8,128)(2,1)S(1)}, u32[]{:S(2)}, u32[]{:S(2)}) %collective-permute-start.15) | collective-permute-done | bytes 131104 | tf_op jit(solution)/shard_map/ppermute | solution.py:297
  76.9 2.2 %shard_map.77 = (bf16[8,2,64,256]{3,2,1,0:T(8,128)(2,1)S(1)}, bf16[2,8,64,256]{3,2,1,0:T(8,128)(2,1)S(1)}, bf16[2,2,64,256]{3,2,1,0:T(8,128)(2,1)S(1)}, bf16[2,2...) custom-call(s32[2]{0:T(128)S(1)} %pad_add_fusion.place, ...), custom_call_target="tpu_custom_call" | custom-call | flops 30000001024 | bytes 5242880 | tf_op jit(solution)/shard_map/pallas_call | solution.py:42
  79.1 0.8 copy-done.14
  79.9 6.7 %collective-permute-start.26 = (bf16[2,2,64,256]{3,2,1,0:T(8,128)(2,1)S(1)}, bf16[2,2,64,256]{3,2,1,0:T(8,128)(2,1)S(1)}, u32[]{:S(2)}, u32[]{:S(2)}) collective-permute-start(bf16[2,2,64,256]{3,2,1,0:T(8,128)(2,1)S(1)} %get-tuple-element.88.refs_1_), channel_id=1, source_target_pairs={{0,8},{8,0},{16,24},{24,16},{1,9},{9,1},{17,25},{25,17},{2,10},{10... | collective-permute-start | bytes 393224 | tf_op jit(solution)/shard_map/ppermute | solution.py:297
  86.6 1.0 collective-permute-start.27
  87.6 1.5 %collective-permute-start.28 = (bf16[2,2,64,256]{3,2,1,0:T(8,128)(2,1)S(1)}, bf16[2,2,64,256]{3,2,1,0:T(8,128)(2,1)}, u32[]{:S(2)}, u32[]{:S(2)}) collective-permute-start(bf16[2,2,64,256]{3,2,1,0:T(8,128)(2,1)S(1)} %get-tuple-element.90.refs_3_), channel_id=1, source_target_pairs={{0,24},{8,16},{16,8},{24,0},{1,25},{9,17},{17,9},{25,1},{2,26},{10... | collective-permute-start | bytes 393224 | tf_op jit(solution)/shard_map/ppermute | solution.py:297
  89.0 3.2 %shard_map.79 = (bf16[8,2,128,256]{3,2,1,0:T(8,128)(2,1)}, bf16[2,8,64,256]{3,2,1,0:T(8,128)(2,1)S(1)}, bf16[2,2,64,256]{3,2,1,0:T(8,128)(2,1)S(1)}, bf16[2,2,64...) custom-call(s32[2]{0:T(128)S(1)} %pad_add_fusion.place, ...), custom_call_target="tpu_custom_call" | custom-call | flops 30000001024 | bytes 5242880 | tf_op jit(solution)/shard_map/pallas_call | solution.py:42
  92.3 1.1 collective-permute-start.23
  93.3 1.9 %collective-permute-start.24 = (bf16[2,2,64,256]{3,2,1,0:T(8,128)(2,1)S(1)}, bf16[2,2,64,256]{3,2,1,0:T(8,128)(2,1)S(1)}, u32[]{:S(2)}, u32[]{:S(2)}) collective-permute-start(bf16[2,2,64,256]{3,2,1,0:T(8,128)(2,1)S(1)} %get-tuple-element.84.refs_2_), channel_id=1, source_target_pairs={{0,16},{8,24},{16,0},{24,8},{1,17},{9,25},{17,1},{25,9},{2,18},{10... | collective-permute-start | bytes 393224 | tf_op jit(solution)/shard_map/ppermute | solution.py:297
  95.2 6.3 %all-to-all-start.1 = ((bf16[8,2,128,256]{3,2,1,0:T(8,128)(2,1)}), bf16[8,2,128,256]{3,2,1,0:T(8,128)(2,1)S(1)}, u32[]{:S(2)}, u32[]{:S(2)}) async-start(bf16[8,2,128,256]{3,2,1,0:T(8,128)(2,1)} %get-tuple-element.80), calls=%async_computation.1 | async-start | bytes 2097152 | tf_op jit(solution)/shard_map/all_to_all | solution.py:285
  101.5 1.5 %collective-permute-start.25 = (bf16[2,2,64,256]{3,2,1,0:T(8,128)(2,1)S(1)}, bf16[2,2,64,256]{3,2,1,0:T(8,128)(2,1)S(1)}, u32[]{:S(2)}, u32[]{:S(2)}) collective-permute-start(bf16[2,2,64,256]{3,2,1,0:T(8,128)(2,1)S(1)} %get-tuple-element.85.refs_3_), channel_id=1, source_target_pairs={{0,24},{8,16},{16,8},{24,0},{1,25},{9,17},{17,9},{25,1},{2,26},{10... | collective-permute-start | bytes 393224 | tf_op jit(solution)/shard_map/ppermute | solution.py:297
  103.0 1.0 copy-done.15
  104.1 1.6 %shard_map.81.refs_8_ = bf16[8,2,64,256]{3,2,1,0:T(8,128)(2,1)S(1)} custom-call(s32[2]{0:T(128)S(1)} %pad_add_fusion.place, f32[8]{0:T(128)S(1)} %copy-done.11, f32[128,256]{1,0:T(8,128)S(1)} %maximum_select_fusion.sums, bf16[2,8,64,256]{3,2,1,0:T(8,128)(2,1)S(1)} %copy-done.15, bf16[2,2,64,256]{3,2,1,0:T(8,128)(2,1)S(1)} %copy-done.17, ...), custom_call_target="tpu_custom_call" | custom-call | flops 30000001024 | bytes 4194304 | tf_op jit(solution)/shard_map/pallas_call | solution.py:42
  105.8 3.5 %collective-permute-done.25.refs_7_ = bf16[2,2,64,256]{3,2,1,0:T(8,128)(2,1)S(1)} collective-permute-done((bf16[2,2,64,256]{3,2,1,0:T(8,128)(2,1)S(1)}, bf16[2,2,64,256]{3,2,1,0:T(8,128)(2,1)S(1)}, u32[]{:S(2)}, u32[]{:S(2)}) %collective-permute-start.25) | collective-permute-done | bytes 131104 | tf_op jit(solution)/shard_map/ppermute | solution.py:297
  109.3 2.1 %shard_map.82 = (bf16[2,128,256]{2,1,0:T(8,128)(2,1)S(1)}, bf16[2,128,256]{2,1,0:T(8,128)(2,1)S(1)}, bf16[2,128,256]{2,1,0:T(8,128)(2,1)S(1)}, bf16[2,128,256]{2...) custom-call(s32[2]{0:T(128)S(1)} %pad_add_fusion.place, ...), custom_call_target="tpu_custom_call" | custom-call | flops 1048576 | bytes 4194304 | tf_op jit(solution)/shard_map/pallas_call | solution.py:42
  111.4 1.7 %collective-permute-start.30 = (bf16[2,128,256]{2,1,0:T(8,128)(2,1)S(1)}, bf16[2,128,256]{2,1,0:T(8,128)(2,1)S(1)}, u32[]{:S(2)}, u32[]{:S(2)}) collective-permute-start(bf16[2,128,256]{2,1,0:T(8,128)(2,1)S(1)} %get-tuple-element.93), channel_id=1, source_target_pairs={{0,2},{1,3},{2,0},{3,1},{4,6},{5,7},{6,4},{7,5},{8,10},{9,11},{10,... | collective-permute-start | bytes 393224 | tf_op jit(solution)/shard_map/ppermute | solution.py:291
  113.1 0.2 collective-permute-start.31
  113.3 2.4 %collective-permute-start.32 = (bf16[2,128,256]{2,1,0:T(8,128)(2,1)}, bf16[2,128,256]{2,1,0:T(8,128)(2,1)S(1)}, u32[]{:S(2)}, u32[]{:S(2)}) collective-permute-start(bf16[2,128,256]{2,1,0:T(8,128)(2,1)} %get-tuple-element.95), channel_id=1, source_target_pairs={{0,4},{1,5},{2,6},{3,7},{4,0},{5,1},{6,2},{7,3},{8,12},{9,13},{10,... | collective-permute-start | bytes 393224 | tf_op jit(solution)/shard_map/ppermute | solution.py:291
  115.8 2.8 %collective-permute-start.34 = (bf16[2,128,256]{2,1,0:T(8,128)(2,1)}, bf16[2,128,256]{2,1,0:T(8,128)(2,1)S(1)}, u32[]{:S(2)}, u32[]{:S(2)}) collective-permute-start(bf16[2,128,256]{2,1,0:T(8,128)(2,1)} %get-tuple-element.97), channel_id=1, source_target_pairs={{0,6},{1,7},{2,4},{3,5},{4,2},{5,3},{6,0},{7,1},{8,14},{9,15},{10,... | collective-permute-start | bytes 393224 | tf_op jit(solution)/shard_map/ppermute | solution.py:291
  118.5 0.7 collective-permute-done.30.refs_2_
  119.3 1.0 collective-permute-start.35
  120.3 0.1 broadcast_in_dim.4.row
  120.5 1.1 copy-done.13
  121.6 8.6 %shard_map.80.source = f32[2,512,512]{2,1,0:T(8,128)} custom-call(s32[2]{0:T(128)S(1)} %pad_add_fusion.place, f32[8]{0:T(128)S(1)} %copy-done.11, f32[2,512,512]{2,1,0:T(8,128)} %bitcast.14, bf16[8,2,128,256]{3,2,1,0:T(8,128)(2,1)S(1)} %all-to-all-done.1.blocks, f32[512,128]{1,0:T(8,128)S(1)} %broadcast_in_dim.4.row, f32[1,512]{1,0:T(1,128)S(1)} %bitcast.20, ...), custom_call_target="tpu_custom_call" | custom-call | flops 3221225472 | bytes 6291456 | tf_op jit(solution)/shard_map/pallas_call | solution.py:42
  130.2 2.8 %shard_map.83 = f32[2,512,512]{2,1,0:T(8,128)} custom-call(s32[2]{0:T(128)S(1)} %pad_add_fusion.place, f32[2,512,512]{2,1,0:T(8,128)} %shard_map.80.source, bf16[2,128,256]{2,1,0:T(8,128)(2,1)S(1)} %get-tuple-element.91.refs_0_, bf16[2,128,256]{2,1,0:T(8,128)(2,1)S(1)} %collective-permute-done.29.refs_1_, ...), custom_call_target="tpu_custom_call", output_to_operand_aliasing={{}: (1, {})} | custom-call | flops 524288 | bytes 5242880 | tf_op jit(solution)/shard_map/pallas_call | solution.py:409
  (77 shorter events, 0.3 us)
Async XLA Ops:
  0.0 18.3 %copy-start.20 = (s32[8]{0:T(128)S(1)}, s32[8]{0:T(128)}, u32[]{:S(2)}) copy-start(s32[8]{0:T(128)} %constant.25.clone) | copy-start | bytes 100
  0.0 19.5 %copy-start.19 = (s32[8]{0:T(128)S(1)}, s32[8]{0:T(128)}, u32[]{:S(2)}) copy-start(s32[8]{0:T(128)} %constant.24.clone) | copy-start | bytes 100
  0.0 20.8 %copy-start.9 = (f32[512]{0:T(512)S(1)}, f32[512]{0:T(512)}, u32[]{:S(2)}) copy-start(f32[512]{0:T(512)} %param.11) | copy-start | bytes 6148
  0.0 8.9 %collective-permute-start = (bf16[3,64,512]{2,1,0:T(8,128)(2,1)}, bf16[3,64,512]{2,1,0:T(8,128)(2,1)S(1)}, u32[]{:S(2)}, u32[]{:S(2)}) collective-permute-start(bf16[3,64,512]{2,1,0:T(8,128)(2,1)} %refs_0_.3), channel_id=1, source_target_pairs={{0,2},{1,3},{2,0},{3,1},{4,6},{5,7},{6,4},{7,5},{8,10},{9,11},{10,... | collective-permute-start | bytes 589832 | tf_op jit(solution)/shard_map/ppermute | solution.py:308
  3.0 10.8 %collective-permute-start.1 = (bf16[3,64,512]{2,1,0:T(8,128)(2,1)}, bf16[3,64,512]{2,1,0:T(8,128)(2,1)S(1)}, u32[]{:S(2)}, u32[]{:S(2)}) collective-permute-start(bf16[3,64,512]{2,1,0:T(8,128)(2,1)} %refs_0_.3), channel_id=1, source_target_pairs={{0,4},{1,5},{2,6},{3,7},{4,0},{5,1},{6,2},{7,3},{8,12},{9,13},{10,... | collective-permute-start | bytes 589832 | tf_op jit(solution)/shard_map/ppermute | solution.py:308
  4.5 9.3 %collective-permute-start.2 = (bf16[3,64,512]{2,1,0:T(8,128)(2,1)}, bf16[3,64,512]{2,1,0:T(8,128)(2,1)S(1)}, u32[]{:S(2)}, u32[]{:S(2)}) collective-permute-start(bf16[3,64,512]{2,1,0:T(8,128)(2,1)} %refs_0_.3), channel_id=1, source_target_pairs={{0,6},{1,7},{2,4},{3,5},{4,2},{5,3},{6,0},{7,1},{8,14},{9,15},{10,... | collective-permute-start | bytes 589832 | tf_op jit(solution)/shard_map/ppermute | solution.py:308
  4.6 1.6 %copy-start = (f32[2,1,512,512]{3,2,1,0:T(8,128)S(1)}, f32[2,1,512,512]{3,2,1,0:T(8,128)}, u32[]{:S(2)}) copy-start(f32[2,1,512,512]{3,2,1,0:T(8,128)} %param.7) | copy-start | bytes 6291460
  6.2 7.6 %copy-start.1 = (bf16[3,64,512]{2,1,0:T(8,128)(2,1)S(1)}, bf16[3,64,512]{2,1,0:T(8,128)(2,1)}, u32[]{:S(2)}) copy-start(bf16[3,64,512]{2,1,0:T(8,128)(2,1)} %refs_0_.3) | copy-start | bytes 589828
  9.0 22.1 %copy-start.3 = (bf16[3,64,512]{2,1,0:T(8,128)(2,1)}, bf16[3,64,512]{2,1,0:T(8,128)(2,1)S(1)}, u32[]{:S(2)}) copy-start(bf16[3,64,512]{2,1,0:T(8,128)(2,1)S(1)} %collective-permute-done.refs_1_) | copy-start | bytes 589828
  13.8 17.2 %copy-start.5 = (bf16[3,64,512]{2,1,0:T(8,128)(2,1)}, bf16[3,64,512]{2,1,0:T(8,128)(2,1)S(1)}, u32[]{:S(2)}) copy-start(bf16[3,64,512]{2,1,0:T(8,128)(2,1)S(1)} %collective-permute-done.1.refs_2_) | copy-start | bytes 589828
  13.8 17.2 %copy-start.7 = (bf16[3,64,512]{2,1,0:T(8,128)(2,1)}, bf16[3,64,512]{2,1,0:T(8,128)(2,1)S(1)}, u32[]{:S(2)}) copy-start(bf16[3,64,512]{2,1,0:T(8,128)(2,1)S(1)} %collective-permute-done.2.refs_3_) | copy-start | bytes 589828
  14.8 8.5 %collective-permute-start.3 = (bf16[4,3,64,512]{3,2,1,0:T(8,128)(2,1)}, bf16[4,3,64,512]{3,2,1,0:T(8,128)(2,1)S(1)}, u32[]{:S(2)}, u32[]{:S(2)}) collective-permute-start(bf16[4,3,64,512]{3,2,1,0:T(8,128)(2,1)} %pad_maximum_fusion), channel_id=1, source_target_pairs={{0,1},{1,0},{2,3},{3,2},{4,5},{5,4},{6,7},{7,6},{8,9},{9,8},{10,11... | collective-permute-start | bytes 2359304 | tf_op jit(solution)/shard_map/ppermute | solution.py:308
  14.8 6.1 %collective-permute-start.10 = (bf16[2,128,256]{2,1,0:T(8,128)(2,1)S(1)}, bf16[2,128,256]{2,1,0:T(8,128)(2,1)S(1)}, u32[]{:S(2)}, u32[]{:S(2)}) collective-permute-start(bf16[2,128,256]{2,1,0:T(8,128)(2,1)S(1)} %get-tuple-element.60), channel_id=1, source_target_pairs={{0,7},{1,6},{2,5},{3,4},{4,3},{5,2},{6,1},{7,0},{8,15},{9,14},{10,... | collective-permute-start | bytes 393224 | tf_op jit(solution)/shard_map/ppermute | solution.py:291
  16.4 6.0 %collective-permute-start.4 = (bf16[2,128,256]{2,1,0:T(8,128)(2,1)S(1)}, bf16[2,128,256]{2,1,0:T(8,128)(2,1)S(1)}, u32[]{:S(2)}, u32[]{:S(2)}) collective-permute-start(bf16[2,128,256]{2,1,0:T(8,128)(2,1)S(1)} %get-tuple-element.54), channel_id=1, source_target_pairs={{0,1},{1,0},{2,3},{3,2},{4,5},{5,4},{6,7},{7,6},{8,9},{9,8},{10,11... | collective-permute-start | bytes 393224 | tf_op jit(solution)/shard_map/ppermute | solution.py:291
  16.4 14.6 %collective-permute-start.5 = (bf16[2,128,256]{2,1,0:T(8,128)(2,1)S(1)}, bf16[2,128,256]{2,1,0:T(8,128)(2,1)S(1)}, u32[]{:S(2)}, u32[]{:S(2)}) collective-permute-start(bf16[2,128,256]{2,1,0:T(8,128)(2,1)S(1)} %get-tuple-element.55), channel_id=1, source_target_pairs={{0,2},{1,3},{2,0},{3,1},{4,6},{5,7},{6,4},{7,5},{8,10},{9,11},{10,... | collective-permute-start | bytes 393224 | tf_op jit(solution)/shard_map/ppermute | solution.py:291
  17.9 13.2 %collective-permute-start.6 = (bf16[2,128,256]{2,1,0:T(8,128)(2,1)S(1)}, bf16[2,128,256]{2,1,0:T(8,128)(2,1)S(1)}, u32[]{:S(2)}, u32[]{:S(2)}) collective-permute-start(bf16[2,128,256]{2,1,0:T(8,128)(2,1)S(1)} %get-tuple-element.56), channel_id=1, source_target_pairs={{0,3},{1,2},{2,1},{3,0},{4,7},{5,6},{6,5},{7,4},{8,11},{9,10},{10,... | collective-permute-start | bytes 393224 | tf_op jit(solution)/shard_map/ppermute | solution.py:291
  20.9 10.2 %collective-permute-start.7 = (bf16[2,128,256]{2,1,0:T(8,128)(2,1)S(1)}, bf16[2,128,256]{2,1,0:T(8,128)(2,1)S(1)}, u32[]{:S(2)}, u32[]{:S(2)}) collective-permute-start(bf16[2,128,256]{2,1,0:T(8,128)(2,1)S(1)} %get-tuple-element.57), channel_id=1, source_target_pairs={{0,4},{1,5},{2,6},{3,7},{4,0},{5,1},{6,2},{7,3},{8,12},{9,13},{10,... | collective-permute-start | bytes 393224 | tf_op jit(solution)/shard_map/ppermute | solution.py:291
  22.4 10.5 %collective-permute-start.8 = (bf16[2,128,256]{2,1,0:T(8,128)(2,1)S(1)}, bf16[2,128,256]{2,1,0:T(8,128)(2,1)S(1)}, u32[]{:S(2)}, u32[]{:S(2)}) collective-permute-start(bf16[2,128,256]{2,1,0:T(8,128)(2,1)S(1)} %get-tuple-element.58), channel_id=1, source_target_pairs={{0,5},{1,4},{2,7},{3,6},{4,1},{5,0},{6,3},{7,2},{8,13},{9,12},{10,... | collective-permute-start | bytes 393224 | tf_op jit(solution)/shard_map/ppermute | solution.py:291
  23.3 7.7 %copy-start.12 = (bf16[4,3,64,512]{3,2,1,0:T(8,128)(2,1)}, bf16[4,3,64,512]{3,2,1,0:T(8,128)(2,1)S(1)}, u32[]{:S(2)}) copy-start(bf16[4,3,64,512]{3,2,1,0:T(8,128)(2,1)S(1)} %collective-permute-done.3.refs_4_) | copy-start | bytes 2359300
  23.3 9.6 %collective-permute-start.9 = (bf16[2,128,256]{2,1,0:T(8,128)(2,1)S(1)}, bf16[2,128,256]{2,1,0:T(8,128)(2,1)S(1)}, u32[]{:S(2)}, u32[]{:S(2)}) collective-permute-start(bf16[2,128,256]{2,1,0:T(8,128)(2,1)S(1)} %get-tuple-element.59), channel_id=1, source_target_pairs={{0,6},{1,7},{2,4},{3,5},{4,2},{5,3},{6,0},{7,1},{8,14},{9,15},{10,... | collective-permute-start | bytes 393224 | tf_op jit(solution)/shard_map/ppermute | solution.py:291
  31.1 10.9 %copy-start.18 = (bf16[8,8]{1,0:T(8,128)(2,1)S(1)}, bf16[8,8]{1,0:T(8,128)(2,1)}, u32[]{:S(2)}) copy-start(bf16[8,8]{1,0:T(8,128)(2,1)} %param.9) | copy-start | bytes 388
  32.9 19.1 %all-to-all-start = ((bf16[8,2,128,256]{3,2,1,0:T(8,128)(2,1)}), bf16[8,2,128,256]{3,2,1,0:T(8,128)(2,1)S(1)}, u32[]{:S(2)}, u32[]{:S(2)}) async-start(bf16[8,2,128,256]{3,2,1,0:T(8,128)(2,1)} %shard_map.74), calls=%async_computation | async-start | bytes 2097152 | tf_op jit(solution)/shard_map/all_to_all | solution.py:285
  37.4 8.8 %collective-permute-start.11 = (bf16[2,2,64,256]{3,2,1,0:T(8,128)(2,1)S(1)}, bf16[2,2,64,256]{3,2,1,0:T(8,128)(2,1)S(1)}, u32[]{:S(2)}, u32[]{:S(2)}) collective-permute-start(bf16[2,2,64,256]{3,2,1,0:T(8,128)(2,1)S(1)} %get-tuple-element.64), channel_id=1, source_target_pairs={{0,8},{8,0},{16,24},{24,16},{1,9},{9,1},{17,25},{25,17},{2,10},{10... | collective-permute-start | bytes 393224 | tf_op jit(solution)/shard_map/ppermute | solution.py:297
  39.1 12.9 %collective-permute-start.12 = (bf16[2,2,64,256]{3,2,1,0:T(8,128)(2,1)S(1)}, bf16[2,2,64,256]{3,2,1,0:T(8,128)(2,1)S(1)}, u32[]{:S(2)}, u32[]{:S(2)}) collective-permute-start(bf16[2,2,64,256]{3,2,1,0:T(8,128)(2,1)S(1)} %get-tuple-element.65), channel_id=1, source_target_pairs={{0,16},{8,24},{16,0},{24,8},{1,17},{9,25},{17,1},{25,9},{2,18},{10... | collective-permute-start | bytes 393224 | tf_op jit(solution)/shard_map/ppermute | solution.py:297
  41.7 10.4 %collective-permute-start.13 = (bf16[2,2,64,256]{3,2,1,0:T(8,128)(2,1)S(1)}, bf16[2,2,64,256]{3,2,1,0:T(8,128)(2,1)S(1)}, u32[]{:S(2)}, u32[]{:S(2)}) collective-permute-start(bf16[2,2,64,256]{3,2,1,0:T(8,128)(2,1)S(1)} %get-tuple-element.66), channel_id=1, source_target_pairs={{0,24},{8,16},{16,8},{24,0},{1,25},{9,17},{17,9},{25,1},{2,26},{10... | collective-permute-start | bytes 393224 | tf_op jit(solution)/shard_map/ppermute | solution.py:297
  42.0 21.7 %collective-permute-start.17 = (bf16[2,2,64,256]{3,2,1,0:T(8,128)(2,1)S(1)}, bf16[2,2,64,256]{3,2,1,0:T(8,128)(2,1)S(1)}, u32[]{:S(2)}, u32[]{:S(2)}) collective-permute-start(bf16[2,2,64,256]{3,2,1,0:T(8,128)(2,1)S(1)} %get-tuple-element.73), channel_id=1, source_target_pairs={{0,8},{8,0},{16,24},{24,16},{1,9},{9,1},{17,25},{25,17},{2,10},{10... | collective-permute-start | bytes 393224 | tf_op jit(solution)/shard_map/ppermute | solution.py:297
  42.8 22.4 %collective-permute-start.18 = (bf16[2,2,64,256]{3,2,1,0:T(8,128)(2,1)S(1)}, bf16[2,2,64,256]{3,2,1,0:T(8,128)(2,1)S(1)}, u32[]{:S(2)}, u32[]{:S(2)}) collective-permute-start(bf16[2,2,64,256]{3,2,1,0:T(8,128)(2,1)S(1)} %get-tuple-element.74), channel_id=1, source_target_pairs={{0,16},{8,24},{16,0},{24,8},{1,17},{9,25},{17,1},{25,9},{2,18},{10... | collective-permute-start | bytes 393224 | tf_op jit(solution)/shard_map/ppermute | solution.py:297
  46.3 18.9 %collective-permute-start.19 = (bf16[2,2,64,256]{3,2,1,0:T(8,128)(2,1)S(1)}, bf16[2,2,64,256]{3,2,1,0:T(8,128)(2,1)S(1)}, u32[]{:S(2)}, u32[]{:S(2)}) collective-permute-start(bf16[2,2,64,256]{3,2,1,0:T(8,128)(2,1)S(1)} %get-tuple-element.75), channel_id=1, source_target_pairs={{0,24},{8,16},{16,8},{24,0},{1,25},{9,17},{17,9},{25,1},{2,26},{10... | collective-permute-start | bytes 393224 | tf_op jit(solution)/shard_map/ppermute | solution.py:297
  53.6 19.4 %collective-permute-start.14 = (bf16[2,2,64,256]{3,2,1,0:T(8,128)(2,1)S(1)}, bf16[2,2,64,256]{3,2,1,0:T(8,128)(2,1)S(1)}, u32[]{:S(2)}, u32[]{:S(2)}) collective-permute-start(bf16[2,2,64,256]{3,2,1,0:T(8,128)(2,1)S(1)} %get-tuple-element.68.refs_1_), channel_id=1, source_target_pairs={{0,8},{8,0},{16,24},{24,16},{1,9},{9,1},{17,25},{25,17},{2,10},{10... | collective-permute-start | bytes 393224 | tf_op jit(solution)/shard_map/ppermute | solution.py:297
  62.6 14.2 %collective-permute-start.15 = (bf16[2,2,64,256]{3,2,1,0:T(8,128)(2,1)S(1)}, bf16[2,2,64,256]{3,2,1,0:T(8,128)(2,1)S(1)}, u32[]{:S(2)}, u32[]{:S(2)}) collective-permute-start(bf16[2,2,64,256]{3,2,1,0:T(8,128)(2,1)S(1)} %get-tuple-element.69.refs_2_), channel_id=1, source_target_pairs={{0,16},{8,24},{16,0},{24,8},{1,17},{9,25},{17,1},{25,9},{2,18},{10... | collective-permute-start | bytes 393224 | tf_op jit(solution)/shard_map/ppermute | solution.py:297
  63.7 13.1 %collective-permute-start.16 = (bf16[2,2,64,256]{3,2,1,0:T(8,128)(2,1)S(1)}, bf16[2,2,64,256]{3,2,1,0:T(8,128)(2,1)S(1)}, u32[]{:S(2)}, u32[]{:S(2)}) collective-permute-start(bf16[2,2,64,256]{3,2,1,0:T(8,128)(2,1)S(1)} %get-tuple-element.70.refs_3_), channel_id=1, source_target_pairs={{0,24},{8,16},{16,8},{24,0},{1,25},{9,17},{17,9},{25,1},{2,26},{10... | collective-permute-start | bytes 393224 | tf_op jit(solution)/shard_map/ppermute | solution.py:297
  65.1 11.7 %copy-start.11 = (f32[8]{0:T(128)S(1)}, f32[8]{0:T(128)}, u32[]{:S(2)}) copy-start(f32[8]{0:T(128)} %occ.9) | copy-start | bytes 100
  66.7 20.8 %collective-permute-start.20 = (bf16[2,2,64,256]{3,2,1,0:T(8,128)(2,1)S(1)}, bf16[2,2,64,256]{3,2,1,0:T(8,128)(2,1)S(1)}, u32[]{:S(2)}, u32[]{:S(2)}) collective-permute-start(bf16[2,2,64,256]{3,2,1,0:T(8,128)(2,1)S(1)} %get-tuple-element.77.refs_2_), channel_id=1, source_target_pairs={{0,8},{8,0},{16,24},{24,16},{1,9},{9,1},{17,25},{25,17},{2,10},{10... | collective-permute-start | bytes 393224 | tf_op jit(solution)/shard_map/ppermute | solution.py:297
  70.5 18.5 %collective-permute-start.21 = (bf16[2,2,64,256]{3,2,1,0:T(8,128)(2,1)S(1)}, bf16[2,2,64,256]{3,2,1,0:T(8,128)(2,1)S(1)}, u32[]{:S(2)}, u32[]{:S(2)}) collective-permute-start(bf16[2,2,64,256]{3,2,1,0:T(8,128)(2,1)S(1)} %get-tuple-element.78.refs_3_), channel_id=1, source_target_pairs={{0,16},{8,24},{16,0},{24,8},{1,17},{9,25},{17,1},{25,9},{2,18},{10... | collective-permute-start | bytes 393224 | tf_op jit(solution)/shard_map/ppermute | solution.py:297
  73.0 16.1 %collective-permute-start.22 = (bf16[2,2,64,256]{3,2,1,0:T(8,128)(2,1)S(1)}, bf16[2,2,64,256]{3,2,1,0:T(8,128)(2,1)S(1)}, u32[]{:S(2)}, u32[]{:S(2)}) collective-permute-start(bf16[2,2,64,256]{3,2,1,0:T(8,128)(2,1)S(1)} %get-tuple-element.79.refs_4_), channel_id=1, source_target_pairs={{0,24},{8,16},{16,8},{24,0},{1,25},{9,17},{17,9},{25,1},{2,26},{10... | collective-permute-start | bytes 393224 | tf_op jit(solution)/shard_map/ppermute | solution.py:297
  79.1 0.8 copy-start.14
  79.9 12.4 %copy-start.16 = (bf16[2,2,64,256]{3,2,1,0:T(8,128)(2,1)}, bf16[2,2,64,256]{3,2,1,0:T(8,128)(2,1)S(1)}, u32[]{:S(2)}) copy-start(bf16[2,2,64,256]{3,2,1,0:T(8,128)(2,1)S(1)} %get-tuple-element.87.refs_0_.refs_4_) | copy-start | bytes 393220
  79.9 21.6 %collective-permute-start.26 = (bf16[2,2,64,256]{3,2,1,0:T(8,128)(2,1)S(1)}, bf16[2,2,64,256]{3,2,1,0:T(8,128)(2,1)S(1)}, u32[]{:S(2)}, u32[]{:S(2)}) collective-permute-start(bf16[2,2,64,256]{3,2,1,0:T(8,128)(2,1)S(1)} %get-tuple-element.88.refs_1_), channel_id=1, source_target_pairs={{0,8},{8,0},{16,24},{24,16},{1,9},{9,1},{17,25},{25,17},{2,10},{10... | collective-permute-start | bytes 393224 | tf_op jit(solution)/shard_map/ppermute | solution.py:297
  86.6 16.4 %collective-permute-start.27 = (bf16[2,2,64,256]{3,2,1,0:T(8,128)(2,1)S(1)}, bf16[2,2,64,256]{3,2,1,0:T(8,128)(2,1)S(1)}, u32[]{:S(2)}, u32[]{:S(2)}) collective-permute-start(bf16[2,2,64,256]{3,2,1,0:T(8,128)(2,1)S(1)} %get-tuple-element.89.refs_2_), channel_id=1, source_target_pairs={{0,16},{8,24},{16,0},{24,8},{1,17},{9,25},{17,1},{25,9},{2,18},{10... | collective-permute-start | bytes 393224 | tf_op jit(solution)/shard_map/ppermute | solution.py:297
  87.6 15.4 %collective-permute-start.28 = (bf16[2,2,64,256]{3,2,1,0:T(8,128)(2,1)S(1)}, bf16[2,2,64,256]{3,2,1,0:T(8,128)(2,1)}, u32[]{:S(2)}, u32[]{:S(2)}) collective-permute-start(bf16[2,2,64,256]{3,2,1,0:T(8,128)(2,1)S(1)} %get-tuple-element.90.refs_3_), channel_id=1, source_target_pairs={{0,24},{8,16},{16,8},{24,0},{1,25},{9,17},{17,9},{25,1},{2,26},{10... | collective-permute-start | bytes 393224 | tf_op jit(solution)/shard_map/ppermute | solution.py:297
  92.3 10.7 %copy-start.17 = (bf16[2,2,64,256]{3,2,1,0:T(8,128)(2,1)S(1)}, bf16[2,2,64,256]{3,2,1,0:T(8,128)(2,1)}, u32[]{:S(2)}) copy-start(bf16[2,2,64,256]{3,2,1,0:T(8,128)(2,1)} %copy-done.16) | copy-start | bytes 393220
  92.3 13.5 %collective-permute-start.23 = (bf16[2,2,64,256]{3,2,1,0:T(8,128)(2,1)S(1)}, bf16[2,2,64,256]{3,2,1,0:T(8,128)(2,1)S(1)}, u32[]{:S(2)}, u32[]{:S(2)}) collective-permute-start(bf16[2,2,64,256]{3,2,1,0:T(8,128)(2,1)S(1)} %get-tuple-element.83.refs_1_), channel_id=1, source_target_pairs={{0,8},{8,0},{16,24},{24,16},{1,9},{9,1},{17,25},{25,17},{2,10},{10... | collective-permute-start | bytes 393224 | tf_op jit(solution)/shard_map/ppermute | solution.py:297
  93.3 12.4 %collective-permute-start.24 = (bf16[2,2,64,256]{3,2,1,0:T(8,128)(2,1)S(1)}, bf16[2,2,64,256]{3,2,1,0:T(8,128)(2,1)S(1)}, u32[]{:S(2)}, u32[]{:S(2)}) collective-permute-start(bf16[2,2,64,256]{3,2,1,0:T(8,128)(2,1)S(1)} %get-tuple-element.84.refs_2_), channel_id=1, source_target_pairs={{0,16},{8,24},{16,0},{24,8},{1,17},{9,25},{17,1},{25,9},{2,18},{10... | collective-permute-start | bytes 393224 | tf_op jit(solution)/shard_map/ppermute | solution.py:297
  95.2 25.1 %all-to-all-start.1 = ((bf16[8,2,128,256]{3,2,1,0:T(8,128)(2,1)}), bf16[8,2,128,256]{3,2,1,0:T(8,128)(2,1)S(1)}, u32[]{:S(2)}, u32[]{:S(2)}) async-start(bf16[8,2,128,256]{3,2,1,0:T(8,128)(2,1)} %get-tuple-element.80), calls=%async_computation.1 | async-start | bytes 2097152 | tf_op jit(solution)/shard_map/all_to_all | solution.py:285
  101.5 7.8 %collective-permute-start.25 = (bf16[2,2,64,256]{3,2,1,0:T(8,128)(2,1)S(1)}, bf16[2,2,64,256]{3,2,1,0:T(8,128)(2,1)S(1)}, u32[]{:S(2)}, u32[]{:S(2)}) collective-permute-start(bf16[2,2,64,256]{3,2,1,0:T(8,128)(2,1)S(1)} %get-tuple-element.85.refs_3_), channel_id=1, source_target_pairs={{0,24},{8,16},{16,8},{24,0},{1,25},{9,17},{17,9},{25,1},{2,26},{10... | collective-permute-start | bytes 393224 | tf_op jit(solution)/shard_map/ppermute | solution.py:297
  103.0 1.0 copy-start.15
  105.7 14.6 %copy-start.10 = (f32[512]{0:T(512)S(1)}, f32[512]{0:T(512)}, u32[]{:S(2)}) copy-start(f32[512]{0:T(512)} %param.11) | copy-start | bytes 6148
  105.7 14.7 %copy-start.2 = (bf16[3,64,512]{2,1,0:T(8,128)(2,1)S(1)}, bf16[3,64,512]{2,1,0:T(8,128)(2,1)}, u32[]{:S(2)}) copy-start(bf16[3,64,512]{2,1,0:T(8,128)(2,1)} %refs_0_.3) | copy-start | bytes 589828
  105.7 14.7 %copy-start.4 = (bf16[3,64,512]{2,1,0:T(8,128)(2,1)S(1)}, bf16[3,64,512]{2,1,0:T(8,128)(2,1)}, u32[]{:S(2)}) copy-start(bf16[3,64,512]{2,1,0:T(8,128)(2,1)} %copy-done.3) | copy-start | bytes 589828
  105.8 14.7 %copy-start.6 = (bf16[3,64,512]{2,1,0:T(8,128)(2,1)S(1)}, bf16[3,64,512]{2,1,0:T(8,128)(2,1)}, u32[]{:S(2)}) copy-start(bf16[3,64,512]{2,1,0:T(8,128)(2,1)} %copy-done.5) | copy-start | bytes 589828
  105.8 14.7 %copy-start.8 = (bf16[3,64,512]{2,1,0:T(8,128)(2,1)S(1)}, bf16[3,64,512]{2,1,0:T(8,128)(2,1)}, u32[]{:S(2)}) copy-start(bf16[3,64,512]{2,1,0:T(8,128)(2,1)} %copy-done.7) | copy-start | bytes 589828
  111.4 4.3 %collective-permute-start.29 = (bf16[2,128,256]{2,1,0:T(8,128)(2,1)S(1)}, bf16[2,128,256]{2,1,0:T(8,128)(2,1)S(1)}, u32[]{:S(2)}, u32[]{:S(2)}) collective-permute-start(bf16[2,128,256]{2,1,0:T(8,128)(2,1)S(1)} %get-tuple-element.92), channel_id=1, source_target_pairs={{0,1},{1,0},{2,3},{3,2},{4,5},{5,4},{6,7},{7,6},{8,9},{9,8},{10,11... | collective-permute-start | bytes 393224 | tf_op jit(solution)/shard_map/ppermute | solution.py:291
  111.4 7.8 %collective-permute-start.30 = (bf16[2,128,256]{2,1,0:T(8,128)(2,1)S(1)}, bf16[2,128,256]{2,1,0:T(8,128)(2,1)S(1)}, u32[]{:S(2)}, u32[]{:S(2)}) collective-permute-start(bf16[2,128,256]{2,1,0:T(8,128)(2,1)S(1)} %get-tuple-element.93), channel_id=1, source_target_pairs={{0,2},{1,3},{2,0},{3,1},{4,6},{5,7},{6,4},{7,5},{8,10},{9,11},{10,... | collective-permute-start | bytes 393224 | tf_op jit(solution)/shard_map/ppermute | solution.py:291
  113.1 17.1 %collective-permute-start.31 = (bf16[2,128,256]{2,1,0:T(8,128)(2,1)}, bf16[2,128,256]{2,1,0:T(8,128)(2,1)S(1)}, u32[]{:S(2)}, u32[]{:S(2)}) collective-permute-start(bf16[2,128,256]{2,1,0:T(8,128)(2,1)} %get-tuple-element.94), channel_id=1, source_target_pairs={{0,3},{1,2},{2,1},{3,0},{4,7},{5,6},{6,5},{7,4},{8,11},{9,10},{10,... | collective-permute-start | bytes 393224 | tf_op jit(solution)/shard_map/ppermute | solution.py:291
  113.3 16.9 %collective-permute-start.32 = (bf16[2,128,256]{2,1,0:T(8,128)(2,1)}, bf16[2,128,256]{2,1,0:T(8,128)(2,1)S(1)}, u32[]{:S(2)}, u32[]{:S(2)}) collective-permute-start(bf16[2,128,256]{2,1,0:T(8,128)(2,1)} %get-tuple-element.95), channel_id=1, source_target_pairs={{0,4},{1,5},{2,6},{3,7},{4,0},{5,1},{6,2},{7,3},{8,12},{9,13},{10,... | collective-permute-start | bytes 393224 | tf_op jit(solution)/shard_map/ppermute | solution.py:291
  115.8 14.4 %collective-permute-start.33 = (bf16[2,128,256]{2,1,0:T(8,128)(2,1)}, bf16[2,128,256]{2,1,0:T(8,128)(2,1)S(1)}, u32[]{:S(2)}, u32[]{:S(2)}) collective-permute-start(bf16[2,128,256]{2,1,0:T(8,128)(2,1)} %get-tuple-element.96), channel_id=1, source_target_pairs={{0,5},{1,4},{2,7},{3,6},{4,1},{5,0},{6,3},{7,2},{8,13},{9,12},{10,... | collective-permute-start | bytes 393224 | tf_op jit(solution)/shard_map/ppermute | solution.py:291
  115.8 14.4 %collective-permute-start.34 = (bf16[2,128,256]{2,1,0:T(8,128)(2,1)}, bf16[2,128,256]{2,1,0:T(8,128)(2,1)S(1)}, u32[]{:S(2)}, u32[]{:S(2)}) collective-permute-start(bf16[2,128,256]{2,1,0:T(8,128)(2,1)} %get-tuple-element.97), channel_id=1, source_target_pairs={{0,6},{1,7},{2,4},{3,5},{4,2},{5,3},{6,0},{7,1},{8,14},{9,15},{10,... | collective-permute-start | bytes 393224 | tf_op jit(solution)/shard_map/ppermute | solution.py:291
  119.3 10.9 %collective-permute-start.35 = (bf16[2,128,256]{2,1,0:T(8,128)(2,1)S(1)}, bf16[2,128,256]{2,1,0:T(8,128)(2,1)S(1)}, u32[]{:S(2)}, u32[]{:S(2)}) collective-permute-start(bf16[2,128,256]{2,1,0:T(8,128)(2,1)S(1)} %get-tuple-element.98), channel_id=1, source_target_pairs={{0,7},{1,6},{2,5},{3,4},{4,3},{5,2},{6,1},{7,0},{8,15},{9,14},{10,... | collective-permute-start | bytes 393224 | tf_op jit(solution)/shard_map/ppermute | solution.py:291
  120.5 1.1 copy-start.13

commit v12 on v10

--- a/solution.py
+++ b/solution.py
@@ -63,38 +63,38 @@
         out[d, pair, c * g:(c + 1) * g, e:] = tile[g:]
 
 
-def unpack_pair(tiles, chunks, pair, put):
-    e = tiles.edge
+def unpack_pair(tiles, blocks, pair, put):
+    e, g = tiles.edge, tiles.rows
     for d, (a, b) in enumerate(tiles.above):
-        block = jnp.concatenate([chunk[d, pair] for chunk in chunks], axis=0).astype(WIDE)
-        put(a, b, block[:, :e])
-        put(b, a, block[:, e:].T)
+        put(a, b, blocks[d, pair, :, :e].astype(WIDE))
+        put(b, a, blocks[d, pair, :, e:].astype(WIDE).T)
     for d, c, k in tiles.diagonal:
-        block = chunks[c][d, pair].astype(WIDE)
-        put(k, k, jnp.concatenate([block[:, :e], block[:, e:]], axis=0))
-
-
-def to_distances(place, whole, outs):
+        upper = blocks[d, pair, c * g:(c + 1) * g, :e]
+        lower = blocks[d, pair, c * g:(c + 1) * g, e:]
+        put(k, k, jnp.concatenate([upper, lower], axis=0).astype(WIDE))
+
+
+def to_distances(origin, whole, outs):
     for k, out in enumerate(outs):
-        out[...] = whole[place[1] ^ k]
-
-
-def from_distances(place, pieces, whole):
+        out[...] = whole[origin ^ k]
+
+
+def from_distances(origin, pieces, whole):
     for k, piece in enumerate(pieces):
-        whole[place[1] ^ k] = piece[...]
+        whole[origin ^ k] = piece[...]
 
 
 def pack_kernel(tiles, place, source, *refs):
     outs, whole = refs[:-1], refs[-1]
     for pair in range(source.shape[0]):
         pack_pair(tiles, source.at[pair], whole, pair, mirrored=True)
-    to_distances(place, whole, outs)
+    to_distances(place[1], whole, outs)
 
 
 def sort_kernel(tiles, groups, place, *refs):
     pieces, outs, whole = refs[:-2 * groups - 1], refs[-2 * groups - 1:-1], refs[-1]
     first = whole.shape[1]
-    from_distances(place, pieces, whole)
+    from_distances(place[1], pieces, whole)
     for s in range(groups):
         for u in range(first):
             block = whole[(place[0] ^ s) * first + u]
@@ -137,7 +137,7 @@
         pack_pair(tiles, total, out, pair)
 
 
-def second_ladder_kernel(tiles, order, place, occ, source, upper, lower, row, column, *refs):
+def second_ladder_kernel(tiles, order, place, occ, source, blocks, row, column, *refs):
     pieces, (out, whole, inner, total, matrix) = refs[:-5], refs[-5:]
     assemble(place, order, pieces, whole)
     count = source.shape[0]
@@ -145,7 +145,7 @@
         def put(a, b, tile):
             matrix[tiles.span(a), tiles.span(b)] = tile.astype(NARROW)
 
-        unpack_pair(tiles, (upper, lower), pair, put)
+        unpack_pair(tiles, blocks, pair, put)
         ladder_pair(matrix[...], whole, inner, total)
         base = occ[place[0] * count + pair] + occ[place[1]]
         strip = math.gcd(64, total.shape[0])
@@ -161,15 +161,27 @@
         lax.fori_loop(0, total.shape[0] // strip, finish, 0)
 
 
-def add_kernel(tiles, place, source, *refs):
-    pieces, (out, whole) = refs[:-2], refs[-2:]
-    from_distances(place, pieces, whole)
+def add_kernel(tiles, first, place, source, *refs):
+    pieces, (out, whole, turned) = refs[:-3], refs[-3:]
+    devices = len(pieces) // 2
+    from_distances(place[1], pieces[:devices], whole)
+    from_distances(place[0] * first + lax.rem(place[1], first), pieces[devices:], turned)
+    e, g = tiles.edge, tiles.rows
 
     def put(a, b, tile):
         here = (0, tiles.span(a), tiles.span(b))
         out[here] = source[here] + tile
 
-    unpack_pair(tiles, [whole.at[:, :, :tiles.rows], whole.at[:, :, tiles.rows:]], 0, put)
+    for d, (a, b) in enumerate(tiles.above):
+        block = whole[d, 0].astype(WIDE) + tiles.mirror_across(turned[d, 0].astype(WIDE))
+        put(a, b, block[:, :e])
+        put(b, a, block[:, e:].T)
+    for d, c, k in tiles.diagonal:
+        def tile_of(blocks):
+            block = blocks[d, 0, c * g:(c + 1) * g].astype(WIDE)
+            return jnp.concatenate([block[:, :e], block[:, e:]], axis=0)
+
+        put(k, k, tile_of(whole) + tile_of(turned).T)
 
 
 def mix(place, fock, first, load, store, rows):
@@ -219,11 +231,14 @@
 
 
 def update_kernel(tiles, groups, first, chunk, place, fock, occ, sums, *refs):
-    own, other = refs[:groups], refs[groups:2 * groups]
-    sent, rest = refs[2 * groups:2 * groups + 2]
-    out = refs[2 * groups + 2:3 * groups + 2]
-    update = refs[3 * groups + 2]
-    here = slice(chunk * tiles.rows, (chunk + 1) * tiles.rows)
+    before, refs = refs[:3 * chunk], refs[3 * chunk:]
+    own, other, refs = refs[:groups], refs[groups:2 * groups], refs[2 * groups:]
+    update = refs[-1]
+    sent, straight, turned = (refs[0], *refs[-3:-1]) if chunk else refs[:3]
+    rows = slice(chunk * tiles.rows, (chunk + 1) * tiles.rows)
+    there = rows if chunk else slice(None)
+    for ref, out in zip(before, (sent, straight, turned)):
+        out[:, :, :tiles.rows, :] = ref[...]
 
     def one(step, carry):
         u, w = step // first, lax.rem(step, first)
@@ -232,11 +247,9 @@
             base = occ[place[0] * first + u] + occ[column]
 
             def finish(mirrored):
-                value = (own[s][u, w].astype(WIDE) + mirrored) * inverse(base - sums[here])
-                narrow = value.astype(NARROW)
+                value = (own[s][u, w].astype(WIDE) + mirrored) * inverse(base - sums[rows])
                 update[u, s * first + w] = value
-                sent[column, u] = narrow
-                rest[u, s * first + w] = (2.0 * (value - narrow.astype(WIDE))).astype(NARROW)
+                sent[column, u, there] = value.astype(NARROW)
 
             with_mirror(tiles, place, other[s][w, u].astype(WIDE), finish)
         return carry
@@ -247,35 +260,21 @@
         return update[u, s * first + r, at, :]
 
     def store(s, u, w, column, at, result):
-        out[s][u, w, at, :] = result.astype(NARROW)
+        strip = pl.ds(pl.multiple_of(chunk * tiles.rows + at.start, 16), at.size)
+        put = strip if chunk else at
+        value = update[u, s * first + w, at, :]
+        base = occ[place[0] * first + u] + occ[column]
+        share = result * inverse(base - sums[strip, :])
+        straight[column, u, put, :] = (
+            share + 2.0 * (value - value.astype(NARROW).astype(WIDE))
+        ).astype(NARROW)
+        turned[(place[0] ^ s) * first + u, w, put, :] = share.astype(NARROW)
 
     mix(place, fock, first, load, store, tiles.rows)
-
-
-def rest_kernel(tiles, groups, first, chunk, place, occ, sums, rest, *refs):
-    own, other, refs = refs[:groups], refs[groups:2 * groups], refs[2 * groups:]
-    out = refs[-1]
-    here = slice(chunk * tiles.rows, (chunk + 1) * tiles.rows)
-    there = here if chunk else slice(None)
     if chunk:
-        out[:, :, :tiles.rows, :] = refs[0][...]
-
-    def one(step, carry):
-        u, w = step // first, lax.rem(step, first)
-        for s in range(groups):
-            column = (place[0] ^ s) * first + w
-            base = occ[place[0] * first + u] + occ[column]
-
-            def finish(mirrored):
-                value = (own[s][u, w].astype(WIDE) + mirrored) * inverse(base - sums[here])
-                out[column, u, there] = (rest[u, s * first + w].astype(WIDE) + value).astype(NARROW)
-
-            with_mirror(tiles, place, other[s][w, u].astype(WIDE), finish)
-        return carry
-
-    lax.fori_loop(0, first * first, one, 0)
-    if chunk:
-        to_distances(place, out, refs[1:-1])
+        devices = straight.shape[0]
+        to_distances(place[1], straight, refs[1:1 + devices])
+        to_distances(place[1], turned, refs[1 + devices:1 + 2 * devices])
 
 
 def exchange(blocks):
@@ -288,6 +287,19 @@
         lax.ppermute(parts[k], "occj", [(d, d ^ k) for d in range(devices)])
         for k in range(devices - 1, 0, -1)
     ][::-1]
+
+
+def to_mirror(parts, groups):
+    devices = len(parts)
+    first = devices // groups
+
+    def turn(x, k):
+        return lax.ppermute(x, ("occi", "occj"), [
+            (p * devices + j, (j ^ k) // first * devices + p * first + (j ^ k) % first)
+            for p in range(groups) for j in range(devices)
+        ])
+
+    return [turn(x, k) for k, x in enumerate(parts)]
 
 
 def across_first(parts, groups):
@@ -389,47 +401,39 @@
             specs=[SMEM] * 2 + [VMEM] * (groups + 1),
         ))
         other.append(across_first(half[c], groups))
-    back, rest, mixed = [], [], []
+    ready = []
     for c in chunks:
-        sent, rest_one, *mixed_one = call(
+        ready = call(
             functools.partial(update_kernel, tiles, groups, first, c),
-            [upper, jax.ShapeDtypeStruct((first, devices, *part.shape[2:]), NARROW)] + [part] * groups,
-            [pltpu.VMEM((first, devices, *part.shape[2:]), WIDE)],
-            LONG, 10 * count, place, fock, occ_energy, sums, *half[c], *other[c],
-            specs=[SMEM] * 3 + [VMEM] * (2 * groups + 1),
+            [packed] + [distant] * (2 * devices) if c else [upper] * 3,
+            ([blocks] * 2 if c else []) + [pltpu.VMEM((first, devices, *part.shape[2:]), WIDE)],
+            LONG, 10 * count, place, fock, occ_energy, sums, *ready, *half[c], *other[c],
+            specs=[SMEM] * 3 + [VMEM] * (2 * groups + 1 + 3 * c),
         )
-        back.append(exchange(tie(sent, *back)))
-        rest, mixed = rest + [rest_one], mixed + [mixed_one]
-    other = [across_first(x, groups) for x in mixed]
+    back = exchange(ready[0])
+    last = to_mirror(ready[1 + devices:], groups)
+    last = by_distance(ready[1:1 + devices]) + last
     base = call(
         functools.partial(second_ladder_kernel, tiles, order), jax.ShapeDtypeStruct(current.shape, WIDE),
         [whole, inner, square, pltpu.VMEM((virtual, virtual), NARROW)],
-        ladder_flops, 12 * count, place, occ_energy, current, *back,
+        ladder_flops, 12 * count, place, occ_energy, current, back,
         jnp.broadcast_to(vir_energy[:, None], (virtual, 128)), vir_energy[None, :], *pieces,
-        specs=[SMEM] * 2 + [VMEM] * (5 + len(pieces)),
+        specs=[SMEM] * 2 + [VMEM] * (4 + len(pieces)),
     )
-    last = []
-    for c in chunks:
-        last = call(
-            functools.partial(rest_kernel, tiles, groups, first, c),
-            [distant] * devices if c else [upper], [blocks] if c else [],
-            2 * count if c else LONG, 8 * count, place, occ_energy, sums, rest[c], *mixed[c], *other[c], *last,
-            specs=[SMEM] * 2 + [VMEM] * (2 * groups + 2 + c),
-        )
     def by_pair(*shape):
         return pl.BlockSpec((1, *shape), lambda pair: (pair, 0, 0))
 
     done = pl.pallas_call(
-        functools.partial(add_kernel, tiles),
+        functools.partial(add_kernel, tiles, first),
         grid=(first,),
         out_shape=jax.ShapeDtypeStruct(current.shape, WIDE),
-        in_specs=[SMEM, by_pair(virtual, virtual)] + [by_pair(edge, 2 * edge)] * devices,
+        in_specs=[SMEM, by_pair(virtual, virtual)] + [by_pair(edge, 2 * edge)] * (2 * devices),
         out_specs=by_pair(virtual, virtual),
-        scratch_shapes=[pltpu.VMEM((devices, 1, edge, 2 * edge), NARROW)],
+        scratch_shapes=[pltpu.VMEM((devices, 1, edge, 2 * edge), NARROW)] * 2,
         compiler_params=PARAMS,
         input_output_aliases={1: 0},
         cost_estimate=pl.CostEstimate(flops=count, bytes_accessed=10 * count, transcendentals=0),
-    )(place, base, *by_distance(last))
+    )(place, base, *last)
     return done.reshape(amplitudes.shape)
 
 

time: 133 us -> 155 us (1.17)
  the two profiles are of different devices: /device:TPU:0 before, /device:TPU:3 now
where the time goes in v12:
time: 155 us; the launch traced here: 154 us
  starting transfers between devices  72.1 us (47%)
  waiting for transfers between devices  40.5 us (26%)
  Pallas kernels  30.3 us (20%)
  local copies, waits for them, and re-layouts  9.1 us (6%)
  between operations  1.72 us (1%)
    pallas_call x8, Pallas kernels, call(): pl.pallas_call(body, out_shape=outs, in_specs=specs, out_specs=jax.tree.m...  26.2 us
    ppermute x8, starting transfers between devices, turn(): lax.ppermute(x, ('occi', 'occj'), [(p * devices + j, (j ^ k) // first * d...  23 us
    ppermute x14, starting transfers between devices, by_distance(): lax.ppermute(parts[k], 'occj', [(d, d ^ k) for d in range(devices)])  18.9 us
    ppermute x12, starting transfers between devices, across_first(): lax.ppermute(parts[s], 'occi', [(k, k ^ s) for k in range(groups)])  15.1 us
    ppermute x14, waiting for transfers between devices, by_distance(): lax.ppermute(parts[k], 'occj', [(d, d ^ k) for d in range(devices)])  12.4 us
    all_to_all x2, starting transfers between devices, exchange(): lax.all_to_all(blocks, 'occj', split_axis=0, concat_axis=0, tiled=True)  12.4 us
    ppermute x12, waiting for transfers between devices, across_first(): lax.ppermute(parts[s], 'occi', [(k, k ^ s) for k in range(groups)])  10.3 us
    ppermute x8, waiting for transfers between devices, turn(): lax.ppermute(x, ('occi', 'occj'), [(p * devices + j, (j ^ k) // first * d...  9.28 us
  transfers between devices with their start and end apart: 40, of which 10 were waited for; matrix products, arithmetic and copies ran while one was open for 1% of the time, Pallas kernels for 15%

profile of v12, /device:TPU:3, one launch (start us, length us, event | category | flops | bytes accessed | tf_op | source)
XLA Modules:
  0.0 154.1 jit_solution(8973397447658725120)
XLA Ops:
  0.1 1.5 collective-permute-start.1
  1.6 1.2 collective-permute-start.2
  2.8 1.6 %copy-done = f32[2,1,512,512]{3,2,1,0:T(8,128)S(1)} copy-done((f32[2,1,512,512]{3,2,1,0:T(8,128)S(1)}, f32[2,1,512,512]{3,2,1,0:T(8,128)}, u32[]{:S(2)}) %copy-start) | copy-done | bytes 2097176
  4.4 0.9 shard_map.73
  5.3 2.7 %collective-permute-start.10 = (bf16[2,128,256]{2,1,0:T(8,128)(2,1)S(1)}, bf16[2,128,256]{2,1,0:T(8,128)(2,1)S(1)}, u32[]{:S(2)}, u32[]{:S(2)}) collective-permute-start(bf16[2,128,256]{2,1,0:T(8,128)(2,1)S(1)} %get-tuple-element.61), channel_id=1, source_target_pairs={{0,7},{1,6},{2,5},{3,4},{4,3},{5,2},{6,1},{7,0},{8,15},{9,14},{10,... | collective-permute-start | bytes 393224 | tf_op jit(solution)/shard_map/ppermute | solution.py:287
  7.9 0.6 dynamic_slice.14
  9.2 0.6 dynamic_slice.12
  10.5 1.3 collective-permute-start.5
  11.7 3.4 %collective-permute-start.6 = (bf16[2,128,256]{2,1,0:T(8,128)(2,1)S(1)}, bf16[2,128,256]{2,1,0:T(8,128)(2,1)S(1)}, u32[]{:S(2)}, u32[]{:S(2)}) collective-permute-start(bf16[2,128,256]{2,1,0:T(8,128)(2,1)S(1)} %get-tuple-element.57), channel_id=1, source_target_pairs={{0,3},{1,2},{2,1},{3,0},{4,7},{5,6},{6,5},{7,4},{8,11},{9,10},{10,... | collective-permute-start | bytes 393224 | tf_op jit(solution)/shard_map/ppermute | solution.py:287
  15.2 0.1 pad_maximum_fusion
  15.6 0.1 broadcast_add_fusion.2
  15.7 0.3 collective-permute-done.10.refs_7_
  16.0 1.8 %collective-permute-start.7 = (bf16[2,128,256]{2,1,0:T(8,128)(2,1)S(1)}, bf16[2,128,256]{2,1,0:T(8,128)(2,1)S(1)}, u32[]{:S(2)}, u32[]{:S(2)}) collective-permute-start(bf16[2,128,256]{2,1,0:T(8,128)(2,1)S(1)} %get-tuple-element.58), channel_id=1, source_target_pairs={{0,4},{1,5},{2,6},{3,7},{4,0},{5,1},{6,2},{7,3},{8,12},{9,13},{10,... | collective-permute-start | bytes 393224 | tf_op jit(solution)/shard_map/ppermute | solution.py:287
  17.8 0.5 collective-permute-start.8
  18.3 1.0 collective-permute-start.9
  19.3 6.2 %shard_map.74 = bf16[8,2,128,256]{3,2,1,0:T(8,128)(2,1)} custom-call(s32[2]{0:T(128)S(1)} %pad_add_fusion.place.source, f32[2,512,512]{2,1,0:T(8,128)} %bitcast.13, bf16[3,64,512]{2,1,0:T(8,128)(2,1)S(1)} %copy-done.1, bf16[3,64,512]{2,1,0:T(8,128)(2,1)S(1)} %collective-permute-done.refs_1_, bf16[3,64,512]{2,1,0:T(8,128)(2,1)S(1)} %collective-permute-done.1.refs_2_, ...), custom_call_target="tpu_custom_call" | custom-call | flops 3221225472 | bytes 4194304 | tf_op jit(solution)/shard_map/pallas_call | solution.py:42
  25.6 1.6 %collective-permute-done.8.refs_5_ = bf16[2,128,256]{2,1,0:T(8,128)(2,1)S(1)} collective-permute-done((bf16[2,128,256]{2,1,0:T(8,128)(2,1)S(1)}, bf16[2,128,256]{2,1,0:T(8,128)(2,1)S(1)}, u32[]{:S(2)}, u32[]{:S(2)}) %collective-permute-start.8) | collective-permute-done | bytes 131104 | tf_op jit(solution)/shard_map/ppermute | solution.py:287
  27.2 0.7 shard_map.75
  27.9 1.4 collective-permute-start.11
  29.3 2.3 %collective-permute-start.12 = (bf16[2,2,64,256]{3,2,1,0:T(8,128)(2,1)S(1)}, bf16[2,2,64,256]{3,2,1,0:T(8,128)(2,1)S(1)}, u32[]{:S(2)}, u32[]{:S(2)}) collective-permute-start(bf16[2,2,64,256]{3,2,1,0:T(8,128)(2,1)S(1)} %get-tuple-element.64), channel_id=1, source_target_pairs={{0,16},{8,24},{16,0},{24,8},{1,17},{9,25},{17,1},{25,9},{2,18},{10... | collective-permute-start | bytes 393224 | tf_op jit(solution)/shard_map/ppermute | solution.py:307
  31.7 4.8 %all-to-all-start = ((bf16[8,2,128,256]{3,2,1,0:T(8,128)(2,1)}), bf16[8,2,128,256]{3,2,1,0:T(8,128)(2,1)S(1)}, u32[]{:S(2)}, u32[]{:S(2)}) async-start(bf16[8,2,128,256]{3,2,1,0:T(8,128)(2,1)} %shard_map.74), calls=%async_computation | async-start | bytes 2097152 | tf_op jit(solution)/shard_map/all_to_all | solution.py:281
  36.5 0.4 collective-permute-start.17
  36.9 3.2 %collective-permute-start.18 = (bf16[2,2,64,256]{3,2,1,0:T(8,128)(2,1)S(1)}, bf16[2,2,64,256]{3,2,1,0:T(8,128)(2,1)S(1)}, u32[]{:S(2)}, u32[]{:S(2)}) collective-permute-start(bf16[2,2,64,256]{3,2,1,0:T(8,128)(2,1)S(1)} %get-tuple-element.76), channel_id=1, source_target_pairs={{0,16},{8,24},{16,0},{24,8},{1,17},{9,25},{17,1},{25,9},{2,18},{10... | collective-permute-start | bytes 393224 | tf_op jit(solution)/shard_map/ppermute | solution.py:307
  40.1 0.6 collective-permute-done.13.refs_3_
  40.7 1.2 shard_map.76.place
  41.9 8.4 %all-to-all-done.ladder = bf16[8,2,128,256]{3,2,1,0:T(8,128)(2,1)S(1)} async-done(((bf16[8,2,128,256]{3,2,1,0:T(8,128)(2,1)}), bf16[8,2,128,256]{3,2,1,0:T(8,128)(2,1)S(1)}, u32[]{:S(2)}, u32[]{:S(2)}) %all-to-all-start) | async-done | bytes 1048608 | tf_op jit(solution)/shard_map/all_to_all | solution.py:281
  50.3 0.6 copy-done.22
  50.9 1.6 %shard_map.77 = (bf16[2,2,64,256]{3,2,1,0:T(8,128)(2,1)S(1)}, bf16[2,2,64,256]{3,2,1,0:T(8,128)(2,1)S(1)}, bf16[2,2,64,256]{3,2,1,0:T(8,128)(2,1)S(1)}, bf16[2,2,64,256]{3,2,1,0:T(8,128)(2,1)S(1)}) custom-call(s32[2]{0:T(128)S(1)} %copy-done.22, f32[8,8]{1,0:T(8,128)S(1)} %convert_element_type.3.fock, bf16[8,2,128,256]{3,2,1,0:T(8,128)(2,1)S(1)} %all-to-all-done.ladder, ...), custom_call_target="tpu_custom_call" | custom-call | flops 30000001024 | bytes 3145728 | tf_op jit(solution)/shard_map/pallas_call | solution.py:42
  52.5 0.5 collective-permute-start.14
  52.9 3.2 %collective-permute-start.15 = (bf16[2,2,64,256]{3,2,1,0:T(8,128)(2,1)S(1)}, bf16[2,2,64,256]{3,2,1,0:T(8,128)(2,1)S(1)}, u32[]{:S(2)}, u32[]{:S(2)}) collective-permute-start(bf16[2,2,64,256]{3,2,1,0:T(8,128)(2,1)S(1)} %get-tuple-element.69.refs_2_), channel_id=1, source_target_pairs={{0,16},{8,24},{16,0},{24,8},{1,17},{9,25},{17,1},{25,9},{2,18},{10... | collective-permute-start | bytes 393224 | tf_op jit(solution)/shard_map/ppermute | solution.py:307
  56.2 1.6 %shard_map.79 = (bf16[2,2,64,256]{3,2,1,0:T(8,128)(2,1)S(1)}, bf16[2,2,64,256]{3,2,1,0:T(8,128)(2,1)S(1)}, bf16[2,2,64,256]{3,2,1,0:T(8,128)(2,1)S(1)}, bf16[2,2,64,256]{3,2,1,0:T(8,128)(2,1)S(1)}) custom-call(s32[2]{0:T(128)S(1)} %copy-done.10, f32[8,8]{1,0:T(8,128)S(1)} %convert_element_type.3.fock, bf16[8,2,128,256]{3,2,1,0:T(8,128)(2,1)S(1)} %all-to-all-done.ladder, ...), custom_call_target="tpu_custom_call" | custom-call | flops 30000001024 | bytes 3145728 | tf_op jit(solution)/shard_map/pallas_call | solution.py:42
  57.8 0.3 collective-permute-start.20
  58.1 3.3 %collective-permute-start.21 = (bf16[2,2,64,256]{3,2,1,0:T(8,128)(2,1)S(1)}, bf16[2,2,64,256]{3,2,1,0:T(8,128)(2,1)S(1)}, u32[]{:S(2)}, u32[]{:S(2)}) collective-permute-start(bf16[2,2,64,256]{3,2,1,0:T(8,128)(2,1)S(1)} %get-tuple-element.80.refs_5_), channel_id=1, source_target_pairs={{0,16},{8,24},{16,0},{24,8},{1,17},{9,25},{17,1},{25,9},{2,18},{10... | collective-permute-start | bytes 393224 | tf_op jit(solution)/shard_map/ppermute | solution.py:307
  61.4 0.6 collective-permute-start.22
  62.0 1.8 %collective-permute-done.16.refs_7_ = bf16[2,2,64,256]{3,2,1,0:T(8,128)(2,1)S(1)} collective-permute-done((bf16[2,2,64,256]{3,2,1,0:T(8,128)(2,1)S(1)}, bf16[2,2,64,256]{3,2,1,0:T(8,128)(2,1)S(1)}, u32[]{:S(2)}, u32[]{:S(2)}) %collective-permute-start.16) | collective-permute-done | bytes 131104 | tf_op jit(solution)/shard_map/ppermute | solution.py:307
  63.7 2.4 %shard_map.78 = (bf16[8,2,64,256]{3,2,1,0:T(8,128)(2,1)S(1)}, bf16[8,2,64,256]{3,2,1,0:T(8,128)(2,1)S(1)}, bf16[8,2,64,256]{3,2,1,0:T(8,128)(2,1)S(1)}) custom-call(s32[2]{0:T(128)S(1)} %copy-done.10, f32[8,8]{1,0:T(8,128)S(1)} %convert_element_type.3.fock, f32[8]{0:T(128)S(1)} %copy-done.19, f32[128,256]{1,0:T(8,128)S(1)} %maximum_select_fusion.sums, ...), custom_call_target="tpu_custom_call" | custom-call | flops 30000001024 | bytes 5242880 | tf_op jit(solution)/shard_map/pallas_call | solution.py:42
  66.2 0.8 copy-done.20
  67.0 0.8 copy-done.21
  67.8 7.9 %collective-permute-done.21.refs_9_ = bf16[2,2,64,256]{3,2,1,0:T(8,128)(2,1)S(1)} collective-permute-done((bf16[2,2,64,256]{3,2,1,0:T(8,128)(2,1)S(1)}, bf16[2,2,64,256]{3,2,1,0:T(8,128)(2,1)S(1)}, u32[]{:S(2)}, u32[]{:S(2)}) %collective-permute-start.21) | collective-permute-done | bytes 131104 | tf_op jit(solution)/shard_map/ppermute | solution.py:307
  75.7 4.3 %shard_map.80 = (bf16[8,2,128,256]{3,2,1,0:T(8,128)(2,1)}, bf16[2,128,256]{2,1,0:T(8,128)(2,1)S(1)}, bf16[2,128,256]{2,1,0:T(8,128)(2,1)S(1)}, bf16[2,128,256]{2...) custom-call(s32[2]{0:T(128)S(1)} %copy-done.10, ...), custom_call_target="tpu_custom_call" | custom-call | flops 30000001024 | bytes 5242880 | tf_op jit(solution)/shard_map/pallas_call | solution.py:42
  80.1 0.6 copy-done.15
  80.7 0.6 copy-done.16
  81.4 0.6 copy-done.17
  82.0 0.6 copy-done.18
  82.7 7.6 %all-to-all-start.1 = ((bf16[8,2,128,256]{3,2,1,0:T(8,128)(2,1)}), bf16[8,2,128,256]{3,2,1,0:T(8,128)(2,1)S(1)}, u32[]{:S(2)}, u32[]{:S(2)}) async-start(bf16[8,2,128,256]{3,2,1,0:T(8,128)(2,1)} %get-tuple-element.82), calls=%async_computation.1 | async-start | bytes 2097152 | tf_op jit(solution)/shard_map/all_to_all | solution.py:281
  90.3 0.4 collective-permute-start.23
  90.6 1.8 %collective-permute-start.25 = (bf16[2,128,256]{2,1,0:T(8,128)(2,1)S(1)}, bf16[2,128,256]{2,1,0:T(8,128)(2,1)S(1)}, u32[]{:S(2)}, u32[]{:S(2)}) collective-permute-start(bf16[2,128,256]{2,1,0:T(8,128)(2,1)S(1)} %get-tuple-element.86), channel_id=1, source_target_pairs={{0,3},{1,2},{2,1},{3,0},{4,7},{5,6},{6,5},{7,4},{8,11},{9,10},{10,... | collective-permute-start | bytes 393224 | tf_op jit(solution)/shard_map/ppermute | solution.py:287
  92.4 1.2 collective-permute-start.26
  93.6 0.5 collective-permute-start.27
  94.1 1.2 collective-permute-start.28
  95.3 10.4 %collective-permute-done.24.refs_2_ = bf16[2,128,256]{2,1,0:T(8,128)(2,1)S(1)} collective-permute-done((bf16[2,128,256]{2,1,0:T(8,128)(2,1)S(1)}, bf16[2,128,256]{2,1,0:T(8,128)(2,1)S(1)}, u32[]{:S(2)}, u32[]{:S(2)}) %collective-permute-start.24) | collective-permute-done | bytes 131104 | tf_op jit(solution)/shard_map/ppermute | solution.py:287
  105.8 3.2 %collective-permute-start.29 = (bf16[2,128,256]{2,1,0:T(8,128)(2,1)S(1)}, bf16[2,128,256]{2,1,0:T(8,128)(2,1)S(1)}, u32[]{:S(2)}, u32[]{:S(2)}) collective-permute-start(bf16[2,128,256]{2,1,0:T(8,128)(2,1)S(1)} %get-tuple-element.90), channel_id=1, source_target_pairs={{0,7},{1,6},{2,5},{3,4},{4,3},{5,2},{6,1},{7,0},{8,15},{9,14},{10,... | collective-permute-start | bytes 393224 | tf_op jit(solution)/shard_map/ppermute | solution.py:287
  109.0 5.9 %collective-permute-start.30 = (bf16[2,128,256]{2,1,0:T(8,128)(2,1)}, bf16[2,128,256]{2,1,0:T(8,128)(2,1)S(1)}, u32[]{:S(2)}, u32[]{:S(2)}) collective-permute-start(bf16[2,128,256]{2,1,0:T(8,128)(2,1)} %get-tuple-element.91), channel_id=1, source_target_pairs={{0,0},{1,1},{2,8},{3,9},{4,16},{5,17},{6,24},{7,25},{8,2},{9,3},{1... | collective-permute-start | bytes 393224 | tf_op jit(solution)/shard_map/ppermute | solution.py:297
  115.0 3.1 %collective-permute-start.33 = (bf16[2,128,256]{2,1,0:T(8,128)(2,1)}, bf16[2,128,256]{2,1,0:T(8,128)(2,1)S(1)}, u32[]{:S(2)}, u32[]{:S(2)}) collective-permute-start(bf16[2,128,256]{2,1,0:T(8,128)(2,1)} %get-tuple-element.94), channel_id=1, source_target_pairs={{0,9},{1,8},{2,1},{3,0},{4,25},{5,24},{6,17},{7,16},{8,11},{9,10},... | collective-permute-start | bytes 393224 | tf_op jit(solution)/shard_map/ppermute | solution.py:297
  118.1 4.5 %collective-permute-start.34 = (bf16[2,128,256]{2,1,0:T(8,128)(2,1)}, bf16[2,128,256]{2,1,0:T(8,128)(2,1)S(1)}, u32[]{:S(2)}, u32[]{:S(2)}) collective-permute-start(bf16[2,128,256]{2,1,0:T(8,128)(2,1)} %copy-done.18), channel_id=1, source_target_pairs={{0,16},{1,17},{2,24},{3,25},{4,0},{5,1},{6,8},{7,9},{8,18},{9,19},... | collective-permute-start | bytes 393224 | tf_op jit(solution)/shard_map/ppermute | solution.py:297
  122.7 2.9 %collective-permute-done.30.refs_8_ = bf16[2,128,256]{2,1,0:T(8,128)(2,1)S(1)} collective-permute-done((bf16[2,128,256]{2,1,0:T(8,128)(2,1)}, bf16[2,128,256]{2,1,0:T(8,128)(2,1)S(1)}, u32[]{:S(2)}, u32[]{:S(2)}) %collective-permute-start.30) | collective-permute-done | bytes 131104 | tf_op jit(solution)/shard_map/ppermute | solution.py:297
  125.6 3.3 %collective-permute-done.31.refs_9_ = bf16[2,128,256]{2,1,0:T(8,128)(2,1)S(1)} collective-permute-done((bf16[2,128,256]{2,1,0:T(8,128)(2,1)}, bf16[2,128,256]{2,1,0:T(8,128)(2,1)S(1)}, u32[]{:S(2)}, u32[]{:S(2)}) %collective-permute-start.31) | collective-permute-done | bytes 131104 | tf_op jit(solution)/shard_map/ppermute | solution.py:297
  128.9 4.5 %collective-permute-start.36 = (bf16[2,128,256]{2,1,0:T(8,128)(2,1)}, bf16[2,128,256]{2,1,0:T(8,128)(2,1)}, u32[]{:S(2)}, u32[]{:S(2)}) collective-permute-start(bf16[2,128,256]{2,1,0:T(8,128)(2,1)} %copy-done.16), channel_id=1, source_target_pairs={{0,24},{1,25},{2,16},{3,17},{4,8},{5,9},{6,0},{7,1},{8,26},{9,27},... | collective-permute-start | bytes 393224 | tf_op jit(solution)/shard_map/ppermute | solution.py:297
  133.3 4.9 %collective-permute-start.37 = (bf16[2,128,256]{2,1,0:T(8,128)(2,1)}, bf16[2,128,256]{2,1,0:T(8,128)(2,1)}, u32[]{:S(2)}, u32[]{:S(2)}) collective-permute-start(bf16[2,128,256]{2,1,0:T(8,128)(2,1)} %copy-done.15), channel_id=1, source_target_pairs={{0,25},{1,24},{2,17},{3,16},{4,9},{5,8},{6,1},{7,0},{8,27},{9,26},... | collective-permute-start | bytes 393224 | tf_op jit(solution)/shard_map/ppermute | solution.py:297
  138.2 0.1 broadcast_in_dim.4.row
  138.4 1.1 copy-done.14
  139.5 8.6 %shard_map.81.source = f32[2,512,512]{2,1,0:T(8,128)} custom-call(s32[2]{0:T(128)S(1)} %copy-done.10, f32[8]{0:T(128)S(1)} %copy-done.19, f32[2,512,512]{2,1,0:T(8,128)} %bitcast.14, bf16[8,2,128,256]{3,2,1,0:T(8,128)(2,1)S(1)} %all-to-all-done.1.blocks, f32[512,128]{1,0:T(8,128)S(1)} %broadcast_in_dim.4.row, f32[1,512]{1,0:T(1,128)S(1)} %bitcast.20, ...), custom_call_target="tpu_custom_call" | custom-call | flops 3221225472 | bytes 6291456 | tf_op jit(solution)/shard_map/pallas_call | solution.py:42
  148.1 3.0 %collective-permute-done.37.refs_15_ = bf16[2,128,256]{2,1,0:T(8,128)(2,1)} collective-permute-done((bf16[2,128,256]{2,1,0:T(8,128)(2,1)}, bf16[2,128,256]{2,1,0:T(8,128)(2,1)}, u32[]{:S(2)}, u32[]{:S(2)}) %collective-permute-start.37) | collective-permute-done | bytes 131104 | tf_op jit(solution)/shard_map/ppermute | solution.py:297
  151.2 2.9 %shard_map.82 = f32[2,512,512]{2,1,0:T(8,128)} custom-call(s32[2]{0:T(128)S(1)} %copy-done.10, f32[2,512,512]{2,1,0:T(8,128)} %shard_map.81.source, bf16[2,128,256]{2,1,0:T(8,128)(2,1)S(1)} %get-tuple-element.83.refs_0_, bf16[2,128,256]{2,1,0:T(8,128)(2,1)S(1)} %collective-permute-done.23.refs_1_, ...), custom_call_target="tpu_custom_call", output_to_operand_aliasing={{}: (1, {})} | custom-call | flops 524288 | bytes 5242880 | tf_op jit(solution)/shard_map/pallas_call | solution.py:426
  (90 shorter events, 0.8 us)
Async XLA Ops:
  0.0 7.9 %copy-start.25 = (s32[8]{0:T(128)S(1)}, s32[8]{0:T(128)}, u32[]{:S(2)}) copy-start(s32[8]{0:T(128)} %constant.25.clone) | copy-start | bytes 100
  0.0 9.2 %copy-start.24 = (s32[8]{0:T(128)S(1)}, s32[8]{0:T(128)}, u32[]{:S(2)}) copy-start(s32[8]{0:T(128)} %constant.24.clone) | copy-start | bytes 100
  0.0 15.3 %copy-start.11 = (f32[512]{0:T(512)S(1)}, f32[512]{0:T(512)}, u32[]{:S(2)}) copy-start(f32[512]{0:T(512)} %param.11) | copy-start | bytes 6148
  0.0 10.4 %collective-permute-start = (bf16[3,64,512]{2,1,0:T(8,128)(2,1)}, bf16[3,64,512]{2,1,0:T(8,128)(2,1)S(1)}, u32[]{:S(2)}, u32[]{:S(2)}) collective-permute-start(bf16[3,64,512]{2,1,0:T(8,128)(2,1)} %refs_0_.3), channel_id=1, source_target_pairs={{0,2},{1,3},{2,0},{3,1},{4,6},{5,7},{6,4},{7,5},{8,10},{9,11},{10,... | collective-permute-start | bytes 589832 | tf_op jit(solution)/shard_map/ppermute | solution.py:333
  0.1 11.7 %collective-permute-start.1 = (bf16[3,64,512]{2,1,0:T(8,128)(2,1)}, bf16[3,64,512]{2,1,0:T(8,128)(2,1)S(1)}, u32[]{:S(2)}, u32[]{:S(2)}) collective-permute-start(bf16[3,64,512]{2,1,0:T(8,128)(2,1)} %refs_0_.3), channel_id=1, source_target_pairs={{0,4},{1,5},{2,6},{3,7},{4,0},{5,1},{6,2},{7,3},{8,12},{9,13},{10,... | collective-permute-start | bytes 589832 | tf_op jit(solution)/shard_map/ppermute | solution.py:333
  1.6 13.6 %collective-permute-start.2 = (bf16[3,64,512]{2,1,0:T(8,128)(2,1)}, bf16[3,64,512]{2,1,0:T(8,128)(2,1)S(1)}, u32[]{:S(2)}, u32[]{:S(2)}) collective-permute-start(bf16[3,64,512]{2,1,0:T(8,128)(2,1)} %refs_0_.3), channel_id=1, source_target_pairs={{0,6},{1,7},{2,4},{3,5},{4,2},{5,3},{6,0},{7,1},{8,14},{9,15},{10,... | collective-permute-start | bytes 589832 | tf_op jit(solution)/shard_map/ppermute | solution.py:333
  2.8 24.4 %copy-start.9 = (s32[2]{0:T(128)}, s32[2]{0:T(128)S(1)}, u32[]{:S(2)}) copy-start(s32[2]{0:T(128)S(1)} %pad_add_fusion.place.source) | copy-start | bytes 28
  2.8 1.6 %copy-start = (f32[2,1,512,512]{3,2,1,0:T(8,128)S(1)}, f32[2,1,512,512]{3,2,1,0:T(8,128)}, u32[]{:S(2)}) copy-start(f32[2,1,512,512]{3,2,1,0:T(8,128)} %param.7) | copy-start | bytes 6291460
  4.4 10.8 %copy-start.1 = (bf16[3,64,512]{2,1,0:T(8,128)(2,1)S(1)}, bf16[3,64,512]{2,1,0:T(8,128)(2,1)}, u32[]{:S(2)}) copy-start(bf16[3,64,512]{2,1,0:T(8,128)(2,1)} %refs_0_.3) | copy-start | bytes 589828
  5.3 10.8 %collective-permute-start.10 = (bf16[2,128,256]{2,1,0:T(8,128)(2,1)S(1)}, bf16[2,128,256]{2,1,0:T(8,128)(2,1)S(1)}, u32[]{:S(2)}, u32[]{:S(2)}) collective-permute-start(bf16[2,128,256]{2,1,0:T(8,128)(2,1)S(1)} %get-tuple-element.61), channel_id=1, source_target_pairs={{0,7},{1,6},{2,5},{3,4},{4,3},{5,2},{6,1},{7,0},{8,15},{9,14},{10,... | collective-permute-start | bytes 393224 | tf_op jit(solution)/shard_map/ppermute | solution.py:287
  7.9 9.9 %collective-permute-start.4 = (bf16[2,128,256]{2,1,0:T(8,128)(2,1)S(1)}, bf16[2,128,256]{2,1,0:T(8,128)(2,1)S(1)}, u32[]{:S(2)}, u32[]{:S(2)}) collective-permute-start(bf16[2,128,256]{2,1,0:T(8,128)(2,1)S(1)} %get-tuple-element.55), channel_id=1, source_target_pairs={{0,1},{1,0},{2,3},{3,2},{4,5},{5,4},{6,7},{7,6},{8,9},{9,8},{10,11... | collective-permute-start | bytes 393224 | tf_op jit(solution)/shard_map/ppermute | solution.py:287
  10.5 15.1 %copy-start.3 = (bf16[3,64,512]{2,1,0:T(8,128)(2,1)}, bf16[3,64,512]{2,1,0:T(8,128)(2,1)S(1)}, u32[]{:S(2)}) copy-start(bf16[3,64,512]{2,1,0:T(8,128)(2,1)S(1)} %collective-permute-done.refs_1_) | copy-start | bytes 589828
  10.5 15.1 %collective-permute-start.5 = (bf16[2,128,256]{2,1,0:T(8,128)(2,1)S(1)}, bf16[2,128,256]{2,1,0:T(8,128)(2,1)S(1)}, u32[]{:S(2)}, u32[]{:S(2)}) collective-permute-start(bf16[2,128,256]{2,1,0:T(8,128)(2,1)S(1)} %get-tuple-element.56), channel_id=1, source_target_pairs={{0,2},{1,3},{2,0},{3,1},{4,6},{5,7},{6,4},{7,5},{8,10},{9,11},{10,... | collective-permute-start | bytes 393224 | tf_op jit(solution)/shard_map/ppermute | solution.py:287
  11.7 13.8 %copy-start.5 = (bf16[3,64,512]{2,1,0:T(8,128)(2,1)}, bf16[3,64,512]{2,1,0:T(8,128)(2,1)S(1)}, u32[]{:S(2)}) copy-start(bf16[3,64,512]{2,1,0:T(8,128)(2,1)S(1)} %collective-permute-done.1.refs_2_) | copy-start | bytes 589828
  11.7 13.8 %collective-permute-start.6 = (bf16[2,128,256]{2,1,0:T(8,128)(2,1)S(1)}, bf16[2,128,256]{2,1,0:T(8,128)(2,1)S(1)}, u32[]{:S(2)}, u32[]{:S(2)}) collective-permute-start(bf16[2,128,256]{2,1,0:T(8,128)(2,1)S(1)} %get-tuple-element.57), channel_id=1, source_target_pairs={{0,3},{1,2},{2,1},{3,0},{4,7},{5,6},{6,5},{7,4},{8,11},{9,10},{10,... | collective-permute-start | bytes 393224 | tf_op jit(solution)/shard_map/ppermute | solution.py:287
  15.2 10.4 %copy-start.7 = (bf16[3,64,512]{2,1,0:T(8,128)(2,1)}, bf16[3,64,512]{2,1,0:T(8,128)(2,1)S(1)}, u32[]{:S(2)}) copy-start(bf16[3,64,512]{2,1,0:T(8,128)(2,1)S(1)} %collective-permute-done.2.refs_3_) | copy-start | bytes 589828
  15.3 3.0 %collective-permute-start.3 = (bf16[4,3,64,512]{3,2,1,0:T(8,128)(2,1)S(1)}, bf16[4,3,64,512]{3,2,1,0:T(8,128)(2,1)S(1)}, u32[]{:S(2)}, u32[]{:S(2)}) collective-permute-start(bf16[4,3,64,512]{3,2,1,0:T(8,128)(2,1)S(1)} %pad_maximum_fusion), channel_id=1, source_target_pairs={{0,1},{1,0},{2,3},{3,2},{4,5},{5,4},{6,7},{7,6},{8,9},{9,8},{10,11... | collective-permute-start | bytes 2359304 | tf_op jit(solution)/shard_map/ppermute | solution.py:333
  16.0 9.5 %collective-permute-start.7 = (bf16[2,128,256]{2,1,0:T(8,128)(2,1)S(1)}, bf16[2,128,256]{2,1,0:T(8,128)(2,1)S(1)}, u32[]{:S(2)}, u32[]{:S(2)}) collective-permute-start(bf16[2,128,256]{2,1,0:T(8,128)(2,1)S(1)} %get-tuple-element.58), channel_id=1, source_target_pairs={{0,4},{1,5},{2,6},{3,7},{4,0},{5,1},{6,2},{7,3},{8,12},{9,13},{10,... | collective-permute-start | bytes 393224 | tf_op jit(solution)/shard_map/ppermute | solution.py:287
  17.8 9.4 %collective-permute-start.8 = (bf16[2,128,256]{2,1,0:T(8,128)(2,1)S(1)}, bf16[2,128,256]{2,1,0:T(8,128)(2,1)S(1)}, u32[]{:S(2)}, u32[]{:S(2)}) collective-permute-start(bf16[2,128,256]{2,1,0:T(8,128)(2,1)S(1)} %get-tuple-element.59), channel_id=1, source_target_pairs={{0,5},{1,4},{2,7},{3,6},{4,1},{5,0},{6,3},{7,2},{8,13},{9,12},{10,... | collective-permute-start | bytes 393224 | tf_op jit(solution)/shard_map/ppermute | solution.py:287
  18.3 7.3 %copy-start.13 = (bf16[4,3,64,512]{3,2,1,0:T(8,128)(2,1)}, bf16[4,3,64,512]{3,2,1,0:T(8,128)(2,1)S(1)}, u32[]{:S(2)}) copy-start(bf16[4,3,64,512]{3,2,1,0:T(8,128)(2,1)S(1)} %collective-permute-done.3.refs_4_) | copy-start | bytes 2359300
  18.3 13.4 %copy-start.23 = (bf16[8,8]{1,0:T(8,128)(2,1)S(1)}, bf16[8,8]{1,0:T(8,128)(2,1)}, u32[]{:S(2)}) copy-start(bf16[8,8]{1,0:T(8,128)(2,1)} %param.9) | copy-start | bytes 388
  18.3 8.9 %collective-permute-start.9 = (bf16[2,128,256]{2,1,0:T(8,128)(2,1)S(1)}, bf16[2,128,256]{2,1,0:T(8,128)(2,1)S(1)}, u32[]{:S(2)}, u32[]{:S(2)}) collective-permute-start(bf16[2,128,256]{2,1,0:T(8,128)(2,1)S(1)} %get-tuple-element.60), channel_id=1, source_target_pairs={{0,6},{1,7},{2,4},{3,5},{4,2},{5,3},{6,0},{7,1},{8,14},{9,15},{10,... | collective-permute-start | bytes 393224 | tf_op jit(solution)/shard_map/ppermute | solution.py:287
  27.9 12.2 %collective-permute-start.11 = (bf16[2,2,64,256]{3,2,1,0:T(8,128)(2,1)S(1)}, bf16[2,2,64,256]{3,2,1,0:T(8,128)(2,1)S(1)}, u32[]{:S(2)}, u32[]{:S(2)}) collective-permute-start(bf16[2,2,64,256]{3,2,1,0:T(8,128)(2,1)S(1)} %get-tuple-element.63), channel_id=1, source_target_pairs={{0,8},{8,0},{16,24},{24,16},{1,9},{9,1},{17,25},{25,17},{2,10},{10... | collective-permute-start | bytes 393224 | tf_op jit(solution)/shard_map/ppermute | solution.py:307
  29.3 10.8 %collective-permute-start.12 = (bf16[2,2,64,256]{3,2,1,0:T(8,128)(2,1)S(1)}, bf16[2,2,64,256]{3,2,1,0:T(8,128)(2,1)S(1)}, u32[]{:S(2)}, u32[]{:S(2)}) collective-permute-start(bf16[2,2,64,256]{3,2,1,0:T(8,128)(2,1)S(1)} %get-tuple-element.64), channel_id=1, source_target_pairs={{0,16},{8,24},{16,0},{24,8},{1,17},{9,25},{17,1},{25,9},{2,18},{10... | collective-permute-start | bytes 393224 | tf_op jit(solution)/shard_map/ppermute | solution.py:307
  31.6 9.1 %collective-permute-start.13 = (bf16[2,2,64,256]{3,2,1,0:T(8,128)(2,1)S(1)}, bf16[2,2,64,256]{3,2,1,0:T(8,128)(2,1)S(1)}, u32[]{:S(2)}, u32[]{:S(2)}) collective-permute-start(bf16[2,2,64,256]{3,2,1,0:T(8,128)(2,1)S(1)} %get-tuple-element.65), channel_id=1, source_target_pairs={{0,24},{8,16},{16,8},{24,0},{1,25},{9,17},{17,9},{25,1},{2,26},{10... | collective-permute-start | bytes 393224 | tf_op jit(solution)/shard_map/ppermute | solution.py:307
  31.7 18.6 %all-to-all-start = ((bf16[8,2,128,256]{3,2,1,0:T(8,128)(2,1)}), bf16[8,2,128,256]{3,2,1,0:T(8,128)(2,1)S(1)}, u32[]{:S(2)}, u32[]{:S(2)}) async-start(bf16[8,2,128,256]{3,2,1,0:T(8,128)(2,1)} %shard_map.74), calls=%async_computation | async-start | bytes 2097152 | tf_op jit(solution)/shard_map/all_to_all | solution.py:281
  36.5 19.7 %collective-permute-start.17 = (bf16[2,2,64,256]{3,2,1,0:T(8,128)(2,1)S(1)}, bf16[2,2,64,256]{3,2,1,0:T(8,128)(2,1)S(1)}, u32[]{:S(2)}, u32[]{:S(2)}) collective-permute-start(bf16[2,2,64,256]{3,2,1,0:T(8,128)(2,1)S(1)} %get-tuple-element.75), channel_id=1, source_target_pairs={{0,8},{8,0},{16,24},{24,16},{1,9},{9,1},{17,25},{25,17},{2,10},{10... | collective-permute-start | bytes 393224 | tf_op jit(solution)/shard_map/ppermute | solution.py:307
  36.9 19.3 %collective-permute-start.18 = (bf16[2,2,64,256]{3,2,1,0:T(8,128)(2,1)S(1)}, bf16[2,2,64,256]{3,2,1,0:T(8,128)(2,1)S(1)}, u32[]{:S(2)}, u32[]{:S(2)}) collective-permute-start(bf16[2,2,64,256]{3,2,1,0:T(8,128)(2,1)S(1)} %get-tuple-element.76), channel_id=1, source_target_pairs={{0,16},{8,24},{16,0},{24,8},{1,17},{9,25},{17,1},{25,9},{2,18},{10... | collective-permute-start | bytes 393224 | tf_op jit(solution)/shard_map/ppermute | solution.py:307
  40.1 16.1 %collective-permute-start.19 = (bf16[2,2,64,256]{3,2,1,0:T(8,128)(2,1)S(1)}, bf16[2,2,64,256]{3,2,1,0:T(8,128)(2,1)S(1)}, u32[]{:S(2)}, u32[]{:S(2)}) collective-permute-start(bf16[2,2,64,256]{3,2,1,0:T(8,128)(2,1)S(1)} %get-tuple-element.77), channel_id=1, source_target_pairs={{0,24},{8,16},{16,8},{24,0},{1,25},{9,17},{17,9},{25,1},{2,26},{10... | collective-permute-start | bytes 393224 | tf_op jit(solution)/shard_map/ppermute | solution.py:307
  41.9 14.3 %copy-start.10 = (s32[2]{0:T(128)S(1)}, s32[2]{0:T(128)}, u32[]{:S(2)}) copy-start(s32[2]{0:T(128)} %copy-done.9) | copy-start | bytes 28
  52.5 8.9 %collective-permute-start.14 = (bf16[2,2,64,256]{3,2,1,0:T(8,128)(2,1)S(1)}, bf16[2,2,64,256]{3,2,1,0:T(8,128)(2,1)S(1)}, u32[]{:S(2)}, u32[]{:S(2)}) collective-permute-start(bf16[2,2,64,256]{3,2,1,0:T(8,128)(2,1)S(1)} %get-tuple-element.68.refs_1_), channel_id=1, source_target_pairs={{0,8},{8,0},{16,24},{24,16},{1,9},{9,1},{17,25},{25,17},{2,10},{10... | collective-permute-start | bytes 393224 | tf_op jit(solution)/shard_map/ppermute | solution.py:307
  52.9 9.0 %collective-permute-start.15 = (bf16[2,2,64,256]{3,2,1,0:T(8,128)(2,1)S(1)}, bf16[2,2,64,256]{3,2,1,0:T(8,128)(2,1)S(1)}, u32[]{:S(2)}, u32[]{:S(2)}) collective-permute-start(bf16[2,2,64,256]{3,2,1,0:T(8,128)(2,1)S(1)} %get-tuple-element.69.refs_2_), channel_id=1, source_target_pairs={{0,16},{8,24},{16,0},{24,8},{1,17},{9,25},{17,1},{25,9},{2,18},{10... | collective-permute-start | bytes 393224 | tf_op jit(solution)/shard_map/ppermute | solution.py:307
  56.2 7.6 %collective-permute-start.16 = (bf16[2,2,64,256]{3,2,1,0:T(8,128)(2,1)S(1)}, bf16[2,2,64,256]{3,2,1,0:T(8,128)(2,1)S(1)}, u32[]{:S(2)}, u32[]{:S(2)}) collective-permute-start(bf16[2,2,64,256]{3,2,1,0:T(8,128)(2,1)S(1)} %get-tuple-element.70.refs_3_), channel_id=1, source_target_pairs={{0,24},{8,16},{16,8},{24,0},{1,25},{9,17},{17,9},{25,1},{2,26},{10... | collective-permute-start | bytes 393224 | tf_op jit(solution)/shard_map/ppermute | solution.py:307
  56.2 7.6 %copy-start.19 = (f32[8]{0:T(128)S(1)}, f32[8]{0:T(128)}, u32[]{:S(2)}) copy-start(f32[8]{0:T(128)} %occ.5) | copy-start | bytes 100
  57.8 10.0 %collective-permute-start.20 = (bf16[2,2,64,256]{3,2,1,0:T(8,128)(2,1)S(1)}, bf16[2,2,64,256]{3,2,1,0:T(8,128)(2,1)S(1)}, u32[]{:S(2)}, u32[]{:S(2)}) collective-permute-start(bf16[2,2,64,256]{3,2,1,0:T(8,128)(2,1)S(1)} %get-tuple-element.79.refs_4_), channel_id=1, source_target_pairs={{0,8},{8,0},{16,24},{24,16},{1,9},{9,1},{17,25},{25,17},{2,10},{10... | collective-permute-start | bytes 393224 | tf_op jit(solution)/shard_map/ppermute | solution.py:307
  58.1 17.6 %collective-permute-start.21 = (bf16[2,2,64,256]{3,2,1,0:T(8,128)(2,1)S(1)}, bf16[2,2,64,256]{3,2,1,0:T(8,128)(2,1)S(1)}, u32[]{:S(2)}, u32[]{:S(2)}) collective-permute-start(bf16[2,2,64,256]{3,2,1,0:T(8,128)(2,1)S(1)} %get-tuple-element.80.refs_5_), channel_id=1, source_target_pairs={{0,16},{8,24},{16,0},{24,8},{1,17},{9,25},{17,1},{25,9},{2,18},{10... | collective-permute-start | bytes 393224 | tf_op jit(solution)/shard_map/ppermute | solution.py:307
  61.4 14.3 %collective-permute-start.22 = (bf16[2,2,64,256]{3,2,1,0:T(8,128)(2,1)S(1)}, bf16[2,2,64,256]{3,2,1,0:T(8,128)(2,1)S(1)}, u32[]{:S(2)}, u32[]{:S(2)}) collective-permute-start(bf16[2,2,64,256]{3,2,1,0:T(8,128)(2,1)S(1)} %get-tuple-element.81.refs_6_), channel_id=1, source_target_pairs={{0,24},{8,16},{16,8},{24,0},{1,25},{9,17},{17,9},{25,1},{2,26},{10... | collective-permute-start | bytes 393224 | tf_op jit(solution)/shard_map/ppermute | solution.py:307
  66.2 0.8 copy-start.20
  67.0 0.8 copy-start.21
  80.1 0.7 copy-start.15
  80.7 0.7 copy-start.16
  82.0 0.6 copy-start.18
  82.7 55.6 %copy-start.12 = (f32[512]{0:T(512)S(1)}, f32[512]{0:T(512)}, u32[]{:S(2)}) copy-start(f32[512]{0:T(512)} %param.11) | copy-start | bytes 6148
  82.7 55.7 %copy-start.2 = (bf16[3,64,512]{2,1,0:T(8,128)(2,1)S(1)}, bf16[3,64,512]{2,1,0:T(8,128)(2,1)}, u32[]{:S(2)}) copy-start(bf16[3,64,512]{2,1,0:T(8,128)(2,1)} %refs_0_.3) | copy-start | bytes 589828
  82.7 55.7 %copy-start.4 = (bf16[3,64,512]{2,1,0:T(8,128)(2,1)S(1)}, bf16[3,64,512]{2,1,0:T(8,128)(2,1)}, u32[]{:S(2)}) copy-start(bf16[3,64,512]{2,1,0:T(8,128)(2,1)} %copy-done.3) | copy-start | bytes 589828
  82.7 55.7 %copy-start.6 = (bf16[3,64,512]{2,1,0:T(8,128)(2,1)S(1)}, bf16[3,64,512]{2,1,0:T(8,128)(2,1)}, u32[]{:S(2)}) copy-start(bf16[3,64,512]{2,1,0:T(8,128)(2,1)} %copy-done.5) | copy-start | bytes 589828
  82.7 55.7 %copy-start.8 = (bf16[3,64,512]{2,1,0:T(8,128)(2,1)S(1)}, bf16[3,64,512]{2,1,0:T(8,128)(2,1)}, u32[]{:S(2)}) copy-start(bf16[3,64,512]{2,1,0:T(8,128)(2,1)} %copy-done.7) | copy-start | bytes 589828
  82.7 55.6 %all-to-all-start.1 = ((bf16[8,2,128,256]{3,2,1,0:T(8,128)(2,1)}), bf16[8,2,128,256]{3,2,1,0:T(8,128)(2,1)S(1)}, u32[]{:S(2)}, u32[]{:S(2)}) async-start(bf16[8,2,128,256]{3,2,1,0:T(8,128)(2,1)} %get-tuple-element.82), calls=%async_computation.1 | async-start | bytes 2097152 | tf_op jit(solution)/shard_map/all_to_all | solution.py:281
  90.3 3.9 %collective-permute-start.23 = (bf16[2,128,256]{2,1,0:T(8,128)(2,1)S(1)}, bf16[2,128,256]{2,1,0:T(8,128)(2,1)S(1)}, u32[]{:S(2)}, u32[]{:S(2)}) collective-permute-start(bf16[2,128,256]{2,1,0:T(8,128)(2,1)S(1)} %get-tuple-element.84), channel_id=1, source_target_pairs={{0,1},{1,0},{2,3},{3,2},{4,5},{5,4},{6,7},{7,6},{8,9},{9,8},{10,11... | collective-permute-start | bytes 393224 | tf_op jit(solution)/shard_map/ppermute | solution.py:287
  90.6 15.1 %collective-permute-start.24 = (bf16[2,128,256]{2,1,0:T(8,128)(2,1)S(1)}, bf16[2,128,256]{2,1,0:T(8,128)(2,1)S(1)}, u32[]{:S(2)}, u32[]{:S(2)}) collective-permute-start(bf16[2,128,256]{2,1,0:T(8,128)(2,1)S(1)} %get-tuple-element.85), channel_id=1, source_target_pairs={{0,2},{1,3},{2,0},{3,1},{4,6},{5,7},{6,4},{7,5},{8,10},{9,11},{10,... | collective-permute-start | bytes 393224 | tf_op jit(solution)/shard_map/ppermute | solution.py:287
  90.6 18.3 %collective-permute-start.25 = (bf16[2,128,256]{2,1,0:T(8,128)(2,1)S(1)}, bf16[2,128,256]{2,1,0:T(8,128)(2,1)S(1)}, u32[]{:S(2)}, u32[]{:S(2)}) collective-permute-start(bf16[2,128,256]{2,1,0:T(8,128)(2,1)S(1)} %get-tuple-element.86), channel_id=1, source_target_pairs={{0,3},{1,2},{2,1},{3,0},{4,7},{5,6},{6,5},{7,4},{8,11},{9,10},{10,... | collective-permute-start | bytes 393224 | tf_op jit(solution)/shard_map/ppermute | solution.py:287
  92.4 22.4 %collective-permute-start.26 = (bf16[2,128,256]{2,1,0:T(8,128)(2,1)S(1)}, bf16[2,128,256]{2,1,0:T(8,128)(2,1)S(1)}, u32[]{:S(2)}, u32[]{:S(2)}) collective-permute-start(bf16[2,128,256]{2,1,0:T(8,128)(2,1)S(1)} %get-tuple-element.87), channel_id=1, source_target_pairs={{0,4},{1,5},{2,6},{3,7},{4,0},{5,1},{6,2},{7,3},{8,12},{9,13},{10,... | collective-permute-start | bytes 393224 | tf_op jit(solution)/shard_map/ppermute | solution.py:287
  93.6 21.3 %collective-permute-start.27 = (bf16[2,128,256]{2,1,0:T(8,128)(2,1)S(1)}, bf16[2,128,256]{2,1,0:T(8,128)(2,1)S(1)}, u32[]{:S(2)}, u32[]{:S(2)}) collective-permute-start(bf16[2,128,256]{2,1,0:T(8,128)(2,1)S(1)} %get-tuple-element.88), channel_id=1, source_target_pairs={{0,5},{1,4},{2,7},{3,6},{4,1},{5,0},{6,3},{7,2},{8,13},{9,12},{10,... | collective-permute-start | bytes 393224 | tf_op jit(solution)/shard_map/ppermute | solution.py:287
  94.1 20.9 %collective-permute-start.28 = (bf16[2,128,256]{2,1,0:T(8,128)(2,1)S(1)}, bf16[2,128,256]{2,1,0:T(8,128)(2,1)S(1)}, u32[]{:S(2)}, u32[]{:S(2)}) collective-permute-start(bf16[2,128,256]{2,1,0:T(8,128)(2,1)S(1)} %get-tuple-element.89), channel_id=1, source_target_pairs={{0,6},{1,7},{2,4},{3,5},{4,2},{5,3},{6,0},{7,1},{8,14},{9,15},{10,... | collective-permute-start | bytes 393224 | tf_op jit(solution)/shard_map/ppermute | solution.py:287
  105.8 12.4 %collective-permute-start.29 = (bf16[2,128,256]{2,1,0:T(8,128)(2,1)S(1)}, bf16[2,128,256]{2,1,0:T(8,128)(2,1)S(1)}, u32[]{:S(2)}, u32[]{:S(2)}) collective-permute-start(bf16[2,128,256]{2,1,0:T(8,128)(2,1)S(1)} %get-tuple-element.90), channel_id=1, source_target_pairs={{0,7},{1,6},{2,5},{3,4},{4,3},{5,2},{6,1},{7,0},{8,15},{9,14},{10,... | collective-permute-start | bytes 393224 | tf_op jit(solution)/shard_map/ppermute | solution.py:287
  109.0 16.6 %collective-permute-start.30 = (bf16[2,128,256]{2,1,0:T(8,128)(2,1)}, bf16[2,128,256]{2,1,0:T(8,128)(2,1)S(1)}, u32[]{:S(2)}, u32[]{:S(2)}) collective-permute-start(bf16[2,128,256]{2,1,0:T(8,128)(2,1)} %get-tuple-element.91), channel_id=1, source_target_pairs={{0,0},{1,1},{2,8},{3,9},{4,16},{5,17},{6,24},{7,25},{8,2},{9,3},{1... | collective-permute-start | bytes 393224 | tf_op jit(solution)/shard_map/ppermute | solution.py:297
  114.9 14.0 %collective-permute-start.31 = (bf16[2,128,256]{2,1,0:T(8,128)(2,1)}, bf16[2,128,256]{2,1,0:T(8,128)(2,1)S(1)}, u32[]{:S(2)}, u32[]{:S(2)}) collective-permute-start(bf16[2,128,256]{2,1,0:T(8,128)(2,1)} %get-tuple-element.92), channel_id=1, source_target_pairs={{0,1},{1,0},{2,9},{3,8},{4,17},{5,16},{6,25},{7,24},{8,3},{9,2},{1... | collective-permute-start | bytes 393224 | tf_op jit(solution)/shard_map/ppermute | solution.py:297
  115.0 18.4 %collective-permute-start.32 = (bf16[2,128,256]{2,1,0:T(8,128)(2,1)}, bf16[2,128,256]{2,1,0:T(8,128)(2,1)S(1)}, u32[]{:S(2)}, u32[]{:S(2)}) collective-permute-start(bf16[2,128,256]{2,1,0:T(8,128)(2,1)} %get-tuple-element.93), channel_id=1, source_target_pairs={{0,8},{1,9},{2,0},{3,1},{4,24},{5,25},{6,16},{7,17},{8,10},{9,11},... | collective-permute-start | bytes 393224 | tf_op jit(solution)/shard_map/ppermute | solution.py:297
  115.0 33.1 %collective-permute-start.33 = (bf16[2,128,256]{2,1,0:T(8,128)(2,1)}, bf16[2,128,256]{2,1,0:T(8,128)(2,1)S(1)}, u32[]{:S(2)}, u32[]{:S(2)}) collective-permute-start(bf16[2,128,256]{2,1,0:T(8,128)(2,1)} %get-tuple-element.94), channel_id=1, source_target_pairs={{0,9},{1,8},{2,1},{3,0},{4,25},{5,24},{6,17},{7,16},{8,11},{9,10},... | collective-permute-start | bytes 393224 | tf_op jit(solution)/shard_map/ppermute | solution.py:297
  118.1 30.0 %collective-permute-start.34 = (bf16[2,128,256]{2,1,0:T(8,128)(2,1)}, bf16[2,128,256]{2,1,0:T(8,128)(2,1)S(1)}, u32[]{:S(2)}, u32[]{:S(2)}) collective-permute-start(bf16[2,128,256]{2,1,0:T(8,128)(2,1)} %copy-done.18), channel_id=1, source_target_pairs={{0,16},{1,17},{2,24},{3,25},{4,0},{5,1},{6,8},{7,9},{8,18},{9,19},... | collective-permute-start | bytes 393224 | tf_op jit(solution)/shard_map/ppermute | solution.py:297
  125.6 22.5 %collective-permute-start.35 = (bf16[2,128,256]{2,1,0:T(8,128)(2,1)}, bf16[2,128,256]{2,1,0:T(8,128)(2,1)}, u32[]{:S(2)}, u32[]{:S(2)}) collective-permute-start(bf16[2,128,256]{2,1,0:T(8,128)(2,1)} %copy-done.17), channel_id=1, source_target_pairs={{0,17},{1,16},{2,25},{3,24},{4,1},{5,0},{6,9},{7,8},{8,19},{9,18},... | collective-permute-start | bytes 393224 | tf_op jit(solution)/shard_map/ppermute | solution.py:297
  128.9 19.2 %collective-permute-start.36 = (bf16[2,128,256]{2,1,0:T(8,128)(2,1)}, bf16[2,128,256]{2,1,0:T(8,128)(2,1)}, u32[]{:S(2)}, u32[]{:S(2)}) collective-permute-start(bf16[2,128,256]{2,1,0:T(8,128)(2,1)} %copy-done.16), channel_id=1, source_target_pairs={{0,24},{1,25},{2,16},{3,17},{4,8},{5,9},{6,0},{7,1},{8,26},{9,27},... | collective-permute-start | bytes 393224 | tf_op jit(solution)/shard_map/ppermute | solution.py:297
  133.3 17.8 %collective-permute-start.37 = (bf16[2,128,256]{2,1,0:T(8,128)(2,1)}, bf16[2,128,256]{2,1,0:T(8,128)(2,1)}, u32[]{:S(2)}, u32[]{:S(2)}) collective-permute-start(bf16[2,128,256]{2,1,0:T(8,128)(2,1)} %copy-done.15), channel_id=1, source_target_pairs={{0,25},{1,24},{2,17},{3,16},{4,9},{5,8},{6,1},{7,0},{8,27},{9,26},... | collective-permute-start | bytes 393224 | tf_op jit(solution)/shard_map/ppermute | solution.py:297
  138.4 1.1 copy-start.14
  (2 other events, 1.2 us)

commit v13 on v12

--- a/solution.py
+++ b/solution.py
@@ -63,15 +63,15 @@
         out[d, pair, c * g:(c + 1) * g, e:] = tile[g:]
 
 
-def unpack_pair(tiles, blocks, pair, put):
-    e, g = tiles.edge, tiles.rows
+def unpack_pair(tiles, chunks, pair, put):
+    e = tiles.edge
     for d, (a, b) in enumerate(tiles.above):
-        put(a, b, blocks[d, pair, :, :e].astype(WIDE))
-        put(b, a, blocks[d, pair, :, e:].astype(WIDE).T)
+        block = jnp.concatenate([chunk[d, pair] for chunk in chunks], axis=0).astype(WIDE)
+        put(a, b, block[:, :e])
+        put(b, a, block[:, e:].T)
     for d, c, k in tiles.diagonal:
-        upper = blocks[d, pair, c * g:(c + 1) * g, :e]
-        lower = blocks[d, pair, c * g:(c + 1) * g, e:]
-        put(k, k, jnp.concatenate([upper, lower], axis=0).astype(WIDE))
+        block = chunks[c][d, pair].astype(WIDE)
+        put(k, k, jnp.concatenate([block[:, :e], block[:, e:]], axis=0))
 
 
 def to_distances(origin, whole, outs):
@@ -137,7 +137,7 @@
         pack_pair(tiles, total, out, pair)
 
 
-def second_ladder_kernel(tiles, order, place, occ, source, blocks, row, column, *refs):
+def second_ladder_kernel(tiles, order, place, occ, source, upper, others, row, column, *refs):
     pieces, (out, whole, inner, total, matrix) = refs[:-5], refs[-5:]
     assemble(place, order, pieces, whole)
     count = source.shape[0]
@@ -145,7 +145,7 @@
         def put(a, b, tile):
             matrix[tiles.span(a), tiles.span(b)] = tile.astype(NARROW)
 
-        unpack_pair(tiles, blocks, pair, put)
+        unpack_pair(tiles, (upper, others.at[:, 0]), pair, put)
         ladder_pair(matrix[...], whole, inner, total)
         base = occ[place[0] * count + pair] + occ[place[1]]
         strip = math.gcd(64, total.shape[0])
@@ -161,27 +161,26 @@
         lax.fori_loop(0, total.shape[0] // strip, finish, 0)
 
 
-def add_kernel(tiles, first, place, source, *refs):
-    pieces, (out, whole, turned) = refs[:-3], refs[-3:]
-    devices = len(pieces) // 2
-    from_distances(place[1], pieces[:devices], whole)
-    from_distances(place[0] * first + lax.rem(place[1], first), pieces[devices:], turned)
+def add_kernel(tiles, first, place, source, others, *refs):
+    pieces, (out, turned) = refs[:-2], refs[-2:]
+    from_distances(place[0] * first + lax.rem(place[1], first), pieces, turned)
     e, g = tiles.edge, tiles.rows
 
     def put(a, b, tile):
         here = (0, tiles.span(a), tiles.span(b))
         out[here] = source[here] + tile
 
+    def tile_of(block):
+        return jnp.concatenate([block[:, :e], block[:, e:]], axis=0)
+
     for d, (a, b) in enumerate(tiles.above):
-        block = whole[d, 0].astype(WIDE) + tiles.mirror_across(turned[d, 0].astype(WIDE))
+        block = jnp.concatenate([others[d, 1, 0], others[d, 2, 0]], axis=0).astype(WIDE)
+        block = block + tiles.mirror_across(turned[d, 0].astype(WIDE))
         put(a, b, block[:, :e])
         put(b, a, block[:, e:].T)
     for d, c, k in tiles.diagonal:
-        def tile_of(blocks):
-            block = blocks[d, 0, c * g:(c + 1) * g].astype(WIDE)
-            return jnp.concatenate([block[:, :e], block[:, e:]], axis=0)
-
-        put(k, k, tile_of(whole) + tile_of(turned).T)
+        rows = slice(c * g, (c + 1) * g)
+        put(k, k, tile_of(others[d, 1 + c, 0].astype(WIDE)) + tile_of(turned[d, 0, rows].astype(WIDE)).T)
 
 
 def mix(place, fock, first, load, store, rows):
@@ -231,14 +230,16 @@
 
 
 def update_kernel(tiles, groups, first, chunk, place, fock, occ, sums, *refs):
-    before, refs = refs[:3 * chunk], refs[3 * chunk:]
+    before, refs = refs[:2 * chunk], refs[2 * chunk:]
     own, other, refs = refs[:groups], refs[groups:2 * groups], refs[2 * groups:]
     update = refs[-1]
-    sent, straight, turned = (refs[0], *refs[-3:-1]) if chunk else refs[:3]
+    if chunk:
+        sent, straight, turned = refs[0].at[:, 0], refs[0].at[:, 2], refs[-2]
+        refs[0][:, 1] = before[0][...]
+        turned[:, :, :tiles.rows, :] = before[1][...]
+    else:
+        sent, straight, turned = refs[:3]
     rows = slice(chunk * tiles.rows, (chunk + 1) * tiles.rows)
-    there = rows if chunk else slice(None)
-    for ref, out in zip(before, (sent, straight, turned)):
-        out[:, :, :tiles.rows, :] = ref[...]
 
     def one(step, carry):
         u, w = step // first, lax.rem(step, first)
@@ -249,7 +250,7 @@
             def finish(mirrored):
                 value = (own[s][u, w].astype(WIDE) + mirrored) * inverse(base - sums[rows])
                 update[u, s * first + w] = value
-                sent[column, u, there] = value.astype(NARROW)
+                sent[column, u] = value.astype(NARROW)
 
             with_mirror(tiles, place, other[s][w, u].astype(WIDE), finish)
         return carry
@@ -261,20 +262,17 @@
 
     def store(s, u, w, column, at, result):
         strip = pl.ds(pl.multiple_of(chunk * tiles.rows + at.start, 16), at.size)
-        put = strip if chunk else at
         value = update[u, s * first + w, at, :]
         base = occ[place[0] * first + u] + occ[column]
         share = result * inverse(base - sums[strip, :])
-        straight[column, u, put, :] = (
+        straight[column, u, at, :] = (
             share + 2.0 * (value - value.astype(NARROW).astype(WIDE))
         ).astype(NARROW)
-        turned[(place[0] ^ s) * first + u, w, put, :] = share.astype(NARROW)
+        turned[(place[0] ^ s) * first + u, w, strip if chunk else at, :] = share.astype(NARROW)
 
     mix(place, fock, first, load, store, tiles.rows)
     if chunk:
-        devices = straight.shape[0]
-        to_distances(place[1], straight, refs[1:1 + devices])
-        to_distances(place[1], turned, refs[1 + devices:1 + 2 * devices])
+        to_distances(place[1], turned, refs[1:-2])
 
 
 def exchange(blocks):
@@ -367,6 +365,7 @@
     packed = jax.ShapeDtypeStruct((devices, first, edge, 2 * edge), NARROW)
     upper = jax.ShapeDtypeStruct((devices, first, tiles.rows, 2 * edge), NARROW)
     part = jax.ShapeDtypeStruct((first, first, tiles.rows, 2 * edge), NARROW)
+    shared = jax.ShapeDtypeStruct((devices, 3, first, tiles.rows, 2 * edge), NARROW)
     singles = vectors.shape[0]
     whole = pltpu.VMEM((virtual, singles * virtual), NARROW)
     inner = pltpu.VMEM((singles * virtual, virtual), NARROW)
@@ -401,24 +400,23 @@
             specs=[SMEM] * 2 + [VMEM] * (groups + 1),
         ))
         other.append(across_first(half[c], groups))
-    ready = []
+    ready, back = [], []
     for c in chunks:
         ready = call(
             functools.partial(update_kernel, tiles, groups, first, c),
-            [packed] + [distant] * (2 * devices) if c else [upper] * 3,
-            ([blocks] * 2 if c else []) + [pltpu.VMEM((first, devices, *part.shape[2:]), WIDE)],
-            LONG, 10 * count, place, fock, occ_energy, sums, *ready, *half[c], *other[c],
-            specs=[SMEM] * 3 + [VMEM] * (2 * groups + 1 + 3 * c),
+            [shared] + [distant] * devices if c else [upper] * 3,
+            ([blocks] if c else []) + [pltpu.VMEM((first, devices, *part.shape[2:]), WIDE)],
+            LONG, 10 * count, place, fock, occ_energy, sums, *ready[1:], *half[c], *other[c],
+            specs=[SMEM] * 3 + [VMEM] * (2 * groups + 1 + 2 * c),
         )
-    back = exchange(ready[0])
-    last = to_mirror(ready[1 + devices:], groups)
-    last = by_distance(ready[1:1 + devices]) + last
+        back.append(exchange(tie(ready[0], *back)))
+    last = to_mirror(ready[1:], groups)
     base = call(
         functools.partial(second_ladder_kernel, tiles, order), jax.ShapeDtypeStruct(current.shape, WIDE),
         [whole, inner, square, pltpu.VMEM((virtual, virtual), NARROW)],
-        ladder_flops, 12 * count, place, occ_energy, current, back,
+        ladder_flops, 12 * count, place, occ_energy, current, *back,
         jnp.broadcast_to(vir_energy[:, None], (virtual, 128)), vir_energy[None, :], *pieces,
-        specs=[SMEM] * 2 + [VMEM] * (4 + len(pieces)),
+        specs=[SMEM] * 2 + [VMEM] * (5 + len(pieces)),
     )
     def by_pair(*shape):
         return pl.BlockSpec((1, *shape), lambda pair: (pair, 0, 0))
@@ -427,13 +425,15 @@
         functools.partial(add_kernel, tiles, first),
         grid=(first,),
         out_shape=jax.ShapeDtypeStruct(current.shape, WIDE),
-        in_specs=[SMEM, by_pair(virtual, virtual)] + [by_pair(edge, 2 * edge)] * (2 * devices),
+        in_specs=[SMEM, by_pair(virtual, virtual)] + [
+            pl.BlockSpec((devices, 3, 1, tiles.rows, 2 * edge), lambda pair: (0, 0, pair, 0, 0))
+        ] + [by_pair(edge, 2 * edge)] * devices,
         out_specs=by_pair(virtual, virtual),
-        scratch_shapes=[pltpu.VMEM((devices, 1, edge, 2 * edge), NARROW)] * 2,
+        scratch_shapes=[pltpu.VMEM((devices, 1, edge, 2 * edge), NARROW)],
         compiler_params=PARAMS,
         input_output_aliases={1: 0},
         cost_estimate=pl.CostEstimate(flops=count, bytes_accessed=10 * count, transcendentals=0),
-    )(place, base, *last)
+    )(place, base, back[1], *last)
     return done.reshape(amplitudes.shape)
 
 

time: 155 us -> 143 us (0.923)
  the two profiles are of different devices: /device:TPU:3 before, /device:TPU:19 now
where the time goes in v13:
time: 143 us
  starting transfers between devices  66.9 us (47%)
  waiting for transfers between devices  35.7 us (25%)
  Pallas kernels  30.6 us (21%)
  local copies, waits for them, and re-layouts  7.54 us (5%)
  between operations  1.65 us (1%)
    pallas_call x8, Pallas kernels, call(): pl.pallas_call(body, out_shape=outs, in_specs=specs, out_specs=jax.tree.m...  26.6 us
    all_to_all x3, starting transfers between devices, exchange(): lax.all_to_all(blocks, 'occj', split_axis=0, concat_axis=0, tiled=True)  22.2 us
    ppermute x8, starting transfers between devices, turn(): lax.ppermute(x, ('occi', 'occj'), [(p * devices + j, (j ^ k) // first * d...  18.1 us
    ppermute x8, waiting for transfers between devices, turn(): lax.ppermute(x, ('occi', 'occj'), [(p * devices + j, (j ^ k) // first * d...  16.1 us
    ppermute x12, waiting for transfers between devices, across_first(): lax.ppermute(parts[s], 'occi', [(k, k ^ s) for k in range(groups)])  15.7 us
    ppermute x12, starting transfers between devices, across_first(): lax.ppermute(parts[s], 'occi', [(k, k ^ s) for k in range(groups)])  13.2 us
    ppermute x7, starting transfers between devices, by_distance(): lax.ppermute(parts[k], 'occj', [(d, d ^ k) for d in range(devices)])  10.6 us
    unnamed x48, local copies, waits for them, and re-layouts  6.02 us
  transfers between devices with their start and end apart: 34, of which 8 were waited for; matrix products, arithmetic and copies ran while one was open for 1% of the time, Pallas kernels for 19%

profile of v13, /device:TPU:19, one launch (start us, length us, event | category | flops | bytes accessed | tf_op | source)
XLA Modules:
  0.0 142.9 jit_solution(1217308379930796615)
XLA Ops:
  0.0 0.3 collective-permute-start
  0.3 1.2 collective-permute-start.1
  1.6 1.2 collective-permute-start.2
  2.7 0.1 pad_add_fusion.place.source
  2.8 1.6 %copy-done = f32[2,1,512,512]{3,2,1,0:T(8,128)S(1)} copy-done((f32[2,1,512,512]{3,2,1,0:T(8,128)S(1)}, f32[2,1,512,512]{3,2,1,0:T(8,128)}, u32[]{:S(2)}) %copy-start) | copy-done | bytes 2097176
  4.4 0.9 shard_map.73
  5.3 2.7 %collective-permute-start.10 = (bf16[2,128,256]{2,1,0:T(8,128)(2,1)S(1)}, bf16[2,128,256]{2,1,0:T(8,128)(2,1)S(1)}, u32[]{:S(2)}, u32[]{:S(2)}) collective-permute-start(bf16[2,128,256]{2,1,0:T(8,128)(2,1)S(1)} %get-tuple-element.54), channel_id=1, source_target_pairs={{0,7},{1,6},{2,5},{3,4},{4,3},{5,2},{6,1},{7,0},{8,15},{9,14},{10,... | collective-permute-start | bytes 393224 | tf_op jit(solution)/shard_map/ppermute | solution.py:285
  7.9 0.0 collective-permute-start.4
  7.9 0.6 dynamic_slice.14
  9.2 0.6 dynamic_slice.12
  10.5 1.3 collective-permute-start.5
  11.7 3.4 %collective-permute-start.6 = (bf16[2,128,256]{2,1,0:T(8,128)(2,1)S(1)}, bf16[2,128,256]{2,1,0:T(8,128)(2,1)S(1)}, u32[]{:S(2)}, u32[]{:S(2)}) collective-permute-start(bf16[2,128,256]{2,1,0:T(8,128)(2,1)S(1)} %get-tuple-element.50), channel_id=1, source_target_pairs={{0,3},{1,2},{2,1},{3,0},{4,7},{5,6},{6,5},{7,4},{8,11},{9,10},{10,... | collective-permute-start | bytes 393224 | tf_op jit(solution)/shard_map/ppermute | solution.py:285
  15.2 0.1 pad_maximum_fusion
  15.3 0.1 collective-permute-start.3
  15.4 0.1 fusion
  15.4 0.1 fusion.1
  15.5 0.1 fusion.2
  15.6 0.1 broadcast_add_fusion.2
  15.7 0.3 collective-permute-done.10.refs_7_
  16.0 1.8 %collective-permute-start.7 = (bf16[2,128,256]{2,1,0:T(8,128)(2,1)S(1)}, bf16[2,128,256]{2,1,0:T(8,128)(2,1)S(1)}, u32[]{:S(2)}, u32[]{:S(2)}) collective-permute-start(bf16[2,128,256]{2,1,0:T(8,128)(2,1)S(1)} %get-tuple-element.51), channel_id=1, source_target_pairs={{0,4},{1,5},{2,6},{3,7},{4,0},{5,1},{6,2},{7,3},{8,12},{9,13},{10,... | collective-permute-start | bytes 393224 | tf_op jit(solution)/shard_map/ppermute | solution.py:285
  17.8 0.5 collective-permute-start.8
  18.3 1.0 collective-permute-start.9
  19.3 6.2 %shard_map.74 = bf16[8,2,128,256]{3,2,1,0:T(8,128)(2,1)} custom-call(s32[2]{0:T(128)S(1)} %pad_add_fusion.place.source, f32[2,512,512]{2,1,0:T(8,128)} %bitcast.13, bf16[3,64,512]{2,1,0:T(8,128)(2,1)S(1)} %copy-done.1, bf16[3,64,512]{2,1,0:T(8,128)(2,1)S(1)} %collective-permute-done.refs_1_, bf16[3,64,512]{2,1,0:T(8,128)(2,1)S(1)} %collective-permute-done.1.refs_2_, ...), custom_call_target="tpu_custom_call" | custom-call | flops 3221225472 | bytes 4194304 | tf_op jit(solution)/shard_map/pallas_call | solution.py:42
  25.6 1.6 %collective-permute-done.8.refs_5_ = bf16[2,128,256]{2,1,0:T(8,128)(2,1)S(1)} collective-permute-done((bf16[2,128,256]{2,1,0:T(8,128)(2,1)S(1)}, bf16[2,128,256]{2,1,0:T(8,128)(2,1)S(1)}, u32[]{:S(2)}, u32[]{:S(2)}) %collective-permute-start.8) | collective-permute-done | bytes 131104 | tf_op jit(solution)/shard_map/ppermute | solution.py:285
  27.2 0.7 shard_map.75
  27.9 1.4 collective-permute-start.11
  29.3 0.1 collective-permute-start.12
  29.3 1.3 collective-permute-start.13
  30.6 0.1 broadcast_add_fusion
  30.8 4.8 %all-to-all-start = ((bf16[8,2,128,256]{3,2,1,0:T(8,128)(2,1)}), bf16[8,2,128,256]{3,2,1,0:T(8,128)(2,1)S(1)}, u32[]{:S(2)}, u32[]{:S(2)}) async-start(bf16[8,2,128,256]{3,2,1,0:T(8,128)(2,1)} %shard_map.74), calls=%async_computation | async-start | bytes 2097152 | tf_op jit(solution)/shard_map/all_to_all | solution.py:279
  35.6 2.2 %collective-permute-start.17 = (bf16[2,2,64,256]{3,2,1,0:T(8,128)(2,1)S(1)}, bf16[2,2,64,256]{3,2,1,0:T(8,128)(2,1)S(1)}, u32[]{:S(2)}, u32[]{:S(2)}) collective-permute-start(bf16[2,2,64,256]{3,2,1,0:T(8,128)(2,1)S(1)} %get-tuple-element.68), channel_id=1, source_target_pairs={{0,8},{8,0},{16,24},{24,16},{1,9},{9,1},{17,25},{25,17},{2,10},{10... | collective-permute-start | bytes 393224 | tf_op jit(solution)/shard_map/ppermute | solution.py:305
  37.8 1.2 collective-permute-start.19
  39.0 9.0 %collective-permute-done.13.refs_3_ = bf16[2,2,64,256]{3,2,1,0:T(8,128)(2,1)S(1)} collective-permute-done((bf16[2,2,64,256]{3,2,1,0:T(8,128)(2,1)S(1)}, bf16[2,2,64,256]{3,2,1,0:T(8,128)(2,1)S(1)}, u32[]{:S(2)}, u32[]{:S(2)}) %collective-permute-start.13) | collective-permute-done | bytes 131104 | tf_op jit(solution)/shard_map/ppermute | solution.py:305
  48.0 1.2 shard_map.76.place
  49.2 0.2 all-to-all-done.ladder
  49.4 0.6 copy-done.20
  50.0 1.6 %shard_map.77 = (bf16[2,2,64,256]{3,2,1,0:T(8,128)(2,1)S(1)}, bf16[2,2,64,256]{3,2,1,0:T(8,128)(2,1)S(1)}, bf16[2,2,64,256]{3,2,1,0:T(8,128)(2,1)S(1)}, bf16[2,2,64,256]{3,2,1,0:T(8,128)(2,1)S(1)}) custom-call(s32[2]{0:T(128)S(1)} %copy-done.20, f32[8,8]{1,0:T(8,128)S(1)} %convert_element_type.3.fock, bf16[8,2,128,256]{3,2,1,0:T(8,128)(2,1)S(1)} %all-to-all-done.ladder, ...), custom_call_target="tpu_custom_call" | custom-call | flops 30000001024 | bytes 3145728 | tf_op jit(solution)/shard_map/pallas_call | solution.py:42
  51.6 2.3 %collective-permute-start.14 = (bf16[2,2,64,256]{3,2,1,0:T(8,128)(2,1)S(1)}, bf16[2,2,64,256]{3,2,1,0:T(8,128)(2,1)S(1)}, u32[]{:S(2)}, u32[]{:S(2)}) collective-permute-start(bf16[2,2,64,256]{3,2,1,0:T(8,128)(2,1)S(1)} %get-tuple-element.61.refs_1_), channel_id=1, source_target_pairs={{0,8},{8,0},{16,24},{24,16},{1,9},{9,1},{17,25},{25,17},{2,10},{10... | collective-permute-start | bytes 393224 | tf_op jit(solution)/shard_map/ppermute | solution.py:305
  53.9 1.3 collective-permute-start.16
  55.1 0.0 copy-start.19
  55.2 1.6 %shard_map.79 = (bf16[2,2,64,256]{3,2,1,0:T(8,128)(2,1)S(1)}, bf16[2,2,64,256]{3,2,1,0:T(8,128)(2,1)S(1)}, bf16[2,2,64,256]{3,2,1,0:T(8,128)(2,1)S(1)}, bf16[2,2,64,256]{3,2,1,0:T(8,128)(2,1)S(1)}) custom-call(s32[2]{0:T(128)S(1)} %copy-done.10, f32[8,8]{1,0:T(8,128)S(1)} %convert_element_type.3.fock, bf16[8,2,128,256]{3,2,1,0:T(8,128)(2,1)S(1)} %all-to-all-done.ladder, ...), custom_call_target="tpu_custom_call" | custom-call | flops 30000001024 | bytes 3145728 | tf_op jit(solution)/shard_map/pallas_call | solution.py:42
  56.8 2.4 %collective-permute-start.20 = (bf16[2,2,64,256]{3,2,1,0:T(8,128)(2,1)S(1)}, bf16[2,2,64,256]{3,2,1,0:T(8,128)(2,1)S(1)}, u32[]{:S(2)}, u32[]{:S(2)}) collective-permute-start(bf16[2,2,64,256]{3,2,1,0:T(8,128)(2,1)S(1)} %get-tuple-element.72.refs_3_), channel_id=1, source_target_pairs={{0,8},{8,0},{16,24},{24,16},{1,9},{9,1},{17,25},{25,17},{2,10},{10... | collective-permute-start | bytes 393224 | tf_op jit(solution)/shard_map/ppermute | solution.py:305
  59.1 1.3 collective-permute-start.22
  60.4 6.6 %collective-permute-done.16.refs_7_ = bf16[2,2,64,256]{3,2,1,0:T(8,128)(2,1)S(1)} collective-permute-done((bf16[2,2,64,256]{3,2,1,0:T(8,128)(2,1)S(1)}, bf16[2,2,64,256]{3,2,1,0:T(8,128)(2,1)S(1)}, u32[]{:S(2)}, u32[]{:S(2)}) %collective-permute-start.16) | collective-permute-done | bytes 131104 | tf_op jit(solution)/shard_map/ppermute | solution.py:305
  67.0 3.3 %shard_map.78 = (bf16[8,2,64,256]{3,2,1,0:T(8,128)(2,1)}, bf16[8,2,64,256]{3,2,1,0:T(8,128)(2,1)S(1)}, bf16[8,2,64,256]{3,2,1,0:T(8,128)(2,1)S(1)}) custom-call(s32[2]{0:T(128)S(1)} %copy-done.10, f32[8,8]{1,0:T(8,128)S(1)} %convert_element_type.3.fock, f32[8]{0:T(128)S(1)} %copy-done.19, f32[128,256]{1,0:T(8,128)S(1)} %maximum_select_fusion.sums, ...), custom_call_target="tpu_custom_call" | custom-call | flops 30000001024 | bytes 5242880 | tf_op jit(solution)/shard_map/pallas_call | solution.py:42
  70.3 12.3 %all-to-all-start.1 = ((bf16[8,2,64,256]{3,2,1,0:T(8,128)(2,1)}), bf16[8,2,64,256]{3,2,1,0:T(8,128)(2,1)S(1)}, u32[]{:S(2)}, u32[]{:S(2)}) async-start(bf16[8,2,64,256]{3,2,1,0:T(8,128)(2,1)} %get-tuple-element.64), calls=%async_computation.1 | async-start | bytes 1048576 | tf_op jit(solution)/shard_map/all_to_all | solution.py:279
  82.6 3.9 %shard_map.80 = (bf16[8,3,2,64,256]{4,3,2,1,0:T(8,128)(2,1)}, bf16[2,128,256]{2,1,0:T(8,128)(2,1)}, bf16[2,128,256]{2,1,0:T(8,128)(2,1)}, bf16[2,128,256]{2,1,0:...) custom-call(s32[2]{0:T(128)S(1)} %copy-done.10, ...), custom_call_target="tpu_custom_call" | custom-call | flops 30000001024 | bytes 5242880 | tf_op jit(solution)/shard_map/pallas_call | solution.py:42
  86.5 0.7 copy-done.15
  87.2 0.6 copy-done.16
  87.8 0.7 copy-done.17
  88.5 0.6 copy-done.18
  89.2 1.7 %all-to-all-done.1.upper = bf16[8,2,64,256]{3,2,1,0:T(8,128)(2,1)S(1)} async-done(((bf16[8,2,64,256]{3,2,1,0:T(8,128)(2,1)}), bf16[8,2,64,256]{3,2,1,0:T(8,128)(2,1)S(1)}, u32[]{:S(2)}, u32[]{:S(2)}) %all-to-all-start.1) | async-done | bytes 524320 | tf_op jit(solution)/shard_map/all_to_all | solution.py:279
  90.8 5.0 %all-to-all-start.2 = ((bf16[8,3,2,64,256]{4,3,2,1,0:T(8,128)(2,1)}), bf16[8,3,2,64,256]{4,3,2,1,0:T(8,128)(2,1)S(1)}, u32[]{:S(2)}, u32[]{:S(2)}) async-start(bf16[8,3,2,64,256]{4,3,2,1,0:T(8,128)(2,1)} %get-tuple-element.76), calls=%async_computation.2 | async-start | bytes 3145728 | tf_op jit(solution)/shard_map/all_to_all | solution.py:279
  95.9 3.2 %collective-permute-start.23 = (bf16[2,128,256]{2,1,0:T(8,128)(2,1)}, bf16[2,128,256]{2,1,0:T(8,128)(2,1)S(1)}, u32[]{:S(2)}, u32[]{:S(2)}) collective-permute-start(bf16[2,128,256]{2,1,0:T(8,128)(2,1)} %get-tuple-element.77), channel_id=1, source_target_pairs={{0,0},{1,1},{2,8},{3,9},{4,16},{5,17},{6,24},{7,25},{8,2},{9,3},{1... | collective-permute-start | bytes 393224 | tf_op jit(solution)/shard_map/ppermute | solution.py:295
  99.1 2.5 %collective-permute-start.24 = (bf16[2,128,256]{2,1,0:T(8,128)(2,1)}, bf16[2,128,256]{2,1,0:T(8,128)(2,1)S(1)}, u32[]{:S(2)}, u32[]{:S(2)}) collective-permute-start(bf16[2,128,256]{2,1,0:T(8,128)(2,1)} %get-tuple-element.78), channel_id=1, source_target_pairs={{0,1},{1,0},{2,9},{3,8},{4,17},{5,16},{6,25},{7,24},{8,3},{9,2},{1... | collective-permute-start | bytes 393224 | tf_op jit(solution)/shard_map/ppermute | solution.py:295
  101.6 2.7 %collective-permute-start.27 = (bf16[2,128,256]{2,1,0:T(8,128)(2,1)}, bf16[2,128,256]{2,1,0:T(8,128)(2,1)S(1)}, u32[]{:S(2)}, u32[]{:S(2)}) collective-permute-start(bf16[2,128,256]{2,1,0:T(8,128)(2,1)} %copy-done.18), channel_id=1, source_target_pairs={{0,16},{1,17},{2,24},{3,25},{4,0},{5,1},{6,8},{7,9},{8,18},{9,19},... | collective-permute-start | bytes 393224 | tf_op jit(solution)/shard_map/ppermute | solution.py:295
  104.3 6.3 %collective-permute-done.23.refs_0_ = bf16[2,128,256]{2,1,0:T(8,128)(2,1)S(1)} collective-permute-done((bf16[2,128,256]{2,1,0:T(8,128)(2,1)}, bf16[2,128,256]{2,1,0:T(8,128)(2,1)S(1)}, u32[]{:S(2)}, u32[]{:S(2)}) %collective-permute-start.23) | collective-permute-done | bytes 131104 | tf_op jit(solution)/shard_map/ppermute | solution.py:295
  110.6 1.6 %collective-permute-start.28 = (bf16[2,128,256]{2,1,0:T(8,128)(2,1)}, bf16[2,128,256]{2,1,0:T(8,128)(2,1)}, u32[]{:S(2)}, u32[]{:S(2)}) collective-permute-start(bf16[2,128,256]{2,1,0:T(8,128)(2,1)} %copy-done.17), channel_id=1, source_target_pairs={{0,17},{1,16},{2,25},{3,24},{4,1},{5,0},{6,9},{7,8},{8,19},{9,18},... | collective-permute-start | bytes 393224 | tf_op jit(solution)/shard_map/ppermute | solution.py:295
  112.2 9.8 %collective-permute-done.24.refs_1_ = bf16[2,128,256]{2,1,0:T(8,128)(2,1)S(1)} collective-permute-done((bf16[2,128,256]{2,1,0:T(8,128)(2,1)}, bf16[2,128,256]{2,1,0:T(8,128)(2,1)S(1)}, u32[]{:S(2)}, u32[]{:S(2)}) %collective-permute-start.24) | collective-permute-done | bytes 131104 | tf_op jit(solution)/shard_map/ppermute | solution.py:295
  122.0 8.0 %collective-permute-start.30 = (bf16[2,128,256]{2,1,0:T(8,128)(2,1)}, bf16[2,128,256]{2,1,0:T(8,128)(2,1)}, u32[]{:S(2)}, u32[]{:S(2)}) collective-permute-start(bf16[2,128,256]{2,1,0:T(8,128)(2,1)} %copy-done.15), channel_id=1, source_target_pairs={{0,25},{1,24},{2,17},{3,16},{4,9},{5,8},{6,1},{7,0},{8,27},{9,26},... | collective-permute-start | bytes 393224 | tf_op jit(solution)/shard_map/ppermute | solution.py:295
  130.1 0.1 broadcast_in_dim.4.row
  130.3 1.1 copy-done.14
  131.4 8.5 %shard_map.81.source = f32[2,512,512]{2,1,0:T(8,128)} custom-call(s32[2]{0:T(128)S(1)} %copy-done.10, f32[8]{0:T(128)S(1)} %copy-done.19, f32[2,512,512]{2,1,0:T(8,128)} %bitcast.14, bf16[8,2,64,256]{3,2,1,0:T(8,128)(2,1)S(1)} %all-to-all-done.1.upper, bf16[8,3,2,64,256]{4,3,2,1,0:T(8,128)(2,1)S(1)} %all-to-all-done.2.others, ...), custom_call_target="tpu_custom_call" | custom-call | flops 3221225472 | bytes 6291456 | tf_op jit(solution)/shard_map/pallas_call | solution.py:42
  140.0 2.9 %shard_map.82 = f32[2,512,512]{2,1,0:T(8,128)} custom-call(s32[2]{0:T(128)S(1)} %copy-done.10, f32[2,512,512]{2,1,0:T(8,128)} %shard_map.81.source, bf16[8,3,2,64,256]{4,3,2,1,0:T(8,128)(2,1)S(1)} %all-to-all-done.2.others, bf16[2,128,256]{2,1,0:T(8,128)(2,1)S(1)} %collective-permute-done.23.refs_0_, ...), custom_call_target="tpu_custom_call", output_to_operand_aliasing={{}: (1, {})} | custom-call | flops 524288 | bytes 5242880 | tf_op jit(solution)/shard_map/pallas_call | solution.py:424
  (74 shorter events, 0.2 us)
Async XLA Ops:
  0.0 7.9 %copy-start.23 = (s32[8]{0:T(128)S(1)}, s32[8]{0:T(128)}, u32[]{:S(2)}) copy-start(s32[8]{0:T(128)} %constant.25.clone) | copy-start | bytes 100
  0.0 9.2 %copy-start.22 = (s32[8]{0:T(128)S(1)}, s32[8]{0:T(128)}, u32[]{:S(2)}) copy-start(s32[8]{0:T(128)} %constant.24.clone) | copy-start | bytes 100
  0.0 15.3 %copy-start.11 = (f32[512]{0:T(512)S(1)}, f32[512]{0:T(512)}, u32[]{:S(2)}) copy-start(f32[512]{0:T(512)} %param.11) | copy-start | bytes 6148
  0.0 10.4 %collective-permute-start = (bf16[3,64,512]{2,1,0:T(8,128)(2,1)}, bf16[3,64,512]{2,1,0:T(8,128)(2,1)S(1)}, u32[]{:S(2)}, u32[]{:S(2)}) collective-permute-start(bf16[3,64,512]{2,1,0:T(8,128)(2,1)} %refs_0_.3), channel_id=1, source_target_pairs={{0,2},{1,3},{2,0},{3,1},{4,6},{5,7},{6,4},{7,5},{8,10},{9,11},{10,... | collective-permute-start | bytes 589832 | tf_op jit(solution)/shard_map/ppermute | solution.py:331
  0.3 11.4 %collective-permute-start.1 = (bf16[3,64,512]{2,1,0:T(8,128)(2,1)}, bf16[3,64,512]{2,1,0:T(8,128)(2,1)S(1)}, u32[]{:S(2)}, u32[]{:S(2)}) collective-permute-start(bf16[3,64,512]{2,1,0:T(8,128)(2,1)} %refs_0_.3), channel_id=1, source_target_pairs={{0,4},{1,5},{2,6},{3,7},{4,0},{5,1},{6,2},{7,3},{8,12},{9,13},{10,... | collective-permute-start | bytes 589832 | tf_op jit(solution)/shard_map/ppermute | solution.py:331
  1.6 13.6 %collective-permute-start.2 = (bf16[3,64,512]{2,1,0:T(8,128)(2,1)}, bf16[3,64,512]{2,1,0:T(8,128)(2,1)S(1)}, u32[]{:S(2)}, u32[]{:S(2)}) collective-permute-start(bf16[3,64,512]{2,1,0:T(8,128)(2,1)} %refs_0_.3), channel_id=1, source_target_pairs={{0,6},{1,7},{2,4},{3,5},{4,2},{5,3},{6,0},{7,1},{8,14},{9,15},{10,... | collective-permute-start | bytes 589832 | tf_op jit(solution)/shard_map/ppermute | solution.py:331
  2.8 24.4 %copy-start.9 = (s32[2]{0:T(128)}, s32[2]{0:T(128)S(1)}, u32[]{:S(2)}) copy-start(s32[2]{0:T(128)S(1)} %pad_add_fusion.place.source) | copy-start | bytes 28
  2.8 1.6 %copy-start = (f32[2,1,512,512]{3,2,1,0:T(8,128)S(1)}, f32[2,1,512,512]{3,2,1,0:T(8,128)}, u32[]{:S(2)}) copy-start(f32[2,1,512,512]{3,2,1,0:T(8,128)} %param.7) | copy-start | bytes 6291460
  4.4 10.8 %copy-start.1 = (bf16[3,64,512]{2,1,0:T(8,128)(2,1)S(1)}, bf16[3,64,512]{2,1,0:T(8,128)(2,1)}, u32[]{:S(2)}) copy-start(bf16[3,64,512]{2,1,0:T(8,128)(2,1)} %refs_0_.3) | copy-start | bytes 589828
  5.3 10.8 %collective-permute-start.10 = (bf16[2,128,256]{2,1,0:T(8,128)(2,1)S(1)}, bf16[2,128,256]{2,1,0:T(8,128)(2,1)S(1)}, u32[]{:S(2)}, u32[]{:S(2)}) collective-permute-start(bf16[2,128,256]{2,1,0:T(8,128)(2,1)S(1)} %get-tuple-element.54), channel_id=1, source_target_pairs={{0,7},{1,6},{2,5},{3,4},{4,3},{5,2},{6,1},{7,0},{8,15},{9,14},{10,... | collective-permute-start | bytes 393224 | tf_op jit(solution)/shard_map/ppermute | solution.py:285
  7.9 9.9 %collective-permute-start.4 = (bf16[2,128,256]{2,1,0:T(8,128)(2,1)S(1)}, bf16[2,128,256]{2,1,0:T(8,128)(2,1)S(1)}, u32[]{:S(2)}, u32[]{:S(2)}) collective-permute-start(bf16[2,128,256]{2,1,0:T(8,128)(2,1)S(1)} %get-tuple-element.48), channel_id=1, source_target_pairs={{0,1},{1,0},{2,3},{3,2},{4,5},{5,4},{6,7},{7,6},{8,9},{9,8},{10,11... | collective-permute-start | bytes 393224 | tf_op jit(solution)/shard_map/ppermute | solution.py:285
  10.5 15.1 %copy-start.3 = (bf16[3,64,512]{2,1,0:T(8,128)(2,1)}, bf16[3,64,512]{2,1,0:T(8,128)(2,1)S(1)}, u32[]{:S(2)}) copy-start(bf16[3,64,512]{2,1,0:T(8,128)(2,1)S(1)} %collective-permute-done.refs_1_) | copy-start | bytes 589828
  10.5 15.1 %collective-permute-start.5 = (bf16[2,128,256]{2,1,0:T(8,128)(2,1)S(1)}, bf16[2,128,256]{2,1,0:T(8,128)(2,1)S(1)}, u32[]{:S(2)}, u32[]{:S(2)}) collective-permute-start(bf16[2,128,256]{2,1,0:T(8,128)(2,1)S(1)} %get-tuple-element.49), channel_id=1, source_target_pairs={{0,2},{1,3},{2,0},{3,1},{4,6},{5,7},{6,4},{7,5},{8,10},{9,11},{10,... | collective-permute-start | bytes 393224 | tf_op jit(solution)/shard_map/ppermute | solution.py:285
  11.7 13.8 %copy-start.5 = (bf16[3,64,512]{2,1,0:T(8,128)(2,1)}, bf16[3,64,512]{2,1,0:T(8,128)(2,1)S(1)}, u32[]{:S(2)}) copy-start(bf16[3,64,512]{2,1,0:T(8,128)(2,1)S(1)} %collective-permute-done.1.refs_2_) | copy-start | bytes 589828
  11.7 13.8 %collective-permute-start.6 = (bf16[2,128,256]{2,1,0:T(8,128)(2,1)S(1)}, bf16[2,128,256]{2,1,0:T(8,128)(2,1)S(1)}, u32[]{:S(2)}, u32[]{:S(2)}) collective-permute-start(bf16[2,128,256]{2,1,0:T(8,128)(2,1)S(1)} %get-tuple-element.50), channel_id=1, source_target_pairs={{0,3},{1,2},{2,1},{3,0},{4,7},{5,6},{6,5},{7,4},{8,11},{9,10},{10,... | collective-permute-start | bytes 393224 | tf_op jit(solution)/shard_map/ppermute | solution.py:285
  15.2 10.4 %copy-start.7 = (bf16[3,64,512]{2,1,0:T(8,128)(2,1)}, bf16[3,64,512]{2,1,0:T(8,128)(2,1)S(1)}, u32[]{:S(2)}) copy-start(bf16[3,64,512]{2,1,0:T(8,128)(2,1)S(1)} %collective-permute-done.2.refs_3_) | copy-start | bytes 589828
  15.3 3.0 %collective-permute-start.3 = (bf16[4,3,64,512]{3,2,1,0:T(8,128)(2,1)S(1)}, bf16[4,3,64,512]{3,2,1,0:T(8,128)(2,1)S(1)}, u32[]{:S(2)}, u32[]{:S(2)}) collective-permute-start(bf16[4,3,64,512]{3,2,1,0:T(8,128)(2,1)S(1)} %pad_maximum_fusion), channel_id=1, source_target_pairs={{0,1},{1,0},{2,3},{3,2},{4,5},{5,4},{6,7},{7,6},{8,9},{9,8},{10,11... | collective-permute-start | bytes 2359304 | tf_op jit(solution)/shard_map/ppermute | solution.py:331
  16.0 9.5 %collective-permute-start.7 = (bf16[2,128,256]{2,1,0:T(8,128)(2,1)S(1)}, bf16[2,128,256]{2,1,0:T(8,128)(2,1)S(1)}, u32[]{:S(2)}, u32[]{:S(2)}) collective-permute-start(bf16[2,128,256]{2,1,0:T(8,128)(2,1)S(1)} %get-tuple-element.51), channel_id=1, source_target_pairs={{0,4},{1,5},{2,6},{3,7},{4,0},{5,1},{6,2},{7,3},{8,12},{9,13},{10,... | collective-permute-start | bytes 393224 | tf_op jit(solution)/shard_map/ppermute | solution.py:285
  17.8 9.4 %collective-permute-start.8 = (bf16[2,128,256]{2,1,0:T(8,128)(2,1)S(1)}, bf16[2,128,256]{2,1,0:T(8,128)(2,1)S(1)}, u32[]{:S(2)}, u32[]{:S(2)}) collective-permute-start(bf16[2,128,256]{2,1,0:T(8,128)(2,1)S(1)} %get-tuple-element.52), channel_id=1, source_target_pairs={{0,5},{1,4},{2,7},{3,6},{4,1},{5,0},{6,3},{7,2},{8,13},{9,12},{10,... | collective-permute-start | bytes 393224 | tf_op jit(solution)/shard_map/ppermute | solution.py:285
  18.3 7.3 %copy-start.13 = (bf16[4,3,64,512]{3,2,1,0:T(8,128)(2,1)}, bf16[4,3,64,512]{3,2,1,0:T(8,128)(2,1)S(1)}, u32[]{:S(2)}) copy-start(bf16[4,3,64,512]{3,2,1,0:T(8,128)(2,1)S(1)} %collective-permute-done.3.refs_4_) | copy-start | bytes 2359300
  18.3 12.4 %copy-start.21 = (bf16[8,8]{1,0:T(8,128)(2,1)S(1)}, bf16[8,8]{1,0:T(8,128)(2,1)}, u32[]{:S(2)}) copy-start(bf16[8,8]{1,0:T(8,128)(2,1)} %param.9) | copy-start | bytes 388
  18.3 8.9 %collective-permute-start.9 = (bf16[2,128,256]{2,1,0:T(8,128)(2,1)S(1)}, bf16[2,128,256]{2,1,0:T(8,128)(2,1)S(1)}, u32[]{:S(2)}, u32[]{:S(2)}) collective-permute-start(bf16[2,128,256]{2,1,0:T(8,128)(2,1)S(1)} %get-tuple-element.53), channel_id=1, source_target_pairs={{0,6},{1,7},{2,4},{3,5},{4,2},{5,3},{6,0},{7,1},{8,14},{9,15},{10,... | collective-permute-start | bytes 393224 | tf_op jit(solution)/shard_map/ppermute | solution.py:285
  27.9 9.9 %collective-permute-start.11 = (bf16[2,2,64,256]{3,2,1,0:T(8,128)(2,1)S(1)}, bf16[2,2,64,256]{3,2,1,0:T(8,128)(2,1)S(1)}, u32[]{:S(2)}, u32[]{:S(2)}) collective-permute-start(bf16[2,2,64,256]{3,2,1,0:T(8,128)(2,1)S(1)} %get-tuple-element.56), channel_id=1, source_target_pairs={{0,8},{8,0},{16,24},{24,16},{1,9},{9,1},{17,25},{25,17},{2,10},{10... | collective-permute-start | bytes 393224 | tf_op jit(solution)/shard_map/ppermute | solution.py:305
  29.3 9.7 %collective-permute-start.12 = (bf16[2,2,64,256]{3,2,1,0:T(8,128)(2,1)S(1)}, bf16[2,2,64,256]{3,2,1,0:T(8,128)(2,1)S(1)}, u32[]{:S(2)}, u32[]{:S(2)}) collective-permute-start(bf16[2,2,64,256]{3,2,1,0:T(8,128)(2,1)S(1)} %get-tuple-element.57), channel_id=1, source_target_pairs={{0,16},{8,24},{16,0},{24,8},{1,17},{9,25},{17,1},{25,9},{2,18},{10... | collective-permute-start | bytes 393224 | tf_op jit(solution)/shard_map/ppermute | solution.py:305
  29.3 18.6 %collective-permute-start.13 = (bf16[2,2,64,256]{3,2,1,0:T(8,128)(2,1)S(1)}, bf16[2,2,64,256]{3,2,1,0:T(8,128)(2,1)S(1)}, u32[]{:S(2)}, u32[]{:S(2)}) collective-permute-start(bf16[2,2,64,256]{3,2,1,0:T(8,128)(2,1)S(1)} %get-tuple-element.58), channel_id=1, source_target_pairs={{0,24},{8,16},{16,8},{24,0},{1,25},{9,17},{17,9},{25,1},{2,26},{10... | collective-permute-start | bytes 393224 | tf_op jit(solution)/shard_map/ppermute | solution.py:305
  30.8 18.7 %all-to-all-start = ((bf16[8,2,128,256]{3,2,1,0:T(8,128)(2,1)}), bf16[8,2,128,256]{3,2,1,0:T(8,128)(2,1)S(1)}, u32[]{:S(2)}, u32[]{:S(2)}) async-start(bf16[8,2,128,256]{3,2,1,0:T(8,128)(2,1)} %shard_map.74), calls=%async_computation | async-start | bytes 2097152 | tf_op jit(solution)/shard_map/all_to_all | solution.py:279
  35.6 18.3 %collective-permute-start.17 = (bf16[2,2,64,256]{3,2,1,0:T(8,128)(2,1)S(1)}, bf16[2,2,64,256]{3,2,1,0:T(8,128)(2,1)S(1)}, u32[]{:S(2)}, u32[]{:S(2)}) collective-permute-start(bf16[2,2,64,256]{3,2,1,0:T(8,128)(2,1)S(1)} %get-tuple-element.68), channel_id=1, source_target_pairs={{0,8},{8,0},{16,24},{24,16},{1,9},{9,1},{17,25},{25,17},{2,10},{10... | collective-permute-start | bytes 393224 | tf_op jit(solution)/shard_map/ppermute | solution.py:305
  37.8 17.3 %collective-permute-start.18 = (bf16[2,2,64,256]{3,2,1,0:T(8,128)(2,1)S(1)}, bf16[2,2,64,256]{3,2,1,0:T(8,128)(2,1)S(1)}, u32[]{:S(2)}, u32[]{:S(2)}) collective-permute-start(bf16[2,2,64,256]{3,2,1,0:T(8,128)(2,1)S(1)} %get-tuple-element.69), channel_id=1, source_target_pairs={{0,16},{8,24},{16,0},{24,8},{1,17},{9,25},{17,1},{25,9},{2,18},{10... | collective-permute-start | bytes 393224 | tf_op jit(solution)/shard_map/ppermute | solution.py:305
  37.8 17.3 %collective-permute-start.19 = (bf16[2,2,64,256]{3,2,1,0:T(8,128)(2,1)S(1)}, bf16[2,2,64,256]{3,2,1,0:T(8,128)(2,1)S(1)}, u32[]{:S(2)}, u32[]{:S(2)}) collective-permute-start(bf16[2,2,64,256]{3,2,1,0:T(8,128)(2,1)S(1)} %get-tuple-element.70), channel_id=1, source_target_pairs={{0,24},{8,16},{16,8},{24,0},{1,25},{9,17},{17,9},{25,1},{2,26},{10... | collective-permute-start | bytes 393224 | tf_op jit(solution)/shard_map/ppermute | solution.py:305
  49.2 6.0 %copy-start.10 = (s32[2]{0:T(128)S(1)}, s32[2]{0:T(128)}, u32[]{:S(2)}) copy-start(s32[2]{0:T(128)} %copy-done.9) | copy-start | bytes 28
  49.4 0.6 copy-start.20
  51.6 7.5 %collective-permute-start.14 = (bf16[2,2,64,256]{3,2,1,0:T(8,128)(2,1)S(1)}, bf16[2,2,64,256]{3,2,1,0:T(8,128)(2,1)S(1)}, u32[]{:S(2)}, u32[]{:S(2)}) collective-permute-start(bf16[2,2,64,256]{3,2,1,0:T(8,128)(2,1)S(1)} %get-tuple-element.61.refs_1_), channel_id=1, source_target_pairs={{0,8},{8,0},{16,24},{24,16},{1,9},{9,1},{17,25},{25,17},{2,10},{10... | collective-permute-start | bytes 393224 | tf_op jit(solution)/shard_map/ppermute | solution.py:305
  53.9 6.5 %collective-permute-start.15 = (bf16[2,2,64,256]{3,2,1,0:T(8,128)(2,1)S(1)}, bf16[2,2,64,256]{3,2,1,0:T(8,128)(2,1)S(1)}, u32[]{:S(2)}, u32[]{:S(2)}) collective-permute-start(bf16[2,2,64,256]{3,2,1,0:T(8,128)(2,1)S(1)} %get-tuple-element.62.refs_2_), channel_id=1, source_target_pairs={{0,16},{8,24},{16,0},{24,8},{1,17},{9,25},{17,1},{25,9},{2,18},{10... | collective-permute-start | bytes 393224 | tf_op jit(solution)/shard_map/ppermute | solution.py:305
  53.9 13.1 %collective-permute-start.16 = (bf16[2,2,64,256]{3,2,1,0:T(8,128)(2,1)S(1)}, bf16[2,2,64,256]{3,2,1,0:T(8,128)(2,1)S(1)}, u32[]{:S(2)}, u32[]{:S(2)}) collective-permute-start(bf16[2,2,64,256]{3,2,1,0:T(8,128)(2,1)S(1)} %get-tuple-element.63.refs_3_), channel_id=1, source_target_pairs={{0,24},{8,16},{16,8},{24,0},{1,25},{9,17},{17,9},{25,1},{2,26},{10... | collective-permute-start | bytes 393224 | tf_op jit(solution)/shard_map/ppermute | solution.py:305
  55.1 11.9 %copy-start.19 = (f32[8]{0:T(128)S(1)}, f32[8]{0:T(128)}, u32[]{:S(2)}) copy-start(f32[8]{0:T(128)} %occ.5) | copy-start | bytes 100
  56.8 25.9 %collective-permute-start.20 = (bf16[2,2,64,256]{3,2,1,0:T(8,128)(2,1)S(1)}, bf16[2,2,64,256]{3,2,1,0:T(8,128)(2,1)S(1)}, u32[]{:S(2)}, u32[]{:S(2)}) collective-permute-start(bf16[2,2,64,256]{3,2,1,0:T(8,128)(2,1)S(1)} %get-tuple-element.72.refs_3_), channel_id=1, source_target_pairs={{0,8},{8,0},{16,24},{24,16},{1,9},{9,1},{17,25},{25,17},{2,10},{10... | collective-permute-start | bytes 393224 | tf_op jit(solution)/shard_map/ppermute | solution.py:305
  59.1 23.5 %collective-permute-start.21 = (bf16[2,2,64,256]{3,2,1,0:T(8,128)(2,1)S(1)}, bf16[2,2,64,256]{3,2,1,0:T(8,128)(2,1)S(1)}, u32[]{:S(2)}, u32[]{:S(2)}) collective-permute-start(bf16[2,2,64,256]{3,2,1,0:T(8,128)(2,1)S(1)} %get-tuple-element.73.refs_4_), channel_id=1, source_target_pairs={{0,16},{8,24},{16,0},{24,8},{1,17},{9,25},{17,1},{25,9},{2,18},{10... | collective-permute-start | bytes 393224 | tf_op jit(solution)/shard_map/ppermute | solution.py:305
  59.1 23.5 %collective-permute-start.22 = (bf16[2,2,64,256]{3,2,1,0:T(8,128)(2,1)S(1)}, bf16[2,2,64,256]{3,2,1,0:T(8,128)(2,1)S(1)}, u32[]{:S(2)}, u32[]{:S(2)}) collective-permute-start(bf16[2,2,64,256]{3,2,1,0:T(8,128)(2,1)S(1)} %get-tuple-element.74.refs_5_), channel_id=1, source_target_pairs={{0,24},{8,16},{16,8},{24,0},{1,25},{9,17},{17,9},{25,1},{2,26},{10... | collective-permute-start | bytes 393224 | tf_op jit(solution)/shard_map/ppermute | solution.py:305
  70.3 20.6 %all-to-all-start.1 = ((bf16[8,2,64,256]{3,2,1,0:T(8,128)(2,1)}), bf16[8,2,64,256]{3,2,1,0:T(8,128)(2,1)S(1)}, u32[]{:S(2)}, u32[]{:S(2)}) async-start(bf16[8,2,64,256]{3,2,1,0:T(8,128)(2,1)} %get-tuple-element.64), calls=%async_computation.1 | async-start | bytes 1048576 | tf_op jit(solution)/shard_map/all_to_all | solution.py:279
  86.5 0.7 copy-start.15
  87.2 0.6 copy-start.16
  87.8 0.7 copy-start.17
  88.5 0.6 copy-start.18
  89.1 40.9 %copy-start.12 = (f32[512]{0:T(512)S(1)}, f32[512]{0:T(512)}, u32[]{:S(2)}) copy-start(f32[512]{0:T(512)} %param.11) | copy-start | bytes 6148
  89.1 41.1 %copy-start.2 = (bf16[3,64,512]{2,1,0:T(8,128)(2,1)S(1)}, bf16[3,64,512]{2,1,0:T(8,128)(2,1)}, u32[]{:S(2)}) copy-start(bf16[3,64,512]{2,1,0:T(8,128)(2,1)} %refs_0_.3) | copy-start | bytes 589828
  89.1 41.1 %copy-start.4 = (bf16[3,64,512]{2,1,0:T(8,128)(2,1)S(1)}, bf16[3,64,512]{2,1,0:T(8,128)(2,1)}, u32[]{:S(2)}) copy-start(bf16[3,64,512]{2,1,0:T(8,128)(2,1)} %copy-done.3) | copy-start | bytes 589828
  89.1 41.1 %copy-start.6 = (bf16[3,64,512]{2,1,0:T(8,128)(2,1)S(1)}, bf16[3,64,512]{2,1,0:T(8,128)(2,1)}, u32[]{:S(2)}) copy-start(bf16[3,64,512]{2,1,0:T(8,128)(2,1)} %copy-done.5) | copy-start | bytes 589828
  89.2 41.1 %copy-start.8 = (bf16[3,64,512]{2,1,0:T(8,128)(2,1)S(1)}, bf16[3,64,512]{2,1,0:T(8,128)(2,1)}, u32[]{:S(2)}) copy-start(bf16[3,64,512]{2,1,0:T(8,128)(2,1)} %copy-done.7) | copy-start | bytes 589828
  90.8 39.3 %all-to-all-start.2 = ((bf16[8,3,2,64,256]{4,3,2,1,0:T(8,128)(2,1)}), bf16[8,3,2,64,256]{4,3,2,1,0:T(8,128)(2,1)S(1)}, u32[]{:S(2)}, u32[]{:S(2)}) async-start(bf16[8,3,2,64,256]{4,3,2,1,0:T(8,128)(2,1)} %get-tuple-element.76), calls=%async_computation.2 | async-start | bytes 3145728 | tf_op jit(solution)/shard_map/all_to_all | solution.py:279
  95.9 14.8 %collective-permute-start.23 = (bf16[2,128,256]{2,1,0:T(8,128)(2,1)}, bf16[2,128,256]{2,1,0:T(8,128)(2,1)S(1)}, u32[]{:S(2)}, u32[]{:S(2)}) collective-permute-start(bf16[2,128,256]{2,1,0:T(8,128)(2,1)} %get-tuple-element.77), channel_id=1, source_target_pairs={{0,0},{1,1},{2,8},{3,9},{4,16},{5,17},{6,24},{7,25},{8,2},{9,3},{1... | collective-permute-start | bytes 393224 | tf_op jit(solution)/shard_map/ppermute | solution.py:295
  99.1 22.9 %collective-permute-start.24 = (bf16[2,128,256]{2,1,0:T(8,128)(2,1)}, bf16[2,128,256]{2,1,0:T(8,128)(2,1)S(1)}, u32[]{:S(2)}, u32[]{:S(2)}) collective-permute-start(bf16[2,128,256]{2,1,0:T(8,128)(2,1)} %get-tuple-element.78), channel_id=1, source_target_pairs={{0,1},{1,0},{2,9},{3,8},{4,17},{5,16},{6,25},{7,24},{8,3},{9,2},{1... | collective-permute-start | bytes 393224 | tf_op jit(solution)/shard_map/ppermute | solution.py:295
  101.6 20.4 %collective-permute-start.25 = (bf16[2,128,256]{2,1,0:T(8,128)(2,1)}, bf16[2,128,256]{2,1,0:T(8,128)(2,1)S(1)}, u32[]{:S(2)}, u32[]{:S(2)}) collective-permute-start(bf16[2,128,256]{2,1,0:T(8,128)(2,1)} %get-tuple-element.79), channel_id=1, source_target_pairs={{0,8},{1,9},{2,0},{3,1},{4,24},{5,25},{6,16},{7,17},{8,10},{9,11},... | collective-permute-start | bytes 393224 | tf_op jit(solution)/shard_map/ppermute | solution.py:295
  101.6 38.3 %collective-permute-start.26 = (bf16[2,128,256]{2,1,0:T(8,128)(2,1)}, bf16[2,128,256]{2,1,0:T(8,128)(2,1)S(1)}, u32[]{:S(2)}, u32[]{:S(2)}) collective-permute-start(bf16[2,128,256]{2,1,0:T(8,128)(2,1)} %get-tuple-element.80), channel_id=1, source_target_pairs={{0,9},{1,8},{2,1},{3,0},{4,25},{5,24},{6,17},{7,16},{8,11},{9,10},... | collective-permute-start | bytes 393224 | tf_op jit(solution)/shard_map/ppermute | solution.py:295
  101.6 38.3 %collective-permute-start.27 = (bf16[2,128,256]{2,1,0:T(8,128)(2,1)}, bf16[2,128,256]{2,1,0:T(8,128)(2,1)S(1)}, u32[]{:S(2)}, u32[]{:S(2)}) collective-permute-start(bf16[2,128,256]{2,1,0:T(8,128)(2,1)} %copy-done.18), channel_id=1, source_target_pairs={{0,16},{1,17},{2,24},{3,25},{4,0},{5,1},{6,8},{7,9},{8,18},{9,19},... | collective-permute-start | bytes 393224 | tf_op jit(solution)/shard_map/ppermute | solution.py:295
  110.6 29.3 %collective-permute-start.28 = (bf16[2,128,256]{2,1,0:T(8,128)(2,1)}, bf16[2,128,256]{2,1,0:T(8,128)(2,1)}, u32[]{:S(2)}, u32[]{:S(2)}) collective-permute-start(bf16[2,128,256]{2,1,0:T(8,128)(2,1)} %copy-done.17), channel_id=1, source_target_pairs={{0,17},{1,16},{2,25},{3,24},{4,1},{5,0},{6,9},{7,8},{8,19},{9,18},... | collective-permute-start | bytes 393224 | tf_op jit(solution)/shard_map/ppermute | solution.py:295
  122.0 17.9 %collective-permute-start.29 = (bf16[2,128,256]{2,1,0:T(8,128)(2,1)}, bf16[2,128,256]{2,1,0:T(8,128)(2,1)}, u32[]{:S(2)}, u32[]{:S(2)}) collective-permute-start(bf16[2,128,256]{2,1,0:T(8,128)(2,1)} %copy-done.16), channel_id=1, source_target_pairs={{0,24},{1,25},{2,16},{3,17},{4,8},{5,9},{6,0},{7,1},{8,26},{9,27},... | collective-permute-start | bytes 393224 | tf_op jit(solution)/shard_map/ppermute | solution.py:295
  122.0 17.9 %collective-permute-start.30 = (bf16[2,128,256]{2,1,0:T(8,128)(2,1)}, bf16[2,128,256]{2,1,0:T(8,128)(2,1)}, u32[]{:S(2)}, u32[]{:S(2)}) collective-permute-start(bf16[2,128,256]{2,1,0:T(8,128)(2,1)} %copy-done.15), channel_id=1, source_target_pairs={{0,25},{1,24},{2,17},{3,16},{4,9},{5,8},{6,1},{7,0},{8,27},{9,26},... | collective-permute-start | bytes 393224 | tf_op jit(solution)/shard_map/ppermute | solution.py:295
  130.3 1.1 copy-start.14

commit v14 on v11

--- a/solution.py
+++ b/solution.py
@@ -137,28 +137,22 @@
         pack_pair(tiles, total, out, pair)
 
 
-def second_ladder_kernel(tiles, order, place, occ, source, blocks, row, column, *refs):
-    pieces, (out, whole, inner, total, matrix) = refs[:-5], refs[-5:]
-    assemble(place, order, pieces, whole)
-    count = source.shape[0]
-    for pair in range(count):
-        def put(a, b, tile):
-            matrix[tiles.span(a), tiles.span(b)] = tile.astype(NARROW)
-
-        unpack_pair(tiles, blocks, pair, put)
-        ladder_pair(matrix[...], whole, inner, total)
-        base = occ[place[0] * count + pair] + occ[place[1]]
-        strip = math.gcd(64, total.shape[0])
-
-        def finish(step, carry):
-            at = pl.ds(pl.multiple_of(step * strip, strip), strip)
-            own = base - row[at, :1] - column[...]
-            out[pair, at, :] = (
-                source[pair, at, :] + 2.0 * (matrix[at, :].astype(WIDE) + total[at, :] * inverse(own))
-            )
-            return carry
-
-        lax.fori_loop(0, total.shape[0] // strip, finish, 0)
+def second_ladder_kernel(tiles, first, place, occ, source, blocks, row, column, whole, out, inner, total, matrix):
+    def put(a, b, tile):
+        matrix[tiles.span(a), tiles.span(b)] = tile.astype(NARROW)
+
+    unpack_pair(tiles, blocks, 0, put)
+    ladder_pair(matrix[...], whole, inner, total)
+    base = occ[place[0] * first + pl.program_id(0)] + occ[place[1]]
+    strip = math.gcd(64, total.shape[0])
+
+    def finish(step, carry):
+        at = pl.ds(pl.multiple_of(step * strip, strip), strip)
+        own = base - row[at, :1] - column[...]
+        out[0, at, :] = source[0, at, :] + 2.0 * (matrix[at, :].astype(WIDE) + total[at, :] * inverse(own))
+        return carry
+
+    lax.fori_loop(0, total.shape[0] // strip, finish, 0)
 
 
 def add_kernel(tiles, place, source, *refs):
@@ -220,10 +214,8 @@
 
 def update_kernel(tiles, groups, first, chunk, place, fock, occ, sums, *refs):
     before, refs = refs[:chunk], refs[chunk:]
-    own, other = refs[:groups], refs[groups:2 * groups]
-    sent, rest = refs[2 * groups:2 * groups + 2]
-    out = refs[2 * groups + 2:3 * groups + 2]
-    update = refs[3 * groups + 2]
+    own, other, refs = refs[:groups], refs[groups:2 * groups], refs[2 * groups:]
+    (sent, rest), out, (update, local_mixed) = refs[:2], refs[2:groups + 1], refs[groups + 1:]
     here = slice(chunk * tiles.rows, (chunk + 1) * tiles.rows)
     for ref in before:
         sent[:, :, :tiles.rows, :] = ref[...]
@@ -236,10 +228,8 @@
 
             def finish(mirrored):
                 value = (own[s][u, w].astype(WIDE) + mirrored) * inverse(base - sums[here])
-                narrow = value.astype(NARROW)
                 update[u, s * first + w] = value
-                sent[column, u, here] = narrow
-                rest[u, s * first + w] = (2.0 * (value - narrow.astype(WIDE))).astype(NARROW)
+                sent[column, u, here] = value.astype(NARROW)
 
             with_mirror(tiles, place, other[s][w, u].astype(WIDE), finish)
         return carry
@@ -249,14 +239,37 @@
     def load(s, u, r, at):
         return update[u, s * first + r, at, :]
 
+    def lost(value):
+        return 2.0 * (value - value.astype(NARROW).astype(WIDE))
+
     def store(s, u, w, column, at, result):
-        out[s][u, w, at, :] = result.astype(NARROW)
+        if s == 0:
+            local_mixed[u, w, at, :] = result
+            return
+        out[s - 1][u, w, at, :] = result.astype(NARROW)
+        strip = pl.ds(pl.multiple_of(chunk * tiles.rows + at.start, 16), at.size)
+        base = occ[place[0] * first + u] + occ[column]
+        share = result * inverse(base - sums[strip, :])
+        rest[u, s * first + w, at, :] = (lost(update[u, s * first + w, at, :]) + share).astype(NARROW)
 
     mix(place, fock, first, load, store, tiles.rows)
 
+    def within(step, carry):
+        u, w = step // first, lax.rem(step, first)
+        base = occ[place[0] * first + u] + occ[place[0] * first + w]
+
+        def finish(mirrored):
+            share = (local_mixed[u, w] + mirrored) * inverse(base - sums[here])
+            rest[u, w] = (lost(update[u, w]) + share).astype(NARROW)
+
+        with_mirror(tiles, place, local_mixed[w, u], finish)
+        return carry
+
+    lax.fori_loop(0, first * first, within, 0)
+
 
 def rest_kernel(tiles, groups, first, chunk, place, occ, sums, rest, *refs):
-    own, other, refs = refs[:groups], refs[groups:2 * groups], refs[2 * groups:]
+    other, refs = refs[:groups - 1], refs[groups - 1:]
     out = refs[-1]
     here = slice(chunk * tiles.rows, (chunk + 1) * tiles.rows)
     there = here if chunk else slice(None)
@@ -265,15 +278,16 @@
 
     def one(step, carry):
         u, w = step // first, lax.rem(step, first)
-        for s in range(groups):
+        out[place[0] * first + w, u, there] = rest[u, w]
+        for s in range(1, groups):
             column = (place[0] ^ s) * first + w
             base = occ[place[0] * first + u] + occ[column]
 
             def finish(mirrored):
-                value = (own[s][u, w].astype(WIDE) + mirrored) * inverse(base - sums[here])
-                out[column, u, there] = (rest[u, s * first + w].astype(WIDE) + value).astype(NARROW)
-
-            with_mirror(tiles, place, other[s][w, u].astype(WIDE), finish)
+                value = rest[u, s * first + w].astype(WIDE) + mirrored * inverse(base - sums[here])
+                out[column, u, there] = value.astype(NARROW)
+
+            with_mirror(tiles, place, other[s - 1][w, u].astype(WIDE), finish)
         return carry
 
     lax.fori_loop(0, first * first, one, 0)
@@ -288,8 +302,9 @@
 def by_distance(parts):
     devices = len(parts)
     return [parts[0]] + [
-        lax.ppermute(parts[k], "occj", [(d, d ^ k) for d in range(devices)]) for k in range(1, devices)
-    ]
+        lax.ppermute(parts[k], "occj", [(d, d ^ k) for d in range(devices)])
+        for k in range(devices - 1, 0, -1)
+    ][::-1]
 
 
 def across_first(parts, groups):
@@ -301,6 +316,21 @@
 
 def tie(x, *others):
     return lax.optimization_barrier((x, *others))[0]
+
+
+def copy_kernel(source, out):
+    for k in range(source.shape[0]):
+        out[k] = source[k]
+
+
+def after(x, *others):
+    return pl.pallas_call(
+        copy_kernel,
+        out_shape=jax.ShapeDtypeStruct(x.shape, x.dtype),
+        in_specs=[SMEM],
+        out_specs=SMEM,
+        cost_estimate=pl.CostEstimate(flops=LONG, bytes_accessed=8, transcendentals=0),
+    )(tie(x, *others))
 
 
 def gather_vectors(vectors, devices, packed):
@@ -343,7 +373,6 @@
     upper = jax.ShapeDtypeStruct((devices, first, tiles.rows, 2 * edge), NARROW)
     part = jax.ShapeDtypeStruct((first, first, tiles.rows, 2 * edge), NARROW)
     singles = vectors.shape[0]
-    whole = pltpu.VMEM((virtual, singles * virtual), NARROW)
     inner = pltpu.VMEM((singles * virtual, virtual), NARROW)
     square = pltpu.VMEM((virtual, virtual), WIDE)
     chunks = range(2)
@@ -357,8 +386,9 @@
     sums = virtual_sums(tiles, vir_energy, q)
 
     ladder_flops = first * singles * 4 * virtual**3
-    ladder = call(
-        functools.partial(first_ladder_kernel, tiles, order), packed, [whole, inner, square],
+    ladder, whole = call(
+        functools.partial(first_ladder_kernel, tiles, order),
+        [packed, jax.ShapeDtypeStruct((virtual, singles * virtual), NARROW)], [inner, square],
         ladder_flops, 8 * count, place, current, *pieces, specs=[SMEM] + [VMEM] * (1 + len(pieces)),
     )
     parts = call(
@@ -366,13 +396,13 @@
         tie(place, ladder), *held, specs=[SMEM] + [VMEM] * devices,
     )
     mirror = [across_first(parts[c * groups:(c + 1) * groups], groups) for c in chunks]
-    ladder = exchange(tie(ladder, *held))
+    ladder = exchange(ladder)
 
     half, other = [], []
     for c in chunks:
         half.append(call(
             functools.partial(half_kernel, tiles, groups, first, c), [part] * groups, [],
-            LONG, 6 * count, place, fock, ladder, *mirror[c],
+            LONG, 6 * count, after(place, *mirror[c]) if c == 0 else place, fock, ladder, *mirror[c],
             specs=[SMEM] * 2 + [VMEM] * (groups + 1),
         ))
         other.append(across_first(half[c], groups))
@@ -380,32 +410,43 @@
     for c in chunks:
         sent_one, rest_one, *mixed_one = call(
             functools.partial(update_kernel, tiles, groups, first, c),
-            [(upper, packed)[c], jax.ShapeDtypeStruct((first, devices, *part.shape[2:]), NARROW)] + [part] * groups,
-            [pltpu.VMEM((first, devices, *part.shape[2:]), WIDE)],
+            [(upper, packed)[c], jax.ShapeDtypeStruct((first, devices, *part.shape[2:]), NARROW)] + [part] * (groups - 1),
+            [pltpu.VMEM((first, devices, *part.shape[2:]), WIDE), pltpu.VMEM(part.shape, WIDE)],
             LONG, 10 * count, place, fock, occ_energy, sums, *sent, *half[c], *other[c],
             specs=[SMEM] * 3 + [VMEM] * (2 * groups + 1 + c),
         )
         sent, rest, mixed = [sent_one], rest + [rest_one], mixed + [mixed_one]
-    other = [across_first(x, groups) for x in mixed]
+    other = [across_first([None] + x, groups)[1:] for x in mixed]
     back = exchange(sent[0])
-    base = call(
-        functools.partial(second_ladder_kernel, tiles, order), jax.ShapeDtypeStruct(current.shape, WIDE),
-        [whole, inner, square, pltpu.VMEM((virtual, virtual), NARROW)],
-        ladder_flops, 12 * count, place, occ_energy, current, back,
-        jnp.broadcast_to(vir_energy[:, None], (virtual, 128)), vir_energy[None, :], *pieces,
-        specs=[SMEM] * 2 + [VMEM] * (4 + len(pieces)),
-    )
+    def by_pair(*shape):
+        return pl.BlockSpec((1, *shape), lambda pair: (pair, 0, 0))
+
+    def all_pairs(*shape):
+        return pl.BlockSpec(shape, lambda pair: (0, 0))
+
+    base = pl.pallas_call(
+        functools.partial(second_ladder_kernel, tiles, first),
+        grid=(first,),
+        out_shape=jax.ShapeDtypeStruct(current.shape, WIDE),
+        in_specs=[
+            SMEM, SMEM, by_pair(virtual, virtual),
+            pl.BlockSpec((devices, 1, edge, 2 * edge), lambda pair: (0, pair, 0, 0)),
+            all_pairs(virtual, 128), all_pairs(1, virtual), all_pairs(*whole.shape),
+        ],
+        out_specs=by_pair(virtual, virtual),
+        scratch_shapes=[inner, square, pltpu.VMEM((virtual, virtual), NARROW)],
+        compiler_params=PARAMS,
+        cost_estimate=pl.CostEstimate(flops=ladder_flops, bytes_accessed=12 * count, transcendentals=0),
+    )(place, occ_energy, current, back, jnp.broadcast_to(vir_energy[:, None], (virtual, 128)),
+      vir_energy[None, :], whole)
     last = []
     for c in chunks:
         last = call(
             functools.partial(rest_kernel, tiles, groups, first, c),
             [distant] * devices if c else [upper], [blocks] if c else [],
-            2 * count if c else LONG, 8 * count, place, occ_energy, sums, rest[c], *mixed[c], *other[c], *last,
-            specs=[SMEM] * 2 + [VMEM] * (2 * groups + 2 + c),
+            LONG, 8 * count, place, occ_energy, sums, rest[c], *other[c], *last,
+            specs=[SMEM] * 2 + [VMEM] * (groups + 1 + c),
         )
-    def by_pair(*shape):
-        return pl.BlockSpec((1, *shape), lambda pair: (pair, 0, 0))
-
     done = pl.pallas_call(
         functools.partial(add_kernel, tiles),
         grid=(first,),

time: 134 us -> 127 us (0.948)
  starting transfers between devices: 74 us -> 66.5 us
    pallas_call x10 -> x9, Pallas kernels: 28.7 us -> 19.3 us  [call(): pl.pallas_call(body, out_shape=outs, in_specs=specs, out_specs=jax.tree.m...]
    pallas_call x0 -> x2, Pallas kernels: none -> 8.97 us  [the longest x1 7.79 us: local(): pl.pallas_call(functools.partial(second_ladder_kernel, tiles, first), gri...]
    ppermute x18, starting transfers between devices: 44.1 us -> 35.3 us  [across_first(): lax.ppermute(parts[s], 'occi', [(k, k ^ s) for k in range(groups)])]
    all_to_all x2, waiting for transfers between devices: 0.01 us -> 7.72 us  [exchange(): lax.all_to_all(blocks, 'occj', split_axis=0, concat_axis=0, tiled=True)]
    ppermute x4, waiting for transfers between devices: 6.71 us -> 2.49 us  [turn(): return lax.ppermute(x, 'occj', [(d, d ^ k) for d in range(devices)])]
    ppermute x18, waiting for transfers between devices: 9.07 us -> 6.86 us  [across_first(): lax.ppermute(parts[s], 'occi', [(k, k ^ s) for k in range(groups)])]
    unnamed x42 -> x28, local copies, waits for them, and re-layouts: 4.63 us -> 5.43 us
  transfers between devices with their start and end apart: 38 -> 38, of which waited for: 7 -> 7; matrix products, arithmetic and copies ran while one was open for 1% -> 2% of each run, Pallas kernels for 22% -> 22%
where the time goes in v14:
time: 127 us; the launch traced here: 126 us
  starting transfers between devices  66.5 us (52%)
  Pallas kernels  31.1 us (24%)
  waiting for transfers between devices  19.2 us (15%)
  local copies, waits for them, and re-layouts  6.95 us (5%)
  between operations  1.64 us (1%)
    ppermute x18, starting transfers between devices, across_first(): lax.ppermute(parts[s], 'occi', [(k, k ^ s) for k in range(groups)])  35.3 us
    pallas_call x9, Pallas kernels, call(): pl.pallas_call(body, out_shape=outs, in_specs=specs, out_specs=jax.tree.m...  19.3 us
    ppermute x14, starting transfers between devices, by_distance(): lax.ppermute(parts[k], 'occj', [(d, d ^ k) for d in range(devices)])  16.4 us
    all_to_all x2, starting transfers between devices, exchange(): lax.all_to_all(blocks, 'occj', split_axis=0, concat_axis=0, tiled=True)  10.2 us
    pallas_call x1, Pallas kernels, local(): pl.pallas_call(functools.partial(second_ladder_kernel, tiles, first), gri...  7.79 us
    all_to_all x2, waiting for transfers between devices, exchange(): lax.all_to_all(blocks, 'occj', split_axis=0, concat_axis=0, tiled=True)  7.72 us
    ppermute x18, waiting for transfers between devices, across_first(): lax.ppermute(parts[s], 'occi', [(k, k ^ s) for k in range(groups)])  6.86 us
    unnamed x28, local copies, waits for them, and re-layouts  5.43 us
  transfers between devices with their start and end apart: 38, of which 7 were waited for; matrix products, arithmetic and copies ran while one was open for 2% of the time, Pallas kernels for 22%

profile of v14, /device:TPU:0, one launch (start us, length us, event | category | flops | bytes accessed | tf_op | source)
XLA Modules:
  0.0 125.7 jit_solution(292044095735332454)
XLA Ops:
  0.0 3.0 %collective-permute-start = (bf16[3,64,512]{2,1,0:T(8,128)(2,1)}, bf16[3,64,512]{2,1,0:T(8,128)(2,1)S(1)}, u32[]{:S(2)}, u32[]{:S(2)}) collective-permute-start(bf16[3,64,512]{2,1,0:T(8,128)(2,1)} %refs_0_.1), channel_id=1, source_target_pairs={{0,2},{1,3},{2,0},{3,1},{4,6},{5,7},{6,4},{7,5},{8,10},{9,11},{10,... | collective-permute-start | bytes 589832 | tf_op jit(solution)/shard_map/ppermute | solution.py:338
  3.0 1.5 %collective-permute-start.1 = (bf16[3,64,512]{2,1,0:T(8,128)(2,1)}, bf16[3,64,512]{2,1,0:T(8,128)(2,1)S(1)}, u32[]{:S(2)}, u32[]{:S(2)}) collective-permute-start(bf16[3,64,512]{2,1,0:T(8,128)(2,1)} %refs_0_.1), channel_id=1, source_target_pairs={{0,4},{1,5},{2,6},{3,7},{4,0},{5,1},{6,2},{7,3},{8,12},{9,13},{10,... | collective-permute-start | bytes 589832 | tf_op jit(solution)/shard_map/ppermute | solution.py:338
  4.6 1.6 %copy-done = f32[2,1,512,512]{3,2,1,0:T(8,128)S(1)} copy-done((f32[2,1,512,512]{3,2,1,0:T(8,128)S(1)}, f32[2,1,512,512]{3,2,1,0:T(8,128)}, u32[]{:S(2)}) %copy-start) | copy-done | bytes 2097176
  6.2 0.9 shard_map.73
  7.1 1.6 %collective-permute-start.10 = (bf16[2,128,256]{2,1,0:T(8,128)(2,1)S(1)}, bf16[2,128,256]{2,1,0:T(8,128)(2,1)S(1)}, u32[]{:S(2)}, u32[]{:S(2)}) collective-permute-start(bf16[2,128,256]{2,1,0:T(8,128)(2,1)S(1)} %get-tuple-element.62), channel_id=1, source_target_pairs={{0,7},{1,6},{2,5},{3,4},{4,3},{5,2},{6,1},{7,0},{8,15},{9,14},{10,... | collective-permute-start | bytes 393224 | tf_op jit(solution)/shard_map/ppermute | solution.py:305
  8.7 1.5 %collective-permute-start.4 = (bf16[2,128,256]{2,1,0:T(8,128)(2,1)S(1)}, bf16[2,128,256]{2,1,0:T(8,128)(2,1)S(1)}, u32[]{:S(2)}, u32[]{:S(2)}) collective-permute-start(bf16[2,128,256]{2,1,0:T(8,128)(2,1)S(1)} %get-tuple-element.56), channel_id=1, source_target_pairs={{0,1},{1,0},{2,3},{3,2},{4,5},{5,4},{6,7},{7,6},{8,9},{9,8},{10,11... | collective-permute-start | bytes 393224 | tf_op jit(solution)/shard_map/ppermute | solution.py:305
  10.2 0.6 dynamic_slice.14
  11.4 0.6 dynamic_slice.12
  12.7 0.6 collective-permute-start.5
  13.3 2.5 %collective-permute-done.1.refs_2_ = bf16[3,64,512]{2,1,0:T(8,128)(2,1)S(1)} collective-permute-done((bf16[3,64,512]{2,1,0:T(8,128)(2,1)}, bf16[3,64,512]{2,1,0:T(8,128)(2,1)S(1)}, u32[]{:S(2)}, u32[]{:S(2)}) %collective-permute-start.1) | collective-permute-done | bytes 196640 | tf_op jit(solution)/shard_map/ppermute | solution.py:338
  15.8 0.1 pad_maximum_fusion
  16.0 0.1 fusion
  16.2 0.1 broadcast_add_fusion.2
  16.3 2.4 %collective-permute-start.7 = (bf16[2,128,256]{2,1,0:T(8,128)(2,1)S(1)}, bf16[2,128,256]{2,1,0:T(8,128)(2,1)S(1)}, u32[]{:S(2)}, u32[]{:S(2)}) collective-permute-start(bf16[2,128,256]{2,1,0:T(8,128)(2,1)S(1)} %get-tuple-element.59), channel_id=1, source_target_pairs={{0,4},{1,5},{2,6},{3,7},{4,0},{5,1},{6,2},{7,3},{8,12},{9,13},{10,... | collective-permute-start | bytes 393224 | tf_op jit(solution)/shard_map/ppermute | solution.py:305
  18.8 0.2 collective-permute-start.8
  18.9 2.9 %collective-permute-start.9 = (bf16[2,128,256]{2,1,0:T(8,128)(2,1)S(1)}, bf16[2,128,256]{2,1,0:T(8,128)(2,1)S(1)}, u32[]{:S(2)}, u32[]{:S(2)}) collective-permute-start(bf16[2,128,256]{2,1,0:T(8,128)(2,1)S(1)} %get-tuple-element.61), channel_id=1, source_target_pairs={{0,6},{1,7},{2,4},{3,5},{4,2},{5,3},{6,0},{7,1},{8,14},{9,15},{10,... | collective-permute-start | bytes 393224 | tf_op jit(solution)/shard_map/ppermute | solution.py:305
  21.8 6.3 %shard_map.74 = (bf16[8,2,128,256]{3,2,1,0:T(8,128)(2,1)}, bf16[512,1536]{1,0:T(8,128)(2,1)}) custom-call(s32[2]{0:T(128)S(1)} %pad_add_fusion.place.source, f32[2,512,512]{2,1,0:T(8,128)} %bitcast.13, bf16[3,64,512]{2,1,0:T(8,128)(2,1)S(1)} %copy-done.1, bf16[3,64,512]{2,1,0:T(8,128)(2,1)S(1)} %collective-permute-done.refs_1_, ...), custom_call_target="tpu_custom_call" | custom-call | flops 3221225472 | bytes 4194304 | tf_op jit(solution)/shard_map/pallas_call | solution.py:42
  28.1 0.2 collective-permute-done.8.refs_5_
  28.3 0.7 shard_map.75
  29.0 1.6 %collective-permute-start.11 = (bf16[2,2,64,256]{3,2,1,0:T(8,128)(2,1)S(1)}, bf16[2,2,64,256]{3,2,1,0:T(8,128)(2,1)S(1)}, u32[]{:S(2)}, u32[]{:S(2)}) collective-permute-start(bf16[2,2,64,256]{3,2,1,0:T(8,128)(2,1)S(1)} %get-tuple-element.64), channel_id=1, source_target_pairs={{0,8},{8,0},{16,24},{24,16},{1,9},{9,1},{17,25},{25,17},{2,10},{10... | collective-permute-start | bytes 393224 | tf_op jit(solution)/shard_map/ppermute | solution.py:312
  30.6 2.6 %collective-permute-start.12 = (bf16[2,2,64,256]{3,2,1,0:T(8,128)(2,1)S(1)}, bf16[2,2,64,256]{3,2,1,0:T(8,128)(2,1)S(1)}, u32[]{:S(2)}, u32[]{:S(2)}) collective-permute-start(bf16[2,2,64,256]{3,2,1,0:T(8,128)(2,1)S(1)} %get-tuple-element.65), channel_id=1, source_target_pairs={{0,16},{8,24},{16,0},{24,8},{1,17},{9,25},{17,1},{25,9},{2,18},{10... | collective-permute-start | bytes 393224 | tf_op jit(solution)/shard_map/ppermute | solution.py:312
  33.2 0.2 collective-permute-start.13
  33.5 0.1 broadcast_add_fusion
  33.6 3.6 %all-to-all-start = ((bf16[8,2,128,256]{3,2,1,0:T(8,128)(2,1)}), bf16[8,2,128,256]{3,2,1,0:T(8,128)(2,1)S(1)}, u32[]{:S(2)}, u32[]{:S(2)}) async-start(bf16[8,2,128,256]{3,2,1,0:T(8,128)(2,1)} %get-tuple-element.54), calls=%async_computation | async-start | bytes 2097152 | tf_op jit(solution)/shard_map/all_to_all | solution.py:299
  37.2 0.7 collective-permute-start.17
  37.9 3.5 %collective-permute-start.18 = (bf16[2,2,64,256]{3,2,1,0:T(8,128)(2,1)S(1)}, bf16[2,2,64,256]{3,2,1,0:T(8,128)(2,1)S(1)}, u32[]{:S(2)}, u32[]{:S(2)}) collective-permute-start(bf16[2,2,64,256]{3,2,1,0:T(8,128)(2,1)S(1)} %get-tuple-element.75), channel_id=1, source_target_pairs={{0,16},{8,24},{16,0},{24,8},{1,17},{9,25},{17,1},{25,9},{2,18},{10... | collective-permute-start | bytes 393224 | tf_op jit(solution)/shard_map/ppermute | solution.py:312
  41.4 0.2 collective-permute-start.19
  41.6 2.0 %collective-permute-done.12.refs_2_ = bf16[2,2,64,256]{3,2,1,0:T(8,128)(2,1)S(1)} collective-permute-done((bf16[2,2,64,256]{3,2,1,0:T(8,128)(2,1)S(1)}, bf16[2,2,64,256]{3,2,1,0:T(8,128)(2,1)S(1)}, u32[]{:S(2)}, u32[]{:S(2)}) %collective-permute-start.12) | collective-permute-done | bytes 131104 | tf_op jit(solution)/shard_map/ppermute | solution.py:312
  43.6 1.2 shard_map.76.place
  44.8 7.7 %all-to-all-done.ladder = bf16[8,2,128,256]{3,2,1,0:T(8,128)(2,1)S(1)} async-done(((bf16[8,2,128,256]{3,2,1,0:T(8,128)(2,1)}), bf16[8,2,128,256]{3,2,1,0:T(8,128)(2,1)S(1)}, u32[]{:S(2)}, u32[]{:S(2)}) %all-to-all-start) | async-done | bytes 1048608 | tf_op jit(solution)/shard_map/all_to_all | solution.py:299
  52.5 0.6 copy-done.10
  53.1 1.6 %shard_map.77 = (bf16[2,2,64,256]{3,2,1,0:T(8,128)(2,1)S(1)}, bf16[2,2,64,256]{3,2,1,0:T(8,128)(2,1)S(1)}, bf16[2,2,64,256]{3,2,1,0:T(8,128)(2,1)S(1)}, bf16[2,2,64,256]{3,2,1,0:T(8,128)(2,1)S(1)}) custom-call(s32[2]{0:T(128)S(1)} %copy-done.10, f32[8,8]{1,0:T(8,128)S(1)} %convert_element_type.3.fock, bf16[8,2,128,256]{3,2,1,0:T(8,128)(2,1)S(1)} %all-to-all-done.ladder, ...), custom_call_target="tpu_custom_call" | custom-call | flops 30000001024 | bytes 3145728 | tf_op jit(solution)/shard_map/pallas_call | solution.py:42
  54.6 1.3 %collective-permute-start.14 = (bf16[2,2,64,256]{3,2,1,0:T(8,128)(2,1)S(1)}, bf16[2,2,64,256]{3,2,1,0:T(8,128)(2,1)S(1)}, u32[]{:S(2)}, u32[]{:S(2)}) collective-permute-start(bf16[2,2,64,256]{3,2,1,0:T(8,128)(2,1)S(1)} %get-tuple-element.69.refs_1_), channel_id=1, source_target_pairs={{0,8},{8,0},{16,24},{24,16},{1,9},{9,1},{17,25},{25,17},{2,10},{10... | collective-permute-start | bytes 393224 | tf_op jit(solution)/shard_map/ppermute | solution.py:312
  56.0 2.9 %collective-permute-start.15 = (bf16[2,2,64,256]{3,2,1,0:T(8,128)(2,1)S(1)}, bf16[2,2,64,256]{3,2,1,0:T(8,128)(2,1)S(1)}, u32[]{:S(2)}, u32[]{:S(2)}) collective-permute-start(bf16[2,2,64,256]{3,2,1,0:T(8,128)(2,1)S(1)} %get-tuple-element.70.refs_2_), channel_id=1, source_target_pairs={{0,16},{8,24},{16,0},{24,8},{1,17},{9,25},{17,1},{25,9},{2,18},{10... | collective-permute-start | bytes 393224 | tf_op jit(solution)/shard_map/ppermute | solution.py:312
  58.9 0.2 collective-permute-start.16
  59.1 1.6 %shard_map.79 = (bf16[2,2,64,256]{3,2,1,0:T(8,128)(2,1)S(1)}, bf16[2,2,64,256]{3,2,1,0:T(8,128)(2,1)S(1)}, bf16[2,2,64,256]{3,2,1,0:T(8,128)(2,1)S(1)}, bf16[2,2,64,256]{3,2,1,0:T(8,128)(2,1)S(1)}) custom-call(s32[2]{0:T(128)S(1)} %copy-done.5, f32[8,8]{1,0:T(8,128)S(1)} %convert_element_type.3.fock, bf16[8,2,128,256]{3,2,1,0:T(8,128)(2,1)S(1)} %all-to-all-done.ladder, ...), custom_call_target="tpu_custom_call" | custom-call | flops 30000001024 | bytes 3145728 | tf_op jit(solution)/shard_map/pallas_call | solution.py:42
  60.7 0.4 collective-permute-start.20
  61.2 3.8 %collective-permute-start.21 = (bf16[2,2,64,256]{3,2,1,0:T(8,128)(2,1)S(1)}, bf16[2,2,64,256]{3,2,1,0:T(8,128)(2,1)S(1)}, u32[]{:S(2)}, u32[]{:S(2)}) collective-permute-start(bf16[2,2,64,256]{3,2,1,0:T(8,128)(2,1)S(1)} %get-tuple-element.79.refs_3_), channel_id=1, source_target_pairs={{0,16},{8,24},{16,0},{24,8},{1,17},{9,25},{17,1},{25,9},{2,18},{10... | collective-permute-start | bytes 393224 | tf_op jit(solution)/shard_map/ppermute | solution.py:312
  65.0 3.0 %collective-permute-start.22 = (bf16[2,2,64,256]{3,2,1,0:T(8,128)(2,1)S(1)}, bf16[2,2,64,256]{3,2,1,0:T(8,128)(2,1)S(1)}, u32[]{:S(2)}, u32[]{:S(2)}) collective-permute-start(bf16[2,2,64,256]{3,2,1,0:T(8,128)(2,1)S(1)} %get-tuple-element.80.refs_4_), channel_id=1, source_target_pairs={{0,24},{8,16},{16,8},{24,0},{1,25},{9,17},{17,9},{25,1},{2,26},{10... | collective-permute-start | bytes 393224 | tf_op jit(solution)/shard_map/ppermute | solution.py:312
  68.0 0.9 collective-permute-done.15.refs_6_
  68.9 2.5 %shard_map.78 = (bf16[8,2,64,256]{3,2,1,0:T(8,128)(2,1)S(1)}, bf16[2,8,64,256]{3,2,1,0:T(8,128)(2,1)S(1)}, bf16[2,2,64,256]{3,2,1,0:T(8,128)(2,1)S(1)}, bf16[2,2...) custom-call(s32[2]{0:T(128)S(1)} %copy-done.5, f32[8,8]{1,0:T(8,128)S(1)} %convert_element_type.3.fock, ...), custom_call_target="tpu_custom_call" | custom-call | flops 30000001024 | bytes 5242880 | tf_op jit(solution)/shard_map/pallas_call | solution.py:42
  71.4 0.8 copy-done.8
  72.2 7.2 %collective-permute-start.26 = (bf16[2,2,64,256]{3,2,1,0:T(8,128)(2,1)S(1)}, bf16[2,2,64,256]{3,2,1,0:T(8,128)(2,1)S(1)}, u32[]{:S(2)}, u32[]{:S(2)}) collective-permute-start(bf16[2,2,64,256]{3,2,1,0:T(8,128)(2,1)S(1)} %get-tuple-element.88), channel_id=1, source_target_pairs={{0,8},{8,0},{16,24},{24,16},{1,9},{9,1},{17,25},{25,17},{2,10},{10... | collective-permute-start | bytes 393224 | tf_op jit(solution)/shard_map/ppermute | solution.py:312
  79.4 0.8 collective-permute-start.27
  80.2 1.6 %collective-permute-start.28 = (bf16[2,2,64,256]{3,2,1,0:T(8,128)(2,1)S(1)}, bf16[2,2,64,256]{3,2,1,0:T(8,128)(2,1)S(1)}, u32[]{:S(2)}, u32[]{:S(2)}) collective-permute-start(bf16[2,2,64,256]{3,2,1,0:T(8,128)(2,1)S(1)} %get-tuple-element.90), channel_id=1, source_target_pairs={{0,24},{8,16},{16,8},{24,0},{1,25},{9,17},{17,9},{25,1},{2,26},{10... | collective-permute-start | bytes 393224 | tf_op jit(solution)/shard_map/ppermute | solution.py:312
  81.8 3.6 %shard_map.80 = (bf16[8,2,128,256]{3,2,1,0:T(8,128)(2,1)}, bf16[2,8,64,256]{3,2,1,0:T(8,128)(2,1)S(1)}, bf16[2,2,64,256]{3,2,1,0:T(8,128)(2,1)S(1)}, bf16[2,2,64...) custom-call(s32[2]{0:T(128)S(1)} %copy-done.5, f32[8,8]{1,0:T(8,128)S(1)} %convert_element_type.3.fock, ...), custom_call_target="tpu_custom_call" | custom-call | flops 30000001024 | bytes 5242880 | tf_op jit(solution)/shard_map/pallas_call | solution.py:42
  85.4 2.7 %collective-permute-start.23 = (bf16[2,2,64,256]{3,2,1,0:T(8,128)(2,1)S(1)}, bf16[2,2,64,256]{3,2,1,0:T(8,128)(2,1)S(1)}, u32[]{:S(2)}, u32[]{:S(2)}) collective-permute-start(bf16[2,2,64,256]{3,2,1,0:T(8,128)(2,1)S(1)} %get-tuple-element.84), channel_id=1, source_target_pairs={{0,8},{8,0},{16,24},{24,16},{1,9},{9,1},{17,25},{25,17},{2,10},{10... | collective-permute-start | bytes 393224 | tf_op jit(solution)/shard_map/ppermute | solution.py:312
  88.1 0.8 collective-permute-start.24
  88.9 6.6 %all-to-all-start.1 = ((bf16[8,2,128,256]{3,2,1,0:T(8,128)(2,1)}), bf16[8,2,128,256]{3,2,1,0:T(8,128)(2,1)S(1)}, u32[]{:S(2)}, u32[]{:S(2)}) async-start(bf16[8,2,128,256]{3,2,1,0:T(8,128)(2,1)} %get-tuple-element.81), calls=%async_computation.1 | async-start | bytes 2097152 | tf_op jit(solution)/shard_map/all_to_all | solution.py:299
  95.5 1.7 %collective-permute-start.25 = (bf16[2,2,64,256]{3,2,1,0:T(8,128)(2,1)S(1)}, bf16[2,2,64,256]{3,2,1,0:T(8,128)(2,1)S(1)}, u32[]{:S(2)}, u32[]{:S(2)}) collective-permute-start(bf16[2,2,64,256]{3,2,1,0:T(8,128)(2,1)S(1)} %get-tuple-element.86), channel_id=1, source_target_pairs={{0,24},{8,16},{16,8},{24,0},{1,25},{9,17},{17,9},{25,1},{2,26},{10... | collective-permute-start | bytes 393224 | tf_op jit(solution)/shard_map/ppermute | solution.py:312
  97.2 1.0 copy-done.9
  98.2 1.1 shard_map.82.refs_3_
  99.3 4.0 %collective-permute-done.25.refs_2_ = bf16[2,2,64,256]{3,2,1,0:T(8,128)(2,1)S(1)} collective-permute-done((bf16[2,2,64,256]{3,2,1,0:T(8,128)(2,1)S(1)}, bf16[2,2,64,256]{3,2,1,0:T(8,128)(2,1)S(1)}, u32[]{:S(2)}, u32[]{:S(2)}) %collective-permute-start.25) | collective-permute-done | bytes 131104 | tf_op jit(solution)/shard_map/ppermute | solution.py:312
  103.3 1.2 shard_map.83
  104.5 1.7 %collective-permute-start.30 = (bf16[2,128,256]{2,1,0:T(8,128)(2,1)S(1)}, bf16[2,128,256]{2,1,0:T(8,128)(2,1)S(1)}, u32[]{:S(2)}, u32[]{:S(2)}) collective-permute-start(bf16[2,128,256]{2,1,0:T(8,128)(2,1)S(1)} %get-tuple-element.93), channel_id=1, source_target_pairs={{0,2},{1,3},{2,0},{3,1},{4,6},{5,7},{6,4},{7,5},{8,10},{9,11},{10,... | collective-permute-start | bytes 393224 | tf_op jit(solution)/shard_map/ppermute | solution.py:305
  106.3 0.1 collective-permute-start.31
  106.4 2.2 %collective-permute-start.32 = (bf16[2,128,256]{2,1,0:T(8,128)(2,1)S(1)}, bf16[2,128,256]{2,1,0:T(8,128)(2,1)S(1)}, u32[]{:S(2)}, u32[]{:S(2)}) collective-permute-start(bf16[2,128,256]{2,1,0:T(8,128)(2,1)S(1)} %get-tuple-element.95), channel_id=1, source_target_pairs={{0,4},{1,5},{2,6},{3,7},{4,0},{5,1},{6,2},{7,3},{8,12},{9,13},{10,... | collective-permute-start | bytes 393224 | tf_op jit(solution)/shard_map/ppermute | solution.py:305
  108.6 2.9 %collective-permute-start.34 = (bf16[2,128,256]{2,1,0:T(8,128)(2,1)S(1)}, bf16[2,128,256]{2,1,0:T(8,128)(2,1)S(1)}, u32[]{:S(2)}, u32[]{:S(2)}) collective-permute-start(bf16[2,128,256]{2,1,0:T(8,128)(2,1)S(1)} %get-tuple-element.97), channel_id=1, source_target_pairs={{0,6},{1,7},{2,4},{3,5},{4,2},{5,3},{6,0},{7,1},{8,14},{9,15},{10,... | collective-permute-start | bytes 393224 | tf_op jit(solution)/shard_map/ppermute | solution.py:305
  111.5 1.8 %collective-permute-done.30.refs_2_ = bf16[2,128,256]{2,1,0:T(8,128)(2,1)S(1)} collective-permute-done((bf16[2,128,256]{2,1,0:T(8,128)(2,1)S(1)}, bf16[2,128,256]{2,1,0:T(8,128)(2,1)S(1)}, u32[]{:S(2)}, u32[]{:S(2)}) %collective-permute-start.30) | collective-permute-done | bytes 131104 | tf_op jit(solution)/shard_map/ppermute | solution.py:305
  113.3 0.2 collective-permute-start.35
  113.5 0.1 broadcast_in_dim.4.row
  113.7 1.4 %copy-done.7 = bf16[512,1536]{1,0:T(8,128)(2,1)S(1)} copy-done((bf16[512,1536]{1,0:T(8,128)(2,1)S(1)}, bf16[512,1536]{1,0:T(8,128)(2,1)}, u32[]{:S(2)}) %copy-start.7) | copy-done | bytes 1572888
  115.1 7.8 %shard_map.81.source = f32[2,512,512]{2,1,0:T(8,128)} custom-call(s32[2]{0:T(128)S(1)} %copy-done.5, f32[8]{0:T(128)S(1)} %copy-done.6, f32[2,512,512]{2,1,0:T(8,128)} %bitcast.14, bf16[8,2,128,256]{3,2,1,0:T(8,128)(2,1)S(1)} %all-to-all-done.1.blocks, f32[512,128]{1,0:T(8,128)S(1)} %broadcast_in_dim.4.row, f32[1,512]{1,0:T(1,128)S(1)} %bitcast.20, ...), custom_call_target="tpu_custom_call" | custom-call | flops 3221225472 | bytes 6291456 | tf_op jit(solution)/shard_map/pallas_call | solution.py:427
  122.9 2.8 %shard_map.84 = f32[2,512,512]{2,1,0:T(8,128)} custom-call(s32[2]{0:T(128)S(1)} %copy-done.5, f32[2,512,512]{2,1,0:T(8,128)} %shard_map.81.source, bf16[2,128,256]{2,1,0:T(8,128)(2,1)S(1)} %get-tuple-element.91.refs_0_, bf16[2,128,256]{2,1,0:T(8,128)(2,1)S(1)} %collective-permute-done.29.refs_1_, ...), custom_call_target="tpu_custom_call", output_to_operand_aliasing={{}: (1, {})} | custom-call | flops 524288 | bytes 5242880 | tf_op jit(solution)/shard_map/pallas_call | solution.py:450
  (64 shorter events, 0.5 us)
Async XLA Ops:
  0.0 10.2 %copy-start.13 = (s32[8]{0:T(128)S(1)}, s32[8]{0:T(128)}, u32[]{:S(2)}) copy-start(s32[8]{0:T(128)} %constant.25.clone) | copy-start | bytes 100
  0.0 11.4 %copy-start.12 = (s32[8]{0:T(128)S(1)}, s32[8]{0:T(128)}, u32[]{:S(2)}) copy-start(s32[8]{0:T(128)} %constant.24.clone) | copy-start | bytes 100
  0.0 16.0 %copy-start.2 = (f32[512]{0:T(512)S(1)}, f32[512]{0:T(512)}, u32[]{:S(2)}) copy-start(f32[512]{0:T(512)} %param.11) | copy-start | bytes 6148
  0.0 12.7 %collective-permute-start = (bf16[3,64,512]{2,1,0:T(8,128)(2,1)}, bf16[3,64,512]{2,1,0:T(8,128)(2,1)S(1)}, u32[]{:S(2)}, u32[]{:S(2)}) collective-permute-start(bf16[3,64,512]{2,1,0:T(8,128)(2,1)} %refs_0_.1), channel_id=1, source_target_pairs={{0,2},{1,3},{2,0},{3,1},{4,6},{5,7},{6,4},{7,5},{8,10},{9,11},{10,... | collective-permute-start | bytes 589832 | tf_op jit(solution)/shard_map/ppermute | solution.py:338
  3.0 12.8 %collective-permute-start.1 = (bf16[3,64,512]{2,1,0:T(8,128)(2,1)}, bf16[3,64,512]{2,1,0:T(8,128)(2,1)S(1)}, u32[]{:S(2)}, u32[]{:S(2)}) collective-permute-start(bf16[3,64,512]{2,1,0:T(8,128)(2,1)} %refs_0_.1), channel_id=1, source_target_pairs={{0,4},{1,5},{2,6},{3,7},{4,0},{5,1},{6,2},{7,3},{8,12},{9,13},{10,... | collective-permute-start | bytes 589832 | tf_op jit(solution)/shard_map/ppermute | solution.py:338
  4.5 11.2 %collective-permute-start.2 = (bf16[3,64,512]{2,1,0:T(8,128)(2,1)}, bf16[3,64,512]{2,1,0:T(8,128)(2,1)S(1)}, u32[]{:S(2)}, u32[]{:S(2)}) collective-permute-start(bf16[3,64,512]{2,1,0:T(8,128)(2,1)} %refs_0_.1), channel_id=1, source_target_pairs={{0,6},{1,7},{2,4},{3,5},{4,2},{5,3},{6,0},{7,1},{8,14},{9,15},{10,... | collective-permute-start | bytes 589832 | tf_op jit(solution)/shard_map/ppermute | solution.py:338
  4.6 23.7 %copy-start.4 = (s32[2]{0:T(128)}, s32[2]{0:T(128)S(1)}, u32[]{:S(2)}) copy-start(s32[2]{0:T(128)S(1)} %pad_add_fusion.place.source) | copy-start | bytes 28
  4.6 1.6 %copy-start = (f32[2,1,512,512]{3,2,1,0:T(8,128)S(1)}, f32[2,1,512,512]{3,2,1,0:T(8,128)}, u32[]{:S(2)}) copy-start(f32[2,1,512,512]{3,2,1,0:T(8,128)} %param.7) | copy-start | bytes 6291460
  6.2 9.6 %copy-start.1 = (bf16[3,64,512]{2,1,0:T(8,128)(2,1)S(1)}, bf16[3,64,512]{2,1,0:T(8,128)(2,1)}, u32[]{:S(2)}) copy-start(bf16[3,64,512]{2,1,0:T(8,128)(2,1)} %refs_0_.1) | copy-start | bytes 589828
  7.1 9.2 %collective-permute-start.10 = (bf16[2,128,256]{2,1,0:T(8,128)(2,1)S(1)}, bf16[2,128,256]{2,1,0:T(8,128)(2,1)S(1)}, u32[]{:S(2)}, u32[]{:S(2)}) collective-permute-start(bf16[2,128,256]{2,1,0:T(8,128)(2,1)S(1)} %get-tuple-element.62), channel_id=1, source_target_pairs={{0,7},{1,6},{2,5},{3,4},{4,3},{5,2},{6,1},{7,0},{8,15},{9,14},{10,... | collective-permute-start | bytes 393224 | tf_op jit(solution)/shard_map/ppermute | solution.py:305
  8.7 10.1 %collective-permute-start.4 = (bf16[2,128,256]{2,1,0:T(8,128)(2,1)S(1)}, bf16[2,128,256]{2,1,0:T(8,128)(2,1)S(1)}, u32[]{:S(2)}, u32[]{:S(2)}) collective-permute-start(bf16[2,128,256]{2,1,0:T(8,128)(2,1)S(1)} %get-tuple-element.56), channel_id=1, source_target_pairs={{0,1},{1,0},{2,3},{3,2},{4,5},{5,4},{6,7},{7,6},{8,9},{9,8},{10,11... | collective-permute-start | bytes 393224 | tf_op jit(solution)/shard_map/ppermute | solution.py:305
  12.7 15.4 %collective-permute-start.5 = (bf16[2,128,256]{2,1,0:T(8,128)(2,1)S(1)}, bf16[2,128,256]{2,1,0:T(8,128)(2,1)S(1)}, u32[]{:S(2)}, u32[]{:S(2)}) collective-permute-start(bf16[2,128,256]{2,1,0:T(8,128)(2,1)S(1)} %get-tuple-element.57), channel_id=1, source_target_pairs={{0,2},{1,3},{2,0},{3,1},{4,6},{5,7},{6,4},{7,5},{8,10},{9,11},{10,... | collective-permute-start | bytes 393224 | tf_op jit(solution)/shard_map/ppermute | solution.py:305
  15.8 12.3 %collective-permute-start.6 = (bf16[2,128,256]{2,1,0:T(8,128)(2,1)S(1)}, bf16[2,128,256]{2,1,0:T(8,128)(2,1)S(1)}, u32[]{:S(2)}, u32[]{:S(2)}) collective-permute-start(bf16[2,128,256]{2,1,0:T(8,128)(2,1)S(1)} %get-tuple-element.58), channel_id=1, source_target_pairs={{0,3},{1,2},{2,1},{3,0},{4,7},{5,6},{6,5},{7,4},{8,11},{9,10},{10,... | collective-permute-start | bytes 393224 | tf_op jit(solution)/shard_map/ppermute | solution.py:305
  15.9 3.0 %collective-permute-start.3 = (bf16[4,3,64,512]{3,2,1,0:T(8,128)(2,1)S(1)}, bf16[4,3,64,512]{3,2,1,0:T(8,128)(2,1)S(1)}, u32[]{:S(2)}, u32[]{:S(2)}) collective-permute-start(bf16[4,3,64,512]{3,2,1,0:T(8,128)(2,1)S(1)} %pad_maximum_fusion), channel_id=1, source_target_pairs={{0,1},{1,0},{2,3},{3,2},{4,5},{5,4},{6,7},{7,6},{8,9},{9,8},{10,11... | collective-permute-start | bytes 2359304 | tf_op jit(solution)/shard_map/ppermute | solution.py:338
  16.3 11.7 %collective-permute-start.7 = (bf16[2,128,256]{2,1,0:T(8,128)(2,1)S(1)}, bf16[2,128,256]{2,1,0:T(8,128)(2,1)S(1)}, u32[]{:S(2)}, u32[]{:S(2)}) collective-permute-start(bf16[2,128,256]{2,1,0:T(8,128)(2,1)S(1)} %get-tuple-element.59), channel_id=1, source_target_pairs={{0,4},{1,5},{2,6},{3,7},{4,0},{5,1},{6,2},{7,3},{8,12},{9,13},{10,... | collective-permute-start | bytes 393224 | tf_op jit(solution)/shard_map/ppermute | solution.py:305
  18.8 9.6 %collective-permute-start.8 = (bf16[2,128,256]{2,1,0:T(8,128)(2,1)S(1)}, bf16[2,128,256]{2,1,0:T(8,128)(2,1)S(1)}, u32[]{:S(2)}, u32[]{:S(2)}) collective-permute-start(bf16[2,128,256]{2,1,0:T(8,128)(2,1)S(1)} %get-tuple-element.60), channel_id=1, source_target_pairs={{0,5},{1,4},{2,7},{3,6},{4,1},{5,0},{6,3},{7,2},{8,13},{9,12},{10,... | collective-permute-start | bytes 393224 | tf_op jit(solution)/shard_map/ppermute | solution.py:305
  18.9 14.6 %copy-start.11 = (bf16[8,8]{1,0:T(8,128)(2,1)S(1)}, bf16[8,8]{1,0:T(8,128)(2,1)}, u32[]{:S(2)}) copy-start(bf16[8,8]{1,0:T(8,128)(2,1)} %param.9) | copy-start | bytes 388
  18.9 9.4 %collective-permute-start.9 = (bf16[2,128,256]{2,1,0:T(8,128)(2,1)S(1)}, bf16[2,128,256]{2,1,0:T(8,128)(2,1)S(1)}, u32[]{:S(2)}, u32[]{:S(2)}) collective-permute-start(bf16[2,128,256]{2,1,0:T(8,128)(2,1)S(1)} %get-tuple-element.61), channel_id=1, source_target_pairs={{0,6},{1,7},{2,4},{3,5},{4,2},{5,3},{6,0},{7,1},{8,14},{9,15},{10,... | collective-permute-start | bytes 393224 | tf_op jit(solution)/shard_map/ppermute | solution.py:305
  29.0 12.4 %collective-permute-start.11 = (bf16[2,2,64,256]{3,2,1,0:T(8,128)(2,1)S(1)}, bf16[2,2,64,256]{3,2,1,0:T(8,128)(2,1)S(1)}, u32[]{:S(2)}, u32[]{:S(2)}) collective-permute-start(bf16[2,2,64,256]{3,2,1,0:T(8,128)(2,1)S(1)} %get-tuple-element.64), channel_id=1, source_target_pairs={{0,8},{8,0},{16,24},{24,16},{1,9},{9,1},{17,25},{25,17},{2,10},{10... | collective-permute-start | bytes 393224 | tf_op jit(solution)/shard_map/ppermute | solution.py:312
  30.6 12.9 %collective-permute-start.12 = (bf16[2,2,64,256]{3,2,1,0:T(8,128)(2,1)S(1)}, bf16[2,2,64,256]{3,2,1,0:T(8,128)(2,1)S(1)}, u32[]{:S(2)}, u32[]{:S(2)}) collective-permute-start(bf16[2,2,64,256]{3,2,1,0:T(8,128)(2,1)S(1)} %get-tuple-element.65), channel_id=1, source_target_pairs={{0,16},{8,24},{16,0},{24,8},{1,17},{9,25},{17,1},{25,9},{2,18},{10... | collective-permute-start | bytes 393224 | tf_op jit(solution)/shard_map/ppermute | solution.py:312
  33.2 10.3 %collective-permute-start.13 = (bf16[2,2,64,256]{3,2,1,0:T(8,128)(2,1)S(1)}, bf16[2,2,64,256]{3,2,1,0:T(8,128)(2,1)S(1)}, u32[]{:S(2)}, u32[]{:S(2)}) collective-permute-start(bf16[2,2,64,256]{3,2,1,0:T(8,128)(2,1)S(1)} %get-tuple-element.66), channel_id=1, source_target_pairs={{0,24},{8,16},{16,8},{24,0},{1,25},{9,17},{17,9},{25,1},{2,26},{10... | collective-permute-start | bytes 393224 | tf_op jit(solution)/shard_map/ppermute | solution.py:312
  33.6 18.9 %all-to-all-start = ((bf16[8,2,128,256]{3,2,1,0:T(8,128)(2,1)}), bf16[8,2,128,256]{3,2,1,0:T(8,128)(2,1)S(1)}, u32[]{:S(2)}, u32[]{:S(2)}) async-start(bf16[8,2,128,256]{3,2,1,0:T(8,128)(2,1)} %get-tuple-element.54), calls=%async_computation | async-start | bytes 2097152 | tf_op jit(solution)/shard_map/all_to_all | solution.py:299
  37.2 21.7 %collective-permute-start.17 = (bf16[2,2,64,256]{3,2,1,0:T(8,128)(2,1)S(1)}, bf16[2,2,64,256]{3,2,1,0:T(8,128)(2,1)S(1)}, u32[]{:S(2)}, u32[]{:S(2)}) collective-permute-start(bf16[2,2,64,256]{3,2,1,0:T(8,128)(2,1)S(1)} %get-tuple-element.74), channel_id=1, source_target_pairs={{0,8},{8,0},{16,24},{24,16},{1,9},{9,1},{17,25},{25,17},{2,10},{10... | collective-permute-start | bytes 393224 | tf_op jit(solution)/shard_map/ppermute | solution.py:312
  37.9 21.2 %collective-permute-start.18 = (bf16[2,2,64,256]{3,2,1,0:T(8,128)(2,1)S(1)}, bf16[2,2,64,256]{3,2,1,0:T(8,128)(2,1)S(1)}, u32[]{:S(2)}, u32[]{:S(2)}) collective-permute-start(bf16[2,2,64,256]{3,2,1,0:T(8,128)(2,1)S(1)} %get-tuple-element.75), channel_id=1, source_target_pairs={{0,16},{8,24},{16,0},{24,8},{1,17},{9,25},{17,1},{25,9},{2,18},{10... | collective-permute-start | bytes 393224 | tf_op jit(solution)/shard_map/ppermute | solution.py:312
  41.4 17.7 %collective-permute-start.19 = (bf16[2,2,64,256]{3,2,1,0:T(8,128)(2,1)S(1)}, bf16[2,2,64,256]{3,2,1,0:T(8,128)(2,1)S(1)}, u32[]{:S(2)}, u32[]{:S(2)}) collective-permute-start(bf16[2,2,64,256]{3,2,1,0:T(8,128)(2,1)S(1)} %get-tuple-element.76), channel_id=1, source_target_pairs={{0,24},{8,16},{16,8},{24,0},{1,25},{9,17},{17,9},{25,1},{2,26},{10... | collective-permute-start | bytes 393224 | tf_op jit(solution)/shard_map/ppermute | solution.py:312
  44.8 14.3 %copy-start.5 = (s32[2]{0:T(128)S(1)}, s32[2]{0:T(128)}, u32[]{:S(2)}) copy-start(s32[2]{0:T(128)} %copy-done.4) | copy-start | bytes 28
  52.5 0.6 copy-start.10
  54.6 10.3 %collective-permute-start.14 = (bf16[2,2,64,256]{3,2,1,0:T(8,128)(2,1)S(1)}, bf16[2,2,64,256]{3,2,1,0:T(8,128)(2,1)S(1)}, u32[]{:S(2)}, u32[]{:S(2)}) collective-permute-start(bf16[2,2,64,256]{3,2,1,0:T(8,128)(2,1)S(1)} %get-tuple-element.69.refs_1_), channel_id=1, source_target_pairs={{0,8},{8,0},{16,24},{24,16},{1,9},{9,1},{17,25},{25,17},{2,10},{10... | collective-permute-start | bytes 393224 | tf_op jit(solution)/shard_map/ppermute | solution.py:312
  56.0 12.9 %collective-permute-start.15 = (bf16[2,2,64,256]{3,2,1,0:T(8,128)(2,1)S(1)}, bf16[2,2,64,256]{3,2,1,0:T(8,128)(2,1)S(1)}, u32[]{:S(2)}, u32[]{:S(2)}) collective-permute-start(bf16[2,2,64,256]{3,2,1,0:T(8,128)(2,1)S(1)} %get-tuple-element.70.refs_2_), channel_id=1, source_target_pairs={{0,16},{8,24},{16,0},{24,8},{1,17},{9,25},{17,1},{25,9},{2,18},{10... | collective-permute-start | bytes 393224 | tf_op jit(solution)/shard_map/ppermute | solution.py:312
  58.9 10.0 %collective-permute-start.16 = (bf16[2,2,64,256]{3,2,1,0:T(8,128)(2,1)S(1)}, bf16[2,2,64,256]{3,2,1,0:T(8,128)(2,1)S(1)}, u32[]{:S(2)}, u32[]{:S(2)}) collective-permute-start(bf16[2,2,64,256]{3,2,1,0:T(8,128)(2,1)S(1)} %get-tuple-element.71.refs_3_), channel_id=1, source_target_pairs={{0,24},{8,16},{16,8},{24,0},{1,25},{9,17},{17,9},{25,1},{2,26},{10... | collective-permute-start | bytes 393224 | tf_op jit(solution)/shard_map/ppermute | solution.py:312
  59.1 9.8 %copy-start.6 = (f32[8]{0:T(128)S(1)}, f32[8]{0:T(128)}, u32[]{:S(2)}) copy-start(f32[8]{0:T(128)} %occ.9) | copy-start | bytes 100
  60.7 19.4 %collective-permute-start.20 = (bf16[2,2,64,256]{3,2,1,0:T(8,128)(2,1)S(1)}, bf16[2,2,64,256]{3,2,1,0:T(8,128)(2,1)S(1)}, u32[]{:S(2)}, u32[]{:S(2)}) collective-permute-start(bf16[2,2,64,256]{3,2,1,0:T(8,128)(2,1)S(1)} %get-tuple-element.78.refs_2_), channel_id=1, source_target_pairs={{0,8},{8,0},{16,24},{24,16},{1,9},{9,1},{17,25},{25,17},{2,10},{10... | collective-permute-start | bytes 393224 | tf_op jit(solution)/shard_map/ppermute | solution.py:312
  61.2 20.6 %collective-permute-start.21 = (bf16[2,2,64,256]{3,2,1,0:T(8,128)(2,1)S(1)}, bf16[2,2,64,256]{3,2,1,0:T(8,128)(2,1)S(1)}, u32[]{:S(2)}, u32[]{:S(2)}) collective-permute-start(bf16[2,2,64,256]{3,2,1,0:T(8,128)(2,1)S(1)} %get-tuple-element.79.refs_3_), channel_id=1, source_target_pairs={{0,16},{8,24},{16,0},{24,8},{1,17},{9,25},{17,1},{25,9},{2,18},{10... | collective-permute-start | bytes 393224 | tf_op jit(solution)/shard_map/ppermute | solution.py:312
  65.0 16.8 %collective-permute-start.22 = (bf16[2,2,64,256]{3,2,1,0:T(8,128)(2,1)S(1)}, bf16[2,2,64,256]{3,2,1,0:T(8,128)(2,1)S(1)}, u32[]{:S(2)}, u32[]{:S(2)}) collective-permute-start(bf16[2,2,64,256]{3,2,1,0:T(8,128)(2,1)S(1)} %get-tuple-element.80.refs_4_), channel_id=1, source_target_pairs={{0,24},{8,16},{16,8},{24,0},{1,25},{9,17},{17,9},{25,1},{2,26},{10... | collective-permute-start | bytes 393224 | tf_op jit(solution)/shard_map/ppermute | solution.py:312
  71.4 0.8 copy-start.8
  72.2 23.3 %collective-permute-start.26 = (bf16[2,2,64,256]{3,2,1,0:T(8,128)(2,1)S(1)}, bf16[2,2,64,256]{3,2,1,0:T(8,128)(2,1)S(1)}, u32[]{:S(2)}, u32[]{:S(2)}) collective-permute-start(bf16[2,2,64,256]{3,2,1,0:T(8,128)(2,1)S(1)} %get-tuple-element.88), channel_id=1, source_target_pairs={{0,8},{8,0},{16,24},{24,16},{1,9},{9,1},{17,25},{25,17},{2,10},{10... | collective-permute-start | bytes 393224 | tf_op jit(solution)/shard_map/ppermute | solution.py:312
  79.4 17.8 %collective-permute-start.27 = (bf16[2,2,64,256]{3,2,1,0:T(8,128)(2,1)S(1)}, bf16[2,2,64,256]{3,2,1,0:T(8,128)(2,1)S(1)}, u32[]{:S(2)}, u32[]{:S(2)}) collective-permute-start(bf16[2,2,64,256]{3,2,1,0:T(8,128)(2,1)S(1)} %get-tuple-element.89), channel_id=1, source_target_pairs={{0,16},{8,24},{16,0},{24,8},{1,17},{9,25},{17,1},{25,9},{2,18},{10... | collective-permute-start | bytes 393224 | tf_op jit(solution)/shard_map/ppermute | solution.py:312
  80.2 17.0 %collective-permute-start.28 = (bf16[2,2,64,256]{3,2,1,0:T(8,128)(2,1)S(1)}, bf16[2,2,64,256]{3,2,1,0:T(8,128)(2,1)S(1)}, u32[]{:S(2)}, u32[]{:S(2)}) collective-permute-start(bf16[2,2,64,256]{3,2,1,0:T(8,128)(2,1)S(1)} %get-tuple-element.90), channel_id=1, source_target_pairs={{0,24},{8,16},{16,8},{24,0},{1,25},{9,17},{17,9},{25,1},{2,26},{10... | collective-permute-start | bytes 393224 | tf_op jit(solution)/shard_map/ppermute | solution.py:312
  85.4 13.9 %collective-permute-start.23 = (bf16[2,2,64,256]{3,2,1,0:T(8,128)(2,1)S(1)}, bf16[2,2,64,256]{3,2,1,0:T(8,128)(2,1)S(1)}, u32[]{:S(2)}, u32[]{:S(2)}) collective-permute-start(bf16[2,2,64,256]{3,2,1,0:T(8,128)(2,1)S(1)} %get-tuple-element.84), channel_id=1, source_target_pairs={{0,8},{8,0},{16,24},{24,16},{1,9},{9,1},{17,25},{25,17},{2,10},{10... | collective-permute-start | bytes 393224 | tf_op jit(solution)/shard_map/ppermute | solution.py:312
  88.1 11.2 %collective-permute-start.24 = (bf16[2,2,64,256]{3,2,1,0:T(8,128)(2,1)S(1)}, bf16[2,2,64,256]{3,2,1,0:T(8,128)(2,1)S(1)}, u32[]{:S(2)}, u32[]{:S(2)}) collective-permute-start(bf16[2,2,64,256]{3,2,1,0:T(8,128)(2,1)S(1)} %get-tuple-element.85), channel_id=1, source_target_pairs={{0,16},{8,24},{16,0},{24,8},{1,17},{9,25},{17,1},{25,9},{2,18},{10... | collective-permute-start | bytes 393224 | tf_op jit(solution)/shard_map/ppermute | solution.py:312
  88.9 24.7 %all-to-all-start.1 = ((bf16[8,2,128,256]{3,2,1,0:T(8,128)(2,1)}), bf16[8,2,128,256]{3,2,1,0:T(8,128)(2,1)S(1)}, u32[]{:S(2)}, u32[]{:S(2)}) async-start(bf16[8,2,128,256]{3,2,1,0:T(8,128)(2,1)} %get-tuple-element.81), calls=%async_computation.1 | async-start | bytes 2097152 | tf_op jit(solution)/shard_map/all_to_all | solution.py:299
  95.5 7.8 %collective-permute-start.25 = (bf16[2,2,64,256]{3,2,1,0:T(8,128)(2,1)S(1)}, bf16[2,2,64,256]{3,2,1,0:T(8,128)(2,1)S(1)}, u32[]{:S(2)}, u32[]{:S(2)}) collective-permute-start(bf16[2,2,64,256]{3,2,1,0:T(8,128)(2,1)S(1)} %get-tuple-element.86), channel_id=1, source_target_pairs={{0,24},{8,16},{16,8},{24,0},{1,25},{9,17},{17,9},{25,1},{2,26},{10... | collective-permute-start | bytes 393224 | tf_op jit(solution)/shard_map/ppermute | solution.py:312
  97.1 1.0 copy-start.9
  103.3 10.3 %copy-start.3 = (f32[512]{0:T(512)S(1)}, f32[512]{0:T(512)}, u32[]{:S(2)}) copy-start(f32[512]{0:T(512)} %param.11) | copy-start | bytes 6148
  104.4 4.1 %collective-permute-start.29 = (bf16[2,128,256]{2,1,0:T(8,128)(2,1)S(1)}, bf16[2,128,256]{2,1,0:T(8,128)(2,1)S(1)}, u32[]{:S(2)}, u32[]{:S(2)}) collective-permute-start(bf16[2,128,256]{2,1,0:T(8,128)(2,1)S(1)} %get-tuple-element.92), channel_id=1, source_target_pairs={{0,1},{1,0},{2,3},{3,2},{4,5},{5,4},{6,7},{7,6},{8,9},{9,8},{10,11... | collective-permute-start | bytes 393224 | tf_op jit(solution)/shard_map/ppermute | solution.py:305
  104.5 8.8 %collective-permute-start.30 = (bf16[2,128,256]{2,1,0:T(8,128)(2,1)S(1)}, bf16[2,128,256]{2,1,0:T(8,128)(2,1)S(1)}, u32[]{:S(2)}, u32[]{:S(2)}) collective-permute-start(bf16[2,128,256]{2,1,0:T(8,128)(2,1)S(1)} %get-tuple-element.93), channel_id=1, source_target_pairs={{0,2},{1,3},{2,0},{3,1},{4,6},{5,7},{6,4},{7,5},{8,10},{9,11},{10,... | collective-permute-start | bytes 393224 | tf_op jit(solution)/shard_map/ppermute | solution.py:305
  106.3 16.6 %collective-permute-start.31 = (bf16[2,128,256]{2,1,0:T(8,128)(2,1)S(1)}, bf16[2,128,256]{2,1,0:T(8,128)(2,1)S(1)}, u32[]{:S(2)}, u32[]{:S(2)}) collective-permute-start(bf16[2,128,256]{2,1,0:T(8,128)(2,1)S(1)} %get-tuple-element.94), channel_id=1, source_target_pairs={{0,3},{1,2},{2,1},{3,0},{4,7},{5,6},{6,5},{7,4},{8,11},{9,10},{10,... | collective-permute-start | bytes 393224 | tf_op jit(solution)/shard_map/ppermute | solution.py:305
  106.4 16.5 %collective-permute-start.32 = (bf16[2,128,256]{2,1,0:T(8,128)(2,1)S(1)}, bf16[2,128,256]{2,1,0:T(8,128)(2,1)S(1)}, u32[]{:S(2)}, u32[]{:S(2)}) collective-permute-start(bf16[2,128,256]{2,1,0:T(8,128)(2,1)S(1)} %get-tuple-element.95), channel_id=1, source_target_pairs={{0,4},{1,5},{2,6},{3,7},{4,0},{5,1},{6,2},{7,3},{8,12},{9,13},{10,... | collective-permute-start | bytes 393224 | tf_op jit(solution)/shard_map/ppermute | solution.py:305
  108.6 14.3 %collective-permute-start.33 = (bf16[2,128,256]{2,1,0:T(8,128)(2,1)S(1)}, bf16[2,128,256]{2,1,0:T(8,128)(2,1)S(1)}, u32[]{:S(2)}, u32[]{:S(2)}) collective-permute-start(bf16[2,128,256]{2,1,0:T(8,128)(2,1)S(1)} %get-tuple-element.96), channel_id=1, source_target_pairs={{0,5},{1,4},{2,7},{3,6},{4,1},{5,0},{6,3},{7,2},{8,13},{9,12},{10,... | collective-permute-start | bytes 393224 | tf_op jit(solution)/shard_map/ppermute | solution.py:305
  108.6 14.3 %collective-permute-start.34 = (bf16[2,128,256]{2,1,0:T(8,128)(2,1)S(1)}, bf16[2,128,256]{2,1,0:T(8,128)(2,1)S(1)}, u32[]{:S(2)}, u32[]{:S(2)}) collective-permute-start(bf16[2,128,256]{2,1,0:T(8,128)(2,1)S(1)} %get-tuple-element.97), channel_id=1, source_target_pairs={{0,6},{1,7},{2,4},{3,5},{4,2},{5,3},{6,0},{7,1},{8,14},{9,15},{10,... | collective-permute-start | bytes 393224 | tf_op jit(solution)/shard_map/ppermute | solution.py:305
  113.3 9.6 %collective-permute-start.35 = (bf16[2,128,256]{2,1,0:T(8,128)(2,1)S(1)}, bf16[2,128,256]{2,1,0:T(8,128)(2,1)S(1)}, u32[]{:S(2)}, u32[]{:S(2)}) collective-permute-start(bf16[2,128,256]{2,1,0:T(8,128)(2,1)S(1)} %get-tuple-element.98), channel_id=1, source_target_pairs={{0,7},{1,6},{2,5},{3,4},{4,3},{5,2},{6,1},{7,0},{8,15},{9,14},{10,... | collective-permute-start | bytes 393224 | tf_op jit(solution)/shard_map/ppermute | solution.py:305
  113.7 1.4 %copy-start.7 = (bf16[512,1536]{1,0:T(8,128)(2,1)S(1)}, bf16[512,1536]{1,0:T(8,128)(2,1)}, u32[]{:S(2)}) copy-start(bf16[512,1536]{1,0:T(8,128)(2,1)} %get-tuple-element.82.whole) | copy-start | bytes 4718596

commit v15 on v14

--- a/solution.py
+++ b/solution.py
@@ -137,11 +137,23 @@
         pack_pair(tiles, total, out, pair)
 
 
-def second_ladder_kernel(tiles, first, place, occ, source, blocks, row, column, whole, out, inner, total, matrix):
+def second_ladder_kernel(tiles, first, place, occ, source, blocks, row, column, vectors, out,
+                         whole, inner, total, matrix, arrived):
+    fetch = pltpu.make_async_copy(vectors, whole, arrived)
+
+    @pl.when(pl.program_id(0) == 0)
+    def _():
+        fetch.start()
+
     def put(a, b, tile):
         matrix[tiles.span(a), tiles.span(b)] = tile.astype(NARROW)
 
     unpack_pair(tiles, blocks, 0, put)
+
+    @pl.when(pl.program_id(0) == 0)
+    def _():
+        fetch.wait()
+
     ladder_pair(matrix[...], whole, inner, total)
     base = occ[place[0] * first + pl.program_id(0)] + occ[place[1]]
     strip = math.gcd(64, total.shape[0])
@@ -417,7 +429,7 @@
         )
         sent, rest, mixed = [sent_one], rest + [rest_one], mixed + [mixed_one]
     other = [across_first([None] + x, groups)[1:] for x in mixed]
-    back = exchange(sent[0])
+    back = exchange(tie(sent[0], other[0][min(1, groups - 2)]))
     def by_pair(*shape):
         return pl.BlockSpec((1, *shape), lambda pair: (pair, 0, 0))
 
@@ -431,10 +443,13 @@
         in_specs=[
             SMEM, SMEM, by_pair(virtual, virtual),
             pl.BlockSpec((devices, 1, edge, 2 * edge), lambda pair: (0, pair, 0, 0)),
-            all_pairs(virtual, 128), all_pairs(1, virtual), all_pairs(*whole.shape),
+            all_pairs(virtual, 128), all_pairs(1, virtual), pl.BlockSpec(memory_space=pl.ANY),
         ],
         out_specs=by_pair(virtual, virtual),
-        scratch_shapes=[inner, square, pltpu.VMEM((virtual, virtual), NARROW)],
+        scratch_shapes=[
+            pltpu.VMEM(whole.shape, NARROW), inner, square, pltpu.VMEM((virtual, virtual), NARROW),
+            pltpu.SemaphoreType.DMA,
+        ],
         compiler_params=PARAMS,
         cost_estimate=pl.CostEstimate(flops=ladder_flops, bytes_accessed=12 * count, transcendentals=0),
     )(place, occ_energy, current, back, jnp.broadcast_to(vir_energy[:, None], (virtual, 128)),

time: 127 us -> 130 us (1.024)
  waiting for transfers between devices: 19.2 us -> 22.1 us
    ppermute x14, waiting for transfers between devices: 2.11 us -> 6.49 us  [by_distance(): lax.ppermute(parts[k], 'occj', [(d, d ^ k) for d in range(devices)])]
    all_to_all x2, starting transfers between devices: 10.2 us -> 7.12 us  [exchange(): lax.all_to_all(blocks, 'occj', split_axis=0, concat_axis=0, tiled=True)]
    ppermute x18, starting transfers between devices: 35.3 us -> 37.2 us  [across_first(): lax.ppermute(parts[s], 'occi', [(k, k ^ s) for k in range(groups)])]
    ppermute x18, waiting for transfers between devices: 6.86 us -> 5.37 us  [across_first(): lax.ppermute(parts[s], 'occi', [(k, k ^ s) for k in range(groups)])]
  transfers between devices with their start and end apart: 38 -> 38, of which waited for: 7 -> 8; matrix products, arithmetic and copies ran while one was open for 2% -> 1% of each run, Pallas kernels for 22% -> 22%
where the time goes in v15:
time: 130 us; the launch traced here: 129 us
  starting transfers between devices  66.2 us (51%)
  Pallas kernels  31.4 us (24%)
  waiting for transfers between devices  22.1 us (17%)
  local copies, waits for them, and re-layouts  6.94 us (5%)
  between operations  1.67 us (1%)
    ppermute x18, starting transfers between devices, across_first(): lax.ppermute(parts[s], 'occi', [(k, k ^ s) for k in range(groups)])  37.2 us
    pallas_call x9, Pallas kernels, call(): pl.pallas_call(body, out_shape=outs, in_specs=specs, out_specs=jax.tree.m...  19.3 us
    ppermute x14, starting transfers between devices, by_distance(): lax.ppermute(parts[k], 'occj', [(d, d ^ k) for d in range(devices)])  17.2 us
    pallas_call x1, Pallas kernels, local(): pl.pallas_call(functools.partial(second_ladder_kernel, tiles, first), gri...  8.15 us
    all_to_all x2, waiting for transfers between devices, exchange(): lax.all_to_all(blocks, 'occj', split_axis=0, concat_axis=0, tiled=True)  7.72 us
    all_to_all x2, starting transfers between devices, exchange(): lax.all_to_all(blocks, 'occj', split_axis=0, concat_axis=0, tiled=True)  7.12 us
    ppermute x14, waiting for transfers between devices, by_distance(): lax.ppermute(parts[k], 'occj', [(d, d ^ k) for d in range(devices)])  6.49 us
    unnamed x28, local copies, waits for them, and re-layouts  5.43 us
  transfers between devices with their start and end apart: 38, of which 8 were waited for; matrix products, arithmetic and copies ran while one was open for 1% of the time, Pallas kernels for 22%

profile of v15, /device:TPU:0, one launch (start us, length us, event | category | flops | bytes accessed | tf_op | source)
XLA Modules:
  0.0 128.6 jit_solution(5821313271857015842)
XLA Ops:
  0.0 3.0 %collective-permute-start = (bf16[3,64,512]{2,1,0:T(8,128)(2,1)}, bf16[3,64,512]{2,1,0:T(8,128)(2,1)S(1)}, u32[]{:S(2)}, u32[]{:S(2)}) collective-permute-start(bf16[3,64,512]{2,1,0:T(8,128)(2,1)} %refs_0_.1), channel_id=1, source_target_pairs={{0,2},{1,3},{2,0},{3,1},{4,6},{5,7},{6,4},{7,5},{8,10},{9,11},{10,... | collective-permute-start | bytes 589832 | tf_op jit(solution)/shard_map/ppermute | solution.py:350
  3.0 1.5 %collective-permute-start.1 = (bf16[3,64,512]{2,1,0:T(8,128)(2,1)}, bf16[3,64,512]{2,1,0:T(8,128)(2,1)S(1)}, u32[]{:S(2)}, u32[]{:S(2)}) collective-permute-start(bf16[3,64,512]{2,1,0:T(8,128)(2,1)} %refs_0_.1), channel_id=1, source_target_pairs={{0,4},{1,5},{2,6},{3,7},{4,0},{5,1},{6,2},{7,3},{8,12},{9,13},{10,... | collective-permute-start | bytes 589832 | tf_op jit(solution)/shard_map/ppermute | solution.py:350
  4.6 1.6 %copy-done = f32[2,1,512,512]{3,2,1,0:T(8,128)S(1)} copy-done((f32[2,1,512,512]{3,2,1,0:T(8,128)S(1)}, f32[2,1,512,512]{3,2,1,0:T(8,128)}, u32[]{:S(2)}) %copy-start) | copy-done | bytes 2097176
  6.2 0.9 shard_map.73
  7.1 1.6 %collective-permute-start.10 = (bf16[2,128,256]{2,1,0:T(8,128)(2,1)S(1)}, bf16[2,128,256]{2,1,0:T(8,128)(2,1)S(1)}, u32[]{:S(2)}, u32[]{:S(2)}) collective-permute-start(bf16[2,128,256]{2,1,0:T(8,128)(2,1)S(1)} %get-tuple-element.63), channel_id=1, source_target_pairs={{0,7},{1,6},{2,5},{3,4},{4,3},{5,2},{6,1},{7,0},{8,15},{9,14},{10,... | collective-permute-start | bytes 393224 | tf_op jit(solution)/shard_map/ppermute | solution.py:317
  8.7 1.5 %collective-permute-start.4 = (bf16[2,128,256]{2,1,0:T(8,128)(2,1)S(1)}, bf16[2,128,256]{2,1,0:T(8,128)(2,1)S(1)}, u32[]{:S(2)}, u32[]{:S(2)}) collective-permute-start(bf16[2,128,256]{2,1,0:T(8,128)(2,1)S(1)} %get-tuple-element.57), channel_id=1, source_target_pairs={{0,1},{1,0},{2,3},{3,2},{4,5},{5,4},{6,7},{7,6},{8,9},{9,8},{10,11... | collective-permute-start | bytes 393224 | tf_op jit(solution)/shard_map/ppermute | solution.py:317
  10.2 0.6 dynamic_slice.14
  11.4 0.6 dynamic_slice.12
  12.7 0.6 collective-permute-start.5
  13.3 2.5 %collective-permute-done.1.refs_2_ = bf16[3,64,512]{2,1,0:T(8,128)(2,1)S(1)} collective-permute-done((bf16[3,64,512]{2,1,0:T(8,128)(2,1)}, bf16[3,64,512]{2,1,0:T(8,128)(2,1)S(1)}, u32[]{:S(2)}, u32[]{:S(2)}) %collective-permute-start.1) | collective-permute-done | bytes 196640 | tf_op jit(solution)/shard_map/ppermute | solution.py:350
  15.8 0.1 pad_maximum_fusion
  16.0 0.1 fusion
  16.2 0.1 broadcast_add_fusion.2
  16.3 2.4 %collective-permute-start.7 = (bf16[2,128,256]{2,1,0:T(8,128)(2,1)S(1)}, bf16[2,128,256]{2,1,0:T(8,128)(2,1)S(1)}, u32[]{:S(2)}, u32[]{:S(2)}) collective-permute-start(bf16[2,128,256]{2,1,0:T(8,128)(2,1)S(1)} %get-tuple-element.60), channel_id=1, source_target_pairs={{0,4},{1,5},{2,6},{3,7},{4,0},{5,1},{6,2},{7,3},{8,12},{9,13},{10,... | collective-permute-start | bytes 393224 | tf_op jit(solution)/shard_map/ppermute | solution.py:317
  18.8 0.2 collective-permute-start.8
  18.9 2.9 %collective-permute-start.9 = (bf16[2,128,256]{2,1,0:T(8,128)(2,1)S(1)}, bf16[2,128,256]{2,1,0:T(8,128)(2,1)S(1)}, u32[]{:S(2)}, u32[]{:S(2)}) collective-permute-start(bf16[2,128,256]{2,1,0:T(8,128)(2,1)S(1)} %get-tuple-element.62), channel_id=1, source_target_pairs={{0,6},{1,7},{2,4},{3,5},{4,2},{5,3},{6,0},{7,1},{8,14},{9,15},{10,... | collective-permute-start | bytes 393224 | tf_op jit(solution)/shard_map/ppermute | solution.py:317
  21.8 6.3 %shard_map.74 = (bf16[8,2,128,256]{3,2,1,0:T(8,128)(2,1)}, bf16[512,1536]{1,0:T(8,128)(2,1)}) custom-call(s32[2]{0:T(128)S(1)} %pad_add_fusion.place.source, f32[2,512,512]{2,1,0:T(8,128)} %bitcast.13, bf16[3,64,512]{2,1,0:T(8,128)(2,1)S(1)} %copy-done.1, bf16[3,64,512]{2,1,0:T(8,128)(2,1)S(1)} %collective-permute-done.refs_1_, ...), custom_call_target="tpu_custom_call" | custom-call | flops 3221225472 | bytes 4194304 | tf_op jit(solution)/shard_map/pallas_call | solution.py:42
  28.1 0.2 collective-permute-done.8.refs_5_
  28.3 0.7 shard_map.75
  29.0 1.6 %collective-permute-start.11 = (bf16[2,2,64,256]{3,2,1,0:T(8,128)(2,1)S(1)}, bf16[2,2,64,256]{3,2,1,0:T(8,128)(2,1)S(1)}, u32[]{:S(2)}, u32[]{:S(2)}) collective-permute-start(bf16[2,2,64,256]{3,2,1,0:T(8,128)(2,1)S(1)} %get-tuple-element.65), channel_id=1, source_target_pairs={{0,8},{8,0},{16,24},{24,16},{1,9},{9,1},{17,25},{25,17},{2,10},{10... | collective-permute-start | bytes 393224 | tf_op jit(solution)/shard_map/ppermute | solution.py:324
  30.6 2.6 %collective-permute-start.12 = (bf16[2,2,64,256]{3,2,1,0:T(8,128)(2,1)S(1)}, bf16[2,2,64,256]{3,2,1,0:T(8,128)(2,1)S(1)}, u32[]{:S(2)}, u32[]{:S(2)}) collective-permute-start(bf16[2,2,64,256]{3,2,1,0:T(8,128)(2,1)S(1)} %get-tuple-element.66), channel_id=1, source_target_pairs={{0,16},{8,24},{16,0},{24,8},{1,17},{9,25},{17,1},{25,9},{2,18},{10... | collective-permute-start | bytes 393224 | tf_op jit(solution)/shard_map/ppermute | solution.py:324
  33.2 0.2 collective-permute-start.13
  33.5 0.1 broadcast_add_fusion
  33.6 3.6 %all-to-all-start = ((bf16[8,2,128,256]{3,2,1,0:T(8,128)(2,1)}), bf16[8,2,128,256]{3,2,1,0:T(8,128)(2,1)S(1)}, u32[]{:S(2)}, u32[]{:S(2)}) async-start(bf16[8,2,128,256]{3,2,1,0:T(8,128)(2,1)} %get-tuple-element.55), calls=%async_computation | async-start | bytes 2097152 | tf_op jit(solution)/shard_map/all_to_all | solution.py:311
  37.2 0.7 collective-permute-start.17
  37.9 3.5 %collective-permute-start.18 = (bf16[2,2,64,256]{3,2,1,0:T(8,128)(2,1)S(1)}, bf16[2,2,64,256]{3,2,1,0:T(8,128)(2,1)S(1)}, u32[]{:S(2)}, u32[]{:S(2)}) collective-permute-start(bf16[2,2,64,256]{3,2,1,0:T(8,128)(2,1)S(1)} %get-tuple-element.76), channel_id=1, source_target_pairs={{0,16},{8,24},{16,0},{24,8},{1,17},{9,25},{17,1},{25,9},{2,18},{10... | collective-permute-start | bytes 393224 | tf_op jit(solution)/shard_map/ppermute | solution.py:324
  41.4 0.2 collective-permute-start.19
  41.6 2.0 %collective-permute-done.12.refs_2_ = bf16[2,2,64,256]{3,2,1,0:T(8,128)(2,1)S(1)} collective-permute-done((bf16[2,2,64,256]{3,2,1,0:T(8,128)(2,1)S(1)}, bf16[2,2,64,256]{3,2,1,0:T(8,128)(2,1)S(1)}, u32[]{:S(2)}, u32[]{:S(2)}) %collective-permute-start.12) | collective-permute-done | bytes 131104 | tf_op jit(solution)/shard_map/ppermute | solution.py:324
  43.6 1.2 shard_map.76.place
  44.8 7.7 %all-to-all-done.ladder = bf16[8,2,128,256]{3,2,1,0:T(8,128)(2,1)S(1)} async-done(((bf16[8,2,128,256]{3,2,1,0:T(8,128)(2,1)}), bf16[8,2,128,256]{3,2,1,0:T(8,128)(2,1)S(1)}, u32[]{:S(2)}, u32[]{:S(2)}) %all-to-all-start) | async-done | bytes 1048608 | tf_op jit(solution)/shard_map/all_to_all | solution.py:311
  52.5 0.6 copy-done.10
  53.1 1.6 %shard_map.77 = (bf16[2,2,64,256]{3,2,1,0:T(8,128)(2,1)S(1)}, bf16[2,2,64,256]{3,2,1,0:T(8,128)(2,1)S(1)}, bf16[2,2,64,256]{3,2,1,0:T(8,128)(2,1)S(1)}, bf16[2,2,64,256]{3,2,1,0:T(8,128)(2,1)S(1)}) custom-call(s32[2]{0:T(128)S(1)} %copy-done.10, f32[8,8]{1,0:T(8,128)S(1)} %convert_element_type.3.fock, bf16[8,2,128,256]{3,2,1,0:T(8,128)(2,1)S(1)} %all-to-all-done.ladder, ...), custom_call_target="tpu_custom_call" | custom-call | flops 30000001024 | bytes 3145728 | tf_op jit(solution)/shard_map/pallas_call | solution.py:42
  54.6 1.3 %collective-permute-start.14 = (bf16[2,2,64,256]{3,2,1,0:T(8,128)(2,1)S(1)}, bf16[2,2,64,256]{3,2,1,0:T(8,128)(2,1)S(1)}, u32[]{:S(2)}, u32[]{:S(2)}) collective-permute-start(bf16[2,2,64,256]{3,2,1,0:T(8,128)(2,1)S(1)} %get-tuple-element.70.refs_1_), channel_id=1, source_target_pairs={{0,8},{8,0},{16,24},{24,16},{1,9},{9,1},{17,25},{25,17},{2,10},{10... | collective-permute-start | bytes 393224 | tf_op jit(solution)/shard_map/ppermute | solution.py:324
  56.0 2.9 %collective-permute-start.15 = (bf16[2,2,64,256]{3,2,1,0:T(8,128)(2,1)S(1)}, bf16[2,2,64,256]{3,2,1,0:T(8,128)(2,1)S(1)}, u32[]{:S(2)}, u32[]{:S(2)}) collective-permute-start(bf16[2,2,64,256]{3,2,1,0:T(8,128)(2,1)S(1)} %get-tuple-element.71.refs_2_), channel_id=1, source_target_pairs={{0,16},{8,24},{16,0},{24,8},{1,17},{9,25},{17,1},{25,9},{2,18},{10... | collective-permute-start | bytes 393224 | tf_op jit(solution)/shard_map/ppermute | solution.py:324
  58.9 0.2 collective-permute-start.16
  59.1 1.6 %shard_map.79 = (bf16[2,2,64,256]{3,2,1,0:T(8,128)(2,1)S(1)}, bf16[2,2,64,256]{3,2,1,0:T(8,128)(2,1)S(1)}, bf16[2,2,64,256]{3,2,1,0:T(8,128)(2,1)S(1)}, bf16[2,2,64,256]{3,2,1,0:T(8,128)(2,1)S(1)}) custom-call(s32[2]{0:T(128)S(1)} %copy-done.5, f32[8,8]{1,0:T(8,128)S(1)} %convert_element_type.3.fock, bf16[8,2,128,256]{3,2,1,0:T(8,128)(2,1)S(1)} %all-to-all-done.ladder, ...), custom_call_target="tpu_custom_call" | custom-call | flops 30000001024 | bytes 3145728 | tf_op jit(solution)/shard_map/pallas_call | solution.py:42
  60.7 0.4 collective-permute-start.20
  61.2 3.8 %collective-permute-start.21 = (bf16[2,2,64,256]{3,2,1,0:T(8,128)(2,1)S(1)}, bf16[2,2,64,256]{3,2,1,0:T(8,128)(2,1)S(1)}, u32[]{:S(2)}, u32[]{:S(2)}) collective-permute-start(bf16[2,2,64,256]{3,2,1,0:T(8,128)(2,1)S(1)} %get-tuple-element.80.refs_3_), channel_id=1, source_target_pairs={{0,16},{8,24},{16,0},{24,8},{1,17},{9,25},{17,1},{25,9},{2,18},{10... | collective-permute-start | bytes 393224 | tf_op jit(solution)/shard_map/ppermute | solution.py:324
  65.0 3.0 %collective-permute-start.22 = (bf16[2,2,64,256]{3,2,1,0:T(8,128)(2,1)S(1)}, bf16[2,2,64,256]{3,2,1,0:T(8,128)(2,1)S(1)}, u32[]{:S(2)}, u32[]{:S(2)}) collective-permute-start(bf16[2,2,64,256]{3,2,1,0:T(8,128)(2,1)S(1)} %get-tuple-element.81.refs_4_), channel_id=1, source_target_pairs={{0,24},{8,16},{16,8},{24,0},{1,25},{9,17},{17,9},{25,1},{2,26},{10... | collective-permute-start | bytes 393224 | tf_op jit(solution)/shard_map/ppermute | solution.py:324
  68.0 0.9 collective-permute-done.15.refs_6_
  68.9 2.5 %shard_map.78 = (bf16[8,2,64,256]{3,2,1,0:T(8,128)(2,1)S(1)}, bf16[2,8,64,256]{3,2,1,0:T(8,128)(2,1)S(1)}, bf16[2,2,64,256]{3,2,1,0:T(8,128)(2,1)S(1)}, bf16[2,2...) custom-call(s32[2]{0:T(128)S(1)} %copy-done.5, f32[8,8]{1,0:T(8,128)S(1)} %convert_element_type.3.fock, ...), custom_call_target="tpu_custom_call" | custom-call | flops 30000001024 | bytes 5242880 | tf_op jit(solution)/shard_map/pallas_call | solution.py:42
  71.4 0.8 copy-done.8
  72.2 7.9 %collective-permute-start.23 = (bf16[2,2,64,256]{3,2,1,0:T(8,128)(2,1)S(1)}, bf16[2,2,64,256]{3,2,1,0:T(8,128)(2,1)S(1)}, u32[]{:S(2)}, u32[]{:S(2)}) collective-permute-start(bf16[2,2,64,256]{3,2,1,0:T(8,128)(2,1)S(1)} %get-tuple-element.83), channel_id=1, source_target_pairs={{0,16},{8,24},{16,0},{24,8},{1,17},{9,25},{17,1},{25,9},{2,18},{10... | collective-permute-start | bytes 393224 | tf_op jit(solution)/shard_map/ppermute | solution.py:324
  80.2 1.6 %collective-permute-start.28 = (bf16[2,2,64,256]{3,2,1,0:T(8,128)(2,1)S(1)}, bf16[2,2,64,256]{3,2,1,0:T(8,128)(2,1)S(1)}, u32[]{:S(2)}, u32[]{:S(2)}) collective-permute-start(bf16[2,2,64,256]{3,2,1,0:T(8,128)(2,1)S(1)} %get-tuple-element.92), channel_id=1, source_target_pairs={{0,24},{8,16},{16,8},{24,0},{1,25},{9,17},{17,9},{25,1},{2,26},{10... | collective-permute-start | bytes 393224 | tf_op jit(solution)/shard_map/ppermute | solution.py:324
  81.8 3.6 %shard_map.80 = (bf16[8,2,128,256]{3,2,1,0:T(8,128)(2,1)}, bf16[2,8,64,256]{3,2,1,0:T(8,128)(2,1)S(1)}, bf16[2,2,64,256]{3,2,1,0:T(8,128)(2,1)S(1)}, bf16[2,2,64...) custom-call(s32[2]{0:T(128)S(1)} %copy-done.5, f32[8,8]{1,0:T(8,128)S(1)} %convert_element_type.3.fock, ...), custom_call_target="tpu_custom_call" | custom-call | flops 30000001024 | bytes 5242880 | tf_op jit(solution)/shard_map/pallas_call | solution.py:42
  85.4 4.2 %collective-permute-start.24 = (bf16[2,2,64,256]{3,2,1,0:T(8,128)(2,1)S(1)}, bf16[2,2,64,256]{3,2,1,0:T(8,128)(2,1)S(1)}, u32[]{:S(2)}, u32[]{:S(2)}) collective-permute-start(bf16[2,2,64,256]{3,2,1,0:T(8,128)(2,1)S(1)} %get-tuple-element.87), channel_id=1, source_target_pairs={{0,8},{8,0},{16,24},{24,16},{1,9},{9,1},{17,25},{25,17},{2,10},{10... | collective-permute-start | bytes 393224 | tf_op jit(solution)/shard_map/ppermute | solution.py:324
  89.5 0.7 collective-permute-start.25
  90.3 2.2 %collective-permute-done.23.refs_1_ = bf16[2,2,64,256]{3,2,1,0:T(8,128)(2,1)S(1)} collective-permute-done((bf16[2,2,64,256]{3,2,1,0:T(8,128)(2,1)S(1)}, bf16[2,2,64,256]{3,2,1,0:T(8,128)(2,1)S(1)}, u32[]{:S(2)}, u32[]{:S(2)}) %collective-permute-start.23) | collective-permute-done | bytes 131104 | tf_op jit(solution)/shard_map/ppermute | solution.py:324
  92.4 2.1 %collective-permute-start.26 = (bf16[2,2,64,256]{3,2,1,0:T(8,128)(2,1)S(1)}, bf16[2,2,64,256]{3,2,1,0:T(8,128)(2,1)S(1)}, u32[]{:S(2)}, u32[]{:S(2)}) collective-permute-start(bf16[2,2,64,256]{3,2,1,0:T(8,128)(2,1)S(1)} %get-tuple-element.89), channel_id=1, source_target_pairs={{0,24},{8,16},{16,8},{24,0},{1,25},{9,17},{17,9},{25,1},{2,26},{10... | collective-permute-start | bytes 393224 | tf_op jit(solution)/shard_map/ppermute | solution.py:324
  94.6 3.6 %all-to-all-start.1 = ((bf16[8,2,128,256]{3,2,1,0:T(8,128)(2,1)}), bf16[8,2,128,256]{3,2,1,0:T(8,128)(2,1)S(1)}, u32[]{:S(2)}, u32[]{:S(2)}) async-start(bf16[8,2,128,256]{3,2,1,0:T(8,128)(2,1)} %get-tuple-element.84), calls=%async_computation.1 | async-start | bytes 2097152 | tf_op jit(solution)/shard_map/all_to_all | solution.py:311
  98.2 1.0 copy-done.9
  99.2 1.1 shard_map.82.refs_3_
  100.3 0.3 collective-permute-done.25.refs_1_
  100.6 1.2 shard_map.83
  101.8 0.2 collective-permute-start.29
  101.9 2.9 %collective-permute-start.30 = (bf16[2,128,256]{2,1,0:T(8,128)(2,1)S(1)}, bf16[2,128,256]{2,1,0:T(8,128)(2,1)S(1)}, u32[]{:S(2)}, u32[]{:S(2)}) collective-permute-start(bf16[2,128,256]{2,1,0:T(8,128)(2,1)S(1)} %get-tuple-element.95), channel_id=1, source_target_pairs={{0,2},{1,3},{2,0},{3,1},{4,6},{5,7},{6,4},{7,5},{8,10},{9,11},{10,... | collective-permute-start | bytes 393224 | tf_op jit(solution)/shard_map/ppermute | solution.py:317
  104.9 1.8 %collective-permute-start.32 = (bf16[2,128,256]{2,1,0:T(8,128)(2,1)S(1)}, bf16[2,128,256]{2,1,0:T(8,128)(2,1)S(1)}, u32[]{:S(2)}, u32[]{:S(2)}) collective-permute-start(bf16[2,128,256]{2,1,0:T(8,128)(2,1)S(1)} %get-tuple-element.97), channel_id=1, source_target_pairs={{0,4},{1,5},{2,6},{3,7},{4,0},{5,1},{6,2},{7,3},{8,12},{9,13},{10,... | collective-permute-start | bytes 393224 | tf_op jit(solution)/shard_map/ppermute | solution.py:317
  106.7 2.9 %collective-permute-start.34 = (bf16[2,128,256]{2,1,0:T(8,128)(2,1)S(1)}, bf16[2,128,256]{2,1,0:T(8,128)(2,1)S(1)}, u32[]{:S(2)}, u32[]{:S(2)}) collective-permute-start(bf16[2,128,256]{2,1,0:T(8,128)(2,1)S(1)} %get-tuple-element.99), channel_id=1, source_target_pairs={{0,6},{1,7},{2,4},{3,5},{4,2},{5,3},{6,0},{7,1},{8,14},{9,15},{10,... | collective-permute-start | bytes 393224 | tf_op jit(solution)/shard_map/ppermute | solution.py:317
  109.6 6.2 %collective-permute-done.30.refs_2_ = bf16[2,128,256]{2,1,0:T(8,128)(2,1)S(1)} collective-permute-done((bf16[2,128,256]{2,1,0:T(8,128)(2,1)S(1)}, bf16[2,128,256]{2,1,0:T(8,128)(2,1)S(1)}, u32[]{:S(2)}, u32[]{:S(2)}) %collective-permute-start.30) | collective-permute-done | bytes 131104 | tf_op jit(solution)/shard_map/ppermute | solution.py:317
  115.9 0.2 collective-permute-start.35
  116.1 0.1 broadcast_in_dim.4.row
  116.3 1.4 %copy-done.7 = bf16[512,1536]{1,0:T(8,128)(2,1)S(1)} copy-done((bf16[512,1536]{1,0:T(8,128)(2,1)S(1)}, bf16[512,1536]{1,0:T(8,128)(2,1)}, u32[]{:S(2)}) %copy-start.7) | copy-done | bytes 1572888
  117.7 8.1 %shard_map.81.source = f32[2,512,512]{2,1,0:T(8,128)} custom-call(s32[2]{0:T(128)S(1)} %copy-done.5, f32[8]{0:T(128)S(1)} %copy-done.6, f32[2,512,512]{2,1,0:T(8,128)} %bitcast.14, bf16[8,2,128,256]{3,2,1,0:T(8,128)(2,1)S(1)} %all-to-all-done.1.blocks, f32[512,128]{1,0:T(8,128)S(1)} %broadcast_in_dim.4.row, f32[1,512]{1,0:T(1,128)S(1)} %bitcast.20, ...), custom_call_target="tpu_custom_call" | custom-call | flops 3221225472 | bytes 6291456 | tf_op jit(solution)/shard_map/pallas_call | solution.py:439
  125.9 2.8 %shard_map.84 = f32[2,512,512]{2,1,0:T(8,128)} custom-call(s32[2]{0:T(128)S(1)} %copy-done.5, f32[2,512,512]{2,1,0:T(8,128)} %shard_map.81.source, bf16[2,128,256]{2,1,0:T(8,128)(2,1)S(1)} %get-tuple-element.93.refs_0_, bf16[2,128,256]{2,1,0:T(8,128)(2,1)S(1)} %collective-permute-done.29.refs_1_, ...), custom_call_target="tpu_custom_call", output_to_operand_aliasing={{}: (1, {})} | custom-call | flops 524288 | bytes 5242880 | tf_op jit(solution)/shard_map/pallas_call | solution.py:465
  (64 shorter events, 0.5 us)
Async XLA Ops:
  0.0 10.2 %copy-start.13 = (s32[8]{0:T(128)S(1)}, s32[8]{0:T(128)}, u32[]{:S(2)}) copy-start(s32[8]{0:T(128)} %constant.25.clone) | copy-start | bytes 100
  0.0 11.4 %copy-start.12 = (s32[8]{0:T(128)S(1)}, s32[8]{0:T(128)}, u32[]{:S(2)}) copy-start(s32[8]{0:T(128)} %constant.24.clone) | copy-start | bytes 100
  0.0 16.0 %copy-start.2 = (f32[512]{0:T(512)S(1)}, f32[512]{0:T(512)}, u32[]{:S(2)}) copy-start(f32[512]{0:T(512)} %param.11) | copy-start | bytes 6148
  0.0 12.7 %collective-permute-start = (bf16[3,64,512]{2,1,0:T(8,128)(2,1)}, bf16[3,64,512]{2,1,0:T(8,128)(2,1)S(1)}, u32[]{:S(2)}, u32[]{:S(2)}) collective-permute-start(bf16[3,64,512]{2,1,0:T(8,128)(2,1)} %refs_0_.1), channel_id=1, source_target_pairs={{0,2},{1,3},{2,0},{3,1},{4,6},{5,7},{6,4},{7,5},{8,10},{9,11},{10,... | collective-permute-start | bytes 589832 | tf_op jit(solution)/shard_map/ppermute | solution.py:350
  3.0 12.8 %collective-permute-start.1 = (bf16[3,64,512]{2,1,0:T(8,128)(2,1)}, bf16[3,64,512]{2,1,0:T(8,128)(2,1)S(1)}, u32[]{:S(2)}, u32[]{:S(2)}) collective-permute-start(bf16[3,64,512]{2,1,0:T(8,128)(2,1)} %refs_0_.1), channel_id=1, source_target_pairs={{0,4},{1,5},{2,6},{3,7},{4,0},{5,1},{6,2},{7,3},{8,12},{9,13},{10,... | collective-permute-start | bytes 589832 | tf_op jit(solution)/shard_map/ppermute | solution.py:350
  4.5 11.2 %collective-permute-start.2 = (bf16[3,64,512]{2,1,0:T(8,128)(2,1)}, bf16[3,64,512]{2,1,0:T(8,128)(2,1)S(1)}, u32[]{:S(2)}, u32[]{:S(2)}) collective-permute-start(bf16[3,64,512]{2,1,0:T(8,128)(2,1)} %refs_0_.1), channel_id=1, source_target_pairs={{0,6},{1,7},{2,4},{3,5},{4,2},{5,3},{6,0},{7,1},{8,14},{9,15},{10,... | collective-permute-start | bytes 589832 | tf_op jit(solution)/shard_map/ppermute | solution.py:350
  4.6 23.7 %copy-start.4 = (s32[2]{0:T(128)}, s32[2]{0:T(128)S(1)}, u32[]{:S(2)}) copy-start(s32[2]{0:T(128)S(1)} %pad_add_fusion.place.source) | copy-start | bytes 28
  4.6 1.6 %copy-start = (f32[2,1,512,512]{3,2,1,0:T(8,128)S(1)}, f32[2,1,512,512]{3,2,1,0:T(8,128)}, u32[]{:S(2)}) copy-start(f32[2,1,512,512]{3,2,1,0:T(8,128)} %param.7) | copy-start | bytes 6291460
  6.2 9.6 %copy-start.1 = (bf16[3,64,512]{2,1,0:T(8,128)(2,1)S(1)}, bf16[3,64,512]{2,1,0:T(8,128)(2,1)}, u32[]{:S(2)}) copy-start(bf16[3,64,512]{2,1,0:T(8,128)(2,1)} %refs_0_.1) | copy-start | bytes 589828
  7.1 9.2 %collective-permute-start.10 = (bf16[2,128,256]{2,1,0:T(8,128)(2,1)S(1)}, bf16[2,128,256]{2,1,0:T(8,128)(2,1)S(1)}, u32[]{:S(2)}, u32[]{:S(2)}) collective-permute-start(bf16[2,128,256]{2,1,0:T(8,128)(2,1)S(1)} %get-tuple-element.63), channel_id=1, source_target_pairs={{0,7},{1,6},{2,5},{3,4},{4,3},{5,2},{6,1},{7,0},{8,15},{9,14},{10,... | collective-permute-start | bytes 393224 | tf_op jit(solution)/shard_map/ppermute | solution.py:317
  8.7 10.1 %collective-permute-start.4 = (bf16[2,128,256]{2,1,0:T(8,128)(2,1)S(1)}, bf16[2,128,256]{2,1,0:T(8,128)(2,1)S(1)}, u32[]{:S(2)}, u32[]{:S(2)}) collective-permute-start(bf16[2,128,256]{2,1,0:T(8,128)(2,1)S(1)} %get-tuple-element.57), channel_id=1, source_target_pairs={{0,1},{1,0},{2,3},{3,2},{4,5},{5,4},{6,7},{7,6},{8,9},{9,8},{10,11... | collective-permute-start | bytes 393224 | tf_op jit(solution)/shard_map/ppermute | solution.py:317
  12.7 15.4 %collective-permute-start.5 = (bf16[2,128,256]{2,1,0:T(8,128)(2,1)S(1)}, bf16[2,128,256]{2,1,0:T(8,128)(2,1)S(1)}, u32[]{:S(2)}, u32[]{:S(2)}) collective-permute-start(bf16[2,128,256]{2,1,0:T(8,128)(2,1)S(1)} %get-tuple-element.58), channel_id=1, source_target_pairs={{0,2},{1,3},{2,0},{3,1},{4,6},{5,7},{6,4},{7,5},{8,10},{9,11},{10,... | collective-permute-start | bytes 393224 | tf_op jit(solution)/shard_map/ppermute | solution.py:317
  15.8 12.3 %collective-permute-start.6 = (bf16[2,128,256]{2,1,0:T(8,128)(2,1)S(1)}, bf16[2,128,256]{2,1,0:T(8,128)(2,1)S(1)}, u32[]{:S(2)}, u32[]{:S(2)}) collective-permute-start(bf16[2,128,256]{2,1,0:T(8,128)(2,1)S(1)} %get-tuple-element.59), channel_id=1, source_target_pairs={{0,3},{1,2},{2,1},{3,0},{4,7},{5,6},{6,5},{7,4},{8,11},{9,10},{10,... | collective-permute-start | bytes 393224 | tf_op jit(solution)/shard_map/ppermute | solution.py:317
  15.9 3.0 %collective-permute-start.3 = (bf16[4,3,64,512]{3,2,1,0:T(8,128)(2,1)S(1)}, bf16[4,3,64,512]{3,2,1,0:T(8,128)(2,1)S(1)}, u32[]{:S(2)}, u32[]{:S(2)}) collective-permute-start(bf16[4,3,64,512]{3,2,1,0:T(8,128)(2,1)S(1)} %pad_maximum_fusion), channel_id=1, source_target_pairs={{0,1},{1,0},{2,3},{3,2},{4,5},{5,4},{6,7},{7,6},{8,9},{9,8},{10,11... | collective-permute-start | bytes 2359304 | tf_op jit(solution)/shard_map/ppermute | solution.py:350
  16.3 11.7 %collective-permute-start.7 = (bf16[2,128,256]{2,1,0:T(8,128)(2,1)S(1)}, bf16[2,128,256]{2,1,0:T(8,128)(2,1)S(1)}, u32[]{:S(2)}, u32[]{:S(2)}) collective-permute-start(bf16[2,128,256]{2,1,0:T(8,128)(2,1)S(1)} %get-tuple-element.60), channel_id=1, source_target_pairs={{0,4},{1,5},{2,6},{3,7},{4,0},{5,1},{6,2},{7,3},{8,12},{9,13},{10,... | collective-permute-start | bytes 393224 | tf_op jit(solution)/shard_map/ppermute | solution.py:317
  18.8 9.6 %collective-permute-start.8 = (bf16[2,128,256]{2,1,0:T(8,128)(2,1)S(1)}, bf16[2,128,256]{2,1,0:T(8,128)(2,1)S(1)}, u32[]{:S(2)}, u32[]{:S(2)}) collective-permute-start(bf16[2,128,256]{2,1,0:T(8,128)(2,1)S(1)} %get-tuple-element.61), channel_id=1, source_target_pairs={{0,5},{1,4},{2,7},{3,6},{4,1},{5,0},{6,3},{7,2},{8,13},{9,12},{10,... | collective-permute-start | bytes 393224 | tf_op jit(solution)/shard_map/ppermute | solution.py:317
  18.9 14.6 %copy-start.11 = (bf16[8,8]{1,0:T(8,128)(2,1)S(1)}, bf16[8,8]{1,0:T(8,128)(2,1)}, u32[]{:S(2)}) copy-start(bf16[8,8]{1,0:T(8,128)(2,1)} %param.9) | copy-start | bytes 388
  18.9 9.4 %collective-permute-start.9 = (bf16[2,128,256]{2,1,0:T(8,128)(2,1)S(1)}, bf16[2,128,256]{2,1,0:T(8,128)(2,1)S(1)}, u32[]{:S(2)}, u32[]{:S(2)}) collective-permute-start(bf16[2,128,256]{2,1,0:T(8,128)(2,1)S(1)} %get-tuple-element.62), channel_id=1, source_target_pairs={{0,6},{1,7},{2,4},{3,5},{4,2},{5,3},{6,0},{7,1},{8,14},{9,15},{10,... | collective-permute-start | bytes 393224 | tf_op jit(solution)/shard_map/ppermute | solution.py:317
  29.0 12.4 %collective-permute-start.11 = (bf16[2,2,64,256]{3,2,1,0:T(8,128)(2,1)S(1)}, bf16[2,2,64,256]{3,2,1,0:T(8,128)(2,1)S(1)}, u32[]{:S(2)}, u32[]{:S(2)}) collective-permute-start(bf16[2,2,64,256]{3,2,1,0:T(8,128)(2,1)S(1)} %get-tuple-element.65), channel_id=1, source_target_pairs={{0,8},{8,0},{16,24},{24,16},{1,9},{9,1},{17,25},{25,17},{2,10},{10... | collective-permute-start | bytes 393224 | tf_op jit(solution)/shard_map/ppermute | solution.py:324
  30.6 12.9 %collective-permute-start.12 = (bf16[2,2,64,256]{3,2,1,0:T(8,128)(2,1)S(1)}, bf16[2,2,64,256]{3,2,1,0:T(8,128)(2,1)S(1)}, u32[]{:S(2)}, u32[]{:S(2)}) collective-permute-start(bf16[2,2,64,256]{3,2,1,0:T(8,128)(2,1)S(1)} %get-tuple-element.66), channel_id=1, source_target_pairs={{0,16},{8,24},{16,0},{24,8},{1,17},{9,25},{17,1},{25,9},{2,18},{10... | collective-permute-start | bytes 393224 | tf_op jit(solution)/shard_map/ppermute | solution.py:324
  33.2 10.3 %collective-permute-start.13 = (bf16[2,2,64,256]{3,2,1,0:T(8,128)(2,1)S(1)}, bf16[2,2,64,256]{3,2,1,0:T(8,128)(2,1)S(1)}, u32[]{:S(2)}, u32[]{:S(2)}) collective-permute-start(bf16[2,2,64,256]{3,2,1,0:T(8,128)(2,1)S(1)} %get-tuple-element.67), channel_id=1, source_target_pairs={{0,24},{8,16},{16,8},{24,0},{1,25},{9,17},{17,9},{25,1},{2,26},{10... | collective-permute-start | bytes 393224 | tf_op jit(solution)/shard_map/ppermute | solution.py:324
  33.6 18.9 %all-to-all-start = ((bf16[8,2,128,256]{3,2,1,0:T(8,128)(2,1)}), bf16[8,2,128,256]{3,2,1,0:T(8,128)(2,1)S(1)}, u32[]{:S(2)}, u32[]{:S(2)}) async-start(bf16[8,2,128,256]{3,2,1,0:T(8,128)(2,1)} %get-tuple-element.55), calls=%async_computation | async-start | bytes 2097152 | tf_op jit(solution)/shard_map/all_to_all | solution.py:311
  37.2 21.7 %collective-permute-start.17 = (bf16[2,2,64,256]{3,2,1,0:T(8,128)(2,1)S(1)}, bf16[2,2,64,256]{3,2,1,0:T(8,128)(2,1)S(1)}, u32[]{:S(2)}, u32[]{:S(2)}) collective-permute-start(bf16[2,2,64,256]{3,2,1,0:T(8,128)(2,1)S(1)} %get-tuple-element.75), channel_id=1, source_target_pairs={{0,8},{8,0},{16,24},{24,16},{1,9},{9,1},{17,25},{25,17},{2,10},{10... | collective-permute-start | bytes 393224 | tf_op jit(solution)/shard_map/ppermute | solution.py:324
  37.9 21.2 %collective-permute-start.18 = (bf16[2,2,64,256]{3,2,1,0:T(8,128)(2,1)S(1)}, bf16[2,2,64,256]{3,2,1,0:T(8,128)(2,1)S(1)}, u32[]{:S(2)}, u32[]{:S(2)}) collective-permute-start(bf16[2,2,64,256]{3,2,1,0:T(8,128)(2,1)S(1)} %get-tuple-element.76), channel_id=1, source_target_pairs={{0,16},{8,24},{16,0},{24,8},{1,17},{9,25},{17,1},{25,9},{2,18},{10... | collective-permute-start | bytes 393224 | tf_op jit(solution)/shard_map/ppermute | solution.py:324
  41.4 17.7 %collective-permute-start.19 = (bf16[2,2,64,256]{3,2,1,0:T(8,128)(2,1)S(1)}, bf16[2,2,64,256]{3,2,1,0:T(8,128)(2,1)S(1)}, u32[]{:S(2)}, u32[]{:S(2)}) collective-permute-start(bf16[2,2,64,256]{3,2,1,0:T(8,128)(2,1)S(1)} %get-tuple-element.77), channel_id=1, source_target_pairs={{0,24},{8,16},{16,8},{24,0},{1,25},{9,17},{17,9},{25,1},{2,26},{10... | collective-permute-start | bytes 393224 | tf_op jit(solution)/shard_map/ppermute | solution.py:324
  44.8 14.3 %copy-start.5 = (s32[2]{0:T(128)S(1)}, s32[2]{0:T(128)}, u32[]{:S(2)}) copy-start(s32[2]{0:T(128)} %copy-done.4) | copy-start | bytes 28
  52.5 0.6 copy-start.10
  54.6 10.3 %collective-permute-start.14 = (bf16[2,2,64,256]{3,2,1,0:T(8,128)(2,1)S(1)}, bf16[2,2,64,256]{3,2,1,0:T(8,128)(2,1)S(1)}, u32[]{:S(2)}, u32[]{:S(2)}) collective-permute-start(bf16[2,2,64,256]{3,2,1,0:T(8,128)(2,1)S(1)} %get-tuple-element.70.refs_1_), channel_id=1, source_target_pairs={{0,8},{8,0},{16,24},{24,16},{1,9},{9,1},{17,25},{25,17},{2,10},{10... | collective-permute-start | bytes 393224 | tf_op jit(solution)/shard_map/ppermute | solution.py:324
  56.0 12.9 %collective-permute-start.15 = (bf16[2,2,64,256]{3,2,1,0:T(8,128)(2,1)S(1)}, bf16[2,2,64,256]{3,2,1,0:T(8,128)(2,1)S(1)}, u32[]{:S(2)}, u32[]{:S(2)}) collective-permute-start(bf16[2,2,64,256]{3,2,1,0:T(8,128)(2,1)S(1)} %get-tuple-element.71.refs_2_), channel_id=1, source_target_pairs={{0,16},{8,24},{16,0},{24,8},{1,17},{9,25},{17,1},{25,9},{2,18},{10... | collective-permute-start | bytes 393224 | tf_op jit(solution)/shard_map/ppermute | solution.py:324
  58.9 10.0 %collective-permute-start.16 = (bf16[2,2,64,256]{3,2,1,0:T(8,128)(2,1)S(1)}, bf16[2,2,64,256]{3,2,1,0:T(8,128)(2,1)S(1)}, u32[]{:S(2)}, u32[]{:S(2)}) collective-permute-start(bf16[2,2,64,256]{3,2,1,0:T(8,128)(2,1)S(1)} %get-tuple-element.72.refs_3_), channel_id=1, source_target_pairs={{0,24},{8,16},{16,8},{24,0},{1,25},{9,17},{17,9},{25,1},{2,26},{10... | collective-permute-start | bytes 393224 | tf_op jit(solution)/shard_map/ppermute | solution.py:324
  59.1 9.8 %copy-start.6 = (f32[8]{0:T(128)S(1)}, f32[8]{0:T(128)}, u32[]{:S(2)}) copy-start(f32[8]{0:T(128)} %occ.9) | copy-start | bytes 100
  60.7 19.4 %collective-permute-start.20 = (bf16[2,2,64,256]{3,2,1,0:T(8,128)(2,1)S(1)}, bf16[2,2,64,256]{3,2,1,0:T(8,128)(2,1)S(1)}, u32[]{:S(2)}, u32[]{:S(2)}) collective-permute-start(bf16[2,2,64,256]{3,2,1,0:T(8,128)(2,1)S(1)} %get-tuple-element.79.refs_2_), channel_id=1, source_target_pairs={{0,8},{8,0},{16,24},{24,16},{1,9},{9,1},{17,25},{25,17},{2,10},{10... | collective-permute-start | bytes 393224 | tf_op jit(solution)/shard_map/ppermute | solution.py:324
  61.2 20.6 %collective-permute-start.21 = (bf16[2,2,64,256]{3,2,1,0:T(8,128)(2,1)S(1)}, bf16[2,2,64,256]{3,2,1,0:T(8,128)(2,1)S(1)}, u32[]{:S(2)}, u32[]{:S(2)}) collective-permute-start(bf16[2,2,64,256]{3,2,1,0:T(8,128)(2,1)S(1)} %get-tuple-element.80.refs_3_), channel_id=1, source_target_pairs={{0,16},{8,24},{16,0},{24,8},{1,17},{9,25},{17,1},{25,9},{2,18},{10... | collective-permute-start | bytes 393224 | tf_op jit(solution)/shard_map/ppermute | solution.py:324
  65.0 16.8 %collective-permute-start.22 = (bf16[2,2,64,256]{3,2,1,0:T(8,128)(2,1)S(1)}, bf16[2,2,64,256]{3,2,1,0:T(8,128)(2,1)S(1)}, u32[]{:S(2)}, u32[]{:S(2)}) collective-permute-start(bf16[2,2,64,256]{3,2,1,0:T(8,128)(2,1)S(1)} %get-tuple-element.81.refs_4_), channel_id=1, source_target_pairs={{0,24},{8,16},{16,8},{24,0},{1,25},{9,17},{17,9},{25,1},{2,26},{10... | collective-permute-start | bytes 393224 | tf_op jit(solution)/shard_map/ppermute | solution.py:324
  71.4 0.8 copy-start.8
  72.2 20.2 %collective-permute-start.23 = (bf16[2,2,64,256]{3,2,1,0:T(8,128)(2,1)S(1)}, bf16[2,2,64,256]{3,2,1,0:T(8,128)(2,1)S(1)}, u32[]{:S(2)}, u32[]{:S(2)}) collective-permute-start(bf16[2,2,64,256]{3,2,1,0:T(8,128)(2,1)S(1)} %get-tuple-element.83), channel_id=1, source_target_pairs={{0,16},{8,24},{16,0},{24,8},{1,17},{9,25},{17,1},{25,9},{2,18},{10... | collective-permute-start | bytes 393224 | tf_op jit(solution)/shard_map/ppermute | solution.py:324
  80.2 18.0 %collective-permute-start.27 = (bf16[2,2,64,256]{3,2,1,0:T(8,128)(2,1)S(1)}, bf16[2,2,64,256]{3,2,1,0:T(8,128)(2,1)S(1)}, u32[]{:S(2)}, u32[]{:S(2)}) collective-permute-start(bf16[2,2,64,256]{3,2,1,0:T(8,128)(2,1)S(1)} %get-tuple-element.91), channel_id=1, source_target_pairs={{0,8},{8,0},{16,24},{24,16},{1,9},{9,1},{17,25},{25,17},{2,10},{10... | collective-permute-start | bytes 393224 | tf_op jit(solution)/shard_map/ppermute | solution.py:324
  80.2 18.0 %collective-permute-start.28 = (bf16[2,2,64,256]{3,2,1,0:T(8,128)(2,1)S(1)}, bf16[2,2,64,256]{3,2,1,0:T(8,128)(2,1)S(1)}, u32[]{:S(2)}, u32[]{:S(2)}) collective-permute-start(bf16[2,2,64,256]{3,2,1,0:T(8,128)(2,1)S(1)} %get-tuple-element.92), channel_id=1, source_target_pairs={{0,24},{8,16},{16,8},{24,0},{1,25},{9,17},{17,9},{25,1},{2,26},{10... | collective-permute-start | bytes 393224 | tf_op jit(solution)/shard_map/ppermute | solution.py:324
  85.4 14.9 %collective-permute-start.24 = (bf16[2,2,64,256]{3,2,1,0:T(8,128)(2,1)S(1)}, bf16[2,2,64,256]{3,2,1,0:T(8,128)(2,1)S(1)}, u32[]{:S(2)}, u32[]{:S(2)}) collective-permute-start(bf16[2,2,64,256]{3,2,1,0:T(8,128)(2,1)S(1)} %get-tuple-element.87), channel_id=1, source_target_pairs={{0,8},{8,0},{16,24},{24,16},{1,9},{9,1},{17,25},{25,17},{2,10},{10... | collective-permute-start | bytes 393224 | tf_op jit(solution)/shard_map/ppermute | solution.py:324
  89.5 11.1 %collective-permute-start.25 = (bf16[2,2,64,256]{3,2,1,0:T(8,128)(2,1)S(1)}, bf16[2,2,64,256]{3,2,1,0:T(8,128)(2,1)S(1)}, u32[]{:S(2)}, u32[]{:S(2)}) collective-permute-start(bf16[2,2,64,256]{3,2,1,0:T(8,128)(2,1)S(1)} %get-tuple-element.88), channel_id=1, source_target_pairs={{0,16},{8,24},{16,0},{24,8},{1,17},{9,25},{17,1},{25,9},{2,18},{10... | collective-permute-start | bytes 393224 | tf_op jit(solution)/shard_map/ppermute | solution.py:324
  92.4 8.1 %collective-permute-start.26 = (bf16[2,2,64,256]{3,2,1,0:T(8,128)(2,1)S(1)}, bf16[2,2,64,256]{3,2,1,0:T(8,128)(2,1)S(1)}, u32[]{:S(2)}, u32[]{:S(2)}) collective-permute-start(bf16[2,2,64,256]{3,2,1,0:T(8,128)(2,1)S(1)} %get-tuple-element.89), channel_id=1, source_target_pairs={{0,24},{8,16},{16,8},{24,0},{1,25},{9,17},{17,9},{25,1},{2,26},{10... | collective-permute-start | bytes 393224 | tf_op jit(solution)/shard_map/ppermute | solution.py:324
  94.6 21.5 %all-to-all-start.1 = ((bf16[8,2,128,256]{3,2,1,0:T(8,128)(2,1)}), bf16[8,2,128,256]{3,2,1,0:T(8,128)(2,1)S(1)}, u32[]{:S(2)}, u32[]{:S(2)}) async-start(bf16[8,2,128,256]{3,2,1,0:T(8,128)(2,1)} %get-tuple-element.84), calls=%async_computation.1 | async-start | bytes 2097152 | tf_op jit(solution)/shard_map/all_to_all | solution.py:311
  98.1 1.0 copy-start.9
  100.6 15.5 %copy-start.3 = (f32[512]{0:T(512)S(1)}, f32[512]{0:T(512)}, u32[]{:S(2)}) copy-start(f32[512]{0:T(512)} %param.11) | copy-start | bytes 6148
  101.8 4.9 %collective-permute-start.29 = (bf16[2,128,256]{2,1,0:T(8,128)(2,1)S(1)}, bf16[2,128,256]{2,1,0:T(8,128)(2,1)S(1)}, u32[]{:S(2)}, u32[]{:S(2)}) collective-permute-start(bf16[2,128,256]{2,1,0:T(8,128)(2,1)S(1)} %get-tuple-element.94), channel_id=1, source_target_pairs={{0,1},{1,0},{2,3},{3,2},{4,5},{5,4},{6,7},{7,6},{8,9},{9,8},{10,11... | collective-permute-start | bytes 393224 | tf_op jit(solution)/shard_map/ppermute | solution.py:317
  101.9 13.9 %collective-permute-start.30 = (bf16[2,128,256]{2,1,0:T(8,128)(2,1)S(1)}, bf16[2,128,256]{2,1,0:T(8,128)(2,1)S(1)}, u32[]{:S(2)}, u32[]{:S(2)}) collective-permute-start(bf16[2,128,256]{2,1,0:T(8,128)(2,1)S(1)} %get-tuple-element.95), channel_id=1, source_target_pairs={{0,2},{1,3},{2,0},{3,1},{4,6},{5,7},{6,4},{7,5},{8,10},{9,11},{10,... | collective-permute-start | bytes 393224 | tf_op jit(solution)/shard_map/ppermute | solution.py:317
  104.9 21.0 %collective-permute-start.31 = (bf16[2,128,256]{2,1,0:T(8,128)(2,1)S(1)}, bf16[2,128,256]{2,1,0:T(8,128)(2,1)S(1)}, u32[]{:S(2)}, u32[]{:S(2)}) collective-permute-start(bf16[2,128,256]{2,1,0:T(8,128)(2,1)S(1)} %get-tuple-element.96), channel_id=1, source_target_pairs={{0,3},{1,2},{2,1},{3,0},{4,7},{5,6},{6,5},{7,4},{8,11},{9,10},{10,... | collective-permute-start | bytes 393224 | tf_op jit(solution)/shard_map/ppermute | solution.py:317
  104.9 20.9 %collective-permute-start.32 = (bf16[2,128,256]{2,1,0:T(8,128)(2,1)S(1)}, bf16[2,128,256]{2,1,0:T(8,128)(2,1)S(1)}, u32[]{:S(2)}, u32[]{:S(2)}) collective-permute-start(bf16[2,128,256]{2,1,0:T(8,128)(2,1)S(1)} %get-tuple-element.97), channel_id=1, source_target_pairs={{0,4},{1,5},{2,6},{3,7},{4,0},{5,1},{6,2},{7,3},{8,12},{9,13},{10,... | collective-permute-start | bytes 393224 | tf_op jit(solution)/shard_map/ppermute | solution.py:317
  106.7 19.1 %collective-permute-start.33 = (bf16[2,128,256]{2,1,0:T(8,128)(2,1)S(1)}, bf16[2,128,256]{2,1,0:T(8,128)(2,1)S(1)}, u32[]{:S(2)}, u32[]{:S(2)}) collective-permute-start(bf16[2,128,256]{2,1,0:T(8,128)(2,1)S(1)} %get-tuple-element.98), channel_id=1, source_target_pairs={{0,5},{1,4},{2,7},{3,6},{4,1},{5,0},{6,3},{7,2},{8,13},{9,12},{10,... | collective-permute-start | bytes 393224 | tf_op jit(solution)/shard_map/ppermute | solution.py:317
  106.7 19.1 %collective-permute-start.34 = (bf16[2,128,256]{2,1,0:T(8,128)(2,1)S(1)}, bf16[2,128,256]{2,1,0:T(8,128)(2,1)S(1)}, u32[]{:S(2)}, u32[]{:S(2)}) collective-permute-start(bf16[2,128,256]{2,1,0:T(8,128)(2,1)S(1)} %get-tuple-element.99), channel_id=1, source_target_pairs={{0,6},{1,7},{2,4},{3,5},{4,2},{5,3},{6,0},{7,1},{8,14},{9,15},{10,... | collective-permute-start | bytes 393224 | tf_op jit(solution)/shard_map/ppermute | solution.py:317
  115.9 10.0 %collective-permute-start.35 = (bf16[2,128,256]{2,1,0:T(8,128)(2,1)S(1)}, bf16[2,128,256]{2,1,0:T(8,128)(2,1)S(1)}, u32[]{:S(2)}, u32[]{:S(2)}) collective-permute-start(bf16[2,128,256]{2,1,0:T(8,128)(2,1)S(1)} %get-tuple-element.100), channel_id=1, source_target_pairs={{0,7},{1,6},{2,5},{3,4},{4,3},{5,2},{6,1},{7,0},{8,15},{9,14},{10,... | collective-permute-start | bytes 393224 | tf_op jit(solution)/shard_map/ppermute | solution.py:317
  116.2 1.4 %copy-start.7 = (bf16[512,1536]{1,0:T(8,128)(2,1)S(1)}, bf16[512,1536]{1,0:T(8,128)(2,1)}, u32[]{:S(2)}) copy-start(bf16[512,1536]{1,0:T(8,128)(2,1)} %get-tuple-element.85.vectors) | copy-start | bytes 4718596

commit v16 on v14

--- a/solution.py
+++ b/solution.py
@@ -11,6 +11,7 @@
 VMEM = pl.BlockSpec(memory_space=pltpu.VMEM)
 SMEM = pl.BlockSpec(memory_space=pltpu.SMEM)
 PARAMS = pltpu.CompilerParams(vmem_limit_bytes=50 * 2**20)
+SMALL = pltpu.CompilerParams(vmem_limit_bytes=20 * 2**20)
 WIDE = jnp.float32
 LONG = 3 * 10**10
 NARROW = jnp.bfloat16
@@ -38,14 +39,14 @@
         return jnp.concatenate([x[:, self.edge:], x[:, :self.edge]], axis=1)
 
 
-def call(body, outs, scratch, flops, moved, *operands, specs):
+def call(body, outs, scratch, flops, moved, *operands, specs, params=PARAMS):
     return pl.pallas_call(
         body,
         out_shape=outs,
         in_specs=specs,
         out_specs=jax.tree.map(lambda _: VMEM, outs),
         scratch_shapes=scratch,
-        compiler_params=PARAMS,
+        compiler_params=params,
         cost_estimate=pl.CostEstimate(flops=flops, bytes_accessed=moved, transcendentals=0),
     )(*operands)
 
@@ -413,7 +414,7 @@
             [(upper, packed)[c], jax.ShapeDtypeStruct((first, devices, *part.shape[2:]), NARROW)] + [part] * (groups - 1),
             [pltpu.VMEM((first, devices, *part.shape[2:]), WIDE), pltpu.VMEM(part.shape, WIDE)],
             LONG, 10 * count, place, fock, occ_energy, sums, *sent, *half[c], *other[c],
-            specs=[SMEM] * 3 + [VMEM] * (2 * groups + 1 + c),
+            specs=[SMEM] * 3 + [VMEM] * (2 * groups + 1 + c), params=SMALL,
         )
         sent, rest, mixed = [sent_one], rest + [rest_one], mixed + [mixed_one]
     other = [across_first([None] + x, groups)[1:] for x in mixed]
@@ -445,7 +446,7 @@
             functools.partial(rest_kernel, tiles, groups, first, c),
             [distant] * devices if c else [upper], [blocks] if c else [],
             LONG, 8 * count, place, occ_energy, sums, rest[c], *other[c], *last,
-            specs=[SMEM] * 2 + [VMEM] * (groups + 1 + c),
+            specs=[SMEM] * 2 + [VMEM] * (groups + 1 + c), params=SMALL,
         )
     done = pl.pallas_call(
         functools.partial(add_kernel, tiles),

time: 127 us -> 127 us (level)
  no operation moved by 1% of the time
where the time goes in v16:
time: 127 us; the launch traced here: 126 us
  starting transfers between devices  66.5 us (52%)
  Pallas kernels  31.1 us (24%)
  waiting for transfers between devices  19.2 us (15%)
  local copies, waits for them, and re-layouts  6.95 us (5%)
  between operations  1.64 us (1%)
    ppermute x18, starting transfers between devices, across_first(): lax.ppermute(parts[s], 'occi', [(k, k ^ s) for k in range(groups)])  35.3 us
    pallas_call x9, Pallas kernels, call(): pl.pallas_call(body, out_shape=outs, in_specs=specs, out_specs=jax.tree.m...  19.3 us
    ppermute x14, starting transfers between devices, by_distance(): lax.ppermute(parts[k], 'occj', [(d, d ^ k) for d in range(devices)])  16.4 us
    all_to_all x2, starting transfers between devices, exchange(): lax.all_to_all(blocks, 'occj', split_axis=0, concat_axis=0, tiled=True)  10.2 us
    pallas_call x1, Pallas kernels, local(): pl.pallas_call(functools.partial(second_ladder_kernel, tiles, first), gri...  7.79 us
    all_to_all x2, waiting for transfers between devices, exchange(): lax.all_to_all(blocks, 'occj', split_axis=0, concat_axis=0, tiled=True)  7.72 us
    ppermute x18, waiting for transfers between devices, across_first(): lax.ppermute(parts[s], 'occi', [(k, k ^ s) for k in range(groups)])  6.86 us
    unnamed x28, local copies, waits for them, and re-layouts  5.43 us
  transfers between devices with their start and end apart: 38, of which 7 were waited for; matrix products, arithmetic and copies ran while one was open for 2% of the time, Pallas kernels for 22%

profile of v16, /device:TPU:0, one launch (start us, length us, event | category | flops | bytes accessed | tf_op | source)
XLA Modules:
  0.0 125.7 jit_solution(5625225232002200762)
XLA Ops:
  0.0 3.0 %collective-permute-start = (bf16[3,64,512]{2,1,0:T(8,128)(2,1)}, bf16[3,64,512]{2,1,0:T(8,128)(2,1)S(1)}, u32[]{:S(2)}, u32[]{:S(2)}) collective-permute-start(bf16[3,64,512]{2,1,0:T(8,128)(2,1)} %refs_0_.1), channel_id=1, source_target_pairs={{0,2},{1,3},{2,0},{3,1},{4,6},{5,7},{6,4},{7,5},{8,10},{9,11},{10,... | collective-permute-start | bytes 589832 | tf_op jit(solution)/shard_map/ppermute | solution.py:339
  3.0 1.5 %collective-permute-start.1 = (bf16[3,64,512]{2,1,0:T(8,128)(2,1)}, bf16[3,64,512]{2,1,0:T(8,128)(2,1)S(1)}, u32[]{:S(2)}, u32[]{:S(2)}) collective-permute-start(bf16[3,64,512]{2,1,0:T(8,128)(2,1)} %refs_0_.1), channel_id=1, source_target_pairs={{0,4},{1,5},{2,6},{3,7},{4,0},{5,1},{6,2},{7,3},{8,12},{9,13},{10,... | collective-permute-start | bytes 589832 | tf_op jit(solution)/shard_map/ppermute | solution.py:339
  4.6 1.6 %copy-done = f32[2,1,512,512]{3,2,1,0:T(8,128)S(1)} copy-done((f32[2,1,512,512]{3,2,1,0:T(8,128)S(1)}, f32[2,1,512,512]{3,2,1,0:T(8,128)}, u32[]{:S(2)}) %copy-start) | copy-done | bytes 2097176
  6.2 0.9 shard_map.73
  7.1 1.6 %collective-permute-start.10 = (bf16[2,128,256]{2,1,0:T(8,128)(2,1)S(1)}, bf16[2,128,256]{2,1,0:T(8,128)(2,1)S(1)}, u32[]{:S(2)}, u32[]{:S(2)}) collective-permute-start(bf16[2,128,256]{2,1,0:T(8,128)(2,1)S(1)} %get-tuple-element.62), channel_id=1, source_target_pairs={{0,7},{1,6},{2,5},{3,4},{4,3},{5,2},{6,1},{7,0},{8,15},{9,14},{10,... | collective-permute-start | bytes 393224 | tf_op jit(solution)/shard_map/ppermute | solution.py:306
  8.7 1.5 %collective-permute-start.4 = (bf16[2,128,256]{2,1,0:T(8,128)(2,1)S(1)}, bf16[2,128,256]{2,1,0:T(8,128)(2,1)S(1)}, u32[]{:S(2)}, u32[]{:S(2)}) collective-permute-start(bf16[2,128,256]{2,1,0:T(8,128)(2,1)S(1)} %get-tuple-element.56), channel_id=1, source_target_pairs={{0,1},{1,0},{2,3},{3,2},{4,5},{5,4},{6,7},{7,6},{8,9},{9,8},{10,11... | collective-permute-start | bytes 393224 | tf_op jit(solution)/shard_map/ppermute | solution.py:306
  10.2 0.6 dynamic_slice.14
  11.4 0.6 dynamic_slice.12
  12.7 0.6 collective-permute-start.5
  13.3 2.5 %collective-permute-done.1.refs_2_ = bf16[3,64,512]{2,1,0:T(8,128)(2,1)S(1)} collective-permute-done((bf16[3,64,512]{2,1,0:T(8,128)(2,1)}, bf16[3,64,512]{2,1,0:T(8,128)(2,1)S(1)}, u32[]{:S(2)}, u32[]{:S(2)}) %collective-permute-start.1) | collective-permute-done | bytes 196640 | tf_op jit(solution)/shard_map/ppermute | solution.py:339
  15.8 0.1 pad_maximum_fusion
  16.0 0.1 fusion
  16.2 0.1 broadcast_add_fusion.2
  16.3 2.4 %collective-permute-start.7 = (bf16[2,128,256]{2,1,0:T(8,128)(2,1)S(1)}, bf16[2,128,256]{2,1,0:T(8,128)(2,1)S(1)}, u32[]{:S(2)}, u32[]{:S(2)}) collective-permute-start(bf16[2,128,256]{2,1,0:T(8,128)(2,1)S(1)} %get-tuple-element.59), channel_id=1, source_target_pairs={{0,4},{1,5},{2,6},{3,7},{4,0},{5,1},{6,2},{7,3},{8,12},{9,13},{10,... | collective-permute-start | bytes 393224 | tf_op jit(solution)/shard_map/ppermute | solution.py:306
  18.8 0.2 collective-permute-start.8
  18.9 2.9 %collective-permute-start.9 = (bf16[2,128,256]{2,1,0:T(8,128)(2,1)S(1)}, bf16[2,128,256]{2,1,0:T(8,128)(2,1)S(1)}, u32[]{:S(2)}, u32[]{:S(2)}) collective-permute-start(bf16[2,128,256]{2,1,0:T(8,128)(2,1)S(1)} %get-tuple-element.61), channel_id=1, source_target_pairs={{0,6},{1,7},{2,4},{3,5},{4,2},{5,3},{6,0},{7,1},{8,14},{9,15},{10,... | collective-permute-start | bytes 393224 | tf_op jit(solution)/shard_map/ppermute | solution.py:306
  21.8 6.3 %shard_map.74 = (bf16[8,2,128,256]{3,2,1,0:T(8,128)(2,1)}, bf16[512,1536]{1,0:T(8,128)(2,1)}) custom-call(s32[2]{0:T(128)S(1)} %pad_add_fusion.place.source, f32[2,512,512]{2,1,0:T(8,128)} %bitcast.13, bf16[3,64,512]{2,1,0:T(8,128)(2,1)S(1)} %copy-done.1, bf16[3,64,512]{2,1,0:T(8,128)(2,1)S(1)} %collective-permute-done.refs_1_, ...), custom_call_target="tpu_custom_call" | custom-call | flops 3221225472 | bytes 4194304 | tf_op jit(solution)/shard_map/pallas_call | solution.py:43
  28.1 0.2 collective-permute-done.8.refs_5_
  28.3 0.7 shard_map.75
  29.0 1.6 %collective-permute-start.11 = (bf16[2,2,64,256]{3,2,1,0:T(8,128)(2,1)S(1)}, bf16[2,2,64,256]{3,2,1,0:T(8,128)(2,1)S(1)}, u32[]{:S(2)}, u32[]{:S(2)}) collective-permute-start(bf16[2,2,64,256]{3,2,1,0:T(8,128)(2,1)S(1)} %get-tuple-element.64), channel_id=1, source_target_pairs={{0,8},{8,0},{16,24},{24,16},{1,9},{9,1},{17,25},{25,17},{2,10},{10... | collective-permute-start | bytes 393224 | tf_op jit(solution)/shard_map/ppermute | solution.py:313
  30.6 2.6 %collective-permute-start.12 = (bf16[2,2,64,256]{3,2,1,0:T(8,128)(2,1)S(1)}, bf16[2,2,64,256]{3,2,1,0:T(8,128)(2,1)S(1)}, u32[]{:S(2)}, u32[]{:S(2)}) collective-permute-start(bf16[2,2,64,256]{3,2,1,0:T(8,128)(2,1)S(1)} %get-tuple-element.65), channel_id=1, source_target_pairs={{0,16},{8,24},{16,0},{24,8},{1,17},{9,25},{17,1},{25,9},{2,18},{10... | collective-permute-start | bytes 393224 | tf_op jit(solution)/shard_map/ppermute | solution.py:313
  33.2 0.2 collective-permute-start.13
  33.5 0.1 broadcast_add_fusion
  33.6 3.6 %all-to-all-start = ((bf16[8,2,128,256]{3,2,1,0:T(8,128)(2,1)}), bf16[8,2,128,256]{3,2,1,0:T(8,128)(2,1)S(1)}, u32[]{:S(2)}, u32[]{:S(2)}) async-start(bf16[8,2,128,256]{3,2,1,0:T(8,128)(2,1)} %get-tuple-element.54), calls=%async_computation | async-start | bytes 2097152 | tf_op jit(solution)/shard_map/all_to_all | solution.py:300
  37.2 0.7 collective-permute-start.17
  37.9 3.5 %collective-permute-start.18 = (bf16[2,2,64,256]{3,2,1,0:T(8,128)(2,1)S(1)}, bf16[2,2,64,256]{3,2,1,0:T(8,128)(2,1)S(1)}, u32[]{:S(2)}, u32[]{:S(2)}) collective-permute-start(bf16[2,2,64,256]{3,2,1,0:T(8,128)(2,1)S(1)} %get-tuple-element.75), channel_id=1, source_target_pairs={{0,16},{8,24},{16,0},{24,8},{1,17},{9,25},{17,1},{25,9},{2,18},{10... | collective-permute-start | bytes 393224 | tf_op jit(solution)/shard_map/ppermute | solution.py:313
  41.4 0.2 collective-permute-start.19
  41.6 2.0 %collective-permute-done.12.refs_2_ = bf16[2,2,64,256]{3,2,1,0:T(8,128)(2,1)S(1)} collective-permute-done((bf16[2,2,64,256]{3,2,1,0:T(8,128)(2,1)S(1)}, bf16[2,2,64,256]{3,2,1,0:T(8,128)(2,1)S(1)}, u32[]{:S(2)}, u32[]{:S(2)}) %collective-permute-start.12) | collective-permute-done | bytes 131104 | tf_op jit(solution)/shard_map/ppermute | solution.py:313
  43.6 1.2 shard_map.76.place
  44.8 7.7 %all-to-all-done.ladder = bf16[8,2,128,256]{3,2,1,0:T(8,128)(2,1)S(1)} async-done(((bf16[8,2,128,256]{3,2,1,0:T(8,128)(2,1)}), bf16[8,2,128,256]{3,2,1,0:T(8,128)(2,1)S(1)}, u32[]{:S(2)}, u32[]{:S(2)}) %all-to-all-start) | async-done | bytes 1048608 | tf_op jit(solution)/shard_map/all_to_all | solution.py:300
  52.5 0.6 copy-done.10
  53.1 1.6 %shard_map.77 = (bf16[2,2,64,256]{3,2,1,0:T(8,128)(2,1)S(1)}, bf16[2,2,64,256]{3,2,1,0:T(8,128)(2,1)S(1)}, bf16[2,2,64,256]{3,2,1,0:T(8,128)(2,1)S(1)}, bf16[2,2,64,256]{3,2,1,0:T(8,128)(2,1)S(1)}) custom-call(s32[2]{0:T(128)S(1)} %copy-done.10, f32[8,8]{1,0:T(8,128)S(1)} %convert_element_type.3.fock, bf16[8,2,128,256]{3,2,1,0:T(8,128)(2,1)S(1)} %all-to-all-done.ladder, ...), custom_call_target="tpu_custom_call" | custom-call | flops 30000001024 | bytes 3145728 | tf_op jit(solution)/shard_map/pallas_call | solution.py:43
  54.6 1.3 %collective-permute-start.14 = (bf16[2,2,64,256]{3,2,1,0:T(8,128)(2,1)S(1)}, bf16[2,2,64,256]{3,2,1,0:T(8,128)(2,1)S(1)}, u32[]{:S(2)}, u32[]{:S(2)}) collective-permute-start(bf16[2,2,64,256]{3,2,1,0:T(8,128)(2,1)S(1)} %get-tuple-element.69.refs_1_), channel_id=1, source_target_pairs={{0,8},{8,0},{16,24},{24,16},{1,9},{9,1},{17,25},{25,17},{2,10},{10... | collective-permute-start | bytes 393224 | tf_op jit(solution)/shard_map/ppermute | solution.py:313
  56.0 2.9 %collective-permute-start.15 = (bf16[2,2,64,256]{3,2,1,0:T(8,128)(2,1)S(1)}, bf16[2,2,64,256]{3,2,1,0:T(8,128)(2,1)S(1)}, u32[]{:S(2)}, u32[]{:S(2)}) collective-permute-start(bf16[2,2,64,256]{3,2,1,0:T(8,128)(2,1)S(1)} %get-tuple-element.70.refs_2_), channel_id=1, source_target_pairs={{0,16},{8,24},{16,0},{24,8},{1,17},{9,25},{17,1},{25,9},{2,18},{10... | collective-permute-start | bytes 393224 | tf_op jit(solution)/shard_map/ppermute | solution.py:313
  58.9 0.2 collective-permute-start.16
  59.1 1.6 %shard_map.79 = (bf16[2,2,64,256]{3,2,1,0:T(8,128)(2,1)S(1)}, bf16[2,2,64,256]{3,2,1,0:T(8,128)(2,1)S(1)}, bf16[2,2,64,256]{3,2,1,0:T(8,128)(2,1)S(1)}, bf16[2,2,64,256]{3,2,1,0:T(8,128)(2,1)S(1)}) custom-call(s32[2]{0:T(128)S(1)} %copy-done.5, f32[8,8]{1,0:T(8,128)S(1)} %convert_element_type.3.fock, bf16[8,2,128,256]{3,2,1,0:T(8,128)(2,1)S(1)} %all-to-all-done.ladder, ...), custom_call_target="tpu_custom_call" | custom-call | flops 30000001024 | bytes 3145728 | tf_op jit(solution)/shard_map/pallas_call | solution.py:43
  60.7 0.4 collective-permute-start.20
  61.2 3.8 %collective-permute-start.21 = (bf16[2,2,64,256]{3,2,1,0:T(8,128)(2,1)S(1)}, bf16[2,2,64,256]{3,2,1,0:T(8,128)(2,1)S(1)}, u32[]{:S(2)}, u32[]{:S(2)}) collective-permute-start(bf16[2,2,64,256]{3,2,1,0:T(8,128)(2,1)S(1)} %get-tuple-element.79.refs_3_), channel_id=1, source_target_pairs={{0,16},{8,24},{16,0},{24,8},{1,17},{9,25},{17,1},{25,9},{2,18},{10... | collective-permute-start | bytes 393224 | tf_op jit(solution)/shard_map/ppermute | solution.py:313
  65.0 3.0 %collective-permute-start.22 = (bf16[2,2,64,256]{3,2,1,0:T(8,128)(2,1)S(1)}, bf16[2,2,64,256]{3,2,1,0:T(8,128)(2,1)S(1)}, u32[]{:S(2)}, u32[]{:S(2)}) collective-permute-start(bf16[2,2,64,256]{3,2,1,0:T(8,128)(2,1)S(1)} %get-tuple-element.80.refs_4_), channel_id=1, source_target_pairs={{0,24},{8,16},{16,8},{24,0},{1,25},{9,17},{17,9},{25,1},{2,26},{10... | collective-permute-start | bytes 393224 | tf_op jit(solution)/shard_map/ppermute | solution.py:313
  68.0 0.9 collective-permute-done.15.refs_6_
  68.9 2.5 %shard_map.78 = (bf16[8,2,64,256]{3,2,1,0:T(8,128)(2,1)S(1)}, bf16[2,8,64,256]{3,2,1,0:T(8,128)(2,1)S(1)}, bf16[2,2,64,256]{3,2,1,0:T(8,128)(2,1)S(1)}, bf16[2,2...) custom-call(s32[2]{0:T(128)S(1)} %copy-done.5, f32[8,8]{1,0:T(8,128)S(1)} %convert_element_type.3.fock, ...), custom_call_target="tpu_custom_call" | custom-call | flops 30000001024 | bytes 5242880 | tf_op jit(solution)/shard_map/pallas_call | solution.py:43
  71.4 0.8 copy-done.8
  72.2 7.2 %collective-permute-start.26 = (bf16[2,2,64,256]{3,2,1,0:T(8,128)(2,1)S(1)}, bf16[2,2,64,256]{3,2,1,0:T(8,128)(2,1)S(1)}, u32[]{:S(2)}, u32[]{:S(2)}) collective-permute-start(bf16[2,2,64,256]{3,2,1,0:T(8,128)(2,1)S(1)} %get-tuple-element.88), channel_id=1, source_target_pairs={{0,8},{8,0},{16,24},{24,16},{1,9},{9,1},{17,25},{25,17},{2,10},{10... | collective-permute-start | bytes 393224 | tf_op jit(solution)/shard_map/ppermute | solution.py:313
  79.4 0.8 collective-permute-start.27
  80.2 1.6 %collective-permute-start.28 = (bf16[2,2,64,256]{3,2,1,0:T(8,128)(2,1)S(1)}, bf16[2,2,64,256]{3,2,1,0:T(8,128)(2,1)S(1)}, u32[]{:S(2)}, u32[]{:S(2)}) collective-permute-start(bf16[2,2,64,256]{3,2,1,0:T(8,128)(2,1)S(1)} %get-tuple-element.90), channel_id=1, source_target_pairs={{0,24},{8,16},{16,8},{24,0},{1,25},{9,17},{17,9},{25,1},{2,26},{10... | collective-permute-start | bytes 393224 | tf_op jit(solution)/shard_map/ppermute | solution.py:313
  81.8 3.6 %shard_map.80 = (bf16[8,2,128,256]{3,2,1,0:T(8,128)(2,1)}, bf16[2,8,64,256]{3,2,1,0:T(8,128)(2,1)S(1)}, bf16[2,2,64,256]{3,2,1,0:T(8,128)(2,1)S(1)}, bf16[2,2,64...) custom-call(s32[2]{0:T(128)S(1)} %copy-done.5, f32[8,8]{1,0:T(8,128)S(1)} %convert_element_type.3.fock, ...), custom_call_target="tpu_custom_call" | custom-call | flops 30000001024 | bytes 5242880 | tf_op jit(solution)/shard_map/pallas_call | solution.py:43
  85.4 2.7 %collective-permute-start.23 = (bf16[2,2,64,256]{3,2,1,0:T(8,128)(2,1)S(1)}, bf16[2,2,64,256]{3,2,1,0:T(8,128)(2,1)S(1)}, u32[]{:S(2)}, u32[]{:S(2)}) collective-permute-start(bf16[2,2,64,256]{3,2,1,0:T(8,128)(2,1)S(1)} %get-tuple-element.84), channel_id=1, source_target_pairs={{0,8},{8,0},{16,24},{24,16},{1,9},{9,1},{17,25},{25,17},{2,10},{10... | collective-permute-start | bytes 393224 | tf_op jit(solution)/shard_map/ppermute | solution.py:313
  88.1 0.8 collective-permute-start.24
  88.9 6.6 %all-to-all-start.1 = ((bf16[8,2,128,256]{3,2,1,0:T(8,128)(2,1)}), bf16[8,2,128,256]{3,2,1,0:T(8,128)(2,1)S(1)}, u32[]{:S(2)}, u32[]{:S(2)}) async-start(bf16[8,2,128,256]{3,2,1,0:T(8,128)(2,1)} %get-tuple-element.81), calls=%async_computation.1 | async-start | bytes 2097152 | tf_op jit(solution)/shard_map/all_to_all | solution.py:300
  95.5 1.7 %collective-permute-start.25 = (bf16[2,2,64,256]{3,2,1,0:T(8,128)(2,1)S(1)}, bf16[2,2,64,256]{3,2,1,0:T(8,128)(2,1)S(1)}, u32[]{:S(2)}, u32[]{:S(2)}) collective-permute-start(bf16[2,2,64,256]{3,2,1,0:T(8,128)(2,1)S(1)} %get-tuple-element.86), channel_id=1, source_target_pairs={{0,24},{8,16},{16,8},{24,0},{1,25},{9,17},{17,9},{25,1},{2,26},{10... | collective-permute-start | bytes 393224 | tf_op jit(solution)/shard_map/ppermute | solution.py:313
  97.2 1.0 copy-done.9
  98.2 1.1 shard_map.82.refs_3_
  99.3 4.0 %collective-permute-done.25.refs_2_ = bf16[2,2,64,256]{3,2,1,0:T(8,128)(2,1)S(1)} collective-permute-done((bf16[2,2,64,256]{3,2,1,0:T(8,128)(2,1)S(1)}, bf16[2,2,64,256]{3,2,1,0:T(8,128)(2,1)S(1)}, u32[]{:S(2)}, u32[]{:S(2)}) %collective-permute-start.25) | collective-permute-done | bytes 131104 | tf_op jit(solution)/shard_map/ppermute | solution.py:313
  103.3 1.2 shard_map.83
  104.5 1.7 %collective-permute-start.30 = (bf16[2,128,256]{2,1,0:T(8,128)(2,1)S(1)}, bf16[2,128,256]{2,1,0:T(8,128)(2,1)S(1)}, u32[]{:S(2)}, u32[]{:S(2)}) collective-permute-start(bf16[2,128,256]{2,1,0:T(8,128)(2,1)S(1)} %get-tuple-element.93), channel_id=1, source_target_pairs={{0,2},{1,3},{2,0},{3,1},{4,6},{5,7},{6,4},{7,5},{8,10},{9,11},{10,... | collective-permute-start | bytes 393224 | tf_op jit(solution)/shard_map/ppermute | solution.py:306
  106.3 0.1 collective-permute-start.31
  106.4 2.2 %collective-permute-start.32 = (bf16[2,128,256]{2,1,0:T(8,128)(2,1)S(1)}, bf16[2,128,256]{2,1,0:T(8,128)(2,1)S(1)}, u32[]{:S(2)}, u32[]{:S(2)}) collective-permute-start(bf16[2,128,256]{2,1,0:T(8,128)(2,1)S(1)} %get-tuple-element.95), channel_id=1, source_target_pairs={{0,4},{1,5},{2,6},{3,7},{4,0},{5,1},{6,2},{7,3},{8,12},{9,13},{10,... | collective-permute-start | bytes 393224 | tf_op jit(solution)/shard_map/ppermute | solution.py:306
  108.6 2.9 %collective-permute-start.34 = (bf16[2,128,256]{2,1,0:T(8,128)(2,1)S(1)}, bf16[2,128,256]{2,1,0:T(8,128)(2,1)S(1)}, u32[]{:S(2)}, u32[]{:S(2)}) collective-permute-start(bf16[2,128,256]{2,1,0:T(8,128)(2,1)S(1)} %get-tuple-element.97), channel_id=1, source_target_pairs={{0,6},{1,7},{2,4},{3,5},{4,2},{5,3},{6,0},{7,1},{8,14},{9,15},{10,... | collective-permute-start | bytes 393224 | tf_op jit(solution)/shard_map/ppermute | solution.py:306
  111.5 1.8 %collective-permute-done.30.refs_2_ = bf16[2,128,256]{2,1,0:T(8,128)(2,1)S(1)} collective-permute-done((bf16[2,128,256]{2,1,0:T(8,128)(2,1)S(1)}, bf16[2,128,256]{2,1,0:T(8,128)(2,1)S(1)}, u32[]{:S(2)}, u32[]{:S(2)}) %collective-permute-start.30) | collective-permute-done | bytes 131104 | tf_op jit(solution)/shard_map/ppermute | solution.py:306
  113.3 0.2 collective-permute-start.35
  113.5 0.1 broadcast_in_dim.4.row
  113.7 1.4 %copy-done.7 = bf16[512,1536]{1,0:T(8,128)(2,1)S(1)} copy-done((bf16[512,1536]{1,0:T(8,128)(2,1)S(1)}, bf16[512,1536]{1,0:T(8,128)(2,1)}, u32[]{:S(2)}) %copy-start.7) | copy-done | bytes 1572888
  115.1 7.8 %shard_map.81.source = f32[2,512,512]{2,1,0:T(8,128)} custom-call(s32[2]{0:T(128)S(1)} %copy-done.5, f32[8]{0:T(128)S(1)} %copy-done.6, f32[2,512,512]{2,1,0:T(8,128)} %bitcast.14, bf16[8,2,128,256]{3,2,1,0:T(8,128)(2,1)S(1)} %all-to-all-done.1.blocks, f32[512,128]{1,0:T(8,128)S(1)} %broadcast_in_dim.4.row, f32[1,512]{1,0:T(1,128)S(1)} %bitcast.20, ...), custom_call_target="tpu_custom_call" | custom-call | flops 3221225472 | bytes 6291456 | tf_op jit(solution)/shard_map/pallas_call | solution.py:428
  122.9 2.8 %shard_map.84 = f32[2,512,512]{2,1,0:T(8,128)} custom-call(s32[2]{0:T(128)S(1)} %copy-done.5, f32[2,512,512]{2,1,0:T(8,128)} %shard_map.81.source, bf16[2,128,256]{2,1,0:T(8,128)(2,1)S(1)} %get-tuple-element.91.refs_0_, bf16[2,128,256]{2,1,0:T(8,128)(2,1)S(1)} %collective-permute-done.29.refs_1_, ...), custom_call_target="tpu_custom_call", output_to_operand_aliasing={{}: (1, {})} | custom-call | flops 524288 | bytes 5242880 | tf_op jit(solution)/shard_map/pallas_call | solution.py:451
  (64 shorter events, 0.5 us)
Async XLA Ops:
  0.0 10.2 %copy-start.13 = (s32[8]{0:T(128)S(1)}, s32[8]{0:T(128)}, u32[]{:S(2)}) copy-start(s32[8]{0:T(128)} %constant.25.clone) | copy-start | bytes 100
  0.0 11.4 %copy-start.12 = (s32[8]{0:T(128)S(1)}, s32[8]{0:T(128)}, u32[]{:S(2)}) copy-start(s32[8]{0:T(128)} %constant.24.clone) | copy-start | bytes 100
  0.0 16.0 %copy-start.2 = (f32[512]{0:T(512)S(1)}, f32[512]{0:T(512)}, u32[]{:S(2)}) copy-start(f32[512]{0:T(512)} %param.11) | copy-start | bytes 6148
  0.0 12.7 %collective-permute-start = (bf16[3,64,512]{2,1,0:T(8,128)(2,1)}, bf16[3,64,512]{2,1,0:T(8,128)(2,1)S(1)}, u32[]{:S(2)}, u32[]{:S(2)}) collective-permute-start(bf16[3,64,512]{2,1,0:T(8,128)(2,1)} %refs_0_.1), channel_id=1, source_target_pairs={{0,2},{1,3},{2,0},{3,1},{4,6},{5,7},{6,4},{7,5},{8,10},{9,11},{10,... | collective-permute-start | bytes 589832 | tf_op jit(solution)/shard_map/ppermute | solution.py:339
  3.0 12.8 %collective-permute-start.1 = (bf16[3,64,512]{2,1,0:T(8,128)(2,1)}, bf16[3,64,512]{2,1,0:T(8,128)(2,1)S(1)}, u32[]{:S(2)}, u32[]{:S(2)}) collective-permute-start(bf16[3,64,512]{2,1,0:T(8,128)(2,1)} %refs_0_.1), channel_id=1, source_target_pairs={{0,4},{1,5},{2,6},{3,7},{4,0},{5,1},{6,2},{7,3},{8,12},{9,13},{10,... | collective-permute-start | bytes 589832 | tf_op jit(solution)/shard_map/ppermute | solution.py:339
  4.5 11.2 %collective-permute-start.2 = (bf16[3,64,512]{2,1,0:T(8,128)(2,1)}, bf16[3,64,512]{2,1,0:T(8,128)(2,1)S(1)}, u32[]{:S(2)}, u32[]{:S(2)}) collective-permute-start(bf16[3,64,512]{2,1,0:T(8,128)(2,1)} %refs_0_.1), channel_id=1, source_target_pairs={{0,6},{1,7},{2,4},{3,5},{4,2},{5,3},{6,0},{7,1},{8,14},{9,15},{10,... | collective-permute-start | bytes 589832 | tf_op jit(solution)/shard_map/ppermute | solution.py:339
  4.6 23.7 %copy-start.4 = (s32[2]{0:T(128)}, s32[2]{0:T(128)S(1)}, u32[]{:S(2)}) copy-start(s32[2]{0:T(128)S(1)} %pad_add_fusion.place.source) | copy-start | bytes 28
  4.6 1.6 %copy-start = (f32[2,1,512,512]{3,2,1,0:T(8,128)S(1)}, f32[2,1,512,512]{3,2,1,0:T(8,128)}, u32[]{:S(2)}) copy-start(f32[2,1,512,512]{3,2,1,0:T(8,128)} %param.7) | copy-start | bytes 6291460
  6.2 9.6 %copy-start.1 = (bf16[3,64,512]{2,1,0:T(8,128)(2,1)S(1)}, bf16[3,64,512]{2,1,0:T(8,128)(2,1)}, u32[]{:S(2)}) copy-start(bf16[3,64,512]{2,1,0:T(8,128)(2,1)} %refs_0_.1) | copy-start | bytes 589828
  7.1 9.2 %collective-permute-start.10 = (bf16[2,128,256]{2,1,0:T(8,128)(2,1)S(1)}, bf16[2,128,256]{2,1,0:T(8,128)(2,1)S(1)}, u32[]{:S(2)}, u32[]{:S(2)}) collective-permute-start(bf16[2,128,256]{2,1,0:T(8,128)(2,1)S(1)} %get-tuple-element.62), channel_id=1, source_target_pairs={{0,7},{1,6},{2,5},{3,4},{4,3},{5,2},{6,1},{7,0},{8,15},{9,14},{10,... | collective-permute-start | bytes 393224 | tf_op jit(solution)/shard_map/ppermute | solution.py:306
  8.7 10.1 %collective-permute-start.4 = (bf16[2,128,256]{2,1,0:T(8,128)(2,1)S(1)}, bf16[2,128,256]{2,1,0:T(8,128)(2,1)S(1)}, u32[]{:S(2)}, u32[]{:S(2)}) collective-permute-start(bf16[2,128,256]{2,1,0:T(8,128)(2,1)S(1)} %get-tuple-element.56), channel_id=1, source_target_pairs={{0,1},{1,0},{2,3},{3,2},{4,5},{5,4},{6,7},{7,6},{8,9},{9,8},{10,11... | collective-permute-start | bytes 393224 | tf_op jit(solution)/shard_map/ppermute | solution.py:306
  12.7 15.4 %collective-permute-start.5 = (bf16[2,128,256]{2,1,0:T(8,128)(2,1)S(1)}, bf16[2,128,256]{2,1,0:T(8,128)(2,1)S(1)}, u32[]{:S(2)}, u32[]{:S(2)}) collective-permute-start(bf16[2,128,256]{2,1,0:T(8,128)(2,1)S(1)} %get-tuple-element.57), channel_id=1, source_target_pairs={{0,2},{1,3},{2,0},{3,1},{4,6},{5,7},{6,4},{7,5},{8,10},{9,11},{10,... | collective-permute-start | bytes 393224 | tf_op jit(solution)/shard_map/ppermute | solution.py:306
  15.8 12.3 %collective-permute-start.6 = (bf16[2,128,256]{2,1,0:T(8,128)(2,1)S(1)}, bf16[2,128,256]{2,1,0:T(8,128)(2,1)S(1)}, u32[]{:S(2)}, u32[]{:S(2)}) collective-permute-start(bf16[2,128,256]{2,1,0:T(8,128)(2,1)S(1)} %get-tuple-element.58), channel_id=1, source_target_pairs={{0,3},{1,2},{2,1},{3,0},{4,7},{5,6},{6,5},{7,4},{8,11},{9,10},{10,... | collective-permute-start | bytes 393224 | tf_op jit(solution)/shard_map/ppermute | solution.py:306
  15.9 3.0 %collective-permute-start.3 = (bf16[4,3,64,512]{3,2,1,0:T(8,128)(2,1)S(1)}, bf16[4,3,64,512]{3,2,1,0:T(8,128)(2,1)S(1)}, u32[]{:S(2)}, u32[]{:S(2)}) collective-permute-start(bf16[4,3,64,512]{3,2,1,0:T(8,128)(2,1)S(1)} %pad_maximum_fusion), channel_id=1, source_target_pairs={{0,1},{1,0},{2,3},{3,2},{4,5},{5,4},{6,7},{7,6},{8,9},{9,8},{10,11... | collective-permute-start | bytes 2359304 | tf_op jit(solution)/shard_map/ppermute | solution.py:339
  16.3 11.7 %collective-permute-start.7 = (bf16[2,128,256]{2,1,0:T(8,128)(2,1)S(1)}, bf16[2,128,256]{2,1,0:T(8,128)(2,1)S(1)}, u32[]{:S(2)}, u32[]{:S(2)}) collective-permute-start(bf16[2,128,256]{2,1,0:T(8,128)(2,1)S(1)} %get-tuple-element.59), channel_id=1, source_target_pairs={{0,4},{1,5},{2,6},{3,7},{4,0},{5,1},{6,2},{7,3},{8,12},{9,13},{10,... | collective-permute-start | bytes 393224 | tf_op jit(solution)/shard_map/ppermute | solution.py:306
  18.8 9.6 %collective-permute-start.8 = (bf16[2,128,256]{2,1,0:T(8,128)(2,1)S(1)}, bf16[2,128,256]{2,1,0:T(8,128)(2,1)S(1)}, u32[]{:S(2)}, u32[]{:S(2)}) collective-permute-start(bf16[2,128,256]{2,1,0:T(8,128)(2,1)S(1)} %get-tuple-element.60), channel_id=1, source_target_pairs={{0,5},{1,4},{2,7},{3,6},{4,1},{5,0},{6,3},{7,2},{8,13},{9,12},{10,... | collective-permute-start | bytes 393224 | tf_op jit(solution)/shard_map/ppermute | solution.py:306
  18.9 14.6 %copy-start.11 = (bf16[8,8]{1,0:T(8,128)(2,1)S(1)}, bf16[8,8]{1,0:T(8,128)(2,1)}, u32[]{:S(2)}) copy-start(bf16[8,8]{1,0:T(8,128)(2,1)} %param.9) | copy-start | bytes 388
  18.9 9.4 %collective-permute-start.9 = (bf16[2,128,256]{2,1,0:T(8,128)(2,1)S(1)}, bf16[2,128,256]{2,1,0:T(8,128)(2,1)S(1)}, u32[]{:S(2)}, u32[]{:S(2)}) collective-permute-start(bf16[2,128,256]{2,1,0:T(8,128)(2,1)S(1)} %get-tuple-element.61), channel_id=1, source_target_pairs={{0,6},{1,7},{2,4},{3,5},{4,2},{5,3},{6,0},{7,1},{8,14},{9,15},{10,... | collective-permute-start | bytes 393224 | tf_op jit(solution)/shard_map/ppermute | solution.py:306
  29.0 12.4 %collective-permute-start.11 = (bf16[2,2,64,256]{3,2,1,0:T(8,128)(2,1)S(1)}, bf16[2,2,64,256]{3,2,1,0:T(8,128)(2,1)S(1)}, u32[]{:S(2)}, u32[]{:S(2)}) collective-permute-start(bf16[2,2,64,256]{3,2,1,0:T(8,128)(2,1)S(1)} %get-tuple-element.64), channel_id=1, source_target_pairs={{0,8},{8,0},{16,24},{24,16},{1,9},{9,1},{17,25},{25,17},{2,10},{10... | collective-permute-start | bytes 393224 | tf_op jit(solution)/shard_map/ppermute | solution.py:313
  30.6 12.9 %collective-permute-start.12 = (bf16[2,2,64,256]{3,2,1,0:T(8,128)(2,1)S(1)}, bf16[2,2,64,256]{3,2,1,0:T(8,128)(2,1)S(1)}, u32[]{:S(2)}, u32[]{:S(2)}) collective-permute-start(bf16[2,2,64,256]{3,2,1,0:T(8,128)(2,1)S(1)} %get-tuple-element.65), channel_id=1, source_target_pairs={{0,16},{8,24},{16,0},{24,8},{1,17},{9,25},{17,1},{25,9},{2,18},{10... | collective-permute-start | bytes 393224 | tf_op jit(solution)/shard_map/ppermute | solution.py:313
  33.2 10.3 %collective-permute-start.13 = (bf16[2,2,64,256]{3,2,1,0:T(8,128)(2,1)S(1)}, bf16[2,2,64,256]{3,2,1,0:T(8,128)(2,1)S(1)}, u32[]{:S(2)}, u32[]{:S(2)}) collective-permute-start(bf16[2,2,64,256]{3,2,1,0:T(8,128)(2,1)S(1)} %get-tuple-element.66), channel_id=1, source_target_pairs={{0,24},{8,16},{16,8},{24,0},{1,25},{9,17},{17,9},{25,1},{2,26},{10... | collective-permute-start | bytes 393224 | tf_op jit(solution)/shard_map/ppermute | solution.py:313
  33.6 18.9 %all-to-all-start = ((bf16[8,2,128,256]{3,2,1,0:T(8,128)(2,1)}), bf16[8,2,128,256]{3,2,1,0:T(8,128)(2,1)S(1)}, u32[]{:S(2)}, u32[]{:S(2)}) async-start(bf16[8,2,128,256]{3,2,1,0:T(8,128)(2,1)} %get-tuple-element.54), calls=%async_computation | async-start | bytes 2097152 | tf_op jit(solution)/shard_map/all_to_all | solution.py:300
  37.2 21.7 %collective-permute-start.17 = (bf16[2,2,64,256]{3,2,1,0:T(8,128)(2,1)S(1)}, bf16[2,2,64,256]{3,2,1,0:T(8,128)(2,1)S(1)}, u32[]{:S(2)}, u32[]{:S(2)}) collective-permute-start(bf16[2,2,64,256]{3,2,1,0:T(8,128)(2,1)S(1)} %get-tuple-element.74), channel_id=1, source_target_pairs={{0,8},{8,0},{16,24},{24,16},{1,9},{9,1},{17,25},{25,17},{2,10},{10... | collective-permute-start | bytes 393224 | tf_op jit(solution)/shard_map/ppermute | solution.py:313
  37.9 21.2 %collective-permute-start.18 = (bf16[2,2,64,256]{3,2,1,0:T(8,128)(2,1)S(1)}, bf16[2,2,64,256]{3,2,1,0:T(8,128)(2,1)S(1)}, u32[]{:S(2)}, u32[]{:S(2)}) collective-permute-start(bf16[2,2,64,256]{3,2,1,0:T(8,128)(2,1)S(1)} %get-tuple-element.75), channel_id=1, source_target_pairs={{0,16},{8,24},{16,0},{24,8},{1,17},{9,25},{17,1},{25,9},{2,18},{10... | collective-permute-start | bytes 393224 | tf_op jit(solution)/shard_map/ppermute | solution.py:313
  41.4 17.7 %collective-permute-start.19 = (bf16[2,2,64,256]{3,2,1,0:T(8,128)(2,1)S(1)}, bf16[2,2,64,256]{3,2,1,0:T(8,128)(2,1)S(1)}, u32[]{:S(2)}, u32[]{:S(2)}) collective-permute-start(bf16[2,2,64,256]{3,2,1,0:T(8,128)(2,1)S(1)} %get-tuple-element.76), channel_id=1, source_target_pairs={{0,24},{8,16},{16,8},{24,0},{1,25},{9,17},{17,9},{25,1},{2,26},{10... | collective-permute-start | bytes 393224 | tf_op jit(solution)/shard_map/ppermute | solution.py:313
  44.8 14.3 %copy-start.5 = (s32[2]{0:T(128)S(1)}, s32[2]{0:T(128)}, u32[]{:S(2)}) copy-start(s32[2]{0:T(128)} %copy-done.4) | copy-start | bytes 28
  52.5 0.6 copy-start.10
  54.6 10.3 %collective-permute-start.14 = (bf16[2,2,64,256]{3,2,1,0:T(8,128)(2,1)S(1)}, bf16[2,2,64,256]{3,2,1,0:T(8,128)(2,1)S(1)}, u32[]{:S(2)}, u32[]{:S(2)}) collective-permute-start(bf16[2,2,64,256]{3,2,1,0:T(8,128)(2,1)S(1)} %get-tuple-element.69.refs_1_), channel_id=1, source_target_pairs={{0,8},{8,0},{16,24},{24,16},{1,9},{9,1},{17,25},{25,17},{2,10},{10... | collective-permute-start | bytes 393224 | tf_op jit(solution)/shard_map/ppermute | solution.py:313
  56.0 12.9 %collective-permute-start.15 = (bf16[2,2,64,256]{3,2,1,0:T(8,128)(2,1)S(1)}, bf16[2,2,64,256]{3,2,1,0:T(8,128)(2,1)S(1)}, u32[]{:S(2)}, u32[]{:S(2)}) collective-permute-start(bf16[2,2,64,256]{3,2,1,0:T(8,128)(2,1)S(1)} %get-tuple-element.70.refs_2_), channel_id=1, source_target_pairs={{0,16},{8,24},{16,0},{24,8},{1,17},{9,25},{17,1},{25,9},{2,18},{10... | collective-permute-start | bytes 393224 | tf_op jit(solution)/shard_map/ppermute | solution.py:313
  58.9 10.0 %collective-permute-start.16 = (bf16[2,2,64,256]{3,2,1,0:T(8,128)(2,1)S(1)}, bf16[2,2,64,256]{3,2,1,0:T(8,128)(2,1)S(1)}, u32[]{:S(2)}, u32[]{:S(2)}) collective-permute-start(bf16[2,2,64,256]{3,2,1,0:T(8,128)(2,1)S(1)} %get-tuple-element.71.refs_3_), channel_id=1, source_target_pairs={{0,24},{8,16},{16,8},{24,0},{1,25},{9,17},{17,9},{25,1},{2,26},{10... | collective-permute-start | bytes 393224 | tf_op jit(solution)/shard_map/ppermute | solution.py:313
  59.1 9.8 %copy-start.6 = (f32[8]{0:T(128)S(1)}, f32[8]{0:T(128)}, u32[]{:S(2)}) copy-start(f32[8]{0:T(128)} %occ.9) | copy-start | bytes 100
  60.7 19.4 %collective-permute-start.20 = (bf16[2,2,64,256]{3,2,1,0:T(8,128)(2,1)S(1)}, bf16[2,2,64,256]{3,2,1,0:T(8,128)(2,1)S(1)}, u32[]{:S(2)}, u32[]{:S(2)}) collective-permute-start(bf16[2,2,64,256]{3,2,1,0:T(8,128)(2,1)S(1)} %get-tuple-element.78.refs_2_), channel_id=1, source_target_pairs={{0,8},{8,0},{16,24},{24,16},{1,9},{9,1},{17,25},{25,17},{2,10},{10... | collective-permute-start | bytes 393224 | tf_op jit(solution)/shard_map/ppermute | solution.py:313
  61.2 20.6 %collective-permute-start.21 = (bf16[2,2,64,256]{3,2,1,0:T(8,128)(2,1)S(1)}, bf16[2,2,64,256]{3,2,1,0:T(8,128)(2,1)S(1)}, u32[]{:S(2)}, u32[]{:S(2)}) collective-permute-start(bf16[2,2,64,256]{3,2,1,0:T(8,128)(2,1)S(1)} %get-tuple-element.79.refs_3_), channel_id=1, source_target_pairs={{0,16},{8,24},{16,0},{24,8},{1,17},{9,25},{17,1},{25,9},{2,18},{10... | collective-permute-start | bytes 393224 | tf_op jit(solution)/shard_map/ppermute | solution.py:313
  65.0 16.8 %collective-permute-start.22 = (bf16[2,2,64,256]{3,2,1,0:T(8,128)(2,1)S(1)}, bf16[2,2,64,256]{3,2,1,0:T(8,128)(2,1)S(1)}, u32[]{:S(2)}, u32[]{:S(2)}) collective-permute-start(bf16[2,2,64,256]{3,2,1,0:T(8,128)(2,1)S(1)} %get-tuple-element.80.refs_4_), channel_id=1, source_target_pairs={{0,24},{8,16},{16,8},{24,0},{1,25},{9,17},{17,9},{25,1},{2,26},{10... | collective-permute-start | bytes 393224 | tf_op jit(solution)/shard_map/ppermute | solution.py:313
  71.4 0.8 copy-start.8
  72.2 23.3 %collective-permute-start.26 = (bf16[2,2,64,256]{3,2,1,0:T(8,128)(2,1)S(1)}, bf16[2,2,64,256]{3,2,1,0:T(8,128)(2,1)S(1)}, u32[]{:S(2)}, u32[]{:S(2)}) collective-permute-start(bf16[2,2,64,256]{3,2,1,0:T(8,128)(2,1)S(1)} %get-tuple-element.88), channel_id=1, source_target_pairs={{0,8},{8,0},{16,24},{24,16},{1,9},{9,1},{17,25},{25,17},{2,10},{10... | collective-permute-start | bytes 393224 | tf_op jit(solution)/shard_map/ppermute | solution.py:313
  79.4 17.8 %collective-permute-start.27 = (bf16[2,2,64,256]{3,2,1,0:T(8,128)(2,1)S(1)}, bf16[2,2,64,256]{3,2,1,0:T(8,128)(2,1)S(1)}, u32[]{:S(2)}, u32[]{:S(2)}) collective-permute-start(bf16[2,2,64,256]{3,2,1,0:T(8,128)(2,1)S(1)} %get-tuple-element.89), channel_id=1, source_target_pairs={{0,16},{8,24},{16,0},{24,8},{1,17},{9,25},{17,1},{25,9},{2,18},{10... | collective-permute-start | bytes 393224 | tf_op jit(solution)/shard_map/ppermute | solution.py:313
  80.2 17.0 %collective-permute-start.28 = (bf16[2,2,64,256]{3,2,1,0:T(8,128)(2,1)S(1)}, bf16[2,2,64,256]{3,2,1,0:T(8,128)(2,1)S(1)}, u32[]{:S(2)}, u32[]{:S(2)}) collective-permute-start(bf16[2,2,64,256]{3,2,1,0:T(8,128)(2,1)S(1)} %get-tuple-element.90), channel_id=1, source_target_pairs={{0,24},{8,16},{16,8},{24,0},{1,25},{9,17},{17,9},{25,1},{2,26},{10... | collective-permute-start | bytes 393224 | tf_op jit(solution)/shard_map/ppermute | solution.py:313
  85.4 13.9 %collective-permute-start.23 = (bf16[2,2,64,256]{3,2,1,0:T(8,128)(2,1)S(1)}, bf16[2,2,64,256]{3,2,1,0:T(8,128)(2,1)S(1)}, u32[]{:S(2)}, u32[]{:S(2)}) collective-permute-start(bf16[2,2,64,256]{3,2,1,0:T(8,128)(2,1)S(1)} %get-tuple-element.84), channel_id=1, source_target_pairs={{0,8},{8,0},{16,24},{24,16},{1,9},{9,1},{17,25},{25,17},{2,10},{10... | collective-permute-start | bytes 393224 | tf_op jit(solution)/shard_map/ppermute | solution.py:313
  88.1 11.2 %collective-permute-start.24 = (bf16[2,2,64,256]{3,2,1,0:T(8,128)(2,1)S(1)}, bf16[2,2,64,256]{3,2,1,0:T(8,128)(2,1)S(1)}, u32[]{:S(2)}, u32[]{:S(2)}) collective-permute-start(bf16[2,2,64,256]{3,2,1,0:T(8,128)(2,1)S(1)} %get-tuple-element.85), channel_id=1, source_target_pairs={{0,16},{8,24},{16,0},{24,8},{1,17},{9,25},{17,1},{25,9},{2,18},{10... | collective-permute-start | bytes 393224 | tf_op jit(solution)/shard_map/ppermute | solution.py:313
  88.9 24.7 %all-to-all-start.1 = ((bf16[8,2,128,256]{3,2,1,0:T(8,128)(2,1)}), bf16[8,2,128,256]{3,2,1,0:T(8,128)(2,1)S(1)}, u32[]{:S(2)}, u32[]{:S(2)}) async-start(bf16[8,2,128,256]{3,2,1,0:T(8,128)(2,1)} %get-tuple-element.81), calls=%async_computation.1 | async-start | bytes 2097152 | tf_op jit(solution)/shard_map/all_to_all | solution.py:300
  95.5 7.8 %collective-permute-start.25 = (bf16[2,2,64,256]{3,2,1,0:T(8,128)(2,1)S(1)}, bf16[2,2,64,256]{3,2,1,0:T(8,128)(2,1)S(1)}, u32[]{:S(2)}, u32[]{:S(2)}) collective-permute-start(bf16[2,2,64,256]{3,2,1,0:T(8,128)(2,1)S(1)} %get-tuple-element.86), channel_id=1, source_target_pairs={{0,24},{8,16},{16,8},{24,0},{1,25},{9,17},{17,9},{25,1},{2,26},{10... | collective-permute-start | bytes 393224 | tf_op jit(solution)/shard_map/ppermute | solution.py:313
  97.1 1.0 copy-start.9
  103.3 10.3 %copy-start.3 = (f32[512]{0:T(512)S(1)}, f32[512]{0:T(512)}, u32[]{:S(2)}) copy-start(f32[512]{0:T(512)} %param.11) | copy-start | bytes 6148
  104.4 4.1 %collective-permute-start.29 = (bf16[2,128,256]{2,1,0:T(8,128)(2,1)S(1)}, bf16[2,128,256]{2,1,0:T(8,128)(2,1)S(1)}, u32[]{:S(2)}, u32[]{:S(2)}) collective-permute-start(bf16[2,128,256]{2,1,0:T(8,128)(2,1)S(1)} %get-tuple-element.92), channel_id=1, source_target_pairs={{0,1},{1,0},{2,3},{3,2},{4,5},{5,4},{6,7},{7,6},{8,9},{9,8},{10,11... | collective-permute-start | bytes 393224 | tf_op jit(solution)/shard_map/ppermute | solution.py:306
  104.5 8.8 %collective-permute-start.30 = (bf16[2,128,256]{2,1,0:T(8,128)(2,1)S(1)}, bf16[2,128,256]{2,1,0:T(8,128)(2,1)S(1)}, u32[]{:S(2)}, u32[]{:S(2)}) collective-permute-start(bf16[2,128,256]{2,1,0:T(8,128)(2,1)S(1)} %get-tuple-element.93), channel_id=1, source_target_pairs={{0,2},{1,3},{2,0},{3,1},{4,6},{5,7},{6,4},{7,5},{8,10},{9,11},{10,... | collective-permute-start | bytes 393224 | tf_op jit(solution)/shard_map/ppermute | solution.py:306
  106.3 16.6 %collective-permute-start.31 = (bf16[2,128,256]{2,1,0:T(8,128)(2,1)S(1)}, bf16[2,128,256]{2,1,0:T(8,128)(2,1)S(1)}, u32[]{:S(2)}, u32[]{:S(2)}) collective-permute-start(bf16[2,128,256]{2,1,0:T(8,128)(2,1)S(1)} %get-tuple-element.94), channel_id=1, source_target_pairs={{0,3},{1,2},{2,1},{3,0},{4,7},{5,6},{6,5},{7,4},{8,11},{9,10},{10,... | collective-permute-start | bytes 393224 | tf_op jit(solution)/shard_map/ppermute | solution.py:306
  106.4 16.5 %collective-permute-start.32 = (bf16[2,128,256]{2,1,0:T(8,128)(2,1)S(1)}, bf16[2,128,256]{2,1,0:T(8,128)(2,1)S(1)}, u32[]{:S(2)}, u32[]{:S(2)}) collective-permute-start(bf16[2,128,256]{2,1,0:T(8,128)(2,1)S(1)} %get-tuple-element.95), channel_id=1, source_target_pairs={{0,4},{1,5},{2,6},{3,7},{4,0},{5,1},{6,2},{7,3},{8,12},{9,13},{10,... | collective-permute-start | bytes 393224 | tf_op jit(solution)/shard_map/ppermute | solution.py:306
  108.6 14.3 %collective-permute-start.33 = (bf16[2,128,256]{2,1,0:T(8,128)(2,1)S(1)}, bf16[2,128,256]{2,1,0:T(8,128)(2,1)S(1)}, u32[]{:S(2)}, u32[]{:S(2)}) collective-permute-start(bf16[2,128,256]{2,1,0:T(8,128)(2,1)S(1)} %get-tuple-element.96), channel_id=1, source_target_pairs={{0,5},{1,4},{2,7},{3,6},{4,1},{5,0},{6,3},{7,2},{8,13},{9,12},{10,... | collective-permute-start | bytes 393224 | tf_op jit(solution)/shard_map/ppermute | solution.py:306
  108.6 14.3 %collective-permute-start.34 = (bf16[2,128,256]{2,1,0:T(8,128)(2,1)S(1)}, bf16[2,128,256]{2,1,0:T(8,128)(2,1)S(1)}, u32[]{:S(2)}, u32[]{:S(2)}) collective-permute-start(bf16[2,128,256]{2,1,0:T(8,128)(2,1)S(1)} %get-tuple-element.97), channel_id=1, source_target_pairs={{0,6},{1,7},{2,4},{3,5},{4,2},{5,3},{6,0},{7,1},{8,14},{9,15},{10,... | collective-permute-start | bytes 393224 | tf_op jit(solution)/shard_map/ppermute | solution.py:306
  113.3 9.6 %collective-permute-start.35 = (bf16[2,128,256]{2,1,0:T(8,128)(2,1)S(1)}, bf16[2,128,256]{2,1,0:T(8,128)(2,1)S(1)}, u32[]{:S(2)}, u32[]{:S(2)}) collective-permute-start(bf16[2,128,256]{2,1,0:T(8,128)(2,1)S(1)} %get-tuple-element.98), channel_id=1, source_target_pairs={{0,7},{1,6},{2,5},{3,4},{4,3},{5,2},{6,1},{7,0},{8,15},{9,14},{10,... | collective-permute-start | bytes 393224 | tf_op jit(solution)/shard_map/ppermute | solution.py:306
  113.7 1.4 %copy-start.7 = (bf16[512,1536]{1,0:T(8,128)(2,1)S(1)}, bf16[512,1536]{1,0:T(8,128)(2,1)}, u32[]{:S(2)}) copy-start(bf16[512,1536]{1,0:T(8,128)(2,1)} %get-tuple-element.82.whole) | copy-start | bytes 4718596

commit v17 on v15

--- a/solution.py
+++ b/solution.py
@@ -11,6 +11,7 @@
 VMEM = pl.BlockSpec(memory_space=pltpu.VMEM)
 SMEM = pl.BlockSpec(memory_space=pltpu.SMEM)
 PARAMS = pltpu.CompilerParams(vmem_limit_bytes=50 * 2**20)
+ALONE = pltpu.CompilerParams(vmem_limit_bytes=62 * 2**20)
 WIDE = jnp.float32
 LONG = 3 * 10**10
 NARROW = jnp.bfloat16
@@ -429,7 +430,7 @@
         )
         sent, rest, mixed = [sent_one], rest + [rest_one], mixed + [mixed_one]
     other = [across_first([None] + x, groups)[1:] for x in mixed]
-    back = exchange(tie(sent[0], other[0][min(1, groups - 2)]))
+    back = exchange(sent[0])
     def by_pair(*shape):
         return pl.BlockSpec((1, *shape), lambda pair: (pair, 0, 0))
 
@@ -450,7 +451,7 @@
             pltpu.VMEM(whole.shape, NARROW), inner, square, pltpu.VMEM((virtual, virtual), NARROW),
             pltpu.SemaphoreType.DMA,
         ],
-        compiler_params=PARAMS,
+        compiler_params=ALONE,
         cost_estimate=pl.CostEstimate(flops=ladder_flops, bytes_accessed=12 * count, transcendentals=0),
     )(place, occ_energy, current, back, jnp.broadcast_to(vir_energy[:, None], (virtual, 128)),
       vir_energy[None, :], whole)

time: 130 us -> 128 us (0.985)
  local copies, waits for them, and re-layouts: 6.94 us -> 4.46 us
  waiting for transfers between devices: 22.1 us -> 20.4 us
  Pallas kernels: 31.4 us -> 32.8 us
    ppermute x14, waiting for transfers between devices: 6.49 us -> 2.09 us  [by_distance(): lax.ppermute(parts[k], 'occj', [(d, d ^ k) for d in range(devices)])]
    unnamed x28, local copies, waits for them, and re-layouts: 5.43 us -> 2.24 us
    ppermute x18, waiting for transfers between devices: 5.37 us -> 8.14 us  [across_first(): lax.ppermute(parts[s], 'occi', [(k, k ^ s) for k in range(groups)])]
    pallas_call x1, Pallas kernels: 8.15 us -> 9.62 us  [local(): pl.pallas_call(functools.partial(second_ladder_kernel, tiles, first), gri...]
    ppermute x18, starting transfers between devices: 37.2 us -> 38.6 us  [across_first(): lax.ppermute(parts[s], 'occi', [(k, k ^ s) for k in range(groups)])]
  transfers between devices with their start and end apart: 38 -> 38, of which waited for: 8 -> 7; matrix products, arithmetic and copies ran while one was open for 1% -> 2% of each run, Pallas kernels for 22% -> 23%
where the time goes in v17:
time: 128 us; the launch traced here: 127 us
  starting transfers between devices  67.5 us (53%)
  Pallas kernels  32.8 us (26%)
  waiting for transfers between devices  20.4 us (16%)
  local copies, waits for them, and re-layouts  4.46 us (3%)
  between operations  1.67 us (1%)
    ppermute x18, starting transfers between devices, across_first(): lax.ppermute(parts[s], 'occi', [(k, k ^ s) for k in range(groups)])  38.6 us
    pallas_call x9, Pallas kernels, call(): pl.pallas_call(body, out_shape=outs, in_specs=specs, out_specs=jax.tree.m...  19.2 us
    ppermute x14, starting transfers between devices, by_distance(): lax.ppermute(parts[k], 'occj', [(d, d ^ k) for d in range(devices)])  16.5 us
    pallas_call x1, Pallas kernels, local(): pl.pallas_call(functools.partial(second_ladder_kernel, tiles, first), gri...  9.62 us
    ppermute x18, waiting for transfers between devices, across_first(): lax.ppermute(parts[s], 'occi', [(k, k ^ s) for k in range(groups)])  8.14 us
    all_to_all x2, starting transfers between devices, exchange(): lax.all_to_all(blocks, 'occj', split_axis=0, concat_axis=0, tiled=True)  7.81 us
    all_to_all x2, waiting for transfers between devices, exchange(): lax.all_to_all(blocks, 'occj', split_axis=0, concat_axis=0, tiled=True)  7.71 us
    ppermute x4, starting transfers between devices, turn(): return lax.ppermute(x, 'occj', [(d, d ^ k) for d in range(devices)])  4.62 us
  transfers between devices with their start and end apart: 38, of which 7 were waited for; matrix products, arithmetic and copies ran while one was open for 2% of the time, Pallas kernels for 23%

profile of v17, /device:TPU:0, one launch (start us, length us, event | category | flops | bytes accessed | tf_op | source)
XLA Modules:
  0.0 127.3 jit_solution(3475526924522311171)
XLA Ops:
  0.0 3.0 %collective-permute-start = (bf16[3,64,512]{2,1,0:T(8,128)(2,1)}, bf16[3,64,512]{2,1,0:T(8,128)(2,1)S(1)}, u32[]{:S(2)}, u32[]{:S(2)}) collective-permute-start(bf16[3,64,512]{2,1,0:T(8,128)(2,1)} %refs_0_.1), channel_id=1, source_target_pairs={{0,2},{1,3},{2,0},{3,1},{4,6},{5,7},{6,4},{7,5},{8,10},{9,11},{10,... | collective-permute-start | bytes 589832 | tf_op jit(solution)/shard_map/ppermute | solution.py:351
  3.0 1.5 %collective-permute-start.1 = (bf16[3,64,512]{2,1,0:T(8,128)(2,1)}, bf16[3,64,512]{2,1,0:T(8,128)(2,1)S(1)}, u32[]{:S(2)}, u32[]{:S(2)}) collective-permute-start(bf16[3,64,512]{2,1,0:T(8,128)(2,1)} %refs_0_.1), channel_id=1, source_target_pairs={{0,4},{1,5},{2,6},{3,7},{4,0},{5,1},{6,2},{7,3},{8,12},{9,13},{10,... | collective-permute-start | bytes 589832 | tf_op jit(solution)/shard_map/ppermute | solution.py:351
  4.6 0.1 pad_add_fusion.place.source
  4.6 1.6 %copy-done = f32[2,1,512,512]{3,2,1,0:T(8,128)S(1)} copy-done((f32[2,1,512,512]{3,2,1,0:T(8,128)S(1)}, f32[2,1,512,512]{3,2,1,0:T(8,128)}, u32[]{:S(2)}) %copy-start) | copy-done | bytes 2097176
  6.2 0.9 shard_map.73
  7.1 1.6 %collective-permute-start.10 = (bf16[2,128,256]{2,1,0:T(8,128)(2,1)S(1)}, bf16[2,128,256]{2,1,0:T(8,128)(2,1)S(1)}, u32[]{:S(2)}, u32[]{:S(2)}) collective-permute-start(bf16[2,128,256]{2,1,0:T(8,128)(2,1)S(1)} %get-tuple-element.62), channel_id=1, source_target_pairs={{0,7},{1,6},{2,5},{3,4},{4,3},{5,2},{6,1},{7,0},{8,15},{9,14},{10,... | collective-permute-start | bytes 393224 | tf_op jit(solution)/shard_map/ppermute | solution.py:318
  8.7 1.5 %collective-permute-start.4 = (bf16[2,128,256]{2,1,0:T(8,128)(2,1)S(1)}, bf16[2,128,256]{2,1,0:T(8,128)(2,1)S(1)}, u32[]{:S(2)}, u32[]{:S(2)}) collective-permute-start(bf16[2,128,256]{2,1,0:T(8,128)(2,1)S(1)} %get-tuple-element.56), channel_id=1, source_target_pairs={{0,1},{1,0},{2,3},{3,2},{4,5},{5,4},{6,7},{7,6},{8,9},{9,8},{10,11... | collective-permute-start | bytes 393224 | tf_op jit(solution)/shard_map/ppermute | solution.py:318
  10.2 0.6 dynamic_slice.14
  11.4 0.6 dynamic_slice.12
  12.7 0.6 collective-permute-start.5
  13.3 2.5 %collective-permute-done.1.refs_2_ = bf16[3,64,512]{2,1,0:T(8,128)(2,1)S(1)} collective-permute-done((bf16[3,64,512]{2,1,0:T(8,128)(2,1)}, bf16[3,64,512]{2,1,0:T(8,128)(2,1)S(1)}, u32[]{:S(2)}, u32[]{:S(2)}) %collective-permute-start.1) | collective-permute-done | bytes 196640 | tf_op jit(solution)/shard_map/ppermute | solution.py:351
  15.8 0.1 pad_maximum_fusion
  16.0 0.1 fusion
  16.1 0.1 fusion.1
  16.1 0.1 fusion.2
  16.2 0.1 broadcast_add_fusion.2
  16.3 2.4 %collective-permute-start.7 = (bf16[2,128,256]{2,1,0:T(8,128)(2,1)S(1)}, bf16[2,128,256]{2,1,0:T(8,128)(2,1)S(1)}, u32[]{:S(2)}, u32[]{:S(2)}) collective-permute-start(bf16[2,128,256]{2,1,0:T(8,128)(2,1)S(1)} %get-tuple-element.59), channel_id=1, source_target_pairs={{0,4},{1,5},{2,6},{3,7},{4,0},{5,1},{6,2},{7,3},{8,12},{9,13},{10,... | collective-permute-start | bytes 393224 | tf_op jit(solution)/shard_map/ppermute | solution.py:318
  18.8 0.2 collective-permute-start.8
  18.9 2.9 %collective-permute-start.9 = (bf16[2,128,256]{2,1,0:T(8,128)(2,1)S(1)}, bf16[2,128,256]{2,1,0:T(8,128)(2,1)S(1)}, u32[]{:S(2)}, u32[]{:S(2)}) collective-permute-start(bf16[2,128,256]{2,1,0:T(8,128)(2,1)S(1)} %get-tuple-element.61), channel_id=1, source_target_pairs={{0,6},{1,7},{2,4},{3,5},{4,2},{5,3},{6,0},{7,1},{8,14},{9,15},{10,... | collective-permute-start | bytes 393224 | tf_op jit(solution)/shard_map/ppermute | solution.py:318
  21.8 6.2 %shard_map.74 = (bf16[8,2,128,256]{3,2,1,0:T(8,128)(2,1)}, bf16[512,1536]{1,0:T(8,128)(2,1)}) custom-call(s32[2]{0:T(128)S(1)} %pad_add_fusion.place.source, f32[2,512,512]{2,1,0:T(8,128)} %bitcast.13, bf16[3,64,512]{2,1,0:T(8,128)(2,1)S(1)} %copy-done.1, bf16[3,64,512]{2,1,0:T(8,128)(2,1)S(1)} %collective-permute-done.refs_1_, ...), custom_call_target="tpu_custom_call" | custom-call | flops 3221225472 | bytes 4194304 | tf_op jit(solution)/shard_map/pallas_call | solution.py:43
  28.0 0.3 collective-permute-done.8.refs_5_
  28.3 0.7 shard_map.75
  29.0 1.6 %collective-permute-start.11 = (bf16[2,2,64,256]{3,2,1,0:T(8,128)(2,1)S(1)}, bf16[2,2,64,256]{3,2,1,0:T(8,128)(2,1)S(1)}, u32[]{:S(2)}, u32[]{:S(2)}) collective-permute-start(bf16[2,2,64,256]{3,2,1,0:T(8,128)(2,1)S(1)} %get-tuple-element.64), channel_id=1, source_target_pairs={{0,8},{8,0},{16,24},{24,16},{1,9},{9,1},{17,25},{25,17},{2,10},{10... | collective-permute-start | bytes 393224 | tf_op jit(solution)/shard_map/ppermute | solution.py:325
  30.6 2.6 %collective-permute-start.12 = (bf16[2,2,64,256]{3,2,1,0:T(8,128)(2,1)S(1)}, bf16[2,2,64,256]{3,2,1,0:T(8,128)(2,1)S(1)}, u32[]{:S(2)}, u32[]{:S(2)}) collective-permute-start(bf16[2,2,64,256]{3,2,1,0:T(8,128)(2,1)S(1)} %get-tuple-element.65), channel_id=1, source_target_pairs={{0,16},{8,24},{16,0},{24,8},{1,17},{9,25},{17,1},{25,9},{2,18},{10... | collective-permute-start | bytes 393224 | tf_op jit(solution)/shard_map/ppermute | solution.py:325
  33.2 0.2 collective-permute-start.13
  33.5 0.1 broadcast_add_fusion
  33.6 3.6 %all-to-all-start = ((bf16[8,2,128,256]{3,2,1,0:T(8,128)(2,1)}), bf16[8,2,128,256]{3,2,1,0:T(8,128)(2,1)S(1)}, u32[]{:S(2)}, u32[]{:S(2)}) async-start(bf16[8,2,128,256]{3,2,1,0:T(8,128)(2,1)} %get-tuple-element.54), calls=%async_computation | async-start | bytes 2097152 | tf_op jit(solution)/shard_map/all_to_all | solution.py:312
  37.2 0.7 collective-permute-start.17
  37.9 3.5 %collective-permute-start.18 = (bf16[2,2,64,256]{3,2,1,0:T(8,128)(2,1)S(1)}, bf16[2,2,64,256]{3,2,1,0:T(8,128)(2,1)S(1)}, u32[]{:S(2)}, u32[]{:S(2)}) collective-permute-start(bf16[2,2,64,256]{3,2,1,0:T(8,128)(2,1)S(1)} %get-tuple-element.75), channel_id=1, source_target_pairs={{0,16},{8,24},{16,0},{24,8},{1,17},{9,25},{17,1},{25,9},{2,18},{10... | collective-permute-start | bytes 393224 | tf_op jit(solution)/shard_map/ppermute | solution.py:325
  41.4 0.2 collective-permute-start.19
  41.6 2.0 %collective-permute-done.12.refs_2_ = bf16[2,2,64,256]{3,2,1,0:T(8,128)(2,1)S(1)} collective-permute-done((bf16[2,2,64,256]{3,2,1,0:T(8,128)(2,1)S(1)}, bf16[2,2,64,256]{3,2,1,0:T(8,128)(2,1)S(1)}, u32[]{:S(2)}, u32[]{:S(2)}) %collective-permute-start.12) | collective-permute-done | bytes 131104 | tf_op jit(solution)/shard_map/ppermute | solution.py:325
  43.6 1.2 shard_map.76.place
  44.8 7.7 %all-to-all-done.ladder = bf16[8,2,128,256]{3,2,1,0:T(8,128)(2,1)S(1)} async-done(((bf16[8,2,128,256]{3,2,1,0:T(8,128)(2,1)}), bf16[8,2,128,256]{3,2,1,0:T(8,128)(2,1)S(1)}, u32[]{:S(2)}, u32[]{:S(2)}) %all-to-all-start) | async-done | bytes 1048608 | tf_op jit(solution)/shard_map/all_to_all | solution.py:312
  52.5 0.6 copy-done.8
  53.1 1.6 %shard_map.77 = (bf16[2,2,64,256]{3,2,1,0:T(8,128)(2,1)S(1)}, bf16[2,2,64,256]{3,2,1,0:T(8,128)(2,1)S(1)}, bf16[2,2,64,256]{3,2,1,0:T(8,128)(2,1)S(1)}, bf16[2,2,64,256]{3,2,1,0:T(8,128)(2,1)S(1)}) custom-call(s32[2]{0:T(128)S(1)} %copy-done.8, f32[8,8]{1,0:T(8,128)S(1)} %convert_element_type.3.fock, bf16[8,2,128,256]{3,2,1,0:T(8,128)(2,1)S(1)} %all-to-all-done.ladder, ...), custom_call_target="tpu_custom_call" | custom-call | flops 30000001024 | bytes 3145728 | tf_op jit(solution)/shard_map/pallas_call | solution.py:43
  54.7 1.4 %collective-permute-start.14 = (bf16[2,2,64,256]{3,2,1,0:T(8,128)(2,1)S(1)}, bf16[2,2,64,256]{3,2,1,0:T(8,128)(2,1)S(1)}, u32[]{:S(2)}, u32[]{:S(2)}) collective-permute-start(bf16[2,2,64,256]{3,2,1,0:T(8,128)(2,1)S(1)} %get-tuple-element.69.refs_1_), channel_id=1, source_target_pairs={{0,8},{8,0},{16,24},{24,16},{1,9},{9,1},{17,25},{25,17},{2,10},{10... | collective-permute-start | bytes 393224 | tf_op jit(solution)/shard_map/ppermute | solution.py:325
  56.0 2.9 %collective-permute-start.15 = (bf16[2,2,64,256]{3,2,1,0:T(8,128)(2,1)S(1)}, bf16[2,2,64,256]{3,2,1,0:T(8,128)(2,1)S(1)}, u32[]{:S(2)}, u32[]{:S(2)}) collective-permute-start(bf16[2,2,64,256]{3,2,1,0:T(8,128)(2,1)S(1)} %get-tuple-element.70.refs_2_), channel_id=1, source_target_pairs={{0,16},{8,24},{16,0},{24,8},{1,17},{9,25},{17,1},{25,9},{2,18},{10... | collective-permute-start | bytes 393224 | tf_op jit(solution)/shard_map/ppermute | solution.py:325
  58.9 0.2 collective-permute-start.16
  59.1 1.6 %shard_map.79 = (bf16[2,2,64,256]{3,2,1,0:T(8,128)(2,1)S(1)}, bf16[2,2,64,256]{3,2,1,0:T(8,128)(2,1)S(1)}, bf16[2,2,64,256]{3,2,1,0:T(8,128)(2,1)S(1)}, bf16[2,2,64,256]{3,2,1,0:T(8,128)(2,1)S(1)}) custom-call(s32[2]{0:T(128)S(1)} %copy-done.3, f32[8,8]{1,0:T(8,128)S(1)} %convert_element_type.3.fock, bf16[8,2,128,256]{3,2,1,0:T(8,128)(2,1)S(1)} %all-to-all-done.ladder, ...), custom_call_target="tpu_custom_call" | custom-call | flops 30000001024 | bytes 3145728 | tf_op jit(solution)/shard_map/pallas_call | solution.py:43
  60.7 0.5 collective-permute-start.20
  61.2 3.8 %collective-permute-start.21 = (bf16[2,2,64,256]{3,2,1,0:T(8,128)(2,1)S(1)}, bf16[2,2,64,256]{3,2,1,0:T(8,128)(2,1)S(1)}, u32[]{:S(2)}, u32[]{:S(2)}) collective-permute-start(bf16[2,2,64,256]{3,2,1,0:T(8,128)(2,1)S(1)} %get-tuple-element.79.refs_3_), channel_id=1, source_target_pairs={{0,16},{8,24},{16,0},{24,8},{1,17},{9,25},{17,1},{25,9},{2,18},{10... | collective-permute-start | bytes 393224 | tf_op jit(solution)/shard_map/ppermute | solution.py:325
  65.0 2.9 %collective-permute-start.22 = (bf16[2,2,64,256]{3,2,1,0:T(8,128)(2,1)S(1)}, bf16[2,2,64,256]{3,2,1,0:T(8,128)(2,1)S(1)}, u32[]{:S(2)}, u32[]{:S(2)}) collective-permute-start(bf16[2,2,64,256]{3,2,1,0:T(8,128)(2,1)S(1)} %get-tuple-element.80.refs_4_), channel_id=1, source_target_pairs={{0,24},{8,16},{16,8},{24,0},{1,25},{9,17},{17,9},{25,1},{2,26},{10... | collective-permute-start | bytes 393224 | tf_op jit(solution)/shard_map/ppermute | solution.py:325
  67.9 1.0 collective-permute-done.15.refs_6_
  68.9 2.5 %shard_map.78 = (bf16[8,2,64,256]{3,2,1,0:T(8,128)(2,1)S(1)}, bf16[2,8,64,256]{3,2,1,0:T(8,128)(2,1)S(1)}, bf16[2,2,64,256]{3,2,1,0:T(8,128)(2,1)S(1)}, bf16[2,2...) custom-call(s32[2]{0:T(128)S(1)} %copy-done.3, f32[8,8]{1,0:T(8,128)S(1)} %convert_element_type.3.fock, ...), custom_call_target="tpu_custom_call" | custom-call | flops 30000001024 | bytes 5242880 | tf_op jit(solution)/shard_map/pallas_call | solution.py:43
  71.4 7.2 %collective-permute-start.26 = (bf16[2,2,64,256]{3,2,1,0:T(8,128)(2,1)S(1)}, bf16[2,2,64,256]{3,2,1,0:T(8,128)(2,1)S(1)}, u32[]{:S(2)}, u32[]{:S(2)}) collective-permute-start(bf16[2,2,64,256]{3,2,1,0:T(8,128)(2,1)S(1)} %get-tuple-element.88), channel_id=1, source_target_pairs={{0,8},{8,0},{16,24},{24,16},{1,9},{9,1},{17,25},{25,17},{2,10},{10... | collective-permute-start | bytes 393224 | tf_op jit(solution)/shard_map/ppermute | solution.py:325
  78.6 0.9 collective-permute-start.27
  79.5 1.6 %collective-permute-start.28 = (bf16[2,2,64,256]{3,2,1,0:T(8,128)(2,1)S(1)}, bf16[2,2,64,256]{3,2,1,0:T(8,128)(2,1)S(1)}, u32[]{:S(2)}, u32[]{:S(2)}) collective-permute-start(bf16[2,2,64,256]{3,2,1,0:T(8,128)(2,1)S(1)} %get-tuple-element.90), channel_id=1, source_target_pairs={{0,24},{8,16},{16,8},{24,0},{1,25},{9,17},{17,9},{25,1},{2,26},{10... | collective-permute-start | bytes 393224 | tf_op jit(solution)/shard_map/ppermute | solution.py:325
  81.1 3.6 %shard_map.80 = (bf16[8,2,128,256]{3,2,1,0:T(8,128)(2,1)}, bf16[2,8,64,256]{3,2,1,0:T(8,128)(2,1)S(1)}, bf16[2,2,64,256]{3,2,1,0:T(8,128)(2,1)S(1)}, bf16[2,2,64...) custom-call(s32[2]{0:T(128)S(1)} %copy-done.3, f32[8,8]{1,0:T(8,128)S(1)} %convert_element_type.3.fock, ...), custom_call_target="tpu_custom_call" | custom-call | flops 30000001024 | bytes 5242880 | tf_op jit(solution)/shard_map/pallas_call | solution.py:43
  84.7 4.9 %collective-permute-start.23 = (bf16[2,2,64,256]{3,2,1,0:T(8,128)(2,1)S(1)}, bf16[2,2,64,256]{3,2,1,0:T(8,128)(2,1)S(1)}, u32[]{:S(2)}, u32[]{:S(2)}) collective-permute-start(bf16[2,2,64,256]{3,2,1,0:T(8,128)(2,1)S(1)} %get-tuple-element.84), channel_id=1, source_target_pairs={{0,8},{8,0},{16,24},{24,16},{1,9},{9,1},{17,25},{25,17},{2,10},{10... | collective-permute-start | bytes 393224 | tf_op jit(solution)/shard_map/ppermute | solution.py:325
  89.6 2.1 %collective-permute-start.24 = (bf16[2,2,64,256]{3,2,1,0:T(8,128)(2,1)S(1)}, bf16[2,2,64,256]{3,2,1,0:T(8,128)(2,1)S(1)}, u32[]{:S(2)}, u32[]{:S(2)}) collective-permute-start(bf16[2,2,64,256]{3,2,1,0:T(8,128)(2,1)S(1)} %get-tuple-element.85), channel_id=1, source_target_pairs={{0,16},{8,24},{16,0},{24,8},{1,17},{9,25},{17,1},{25,9},{2,18},{10... | collective-permute-start | bytes 393224 | tf_op jit(solution)/shard_map/ppermute | solution.py:325
  91.7 4.2 %all-to-all-start.1 = ((bf16[8,2,128,256]{3,2,1,0:T(8,128)(2,1)}), bf16[8,2,128,256]{3,2,1,0:T(8,128)(2,1)}, u32[]{:S(2)}, u32[]{:S(2)}) async-start(bf16[8,2,128,256]{3,2,1,0:T(8,128)(2,1)} %get-tuple-element.81), calls=%async_computation.1 | async-start | bytes 2097152 | tf_op jit(solution)/shard_map/all_to_all | solution.py:312
  95.9 1.5 %collective-permute-start.25 = (bf16[2,2,64,256]{3,2,1,0:T(8,128)(2,1)S(1)}, bf16[2,2,64,256]{3,2,1,0:T(8,128)(2,1)S(1)}, u32[]{:S(2)}, u32[]{:S(2)}) collective-permute-start(bf16[2,2,64,256]{3,2,1,0:T(8,128)(2,1)S(1)} %get-tuple-element.86), channel_id=1, source_target_pairs={{0,24},{8,16},{16,8},{24,0},{1,25},{9,17},{17,9},{25,1},{2,26},{10... | collective-permute-start | bytes 393224 | tf_op jit(solution)/shard_map/ppermute | solution.py:325
  97.4 1.1 shard_map.82.refs_3_
  98.5 5.1 %collective-permute-done.25.refs_2_ = bf16[2,2,64,256]{3,2,1,0:T(8,128)(2,1)S(1)} collective-permute-done((bf16[2,2,64,256]{3,2,1,0:T(8,128)(2,1)S(1)}, bf16[2,2,64,256]{3,2,1,0:T(8,128)(2,1)S(1)}, u32[]{:S(2)}, u32[]{:S(2)}) %collective-permute-start.25) | collective-permute-done | bytes 131104 | tf_op jit(solution)/shard_map/ppermute | solution.py:325
  103.6 1.2 shard_map.83
  104.9 1.7 %collective-permute-start.30 = (bf16[2,128,256]{2,1,0:T(8,128)(2,1)S(1)}, bf16[2,128,256]{2,1,0:T(8,128)(2,1)S(1)}, u32[]{:S(2)}, u32[]{:S(2)}) collective-permute-start(bf16[2,128,256]{2,1,0:T(8,128)(2,1)S(1)} %get-tuple-element.93), channel_id=1, source_target_pairs={{0,2},{1,3},{2,0},{3,1},{4,6},{5,7},{6,4},{7,5},{8,10},{9,11},{10,... | collective-permute-start | bytes 393224 | tf_op jit(solution)/shard_map/ppermute | solution.py:318
  106.6 0.1 collective-permute-start.31
  106.7 2.2 %collective-permute-start.32 = (bf16[2,128,256]{2,1,0:T(8,128)(2,1)S(1)}, bf16[2,128,256]{2,1,0:T(8,128)(2,1)S(1)}, u32[]{:S(2)}, u32[]{:S(2)}) collective-permute-start(bf16[2,128,256]{2,1,0:T(8,128)(2,1)S(1)} %get-tuple-element.95), channel_id=1, source_target_pairs={{0,4},{1,5},{2,6},{3,7},{4,0},{5,1},{6,2},{7,3},{8,12},{9,13},{10,... | collective-permute-start | bytes 393224 | tf_op jit(solution)/shard_map/ppermute | solution.py:318
  109.0 2.9 %collective-permute-start.34 = (bf16[2,128,256]{2,1,0:T(8,128)(2,1)S(1)}, bf16[2,128,256]{2,1,0:T(8,128)(2,1)S(1)}, u32[]{:S(2)}, u32[]{:S(2)}) collective-permute-start(bf16[2,128,256]{2,1,0:T(8,128)(2,1)S(1)} %get-tuple-element.97), channel_id=1, source_target_pairs={{0,6},{1,7},{2,4},{3,5},{4,2},{5,3},{6,0},{7,1},{8,14},{9,15},{10,... | collective-permute-start | bytes 393224 | tf_op jit(solution)/shard_map/ppermute | solution.py:318
  111.8 1.8 %collective-permute-done.30.refs_2_ = bf16[2,128,256]{2,1,0:T(8,128)(2,1)S(1)} collective-permute-done((bf16[2,128,256]{2,1,0:T(8,128)(2,1)S(1)}, bf16[2,128,256]{2,1,0:T(8,128)(2,1)S(1)}, u32[]{:S(2)}, u32[]{:S(2)}) %collective-permute-start.30) | collective-permute-done | bytes 131104 | tf_op jit(solution)/shard_map/ppermute | solution.py:318
  113.6 0.4 collective-permute-start.35
  114.0 0.8 broadcast_in_dim.4.row
  114.8 9.6 %shard_map.81.source = f32[2,512,512]{2,1,0:T(8,128)} custom-call(s32[2]{0:T(128)} %copy-done.2, f32[8]{0:T(128)} %occ.9, f32[2,512,512]{2,1,0:T(8,128)} %bitcast.14, bf16[8,2,128,256]{3,2,1,0:T(8,128)(2,1)} %all-to-all-done.1.blocks, f32[512,128]{1,0:T(8,128)} %broadcast_in_dim.4.row, f32[1,512]{1,0:T(1,128)} %bitcast.20, ...), custom_call_target="tpu_custom_call" | custom-call | flops 3221225472 | bytes 6291456 | tf_op jit(solution)/shard_map/pallas_call | solution.py:440
  124.5 2.8 %shard_map.84 = f32[2,512,512]{2,1,0:T(8,128)} custom-call(s32[2]{0:T(128)S(1)} %copy-done.4, f32[2,512,512]{2,1,0:T(8,128)} %shard_map.81.source, bf16[2,128,256]{2,1,0:T(8,128)(2,1)S(1)} %get-tuple-element.91.refs_0_, bf16[2,128,256]{2,1,0:T(8,128)(2,1)S(1)} %collective-permute-done.29.refs_1_, ...), custom_call_target="tpu_custom_call", output_to_operand_aliasing={{}: (1, {})} | custom-call | flops 524288 | bytes 5242880 | tf_op jit(solution)/shard_map/pallas_call | solution.py:466
  (64 shorter events, 0.4 us)
Async XLA Ops:
  0.0 10.2 %copy-start.13 = (s32[8]{0:T(128)S(1)}, s32[8]{0:T(128)}, u32[]{:S(2)}) copy-start(s32[8]{0:T(128)} %constant.25.clone) | copy-start | bytes 100
  0.0 11.4 %copy-start.12 = (s32[8]{0:T(128)S(1)}, s32[8]{0:T(128)}, u32[]{:S(2)}) copy-start(s32[8]{0:T(128)} %constant.24.clone) | copy-start | bytes 100
  0.0 16.0 %copy-start.9 = (f32[512]{0:T(512)S(1)}, f32[512]{0:T(512)}, u32[]{:S(2)}) copy-start(f32[512]{0:T(512)} %param.11) | copy-start | bytes 6148
  0.0 12.7 %collective-permute-start = (bf16[3,64,512]{2,1,0:T(8,128)(2,1)}, bf16[3,64,512]{2,1,0:T(8,128)(2,1)S(1)}, u32[]{:S(2)}, u32[]{:S(2)}) collective-permute-start(bf16[3,64,512]{2,1,0:T(8,128)(2,1)} %refs_0_.1), channel_id=1, source_target_pairs={{0,2},{1,3},{2,0},{3,1},{4,6},{5,7},{6,4},{7,5},{8,10},{9,11},{10,... | collective-permute-start | bytes 589832 | tf_op jit(solution)/shard_map/ppermute | solution.py:351
  3.0 12.8 %collective-permute-start.1 = (bf16[3,64,512]{2,1,0:T(8,128)(2,1)}, bf16[3,64,512]{2,1,0:T(8,128)(2,1)S(1)}, u32[]{:S(2)}, u32[]{:S(2)}) collective-permute-start(bf16[3,64,512]{2,1,0:T(8,128)(2,1)} %refs_0_.1), channel_id=1, source_target_pairs={{0,4},{1,5},{2,6},{3,7},{4,0},{5,1},{6,2},{7,3},{8,12},{9,13},{10,... | collective-permute-start | bytes 589832 | tf_op jit(solution)/shard_map/ppermute | solution.py:351
  4.5 11.2 %collective-permute-start.2 = (bf16[3,64,512]{2,1,0:T(8,128)(2,1)}, bf16[3,64,512]{2,1,0:T(8,128)(2,1)S(1)}, u32[]{:S(2)}, u32[]{:S(2)}) collective-permute-start(bf16[3,64,512]{2,1,0:T(8,128)(2,1)} %refs_0_.1), channel_id=1, source_target_pairs={{0,6},{1,7},{2,4},{3,5},{4,2},{5,3},{6,0},{7,1},{8,14},{9,15},{10,... | collective-permute-start | bytes 589832 | tf_op jit(solution)/shard_map/ppermute | solution.py:351
  4.6 23.7 %copy-start.2 = (s32[2]{0:T(128)}, s32[2]{0:T(128)S(1)}, u32[]{:S(2)}) copy-start(s32[2]{0:T(128)S(1)} %pad_add_fusion.place.source) | copy-start | bytes 28
  4.6 1.6 %copy-start = (f32[2,1,512,512]{3,2,1,0:T(8,128)S(1)}, f32[2,1,512,512]{3,2,1,0:T(8,128)}, u32[]{:S(2)}) copy-start(f32[2,1,512,512]{3,2,1,0:T(8,128)} %param.7) | copy-start | bytes 6291460
  6.2 9.6 %copy-start.1 = (bf16[3,64,512]{2,1,0:T(8,128)(2,1)S(1)}, bf16[3,64,512]{2,1,0:T(8,128)(2,1)}, u32[]{:S(2)}) copy-start(bf16[3,64,512]{2,1,0:T(8,128)(2,1)} %refs_0_.1) | copy-start | bytes 589828
  7.1 9.2 %collective-permute-start.10 = (bf16[2,128,256]{2,1,0:T(8,128)(2,1)S(1)}, bf16[2,128,256]{2,1,0:T(8,128)(2,1)S(1)}, u32[]{:S(2)}, u32[]{:S(2)}) collective-permute-start(bf16[2,128,256]{2,1,0:T(8,128)(2,1)S(1)} %get-tuple-element.62), channel_id=1, source_target_pairs={{0,7},{1,6},{2,5},{3,4},{4,3},{5,2},{6,1},{7,0},{8,15},{9,14},{10,... | collective-permute-start | bytes 393224 | tf_op jit(solution)/shard_map/ppermute | solution.py:318
  8.7 10.1 %collective-permute-start.4 = (bf16[2,128,256]{2,1,0:T(8,128)(2,1)S(1)}, bf16[2,128,256]{2,1,0:T(8,128)(2,1)S(1)}, u32[]{:S(2)}, u32[]{:S(2)}) collective-permute-start(bf16[2,128,256]{2,1,0:T(8,128)(2,1)S(1)} %get-tuple-element.56), channel_id=1, source_target_pairs={{0,1},{1,0},{2,3},{3,2},{4,5},{5,4},{6,7},{7,6},{8,9},{9,8},{10,11... | collective-permute-start | bytes 393224 | tf_op jit(solution)/shard_map/ppermute | solution.py:318
  12.7 15.3 %collective-permute-start.5 = (bf16[2,128,256]{2,1,0:T(8,128)(2,1)S(1)}, bf16[2,128,256]{2,1,0:T(8,128)(2,1)S(1)}, u32[]{:S(2)}, u32[]{:S(2)}) collective-permute-start(bf16[2,128,256]{2,1,0:T(8,128)(2,1)S(1)} %get-tuple-element.57), channel_id=1, source_target_pairs={{0,2},{1,3},{2,0},{3,1},{4,6},{5,7},{6,4},{7,5},{8,10},{9,11},{10,... | collective-permute-start | bytes 393224 | tf_op jit(solution)/shard_map/ppermute | solution.py:318
  15.8 12.2 %collective-permute-start.6 = (bf16[2,128,256]{2,1,0:T(8,128)(2,1)S(1)}, bf16[2,128,256]{2,1,0:T(8,128)(2,1)S(1)}, u32[]{:S(2)}, u32[]{:S(2)}) collective-permute-start(bf16[2,128,256]{2,1,0:T(8,128)(2,1)S(1)} %get-tuple-element.58), channel_id=1, source_target_pairs={{0,3},{1,2},{2,1},{3,0},{4,7},{5,6},{6,5},{7,4},{8,11},{9,10},{10,... | collective-permute-start | bytes 393224 | tf_op jit(solution)/shard_map/ppermute | solution.py:318
  15.9 3.0 %collective-permute-start.3 = (bf16[4,3,64,512]{3,2,1,0:T(8,128)(2,1)S(1)}, bf16[4,3,64,512]{3,2,1,0:T(8,128)(2,1)S(1)}, u32[]{:S(2)}, u32[]{:S(2)}) collective-permute-start(bf16[4,3,64,512]{3,2,1,0:T(8,128)(2,1)S(1)} %pad_maximum_fusion), channel_id=1, source_target_pairs={{0,1},{1,0},{2,3},{3,2},{4,5},{5,4},{6,7},{7,6},{8,9},{9,8},{10,11... | collective-permute-start | bytes 2359304 | tf_op jit(solution)/shard_map/ppermute | solution.py:351
  16.3 11.7 %collective-permute-start.7 = (bf16[2,128,256]{2,1,0:T(8,128)(2,1)S(1)}, bf16[2,128,256]{2,1,0:T(8,128)(2,1)S(1)}, u32[]{:S(2)}, u32[]{:S(2)}) collective-permute-start(bf16[2,128,256]{2,1,0:T(8,128)(2,1)S(1)} %get-tuple-element.59), channel_id=1, source_target_pairs={{0,4},{1,5},{2,6},{3,7},{4,0},{5,1},{6,2},{7,3},{8,12},{9,13},{10,... | collective-permute-start | bytes 393224 | tf_op jit(solution)/shard_map/ppermute | solution.py:318
  18.8 9.6 %collective-permute-start.8 = (bf16[2,128,256]{2,1,0:T(8,128)(2,1)S(1)}, bf16[2,128,256]{2,1,0:T(8,128)(2,1)S(1)}, u32[]{:S(2)}, u32[]{:S(2)}) collective-permute-start(bf16[2,128,256]{2,1,0:T(8,128)(2,1)S(1)} %get-tuple-element.60), channel_id=1, source_target_pairs={{0,5},{1,4},{2,7},{3,6},{4,1},{5,0},{6,3},{7,2},{8,13},{9,12},{10,... | collective-permute-start | bytes 393224 | tf_op jit(solution)/shard_map/ppermute | solution.py:318
  18.9 14.6 %copy-start.11 = (bf16[8,8]{1,0:T(8,128)(2,1)S(1)}, bf16[8,8]{1,0:T(8,128)(2,1)}, u32[]{:S(2)}) copy-start(bf16[8,8]{1,0:T(8,128)(2,1)} %param.9) | copy-start | bytes 388
  18.9 9.4 %collective-permute-start.9 = (bf16[2,128,256]{2,1,0:T(8,128)(2,1)S(1)}, bf16[2,128,256]{2,1,0:T(8,128)(2,1)S(1)}, u32[]{:S(2)}, u32[]{:S(2)}) collective-permute-start(bf16[2,128,256]{2,1,0:T(8,128)(2,1)S(1)} %get-tuple-element.61), channel_id=1, source_target_pairs={{0,6},{1,7},{2,4},{3,5},{4,2},{5,3},{6,0},{7,1},{8,14},{9,15},{10,... | collective-permute-start | bytes 393224 | tf_op jit(solution)/shard_map/ppermute | solution.py:318
  29.0 12.4 %collective-permute-start.11 = (bf16[2,2,64,256]{3,2,1,0:T(8,128)(2,1)S(1)}, bf16[2,2,64,256]{3,2,1,0:T(8,128)(2,1)S(1)}, u32[]{:S(2)}, u32[]{:S(2)}) collective-permute-start(bf16[2,2,64,256]{3,2,1,0:T(8,128)(2,1)S(1)} %get-tuple-element.64), channel_id=1, source_target_pairs={{0,8},{8,0},{16,24},{24,16},{1,9},{9,1},{17,25},{25,17},{2,10},{10... | collective-permute-start | bytes 393224 | tf_op jit(solution)/shard_map/ppermute | solution.py:325
  30.6 12.9 %collective-permute-start.12 = (bf16[2,2,64,256]{3,2,1,0:T(8,128)(2,1)S(1)}, bf16[2,2,64,256]{3,2,1,0:T(8,128)(2,1)S(1)}, u32[]{:S(2)}, u32[]{:S(2)}) collective-permute-start(bf16[2,2,64,256]{3,2,1,0:T(8,128)(2,1)S(1)} %get-tuple-element.65), channel_id=1, source_target_pairs={{0,16},{8,24},{16,0},{24,8},{1,17},{9,25},{17,1},{25,9},{2,18},{10... | collective-permute-start | bytes 393224 | tf_op jit(solution)/shard_map/ppermute | solution.py:325
  33.2 10.4 %collective-permute-start.13 = (bf16[2,2,64,256]{3,2,1,0:T(8,128)(2,1)S(1)}, bf16[2,2,64,256]{3,2,1,0:T(8,128)(2,1)S(1)}, u32[]{:S(2)}, u32[]{:S(2)}) collective-permute-start(bf16[2,2,64,256]{3,2,1,0:T(8,128)(2,1)S(1)} %get-tuple-element.66), channel_id=1, source_target_pairs={{0,24},{8,16},{16,8},{24,0},{1,25},{9,17},{17,9},{25,1},{2,26},{10... | collective-permute-start | bytes 393224 | tf_op jit(solution)/shard_map/ppermute | solution.py:325
  33.6 18.9 %all-to-all-start = ((bf16[8,2,128,256]{3,2,1,0:T(8,128)(2,1)}), bf16[8,2,128,256]{3,2,1,0:T(8,128)(2,1)S(1)}, u32[]{:S(2)}, u32[]{:S(2)}) async-start(bf16[8,2,128,256]{3,2,1,0:T(8,128)(2,1)} %get-tuple-element.54), calls=%async_computation | async-start | bytes 2097152 | tf_op jit(solution)/shard_map/all_to_all | solution.py:312
  37.2 21.7 %collective-permute-start.17 = (bf16[2,2,64,256]{3,2,1,0:T(8,128)(2,1)S(1)}, bf16[2,2,64,256]{3,2,1,0:T(8,128)(2,1)S(1)}, u32[]{:S(2)}, u32[]{:S(2)}) collective-permute-start(bf16[2,2,64,256]{3,2,1,0:T(8,128)(2,1)S(1)} %get-tuple-element.74), channel_id=1, source_target_pairs={{0,8},{8,0},{16,24},{24,16},{1,9},{9,1},{17,25},{25,17},{2,10},{10... | collective-permute-start | bytes 393224 | tf_op jit(solution)/shard_map/ppermute | solution.py:325
  37.9 21.2 %collective-permute-start.18 = (bf16[2,2,64,256]{3,2,1,0:T(8,128)(2,1)S(1)}, bf16[2,2,64,256]{3,2,1,0:T(8,128)(2,1)S(1)}, u32[]{:S(2)}, u32[]{:S(2)}) collective-permute-start(bf16[2,2,64,256]{3,2,1,0:T(8,128)(2,1)S(1)} %get-tuple-element.75), channel_id=1, source_target_pairs={{0,16},{8,24},{16,0},{24,8},{1,17},{9,25},{17,1},{25,9},{2,18},{10... | collective-permute-start | bytes 393224 | tf_op jit(solution)/shard_map/ppermute | solution.py:325
  41.4 17.7 %collective-permute-start.19 = (bf16[2,2,64,256]{3,2,1,0:T(8,128)(2,1)S(1)}, bf16[2,2,64,256]{3,2,1,0:T(8,128)(2,1)S(1)}, u32[]{:S(2)}, u32[]{:S(2)}) collective-permute-start(bf16[2,2,64,256]{3,2,1,0:T(8,128)(2,1)S(1)} %get-tuple-element.76), channel_id=1, source_target_pairs={{0,24},{8,16},{16,8},{24,0},{1,25},{9,17},{17,9},{25,1},{2,26},{10... | collective-permute-start | bytes 393224 | tf_op jit(solution)/shard_map/ppermute | solution.py:325
  44.8 14.3 %copy-start.3 = (s32[2]{0:T(128)S(1)}, s32[2]{0:T(128)}, u32[]{:S(2)}) copy-start(s32[2]{0:T(128)} %copy-done.2) | copy-start | bytes 28
  52.5 0.6 copy-start.8
  54.7 10.3 %collective-permute-start.14 = (bf16[2,2,64,256]{3,2,1,0:T(8,128)(2,1)S(1)}, bf16[2,2,64,256]{3,2,1,0:T(8,128)(2,1)S(1)}, u32[]{:S(2)}, u32[]{:S(2)}) collective-permute-start(bf16[2,2,64,256]{3,2,1,0:T(8,128)(2,1)S(1)} %get-tuple-element.69.refs_1_), channel_id=1, source_target_pairs={{0,8},{8,0},{16,24},{24,16},{1,9},{9,1},{17,25},{25,17},{2,10},{10... | collective-permute-start | bytes 393224 | tf_op jit(solution)/shard_map/ppermute | solution.py:325
  56.0 12.8 %collective-permute-start.15 = (bf16[2,2,64,256]{3,2,1,0:T(8,128)(2,1)S(1)}, bf16[2,2,64,256]{3,2,1,0:T(8,128)(2,1)S(1)}, u32[]{:S(2)}, u32[]{:S(2)}) collective-permute-start(bf16[2,2,64,256]{3,2,1,0:T(8,128)(2,1)S(1)} %get-tuple-element.70.refs_2_), channel_id=1, source_target_pairs={{0,16},{8,24},{16,0},{24,8},{1,17},{9,25},{17,1},{25,9},{2,18},{10... | collective-permute-start | bytes 393224 | tf_op jit(solution)/shard_map/ppermute | solution.py:325
  58.9 10.0 %collective-permute-start.16 = (bf16[2,2,64,256]{3,2,1,0:T(8,128)(2,1)S(1)}, bf16[2,2,64,256]{3,2,1,0:T(8,128)(2,1)S(1)}, u32[]{:S(2)}, u32[]{:S(2)}) collective-permute-start(bf16[2,2,64,256]{3,2,1,0:T(8,128)(2,1)S(1)} %get-tuple-element.71.refs_3_), channel_id=1, source_target_pairs={{0,24},{8,16},{16,8},{24,0},{1,25},{9,17},{17,9},{25,1},{2,26},{10... | collective-permute-start | bytes 393224 | tf_op jit(solution)/shard_map/ppermute | solution.py:325
  59.1 9.7 %copy-start.5 = (f32[8]{0:T(128)S(1)}, f32[8]{0:T(128)}, u32[]{:S(2)}) copy-start(f32[8]{0:T(128)} %occ.9) | copy-start | bytes 100
  60.7 18.8 %collective-permute-start.20 = (bf16[2,2,64,256]{3,2,1,0:T(8,128)(2,1)S(1)}, bf16[2,2,64,256]{3,2,1,0:T(8,128)(2,1)S(1)}, u32[]{:S(2)}, u32[]{:S(2)}) collective-permute-start(bf16[2,2,64,256]{3,2,1,0:T(8,128)(2,1)S(1)} %get-tuple-element.78.refs_2_), channel_id=1, source_target_pairs={{0,8},{8,0},{16,24},{24,16},{1,9},{9,1},{17,25},{25,17},{2,10},{10... | collective-permute-start | bytes 393224 | tf_op jit(solution)/shard_map/ppermute | solution.py:325
  61.2 19.9 %collective-permute-start.21 = (bf16[2,2,64,256]{3,2,1,0:T(8,128)(2,1)S(1)}, bf16[2,2,64,256]{3,2,1,0:T(8,128)(2,1)S(1)}, u32[]{:S(2)}, u32[]{:S(2)}) collective-permute-start(bf16[2,2,64,256]{3,2,1,0:T(8,128)(2,1)S(1)} %get-tuple-element.79.refs_3_), channel_id=1, source_target_pairs={{0,16},{8,24},{16,0},{24,8},{1,17},{9,25},{17,1},{25,9},{2,18},{10... | collective-permute-start | bytes 393224 | tf_op jit(solution)/shard_map/ppermute | solution.py:325
  65.0 16.1 %collective-permute-start.22 = (bf16[2,2,64,256]{3,2,1,0:T(8,128)(2,1)S(1)}, bf16[2,2,64,256]{3,2,1,0:T(8,128)(2,1)S(1)}, u32[]{:S(2)}, u32[]{:S(2)}) collective-permute-start(bf16[2,2,64,256]{3,2,1,0:T(8,128)(2,1)S(1)} %get-tuple-element.80.refs_4_), channel_id=1, source_target_pairs={{0,24},{8,16},{16,8},{24,0},{1,25},{9,17},{17,9},{25,1},{2,26},{10... | collective-permute-start | bytes 393224 | tf_op jit(solution)/shard_map/ppermute | solution.py:325
  71.4 13.3 %copy-start.6 = (bf16[2,8,64,256]{3,2,1,0:T(8,128)(2,1)}, bf16[2,8,64,256]{3,2,1,0:T(8,128)(2,1)S(1)}, u32[]{:S(2)}) copy-start(bf16[2,8,64,256]{3,2,1,0:T(8,128)(2,1)S(1)} %get-tuple-element.87.rest) | copy-start | bytes 1572868
  71.4 24.5 %collective-permute-start.26 = (bf16[2,2,64,256]{3,2,1,0:T(8,128)(2,1)S(1)}, bf16[2,2,64,256]{3,2,1,0:T(8,128)(2,1)S(1)}, u32[]{:S(2)}, u32[]{:S(2)}) collective-permute-start(bf16[2,2,64,256]{3,2,1,0:T(8,128)(2,1)S(1)} %get-tuple-element.88), channel_id=1, source_target_pairs={{0,8},{8,0},{16,24},{24,16},{1,9},{9,1},{17,25},{25,17},{2,10},{10... | collective-permute-start | bytes 393224 | tf_op jit(solution)/shard_map/ppermute | solution.py:325
  78.6 18.8 %collective-permute-start.27 = (bf16[2,2,64,256]{3,2,1,0:T(8,128)(2,1)S(1)}, bf16[2,2,64,256]{3,2,1,0:T(8,128)(2,1)S(1)}, u32[]{:S(2)}, u32[]{:S(2)}) collective-permute-start(bf16[2,2,64,256]{3,2,1,0:T(8,128)(2,1)S(1)} %get-tuple-element.89), channel_id=1, source_target_pairs={{0,16},{8,24},{16,0},{24,8},{1,17},{9,25},{17,1},{25,9},{2,18},{10... | collective-permute-start | bytes 393224 | tf_op jit(solution)/shard_map/ppermute | solution.py:325
  79.5 17.9 %collective-permute-start.28 = (bf16[2,2,64,256]{3,2,1,0:T(8,128)(2,1)S(1)}, bf16[2,2,64,256]{3,2,1,0:T(8,128)(2,1)S(1)}, u32[]{:S(2)}, u32[]{:S(2)}) collective-permute-start(bf16[2,2,64,256]{3,2,1,0:T(8,128)(2,1)S(1)} %get-tuple-element.90), channel_id=1, source_target_pairs={{0,24},{8,16},{16,8},{24,0},{1,25},{9,17},{17,9},{25,1},{2,26},{10... | collective-permute-start | bytes 393224 | tf_op jit(solution)/shard_map/ppermute | solution.py:325
  84.7 12.7 %copy-start.7 = (bf16[2,8,64,256]{3,2,1,0:T(8,128)(2,1)S(1)}, bf16[2,8,64,256]{3,2,1,0:T(8,128)(2,1)}, u32[]{:S(2)}) copy-start(bf16[2,8,64,256]{3,2,1,0:T(8,128)(2,1)} %copy-done.6) | copy-start | bytes 1572868
  84.7 13.8 %collective-permute-start.23 = (bf16[2,2,64,256]{3,2,1,0:T(8,128)(2,1)S(1)}, bf16[2,2,64,256]{3,2,1,0:T(8,128)(2,1)S(1)}, u32[]{:S(2)}, u32[]{:S(2)}) collective-permute-start(bf16[2,2,64,256]{3,2,1,0:T(8,128)(2,1)S(1)} %get-tuple-element.84), channel_id=1, source_target_pairs={{0,8},{8,0},{16,24},{24,16},{1,9},{9,1},{17,25},{25,17},{2,10},{10... | collective-permute-start | bytes 393224 | tf_op jit(solution)/shard_map/ppermute | solution.py:325
  89.6 8.9 %collective-permute-start.24 = (bf16[2,2,64,256]{3,2,1,0:T(8,128)(2,1)S(1)}, bf16[2,2,64,256]{3,2,1,0:T(8,128)(2,1)S(1)}, u32[]{:S(2)}, u32[]{:S(2)}) collective-permute-start(bf16[2,2,64,256]{3,2,1,0:T(8,128)(2,1)S(1)} %get-tuple-element.85), channel_id=1, source_target_pairs={{0,16},{8,24},{16,0},{24,8},{1,17},{9,25},{17,1},{25,9},{2,18},{10... | collective-permute-start | bytes 393224 | tf_op jit(solution)/shard_map/ppermute | solution.py:325
  91.7 22.3 %all-to-all-start.1 = ((bf16[8,2,128,256]{3,2,1,0:T(8,128)(2,1)}), bf16[8,2,128,256]{3,2,1,0:T(8,128)(2,1)}, u32[]{:S(2)}, u32[]{:S(2)}) async-start(bf16[8,2,128,256]{3,2,1,0:T(8,128)(2,1)} %get-tuple-element.81), calls=%async_computation.1 | async-start | bytes 2097152 | tf_op jit(solution)/shard_map/all_to_all | solution.py:312
  95.9 7.7 %collective-permute-start.25 = (bf16[2,2,64,256]{3,2,1,0:T(8,128)(2,1)S(1)}, bf16[2,2,64,256]{3,2,1,0:T(8,128)(2,1)S(1)}, u32[]{:S(2)}, u32[]{:S(2)}) collective-permute-start(bf16[2,2,64,256]{3,2,1,0:T(8,128)(2,1)S(1)} %get-tuple-element.86), channel_id=1, source_target_pairs={{0,24},{8,16},{16,8},{24,0},{1,25},{9,17},{17,9},{25,1},{2,26},{10... | collective-permute-start | bytes 393224 | tf_op jit(solution)/shard_map/ppermute | solution.py:325
  103.6 10.3 %copy-start.10 = (f32[512]{0:T(512)S(1)}, f32[512]{0:T(512)}, u32[]{:S(2)}) copy-start(f32[512]{0:T(512)} %param.11) | copy-start | bytes 6148
  104.8 4.2 %collective-permute-start.29 = (bf16[2,128,256]{2,1,0:T(8,128)(2,1)S(1)}, bf16[2,128,256]{2,1,0:T(8,128)(2,1)S(1)}, u32[]{:S(2)}, u32[]{:S(2)}) collective-permute-start(bf16[2,128,256]{2,1,0:T(8,128)(2,1)S(1)} %get-tuple-element.92), channel_id=1, source_target_pairs={{0,1},{1,0},{2,3},{3,2},{4,5},{5,4},{6,7},{7,6},{8,9},{9,8},{10,11... | collective-permute-start | bytes 393224 | tf_op jit(solution)/shard_map/ppermute | solution.py:318
  104.9 8.7 %collective-permute-start.30 = (bf16[2,128,256]{2,1,0:T(8,128)(2,1)S(1)}, bf16[2,128,256]{2,1,0:T(8,128)(2,1)S(1)}, u32[]{:S(2)}, u32[]{:S(2)}) collective-permute-start(bf16[2,128,256]{2,1,0:T(8,128)(2,1)S(1)} %get-tuple-element.93), channel_id=1, source_target_pairs={{0,2},{1,3},{2,0},{3,1},{4,6},{5,7},{6,4},{7,5},{8,10},{9,11},{10,... | collective-permute-start | bytes 393224 | tf_op jit(solution)/shard_map/ppermute | solution.py:318
  106.6 17.8 %collective-permute-start.31 = (bf16[2,128,256]{2,1,0:T(8,128)(2,1)S(1)}, bf16[2,128,256]{2,1,0:T(8,128)(2,1)S(1)}, u32[]{:S(2)}, u32[]{:S(2)}) collective-permute-start(bf16[2,128,256]{2,1,0:T(8,128)(2,1)S(1)} %get-tuple-element.94), channel_id=1, source_target_pairs={{0,3},{1,2},{2,1},{3,0},{4,7},{5,6},{6,5},{7,4},{8,11},{9,10},{10,... | collective-permute-start | bytes 393224 | tf_op jit(solution)/shard_map/ppermute | solution.py:318
  106.7 17.7 %collective-permute-start.32 = (bf16[2,128,256]{2,1,0:T(8,128)(2,1)S(1)}, bf16[2,128,256]{2,1,0:T(8,128)(2,1)S(1)}, u32[]{:S(2)}, u32[]{:S(2)}) collective-permute-start(bf16[2,128,256]{2,1,0:T(8,128)(2,1)S(1)} %get-tuple-element.95), channel_id=1, source_target_pairs={{0,4},{1,5},{2,6},{3,7},{4,0},{5,1},{6,2},{7,3},{8,12},{9,13},{10,... | collective-permute-start | bytes 393224 | tf_op jit(solution)/shard_map/ppermute | solution.py:318
  109.0 15.5 %collective-permute-start.33 = (bf16[2,128,256]{2,1,0:T(8,128)(2,1)S(1)}, bf16[2,128,256]{2,1,0:T(8,128)(2,1)S(1)}, u32[]{:S(2)}, u32[]{:S(2)}) collective-permute-start(bf16[2,128,256]{2,1,0:T(8,128)(2,1)S(1)} %get-tuple-element.96), channel_id=1, source_target_pairs={{0,5},{1,4},{2,7},{3,6},{4,1},{5,0},{6,3},{7,2},{8,13},{9,12},{10,... | collective-permute-start | bytes 393224 | tf_op jit(solution)/shard_map/ppermute | solution.py:318
  109.0 15.5 %collective-permute-start.34 = (bf16[2,128,256]{2,1,0:T(8,128)(2,1)S(1)}, bf16[2,128,256]{2,1,0:T(8,128)(2,1)S(1)}, u32[]{:S(2)}, u32[]{:S(2)}) collective-permute-start(bf16[2,128,256]{2,1,0:T(8,128)(2,1)S(1)} %get-tuple-element.97), channel_id=1, source_target_pairs={{0,6},{1,7},{2,4},{3,5},{4,2},{5,3},{6,0},{7,1},{8,14},{9,15},{10,... | collective-permute-start | bytes 393224 | tf_op jit(solution)/shard_map/ppermute | solution.py:318
  113.6 10.9 %collective-permute-start.35 = (bf16[2,128,256]{2,1,0:T(8,128)(2,1)S(1)}, bf16[2,128,256]{2,1,0:T(8,128)(2,1)S(1)}, u32[]{:S(2)}, u32[]{:S(2)}) collective-permute-start(bf16[2,128,256]{2,1,0:T(8,128)(2,1)S(1)} %get-tuple-element.98), channel_id=1, source_target_pairs={{0,7},{1,6},{2,5},{3,4},{4,3},{5,2},{6,1},{7,0},{8,15},{9,14},{10,... | collective-permute-start | bytes 393224 | tf_op jit(solution)/shard_map/ppermute | solution.py:318
  114.8 9.7 %copy-start.4 = (s32[2]{0:T(128)S(1)}, s32[2]{0:T(128)}, u32[]{:S(2)}) copy-start(s32[2]{0:T(128)} %copy-done.2) | copy-start | bytes 28

commit v18 on v14

--- a/solution.py
+++ b/solution.py
@@ -383,7 +383,6 @@
                    place, current, specs=[SMEM, VMEM])
     pieces, order = gather_vectors(vectors, devices, started[0])
     held = by_distance(started)
-    sums = virtual_sums(tiles, vir_energy, q)
 
     ladder_flops = first * singles * 4 * virtual**3
     ladder, whole = call(
@@ -396,6 +395,7 @@
         tie(place, ladder), *held, specs=[SMEM] + [VMEM] * devices,
     )
     mirror = [across_first(parts[c * groups:(c + 1) * groups], groups) for c in chunks]
+    sums = virtual_sums(tiles, vir_energy, tie(q, mirror[0][-1]))
     ladder = exchange(ladder)
 
     half, other = [], []

time: 127 us -> 130 us (1.024)
  waiting for transfers between devices: 19.2 us -> 26.8 us
  starting transfers between devices: 66.5 us -> 61.7 us
    ppermute x14, waiting for transfers between devices: 2.11 us -> 6.4 us  [by_distance(): lax.ppermute(parts[k], 'occj', [(d, d ^ k) for d in range(devices)])]
    ppermute x4, waiting for transfers between devices: 2.49 us -> 6.73 us  [turn(): return lax.ppermute(x, 'occj', [(d, d ^ k) for d in range(devices)])]
    all_to_all x2, starting transfers between devices: 10.2 us -> 7.38 us  [exchange(): lax.all_to_all(blocks, 'occj', split_axis=0, concat_axis=0, tiled=True)]
    all_to_all x2, waiting for transfers between devices: 7.72 us -> 5.54 us  [exchange(): lax.all_to_all(blocks, 'occj', split_axis=0, concat_axis=0, tiled=True)]
    ppermute x14, starting transfers between devices: 16.4 us -> 14.5 us  [by_distance(): lax.ppermute(parts[k], 'occj', [(d, d ^ k) for d in range(devices)])]
    ppermute x18, waiting for transfers between devices: 6.86 us -> 8.17 us  [across_first(): lax.ppermute(parts[s], 'occi', [(k, k ^ s) for k in range(groups)])]
  transfers between devices with their start and end apart: 38 -> 38, of which waited for: 7 -> 9; matrix products, arithmetic and copies ran while one was open for 2% -> 1% of each run, Pallas kernels for 22% -> 22%
where the time goes in v18:
time: 130 us; the launch traced here: 129 us
  starting transfers between devices  61.7 us (47%)
  Pallas kernels  31.2 us (24%)
  waiting for transfers between devices  26.8 us (21%)
  local copies, waits for them, and re-layouts  7.04 us (5%)
  between operations  1.52 us (1%)
    ppermute x18, starting transfers between devices, across_first(): lax.ppermute(parts[s], 'occi', [(k, k ^ s) for k in range(groups)])  35.3 us
    pallas_call x9, Pallas kernels, call(): pl.pallas_call(body, out_shape=outs, in_specs=specs, out_specs=jax.tree.m...  19.3 us
    ppermute x14, starting transfers between devices, by_distance(): lax.ppermute(parts[k], 'occj', [(d, d ^ k) for d in range(devices)])  14.5 us
    ppermute x18, waiting for transfers between devices, across_first(): lax.ppermute(parts[s], 'occi', [(k, k ^ s) for k in range(groups)])  8.17 us
    pallas_call x1, Pallas kernels, local(): pl.pallas_call(functools.partial(second_ladder_kernel, tiles, first), gri...  7.78 us
    all_to_all x2, starting transfers between devices, exchange(): lax.all_to_all(blocks, 'occj', split_axis=0, concat_axis=0, tiled=True)  7.38 us
    ppermute x4, waiting for transfers between devices, turn(): return lax.ppermute(x, 'occj', [(d, d ^ k) for d in range(devices)])  6.73 us
    ppermute x14, waiting for transfers between devices, by_distance(): lax.ppermute(parts[k], 'occj', [(d, d ^ k) for d in range(devices)])  6.4 us
  transfers between devices with their start and end apart: 38, of which 9 were waited for; matrix products, arithmetic and copies ran while one was open for 1% of the time, Pallas kernels for 22%

profile of v18, /device:TPU:0, one launch (start us, length us, event | category | flops | bytes accessed | tf_op | source)
XLA Modules:
  0.0 128.7 jit_solution(1509054082524897765)
XLA Ops:
  0.0 2.9 %collective-permute-start = (bf16[3,64,512]{2,1,0:T(8,128)(2,1)}, bf16[3,64,512]{2,1,0:T(8,128)(2,1)S(1)}, u32[]{:S(2)}, u32[]{:S(2)}) collective-permute-start(bf16[3,64,512]{2,1,0:T(8,128)(2,1)} %refs_0_.1), channel_id=1, source_target_pairs={{0,2},{1,3},{2,0},{3,1},{4,6},{5,7},{6,4},{7,5},{8,10},{9,11},{10,... | collective-permute-start | bytes 589832 | tf_op jit(solution)/shard_map/ppermute | solution.py:338
  2.9 1.5 %collective-permute-start.1 = (bf16[3,64,512]{2,1,0:T(8,128)(2,1)}, bf16[3,64,512]{2,1,0:T(8,128)(2,1)S(1)}, u32[]{:S(2)}, u32[]{:S(2)}) collective-permute-start(bf16[3,64,512]{2,1,0:T(8,128)(2,1)} %refs_0_.1), channel_id=1, source_target_pairs={{0,4},{1,5},{2,6},{3,7},{4,0},{5,1},{6,2},{7,3},{8,12},{9,13},{10,... | collective-permute-start | bytes 589832 | tf_op jit(solution)/shard_map/ppermute | solution.py:338
  4.5 1.6 %copy-done = f32[2,1,512,512]{3,2,1,0:T(8,128)S(1)} copy-done((f32[2,1,512,512]{3,2,1,0:T(8,128)S(1)}, f32[2,1,512,512]{3,2,1,0:T(8,128)}, u32[]{:S(2)}) %copy-start) | copy-done | bytes 2097176
  6.1 0.9 shard_map.73
  7.0 1.9 %collective-permute-done.refs_1_ = bf16[3,64,512]{2,1,0:T(8,128)(2,1)S(1)} collective-permute-done((bf16[3,64,512]{2,1,0:T(8,128)(2,1)}, bf16[3,64,512]{2,1,0:T(8,128)(2,1)S(1)}, u32[]{:S(2)}, u32[]{:S(2)}) %collective-permute-start) | collective-permute-done | bytes 196640 | tf_op jit(solution)/shard_map/ppermute | solution.py:338
  8.9 4.8 %collective-permute-done.1.refs_2_ = bf16[3,64,512]{2,1,0:T(8,128)(2,1)S(1)} collective-permute-done((bf16[3,64,512]{2,1,0:T(8,128)(2,1)}, bf16[3,64,512]{2,1,0:T(8,128)(2,1)S(1)}, u32[]{:S(2)}, u32[]{:S(2)}) %collective-permute-start.1) | collective-permute-done | bytes 196640 | tf_op jit(solution)/shard_map/ppermute | solution.py:338
  13.7 0.1 pad_maximum_fusion
  13.9 1.6 %collective-permute-start.10 = (bf16[2,128,256]{2,1,0:T(8,128)(2,1)S(1)}, bf16[2,128,256]{2,1,0:T(8,128)(2,1)S(1)}, u32[]{:S(2)}, u32[]{:S(2)}) collective-permute-start(bf16[2,128,256]{2,1,0:T(8,128)(2,1)S(1)} %get-tuple-element.63), channel_id=1, source_target_pairs={{0,7},{1,6},{2,5},{3,4},{4,3},{5,2},{6,1},{7,0},{8,15},{9,14},{10,... | collective-permute-start | bytes 393224 | tf_op jit(solution)/shard_map/ppermute | solution.py:305
  15.6 1.5 %collective-permute-start.5 = (bf16[2,128,256]{2,1,0:T(8,128)(2,1)S(1)}, bf16[2,128,256]{2,1,0:T(8,128)(2,1)S(1)}, u32[]{:S(2)}, u32[]{:S(2)}) collective-permute-start(bf16[2,128,256]{2,1,0:T(8,128)(2,1)S(1)} %get-tuple-element.58), channel_id=1, source_target_pairs={{0,2},{1,3},{2,0},{3,1},{4,6},{5,7},{6,4},{7,5},{8,10},{9,11},{10,... | collective-permute-start | bytes 393224 | tf_op jit(solution)/shard_map/ppermute | solution.py:305
  17.1 0.3 collective-permute-start.6
  17.4 2.7 %collective-permute-done.10.refs_7_ = bf16[2,128,256]{2,1,0:T(8,128)(2,1)S(1)} collective-permute-done((bf16[2,128,256]{2,1,0:T(8,128)(2,1)S(1)}, bf16[2,128,256]{2,1,0:T(8,128)(2,1)S(1)}, u32[]{:S(2)}, u32[]{:S(2)}) %collective-permute-start.10) | collective-permute-done | bytes 131104 | tf_op jit(solution)/shard_map/ppermute | solution.py:305
  20.1 1.5 %collective-permute-start.7 = (bf16[2,128,256]{2,1,0:T(8,128)(2,1)S(1)}, bf16[2,128,256]{2,1,0:T(8,128)(2,1)S(1)}, u32[]{:S(2)}, u32[]{:S(2)}) collective-permute-start(bf16[2,128,256]{2,1,0:T(8,128)(2,1)S(1)} %get-tuple-element.60), channel_id=1, source_target_pairs={{0,4},{1,5},{2,6},{3,7},{4,0},{5,1},{6,2},{7,3},{8,12},{9,13},{10,... | collective-permute-start | bytes 393224 | tf_op jit(solution)/shard_map/ppermute | solution.py:305
  21.6 0.8 collective-permute-start.8
  22.4 1.5 %collective-permute-start.9 = (bf16[2,128,256]{2,1,0:T(8,128)(2,1)S(1)}, bf16[2,128,256]{2,1,0:T(8,128)(2,1)S(1)}, u32[]{:S(2)}, u32[]{:S(2)}) collective-permute-start(bf16[2,128,256]{2,1,0:T(8,128)(2,1)S(1)} %get-tuple-element.62), channel_id=1, source_target_pairs={{0,6},{1,7},{2,4},{3,5},{4,2},{5,3},{6,0},{7,1},{8,14},{9,15},{10,... | collective-permute-start | bytes 393224 | tf_op jit(solution)/shard_map/ppermute | solution.py:305
  23.9 6.3 %shard_map.74 = (bf16[8,2,128,256]{3,2,1,0:T(8,128)(2,1)}, bf16[512,1536]{1,0:T(8,128)(2,1)}) custom-call(s32[2]{0:T(128)S(1)} %pad_add_fusion.place.source, f32[2,512,512]{2,1,0:T(8,128)} %bitcast.13, bf16[3,64,512]{2,1,0:T(8,128)(2,1)S(1)} %copy-done.1, bf16[3,64,512]{2,1,0:T(8,128)(2,1)S(1)} %collective-permute-done.refs_1_, ...), custom_call_target="tpu_custom_call" | custom-call | flops 3221225472 | bytes 4194304 | tf_op jit(solution)/shard_map/pallas_call | solution.py:42
  30.2 1.9 %collective-permute-done.8.refs_5_ = bf16[2,128,256]{2,1,0:T(8,128)(2,1)S(1)} collective-permute-done((bf16[2,128,256]{2,1,0:T(8,128)(2,1)S(1)}, bf16[2,128,256]{2,1,0:T(8,128)(2,1)S(1)}, u32[]{:S(2)}, u32[]{:S(2)}) %collective-permute-start.8) | collective-permute-done | bytes 131104 | tf_op jit(solution)/shard_map/ppermute | solution.py:305
  32.1 0.7 shard_map.75
  32.8 3.7 %collective-permute-start.11 = (bf16[2,2,64,256]{3,2,1,0:T(8,128)(2,1)S(1)}, bf16[2,2,64,256]{3,2,1,0:T(8,128)(2,1)S(1)}, u32[]{:S(2)}, u32[]{:S(2)}) collective-permute-start(bf16[2,2,64,256]{3,2,1,0:T(8,128)(2,1)S(1)} %get-tuple-element.64), channel_id=1, source_target_pairs={{0,24},{8,16},{16,8},{24,0},{1,25},{9,17},{17,9},{25,1},{2,26},{10... | collective-permute-start | bytes 393224 | tf_op jit(solution)/shard_map/ppermute | solution.py:312
  36.4 0.8 collective-permute-start.13
  37.2 3.6 %all-to-all-start = ((bf16[8,2,128,256]{3,2,1,0:T(8,128)(2,1)}), bf16[8,2,128,256]{3,2,1,0:T(8,128)(2,1)S(1)}, u32[]{:S(2)}, u32[]{:S(2)}) async-start(bf16[8,2,128,256]{3,2,1,0:T(8,128)(2,1)} %get-tuple-element.55), calls=%async_computation | async-start | bytes 2097152 | tf_op jit(solution)/shard_map/all_to_all | solution.py:299
  40.8 1.3 %collective-permute-start.17 = (bf16[2,2,64,256]{3,2,1,0:T(8,128)(2,1)S(1)}, bf16[2,2,64,256]{3,2,1,0:T(8,128)(2,1)S(1)}, u32[]{:S(2)}, u32[]{:S(2)}) collective-permute-start(bf16[2,2,64,256]{3,2,1,0:T(8,128)(2,1)S(1)} %get-tuple-element.76), channel_id=1, source_target_pairs={{0,8},{8,0},{16,24},{24,16},{1,9},{9,1},{17,25},{25,17},{2,10},{10... | collective-permute-start | bytes 393224 | tf_op jit(solution)/shard_map/ppermute | solution.py:312
  42.1 2.9 %collective-permute-start.18 = (bf16[2,2,64,256]{3,2,1,0:T(8,128)(2,1)S(1)}, bf16[2,2,64,256]{3,2,1,0:T(8,128)(2,1)S(1)}, u32[]{:S(2)}, u32[]{:S(2)}) collective-permute-start(bf16[2,2,64,256]{3,2,1,0:T(8,128)(2,1)S(1)} %get-tuple-element.77), channel_id=1, source_target_pairs={{0,16},{8,24},{16,0},{24,8},{1,17},{9,25},{17,1},{25,9},{2,18},{10... | collective-permute-start | bytes 393224 | tf_op jit(solution)/shard_map/ppermute | solution.py:312
  45.0 0.2 collective-permute-start.19
  45.2 0.6 dynamic_slice.14
  46.4 0.6 dynamic_slice.12
  47.7 1.1 collective-permute-done.13.refs_2_
  48.8 1.3 %shard_map.76.place = s32[2]{0:T(128)} custom-call(s32[2]{0:T(128)} %copy-done.4), custom_call_target="tpu_custom_call" | custom-call | flops 30000001024 | bytes 8 | tf_op jit(solution)/shard_map/pallas_call | solution.py:327
  50.1 0.1 fusion
  50.4 0.1 broadcast_add_fusion.2
  50.6 5.5 %all-to-all-done.ladder = bf16[8,2,128,256]{3,2,1,0:T(8,128)(2,1)S(1)} async-done(((bf16[8,2,128,256]{3,2,1,0:T(8,128)(2,1)}), bf16[8,2,128,256]{3,2,1,0:T(8,128)(2,1)S(1)}, u32[]{:S(2)}, u32[]{:S(2)}) %all-to-all-start) | async-done | bytes 1048608 | tf_op jit(solution)/shard_map/all_to_all | solution.py:299
  56.1 0.7 copy-done.10
  56.8 1.6 %shard_map.77 = (bf16[2,2,64,256]{3,2,1,0:T(8,128)(2,1)S(1)}, bf16[2,2,64,256]{3,2,1,0:T(8,128)(2,1)S(1)}, bf16[2,2,64,256]{3,2,1,0:T(8,128)(2,1)S(1)}, bf16[2,2,64,256]{3,2,1,0:T(8,128)(2,1)S(1)}) custom-call(s32[2]{0:T(128)S(1)} %copy-done.10, f32[8,8]{1,0:T(8,128)S(1)} %convert_element_type.3.fock, bf16[8,2,128,256]{3,2,1,0:T(8,128)(2,1)S(1)} %all-to-all-done.ladder, ...), custom_call_target="tpu_custom_call" | custom-call | flops 30000001024 | bytes 3145728 | tf_op jit(solution)/shard_map/pallas_call | solution.py:42
  58.3 1.3 %collective-permute-start.14 = (bf16[2,2,64,256]{3,2,1,0:T(8,128)(2,1)S(1)}, bf16[2,2,64,256]{3,2,1,0:T(8,128)(2,1)S(1)}, u32[]{:S(2)}, u32[]{:S(2)}) collective-permute-start(bf16[2,2,64,256]{3,2,1,0:T(8,128)(2,1)S(1)} %get-tuple-element.71.refs_1_), channel_id=1, source_target_pairs={{0,8},{8,0},{16,24},{24,16},{1,9},{9,1},{17,25},{25,17},{2,10},{10... | collective-permute-start | bytes 393224 | tf_op jit(solution)/shard_map/ppermute | solution.py:312
  59.7 2.9 %collective-permute-start.15 = (bf16[2,2,64,256]{3,2,1,0:T(8,128)(2,1)S(1)}, bf16[2,2,64,256]{3,2,1,0:T(8,128)(2,1)S(1)}, u32[]{:S(2)}, u32[]{:S(2)}) collective-permute-start(bf16[2,2,64,256]{3,2,1,0:T(8,128)(2,1)S(1)} %get-tuple-element.72.refs_2_), channel_id=1, source_target_pairs={{0,16},{8,24},{16,0},{24,8},{1,17},{9,25},{17,1},{25,9},{2,18},{10... | collective-permute-start | bytes 393224 | tf_op jit(solution)/shard_map/ppermute | solution.py:312
  62.6 0.2 collective-permute-start.16
  62.8 1.6 %shard_map.79 = (bf16[2,2,64,256]{3,2,1,0:T(8,128)(2,1)S(1)}, bf16[2,2,64,256]{3,2,1,0:T(8,128)(2,1)S(1)}, bf16[2,2,64,256]{3,2,1,0:T(8,128)(2,1)S(1)}, bf16[2,2,64,256]{3,2,1,0:T(8,128)(2,1)S(1)}) custom-call(s32[2]{0:T(128)S(1)} %copy-done.5, f32[8,8]{1,0:T(8,128)S(1)} %convert_element_type.3.fock, bf16[8,2,128,256]{3,2,1,0:T(8,128)(2,1)S(1)} %all-to-all-done.ladder, ...), custom_call_target="tpu_custom_call" | custom-call | flops 30000001024 | bytes 3145728 | tf_op jit(solution)/shard_map/pallas_call | solution.py:42
  64.4 0.4 collective-permute-start.20
  64.8 3.8 %collective-permute-start.21 = (bf16[2,2,64,256]{3,2,1,0:T(8,128)(2,1)S(1)}, bf16[2,2,64,256]{3,2,1,0:T(8,128)(2,1)S(1)}, u32[]{:S(2)}, u32[]{:S(2)}) collective-permute-start(bf16[2,2,64,256]{3,2,1,0:T(8,128)(2,1)S(1)} %get-tuple-element.81.refs_3_), channel_id=1, source_target_pairs={{0,16},{8,24},{16,0},{24,8},{1,17},{9,25},{17,1},{25,9},{2,18},{10... | collective-permute-start | bytes 393224 | tf_op jit(solution)/shard_map/ppermute | solution.py:312
  68.7 1.2 collective-permute-start.22
  69.9 2.9 %collective-permute-done.15.refs_6_ = bf16[2,2,64,256]{3,2,1,0:T(8,128)(2,1)S(1)} collective-permute-done((bf16[2,2,64,256]{3,2,1,0:T(8,128)(2,1)S(1)}, bf16[2,2,64,256]{3,2,1,0:T(8,128)(2,1)S(1)}, u32[]{:S(2)}, u32[]{:S(2)}) %collective-permute-start.15) | collective-permute-done | bytes 131104 | tf_op jit(solution)/shard_map/ppermute | solution.py:312
  72.7 2.5 %shard_map.78 = (bf16[8,2,64,256]{3,2,1,0:T(8,128)(2,1)S(1)}, bf16[2,8,64,256]{3,2,1,0:T(8,128)(2,1)S(1)}, bf16[2,2,64,256]{3,2,1,0:T(8,128)(2,1)S(1)}, bf16[2,2...) custom-call(s32[2]{0:T(128)S(1)} %copy-done.5, f32[8,8]{1,0:T(8,128)S(1)} %convert_element_type.3.fock, ...), custom_call_target="tpu_custom_call" | custom-call | flops 30000001024 | bytes 5242880 | tf_op jit(solution)/shard_map/pallas_call | solution.py:42
  75.3 0.8 copy-done.8
  76.1 9.8 %collective-permute-start.26 = (bf16[2,2,64,256]{3,2,1,0:T(8,128)(2,1)S(1)}, bf16[2,2,64,256]{3,2,1,0:T(8,128)(2,1)S(1)}, u32[]{:S(2)}, u32[]{:S(2)}) collective-permute-start(bf16[2,2,64,256]{3,2,1,0:T(8,128)(2,1)S(1)} %get-tuple-element.90), channel_id=1, source_target_pairs={{0,8},{8,0},{16,24},{24,16},{1,9},{9,1},{17,25},{25,17},{2,10},{10... | collective-permute-start | bytes 393224 | tf_op jit(solution)/shard_map/ppermute | solution.py:312
  85.9 0.7 collective-permute-start.27
  86.6 1.7 %collective-permute-start.28 = (bf16[2,2,64,256]{3,2,1,0:T(8,128)(2,1)S(1)}, bf16[2,2,64,256]{3,2,1,0:T(8,128)(2,1)S(1)}, u32[]{:S(2)}, u32[]{:S(2)}) collective-permute-start(bf16[2,2,64,256]{3,2,1,0:T(8,128)(2,1)S(1)} %get-tuple-element.92), channel_id=1, source_target_pairs={{0,24},{8,16},{16,8},{24,0},{1,25},{9,17},{17,9},{25,1},{2,26},{10... | collective-permute-start | bytes 393224 | tf_op jit(solution)/shard_map/ppermute | solution.py:312
  88.3 3.6 %shard_map.80 = (bf16[8,2,128,256]{3,2,1,0:T(8,128)(2,1)}, bf16[2,8,64,256]{3,2,1,0:T(8,128)(2,1)S(1)}, bf16[2,2,64,256]{3,2,1,0:T(8,128)(2,1)S(1)}, bf16[2,2,64...) custom-call(s32[2]{0:T(128)S(1)} %copy-done.5, f32[8,8]{1,0:T(8,128)S(1)} %convert_element_type.3.fock, ...), custom_call_target="tpu_custom_call" | custom-call | flops 30000001024 | bytes 5242880 | tf_op jit(solution)/shard_map/pallas_call | solution.py:42
  91.9 1.1 collective-permute-start.23
  93.0 1.6 %collective-permute-start.24 = (bf16[2,2,64,256]{3,2,1,0:T(8,128)(2,1)S(1)}, bf16[2,2,64,256]{3,2,1,0:T(8,128)(2,1)S(1)}, u32[]{:S(2)}, u32[]{:S(2)}) collective-permute-start(bf16[2,2,64,256]{3,2,1,0:T(8,128)(2,1)S(1)} %get-tuple-element.87), channel_id=1, source_target_pairs={{0,16},{8,24},{16,0},{24,8},{1,17},{9,25},{17,1},{25,9},{2,18},{10... | collective-permute-start | bytes 393224 | tf_op jit(solution)/shard_map/ppermute | solution.py:312
  94.6 3.8 %all-to-all-start.1 = ((bf16[8,2,128,256]{3,2,1,0:T(8,128)(2,1)}), bf16[8,2,128,256]{3,2,1,0:T(8,128)(2,1)S(1)}, u32[]{:S(2)}, u32[]{:S(2)}) async-start(bf16[8,2,128,256]{3,2,1,0:T(8,128)(2,1)} %get-tuple-element.83), calls=%async_computation.1 | async-start | bytes 2097152 | tf_op jit(solution)/shard_map/all_to_all | solution.py:299
  98.5 1.5 %collective-permute-start.25 = (bf16[2,2,64,256]{3,2,1,0:T(8,128)(2,1)S(1)}, bf16[2,2,64,256]{3,2,1,0:T(8,128)(2,1)S(1)}, u32[]{:S(2)}, u32[]{:S(2)}) collective-permute-start(bf16[2,2,64,256]{3,2,1,0:T(8,128)(2,1)S(1)} %get-tuple-element.88), channel_id=1, source_target_pairs={{0,24},{8,16},{16,8},{24,0},{1,25},{9,17},{17,9},{25,1},{2,26},{10... | collective-permute-start | bytes 393224 | tf_op jit(solution)/shard_map/ppermute | solution.py:312
  100.0 1.0 copy-done.9
  101.0 1.1 shard_map.82.refs_3_
  102.1 4.1 %collective-permute-done.25.refs_2_ = bf16[2,2,64,256]{3,2,1,0:T(8,128)(2,1)S(1)} collective-permute-done((bf16[2,2,64,256]{3,2,1,0:T(8,128)(2,1)S(1)}, bf16[2,2,64,256]{3,2,1,0:T(8,128)(2,1)S(1)}, u32[]{:S(2)}, u32[]{:S(2)}) %collective-permute-start.25) | collective-permute-done | bytes 131104 | tf_op jit(solution)/shard_map/ppermute | solution.py:312
  106.3 1.2 shard_map.83
  107.5 1.7 %collective-permute-start.30 = (bf16[2,128,256]{2,1,0:T(8,128)(2,1)S(1)}, bf16[2,128,256]{2,1,0:T(8,128)(2,1)S(1)}, u32[]{:S(2)}, u32[]{:S(2)}) collective-permute-start(bf16[2,128,256]{2,1,0:T(8,128)(2,1)S(1)} %get-tuple-element.95), channel_id=1, source_target_pairs={{0,2},{1,3},{2,0},{3,1},{4,6},{5,7},{6,4},{7,5},{8,10},{9,11},{10,... | collective-permute-start | bytes 393224 | tf_op jit(solution)/shard_map/ppermute | solution.py:305
  109.2 0.1 collective-permute-start.31
  109.4 2.2 %collective-permute-start.32 = (bf16[2,128,256]{2,1,0:T(8,128)(2,1)S(1)}, bf16[2,128,256]{2,1,0:T(8,128)(2,1)S(1)}, u32[]{:S(2)}, u32[]{:S(2)}) collective-permute-start(bf16[2,128,256]{2,1,0:T(8,128)(2,1)S(1)} %get-tuple-element.97), channel_id=1, source_target_pairs={{0,4},{1,5},{2,6},{3,7},{4,0},{5,1},{6,2},{7,3},{8,12},{9,13},{10,... | collective-permute-start | bytes 393224 | tf_op jit(solution)/shard_map/ppermute | solution.py:305
  111.6 2.9 %collective-permute-start.34 = (bf16[2,128,256]{2,1,0:T(8,128)(2,1)S(1)}, bf16[2,128,256]{2,1,0:T(8,128)(2,1)S(1)}, u32[]{:S(2)}, u32[]{:S(2)}) collective-permute-start(bf16[2,128,256]{2,1,0:T(8,128)(2,1)S(1)} %get-tuple-element.99), channel_id=1, source_target_pairs={{0,6},{1,7},{2,4},{3,5},{4,2},{5,3},{6,0},{7,1},{8,14},{9,15},{10,... | collective-permute-start | bytes 393224 | tf_op jit(solution)/shard_map/ppermute | solution.py:305
  114.4 1.8 %collective-permute-done.30.refs_2_ = bf16[2,128,256]{2,1,0:T(8,128)(2,1)S(1)} collective-permute-done((bf16[2,128,256]{2,1,0:T(8,128)(2,1)S(1)}, bf16[2,128,256]{2,1,0:T(8,128)(2,1)S(1)}, u32[]{:S(2)}, u32[]{:S(2)}) %collective-permute-start.30) | collective-permute-done | bytes 131104 | tf_op jit(solution)/shard_map/ppermute | solution.py:305
  116.2 0.3 collective-permute-start.35
  116.5 0.1 broadcast_in_dim.4.row
  116.7 1.4 %copy-done.7 = bf16[512,1536]{1,0:T(8,128)(2,1)S(1)} copy-done((bf16[512,1536]{1,0:T(8,128)(2,1)S(1)}, bf16[512,1536]{1,0:T(8,128)(2,1)}, u32[]{:S(2)}) %copy-start.7) | copy-done | bytes 1572888
  118.1 7.8 %shard_map.81.source = f32[2,512,512]{2,1,0:T(8,128)} custom-call(s32[2]{0:T(128)S(1)} %copy-done.5, f32[8]{0:T(128)S(1)} %copy-done.6, f32[2,512,512]{2,1,0:T(8,128)} %bitcast.14, bf16[8,2,128,256]{3,2,1,0:T(8,128)(2,1)S(1)} %all-to-all-done.1.blocks, f32[512,128]{1,0:T(8,128)S(1)} %broadcast_in_dim.4.row, f32[1,512]{1,0:T(1,128)S(1)} %bitcast.20, ...), custom_call_target="tpu_custom_call" | custom-call | flops 3221225472 | bytes 6291456 | tf_op jit(solution)/shard_map/pallas_call | solution.py:427
  125.9 2.8 %shard_map.84 = f32[2,512,512]{2,1,0:T(8,128)} custom-call(s32[2]{0:T(128)S(1)} %copy-done.5, f32[2,512,512]{2,1,0:T(8,128)} %shard_map.81.source, bf16[2,128,256]{2,1,0:T(8,128)(2,1)S(1)} %get-tuple-element.93.refs_0_, bf16[2,128,256]{2,1,0:T(8,128)(2,1)S(1)} %collective-permute-done.29.refs_1_, ...), custom_call_target="tpu_custom_call", output_to_operand_aliasing={{}: (1, {})} | custom-call | flops 524288 | bytes 5242880 | tf_op jit(solution)/shard_map/pallas_call | solution.py:450
  (64 shorter events, 0.7 us)
Async XLA Ops:
  0.0 8.9 %collective-permute-start = (bf16[3,64,512]{2,1,0:T(8,128)(2,1)}, bf16[3,64,512]{2,1,0:T(8,128)(2,1)S(1)}, u32[]{:S(2)}, u32[]{:S(2)}) collective-permute-start(bf16[3,64,512]{2,1,0:T(8,128)(2,1)} %refs_0_.1), channel_id=1, source_target_pairs={{0,2},{1,3},{2,0},{3,1},{4,6},{5,7},{6,4},{7,5},{8,10},{9,11},{10,... | collective-permute-start | bytes 589832 | tf_op jit(solution)/shard_map/ppermute | solution.py:338
  2.9 10.8 %collective-permute-start.1 = (bf16[3,64,512]{2,1,0:T(8,128)(2,1)}, bf16[3,64,512]{2,1,0:T(8,128)(2,1)S(1)}, u32[]{:S(2)}, u32[]{:S(2)}) collective-permute-start(bf16[3,64,512]{2,1,0:T(8,128)(2,1)} %refs_0_.1), channel_id=1, source_target_pairs={{0,4},{1,5},{2,6},{3,7},{4,0},{5,1},{6,2},{7,3},{8,12},{9,13},{10,... | collective-permute-start | bytes 589832 | tf_op jit(solution)/shard_map/ppermute | solution.py:338
  4.5 9.3 %collective-permute-start.2 = (bf16[3,64,512]{2,1,0:T(8,128)(2,1)}, bf16[3,64,512]{2,1,0:T(8,128)(2,1)S(1)}, u32[]{:S(2)}, u32[]{:S(2)}) collective-permute-start(bf16[3,64,512]{2,1,0:T(8,128)(2,1)} %refs_0_.1), channel_id=1, source_target_pairs={{0,6},{1,7},{2,4},{3,5},{4,2},{5,3},{6,0},{7,1},{8,14},{9,15},{10,... | collective-permute-start | bytes 589832 | tf_op jit(solution)/shard_map/ppermute | solution.py:338
  4.5 27.5 %copy-start.4 = (s32[2]{0:T(128)}, s32[2]{0:T(128)S(1)}, u32[]{:S(2)}) copy-start(s32[2]{0:T(128)S(1)} %pad_add_fusion.place.source) | copy-start | bytes 28
  4.5 1.6 %copy-start = (f32[2,1,512,512]{3,2,1,0:T(8,128)S(1)}, f32[2,1,512,512]{3,2,1,0:T(8,128)}, u32[]{:S(2)}) copy-start(f32[2,1,512,512]{3,2,1,0:T(8,128)} %param.7) | copy-start | bytes 6291460
  6.1 7.6 %copy-start.1 = (bf16[3,64,512]{2,1,0:T(8,128)(2,1)S(1)}, bf16[3,64,512]{2,1,0:T(8,128)(2,1)}, u32[]{:S(2)}) copy-start(bf16[3,64,512]{2,1,0:T(8,128)(2,1)} %refs_0_.1) | copy-start | bytes 589828
  13.8 8.6 %collective-permute-start.3 = (bf16[4,3,64,512]{3,2,1,0:T(8,128)(2,1)S(1)}, bf16[4,3,64,512]{3,2,1,0:T(8,128)(2,1)S(1)}, u32[]{:S(2)}, u32[]{:S(2)}) collective-permute-start(bf16[4,3,64,512]{3,2,1,0:T(8,128)(2,1)S(1)} %pad_maximum_fusion), channel_id=1, source_target_pairs={{0,1},{1,0},{2,3},{3,2},{4,5},{5,4},{6,7},{7,6},{8,9},{9,8},{10,11... | collective-permute-start | bytes 2359304 | tf_op jit(solution)/shard_map/ppermute | solution.py:338
  13.9 6.2 %collective-permute-start.10 = (bf16[2,128,256]{2,1,0:T(8,128)(2,1)S(1)}, bf16[2,128,256]{2,1,0:T(8,128)(2,1)S(1)}, u32[]{:S(2)}, u32[]{:S(2)}) collective-permute-start(bf16[2,128,256]{2,1,0:T(8,128)(2,1)S(1)} %get-tuple-element.63), channel_id=1, source_target_pairs={{0,7},{1,6},{2,5},{3,4},{4,3},{5,2},{6,1},{7,0},{8,15},{9,14},{10,... | collective-permute-start | bytes 393224 | tf_op jit(solution)/shard_map/ppermute | solution.py:305
  15.5 6.1 %collective-permute-start.4 = (bf16[2,128,256]{2,1,0:T(8,128)(2,1)S(1)}, bf16[2,128,256]{2,1,0:T(8,128)(2,1)S(1)}, u32[]{:S(2)}, u32[]{:S(2)}) collective-permute-start(bf16[2,128,256]{2,1,0:T(8,128)(2,1)S(1)} %get-tuple-element.57), channel_id=1, source_target_pairs={{0,1},{1,0},{2,3},{3,2},{4,5},{5,4},{6,7},{7,6},{8,9},{9,8},{10,11... | collective-permute-start | bytes 393224 | tf_op jit(solution)/shard_map/ppermute | solution.py:305
  15.6 14.6 %collective-permute-start.5 = (bf16[2,128,256]{2,1,0:T(8,128)(2,1)S(1)}, bf16[2,128,256]{2,1,0:T(8,128)(2,1)S(1)}, u32[]{:S(2)}, u32[]{:S(2)}) collective-permute-start(bf16[2,128,256]{2,1,0:T(8,128)(2,1)S(1)} %get-tuple-element.58), channel_id=1, source_target_pairs={{0,2},{1,3},{2,0},{3,1},{4,6},{5,7},{6,4},{7,5},{8,10},{9,11},{10,... | collective-permute-start | bytes 393224 | tf_op jit(solution)/shard_map/ppermute | solution.py:305
  17.1 13.1 %collective-permute-start.6 = (bf16[2,128,256]{2,1,0:T(8,128)(2,1)S(1)}, bf16[2,128,256]{2,1,0:T(8,128)(2,1)S(1)}, u32[]{:S(2)}, u32[]{:S(2)}) collective-permute-start(bf16[2,128,256]{2,1,0:T(8,128)(2,1)S(1)} %get-tuple-element.59), channel_id=1, source_target_pairs={{0,3},{1,2},{2,1},{3,0},{4,7},{5,6},{6,5},{7,4},{8,11},{9,10},{10,... | collective-permute-start | bytes 393224 | tf_op jit(solution)/shard_map/ppermute | solution.py:305
  20.1 10.1 %collective-permute-start.7 = (bf16[2,128,256]{2,1,0:T(8,128)(2,1)S(1)}, bf16[2,128,256]{2,1,0:T(8,128)(2,1)S(1)}, u32[]{:S(2)}, u32[]{:S(2)}) collective-permute-start(bf16[2,128,256]{2,1,0:T(8,128)(2,1)S(1)} %get-tuple-element.60), channel_id=1, source_target_pairs={{0,4},{1,5},{2,6},{3,7},{4,0},{5,1},{6,2},{7,3},{8,12},{9,13},{10,... | collective-permute-start | bytes 393224 | tf_op jit(solution)/shard_map/ppermute | solution.py:305
  21.6 10.4 %collective-permute-start.8 = (bf16[2,128,256]{2,1,0:T(8,128)(2,1)S(1)}, bf16[2,128,256]{2,1,0:T(8,128)(2,1)S(1)}, u32[]{:S(2)}, u32[]{:S(2)}) collective-permute-start(bf16[2,128,256]{2,1,0:T(8,128)(2,1)S(1)} %get-tuple-element.61), channel_id=1, source_target_pairs={{0,5},{1,4},{2,7},{3,6},{4,1},{5,0},{6,3},{7,2},{8,13},{9,12},{10,... | collective-permute-start | bytes 393224 | tf_op jit(solution)/shard_map/ppermute | solution.py:305
  22.4 14.8 %copy-start.11 = (bf16[8,8]{1,0:T(8,128)(2,1)S(1)}, bf16[8,8]{1,0:T(8,128)(2,1)}, u32[]{:S(2)}) copy-start(bf16[8,8]{1,0:T(8,128)(2,1)} %param.9) | copy-start | bytes 388
  22.4 9.6 %collective-permute-start.9 = (bf16[2,128,256]{2,1,0:T(8,128)(2,1)S(1)}, bf16[2,128,256]{2,1,0:T(8,128)(2,1)S(1)}, u32[]{:S(2)}, u32[]{:S(2)}) collective-permute-start(bf16[2,128,256]{2,1,0:T(8,128)(2,1)S(1)} %get-tuple-element.62), channel_id=1, source_target_pairs={{0,6},{1,7},{2,4},{3,5},{4,2},{5,3},{6,0},{7,1},{8,14},{9,15},{10,... | collective-permute-start | bytes 393224 | tf_op jit(solution)/shard_map/ppermute | solution.py:305
  30.2 15.1 %copy-start.13 = (s32[8]{0:T(128)S(1)}, s32[8]{0:T(128)}, u32[]{:S(2)}) copy-start(s32[8]{0:T(128)} %constant.25.clone) | copy-start | bytes 100
  30.2 16.2 %copy-start.12 = (s32[8]{0:T(128)S(1)}, s32[8]{0:T(128)}, u32[]{:S(2)}) copy-start(s32[8]{0:T(128)} %constant.24.clone) | copy-start | bytes 100
  32.8 12.3 %collective-permute-start.11 = (bf16[2,2,64,256]{3,2,1,0:T(8,128)(2,1)S(1)}, bf16[2,2,64,256]{3,2,1,0:T(8,128)(2,1)S(1)}, u32[]{:S(2)}, u32[]{:S(2)}) collective-permute-start(bf16[2,2,64,256]{3,2,1,0:T(8,128)(2,1)S(1)} %get-tuple-element.64), channel_id=1, source_target_pairs={{0,24},{8,16},{16,8},{24,0},{1,25},{9,17},{17,9},{25,1},{2,26},{10... | collective-permute-start | bytes 393224 | tf_op jit(solution)/shard_map/ppermute | solution.py:312
  36.4 11.2 %collective-permute-start.12 = (bf16[2,2,64,256]{3,2,1,0:T(8,128)(2,1)S(1)}, bf16[2,2,64,256]{3,2,1,0:T(8,128)(2,1)S(1)}, u32[]{:S(2)}, u32[]{:S(2)}) collective-permute-start(bf16[2,2,64,256]{3,2,1,0:T(8,128)(2,1)S(1)} %get-tuple-element.67), channel_id=1, source_target_pairs={{0,8},{8,0},{16,24},{24,16},{1,9},{9,1},{17,25},{25,17},{2,10},{10... | collective-permute-start | bytes 393224 | tf_op jit(solution)/shard_map/ppermute | solution.py:312
  36.4 12.3 %collective-permute-start.13 = (bf16[2,2,64,256]{3,2,1,0:T(8,128)(2,1)S(1)}, bf16[2,2,64,256]{3,2,1,0:T(8,128)(2,1)S(1)}, u32[]{:S(2)}, u32[]{:S(2)}) collective-permute-start(bf16[2,2,64,256]{3,2,1,0:T(8,128)(2,1)S(1)} %get-tuple-element.68), channel_id=1, source_target_pairs={{0,16},{8,24},{16,0},{24,8},{1,17},{9,25},{17,1},{25,9},{2,18},{10... | collective-permute-start | bytes 393224 | tf_op jit(solution)/shard_map/ppermute | solution.py:312
  37.2 18.9 %all-to-all-start = ((bf16[8,2,128,256]{3,2,1,0:T(8,128)(2,1)}), bf16[8,2,128,256]{3,2,1,0:T(8,128)(2,1)S(1)}, u32[]{:S(2)}, u32[]{:S(2)}) async-start(bf16[8,2,128,256]{3,2,1,0:T(8,128)(2,1)} %get-tuple-element.55), calls=%async_computation | async-start | bytes 2097152 | tf_op jit(solution)/shard_map/all_to_all | solution.py:299
  40.8 21.8 %collective-permute-start.17 = (bf16[2,2,64,256]{3,2,1,0:T(8,128)(2,1)S(1)}, bf16[2,2,64,256]{3,2,1,0:T(8,128)(2,1)S(1)}, u32[]{:S(2)}, u32[]{:S(2)}) collective-permute-start(bf16[2,2,64,256]{3,2,1,0:T(8,128)(2,1)S(1)} %get-tuple-element.76), channel_id=1, source_target_pairs={{0,8},{8,0},{16,24},{24,16},{1,9},{9,1},{17,25},{25,17},{2,10},{10... | collective-permute-start | bytes 393224 | tf_op jit(solution)/shard_map/ppermute | solution.py:312
  42.1 20.7 %collective-permute-start.18 = (bf16[2,2,64,256]{3,2,1,0:T(8,128)(2,1)S(1)}, bf16[2,2,64,256]{3,2,1,0:T(8,128)(2,1)S(1)}, u32[]{:S(2)}, u32[]{:S(2)}) collective-permute-start(bf16[2,2,64,256]{3,2,1,0:T(8,128)(2,1)S(1)} %get-tuple-element.77), channel_id=1, source_target_pairs={{0,16},{8,24},{16,0},{24,8},{1,17},{9,25},{17,1},{25,9},{2,18},{10... | collective-permute-start | bytes 393224 | tf_op jit(solution)/shard_map/ppermute | solution.py:312
  45.0 17.8 %collective-permute-start.19 = (bf16[2,2,64,256]{3,2,1,0:T(8,128)(2,1)S(1)}, bf16[2,2,64,256]{3,2,1,0:T(8,128)(2,1)S(1)}, u32[]{:S(2)}, u32[]{:S(2)}) collective-permute-start(bf16[2,2,64,256]{3,2,1,0:T(8,128)(2,1)S(1)} %get-tuple-element.78), channel_id=1, source_target_pairs={{0,24},{8,16},{16,8},{24,0},{1,25},{9,17},{17,9},{25,1},{2,26},{10... | collective-permute-start | bytes 393224 | tf_op jit(solution)/shard_map/ppermute | solution.py:312
  48.8 1.3 %copy-start.2 = (f32[512]{0:T(512)S(1)}, f32[512]{0:T(512)}, u32[]{:S(2)}) copy-start(f32[512]{0:T(512)} %param.11) | copy-start | bytes 6148
  50.6 12.2 %copy-start.5 = (s32[2]{0:T(128)S(1)}, s32[2]{0:T(128)}, u32[]{:S(2)}) copy-start(s32[2]{0:T(128)} %copy-done.4) | copy-start | bytes 28
  56.1 0.7 copy-start.10
  58.3 10.3 %collective-permute-start.14 = (bf16[2,2,64,256]{3,2,1,0:T(8,128)(2,1)S(1)}, bf16[2,2,64,256]{3,2,1,0:T(8,128)(2,1)S(1)}, u32[]{:S(2)}, u32[]{:S(2)}) collective-permute-start(bf16[2,2,64,256]{3,2,1,0:T(8,128)(2,1)S(1)} %get-tuple-element.71.refs_1_), channel_id=1, source_target_pairs={{0,8},{8,0},{16,24},{24,16},{1,9},{9,1},{17,25},{25,17},{2,10},{10... | collective-permute-start | bytes 393224 | tf_op jit(solution)/shard_map/ppermute | solution.py:312
  59.7 13.1 %collective-permute-start.15 = (bf16[2,2,64,256]{3,2,1,0:T(8,128)(2,1)S(1)}, bf16[2,2,64,256]{3,2,1,0:T(8,128)(2,1)S(1)}, u32[]{:S(2)}, u32[]{:S(2)}) collective-permute-start(bf16[2,2,64,256]{3,2,1,0:T(8,128)(2,1)S(1)} %get-tuple-element.72.refs_2_), channel_id=1, source_target_pairs={{0,16},{8,24},{16,0},{24,8},{1,17},{9,25},{17,1},{25,9},{2,18},{10... | collective-permute-start | bytes 393224 | tf_op jit(solution)/shard_map/ppermute | solution.py:312
  62.6 10.2 %collective-permute-start.16 = (bf16[2,2,64,256]{3,2,1,0:T(8,128)(2,1)S(1)}, bf16[2,2,64,256]{3,2,1,0:T(8,128)(2,1)S(1)}, u32[]{:S(2)}, u32[]{:S(2)}) collective-permute-start(bf16[2,2,64,256]{3,2,1,0:T(8,128)(2,1)S(1)} %get-tuple-element.73.refs_3_), channel_id=1, source_target_pairs={{0,24},{8,16},{16,8},{24,0},{1,25},{9,17},{17,9},{25,1},{2,26},{10... | collective-permute-start | bytes 393224 | tf_op jit(solution)/shard_map/ppermute | solution.py:312
  62.8 9.9 %copy-start.6 = (f32[8]{0:T(128)S(1)}, f32[8]{0:T(128)}, u32[]{:S(2)}) copy-start(f32[8]{0:T(128)} %occ.9) | copy-start | bytes 100
  64.4 22.2 %collective-permute-start.20 = (bf16[2,2,64,256]{3,2,1,0:T(8,128)(2,1)S(1)}, bf16[2,2,64,256]{3,2,1,0:T(8,128)(2,1)S(1)}, u32[]{:S(2)}, u32[]{:S(2)}) collective-permute-start(bf16[2,2,64,256]{3,2,1,0:T(8,128)(2,1)S(1)} %get-tuple-element.80.refs_2_), channel_id=1, source_target_pairs={{0,8},{8,0},{16,24},{24,16},{1,9},{9,1},{17,25},{25,17},{2,10},{10... | collective-permute-start | bytes 393224 | tf_op jit(solution)/shard_map/ppermute | solution.py:312
  64.8 23.4 %collective-permute-start.21 = (bf16[2,2,64,256]{3,2,1,0:T(8,128)(2,1)S(1)}, bf16[2,2,64,256]{3,2,1,0:T(8,128)(2,1)S(1)}, u32[]{:S(2)}, u32[]{:S(2)}) collective-permute-start(bf16[2,2,64,256]{3,2,1,0:T(8,128)(2,1)S(1)} %get-tuple-element.81.refs_3_), channel_id=1, source_target_pairs={{0,16},{8,24},{16,0},{24,8},{1,17},{9,25},{17,1},{25,9},{2,18},{10... | collective-permute-start | bytes 393224 | tf_op jit(solution)/shard_map/ppermute | solution.py:312
  68.7 19.6 %collective-permute-start.22 = (bf16[2,2,64,256]{3,2,1,0:T(8,128)(2,1)S(1)}, bf16[2,2,64,256]{3,2,1,0:T(8,128)(2,1)S(1)}, u32[]{:S(2)}, u32[]{:S(2)}) collective-permute-start(bf16[2,2,64,256]{3,2,1,0:T(8,128)(2,1)S(1)} %get-tuple-element.82.refs_4_), channel_id=1, source_target_pairs={{0,24},{8,16},{16,8},{24,0},{1,25},{9,17},{17,9},{25,1},{2,26},{10... | collective-permute-start | bytes 393224 | tf_op jit(solution)/shard_map/ppermute | solution.py:312
  75.3 0.8 copy-start.8
  76.1 22.4 %collective-permute-start.26 = (bf16[2,2,64,256]{3,2,1,0:T(8,128)(2,1)S(1)}, bf16[2,2,64,256]{3,2,1,0:T(8,128)(2,1)S(1)}, u32[]{:S(2)}, u32[]{:S(2)}) collective-permute-start(bf16[2,2,64,256]{3,2,1,0:T(8,128)(2,1)S(1)} %get-tuple-element.90), channel_id=1, source_target_pairs={{0,8},{8,0},{16,24},{24,16},{1,9},{9,1},{17,25},{25,17},{2,10},{10... | collective-permute-start | bytes 393224 | tf_op jit(solution)/shard_map/ppermute | solution.py:312
  85.9 14.1 %collective-permute-start.27 = (bf16[2,2,64,256]{3,2,1,0:T(8,128)(2,1)S(1)}, bf16[2,2,64,256]{3,2,1,0:T(8,128)(2,1)S(1)}, u32[]{:S(2)}, u32[]{:S(2)}) collective-permute-start(bf16[2,2,64,256]{3,2,1,0:T(8,128)(2,1)S(1)} %get-tuple-element.91), channel_id=1, source_target_pairs={{0,16},{8,24},{16,0},{24,8},{1,17},{9,25},{17,1},{25,9},{2,18},{10... | collective-permute-start | bytes 393224 | tf_op jit(solution)/shard_map/ppermute | solution.py:312
  86.6 13.4 %collective-permute-start.28 = (bf16[2,2,64,256]{3,2,1,0:T(8,128)(2,1)S(1)}, bf16[2,2,64,256]{3,2,1,0:T(8,128)(2,1)S(1)}, u32[]{:S(2)}, u32[]{:S(2)}) collective-permute-start(bf16[2,2,64,256]{3,2,1,0:T(8,128)(2,1)S(1)} %get-tuple-element.92), channel_id=1, source_target_pairs={{0,24},{8,16},{16,8},{24,0},{1,25},{9,17},{17,9},{25,1},{2,26},{10... | collective-permute-start | bytes 393224 | tf_op jit(solution)/shard_map/ppermute | solution.py:312
  91.9 10.2 %collective-permute-start.23 = (bf16[2,2,64,256]{3,2,1,0:T(8,128)(2,1)S(1)}, bf16[2,2,64,256]{3,2,1,0:T(8,128)(2,1)S(1)}, u32[]{:S(2)}, u32[]{:S(2)}) collective-permute-start(bf16[2,2,64,256]{3,2,1,0:T(8,128)(2,1)S(1)} %get-tuple-element.86), channel_id=1, source_target_pairs={{0,8},{8,0},{16,24},{24,16},{1,9},{9,1},{17,25},{25,17},{2,10},{10... | collective-permute-start | bytes 393224 | tf_op jit(solution)/shard_map/ppermute | solution.py:312
  93.0 9.1 %collective-permute-start.24 = (bf16[2,2,64,256]{3,2,1,0:T(8,128)(2,1)S(1)}, bf16[2,2,64,256]{3,2,1,0:T(8,128)(2,1)S(1)}, u32[]{:S(2)}, u32[]{:S(2)}) collective-permute-start(bf16[2,2,64,256]{3,2,1,0:T(8,128)(2,1)S(1)} %get-tuple-element.87), channel_id=1, source_target_pairs={{0,16},{8,24},{16,0},{24,8},{1,17},{9,25},{17,1},{25,9},{2,18},{10... | collective-permute-start | bytes 393224 | tf_op jit(solution)/shard_map/ppermute | solution.py:312
  94.6 21.9 %all-to-all-start.1 = ((bf16[8,2,128,256]{3,2,1,0:T(8,128)(2,1)}), bf16[8,2,128,256]{3,2,1,0:T(8,128)(2,1)S(1)}, u32[]{:S(2)}, u32[]{:S(2)}) async-start(bf16[8,2,128,256]{3,2,1,0:T(8,128)(2,1)} %get-tuple-element.83), calls=%async_computation.1 | async-start | bytes 2097152 | tf_op jit(solution)/shard_map/all_to_all | solution.py:299
  98.5 7.8 %collective-permute-start.25 = (bf16[2,2,64,256]{3,2,1,0:T(8,128)(2,1)S(1)}, bf16[2,2,64,256]{3,2,1,0:T(8,128)(2,1)S(1)}, u32[]{:S(2)}, u32[]{:S(2)}) collective-permute-start(bf16[2,2,64,256]{3,2,1,0:T(8,128)(2,1)S(1)} %get-tuple-element.88), channel_id=1, source_target_pairs={{0,24},{8,16},{16,8},{24,0},{1,25},{9,17},{17,9},{25,1},{2,26},{10... | collective-permute-start | bytes 393224 | tf_op jit(solution)/shard_map/ppermute | solution.py:312
  100.0 1.0 copy-start.9
  106.3 10.3 %copy-start.3 = (f32[512]{0:T(512)S(1)}, f32[512]{0:T(512)}, u32[]{:S(2)}) copy-start(f32[512]{0:T(512)} %param.11) | copy-start | bytes 6148
  107.4 4.1 %collective-permute-start.29 = (bf16[2,128,256]{2,1,0:T(8,128)(2,1)S(1)}, bf16[2,128,256]{2,1,0:T(8,128)(2,1)S(1)}, u32[]{:S(2)}, u32[]{:S(2)}) collective-permute-start(bf16[2,128,256]{2,1,0:T(8,128)(2,1)S(1)} %get-tuple-element.94), channel_id=1, source_target_pairs={{0,1},{1,0},{2,3},{3,2},{4,5},{5,4},{6,7},{7,6},{8,9},{9,8},{10,11... | collective-permute-start | bytes 393224 | tf_op jit(solution)/shard_map/ppermute | solution.py:305
  107.5 8.7 %collective-permute-start.30 = (bf16[2,128,256]{2,1,0:T(8,128)(2,1)S(1)}, bf16[2,128,256]{2,1,0:T(8,128)(2,1)S(1)}, u32[]{:S(2)}, u32[]{:S(2)}) collective-permute-start(bf16[2,128,256]{2,1,0:T(8,128)(2,1)S(1)} %get-tuple-element.95), channel_id=1, source_target_pairs={{0,2},{1,3},{2,0},{3,1},{4,6},{5,7},{6,4},{7,5},{8,10},{9,11},{10,... | collective-permute-start | bytes 393224 | tf_op jit(solution)/shard_map/ppermute | solution.py:305
  109.2 16.6 %collective-permute-start.31 = (bf16[2,128,256]{2,1,0:T(8,128)(2,1)S(1)}, bf16[2,128,256]{2,1,0:T(8,128)(2,1)S(1)}, u32[]{:S(2)}, u32[]{:S(2)}) collective-permute-start(bf16[2,128,256]{2,1,0:T(8,128)(2,1)S(1)} %get-tuple-element.96), channel_id=1, source_target_pairs={{0,3},{1,2},{2,1},{3,0},{4,7},{5,6},{6,5},{7,4},{8,11},{9,10},{10,... | collective-permute-start | bytes 393224 | tf_op jit(solution)/shard_map/ppermute | solution.py:305
  109.4 16.5 %collective-permute-start.32 = (bf16[2,128,256]{2,1,0:T(8,128)(2,1)S(1)}, bf16[2,128,256]{2,1,0:T(8,128)(2,1)S(1)}, u32[]{:S(2)}, u32[]{:S(2)}) collective-permute-start(bf16[2,128,256]{2,1,0:T(8,128)(2,1)S(1)} %get-tuple-element.97), channel_id=1, source_target_pairs={{0,4},{1,5},{2,6},{3,7},{4,0},{5,1},{6,2},{7,3},{8,12},{9,13},{10,... | collective-permute-start | bytes 393224 | tf_op jit(solution)/shard_map/ppermute | solution.py:305
  111.6 14.3 %collective-permute-start.33 = (bf16[2,128,256]{2,1,0:T(8,128)(2,1)S(1)}, bf16[2,128,256]{2,1,0:T(8,128)(2,1)S(1)}, u32[]{:S(2)}, u32[]{:S(2)}) collective-permute-start(bf16[2,128,256]{2,1,0:T(8,128)(2,1)S(1)} %get-tuple-element.98), channel_id=1, source_target_pairs={{0,5},{1,4},{2,7},{3,6},{4,1},{5,0},{6,3},{7,2},{8,13},{9,12},{10,... | collective-permute-start | bytes 393224 | tf_op jit(solution)/shard_map/ppermute | solution.py:305
  111.6 14.3 %collective-permute-start.34 = (bf16[2,128,256]{2,1,0:T(8,128)(2,1)S(1)}, bf16[2,128,256]{2,1,0:T(8,128)(2,1)S(1)}, u32[]{:S(2)}, u32[]{:S(2)}) collective-permute-start(bf16[2,128,256]{2,1,0:T(8,128)(2,1)S(1)} %get-tuple-element.99), channel_id=1, source_target_pairs={{0,6},{1,7},{2,4},{3,5},{4,2},{5,3},{6,0},{7,1},{8,14},{9,15},{10,... | collective-permute-start | bytes 393224 | tf_op jit(solution)/shard_map/ppermute | solution.py:305
  116.2 9.6 %collective-permute-start.35 = (bf16[2,128,256]{2,1,0:T(8,128)(2,1)S(1)}, bf16[2,128,256]{2,1,0:T(8,128)(2,1)S(1)}, u32[]{:S(2)}, u32[]{:S(2)}) collective-permute-start(bf16[2,128,256]{2,1,0:T(8,128)(2,1)S(1)} %get-tuple-element.100), channel_id=1, source_target_pairs={{0,7},{1,6},{2,5},{3,4},{4,3},{5,2},{6,1},{7,0},{8,15},{9,14},{10,... | collective-permute-start | bytes 393224 | tf_op jit(solution)/shard_map/ppermute | solution.py:305
  116.7 1.4 %copy-start.7 = (bf16[512,1536]{1,0:T(8,128)(2,1)S(1)}, bf16[512,1536]{1,0:T(8,128)(2,1)}, u32[]{:S(2)}) copy-start(bf16[512,1536]{1,0:T(8,128)(2,1)} %get-tuple-element.84.whole) | copy-start | bytes 4718596

commit v19 on v18

--- a/solution.py
+++ b/solution.py
@@ -333,13 +333,13 @@
     )(tie(x, *others))
 
 
-def gather_vectors(vectors, devices, packed):
+def gather_vectors(vectors, devices, *earlier):
     def turn(x, k):
         return lax.ppermute(x, "occj", [(d, d ^ k) for d in range(devices)])
 
     even = list(range(0, devices, 2))
     held = [vectors] + [turn(vectors, k) for k in even[1:]]
-    other = turn(tie(jnp.stack(held), packed), 1)
+    other = turn(tie(jnp.stack(held), *earlier), 1)
     return [*held, other], even + [k ^ 1 for k in even]
 
 
@@ -381,8 +381,8 @@
     blocks = pltpu.VMEM(packed.shape, NARROW)
     started = call(functools.partial(pack_kernel, tiles), [distant] * devices, [blocks], count, 6 * count,
                    place, current, specs=[SMEM, VMEM])
-    pieces, order = gather_vectors(vectors, devices, started[0])
     held = by_distance(started)
+    pieces, order = gather_vectors(vectors, devices, held[1], held[-1])
 
     ladder_flops = first * singles * 4 * virtual**3
     ladder, whole = call(

time: 130 us -> 127 us (0.977)
  waiting for transfers between devices: 26.8 us -> 22.9 us
    ppermute x14, waiting for transfers between devices: 6.4 us -> 2.76 us  [by_distance(): lax.ppermute(parts[k], 'occj', [(d, d ^ k) for d in range(devices)])]
  transfers between devices with their start and end apart: 38 -> 38, of which waited for: 9 -> 8; matrix products, arithmetic and copies ran while one was open for 1% -> 2% of each run, Pallas kernels for 22% -> 22%
where the time goes in v19:
time: 127 us; the launch traced here: 126 us
  starting transfers between devices  62.6 us (49%)
  Pallas kernels  31.2 us (25%)
  waiting for transfers between devices  22.9 us (18%)
  local copies, waits for them, and re-layouts  7.04 us (6%)
  between operations  1.53 us (1%)
    ppermute x18, starting transfers between devices, across_first(): lax.ppermute(parts[s], 'occi', [(k, k ^ s) for k in range(groups)])  35.3 us
    pallas_call x9, Pallas kernels, call(): pl.pallas_call(body, out_shape=outs, in_specs=specs, out_specs=jax.tree.m...  19.3 us
    ppermute x14, starting transfers between devices, by_distance(): lax.ppermute(parts[k], 'occj', [(d, d ^ k) for d in range(devices)])  15.4 us
    ppermute x18, waiting for transfers between devices, across_first(): lax.ppermute(parts[s], 'occi', [(k, k ^ s) for k in range(groups)])  8.17 us
    pallas_call x1, Pallas kernels, local(): pl.pallas_call(functools.partial(second_ladder_kernel, tiles, first), gri...  7.78 us
    all_to_all x2, starting transfers between devices, exchange(): lax.all_to_all(blocks, 'occj', split_axis=0, concat_axis=0, tiled=True)  7.38 us
    ppermute x4, waiting for transfers between devices, turn(): return lax.ppermute(x, 'occj', [(d, d ^ k) for d in range(devices)])  6.42 us
    all_to_all x2, waiting for transfers between devices, exchange(): lax.all_to_all(blocks, 'occj', split_axis=0, concat_axis=0, tiled=True)  5.54 us
  transfers between devices with their start and end apart: 38, of which 8 were waited for; matrix products, arithmetic and copies ran while one was open for 2% of the time, Pallas kernels for 22%

profile of v19, /device:TPU:0, one launch (start us, length us, event | category | flops | bytes accessed | tf_op | source)
XLA Modules:
  0.0 125.6 jit_solution(14432276472924104651)
XLA Ops:
  0.0 2.9 %collective-permute-start = (bf16[3,64,512]{2,1,0:T(8,128)(2,1)}, bf16[3,64,512]{2,1,0:T(8,128)(2,1)S(1)}, u32[]{:S(2)}, u32[]{:S(2)}) collective-permute-start(bf16[3,64,512]{2,1,0:T(8,128)(2,1)} %refs_0_.1), channel_id=1, source_target_pairs={{0,2},{1,3},{2,0},{3,1},{4,6},{5,7},{6,4},{7,5},{8,10},{9,11},{10,... | collective-permute-start | bytes 589832 | tf_op jit(solution)/shard_map/ppermute | solution.py:338
  2.9 1.5 %collective-permute-start.1 = (bf16[3,64,512]{2,1,0:T(8,128)(2,1)}, bf16[3,64,512]{2,1,0:T(8,128)(2,1)S(1)}, u32[]{:S(2)}, u32[]{:S(2)}) collective-permute-start(bf16[3,64,512]{2,1,0:T(8,128)(2,1)} %refs_0_.1), channel_id=1, source_target_pairs={{0,4},{1,5},{2,6},{3,7},{4,0},{5,1},{6,2},{7,3},{8,12},{9,13},{10,... | collective-permute-start | bytes 589832 | tf_op jit(solution)/shard_map/ppermute | solution.py:338
  4.5 0.1 pad_add_fusion.place.source
  4.5 1.6 %copy-done = f32[2,1,512,512]{3,2,1,0:T(8,128)S(1)} copy-done((f32[2,1,512,512]{3,2,1,0:T(8,128)S(1)}, f32[2,1,512,512]{3,2,1,0:T(8,128)}, u32[]{:S(2)}) %copy-start) | copy-done | bytes 2097176
  6.1 0.9 shard_map.73
  7.1 3.0 %collective-permute-start.4 = (bf16[2,128,256]{2,1,0:T(8,128)(2,1)S(1)}, bf16[2,128,256]{2,1,0:T(8,128)(2,1)S(1)}, u32[]{:S(2)}, u32[]{:S(2)}) collective-permute-start(bf16[2,128,256]{2,1,0:T(8,128)(2,1)S(1)} %get-tuple-element.54), channel_id=1, source_target_pairs={{0,7},{1,6},{2,5},{3,4},{4,3},{5,2},{6,1},{7,0},{8,15},{9,14},{10,... | collective-permute-start | bytes 393224 | tf_op jit(solution)/shard_map/ppermute | solution.py:305
  10.1 6.4 %collective-permute-done.1.refs_2_ = bf16[3,64,512]{2,1,0:T(8,128)(2,1)S(1)} collective-permute-done((bf16[3,64,512]{2,1,0:T(8,128)(2,1)}, bf16[3,64,512]{2,1,0:T(8,128)(2,1)S(1)}, u32[]{:S(2)}, u32[]{:S(2)}) %collective-permute-start.1) | collective-permute-done | bytes 196640 | tf_op jit(solution)/shard_map/ppermute | solution.py:338
  16.5 0.1 pad_maximum_fusion
  16.7 1.6 %collective-permute-start.10 = (bf16[2,128,256]{2,1,0:T(8,128)(2,1)S(1)}, bf16[2,128,256]{2,1,0:T(8,128)(2,1)S(1)}, u32[]{:S(2)}, u32[]{:S(2)}) collective-permute-start(bf16[2,128,256]{2,1,0:T(8,128)(2,1)S(1)} %get-tuple-element.63), channel_id=1, source_target_pairs={{0,6},{1,7},{2,4},{3,5},{4,2},{5,3},{6,0},{7,1},{8,14},{9,15},{10,... | collective-permute-start | bytes 393224 | tf_op jit(solution)/shard_map/ppermute | solution.py:305
  18.3 1.5 %collective-permute-start.6 = (bf16[2,128,256]{2,1,0:T(8,128)(2,1)S(1)}, bf16[2,128,256]{2,1,0:T(8,128)(2,1)S(1)}, u32[]{:S(2)}, u32[]{:S(2)}) collective-permute-start(bf16[2,128,256]{2,1,0:T(8,128)(2,1)S(1)} %get-tuple-element.59), channel_id=1, source_target_pairs={{0,2},{1,3},{2,0},{3,1},{4,6},{5,7},{6,4},{7,5},{8,10},{9,11},{10,... | collective-permute-start | bytes 393224 | tf_op jit(solution)/shard_map/ppermute | solution.py:305
  19.8 0.5 collective-permute-start.8
  20.3 1.5 %collective-permute-start.9 = (bf16[2,128,256]{2,1,0:T(8,128)(2,1)S(1)}, bf16[2,128,256]{2,1,0:T(8,128)(2,1)S(1)}, u32[]{:S(2)}, u32[]{:S(2)}) collective-permute-start(bf16[2,128,256]{2,1,0:T(8,128)(2,1)S(1)} %get-tuple-element.62), channel_id=1, source_target_pairs={{0,5},{1,4},{2,7},{3,6},{4,1},{5,0},{6,3},{7,2},{8,13},{9,12},{10,... | collective-permute-start | bytes 393224 | tf_op jit(solution)/shard_map/ppermute | solution.py:305
  21.8 6.3 %shard_map.74 = (bf16[8,2,128,256]{3,2,1,0:T(8,128)(2,1)}, bf16[512,1536]{1,0:T(8,128)(2,1)}) custom-call(s32[2]{0:T(128)S(1)} %pad_add_fusion.place.source, f32[2,512,512]{2,1,0:T(8,128)} %bitcast.13, bf16[3,64,512]{2,1,0:T(8,128)(2,1)S(1)} %copy-done.1, bf16[3,64,512]{2,1,0:T(8,128)(2,1)S(1)} %collective-permute-done.refs_1_, ...), custom_call_target="tpu_custom_call" | custom-call | flops 3221225472 | bytes 4194304 | tf_op jit(solution)/shard_map/pallas_call | solution.py:42
  28.1 0.7 collective-permute-done.7.refs_3_
  28.8 0.2 collective-permute-done.9.refs_5_
  29.0 0.7 shard_map.75
  29.7 3.7 %collective-permute-start.11 = (bf16[2,2,64,256]{3,2,1,0:T(8,128)(2,1)S(1)}, bf16[2,2,64,256]{3,2,1,0:T(8,128)(2,1)S(1)}, u32[]{:S(2)}, u32[]{:S(2)}) collective-permute-start(bf16[2,2,64,256]{3,2,1,0:T(8,128)(2,1)S(1)} %get-tuple-element.64), channel_id=1, source_target_pairs={{0,24},{8,16},{16,8},{24,0},{1,25},{9,17},{17,9},{25,1},{2,26},{10... | collective-permute-start | bytes 393224 | tf_op jit(solution)/shard_map/ppermute | solution.py:312
  33.4 0.8 collective-permute-start.13
  34.2 3.6 %all-to-all-start = ((bf16[8,2,128,256]{3,2,1,0:T(8,128)(2,1)}), bf16[8,2,128,256]{3,2,1,0:T(8,128)(2,1)S(1)}, u32[]{:S(2)}, u32[]{:S(2)}) async-start(bf16[8,2,128,256]{3,2,1,0:T(8,128)(2,1)} %get-tuple-element.56), calls=%async_computation | async-start | bytes 2097152 | tf_op jit(solution)/shard_map/all_to_all | solution.py:299
  37.7 1.3 %collective-permute-start.17 = (bf16[2,2,64,256]{3,2,1,0:T(8,128)(2,1)S(1)}, bf16[2,2,64,256]{3,2,1,0:T(8,128)(2,1)S(1)}, u32[]{:S(2)}, u32[]{:S(2)}) collective-permute-start(bf16[2,2,64,256]{3,2,1,0:T(8,128)(2,1)S(1)} %get-tuple-element.76), channel_id=1, source_target_pairs={{0,8},{8,0},{16,24},{24,16},{1,9},{9,1},{17,25},{25,17},{2,10},{10... | collective-permute-start | bytes 393224 | tf_op jit(solution)/shard_map/ppermute | solution.py:312
  39.1 2.9 %collective-permute-start.18 = (bf16[2,2,64,256]{3,2,1,0:T(8,128)(2,1)S(1)}, bf16[2,2,64,256]{3,2,1,0:T(8,128)(2,1)S(1)}, u32[]{:S(2)}, u32[]{:S(2)}) collective-permute-start(bf16[2,2,64,256]{3,2,1,0:T(8,128)(2,1)S(1)} %get-tuple-element.77), channel_id=1, source_target_pairs={{0,16},{8,24},{16,0},{24,8},{1,17},{9,25},{17,1},{25,9},{2,18},{10... | collective-permute-start | bytes 393224 | tf_op jit(solution)/shard_map/ppermute | solution.py:312
  42.0 0.2 collective-permute-start.19
  42.2 0.6 dynamic_slice.14
  43.4 0.6 dynamic_slice.12
  44.6 1.1 collective-permute-done.13.refs_2_
  45.7 1.3 %shard_map.76.place = s32[2]{0:T(128)} custom-call(s32[2]{0:T(128)} %copy-done.4), custom_call_target="tpu_custom_call" | custom-call | flops 30000001024 | bytes 8 | tf_op jit(solution)/shard_map/pallas_call | solution.py:327
  47.1 0.1 fusion
  47.3 0.1 broadcast_add_fusion
  47.4 0.1 broadcast_add_fusion.2
  47.5 5.5 %all-to-all-done.ladder = bf16[8,2,128,256]{3,2,1,0:T(8,128)(2,1)S(1)} async-done(((bf16[8,2,128,256]{3,2,1,0:T(8,128)(2,1)}), bf16[8,2,128,256]{3,2,1,0:T(8,128)(2,1)S(1)}, u32[]{:S(2)}, u32[]{:S(2)}) %all-to-all-start) | async-done | bytes 1048608 | tf_op jit(solution)/shard_map/all_to_all | solution.py:299
  53.1 0.7 copy-done.10
  53.7 1.6 %shard_map.77 = (bf16[2,2,64,256]{3,2,1,0:T(8,128)(2,1)S(1)}, bf16[2,2,64,256]{3,2,1,0:T(8,128)(2,1)S(1)}, bf16[2,2,64,256]{3,2,1,0:T(8,128)(2,1)S(1)}, bf16[2,2,64,256]{3,2,1,0:T(8,128)(2,1)S(1)}) custom-call(s32[2]{0:T(128)S(1)} %copy-done.10, f32[8,8]{1,0:T(8,128)S(1)} %convert_element_type.3.fock, bf16[8,2,128,256]{3,2,1,0:T(8,128)(2,1)S(1)} %all-to-all-done.ladder, ...), custom_call_target="tpu_custom_call" | custom-call | flops 30000001024 | bytes 3145728 | tf_op jit(solution)/shard_map/pallas_call | solution.py:42
  55.3 1.3 %collective-permute-start.14 = (bf16[2,2,64,256]{3,2,1,0:T(8,128)(2,1)S(1)}, bf16[2,2,64,256]{3,2,1,0:T(8,128)(2,1)S(1)}, u32[]{:S(2)}, u32[]{:S(2)}) collective-permute-start(bf16[2,2,64,256]{3,2,1,0:T(8,128)(2,1)S(1)} %get-tuple-element.71.refs_1_), channel_id=1, source_target_pairs={{0,8},{8,0},{16,24},{24,16},{1,9},{9,1},{17,25},{25,17},{2,10},{10... | collective-permute-start | bytes 393224 | tf_op jit(solution)/shard_map/ppermute | solution.py:312
  56.6 2.9 %collective-permute-start.15 = (bf16[2,2,64,256]{3,2,1,0:T(8,128)(2,1)S(1)}, bf16[2,2,64,256]{3,2,1,0:T(8,128)(2,1)S(1)}, u32[]{:S(2)}, u32[]{:S(2)}) collective-permute-start(bf16[2,2,64,256]{3,2,1,0:T(8,128)(2,1)S(1)} %get-tuple-element.72.refs_2_), channel_id=1, source_target_pairs={{0,16},{8,24},{16,0},{24,8},{1,17},{9,25},{17,1},{25,9},{2,18},{10... | collective-permute-start | bytes 393224 | tf_op jit(solution)/shard_map/ppermute | solution.py:312
  59.5 0.2 collective-permute-start.16
  59.8 1.6 %shard_map.79 = (bf16[2,2,64,256]{3,2,1,0:T(8,128)(2,1)S(1)}, bf16[2,2,64,256]{3,2,1,0:T(8,128)(2,1)S(1)}, bf16[2,2,64,256]{3,2,1,0:T(8,128)(2,1)S(1)}, bf16[2,2,64,256]{3,2,1,0:T(8,128)(2,1)S(1)}) custom-call(s32[2]{0:T(128)S(1)} %copy-done.5, f32[8,8]{1,0:T(8,128)S(1)} %convert_element_type.3.fock, bf16[8,2,128,256]{3,2,1,0:T(8,128)(2,1)S(1)} %all-to-all-done.ladder, ...), custom_call_target="tpu_custom_call" | custom-call | flops 30000001024 | bytes 3145728 | tf_op jit(solution)/shard_map/pallas_call | solution.py:42
  61.4 0.4 collective-permute-start.20
  61.8 3.8 %collective-permute-start.21 = (bf16[2,2,64,256]{3,2,1,0:T(8,128)(2,1)S(1)}, bf16[2,2,64,256]{3,2,1,0:T(8,128)(2,1)S(1)}, u32[]{:S(2)}, u32[]{:S(2)}) collective-permute-start(bf16[2,2,64,256]{3,2,1,0:T(8,128)(2,1)S(1)} %get-tuple-element.81.refs_3_), channel_id=1, source_target_pairs={{0,16},{8,24},{16,0},{24,8},{1,17},{9,25},{17,1},{25,9},{2,18},{10... | collective-permute-start | bytes 393224 | tf_op jit(solution)/shard_map/ppermute | solution.py:312
  65.6 1.2 collective-permute-start.22
  66.8 2.9 %collective-permute-done.15.refs_6_ = bf16[2,2,64,256]{3,2,1,0:T(8,128)(2,1)S(1)} collective-permute-done((bf16[2,2,64,256]{3,2,1,0:T(8,128)(2,1)S(1)}, bf16[2,2,64,256]{3,2,1,0:T(8,128)(2,1)S(1)}, u32[]{:S(2)}, u32[]{:S(2)}) %collective-permute-start.15) | collective-permute-done | bytes 131104 | tf_op jit(solution)/shard_map/ppermute | solution.py:312
  69.7 2.5 %shard_map.78 = (bf16[8,2,64,256]{3,2,1,0:T(8,128)(2,1)S(1)}, bf16[2,8,64,256]{3,2,1,0:T(8,128)(2,1)S(1)}, bf16[2,2,64,256]{3,2,1,0:T(8,128)(2,1)S(1)}, bf16[2,2...) custom-call(s32[2]{0:T(128)S(1)} %copy-done.5, f32[8,8]{1,0:T(8,128)S(1)} %convert_element_type.3.fock, ...), custom_call_target="tpu_custom_call" | custom-call | flops 30000001024 | bytes 5242880 | tf_op jit(solution)/shard_map/pallas_call | solution.py:42
  72.3 0.8 copy-done.8
  73.0 9.8 %collective-permute-start.26 = (bf16[2,2,64,256]{3,2,1,0:T(8,128)(2,1)S(1)}, bf16[2,2,64,256]{3,2,1,0:T(8,128)(2,1)S(1)}, u32[]{:S(2)}, u32[]{:S(2)}) collective-permute-start(bf16[2,2,64,256]{3,2,1,0:T(8,128)(2,1)S(1)} %get-tuple-element.90), channel_id=1, source_target_pairs={{0,8},{8,0},{16,24},{24,16},{1,9},{9,1},{17,25},{25,17},{2,10},{10... | collective-permute-start | bytes 393224 | tf_op jit(solution)/shard_map/ppermute | solution.py:312
  82.9 0.7 collective-permute-start.27
  83.6 1.7 %collective-permute-start.28 = (bf16[2,2,64,256]{3,2,1,0:T(8,128)(2,1)S(1)}, bf16[2,2,64,256]{3,2,1,0:T(8,128)(2,1)S(1)}, u32[]{:S(2)}, u32[]{:S(2)}) collective-permute-start(bf16[2,2,64,256]{3,2,1,0:T(8,128)(2,1)S(1)} %get-tuple-element.92), channel_id=1, source_target_pairs={{0,24},{8,16},{16,8},{24,0},{1,25},{9,17},{17,9},{25,1},{2,26},{10... | collective-permute-start | bytes 393224 | tf_op jit(solution)/shard_map/ppermute | solution.py:312
  85.2 3.6 %shard_map.80 = (bf16[8,2,128,256]{3,2,1,0:T(8,128)(2,1)}, bf16[2,8,64,256]{3,2,1,0:T(8,128)(2,1)S(1)}, bf16[2,2,64,256]{3,2,1,0:T(8,128)(2,1)S(1)}, bf16[2,2,64...) custom-call(s32[2]{0:T(128)S(1)} %copy-done.5, f32[8,8]{1,0:T(8,128)S(1)} %convert_element_type.3.fock, ...), custom_call_target="tpu_custom_call" | custom-call | flops 30000001024 | bytes 5242880 | tf_op jit(solution)/shard_map/pallas_call | solution.py:42
  88.9 1.1 collective-permute-start.23
  90.0 1.6 %collective-permute-start.24 = (bf16[2,2,64,256]{3,2,1,0:T(8,128)(2,1)S(1)}, bf16[2,2,64,256]{3,2,1,0:T(8,128)(2,1)S(1)}, u32[]{:S(2)}, u32[]{:S(2)}) collective-permute-start(bf16[2,2,64,256]{3,2,1,0:T(8,128)(2,1)S(1)} %get-tuple-element.87), channel_id=1, source_target_pairs={{0,16},{8,24},{16,0},{24,8},{1,17},{9,25},{17,1},{25,9},{2,18},{10... | collective-permute-start | bytes 393224 | tf_op jit(solution)/shard_map/ppermute | solution.py:312
  91.6 3.8 %all-to-all-start.1 = ((bf16[8,2,128,256]{3,2,1,0:T(8,128)(2,1)}), bf16[8,2,128,256]{3,2,1,0:T(8,128)(2,1)S(1)}, u32[]{:S(2)}, u32[]{:S(2)}) async-start(bf16[8,2,128,256]{3,2,1,0:T(8,128)(2,1)} %get-tuple-element.83), calls=%async_computation.1 | async-start | bytes 2097152 | tf_op jit(solution)/shard_map/all_to_all | solution.py:299
  95.4 1.5 %collective-permute-start.25 = (bf16[2,2,64,256]{3,2,1,0:T(8,128)(2,1)S(1)}, bf16[2,2,64,256]{3,2,1,0:T(8,128)(2,1)S(1)}, u32[]{:S(2)}, u32[]{:S(2)}) collective-permute-start(bf16[2,2,64,256]{3,2,1,0:T(8,128)(2,1)S(1)} %get-tuple-element.88), channel_id=1, source_target_pairs={{0,24},{8,16},{16,8},{24,0},{1,25},{9,17},{17,9},{25,1},{2,26},{10... | collective-permute-start | bytes 393224 | tf_op jit(solution)/shard_map/ppermute | solution.py:312
  97.0 1.0 copy-done.9
  98.0 1.1 shard_map.82.refs_3_
  99.1 4.1 %collective-permute-done.25.refs_2_ = bf16[2,2,64,256]{3,2,1,0:T(8,128)(2,1)S(1)} collective-permute-done((bf16[2,2,64,256]{3,2,1,0:T(8,128)(2,1)S(1)}, bf16[2,2,64,256]{3,2,1,0:T(8,128)(2,1)S(1)}, u32[]{:S(2)}, u32[]{:S(2)}) %collective-permute-start.25) | collective-permute-done | bytes 131104 | tf_op jit(solution)/shard_map/ppermute | solution.py:312
  103.2 1.2 shard_map.83
  104.5 1.7 %collective-permute-start.30 = (bf16[2,128,256]{2,1,0:T(8,128)(2,1)S(1)}, bf16[2,128,256]{2,1,0:T(8,128)(2,1)S(1)}, u32[]{:S(2)}, u32[]{:S(2)}) collective-permute-start(bf16[2,128,256]{2,1,0:T(8,128)(2,1)S(1)} %get-tuple-element.95), channel_id=1, source_target_pairs={{0,2},{1,3},{2,0},{3,1},{4,6},{5,7},{6,4},{7,5},{8,10},{9,11},{10,... | collective-permute-start | bytes 393224 | tf_op jit(solution)/shard_map/ppermute | solution.py:305
  106.2 0.1 collective-permute-start.31
  106.3 2.2 %collective-permute-start.32 = (bf16[2,128,256]{2,1,0:T(8,128)(2,1)S(1)}, bf16[2,128,256]{2,1,0:T(8,128)(2,1)S(1)}, u32[]{:S(2)}, u32[]{:S(2)}) collective-permute-start(bf16[2,128,256]{2,1,0:T(8,128)(2,1)S(1)} %get-tuple-element.97), channel_id=1, source_target_pairs={{0,4},{1,5},{2,6},{3,7},{4,0},{5,1},{6,2},{7,3},{8,12},{9,13},{10,... | collective-permute-start | bytes 393224 | tf_op jit(solution)/shard_map/ppermute | solution.py:305
  108.5 2.9 %collective-permute-start.34 = (bf16[2,128,256]{2,1,0:T(8,128)(2,1)S(1)}, bf16[2,128,256]{2,1,0:T(8,128)(2,1)S(1)}, u32[]{:S(2)}, u32[]{:S(2)}) collective-permute-start(bf16[2,128,256]{2,1,0:T(8,128)(2,1)S(1)} %get-tuple-element.99), channel_id=1, source_target_pairs={{0,6},{1,7},{2,4},{3,5},{4,2},{5,3},{6,0},{7,1},{8,14},{9,15},{10,... | collective-permute-start | bytes 393224 | tf_op jit(solution)/shard_map/ppermute | solution.py:305
  111.4 1.8 %collective-permute-done.30.refs_2_ = bf16[2,128,256]{2,1,0:T(8,128)(2,1)S(1)} collective-permute-done((bf16[2,128,256]{2,1,0:T(8,128)(2,1)S(1)}, bf16[2,128,256]{2,1,0:T(8,128)(2,1)S(1)}, u32[]{:S(2)}, u32[]{:S(2)}) %collective-permute-start.30) | collective-permute-done | bytes 131104 | tf_op jit(solution)/shard_map/ppermute | solution.py:305
  113.2 0.3 collective-permute-start.35
  113.5 0.1 broadcast_in_dim.4.row
  113.6 1.4 %copy-done.7 = bf16[512,1536]{1,0:T(8,128)(2,1)S(1)} copy-done((bf16[512,1536]{1,0:T(8,128)(2,1)S(1)}, bf16[512,1536]{1,0:T(8,128)(2,1)}, u32[]{:S(2)}) %copy-start.7) | copy-done | bytes 1572888
  115.0 7.8 %shard_map.81.source = f32[2,512,512]{2,1,0:T(8,128)} custom-call(s32[2]{0:T(128)S(1)} %copy-done.5, f32[8]{0:T(128)S(1)} %copy-done.6, f32[2,512,512]{2,1,0:T(8,128)} %bitcast.14, bf16[8,2,128,256]{3,2,1,0:T(8,128)(2,1)S(1)} %all-to-all-done.1.blocks, f32[512,128]{1,0:T(8,128)S(1)} %broadcast_in_dim.4.row, f32[1,512]{1,0:T(1,128)S(1)} %bitcast.20, ...), custom_call_target="tpu_custom_call" | custom-call | flops 3221225472 | bytes 6291456 | tf_op jit(solution)/shard_map/pallas_call | solution.py:427
  122.8 2.8 %shard_map.84 = f32[2,512,512]{2,1,0:T(8,128)} custom-call(s32[2]{0:T(128)S(1)} %copy-done.5, f32[2,512,512]{2,1,0:T(8,128)} %shard_map.81.source, bf16[2,128,256]{2,1,0:T(8,128)(2,1)S(1)} %get-tuple-element.93.refs_0_, bf16[2,128,256]{2,1,0:T(8,128)(2,1)S(1)} %collective-permute-done.29.refs_1_, ...), custom_call_target="tpu_custom_call", output_to_operand_aliasing={{}: (1, {})} | custom-call | flops 524288 | bytes 5242880 | tf_op jit(solution)/shard_map/pallas_call | solution.py:450
  (64 shorter events, 0.5 us)
Async XLA Ops:
  0.0 10.1 %collective-permute-start = (bf16[3,64,512]{2,1,0:T(8,128)(2,1)}, bf16[3,64,512]{2,1,0:T(8,128)(2,1)S(1)}, u32[]{:S(2)}, u32[]{:S(2)}) collective-permute-start(bf16[3,64,512]{2,1,0:T(8,128)(2,1)} %refs_0_.1), channel_id=1, source_target_pairs={{0,2},{1,3},{2,0},{3,1},{4,6},{5,7},{6,4},{7,5},{8,10},{9,11},{10,... | collective-permute-start | bytes 589832 | tf_op jit(solution)/shard_map/ppermute | solution.py:338
  2.9 13.6 %collective-permute-start.1 = (bf16[3,64,512]{2,1,0:T(8,128)(2,1)}, bf16[3,64,512]{2,1,0:T(8,128)(2,1)S(1)}, u32[]{:S(2)}, u32[]{:S(2)}) collective-permute-start(bf16[3,64,512]{2,1,0:T(8,128)(2,1)} %refs_0_.1), channel_id=1, source_target_pairs={{0,4},{1,5},{2,6},{3,7},{4,0},{5,1},{6,2},{7,3},{8,12},{9,13},{10,... | collective-permute-start | bytes 589832 | tf_op jit(solution)/shard_map/ppermute | solution.py:338
  4.5 12.1 %collective-permute-start.2 = (bf16[3,64,512]{2,1,0:T(8,128)(2,1)}, bf16[3,64,512]{2,1,0:T(8,128)(2,1)S(1)}, u32[]{:S(2)}, u32[]{:S(2)}) collective-permute-start(bf16[3,64,512]{2,1,0:T(8,128)(2,1)} %refs_0_.1), channel_id=1, source_target_pairs={{0,6},{1,7},{2,4},{3,5},{4,2},{5,3},{6,0},{7,1},{8,14},{9,15},{10,... | collective-permute-start | bytes 589832 | tf_op jit(solution)/shard_map/ppermute | solution.py:338
  4.5 24.5 %copy-start.4 = (s32[2]{0:T(128)}, s32[2]{0:T(128)S(1)}, u32[]{:S(2)}) copy-start(s32[2]{0:T(128)S(1)} %pad_add_fusion.place.source) | copy-start | bytes 28
  4.5 1.6 %copy-start = (f32[2,1,512,512]{3,2,1,0:T(8,128)S(1)}, f32[2,1,512,512]{3,2,1,0:T(8,128)}, u32[]{:S(2)}) copy-start(f32[2,1,512,512]{3,2,1,0:T(8,128)} %param.7) | copy-start | bytes 6291460
  6.1 10.4 %copy-start.1 = (bf16[3,64,512]{2,1,0:T(8,128)(2,1)S(1)}, bf16[3,64,512]{2,1,0:T(8,128)(2,1)}, u32[]{:S(2)}) copy-start(bf16[3,64,512]{2,1,0:T(8,128)(2,1)} %refs_0_.1) | copy-start | bytes 589828
  7.0 9.6 %collective-permute-start.3 = (bf16[2,128,256]{2,1,0:T(8,128)(2,1)S(1)}, bf16[2,128,256]{2,1,0:T(8,128)(2,1)S(1)}, u32[]{:S(2)}, u32[]{:S(2)}) collective-permute-start(bf16[2,128,256]{2,1,0:T(8,128)(2,1)S(1)} %get-tuple-element.53), channel_id=1, source_target_pairs={{0,1},{1,0},{2,3},{3,2},{4,5},{5,4},{6,7},{7,6},{8,9},{9,8},{10,11... | collective-permute-start | bytes 393224 | tf_op jit(solution)/shard_map/ppermute | solution.py:305
  7.1 9.6 %collective-permute-start.4 = (bf16[2,128,256]{2,1,0:T(8,128)(2,1)S(1)}, bf16[2,128,256]{2,1,0:T(8,128)(2,1)S(1)}, u32[]{:S(2)}, u32[]{:S(2)}) collective-permute-start(bf16[2,128,256]{2,1,0:T(8,128)(2,1)S(1)} %get-tuple-element.54), channel_id=1, source_target_pairs={{0,7},{1,6},{2,5},{3,4},{4,3},{5,2},{6,1},{7,0},{8,15},{9,14},{10,... | collective-permute-start | bytes 393224 | tf_op jit(solution)/shard_map/ppermute | solution.py:305
  16.7 3.6 %collective-permute-start.5 = (bf16[4,3,64,512]{3,2,1,0:T(8,128)(2,1)S(1)}, bf16[4,3,64,512]{3,2,1,0:T(8,128)(2,1)S(1)}, u32[]{:S(2)}, u32[]{:S(2)}) collective-permute-start(bf16[4,3,64,512]{3,2,1,0:T(8,128)(2,1)S(1)} %pad_maximum_fusion), channel_id=1, source_target_pairs={{0,1},{1,0},{2,3},{3,2},{4,5},{5,4},{6,7},{7,6},{8,9},{9,8},{10,11... | collective-permute-start | bytes 2359304 | tf_op jit(solution)/shard_map/ppermute | solution.py:338
  16.7 11.3 %collective-permute-start.10 = (bf16[2,128,256]{2,1,0:T(8,128)(2,1)S(1)}, bf16[2,128,256]{2,1,0:T(8,128)(2,1)S(1)}, u32[]{:S(2)}, u32[]{:S(2)}) collective-permute-start(bf16[2,128,256]{2,1,0:T(8,128)(2,1)S(1)} %get-tuple-element.63), channel_id=1, source_target_pairs={{0,6},{1,7},{2,4},{3,5},{4,2},{5,3},{6,0},{7,1},{8,14},{9,15},{10,... | collective-permute-start | bytes 393224 | tf_op jit(solution)/shard_map/ppermute | solution.py:305
  18.3 9.8 %collective-permute-start.6 = (bf16[2,128,256]{2,1,0:T(8,128)(2,1)S(1)}, bf16[2,128,256]{2,1,0:T(8,128)(2,1)S(1)}, u32[]{:S(2)}, u32[]{:S(2)}) collective-permute-start(bf16[2,128,256]{2,1,0:T(8,128)(2,1)S(1)} %get-tuple-element.59), channel_id=1, source_target_pairs={{0,2},{1,3},{2,0},{3,1},{4,6},{5,7},{6,4},{7,5},{8,10},{9,11},{10,... | collective-permute-start | bytes 393224 | tf_op jit(solution)/shard_map/ppermute | solution.py:305
  19.8 9.0 %collective-permute-start.7 = (bf16[2,128,256]{2,1,0:T(8,128)(2,1)S(1)}, bf16[2,128,256]{2,1,0:T(8,128)(2,1)S(1)}, u32[]{:S(2)}, u32[]{:S(2)}) collective-permute-start(bf16[2,128,256]{2,1,0:T(8,128)(2,1)S(1)} %get-tuple-element.60), channel_id=1, source_target_pairs={{0,3},{1,2},{2,1},{3,0},{4,7},{5,6},{6,5},{7,4},{8,11},{9,10},{10,... | collective-permute-start | bytes 393224 | tf_op jit(solution)/shard_map/ppermute | solution.py:305
  19.8 8.9 %collective-permute-start.8 = (bf16[2,128,256]{2,1,0:T(8,128)(2,1)S(1)}, bf16[2,128,256]{2,1,0:T(8,128)(2,1)S(1)}, u32[]{:S(2)}, u32[]{:S(2)}) collective-permute-start(bf16[2,128,256]{2,1,0:T(8,128)(2,1)S(1)} %get-tuple-element.61), channel_id=1, source_target_pairs={{0,4},{1,5},{2,6},{3,7},{4,0},{5,1},{6,2},{7,3},{8,12},{9,13},{10,... | collective-permute-start | bytes 393224 | tf_op jit(solution)/shard_map/ppermute | solution.py:305
  20.3 13.9 %copy-start.11 = (bf16[8,8]{1,0:T(8,128)(2,1)S(1)}, bf16[8,8]{1,0:T(8,128)(2,1)}, u32[]{:S(2)}) copy-start(bf16[8,8]{1,0:T(8,128)(2,1)} %param.9) | copy-start | bytes 388
  20.3 8.7 %collective-permute-start.9 = (bf16[2,128,256]{2,1,0:T(8,128)(2,1)S(1)}, bf16[2,128,256]{2,1,0:T(8,128)(2,1)S(1)}, u32[]{:S(2)}, u32[]{:S(2)}) collective-permute-start(bf16[2,128,256]{2,1,0:T(8,128)(2,1)S(1)} %get-tuple-element.62), channel_id=1, source_target_pairs={{0,5},{1,4},{2,7},{3,6},{4,1},{5,0},{6,3},{7,2},{8,13},{9,12},{10,... | collective-permute-start | bytes 393224 | tf_op jit(solution)/shard_map/ppermute | solution.py:305
  28.1 14.1 %copy-start.13 = (s32[8]{0:T(128)S(1)}, s32[8]{0:T(128)}, u32[]{:S(2)}) copy-start(s32[8]{0:T(128)} %constant.25.clone) | copy-start | bytes 100
  28.1 15.3 %copy-start.12 = (s32[8]{0:T(128)S(1)}, s32[8]{0:T(128)}, u32[]{:S(2)}) copy-start(s32[8]{0:T(128)} %constant.24.clone) | copy-start | bytes 100
  29.7 12.3 %collective-permute-start.11 = (bf16[2,2,64,256]{3,2,1,0:T(8,128)(2,1)S(1)}, bf16[2,2,64,256]{3,2,1,0:T(8,128)(2,1)S(1)}, u32[]{:S(2)}, u32[]{:S(2)}) collective-permute-start(bf16[2,2,64,256]{3,2,1,0:T(8,128)(2,1)S(1)} %get-tuple-element.64), channel_id=1, source_target_pairs={{0,24},{8,16},{16,8},{24,0},{1,25},{9,17},{17,9},{25,1},{2,26},{10... | collective-permute-start | bytes 393224 | tf_op jit(solution)/shard_map/ppermute | solution.py:312
  33.4 11.2 %collective-permute-start.12 = (bf16[2,2,64,256]{3,2,1,0:T(8,128)(2,1)S(1)}, bf16[2,2,64,256]{3,2,1,0:T(8,128)(2,1)S(1)}, u32[]{:S(2)}, u32[]{:S(2)}) collective-permute-start(bf16[2,2,64,256]{3,2,1,0:T(8,128)(2,1)S(1)} %get-tuple-element.67), channel_id=1, source_target_pairs={{0,8},{8,0},{16,24},{24,16},{1,9},{9,1},{17,25},{25,17},{2,10},{10... | collective-permute-start | bytes 393224 | tf_op jit(solution)/shard_map/ppermute | solution.py:312
  33.4 12.4 %collective-permute-start.13 = (bf16[2,2,64,256]{3,2,1,0:T(8,128)(2,1)S(1)}, bf16[2,2,64,256]{3,2,1,0:T(8,128)(2,1)S(1)}, u32[]{:S(2)}, u32[]{:S(2)}) collective-permute-start(bf16[2,2,64,256]{3,2,1,0:T(8,128)(2,1)S(1)} %get-tuple-element.68), channel_id=1, source_target_pairs={{0,16},{8,24},{16,0},{24,8},{1,17},{9,25},{17,1},{25,9},{2,18},{10... | collective-permute-start | bytes 393224 | tf_op jit(solution)/shard_map/ppermute | solution.py:312
  34.2 18.9 %all-to-all-start = ((bf16[8,2,128,256]{3,2,1,0:T(8,128)(2,1)}), bf16[8,2,128,256]{3,2,1,0:T(8,128)(2,1)S(1)}, u32[]{:S(2)}, u32[]{:S(2)}) async-start(bf16[8,2,128,256]{3,2,1,0:T(8,128)(2,1)} %get-tuple-element.56), calls=%async_computation | async-start | bytes 2097152 | tf_op jit(solution)/shard_map/all_to_all | solution.py:299
  37.7 21.8 %collective-permute-start.17 = (bf16[2,2,64,256]{3,2,1,0:T(8,128)(2,1)S(1)}, bf16[2,2,64,256]{3,2,1,0:T(8,128)(2,1)S(1)}, u32[]{:S(2)}, u32[]{:S(2)}) collective-permute-start(bf16[2,2,64,256]{3,2,1,0:T(8,128)(2,1)S(1)} %get-tuple-element.76), channel_id=1, source_target_pairs={{0,8},{8,0},{16,24},{24,16},{1,9},{9,1},{17,25},{25,17},{2,10},{10... | collective-permute-start | bytes 393224 | tf_op jit(solution)/shard_map/ppermute | solution.py:312
  39.1 20.7 %collective-permute-start.18 = (bf16[2,2,64,256]{3,2,1,0:T(8,128)(2,1)S(1)}, bf16[2,2,64,256]{3,2,1,0:T(8,128)(2,1)S(1)}, u32[]{:S(2)}, u32[]{:S(2)}) collective-permute-start(bf16[2,2,64,256]{3,2,1,0:T(8,128)(2,1)S(1)} %get-tuple-element.77), channel_id=1, source_target_pairs={{0,16},{8,24},{16,0},{24,8},{1,17},{9,25},{17,1},{25,9},{2,18},{10... | collective-permute-start | bytes 393224 | tf_op jit(solution)/shard_map/ppermute | solution.py:312
  42.0 17.8 %collective-permute-start.19 = (bf16[2,2,64,256]{3,2,1,0:T(8,128)(2,1)S(1)}, bf16[2,2,64,256]{3,2,1,0:T(8,128)(2,1)S(1)}, u32[]{:S(2)}, u32[]{:S(2)}) collective-permute-start(bf16[2,2,64,256]{3,2,1,0:T(8,128)(2,1)S(1)} %get-tuple-element.78), channel_id=1, source_target_pairs={{0,24},{8,16},{16,8},{24,0},{1,25},{9,17},{17,9},{25,1},{2,26},{10... | collective-permute-start | bytes 393224 | tf_op jit(solution)/shard_map/ppermute | solution.py:312
  45.7 1.3 %copy-start.2 = (f32[512]{0:T(512)S(1)}, f32[512]{0:T(512)}, u32[]{:S(2)}) copy-start(f32[512]{0:T(512)} %param.11) | copy-start | bytes 6148
  47.5 12.2 %copy-start.5 = (s32[2]{0:T(128)S(1)}, s32[2]{0:T(128)}, u32[]{:S(2)}) copy-start(s32[2]{0:T(128)} %copy-done.4) | copy-start | bytes 28
  53.1 0.7 copy-start.10
  55.3 10.3 %collective-permute-start.14 = (bf16[2,2,64,256]{3,2,1,0:T(8,128)(2,1)S(1)}, bf16[2,2,64,256]{3,2,1,0:T(8,128)(2,1)S(1)}, u32[]{:S(2)}, u32[]{:S(2)}) collective-permute-start(bf16[2,2,64,256]{3,2,1,0:T(8,128)(2,1)S(1)} %get-tuple-element.71.refs_1_), channel_id=1, source_target_pairs={{0,8},{8,0},{16,24},{24,16},{1,9},{9,1},{17,25},{25,17},{2,10},{10... | collective-permute-start | bytes 393224 | tf_op jit(solution)/shard_map/ppermute | solution.py:312
  56.6 13.1 %collective-permute-start.15 = (bf16[2,2,64,256]{3,2,1,0:T(8,128)(2,1)S(1)}, bf16[2,2,64,256]{3,2,1,0:T(8,128)(2,1)S(1)}, u32[]{:S(2)}, u32[]{:S(2)}) collective-permute-start(bf16[2,2,64,256]{3,2,1,0:T(8,128)(2,1)S(1)} %get-tuple-element.72.refs_2_), channel_id=1, source_target_pairs={{0,16},{8,24},{16,0},{24,8},{1,17},{9,25},{17,1},{25,9},{2,18},{10... | collective-permute-start | bytes 393224 | tf_op jit(solution)/shard_map/ppermute | solution.py:312
  59.5 10.2 %collective-permute-start.16 = (bf16[2,2,64,256]{3,2,1,0:T(8,128)(2,1)S(1)}, bf16[2,2,64,256]{3,2,1,0:T(8,128)(2,1)S(1)}, u32[]{:S(2)}, u32[]{:S(2)}) collective-permute-start(bf16[2,2,64,256]{3,2,1,0:T(8,128)(2,1)S(1)} %get-tuple-element.73.refs_3_), channel_id=1, source_target_pairs={{0,24},{8,16},{16,8},{24,0},{1,25},{9,17},{17,9},{25,1},{2,26},{10... | collective-permute-start | bytes 393224 | tf_op jit(solution)/shard_map/ppermute | solution.py:312
  59.8 9.9 %copy-start.6 = (f32[8]{0:T(128)S(1)}, f32[8]{0:T(128)}, u32[]{:S(2)}) copy-start(f32[8]{0:T(128)} %occ.9) | copy-start | bytes 100
  61.4 22.2 %collective-permute-start.20 = (bf16[2,2,64,256]{3,2,1,0:T(8,128)(2,1)S(1)}, bf16[2,2,64,256]{3,2,1,0:T(8,128)(2,1)S(1)}, u32[]{:S(2)}, u32[]{:S(2)}) collective-permute-start(bf16[2,2,64,256]{3,2,1,0:T(8,128)(2,1)S(1)} %get-tuple-element.80.refs_2_), channel_id=1, source_target_pairs={{0,8},{8,0},{16,24},{24,16},{1,9},{9,1},{17,25},{25,17},{2,10},{10... | collective-permute-start | bytes 393224 | tf_op jit(solution)/shard_map/ppermute | solution.py:312
  61.8 23.4 %collective-permute-start.21 = (bf16[2,2,64,256]{3,2,1,0:T(8,128)(2,1)S(1)}, bf16[2,2,64,256]{3,2,1,0:T(8,128)(2,1)S(1)}, u32[]{:S(2)}, u32[]{:S(2)}) collective-permute-start(bf16[2,2,64,256]{3,2,1,0:T(8,128)(2,1)S(1)} %get-tuple-element.81.refs_3_), channel_id=1, source_target_pairs={{0,16},{8,24},{16,0},{24,8},{1,17},{9,25},{17,1},{25,9},{2,18},{10... | collective-permute-start | bytes 393224 | tf_op jit(solution)/shard_map/ppermute | solution.py:312
  65.6 19.6 %collective-permute-start.22 = (bf16[2,2,64,256]{3,2,1,0:T(8,128)(2,1)S(1)}, bf16[2,2,64,256]{3,2,1,0:T(8,128)(2,1)S(1)}, u32[]{:S(2)}, u32[]{:S(2)}) collective-permute-start(bf16[2,2,64,256]{3,2,1,0:T(8,128)(2,1)S(1)} %get-tuple-element.82.refs_4_), channel_id=1, source_target_pairs={{0,24},{8,16},{16,8},{24,0},{1,25},{9,17},{17,9},{25,1},{2,26},{10... | collective-permute-start | bytes 393224 | tf_op jit(solution)/shard_map/ppermute | solution.py:312
  72.2 0.8 copy-start.8
  73.0 22.4 %collective-permute-start.26 = (bf16[2,2,64,256]{3,2,1,0:T(8,128)(2,1)S(1)}, bf16[2,2,64,256]{3,2,1,0:T(8,128)(2,1)S(1)}, u32[]{:S(2)}, u32[]{:S(2)}) collective-permute-start(bf16[2,2,64,256]{3,2,1,0:T(8,128)(2,1)S(1)} %get-tuple-element.90), channel_id=1, source_target_pairs={{0,8},{8,0},{16,24},{24,16},{1,9},{9,1},{17,25},{25,17},{2,10},{10... | collective-permute-start | bytes 393224 | tf_op jit(solution)/shard_map/ppermute | solution.py:312
  82.9 14.1 %collective-permute-start.27 = (bf16[2,2,64,256]{3,2,1,0:T(8,128)(2,1)S(1)}, bf16[2,2,64,256]{3,2,1,0:T(8,128)(2,1)S(1)}, u32[]{:S(2)}, u32[]{:S(2)}) collective-permute-start(bf16[2,2,64,256]{3,2,1,0:T(8,128)(2,1)S(1)} %get-tuple-element.91), channel_id=1, source_target_pairs={{0,16},{8,24},{16,0},{24,8},{1,17},{9,25},{17,1},{25,9},{2,18},{10... | collective-permute-start | bytes 393224 | tf_op jit(solution)/shard_map/ppermute | solution.py:312
  83.6 13.4 %collective-permute-start.28 = (bf16[2,2,64,256]{3,2,1,0:T(8,128)(2,1)S(1)}, bf16[2,2,64,256]{3,2,1,0:T(8,128)(2,1)S(1)}, u32[]{:S(2)}, u32[]{:S(2)}) collective-permute-start(bf16[2,2,64,256]{3,2,1,0:T(8,128)(2,1)S(1)} %get-tuple-element.92), channel_id=1, source_target_pairs={{0,24},{8,16},{16,8},{24,0},{1,25},{9,17},{17,9},{25,1},{2,26},{10... | collective-permute-start | bytes 393224 | tf_op jit(solution)/shard_map/ppermute | solution.py:312
  88.9 10.2 %collective-permute-start.23 = (bf16[2,2,64,256]{3,2,1,0:T(8,128)(2,1)S(1)}, bf16[2,2,64,256]{3,2,1,0:T(8,128)(2,1)S(1)}, u32[]{:S(2)}, u32[]{:S(2)}) collective-permute-start(bf16[2,2,64,256]{3,2,1,0:T(8,128)(2,1)S(1)} %get-tuple-element.86), channel_id=1, source_target_pairs={{0,8},{8,0},{16,24},{24,16},{1,9},{9,1},{17,25},{25,17},{2,10},{10... | collective-permute-start | bytes 393224 | tf_op jit(solution)/shard_map/ppermute | solution.py:312
  90.0 9.1 %collective-permute-start.24 = (bf16[2,2,64,256]{3,2,1,0:T(8,128)(2,1)S(1)}, bf16[2,2,64,256]{3,2,1,0:T(8,128)(2,1)S(1)}, u32[]{:S(2)}, u32[]{:S(2)}) collective-permute-start(bf16[2,2,64,256]{3,2,1,0:T(8,128)(2,1)S(1)} %get-tuple-element.87), channel_id=1, source_target_pairs={{0,16},{8,24},{16,0},{24,8},{1,17},{9,25},{17,1},{25,9},{2,18},{10... | collective-permute-start | bytes 393224 | tf_op jit(solution)/shard_map/ppermute | solution.py:312
  91.6 21.9 %all-to-all-start.1 = ((bf16[8,2,128,256]{3,2,1,0:T(8,128)(2,1)}), bf16[8,2,128,256]{3,2,1,0:T(8,128)(2,1)S(1)}, u32[]{:S(2)}, u32[]{:S(2)}) async-start(bf16[8,2,128,256]{3,2,1,0:T(8,128)(2,1)} %get-tuple-element.83), calls=%async_computation.1 | async-start | bytes 2097152 | tf_op jit(solution)/shard_map/all_to_all | solution.py:299
  95.4 7.8 %collective-permute-start.25 = (bf16[2,2,64,256]{3,2,1,0:T(8,128)(2,1)S(1)}, bf16[2,2,64,256]{3,2,1,0:T(8,128)(2,1)S(1)}, u32[]{:S(2)}, u32[]{:S(2)}) collective-permute-start(bf16[2,2,64,256]{3,2,1,0:T(8,128)(2,1)S(1)} %get-tuple-element.88), channel_id=1, source_target_pairs={{0,24},{8,16},{16,8},{24,0},{1,25},{9,17},{17,9},{25,1},{2,26},{10... | collective-permute-start | bytes 393224 | tf_op jit(solution)/shard_map/ppermute | solution.py:312
  97.0 1.0 copy-start.9
  103.2 10.3 %copy-start.3 = (f32[512]{0:T(512)S(1)}, f32[512]{0:T(512)}, u32[]{:S(2)}) copy-start(f32[512]{0:T(512)} %param.11) | copy-start | bytes 6148
  104.4 4.1 %collective-permute-start.29 = (bf16[2,128,256]{2,1,0:T(8,128)(2,1)S(1)}, bf16[2,128,256]{2,1,0:T(8,128)(2,1)S(1)}, u32[]{:S(2)}, u32[]{:S(2)}) collective-permute-start(bf16[2,128,256]{2,1,0:T(8,128)(2,1)S(1)} %get-tuple-element.94), channel_id=1, source_target_pairs={{0,1},{1,0},{2,3},{3,2},{4,5},{5,4},{6,7},{7,6},{8,9},{9,8},{10,11... | collective-permute-start | bytes 393224 | tf_op jit(solution)/shard_map/ppermute | solution.py:305
  104.5 8.7 %collective-permute-start.30 = (bf16[2,128,256]{2,1,0:T(8,128)(2,1)S(1)}, bf16[2,128,256]{2,1,0:T(8,128)(2,1)S(1)}, u32[]{:S(2)}, u32[]{:S(2)}) collective-permute-start(bf16[2,128,256]{2,1,0:T(8,128)(2,1)S(1)} %get-tuple-element.95), channel_id=1, source_target_pairs={{0,2},{1,3},{2,0},{3,1},{4,6},{5,7},{6,4},{7,5},{8,10},{9,11},{10,... | collective-permute-start | bytes 393224 | tf_op jit(solution)/shard_map/ppermute | solution.py:305
  106.2 16.6 %collective-permute-start.31 = (bf16[2,128,256]{2,1,0:T(8,128)(2,1)S(1)}, bf16[2,128,256]{2,1,0:T(8,128)(2,1)S(1)}, u32[]{:S(2)}, u32[]{:S(2)}) collective-permute-start(bf16[2,128,256]{2,1,0:T(8,128)(2,1)S(1)} %get-tuple-element.96), channel_id=1, source_target_pairs={{0,3},{1,2},{2,1},{3,0},{4,7},{5,6},{6,5},{7,4},{8,11},{9,10},{10,... | collective-permute-start | bytes 393224 | tf_op jit(solution)/shard_map/ppermute | solution.py:305
  106.3 16.5 %collective-permute-start.32 = (bf16[2,128,256]{2,1,0:T(8,128)(2,1)S(1)}, bf16[2,128,256]{2,1,0:T(8,128)(2,1)S(1)}, u32[]{:S(2)}, u32[]{:S(2)}) collective-permute-start(bf16[2,128,256]{2,1,0:T(8,128)(2,1)S(1)} %get-tuple-element.97), channel_id=1, source_target_pairs={{0,4},{1,5},{2,6},{3,7},{4,0},{5,1},{6,2},{7,3},{8,12},{9,13},{10,... | collective-permute-start | bytes 393224 | tf_op jit(solution)/shard_map/ppermute | solution.py:305
  108.5 14.3 %collective-permute-start.33 = (bf16[2,128,256]{2,1,0:T(8,128)(2,1)S(1)}, bf16[2,128,256]{2,1,0:T(8,128)(2,1)S(1)}, u32[]{:S(2)}, u32[]{:S(2)}) collective-permute-start(bf16[2,128,256]{2,1,0:T(8,128)(2,1)S(1)} %get-tuple-element.98), channel_id=1, source_target_pairs={{0,5},{1,4},{2,7},{3,6},{4,1},{5,0},{6,3},{7,2},{8,13},{9,12},{10,... | collective-permute-start | bytes 393224 | tf_op jit(solution)/shard_map/ppermute | solution.py:305
  108.5 14.3 %collective-permute-start.34 = (bf16[2,128,256]{2,1,0:T(8,128)(2,1)S(1)}, bf16[2,128,256]{2,1,0:T(8,128)(2,1)S(1)}, u32[]{:S(2)}, u32[]{:S(2)}) collective-permute-start(bf16[2,128,256]{2,1,0:T(8,128)(2,1)S(1)} %get-tuple-element.99), channel_id=1, source_target_pairs={{0,6},{1,7},{2,4},{3,5},{4,2},{5,3},{6,0},{7,1},{8,14},{9,15},{10,... | collective-permute-start | bytes 393224 | tf_op jit(solution)/shard_map/ppermute | solution.py:305
  113.2 9.6 %collective-permute-start.35 = (bf16[2,128,256]{2,1,0:T(8,128)(2,1)S(1)}, bf16[2,128,256]{2,1,0:T(8,128)(2,1)S(1)}, u32[]{:S(2)}, u32[]{:S(2)}) collective-permute-start(bf16[2,128,256]{2,1,0:T(8,128)(2,1)S(1)} %get-tuple-element.100), channel_id=1, source_target_pairs={{0,7},{1,6},{2,5},{3,4},{4,3},{5,2},{6,1},{7,0},{8,15},{9,14},{10,... | collective-permute-start | bytes 393224 | tf_op jit(solution)/shard_map/ppermute | solution.py:305
  113.6 1.4 %copy-start.7 = (bf16[512,1536]{1,0:T(8,128)(2,1)S(1)}, bf16[512,1536]{1,0:T(8,128)(2,1)}, u32[]{:S(2)}) copy-start(bf16[512,1536]{1,0:T(8,128)(2,1)} %get-tuple-element.84.whole) | copy-start | bytes 4718596

commit v20 on v14

--- a/solution.py
+++ b/solution.py
@@ -455,7 +455,6 @@
         out_specs=by_pair(virtual, virtual),
         scratch_shapes=[pltpu.VMEM((devices, 1, edge, 2 * edge), NARROW)],
         compiler_params=PARAMS,
-        input_output_aliases={1: 0},
         cost_estimate=pl.CostEstimate(flops=count, bytes_accessed=10 * count, transcendentals=0),
     )(place, base, *by_distance(last))
     return done.reshape(amplitudes.shape)

time: 127 us -> 128 us (level)
  local copies, waits for them, and re-layouts: 6.95 us -> 8.62 us
    unnamed x28 -> x30, local copies, waits for them, and re-layouts: 5.43 us -> 7.1 us
  transfers between devices with their start and end apart: 38 -> 38, of which waited for: 7 -> 7; matrix products, arithmetic and copies ran while one was open for 2% -> 1% of each run, Pallas kernels for 22% -> 22%
where the time goes in v20:
time: 128 us; the launch traced here: 127 us
  starting transfers between devices  66.5 us (52%)
  Pallas kernels  30.3 us (24%)
  waiting for transfers between devices  19.2 us (15%)
  local copies, waits for them, and re-layouts  8.62 us (7%)
  between operations  1.64 us (1%)
    ppermute x18, starting transfers between devices, across_first(): lax.ppermute(parts[s], 'occi', [(k, k ^ s) for k in range(groups)])  35.3 us
    pallas_call x9, Pallas kernels, call(): pl.pallas_call(body, out_shape=outs, in_specs=specs, out_specs=jax.tree.m...  19.3 us
    ppermute x14, starting transfers between devices, by_distance(): lax.ppermute(parts[k], 'occj', [(d, d ^ k) for d in range(devices)])  16.4 us
    all_to_all x2, starting transfers between devices, exchange(): lax.all_to_all(blocks, 'occj', split_axis=0, concat_axis=0, tiled=True)  10.2 us
    pallas_call x1, Pallas kernels, local(): pl.pallas_call(functools.partial(second_ladder_kernel, tiles, first), gri...  7.79 us
    all_to_all x2, waiting for transfers between devices, exchange(): lax.all_to_all(blocks, 'occj', split_axis=0, concat_axis=0, tiled=True)  7.73 us
    unnamed x30, local copies, waits for them, and re-layouts  7.1 us
    ppermute x18, waiting for transfers between devices, across_first(): lax.ppermute(parts[s], 'occi', [(k, k ^ s) for k in range(groups)])  6.87 us
  transfers between devices with their start and end apart: 38, of which 7 were waited for; matrix products, arithmetic and copies ran while one was open for 1% of the time, Pallas kernels for 22%

profile of v20, /device:TPU:0, one launch (start us, length us, event | category | flops | bytes accessed | tf_op | source)
XLA Modules:
  0.0 126.6 jit_solution(15672547964429910394)
XLA Ops:
  0.0 3.0 %collective-permute-start = (bf16[3,64,512]{2,1,0:T(8,128)(2,1)}, bf16[3,64,512]{2,1,0:T(8,128)(2,1)S(1)}, u32[]{:S(2)}, u32[]{:S(2)}) collective-permute-start(bf16[3,64,512]{2,1,0:T(8,128)(2,1)} %refs_0_.1), channel_id=1, source_target_pairs={{0,2},{1,3},{2,0},{3,1},{4,6},{5,7},{6,4},{7,5},{8,10},{9,11},{10,... | collective-permute-start | bytes 589832 | tf_op jit(solution)/shard_map/ppermute | solution.py:338
  3.0 1.5 %collective-permute-start.1 = (bf16[3,64,512]{2,1,0:T(8,128)(2,1)}, bf16[3,64,512]{2,1,0:T(8,128)(2,1)S(1)}, u32[]{:S(2)}, u32[]{:S(2)}) collective-permute-start(bf16[3,64,512]{2,1,0:T(8,128)(2,1)} %refs_0_.1), channel_id=1, source_target_pairs={{0,4},{1,5},{2,6},{3,7},{4,0},{5,1},{6,2},{7,3},{8,12},{9,13},{10,... | collective-permute-start | bytes 589832 | tf_op jit(solution)/shard_map/ppermute | solution.py:338
  4.6 1.6 %copy-done = f32[2,1,512,512]{3,2,1,0:T(8,128)S(1)} copy-done((f32[2,1,512,512]{3,2,1,0:T(8,128)S(1)}, f32[2,1,512,512]{3,2,1,0:T(8,128)}, u32[]{:S(2)}) %copy-start) | copy-done | bytes 2097176
  6.2 0.9 shard_map.73
  7.1 1.6 %collective-permute-start.10 = (bf16[2,128,256]{2,1,0:T(8,128)(2,1)S(1)}, bf16[2,128,256]{2,1,0:T(8,128)(2,1)S(1)}, u32[]{:S(2)}, u32[]{:S(2)}) collective-permute-start(bf16[2,128,256]{2,1,0:T(8,128)(2,1)S(1)} %get-tuple-element.62), channel_id=1, source_target_pairs={{0,7},{1,6},{2,5},{3,4},{4,3},{5,2},{6,1},{7,0},{8,15},{9,14},{10,... | collective-permute-start | bytes 393224 | tf_op jit(solution)/shard_map/ppermute | solution.py:305
  8.7 1.5 %collective-permute-start.4 = (bf16[2,128,256]{2,1,0:T(8,128)(2,1)S(1)}, bf16[2,128,256]{2,1,0:T(8,128)(2,1)S(1)}, u32[]{:S(2)}, u32[]{:S(2)}) collective-permute-start(bf16[2,128,256]{2,1,0:T(8,128)(2,1)S(1)} %get-tuple-element.56), channel_id=1, source_target_pairs={{0,1},{1,0},{2,3},{3,2},{4,5},{5,4},{6,7},{7,6},{8,9},{9,8},{10,11... | collective-permute-start | bytes 393224 | tf_op jit(solution)/shard_map/ppermute | solution.py:305
  10.2 0.6 dynamic_slice.14
  11.4 0.6 dynamic_slice.12
  12.7 0.6 collective-permute-start.5
  13.3 2.5 %collective-permute-done.1.refs_2_ = bf16[3,64,512]{2,1,0:T(8,128)(2,1)S(1)} collective-permute-done((bf16[3,64,512]{2,1,0:T(8,128)(2,1)}, bf16[3,64,512]{2,1,0:T(8,128)(2,1)S(1)}, u32[]{:S(2)}, u32[]{:S(2)}) %collective-permute-start.1) | collective-permute-done | bytes 196640 | tf_op jit(solution)/shard_map/ppermute | solution.py:338
  15.8 0.1 pad_maximum_fusion
  16.0 0.1 fusion
  16.2 0.1 broadcast_add_fusion.2
  16.3 2.4 %collective-permute-start.7 = (bf16[2,128,256]{2,1,0:T(8,128)(2,1)S(1)}, bf16[2,128,256]{2,1,0:T(8,128)(2,1)S(1)}, u32[]{:S(2)}, u32[]{:S(2)}) collective-permute-start(bf16[2,128,256]{2,1,0:T(8,128)(2,1)S(1)} %get-tuple-element.59), channel_id=1, source_target_pairs={{0,4},{1,5},{2,6},{3,7},{4,0},{5,1},{6,2},{7,3},{8,12},{9,13},{10,... | collective-permute-start | bytes 393224 | tf_op jit(solution)/shard_map/ppermute | solution.py:305
  18.8 0.2 collective-permute-start.8
  18.9 2.9 %collective-permute-start.9 = (bf16[2,128,256]{2,1,0:T(8,128)(2,1)S(1)}, bf16[2,128,256]{2,1,0:T(8,128)(2,1)S(1)}, u32[]{:S(2)}, u32[]{:S(2)}) collective-permute-start(bf16[2,128,256]{2,1,0:T(8,128)(2,1)S(1)} %get-tuple-element.61), channel_id=1, source_target_pairs={{0,6},{1,7},{2,4},{3,5},{4,2},{5,3},{6,0},{7,1},{8,14},{9,15},{10,... | collective-permute-start | bytes 393224 | tf_op jit(solution)/shard_map/ppermute | solution.py:305
  21.8 6.3 %shard_map.74 = (bf16[8,2,128,256]{3,2,1,0:T(8,128)(2,1)}, bf16[512,1536]{1,0:T(8,128)(2,1)}) custom-call(s32[2]{0:T(128)S(1)} %pad_add_fusion.place.source, f32[2,512,512]{2,1,0:T(8,128)} %bitcast.13, bf16[3,64,512]{2,1,0:T(8,128)(2,1)S(1)} %copy-done.2, bf16[3,64,512]{2,1,0:T(8,128)(2,1)S(1)} %collective-permute-done.refs_1_, ...), custom_call_target="tpu_custom_call" | custom-call | flops 3221225472 | bytes 4194304 | tf_op jit(solution)/shard_map/pallas_call | solution.py:42
  28.1 0.2 collective-permute-done.8.refs_5_
  28.3 0.7 shard_map.75
  29.0 1.6 %collective-permute-start.11 = (bf16[2,2,64,256]{3,2,1,0:T(8,128)(2,1)S(1)}, bf16[2,2,64,256]{3,2,1,0:T(8,128)(2,1)S(1)}, u32[]{:S(2)}, u32[]{:S(2)}) collective-permute-start(bf16[2,2,64,256]{3,2,1,0:T(8,128)(2,1)S(1)} %get-tuple-element.64), channel_id=1, source_target_pairs={{0,8},{8,0},{16,24},{24,16},{1,9},{9,1},{17,25},{25,17},{2,10},{10... | collective-permute-start | bytes 393224 | tf_op jit(solution)/shard_map/ppermute | solution.py:312
  30.6 2.6 %collective-permute-start.12 = (bf16[2,2,64,256]{3,2,1,0:T(8,128)(2,1)S(1)}, bf16[2,2,64,256]{3,2,1,0:T(8,128)(2,1)S(1)}, u32[]{:S(2)}, u32[]{:S(2)}) collective-permute-start(bf16[2,2,64,256]{3,2,1,0:T(8,128)(2,1)S(1)} %get-tuple-element.65), channel_id=1, source_target_pairs={{0,16},{8,24},{16,0},{24,8},{1,17},{9,25},{17,1},{25,9},{2,18},{10... | collective-permute-start | bytes 393224 | tf_op jit(solution)/shard_map/ppermute | solution.py:312
  33.2 0.2 collective-permute-start.13
  33.6 3.6 %all-to-all-start = ((bf16[8,2,128,256]{3,2,1,0:T(8,128)(2,1)}), bf16[8,2,128,256]{3,2,1,0:T(8,128)(2,1)S(1)}, u32[]{:S(2)}, u32[]{:S(2)}) async-start(bf16[8,2,128,256]{3,2,1,0:T(8,128)(2,1)} %get-tuple-element.54), calls=%async_computation | async-start | bytes 2097152 | tf_op jit(solution)/shard_map/all_to_all | solution.py:299
  37.2 0.7 collective-permute-start.17
  37.9 3.5 %collective-permute-start.18 = (bf16[2,2,64,256]{3,2,1,0:T(8,128)(2,1)S(1)}, bf16[2,2,64,256]{3,2,1,0:T(8,128)(2,1)S(1)}, u32[]{:S(2)}, u32[]{:S(2)}) collective-permute-start(bf16[2,2,64,256]{3,2,1,0:T(8,128)(2,1)S(1)} %get-tuple-element.75), channel_id=1, source_target_pairs={{0,16},{8,24},{16,0},{24,8},{1,17},{9,25},{17,1},{25,9},{2,18},{10... | collective-permute-start | bytes 393224 | tf_op jit(solution)/shard_map/ppermute | solution.py:312
  41.4 0.2 collective-permute-start.19
  41.6 1.9 %collective-permute-done.12.refs_2_ = bf16[2,2,64,256]{3,2,1,0:T(8,128)(2,1)S(1)} collective-permute-done((bf16[2,2,64,256]{3,2,1,0:T(8,128)(2,1)S(1)}, bf16[2,2,64,256]{3,2,1,0:T(8,128)(2,1)S(1)}, u32[]{:S(2)}, u32[]{:S(2)}) %collective-permute-start.12) | collective-permute-done | bytes 131104 | tf_op jit(solution)/shard_map/ppermute | solution.py:312
  43.6 1.2 shard_map.76.place
  44.8 7.7 %all-to-all-done.ladder = bf16[8,2,128,256]{3,2,1,0:T(8,128)(2,1)S(1)} async-done(((bf16[8,2,128,256]{3,2,1,0:T(8,128)(2,1)}), bf16[8,2,128,256]{3,2,1,0:T(8,128)(2,1)S(1)}, u32[]{:S(2)}, u32[]{:S(2)}) %all-to-all-start) | async-done | bytes 1048608 | tf_op jit(solution)/shard_map/all_to_all | solution.py:299
  52.5 0.7 copy-done.11
  53.2 1.6 %shard_map.77 = (bf16[2,2,64,256]{3,2,1,0:T(8,128)(2,1)S(1)}, bf16[2,2,64,256]{3,2,1,0:T(8,128)(2,1)S(1)}, bf16[2,2,64,256]{3,2,1,0:T(8,128)(2,1)S(1)}, bf16[2,2,64,256]{3,2,1,0:T(8,128)(2,1)S(1)}) custom-call(s32[2]{0:T(128)S(1)} %copy-done.11, f32[8,8]{1,0:T(8,128)S(1)} %convert_element_type.3.fock, bf16[8,2,128,256]{3,2,1,0:T(8,128)(2,1)S(1)} %all-to-all-done.ladder, ...), custom_call_target="tpu_custom_call" | custom-call | flops 30000001024 | bytes 3145728 | tf_op jit(solution)/shard_map/pallas_call | solution.py:42
  54.7 1.3 %collective-permute-start.14 = (bf16[2,2,64,256]{3,2,1,0:T(8,128)(2,1)S(1)}, bf16[2,2,64,256]{3,2,1,0:T(8,128)(2,1)S(1)}, u32[]{:S(2)}, u32[]{:S(2)}) collective-permute-start(bf16[2,2,64,256]{3,2,1,0:T(8,128)(2,1)S(1)} %get-tuple-element.69.refs_1_), channel_id=1, source_target_pairs={{0,8},{8,0},{16,24},{24,16},{1,9},{9,1},{17,25},{25,17},{2,10},{10... | collective-permute-start | bytes 393224 | tf_op jit(solution)/shard_map/ppermute | solution.py:312
  56.1 2.9 %collective-permute-start.15 = (bf16[2,2,64,256]{3,2,1,0:T(8,128)(2,1)S(1)}, bf16[2,2,64,256]{3,2,1,0:T(8,128)(2,1)S(1)}, u32[]{:S(2)}, u32[]{:S(2)}) collective-permute-start(bf16[2,2,64,256]{3,2,1,0:T(8,128)(2,1)S(1)} %get-tuple-element.70.refs_2_), channel_id=1, source_target_pairs={{0,16},{8,24},{16,0},{24,8},{1,17},{9,25},{17,1},{25,9},{2,18},{10... | collective-permute-start | bytes 393224 | tf_op jit(solution)/shard_map/ppermute | solution.py:312
  59.0 0.2 collective-permute-start.16
  59.2 1.6 %shard_map.79 = (bf16[2,2,64,256]{3,2,1,0:T(8,128)(2,1)S(1)}, bf16[2,2,64,256]{3,2,1,0:T(8,128)(2,1)S(1)}, bf16[2,2,64,256]{3,2,1,0:T(8,128)(2,1)S(1)}, bf16[2,2,64,256]{3,2,1,0:T(8,128)(2,1)S(1)}) custom-call(s32[2]{0:T(128)S(1)} %copy-done.6, f32[8,8]{1,0:T(8,128)S(1)} %convert_element_type.3.fock, bf16[8,2,128,256]{3,2,1,0:T(8,128)(2,1)S(1)} %all-to-all-done.ladder, ...), custom_call_target="tpu_custom_call" | custom-call | flops 30000001024 | bytes 3145728 | tf_op jit(solution)/shard_map/pallas_call | solution.py:42
  60.8 0.4 collective-permute-start.20
  61.2 3.8 %collective-permute-start.21 = (bf16[2,2,64,256]{3,2,1,0:T(8,128)(2,1)S(1)}, bf16[2,2,64,256]{3,2,1,0:T(8,128)(2,1)S(1)}, u32[]{:S(2)}, u32[]{:S(2)}) collective-permute-start(bf16[2,2,64,256]{3,2,1,0:T(8,128)(2,1)S(1)} %get-tuple-element.79.refs_3_), channel_id=1, source_target_pairs={{0,16},{8,24},{16,0},{24,8},{1,17},{9,25},{17,1},{25,9},{2,18},{10... | collective-permute-start | bytes 393224 | tf_op jit(solution)/shard_map/ppermute | solution.py:312
  65.0 3.0 %collective-permute-start.22 = (bf16[2,2,64,256]{3,2,1,0:T(8,128)(2,1)S(1)}, bf16[2,2,64,256]{3,2,1,0:T(8,128)(2,1)S(1)}, u32[]{:S(2)}, u32[]{:S(2)}) collective-permute-start(bf16[2,2,64,256]{3,2,1,0:T(8,128)(2,1)S(1)} %get-tuple-element.80.refs_4_), channel_id=1, source_target_pairs={{0,24},{8,16},{16,8},{24,0},{1,25},{9,17},{17,9},{25,1},{2,26},{10... | collective-permute-start | bytes 393224 | tf_op jit(solution)/shard_map/ppermute | solution.py:312
  68.1 0.9 collective-permute-done.15.refs_6_
  68.9 2.5 %shard_map.78 = (bf16[8,2,64,256]{3,2,1,0:T(8,128)(2,1)S(1)}, bf16[2,8,64,256]{3,2,1,0:T(8,128)(2,1)S(1)}, bf16[2,2,64,256]{3,2,1,0:T(8,128)(2,1)S(1)}, bf16[2,2...) custom-call(s32[2]{0:T(128)S(1)} %copy-done.6, f32[8,8]{1,0:T(8,128)S(1)} %convert_element_type.3.fock, ...), custom_call_target="tpu_custom_call" | custom-call | flops 30000001024 | bytes 5242880 | tf_op jit(solution)/shard_map/pallas_call | solution.py:42
  71.5 0.8 copy-done.9
  72.3 7.2 %collective-permute-start.26 = (bf16[2,2,64,256]{3,2,1,0:T(8,128)(2,1)S(1)}, bf16[2,2,64,256]{3,2,1,0:T(8,128)(2,1)S(1)}, u32[]{:S(2)}, u32[]{:S(2)}) collective-permute-start(bf16[2,2,64,256]{3,2,1,0:T(8,128)(2,1)S(1)} %get-tuple-element.88), channel_id=1, source_target_pairs={{0,8},{8,0},{16,24},{24,16},{1,9},{9,1},{17,25},{25,17},{2,10},{10... | collective-permute-start | bytes 393224 | tf_op jit(solution)/shard_map/ppermute | solution.py:312
  79.5 0.8 collective-permute-start.27
  80.2 1.6 %collective-permute-start.28 = (bf16[2,2,64,256]{3,2,1,0:T(8,128)(2,1)S(1)}, bf16[2,2,64,256]{3,2,1,0:T(8,128)(2,1)S(1)}, u32[]{:S(2)}, u32[]{:S(2)}) collective-permute-start(bf16[2,2,64,256]{3,2,1,0:T(8,128)(2,1)S(1)} %get-tuple-element.90), channel_id=1, source_target_pairs={{0,24},{8,16},{16,8},{24,0},{1,25},{9,17},{17,9},{25,1},{2,26},{10... | collective-permute-start | bytes 393224 | tf_op jit(solution)/shard_map/ppermute | solution.py:312
  81.8 3.6 %shard_map.80 = (bf16[8,2,128,256]{3,2,1,0:T(8,128)(2,1)}, bf16[2,8,64,256]{3,2,1,0:T(8,128)(2,1)S(1)}, bf16[2,2,64,256]{3,2,1,0:T(8,128)(2,1)S(1)}, bf16[2,2,64...) custom-call(s32[2]{0:T(128)S(1)} %copy-done.6, f32[8,8]{1,0:T(8,128)S(1)} %convert_element_type.3.fock, ...), custom_call_target="tpu_custom_call" | custom-call | flops 30000001024 | bytes 5242880 | tf_op jit(solution)/shard_map/pallas_call | solution.py:42
  85.4 2.7 %collective-permute-start.23 = (bf16[2,2,64,256]{3,2,1,0:T(8,128)(2,1)S(1)}, bf16[2,2,64,256]{3,2,1,0:T(8,128)(2,1)S(1)}, u32[]{:S(2)}, u32[]{:S(2)}) collective-permute-start(bf16[2,2,64,256]{3,2,1,0:T(8,128)(2,1)S(1)} %get-tuple-element.84), channel_id=1, source_target_pairs={{0,8},{8,0},{16,24},{24,16},{1,9},{9,1},{17,25},{25,17},{2,10},{10... | collective-permute-start | bytes 393224 | tf_op jit(solution)/shard_map/ppermute | solution.py:312
  88.2 0.8 collective-permute-start.24
  88.9 6.6 %all-to-all-start.1 = ((bf16[8,2,128,256]{3,2,1,0:T(8,128)(2,1)}), bf16[8,2,128,256]{3,2,1,0:T(8,128)(2,1)S(1)}, u32[]{:S(2)}, u32[]{:S(2)}) async-start(bf16[8,2,128,256]{3,2,1,0:T(8,128)(2,1)} %get-tuple-element.81), calls=%async_computation.1 | async-start | bytes 2097152 | tf_op jit(solution)/shard_map/all_to_all | solution.py:299
  95.5 1.7 %collective-permute-start.25 = (bf16[2,2,64,256]{3,2,1,0:T(8,128)(2,1)S(1)}, bf16[2,2,64,256]{3,2,1,0:T(8,128)(2,1)S(1)}, u32[]{:S(2)}, u32[]{:S(2)}) collective-permute-start(bf16[2,2,64,256]{3,2,1,0:T(8,128)(2,1)S(1)} %get-tuple-element.86), channel_id=1, source_target_pairs={{0,24},{8,16},{16,8},{24,0},{1,25},{9,17},{17,9},{25,1},{2,26},{10... | collective-permute-start | bytes 393224 | tf_op jit(solution)/shard_map/ppermute | solution.py:312
  97.2 1.0 copy-done.10
  98.3 1.1 shard_map.82.refs_3_
  99.4 4.0 %collective-permute-done.25.refs_2_ = bf16[2,2,64,256]{3,2,1,0:T(8,128)(2,1)S(1)} collective-permute-done((bf16[2,2,64,256]{3,2,1,0:T(8,128)(2,1)S(1)}, bf16[2,2,64,256]{3,2,1,0:T(8,128)(2,1)S(1)}, u32[]{:S(2)}, u32[]{:S(2)}) %collective-permute-start.25) | collective-permute-done | bytes 131104 | tf_op jit(solution)/shard_map/ppermute | solution.py:312
  103.4 1.2 shard_map.83
  104.6 1.7 %collective-permute-start.30 = (bf16[2,128,256]{2,1,0:T(8,128)(2,1)S(1)}, bf16[2,128,256]{2,1,0:T(8,128)(2,1)S(1)}, u32[]{:S(2)}, u32[]{:S(2)}) collective-permute-start(bf16[2,128,256]{2,1,0:T(8,128)(2,1)S(1)} %get-tuple-element.93), channel_id=1, source_target_pairs={{0,2},{1,3},{2,0},{3,1},{4,6},{5,7},{6,4},{7,5},{8,10},{9,11},{10,... | collective-permute-start | bytes 393224 | tf_op jit(solution)/shard_map/ppermute | solution.py:305
  106.3 0.1 collective-permute-start.31
  106.5 2.2 %collective-permute-start.32 = (bf16[2,128,256]{2,1,0:T(8,128)(2,1)S(1)}, bf16[2,128,256]{2,1,0:T(8,128)(2,1)S(1)}, u32[]{:S(2)}, u32[]{:S(2)}) collective-permute-start(bf16[2,128,256]{2,1,0:T(8,128)(2,1)S(1)} %get-tuple-element.95), channel_id=1, source_target_pairs={{0,4},{1,5},{2,6},{3,7},{4,0},{5,1},{6,2},{7,3},{8,12},{9,13},{10,... | collective-permute-start | bytes 393224 | tf_op jit(solution)/shard_map/ppermute | solution.py:305
  108.7 2.9 %collective-permute-start.34 = (bf16[2,128,256]{2,1,0:T(8,128)(2,1)S(1)}, bf16[2,128,256]{2,1,0:T(8,128)(2,1)S(1)}, u32[]{:S(2)}, u32[]{:S(2)}) collective-permute-start(bf16[2,128,256]{2,1,0:T(8,128)(2,1)S(1)} %get-tuple-element.97), channel_id=1, source_target_pairs={{0,6},{1,7},{2,4},{3,5},{4,2},{5,3},{6,0},{7,1},{8,14},{9,15},{10,... | collective-permute-start | bytes 393224 | tf_op jit(solution)/shard_map/ppermute | solution.py:305
  111.5 1.8 %collective-permute-done.30.refs_2_ = bf16[2,128,256]{2,1,0:T(8,128)(2,1)S(1)} collective-permute-done((bf16[2,128,256]{2,1,0:T(8,128)(2,1)S(1)}, bf16[2,128,256]{2,1,0:T(8,128)(2,1)S(1)}, u32[]{:S(2)}, u32[]{:S(2)}) %collective-permute-start.30) | collective-permute-done | bytes 131104 | tf_op jit(solution)/shard_map/ppermute | solution.py:305
  113.4 0.2 collective-permute-start.35
  113.6 0.1 broadcast_in_dim.4.row
  113.8 1.4 %copy-done.8 = bf16[512,1536]{1,0:T(8,128)(2,1)S(1)} copy-done((bf16[512,1536]{1,0:T(8,128)(2,1)S(1)}, bf16[512,1536]{1,0:T(8,128)(2,1)}, u32[]{:S(2)}) %copy-start.8) | copy-done | bytes 1572888
  115.2 7.8 %shard_map.81.source = f32[2,512,512]{2,1,0:T(8,128)} custom-call(s32[2]{0:T(128)S(1)} %copy-done.6, f32[8]{0:T(128)S(1)} %copy-done.7, f32[2,512,512]{2,1,0:T(8,128)} %bitcast.14, bf16[8,2,128,256]{3,2,1,0:T(8,128)(2,1)S(1)} %all-to-all-done.1.blocks, f32[512,128]{1,0:T(8,128)S(1)} %broadcast_in_dim.4.row, f32[1,512]{1,0:T(1,128)S(1)} %bitcast.20, ...), custom_call_target="tpu_custom_call" | custom-call | flops 3221225472 | bytes 6291456 | tf_op jit(solution)/shard_map/pallas_call | solution.py:427
  123.0 1.6 %copy-done.1 = f32[2,512,512]{2,1,0:T(8,128)S(1)} copy-done((f32[2,512,512]{2,1,0:T(8,128)S(1)}, f32[2,512,512]{2,1,0:T(8,128)}, u32[]{:S(2)}) %copy-start.1) | copy-done | bytes 2097176
  124.6 2.1 %shard_map.84 = f32[2,512,512]{2,1,0:T(8,128)} custom-call(s32[2]{0:T(128)S(1)} %copy-done.6, f32[2,512,512]{2,1,0:T(8,128)S(1)} %copy-done.1, bf16[2,128,256]{2,1,0:T(8,128)(2,1)S(1)} %get-tuple-element.91.refs_0_, bf16[2,128,256]{2,1,0:T(8,128)(2,1)S(1)} %collective-permute-done.29.refs_1_, bf16[2,128,256]{2,1,0:T(8,128)(2,1)S(1)} %collective-permute-done.30.refs_2_, ...), custom_call_target="tpu_custom_call" | custom-call | flops 524288 | bytes 5242880 | tf_op jit(solution)/shard_map/pallas_call | solution.py:450
  (66 shorter events, 0.6 us)
Async XLA Ops:
  0.0 10.2 %copy-start.14 = (s32[8]{0:T(128)S(1)}, s32[8]{0:T(128)}, u32[]{:S(2)}) copy-start(s32[8]{0:T(128)} %constant.25.clone) | copy-start | bytes 100
  0.0 11.4 %copy-start.13 = (s32[8]{0:T(128)S(1)}, s32[8]{0:T(128)}, u32[]{:S(2)}) copy-start(s32[8]{0:T(128)} %constant.24.clone) | copy-start | bytes 100
  0.0 16.0 %copy-start.3 = (f32[512]{0:T(512)S(1)}, f32[512]{0:T(512)}, u32[]{:S(2)}) copy-start(f32[512]{0:T(512)} %param.11) | copy-start | bytes 6148
  0.0 12.7 %collective-permute-start = (bf16[3,64,512]{2,1,0:T(8,128)(2,1)}, bf16[3,64,512]{2,1,0:T(8,128)(2,1)S(1)}, u32[]{:S(2)}, u32[]{:S(2)}) collective-permute-start(bf16[3,64,512]{2,1,0:T(8,128)(2,1)} %refs_0_.1), channel_id=1, source_target_pairs={{0,2},{1,3},{2,0},{3,1},{4,6},{5,7},{6,4},{7,5},{8,10},{9,11},{10,... | collective-permute-start | bytes 589832 | tf_op jit(solution)/shard_map/ppermute | solution.py:338
  3.0 12.8 %collective-permute-start.1 = (bf16[3,64,512]{2,1,0:T(8,128)(2,1)}, bf16[3,64,512]{2,1,0:T(8,128)(2,1)S(1)}, u32[]{:S(2)}, u32[]{:S(2)}) collective-permute-start(bf16[3,64,512]{2,1,0:T(8,128)(2,1)} %refs_0_.1), channel_id=1, source_target_pairs={{0,4},{1,5},{2,6},{3,7},{4,0},{5,1},{6,2},{7,3},{8,12},{9,13},{10,... | collective-permute-start | bytes 589832 | tf_op jit(solution)/shard_map/ppermute | solution.py:338
  4.5 11.2 %collective-permute-start.2 = (bf16[3,64,512]{2,1,0:T(8,128)(2,1)}, bf16[3,64,512]{2,1,0:T(8,128)(2,1)S(1)}, u32[]{:S(2)}, u32[]{:S(2)}) collective-permute-start(bf16[3,64,512]{2,1,0:T(8,128)(2,1)} %refs_0_.1), channel_id=1, source_target_pairs={{0,6},{1,7},{2,4},{3,5},{4,2},{5,3},{6,0},{7,1},{8,14},{9,15},{10,... | collective-permute-start | bytes 589832 | tf_op jit(solution)/shard_map/ppermute | solution.py:338
  4.6 23.7 %copy-start.5 = (s32[2]{0:T(128)}, s32[2]{0:T(128)S(1)}, u32[]{:S(2)}) copy-start(s32[2]{0:T(128)S(1)} %pad_add_fusion.place.source) | copy-start | bytes 28
  4.6 1.6 %copy-start = (f32[2,1,512,512]{3,2,1,0:T(8,128)S(1)}, f32[2,1,512,512]{3,2,1,0:T(8,128)}, u32[]{:S(2)}) copy-start(f32[2,1,512,512]{3,2,1,0:T(8,128)} %param.7) | copy-start | bytes 6291460
  6.2 9.6 %copy-start.2 = (bf16[3,64,512]{2,1,0:T(8,128)(2,1)S(1)}, bf16[3,64,512]{2,1,0:T(8,128)(2,1)}, u32[]{:S(2)}) copy-start(bf16[3,64,512]{2,1,0:T(8,128)(2,1)} %refs_0_.1) | copy-start | bytes 589828
  7.1 9.2 %collective-permute-start.10 = (bf16[2,128,256]{2,1,0:T(8,128)(2,1)S(1)}, bf16[2,128,256]{2,1,0:T(8,128)(2,1)S(1)}, u32[]{:S(2)}, u32[]{:S(2)}) collective-permute-start(bf16[2,128,256]{2,1,0:T(8,128)(2,1)S(1)} %get-tuple-element.62), channel_id=1, source_target_pairs={{0,7},{1,6},{2,5},{3,4},{4,3},{5,2},{6,1},{7,0},{8,15},{9,14},{10,... | collective-permute-start | bytes 393224 | tf_op jit(solution)/shard_map/ppermute | solution.py:305
  8.7 10.1 %collective-permute-start.4 = (bf16[2,128,256]{2,1,0:T(8,128)(2,1)S(1)}, bf16[2,128,256]{2,1,0:T(8,128)(2,1)S(1)}, u32[]{:S(2)}, u32[]{:S(2)}) collective-permute-start(bf16[2,128,256]{2,1,0:T(8,128)(2,1)S(1)} %get-tuple-element.56), channel_id=1, source_target_pairs={{0,1},{1,0},{2,3},{3,2},{4,5},{5,4},{6,7},{7,6},{8,9},{9,8},{10,11... | collective-permute-start | bytes 393224 | tf_op jit(solution)/shard_map/ppermute | solution.py:305
  12.7 15.4 %collective-permute-start.5 = (bf16[2,128,256]{2,1,0:T(8,128)(2,1)S(1)}, bf16[2,128,256]{2,1,0:T(8,128)(2,1)S(1)}, u32[]{:S(2)}, u32[]{:S(2)}) collective-permute-start(bf16[2,128,256]{2,1,0:T(8,128)(2,1)S(1)} %get-tuple-element.57), channel_id=1, source_target_pairs={{0,2},{1,3},{2,0},{3,1},{4,6},{5,7},{6,4},{7,5},{8,10},{9,11},{10,... | collective-permute-start | bytes 393224 | tf_op jit(solution)/shard_map/ppermute | solution.py:305
  15.8 12.3 %collective-permute-start.6 = (bf16[2,128,256]{2,1,0:T(8,128)(2,1)S(1)}, bf16[2,128,256]{2,1,0:T(8,128)(2,1)S(1)}, u32[]{:S(2)}, u32[]{:S(2)}) collective-permute-start(bf16[2,128,256]{2,1,0:T(8,128)(2,1)S(1)} %get-tuple-element.58), channel_id=1, source_target_pairs={{0,3},{1,2},{2,1},{3,0},{4,7},{5,6},{6,5},{7,4},{8,11},{9,10},{10,... | collective-permute-start | bytes 393224 | tf_op jit(solution)/shard_map/ppermute | solution.py:305
  15.9 3.0 %collective-permute-start.3 = (bf16[4,3,64,512]{3,2,1,0:T(8,128)(2,1)S(1)}, bf16[4,3,64,512]{3,2,1,0:T(8,128)(2,1)S(1)}, u32[]{:S(2)}, u32[]{:S(2)}) collective-permute-start(bf16[4,3,64,512]{3,2,1,0:T(8,128)(2,1)S(1)} %pad_maximum_fusion), channel_id=1, source_target_pairs={{0,1},{1,0},{2,3},{3,2},{4,5},{5,4},{6,7},{7,6},{8,9},{9,8},{10,11... | collective-permute-start | bytes 2359304 | tf_op jit(solution)/shard_map/ppermute | solution.py:338
  16.3 11.7 %collective-permute-start.7 = (bf16[2,128,256]{2,1,0:T(8,128)(2,1)S(1)}, bf16[2,128,256]{2,1,0:T(8,128)(2,1)S(1)}, u32[]{:S(2)}, u32[]{:S(2)}) collective-permute-start(bf16[2,128,256]{2,1,0:T(8,128)(2,1)S(1)} %get-tuple-element.59), channel_id=1, source_target_pairs={{0,4},{1,5},{2,6},{3,7},{4,0},{5,1},{6,2},{7,3},{8,12},{9,13},{10,... | collective-permute-start | bytes 393224 | tf_op jit(solution)/shard_map/ppermute | solution.py:305
  18.8 9.6 %collective-permute-start.8 = (bf16[2,128,256]{2,1,0:T(8,128)(2,1)S(1)}, bf16[2,128,256]{2,1,0:T(8,128)(2,1)S(1)}, u32[]{:S(2)}, u32[]{:S(2)}) collective-permute-start(bf16[2,128,256]{2,1,0:T(8,128)(2,1)S(1)} %get-tuple-element.60), channel_id=1, source_target_pairs={{0,5},{1,4},{2,7},{3,6},{4,1},{5,0},{6,3},{7,2},{8,13},{9,12},{10,... | collective-permute-start | bytes 393224 | tf_op jit(solution)/shard_map/ppermute | solution.py:305
  18.9 14.6 %copy-start.12 = (bf16[8,8]{1,0:T(8,128)(2,1)S(1)}, bf16[8,8]{1,0:T(8,128)(2,1)}, u32[]{:S(2)}) copy-start(bf16[8,8]{1,0:T(8,128)(2,1)} %param.9) | copy-start | bytes 388
  18.9 9.4 %collective-permute-start.9 = (bf16[2,128,256]{2,1,0:T(8,128)(2,1)S(1)}, bf16[2,128,256]{2,1,0:T(8,128)(2,1)S(1)}, u32[]{:S(2)}, u32[]{:S(2)}) collective-permute-start(bf16[2,128,256]{2,1,0:T(8,128)(2,1)S(1)} %get-tuple-element.61), channel_id=1, source_target_pairs={{0,6},{1,7},{2,4},{3,5},{4,2},{5,3},{6,0},{7,1},{8,14},{9,15},{10,... | collective-permute-start | bytes 393224 | tf_op jit(solution)/shard_map/ppermute | solution.py:305
  29.0 12.4 %collective-permute-start.11 = (bf16[2,2,64,256]{3,2,1,0:T(8,128)(2,1)S(1)}, bf16[2,2,64,256]{3,2,1,0:T(8,128)(2,1)S(1)}, u32[]{:S(2)}, u32[]{:S(2)}) collective-permute-start(bf16[2,2,64,256]{3,2,1,0:T(8,128)(2,1)S(1)} %get-tuple-element.64), channel_id=1, source_target_pairs={{0,8},{8,0},{16,24},{24,16},{1,9},{9,1},{17,25},{25,17},{2,10},{10... | collective-permute-start | bytes 393224 | tf_op jit(solution)/shard_map/ppermute | solution.py:312
  30.6 12.9 %collective-permute-start.12 = (bf16[2,2,64,256]{3,2,1,0:T(8,128)(2,1)S(1)}, bf16[2,2,64,256]{3,2,1,0:T(8,128)(2,1)S(1)}, u32[]{:S(2)}, u32[]{:S(2)}) collective-permute-start(bf16[2,2,64,256]{3,2,1,0:T(8,128)(2,1)S(1)} %get-tuple-element.65), channel_id=1, source_target_pairs={{0,16},{8,24},{16,0},{24,8},{1,17},{9,25},{17,1},{25,9},{2,18},{10... | collective-permute-start | bytes 393224 | tf_op jit(solution)/shard_map/ppermute | solution.py:312
  33.2 10.3 %collective-permute-start.13 = (bf16[2,2,64,256]{3,2,1,0:T(8,128)(2,1)S(1)}, bf16[2,2,64,256]{3,2,1,0:T(8,128)(2,1)S(1)}, u32[]{:S(2)}, u32[]{:S(2)}) collective-permute-start(bf16[2,2,64,256]{3,2,1,0:T(8,128)(2,1)S(1)} %get-tuple-element.66), channel_id=1, source_target_pairs={{0,24},{8,16},{16,8},{24,0},{1,25},{9,17},{17,9},{25,1},{2,26},{10... | collective-permute-start | bytes 393224 | tf_op jit(solution)/shard_map/ppermute | solution.py:312
  33.6 18.9 %all-to-all-start = ((bf16[8,2,128,256]{3,2,1,0:T(8,128)(2,1)}), bf16[8,2,128,256]{3,2,1,0:T(8,128)(2,1)S(1)}, u32[]{:S(2)}, u32[]{:S(2)}) async-start(bf16[8,2,128,256]{3,2,1,0:T(8,128)(2,1)} %get-tuple-element.54), calls=%async_computation | async-start | bytes 2097152 | tf_op jit(solution)/shard_map/all_to_all | solution.py:299
  37.2 21.8 %collective-permute-start.17 = (bf16[2,2,64,256]{3,2,1,0:T(8,128)(2,1)S(1)}, bf16[2,2,64,256]{3,2,1,0:T(8,128)(2,1)S(1)}, u32[]{:S(2)}, u32[]{:S(2)}) collective-permute-start(bf16[2,2,64,256]{3,2,1,0:T(8,128)(2,1)S(1)} %get-tuple-element.74), channel_id=1, source_target_pairs={{0,8},{8,0},{16,24},{24,16},{1,9},{9,1},{17,25},{25,17},{2,10},{10... | collective-permute-start | bytes 393224 | tf_op jit(solution)/shard_map/ppermute | solution.py:312
  37.9 21.3 %collective-permute-start.18 = (bf16[2,2,64,256]{3,2,1,0:T(8,128)(2,1)S(1)}, bf16[2,2,64,256]{3,2,1,0:T(8,128)(2,1)S(1)}, u32[]{:S(2)}, u32[]{:S(2)}) collective-permute-start(bf16[2,2,64,256]{3,2,1,0:T(8,128)(2,1)S(1)} %get-tuple-element.75), channel_id=1, source_target_pairs={{0,16},{8,24},{16,0},{24,8},{1,17},{9,25},{17,1},{25,9},{2,18},{10... | collective-permute-start | bytes 393224 | tf_op jit(solution)/shard_map/ppermute | solution.py:312
  41.4 17.8 %collective-permute-start.19 = (bf16[2,2,64,256]{3,2,1,0:T(8,128)(2,1)S(1)}, bf16[2,2,64,256]{3,2,1,0:T(8,128)(2,1)S(1)}, u32[]{:S(2)}, u32[]{:S(2)}) collective-permute-start(bf16[2,2,64,256]{3,2,1,0:T(8,128)(2,1)S(1)} %get-tuple-element.76), channel_id=1, source_target_pairs={{0,24},{8,16},{16,8},{24,0},{1,25},{9,17},{17,9},{25,1},{2,26},{10... | collective-permute-start | bytes 393224 | tf_op jit(solution)/shard_map/ppermute | solution.py:312
  44.8 14.4 %copy-start.6 = (s32[2]{0:T(128)S(1)}, s32[2]{0:T(128)}, u32[]{:S(2)}) copy-start(s32[2]{0:T(128)} %copy-done.5) | copy-start | bytes 28
  52.5 0.7 copy-start.11
  54.7 10.3 %collective-permute-start.14 = (bf16[2,2,64,256]{3,2,1,0:T(8,128)(2,1)S(1)}, bf16[2,2,64,256]{3,2,1,0:T(8,128)(2,1)S(1)}, u32[]{:S(2)}, u32[]{:S(2)}) collective-permute-start(bf16[2,2,64,256]{3,2,1,0:T(8,128)(2,1)S(1)} %get-tuple-element.69.refs_1_), channel_id=1, source_target_pairs={{0,8},{8,0},{16,24},{24,16},{1,9},{9,1},{17,25},{25,17},{2,10},{10... | collective-permute-start | bytes 393224 | tf_op jit(solution)/shard_map/ppermute | solution.py:312
  56.1 12.9 %collective-permute-start.15 = (bf16[2,2,64,256]{3,2,1,0:T(8,128)(2,1)S(1)}, bf16[2,2,64,256]{3,2,1,0:T(8,128)(2,1)S(1)}, u32[]{:S(2)}, u32[]{:S(2)}) collective-permute-start(bf16[2,2,64,256]{3,2,1,0:T(8,128)(2,1)S(1)} %get-tuple-element.70.refs_2_), channel_id=1, source_target_pairs={{0,16},{8,24},{16,0},{24,8},{1,17},{9,25},{17,1},{25,9},{2,18},{10... | collective-permute-start | bytes 393224 | tf_op jit(solution)/shard_map/ppermute | solution.py:312
  59.0 10.0 %collective-permute-start.16 = (bf16[2,2,64,256]{3,2,1,0:T(8,128)(2,1)S(1)}, bf16[2,2,64,256]{3,2,1,0:T(8,128)(2,1)S(1)}, u32[]{:S(2)}, u32[]{:S(2)}) collective-permute-start(bf16[2,2,64,256]{3,2,1,0:T(8,128)(2,1)S(1)} %get-tuple-element.71.refs_3_), channel_id=1, source_target_pairs={{0,24},{8,16},{16,8},{24,0},{1,25},{9,17},{17,9},{25,1},{2,26},{10... | collective-permute-start | bytes 393224 | tf_op jit(solution)/shard_map/ppermute | solution.py:312
  59.2 9.8 %copy-start.7 = (f32[8]{0:T(128)S(1)}, f32[8]{0:T(128)}, u32[]{:S(2)}) copy-start(f32[8]{0:T(128)} %occ.9) | copy-start | bytes 100
  60.8 19.4 %collective-permute-start.20 = (bf16[2,2,64,256]{3,2,1,0:T(8,128)(2,1)S(1)}, bf16[2,2,64,256]{3,2,1,0:T(8,128)(2,1)S(1)}, u32[]{:S(2)}, u32[]{:S(2)}) collective-permute-start(bf16[2,2,64,256]{3,2,1,0:T(8,128)(2,1)S(1)} %get-tuple-element.78.refs_2_), channel_id=1, source_target_pairs={{0,8},{8,0},{16,24},{24,16},{1,9},{9,1},{17,25},{25,17},{2,10},{10... | collective-permute-start | bytes 393224 | tf_op jit(solution)/shard_map/ppermute | solution.py:312
  61.2 20.6 %collective-permute-start.21 = (bf16[2,2,64,256]{3,2,1,0:T(8,128)(2,1)S(1)}, bf16[2,2,64,256]{3,2,1,0:T(8,128)(2,1)S(1)}, u32[]{:S(2)}, u32[]{:S(2)}) collective-permute-start(bf16[2,2,64,256]{3,2,1,0:T(8,128)(2,1)S(1)} %get-tuple-element.79.refs_3_), channel_id=1, source_target_pairs={{0,16},{8,24},{16,0},{24,8},{1,17},{9,25},{17,1},{25,9},{2,18},{10... | collective-permute-start | bytes 393224 | tf_op jit(solution)/shard_map/ppermute | solution.py:312
  65.0 16.8 %collective-permute-start.22 = (bf16[2,2,64,256]{3,2,1,0:T(8,128)(2,1)S(1)}, bf16[2,2,64,256]{3,2,1,0:T(8,128)(2,1)S(1)}, u32[]{:S(2)}, u32[]{:S(2)}) collective-permute-start(bf16[2,2,64,256]{3,2,1,0:T(8,128)(2,1)S(1)} %get-tuple-element.80.refs_4_), channel_id=1, source_target_pairs={{0,24},{8,16},{16,8},{24,0},{1,25},{9,17},{17,9},{25,1},{2,26},{10... | collective-permute-start | bytes 393224 | tf_op jit(solution)/shard_map/ppermute | solution.py:312
  71.5 0.8 copy-start.9
  72.3 23.3 %collective-permute-start.26 = (bf16[2,2,64,256]{3,2,1,0:T(8,128)(2,1)S(1)}, bf16[2,2,64,256]{3,2,1,0:T(8,128)(2,1)S(1)}, u32[]{:S(2)}, u32[]{:S(2)}) collective-permute-start(bf16[2,2,64,256]{3,2,1,0:T(8,128)(2,1)S(1)} %get-tuple-element.88), channel_id=1, source_target_pairs={{0,8},{8,0},{16,24},{24,16},{1,9},{9,1},{17,25},{25,17},{2,10},{10... | collective-permute-start | bytes 393224 | tf_op jit(solution)/shard_map/ppermute | solution.py:312
  79.5 17.8 %collective-permute-start.27 = (bf16[2,2,64,256]{3,2,1,0:T(8,128)(2,1)S(1)}, bf16[2,2,64,256]{3,2,1,0:T(8,128)(2,1)S(1)}, u32[]{:S(2)}, u32[]{:S(2)}) collective-permute-start(bf16[2,2,64,256]{3,2,1,0:T(8,128)(2,1)S(1)} %get-tuple-element.89), channel_id=1, source_target_pairs={{0,16},{8,24},{16,0},{24,8},{1,17},{9,25},{17,1},{25,9},{2,18},{10... | collective-permute-start | bytes 393224 | tf_op jit(solution)/shard_map/ppermute | solution.py:312
  80.2 17.0 %collective-permute-start.28 = (bf16[2,2,64,256]{3,2,1,0:T(8,128)(2,1)S(1)}, bf16[2,2,64,256]{3,2,1,0:T(8,128)(2,1)S(1)}, u32[]{:S(2)}, u32[]{:S(2)}) collective-permute-start(bf16[2,2,64,256]{3,2,1,0:T(8,128)(2,1)S(1)} %get-tuple-element.90), channel_id=1, source_target_pairs={{0,24},{8,16},{16,8},{24,0},{1,25},{9,17},{17,9},{25,1},{2,26},{10... | collective-permute-start | bytes 393224 | tf_op jit(solution)/shard_map/ppermute | solution.py:312
  85.4 13.9 %collective-permute-start.23 = (bf16[2,2,64,256]{3,2,1,0:T(8,128)(2,1)S(1)}, bf16[2,2,64,256]{3,2,1,0:T(8,128)(2,1)S(1)}, u32[]{:S(2)}, u32[]{:S(2)}) collective-permute-start(bf16[2,2,64,256]{3,2,1,0:T(8,128)(2,1)S(1)} %get-tuple-element.84), channel_id=1, source_target_pairs={{0,8},{8,0},{16,24},{24,16},{1,9},{9,1},{17,25},{25,17},{2,10},{10... | collective-permute-start | bytes 393224 | tf_op jit(solution)/shard_map/ppermute | solution.py:312
  88.2 11.2 %collective-permute-start.24 = (bf16[2,2,64,256]{3,2,1,0:T(8,128)(2,1)S(1)}, bf16[2,2,64,256]{3,2,1,0:T(8,128)(2,1)S(1)}, u32[]{:S(2)}, u32[]{:S(2)}) collective-permute-start(bf16[2,2,64,256]{3,2,1,0:T(8,128)(2,1)S(1)} %get-tuple-element.85), channel_id=1, source_target_pairs={{0,16},{8,24},{16,0},{24,8},{1,17},{9,25},{17,1},{25,9},{2,18},{10... | collective-permute-start | bytes 393224 | tf_op jit(solution)/shard_map/ppermute | solution.py:312
  88.9 24.7 %all-to-all-start.1 = ((bf16[8,2,128,256]{3,2,1,0:T(8,128)(2,1)}), bf16[8,2,128,256]{3,2,1,0:T(8,128)(2,1)S(1)}, u32[]{:S(2)}, u32[]{:S(2)}) async-start(bf16[8,2,128,256]{3,2,1,0:T(8,128)(2,1)} %get-tuple-element.81), calls=%async_computation.1 | async-start | bytes 2097152 | tf_op jit(solution)/shard_map/all_to_all | solution.py:299
  95.5 7.8 %collective-permute-start.25 = (bf16[2,2,64,256]{3,2,1,0:T(8,128)(2,1)S(1)}, bf16[2,2,64,256]{3,2,1,0:T(8,128)(2,1)S(1)}, u32[]{:S(2)}, u32[]{:S(2)}) collective-permute-start(bf16[2,2,64,256]{3,2,1,0:T(8,128)(2,1)S(1)} %get-tuple-element.86), channel_id=1, source_target_pairs={{0,24},{8,16},{16,8},{24,0},{1,25},{9,17},{17,9},{25,1},{2,26},{10... | collective-permute-start | bytes 393224 | tf_op jit(solution)/shard_map/ppermute | solution.py:312
  97.2 1.0 copy-start.10
  103.4 10.3 %copy-start.4 = (f32[512]{0:T(512)S(1)}, f32[512]{0:T(512)}, u32[]{:S(2)}) copy-start(f32[512]{0:T(512)} %param.11) | copy-start | bytes 6148
  104.5 4.1 %collective-permute-start.29 = (bf16[2,128,256]{2,1,0:T(8,128)(2,1)S(1)}, bf16[2,128,256]{2,1,0:T(8,128)(2,1)S(1)}, u32[]{:S(2)}, u32[]{:S(2)}) collective-permute-start(bf16[2,128,256]{2,1,0:T(8,128)(2,1)S(1)} %get-tuple-element.92), channel_id=1, source_target_pairs={{0,1},{1,0},{2,3},{3,2},{4,5},{5,4},{6,7},{7,6},{8,9},{9,8},{10,11... | collective-permute-start | bytes 393224 | tf_op jit(solution)/shard_map/ppermute | solution.py:305
  104.6 8.8 %collective-permute-start.30 = (bf16[2,128,256]{2,1,0:T(8,128)(2,1)S(1)}, bf16[2,128,256]{2,1,0:T(8,128)(2,1)S(1)}, u32[]{:S(2)}, u32[]{:S(2)}) collective-permute-start(bf16[2,128,256]{2,1,0:T(8,128)(2,1)S(1)} %get-tuple-element.93), channel_id=1, source_target_pairs={{0,2},{1,3},{2,0},{3,1},{4,6},{5,7},{6,4},{7,5},{8,10},{9,11},{10,... | collective-permute-start | bytes 393224 | tf_op jit(solution)/shard_map/ppermute | solution.py:305
  106.3 16.6 %collective-permute-start.31 = (bf16[2,128,256]{2,1,0:T(8,128)(2,1)S(1)}, bf16[2,128,256]{2,1,0:T(8,128)(2,1)S(1)}, u32[]{:S(2)}, u32[]{:S(2)}) collective-permute-start(bf16[2,128,256]{2,1,0:T(8,128)(2,1)S(1)} %get-tuple-element.94), channel_id=1, source_target_pairs={{0,3},{1,2},{2,1},{3,0},{4,7},{5,6},{6,5},{7,4},{8,11},{9,10},{10,... | collective-permute-start | bytes 393224 | tf_op jit(solution)/shard_map/ppermute | solution.py:305
  106.5 16.5 %collective-permute-start.32 = (bf16[2,128,256]{2,1,0:T(8,128)(2,1)S(1)}, bf16[2,128,256]{2,1,0:T(8,128)(2,1)S(1)}, u32[]{:S(2)}, u32[]{:S(2)}) collective-permute-start(bf16[2,128,256]{2,1,0:T(8,128)(2,1)S(1)} %get-tuple-element.95), channel_id=1, source_target_pairs={{0,4},{1,5},{2,6},{3,7},{4,0},{5,1},{6,2},{7,3},{8,12},{9,13},{10,... | collective-permute-start | bytes 393224 | tf_op jit(solution)/shard_map/ppermute | solution.py:305
  108.7 14.3 %collective-permute-start.33 = (bf16[2,128,256]{2,1,0:T(8,128)(2,1)S(1)}, bf16[2,128,256]{2,1,0:T(8,128)(2,1)S(1)}, u32[]{:S(2)}, u32[]{:S(2)}) collective-permute-start(bf16[2,128,256]{2,1,0:T(8,128)(2,1)S(1)} %get-tuple-element.96), channel_id=1, source_target_pairs={{0,5},{1,4},{2,7},{3,6},{4,1},{5,0},{6,3},{7,2},{8,13},{9,12},{10,... | collective-permute-start | bytes 393224 | tf_op jit(solution)/shard_map/ppermute | solution.py:305
  108.7 14.3 %collective-permute-start.34 = (bf16[2,128,256]{2,1,0:T(8,128)(2,1)S(1)}, bf16[2,128,256]{2,1,0:T(8,128)(2,1)S(1)}, u32[]{:S(2)}, u32[]{:S(2)}) collective-permute-start(bf16[2,128,256]{2,1,0:T(8,128)(2,1)S(1)} %get-tuple-element.97), channel_id=1, source_target_pairs={{0,6},{1,7},{2,4},{3,5},{4,2},{5,3},{6,0},{7,1},{8,14},{9,15},{10,... | collective-permute-start | bytes 393224 | tf_op jit(solution)/shard_map/ppermute | solution.py:305
  113.4 9.6 %collective-permute-start.35 = (bf16[2,128,256]{2,1,0:T(8,128)(2,1)S(1)}, bf16[2,128,256]{2,1,0:T(8,128)(2,1)S(1)}, u32[]{:S(2)}, u32[]{:S(2)}) collective-permute-start(bf16[2,128,256]{2,1,0:T(8,128)(2,1)S(1)} %get-tuple-element.98), channel_id=1, source_target_pairs={{0,7},{1,6},{2,5},{3,4},{4,3},{5,2},{6,1},{7,0},{8,15},{9,14},{10,... | collective-permute-start | bytes 393224 | tf_op jit(solution)/shard_map/ppermute | solution.py:305
  113.7 1.4 %copy-start.8 = (bf16[512,1536]{1,0:T(8,128)(2,1)S(1)}, bf16[512,1536]{1,0:T(8,128)(2,1)}, u32[]{:S(2)}) copy-start(bf16[512,1536]{1,0:T(8,128)(2,1)} %get-tuple-element.82.whole) | copy-start | bytes 4718596
  123.0 1.6 %copy-start.1 = (f32[2,512,512]{2,1,0:T(8,128)S(1)}, f32[2,512,512]{2,1,0:T(8,128)}, u32[]{:S(2)}) copy-start(f32[2,512,512]{2,1,0:T(8,128)} %shard_map.81.source) | copy-start | bytes 6291460

commit v21 on v14

--- a/solution.py
+++ b/solution.py
@@ -444,8 +444,8 @@
         last = call(
             functools.partial(rest_kernel, tiles, groups, first, c),
             [distant] * devices if c else [upper], [blocks] if c else [],
-            LONG, 8 * count, place, occ_energy, sums, rest[c], *other[c], *last,
-            specs=[SMEM] * 2 + [VMEM] * (groups + 1 + c),
+            LONG, 8 * count, place, occ_energy, sums, rest[c], *other[c], *(last if c else [whole]),
+            specs=[SMEM] * 2 + [VMEM] * (groups + 2),
         )
     done = pl.pallas_call(
         functools.partial(add_kernel, tiles),

time: 127 us -> 128 us (level)
    ppermute x18, starting transfers between devices: 35.3 us -> 38.7 us  [across_first(): lax.ppermute(parts[s], 'occi', [(k, k ^ s) for k in range(groups)])]
    all_to_all x2, starting transfers between devices: 10.2 us -> 7.12 us  [exchange(): lax.all_to_all(blocks, 'occj', split_axis=0, concat_axis=0, tiled=True)]
    unnamed x28 -> x30, local copies, waits for them, and re-layouts: 5.43 us -> 5.89 us
  transfers between devices with their start and end apart: 38 -> 38, of which waited for: 7 -> 8; matrix products, arithmetic and copies ran while one was open for 2% -> 2% of each run, Pallas kernels for 22% -> 22%
where the time goes in v21:
time: 128 us; the launch traced here: 126 us
  starting transfers between devices  67 us (52%)
  Pallas kernels  31.1 us (24%)
  waiting for transfers between devices  18.9 us (15%)
  local copies, waits for them, and re-layouts  7.41 us (6%)
  between operations  1.64 us (1%)
    ppermute x18, starting transfers between devices, across_first(): lax.ppermute(parts[s], 'occi', [(k, k ^ s) for k in range(groups)])  38.7 us
    pallas_call x9, Pallas kernels, call(): pl.pallas_call(body, out_shape=outs, in_specs=specs, out_specs=jax.tree.m...  19.3 us
    ppermute x14, starting transfers between devices, by_distance(): lax.ppermute(parts[k], 'occj', [(d, d ^ k) for d in range(devices)])  16.5 us
    pallas_call x1, Pallas kernels, local(): pl.pallas_call(functools.partial(second_ladder_kernel, tiles, first), gri...  7.78 us
    all_to_all x2, waiting for transfers between devices, exchange(): lax.all_to_all(blocks, 'occj', split_axis=0, concat_axis=0, tiled=True)  7.73 us
    all_to_all x2, starting transfers between devices, exchange(): lax.all_to_all(blocks, 'occj', split_axis=0, concat_axis=0, tiled=True)  7.12 us
    ppermute x18, waiting for transfers between devices, across_first(): lax.ppermute(parts[s], 'occi', [(k, k ^ s) for k in range(groups)])  6.61 us
    unnamed x30, local copies, waits for them, and re-layouts  5.89 us
  transfers between devices with their start and end apart: 38, of which 8 were waited for; matrix products, arithmetic and copies ran while one was open for 2% of the time, Pallas kernels for 22%

profile of v21, /device:TPU:0, one launch (start us, length us, event | category | flops | bytes accessed | tf_op | source)
XLA Modules:
  0.0 126.3 jit_solution(9903914708922908358)
XLA Ops:
  0.0 3.0 %collective-permute-start = (bf16[3,64,512]{2,1,0:T(8,128)(2,1)}, bf16[3,64,512]{2,1,0:T(8,128)(2,1)S(1)}, u32[]{:S(2)}, u32[]{:S(2)}) collective-permute-start(bf16[3,64,512]{2,1,0:T(8,128)(2,1)} %refs_0_.1), channel_id=1, source_target_pairs={{0,2},{1,3},{2,0},{3,1},{4,6},{5,7},{6,4},{7,5},{8,10},{9,11},{10,... | collective-permute-start | bytes 589832 | tf_op jit(solution)/shard_map/ppermute | solution.py:338
  3.0 1.5 %collective-permute-start.1 = (bf16[3,64,512]{2,1,0:T(8,128)(2,1)}, bf16[3,64,512]{2,1,0:T(8,128)(2,1)S(1)}, u32[]{:S(2)}, u32[]{:S(2)}) collective-permute-start(bf16[3,64,512]{2,1,0:T(8,128)(2,1)} %refs_0_.1), channel_id=1, source_target_pairs={{0,4},{1,5},{2,6},{3,7},{4,0},{5,1},{6,2},{7,3},{8,12},{9,13},{10,... | collective-permute-start | bytes 589832 | tf_op jit(solution)/shard_map/ppermute | solution.py:338
  4.6 1.6 %copy-done = f32[2,1,512,512]{3,2,1,0:T(8,128)S(1)} copy-done((f32[2,1,512,512]{3,2,1,0:T(8,128)S(1)}, f32[2,1,512,512]{3,2,1,0:T(8,128)}, u32[]{:S(2)}) %copy-start) | copy-done | bytes 2097176
  6.2 0.9 shard_map.73
  7.1 1.6 %collective-permute-start.10 = (bf16[2,128,256]{2,1,0:T(8,128)(2,1)S(1)}, bf16[2,128,256]{2,1,0:T(8,128)(2,1)S(1)}, u32[]{:S(2)}, u32[]{:S(2)}) collective-permute-start(bf16[2,128,256]{2,1,0:T(8,128)(2,1)S(1)} %get-tuple-element.62), channel_id=1, source_target_pairs={{0,7},{1,6},{2,5},{3,4},{4,3},{5,2},{6,1},{7,0},{8,15},{9,14},{10,... | collective-permute-start | bytes 393224 | tf_op jit(solution)/shard_map/ppermute | solution.py:305
  8.7 1.5 %collective-permute-start.4 = (bf16[2,128,256]{2,1,0:T(8,128)(2,1)S(1)}, bf16[2,128,256]{2,1,0:T(8,128)(2,1)S(1)}, u32[]{:S(2)}, u32[]{:S(2)}) collective-permute-start(bf16[2,128,256]{2,1,0:T(8,128)(2,1)S(1)} %get-tuple-element.56), channel_id=1, source_target_pairs={{0,1},{1,0},{2,3},{3,2},{4,5},{5,4},{6,7},{7,6},{8,9},{9,8},{10,11... | collective-permute-start | bytes 393224 | tf_op jit(solution)/shard_map/ppermute | solution.py:305
  10.2 0.6 dynamic_slice.14
  11.4 0.6 dynamic_slice.12
  12.7 0.6 collective-permute-start.5
  13.3 2.5 %collective-permute-done.1.refs_2_ = bf16[3,64,512]{2,1,0:T(8,128)(2,1)S(1)} collective-permute-done((bf16[3,64,512]{2,1,0:T(8,128)(2,1)}, bf16[3,64,512]{2,1,0:T(8,128)(2,1)S(1)}, u32[]{:S(2)}, u32[]{:S(2)}) %collective-permute-start.1) | collective-permute-done | bytes 196640 | tf_op jit(solution)/shard_map/ppermute | solution.py:338
  15.8 0.1 pad_maximum_fusion
  16.0 0.1 fusion
  16.2 0.1 broadcast_add_fusion.2
  16.3 2.4 %collective-permute-start.7 = (bf16[2,128,256]{2,1,0:T(8,128)(2,1)S(1)}, bf16[2,128,256]{2,1,0:T(8,128)(2,1)S(1)}, u32[]{:S(2)}, u32[]{:S(2)}) collective-permute-start(bf16[2,128,256]{2,1,0:T(8,128)(2,1)S(1)} %get-tuple-element.59), channel_id=1, source_target_pairs={{0,4},{1,5},{2,6},{3,7},{4,0},{5,1},{6,2},{7,3},{8,12},{9,13},{10,... | collective-permute-start | bytes 393224 | tf_op jit(solution)/shard_map/ppermute | solution.py:305
  18.8 0.2 collective-permute-start.8
  18.9 2.9 %collective-permute-start.9 = (bf16[2,128,256]{2,1,0:T(8,128)(2,1)S(1)}, bf16[2,128,256]{2,1,0:T(8,128)(2,1)S(1)}, u32[]{:S(2)}, u32[]{:S(2)}) collective-permute-start(bf16[2,128,256]{2,1,0:T(8,128)(2,1)S(1)} %get-tuple-element.61), channel_id=1, source_target_pairs={{0,6},{1,7},{2,4},{3,5},{4,2},{5,3},{6,0},{7,1},{8,14},{9,15},{10,... | collective-permute-start | bytes 393224 | tf_op jit(solution)/shard_map/ppermute | solution.py:305
  21.8 6.3 %shard_map.74 = (bf16[8,2,128,256]{3,2,1,0:T(8,128)(2,1)}, bf16[512,1536]{1,0:T(8,128)(2,1)}) custom-call(s32[2]{0:T(128)S(1)} %pad_add_fusion.place.source, f32[2,512,512]{2,1,0:T(8,128)} %bitcast.13, bf16[3,64,512]{2,1,0:T(8,128)(2,1)S(1)} %copy-done.1, bf16[3,64,512]{2,1,0:T(8,128)(2,1)S(1)} %collective-permute-done.refs_1_, ...), custom_call_target="tpu_custom_call" | custom-call | flops 3221225472 | bytes 4194304 | tf_op jit(solution)/shard_map/pallas_call | solution.py:42
  28.1 0.2 collective-permute-done.8.refs_5_
  28.3 0.7 shard_map.75
  29.0 1.6 %collective-permute-start.11 = (bf16[2,2,64,256]{3,2,1,0:T(8,128)(2,1)S(1)}, bf16[2,2,64,256]{3,2,1,0:T(8,128)(2,1)S(1)}, u32[]{:S(2)}, u32[]{:S(2)}) collective-permute-start(bf16[2,2,64,256]{3,2,1,0:T(8,128)(2,1)S(1)} %get-tuple-element.64), channel_id=1, source_target_pairs={{0,8},{8,0},{16,24},{24,16},{1,9},{9,1},{17,25},{25,17},{2,10},{10... | collective-permute-start | bytes 393224 | tf_op jit(solution)/shard_map/ppermute | solution.py:312
  30.6 2.6 %collective-permute-start.12 = (bf16[2,2,64,256]{3,2,1,0:T(8,128)(2,1)S(1)}, bf16[2,2,64,256]{3,2,1,0:T(8,128)(2,1)S(1)}, u32[]{:S(2)}, u32[]{:S(2)}) collective-permute-start(bf16[2,2,64,256]{3,2,1,0:T(8,128)(2,1)S(1)} %get-tuple-element.65), channel_id=1, source_target_pairs={{0,16},{8,24},{16,0},{24,8},{1,17},{9,25},{17,1},{25,9},{2,18},{10... | collective-permute-start | bytes 393224 | tf_op jit(solution)/shard_map/ppermute | solution.py:312
  33.2 0.2 collective-permute-start.13
  33.6 3.6 %all-to-all-start = ((bf16[8,2,128,256]{3,2,1,0:T(8,128)(2,1)}), bf16[8,2,128,256]{3,2,1,0:T(8,128)(2,1)S(1)}, u32[]{:S(2)}, u32[]{:S(2)}) async-start(bf16[8,2,128,256]{3,2,1,0:T(8,128)(2,1)} %get-tuple-element.54), calls=%async_computation | async-start | bytes 2097152 | tf_op jit(solution)/shard_map/all_to_all | solution.py:299
  37.2 0.7 collective-permute-start.17
  37.9 3.5 %collective-permute-start.18 = (bf16[2,2,64,256]{3,2,1,0:T(8,128)(2,1)S(1)}, bf16[2,2,64,256]{3,2,1,0:T(8,128)(2,1)S(1)}, u32[]{:S(2)}, u32[]{:S(2)}) collective-permute-start(bf16[2,2,64,256]{3,2,1,0:T(8,128)(2,1)S(1)} %get-tuple-element.75), channel_id=1, source_target_pairs={{0,16},{8,24},{16,0},{24,8},{1,17},{9,25},{17,1},{25,9},{2,18},{10... | collective-permute-start | bytes 393224 | tf_op jit(solution)/shard_map/ppermute | solution.py:312
  41.4 0.2 collective-permute-start.19
  41.6 1.9 %collective-permute-done.12.refs_2_ = bf16[2,2,64,256]{3,2,1,0:T(8,128)(2,1)S(1)} collective-permute-done((bf16[2,2,64,256]{3,2,1,0:T(8,128)(2,1)S(1)}, bf16[2,2,64,256]{3,2,1,0:T(8,128)(2,1)S(1)}, u32[]{:S(2)}, u32[]{:S(2)}) %collective-permute-start.12) | collective-permute-done | bytes 131104 | tf_op jit(solution)/shard_map/ppermute | solution.py:312
  43.6 1.2 shard_map.76.place
  44.8 7.7 %all-to-all-done.ladder = bf16[8,2,128,256]{3,2,1,0:T(8,128)(2,1)S(1)} async-done(((bf16[8,2,128,256]{3,2,1,0:T(8,128)(2,1)}), bf16[8,2,128,256]{3,2,1,0:T(8,128)(2,1)S(1)}, u32[]{:S(2)}, u32[]{:S(2)}) %all-to-all-start) | async-done | bytes 1048608 | tf_op jit(solution)/shard_map/all_to_all | solution.py:299
  52.5 0.7 copy-done.11
  53.2 1.6 %shard_map.77 = (bf16[2,2,64,256]{3,2,1,0:T(8,128)(2,1)S(1)}, bf16[2,2,64,256]{3,2,1,0:T(8,128)(2,1)S(1)}, bf16[2,2,64,256]{3,2,1,0:T(8,128)(2,1)S(1)}, bf16[2,2,64,256]{3,2,1,0:T(8,128)(2,1)S(1)}) custom-call(s32[2]{0:T(128)S(1)} %copy-done.11, f32[8,8]{1,0:T(8,128)S(1)} %convert_element_type.3.fock, bf16[8,2,128,256]{3,2,1,0:T(8,128)(2,1)S(1)} %all-to-all-done.ladder, ...), custom_call_target="tpu_custom_call" | custom-call | flops 30000001024 | bytes 3145728 | tf_op jit(solution)/shard_map/pallas_call | solution.py:42
  54.7 1.3 %collective-permute-start.14 = (bf16[2,2,64,256]{3,2,1,0:T(8,128)(2,1)S(1)}, bf16[2,2,64,256]{3,2,1,0:T(8,128)(2,1)S(1)}, u32[]{:S(2)}, u32[]{:S(2)}) collective-permute-start(bf16[2,2,64,256]{3,2,1,0:T(8,128)(2,1)S(1)} %get-tuple-element.69.refs_1_), channel_id=1, source_target_pairs={{0,8},{8,0},{16,24},{24,16},{1,9},{9,1},{17,25},{25,17},{2,10},{10... | collective-permute-start | bytes 393224 | tf_op jit(solution)/shard_map/ppermute | solution.py:312
  56.1 2.9 %collective-permute-start.15 = (bf16[2,2,64,256]{3,2,1,0:T(8,128)(2,1)S(1)}, bf16[2,2,64,256]{3,2,1,0:T(8,128)(2,1)S(1)}, u32[]{:S(2)}, u32[]{:S(2)}) collective-permute-start(bf16[2,2,64,256]{3,2,1,0:T(8,128)(2,1)S(1)} %get-tuple-element.70.refs_2_), channel_id=1, source_target_pairs={{0,16},{8,24},{16,0},{24,8},{1,17},{9,25},{17,1},{25,9},{2,18},{10... | collective-permute-start | bytes 393224 | tf_op jit(solution)/shard_map/ppermute | solution.py:312
  59.0 0.2 collective-permute-start.16
  59.2 1.6 %shard_map.79 = (bf16[2,2,64,256]{3,2,1,0:T(8,128)(2,1)S(1)}, bf16[2,2,64,256]{3,2,1,0:T(8,128)(2,1)S(1)}, bf16[2,2,64,256]{3,2,1,0:T(8,128)(2,1)S(1)}, bf16[2,2,64,256]{3,2,1,0:T(8,128)(2,1)S(1)}) custom-call(s32[2]{0:T(128)S(1)} %copy-done.5, f32[8,8]{1,0:T(8,128)S(1)} %convert_element_type.3.fock, bf16[8,2,128,256]{3,2,1,0:T(8,128)(2,1)S(1)} %all-to-all-done.ladder, ...), custom_call_target="tpu_custom_call" | custom-call | flops 30000001024 | bytes 3145728 | tf_op jit(solution)/shard_map/pallas_call | solution.py:42
  60.8 0.4 collective-permute-start.20
  61.2 3.8 %collective-permute-start.21 = (bf16[2,2,64,256]{3,2,1,0:T(8,128)(2,1)S(1)}, bf16[2,2,64,256]{3,2,1,0:T(8,128)(2,1)S(1)}, u32[]{:S(2)}, u32[]{:S(2)}) collective-permute-start(bf16[2,2,64,256]{3,2,1,0:T(8,128)(2,1)S(1)} %get-tuple-element.79.refs_3_), channel_id=1, source_target_pairs={{0,16},{8,24},{16,0},{24,8},{1,17},{9,25},{17,1},{25,9},{2,18},{10... | collective-permute-start | bytes 393224 | tf_op jit(solution)/shard_map/ppermute | solution.py:312
  65.0 3.0 %collective-permute-start.22 = (bf16[2,2,64,256]{3,2,1,0:T(8,128)(2,1)S(1)}, bf16[2,2,64,256]{3,2,1,0:T(8,128)(2,1)S(1)}, u32[]{:S(2)}, u32[]{:S(2)}) collective-permute-start(bf16[2,2,64,256]{3,2,1,0:T(8,128)(2,1)S(1)} %get-tuple-element.80.refs_4_), channel_id=1, source_target_pairs={{0,24},{8,16},{16,8},{24,0},{1,25},{9,17},{17,9},{25,1},{2,26},{10... | collective-permute-start | bytes 393224 | tf_op jit(solution)/shard_map/ppermute | solution.py:312
  68.1 0.9 collective-permute-done.15.refs_6_
  68.9 2.5 %shard_map.78 = (bf16[8,2,64,256]{3,2,1,0:T(8,128)(2,1)S(1)}, bf16[2,8,64,256]{3,2,1,0:T(8,128)(2,1)S(1)}, bf16[2,2,64,256]{3,2,1,0:T(8,128)(2,1)S(1)}, bf16[2,2...) custom-call(s32[2]{0:T(128)S(1)} %copy-done.5, f32[8,8]{1,0:T(8,128)S(1)} %convert_element_type.3.fock, ...), custom_call_target="tpu_custom_call" | custom-call | flops 30000001024 | bytes 5242880 | tf_op jit(solution)/shard_map/pallas_call | solution.py:42
  71.5 7.2 %collective-permute-start.26 = (bf16[2,2,64,256]{3,2,1,0:T(8,128)(2,1)S(1)}, bf16[2,2,64,256]{3,2,1,0:T(8,128)(2,1)S(1)}, u32[]{:S(2)}, u32[]{:S(2)}) collective-permute-start(bf16[2,2,64,256]{3,2,1,0:T(8,128)(2,1)S(1)} %get-tuple-element.88), channel_id=1, source_target_pairs={{0,8},{8,0},{16,24},{24,16},{1,9},{9,1},{17,25},{25,17},{2,10},{10... | collective-permute-start | bytes 393224 | tf_op jit(solution)/shard_map/ppermute | solution.py:312
  78.7 0.9 collective-permute-start.27
  79.6 1.6 %collective-permute-start.28 = (bf16[2,2,64,256]{3,2,1,0:T(8,128)(2,1)S(1)}, bf16[2,2,64,256]{3,2,1,0:T(8,128)(2,1)S(1)}, u32[]{:S(2)}, u32[]{:S(2)}) collective-permute-start(bf16[2,2,64,256]{3,2,1,0:T(8,128)(2,1)S(1)} %get-tuple-element.90), channel_id=1, source_target_pairs={{0,24},{8,16},{16,8},{24,0},{1,25},{9,17},{17,9},{25,1},{2,26},{10... | collective-permute-start | bytes 393224 | tf_op jit(solution)/shard_map/ppermute | solution.py:312
  81.2 0.1 collective-permute-done.21.refs_7_
  81.3 3.6 %shard_map.80 = (bf16[8,2,128,256]{3,2,1,0:T(8,128)(2,1)}, bf16[2,8,64,256]{3,2,1,0:T(8,128)(2,1)S(1)}, bf16[2,2,64,256]{3,2,1,0:T(8,128)(2,1)S(1)}, bf16[2,2,64...) custom-call(s32[2]{0:T(128)S(1)} %copy-done.5, f32[8,8]{1,0:T(8,128)S(1)} %convert_element_type.3.fock, ...), custom_call_target="tpu_custom_call" | custom-call | flops 30000001024 | bytes 5242880 | tf_op jit(solution)/shard_map/pallas_call | solution.py:42
  84.9 0.8 copy-done.9
  85.7 4.8 %collective-permute-start.23 = (bf16[2,2,64,256]{3,2,1,0:T(8,128)(2,1)S(1)}, bf16[2,2,64,256]{3,2,1,0:T(8,128)(2,1)S(1)}, u32[]{:S(2)}, u32[]{:S(2)}) collective-permute-start(bf16[2,2,64,256]{3,2,1,0:T(8,128)(2,1)S(1)} %get-tuple-element.84), channel_id=1, source_target_pairs={{0,8},{8,0},{16,24},{24,16},{1,9},{9,1},{17,25},{25,17},{2,10},{10... | collective-permute-start | bytes 393224 | tf_op jit(solution)/shard_map/ppermute | solution.py:312
  90.5 2.1 %collective-permute-start.24 = (bf16[2,2,64,256]{3,2,1,0:T(8,128)(2,1)S(1)}, bf16[2,2,64,256]{3,2,1,0:T(8,128)(2,1)S(1)}, u32[]{:S(2)}, u32[]{:S(2)}) collective-permute-start(bf16[2,2,64,256]{3,2,1,0:T(8,128)(2,1)S(1)} %get-tuple-element.85), channel_id=1, source_target_pairs={{0,16},{8,24},{16,0},{24,8},{1,17},{9,25},{17,1},{25,9},{2,18},{10... | collective-permute-start | bytes 393224 | tf_op jit(solution)/shard_map/ppermute | solution.py:312
  92.5 3.6 %all-to-all-start.1 = ((bf16[8,2,128,256]{3,2,1,0:T(8,128)(2,1)}), bf16[8,2,128,256]{3,2,1,0:T(8,128)(2,1)S(1)}, u32[]{:S(2)}, u32[]{:S(2)}) async-start(bf16[8,2,128,256]{3,2,1,0:T(8,128)(2,1)} %get-tuple-element.81), calls=%async_computation.1 | async-start | bytes 2097152 | tf_op jit(solution)/shard_map/all_to_all | solution.py:299
  96.1 1.5 %collective-permute-start.25 = (bf16[2,2,64,256]{3,2,1,0:T(8,128)(2,1)S(1)}, bf16[2,2,64,256]{3,2,1,0:T(8,128)(2,1)S(1)}, u32[]{:S(2)}, u32[]{:S(2)}) collective-permute-start(bf16[2,2,64,256]{3,2,1,0:T(8,128)(2,1)S(1)} %get-tuple-element.86), channel_id=1, source_target_pairs={{0,24},{8,16},{16,8},{24,0},{1,25},{9,17},{17,9},{25,1},{2,26},{10... | collective-permute-start | bytes 393224 | tf_op jit(solution)/shard_map/ppermute | solution.py:312
  97.7 1.4 %copy-done.7 = bf16[512,1536]{1,0:T(8,128)(2,1)S(1)} copy-done((bf16[512,1536]{1,0:T(8,128)(2,1)S(1)}, bf16[512,1536]{1,0:T(8,128)(2,1)}, u32[]{:S(2)}) %copy-start.7) | copy-done | bytes 1572888
  99.1 1.1 shard_map.82.refs_3_
  100.1 3.7 %collective-permute-done.25.refs_2_ = bf16[2,2,64,256]{3,2,1,0:T(8,128)(2,1)S(1)} collective-permute-done((bf16[2,2,64,256]{3,2,1,0:T(8,128)(2,1)S(1)}, bf16[2,2,64,256]{3,2,1,0:T(8,128)(2,1)S(1)}, u32[]{:S(2)}, u32[]{:S(2)}) %collective-permute-start.25) | collective-permute-done | bytes 131104 | tf_op jit(solution)/shard_map/ppermute | solution.py:312
  103.8 1.2 shard_map.83
  105.1 1.7 %collective-permute-start.30 = (bf16[2,128,256]{2,1,0:T(8,128)(2,1)S(1)}, bf16[2,128,256]{2,1,0:T(8,128)(2,1)S(1)}, u32[]{:S(2)}, u32[]{:S(2)}) collective-permute-start(bf16[2,128,256]{2,1,0:T(8,128)(2,1)S(1)} %get-tuple-element.93), channel_id=1, source_target_pairs={{0,2},{1,3},{2,0},{3,1},{4,6},{5,7},{6,4},{7,5},{8,10},{9,11},{10,... | collective-permute-start | bytes 393224 | tf_op jit(solution)/shard_map/ppermute | solution.py:305
  106.8 0.1 collective-permute-start.31
  106.9 2.2 %collective-permute-start.32 = (bf16[2,128,256]{2,1,0:T(8,128)(2,1)S(1)}, bf16[2,128,256]{2,1,0:T(8,128)(2,1)S(1)}, u32[]{:S(2)}, u32[]{:S(2)}) collective-permute-start(bf16[2,128,256]{2,1,0:T(8,128)(2,1)S(1)} %get-tuple-element.95), channel_id=1, source_target_pairs={{0,4},{1,5},{2,6},{3,7},{4,0},{5,1},{6,2},{7,3},{8,12},{9,13},{10,... | collective-permute-start | bytes 393224 | tf_op jit(solution)/shard_map/ppermute | solution.py:305
  109.2 2.9 %collective-permute-start.34 = (bf16[2,128,256]{2,1,0:T(8,128)(2,1)S(1)}, bf16[2,128,256]{2,1,0:T(8,128)(2,1)S(1)}, u32[]{:S(2)}, u32[]{:S(2)}) collective-permute-start(bf16[2,128,256]{2,1,0:T(8,128)(2,1)S(1)} %get-tuple-element.97), channel_id=1, source_target_pairs={{0,6},{1,7},{2,4},{3,5},{4,2},{5,3},{6,0},{7,1},{8,14},{9,15},{10,... | collective-permute-start | bytes 393224 | tf_op jit(solution)/shard_map/ppermute | solution.py:305
  112.0 1.8 %collective-permute-done.30.refs_2_ = bf16[2,128,256]{2,1,0:T(8,128)(2,1)S(1)} collective-permute-done((bf16[2,128,256]{2,1,0:T(8,128)(2,1)S(1)}, bf16[2,128,256]{2,1,0:T(8,128)(2,1)S(1)}, u32[]{:S(2)}, u32[]{:S(2)}) %collective-permute-start.30) | collective-permute-done | bytes 131104 | tf_op jit(solution)/shard_map/ppermute | solution.py:305
  113.8 0.4 collective-permute-start.35
  114.2 0.1 broadcast_in_dim.4.row
  114.3 1.4 %copy-done.8 = bf16[512,1536]{1,0:T(8,128)(2,1)S(1)} copy-done((bf16[512,1536]{1,0:T(8,128)(2,1)S(1)}, bf16[512,1536]{1,0:T(8,128)(2,1)}, u32[]{:S(2)}) %copy-start.8) | copy-done | bytes 1572888
  115.7 7.8 %shard_map.81.source = f32[2,512,512]{2,1,0:T(8,128)} custom-call(s32[2]{0:T(128)S(1)} %copy-done.5, f32[8]{0:T(128)S(1)} %copy-done.6, f32[2,512,512]{2,1,0:T(8,128)} %bitcast.14, bf16[8,2,128,256]{3,2,1,0:T(8,128)(2,1)S(1)} %all-to-all-done.1.blocks, f32[512,128]{1,0:T(8,128)S(1)} %broadcast_in_dim.4.row, f32[1,512]{1,0:T(1,128)S(1)} %bitcast.20, ...), custom_call_target="tpu_custom_call" | custom-call | flops 3221225472 | bytes 6291456 | tf_op jit(solution)/shard_map/pallas_call | solution.py:427
  123.5 2.8 %shard_map.84 = f32[2,512,512]{2,1,0:T(8,128)} custom-call(s32[2]{0:T(128)S(1)} %copy-done.5, f32[2,512,512]{2,1,0:T(8,128)} %shard_map.81.source, bf16[2,128,256]{2,1,0:T(8,128)(2,1)S(1)} %get-tuple-element.91.refs_0_, bf16[2,128,256]{2,1,0:T(8,128)(2,1)S(1)} %collective-permute-done.29.refs_1_, ...), custom_call_target="tpu_custom_call", output_to_operand_aliasing={{}: (1, {})} | custom-call | flops 524288 | bytes 5242880 | tf_op jit(solution)/shard_map/pallas_call | solution.py:450
  (66 shorter events, 0.6 us)
Async XLA Ops:
  0.0 10.2 %copy-start.14 = (s32[8]{0:T(128)S(1)}, s32[8]{0:T(128)}, u32[]{:S(2)}) copy-start(s32[8]{0:T(128)} %constant.25.clone) | copy-start | bytes 100
  0.0 11.4 %copy-start.13 = (s32[8]{0:T(128)S(1)}, s32[8]{0:T(128)}, u32[]{:S(2)}) copy-start(s32[8]{0:T(128)} %constant.24.clone) | copy-start | bytes 100
  0.0 16.0 %copy-start.2 = (f32[512]{0:T(512)S(1)}, f32[512]{0:T(512)}, u32[]{:S(2)}) copy-start(f32[512]{0:T(512)} %param.11) | copy-start | bytes 6148
  0.0 12.7 %collective-permute-start = (bf16[3,64,512]{2,1,0:T(8,128)(2,1)}, bf16[3,64,512]{2,1,0:T(8,128)(2,1)S(1)}, u32[]{:S(2)}, u32[]{:S(2)}) collective-permute-start(bf16[3,64,512]{2,1,0:T(8,128)(2,1)} %refs_0_.1), channel_id=1, source_target_pairs={{0,2},{1,3},{2,0},{3,1},{4,6},{5,7},{6,4},{7,5},{8,10},{9,11},{10,... | collective-permute-start | bytes 589832 | tf_op jit(solution)/shard_map/ppermute | solution.py:338
  3.0 12.8 %collective-permute-start.1 = (bf16[3,64,512]{2,1,0:T(8,128)(2,1)}, bf16[3,64,512]{2,1,0:T(8,128)(2,1)S(1)}, u32[]{:S(2)}, u32[]{:S(2)}) collective-permute-start(bf16[3,64,512]{2,1,0:T(8,128)(2,1)} %refs_0_.1), channel_id=1, source_target_pairs={{0,4},{1,5},{2,6},{3,7},{4,0},{5,1},{6,2},{7,3},{8,12},{9,13},{10,... | collective-permute-start | bytes 589832 | tf_op jit(solution)/shard_map/ppermute | solution.py:338
  4.5 11.2 %collective-permute-start.2 = (bf16[3,64,512]{2,1,0:T(8,128)(2,1)}, bf16[3,64,512]{2,1,0:T(8,128)(2,1)S(1)}, u32[]{:S(2)}, u32[]{:S(2)}) collective-permute-start(bf16[3,64,512]{2,1,0:T(8,128)(2,1)} %refs_0_.1), channel_id=1, source_target_pairs={{0,6},{1,7},{2,4},{3,5},{4,2},{5,3},{6,0},{7,1},{8,14},{9,15},{10,... | collective-permute-start | bytes 589832 | tf_op jit(solution)/shard_map/ppermute | solution.py:338
  4.6 23.7 %copy-start.4 = (s32[2]{0:T(128)}, s32[2]{0:T(128)S(1)}, u32[]{:S(2)}) copy-start(s32[2]{0:T(128)S(1)} %pad_add_fusion.place.source) | copy-start | bytes 28
  4.6 1.6 %copy-start = (f32[2,1,512,512]{3,2,1,0:T(8,128)S(1)}, f32[2,1,512,512]{3,2,1,0:T(8,128)}, u32[]{:S(2)}) copy-start(f32[2,1,512,512]{3,2,1,0:T(8,128)} %param.7) | copy-start | bytes 6291460
  6.2 9.6 %copy-start.1 = (bf16[3,64,512]{2,1,0:T(8,128)(2,1)S(1)}, bf16[3,64,512]{2,1,0:T(8,128)(2,1)}, u32[]{:S(2)}) copy-start(bf16[3,64,512]{2,1,0:T(8,128)(2,1)} %refs_0_.1) | copy-start | bytes 589828
  7.1 9.2 %collective-permute-start.10 = (bf16[2,128,256]{2,1,0:T(8,128)(2,1)S(1)}, bf16[2,128,256]{2,1,0:T(8,128)(2,1)S(1)}, u32[]{:S(2)}, u32[]{:S(2)}) collective-permute-start(bf16[2,128,256]{2,1,0:T(8,128)(2,1)S(1)} %get-tuple-element.62), channel_id=1, source_target_pairs={{0,7},{1,6},{2,5},{3,4},{4,3},{5,2},{6,1},{7,0},{8,15},{9,14},{10,... | collective-permute-start | bytes 393224 | tf_op jit(solution)/shard_map/ppermute | solution.py:305
  8.7 10.1 %collective-permute-start.4 = (bf16[2,128,256]{2,1,0:T(8,128)(2,1)S(1)}, bf16[2,128,256]{2,1,0:T(8,128)(2,1)S(1)}, u32[]{:S(2)}, u32[]{:S(2)}) collective-permute-start(bf16[2,128,256]{2,1,0:T(8,128)(2,1)S(1)} %get-tuple-element.56), channel_id=1, source_target_pairs={{0,1},{1,0},{2,3},{3,2},{4,5},{5,4},{6,7},{7,6},{8,9},{9,8},{10,11... | collective-permute-start | bytes 393224 | tf_op jit(solution)/shard_map/ppermute | solution.py:305
  12.7 15.4 %collective-permute-start.5 = (bf16[2,128,256]{2,1,0:T(8,128)(2,1)S(1)}, bf16[2,128,256]{2,1,0:T(8,128)(2,1)S(1)}, u32[]{:S(2)}, u32[]{:S(2)}) collective-permute-start(bf16[2,128,256]{2,1,0:T(8,128)(2,1)S(1)} %get-tuple-element.57), channel_id=1, source_target_pairs={{0,2},{1,3},{2,0},{3,1},{4,6},{5,7},{6,4},{7,5},{8,10},{9,11},{10,... | collective-permute-start | bytes 393224 | tf_op jit(solution)/shard_map/ppermute | solution.py:305
  15.8 12.3 %collective-permute-start.6 = (bf16[2,128,256]{2,1,0:T(8,128)(2,1)S(1)}, bf16[2,128,256]{2,1,0:T(8,128)(2,1)S(1)}, u32[]{:S(2)}, u32[]{:S(2)}) collective-permute-start(bf16[2,128,256]{2,1,0:T(8,128)(2,1)S(1)} %get-tuple-element.58), channel_id=1, source_target_pairs={{0,3},{1,2},{2,1},{3,0},{4,7},{5,6},{6,5},{7,4},{8,11},{9,10},{10,... | collective-permute-start | bytes 393224 | tf_op jit(solution)/shard_map/ppermute | solution.py:305
  15.9 3.0 %collective-permute-start.3 = (bf16[4,3,64,512]{3,2,1,0:T(8,128)(2,1)S(1)}, bf16[4,3,64,512]{3,2,1,0:T(8,128)(2,1)S(1)}, u32[]{:S(2)}, u32[]{:S(2)}) collective-permute-start(bf16[4,3,64,512]{3,2,1,0:T(8,128)(2,1)S(1)} %pad_maximum_fusion), channel_id=1, source_target_pairs={{0,1},{1,0},{2,3},{3,2},{4,5},{5,4},{6,7},{7,6},{8,9},{9,8},{10,11... | collective-permute-start | bytes 2359304 | tf_op jit(solution)/shard_map/ppermute | solution.py:338
  16.3 11.7 %collective-permute-start.7 = (bf16[2,128,256]{2,1,0:T(8,128)(2,1)S(1)}, bf16[2,128,256]{2,1,0:T(8,128)(2,1)S(1)}, u32[]{:S(2)}, u32[]{:S(2)}) collective-permute-start(bf16[2,128,256]{2,1,0:T(8,128)(2,1)S(1)} %get-tuple-element.59), channel_id=1, source_target_pairs={{0,4},{1,5},{2,6},{3,7},{4,0},{5,1},{6,2},{7,3},{8,12},{9,13},{10,... | collective-permute-start | bytes 393224 | tf_op jit(solution)/shard_map/ppermute | solution.py:305
  18.8 9.6 %collective-permute-start.8 = (bf16[2,128,256]{2,1,0:T(8,128)(2,1)S(1)}, bf16[2,128,256]{2,1,0:T(8,128)(2,1)S(1)}, u32[]{:S(2)}, u32[]{:S(2)}) collective-permute-start(bf16[2,128,256]{2,1,0:T(8,128)(2,1)S(1)} %get-tuple-element.60), channel_id=1, source_target_pairs={{0,5},{1,4},{2,7},{3,6},{4,1},{5,0},{6,3},{7,2},{8,13},{9,12},{10,... | collective-permute-start | bytes 393224 | tf_op jit(solution)/shard_map/ppermute | solution.py:305
  18.9 14.6 %copy-start.12 = (bf16[8,8]{1,0:T(8,128)(2,1)S(1)}, bf16[8,8]{1,0:T(8,128)(2,1)}, u32[]{:S(2)}) copy-start(bf16[8,8]{1,0:T(8,128)(2,1)} %param.9) | copy-start | bytes 388
  18.9 9.4 %collective-permute-start.9 = (bf16[2,128,256]{2,1,0:T(8,128)(2,1)S(1)}, bf16[2,128,256]{2,1,0:T(8,128)(2,1)S(1)}, u32[]{:S(2)}, u32[]{:S(2)}) collective-permute-start(bf16[2,128,256]{2,1,0:T(8,128)(2,1)S(1)} %get-tuple-element.61), channel_id=1, source_target_pairs={{0,6},{1,7},{2,4},{3,5},{4,2},{5,3},{6,0},{7,1},{8,14},{9,15},{10,... | collective-permute-start | bytes 393224 | tf_op jit(solution)/shard_map/ppermute | solution.py:305
  29.0 12.4 %collective-permute-start.11 = (bf16[2,2,64,256]{3,2,1,0:T(8,128)(2,1)S(1)}, bf16[2,2,64,256]{3,2,1,0:T(8,128)(2,1)S(1)}, u32[]{:S(2)}, u32[]{:S(2)}) collective-permute-start(bf16[2,2,64,256]{3,2,1,0:T(8,128)(2,1)S(1)} %get-tuple-element.64), channel_id=1, source_target_pairs={{0,8},{8,0},{16,24},{24,16},{1,9},{9,1},{17,25},{25,17},{2,10},{10... | collective-permute-start | bytes 393224 | tf_op jit(solution)/shard_map/ppermute | solution.py:312
  30.6 12.9 %collective-permute-start.12 = (bf16[2,2,64,256]{3,2,1,0:T(8,128)(2,1)S(1)}, bf16[2,2,64,256]{3,2,1,0:T(8,128)(2,1)S(1)}, u32[]{:S(2)}, u32[]{:S(2)}) collective-permute-start(bf16[2,2,64,256]{3,2,1,0:T(8,128)(2,1)S(1)} %get-tuple-element.65), channel_id=1, source_target_pairs={{0,16},{8,24},{16,0},{24,8},{1,17},{9,25},{17,1},{25,9},{2,18},{10... | collective-permute-start | bytes 393224 | tf_op jit(solution)/shard_map/ppermute | solution.py:312
  33.2 10.3 %collective-permute-start.13 = (bf16[2,2,64,256]{3,2,1,0:T(8,128)(2,1)S(1)}, bf16[2,2,64,256]{3,2,1,0:T(8,128)(2,1)S(1)}, u32[]{:S(2)}, u32[]{:S(2)}) collective-permute-start(bf16[2,2,64,256]{3,2,1,0:T(8,128)(2,1)S(1)} %get-tuple-element.66), channel_id=1, source_target_pairs={{0,24},{8,16},{16,8},{24,0},{1,25},{9,17},{17,9},{25,1},{2,26},{10... | collective-permute-start | bytes 393224 | tf_op jit(solution)/shard_map/ppermute | solution.py:312
  33.6 18.9 %all-to-all-start = ((bf16[8,2,128,256]{3,2,1,0:T(8,128)(2,1)}), bf16[8,2,128,256]{3,2,1,0:T(8,128)(2,1)S(1)}, u32[]{:S(2)}, u32[]{:S(2)}) async-start(bf16[8,2,128,256]{3,2,1,0:T(8,128)(2,1)} %get-tuple-element.54), calls=%async_computation | async-start | bytes 2097152 | tf_op jit(solution)/shard_map/all_to_all | solution.py:299
  37.2 21.8 %collective-permute-start.17 = (bf16[2,2,64,256]{3,2,1,0:T(8,128)(2,1)S(1)}, bf16[2,2,64,256]{3,2,1,0:T(8,128)(2,1)S(1)}, u32[]{:S(2)}, u32[]{:S(2)}) collective-permute-start(bf16[2,2,64,256]{3,2,1,0:T(8,128)(2,1)S(1)} %get-tuple-element.74), channel_id=1, source_target_pairs={{0,8},{8,0},{16,24},{24,16},{1,9},{9,1},{17,25},{25,17},{2,10},{10... | collective-permute-start | bytes 393224 | tf_op jit(solution)/shard_map/ppermute | solution.py:312
  37.9 21.3 %collective-permute-start.18 = (bf16[2,2,64,256]{3,2,1,0:T(8,128)(2,1)S(1)}, bf16[2,2,64,256]{3,2,1,0:T(8,128)(2,1)S(1)}, u32[]{:S(2)}, u32[]{:S(2)}) collective-permute-start(bf16[2,2,64,256]{3,2,1,0:T(8,128)(2,1)S(1)} %get-tuple-element.75), channel_id=1, source_target_pairs={{0,16},{8,24},{16,0},{24,8},{1,17},{9,25},{17,1},{25,9},{2,18},{10... | collective-permute-start | bytes 393224 | tf_op jit(solution)/shard_map/ppermute | solution.py:312
  41.4 17.8 %collective-permute-start.19 = (bf16[2,2,64,256]{3,2,1,0:T(8,128)(2,1)S(1)}, bf16[2,2,64,256]{3,2,1,0:T(8,128)(2,1)S(1)}, u32[]{:S(2)}, u32[]{:S(2)}) collective-permute-start(bf16[2,2,64,256]{3,2,1,0:T(8,128)(2,1)S(1)} %get-tuple-element.76), channel_id=1, source_target_pairs={{0,24},{8,16},{16,8},{24,0},{1,25},{9,17},{17,9},{25,1},{2,26},{10... | collective-permute-start | bytes 393224 | tf_op jit(solution)/shard_map/ppermute | solution.py:312
  44.8 14.4 %copy-start.5 = (s32[2]{0:T(128)S(1)}, s32[2]{0:T(128)}, u32[]{:S(2)}) copy-start(s32[2]{0:T(128)} %copy-done.4) | copy-start | bytes 28
  52.5 0.7 copy-start.11
  54.7 10.3 %collective-permute-start.14 = (bf16[2,2,64,256]{3,2,1,0:T(8,128)(2,1)S(1)}, bf16[2,2,64,256]{3,2,1,0:T(8,128)(2,1)S(1)}, u32[]{:S(2)}, u32[]{:S(2)}) collective-permute-start(bf16[2,2,64,256]{3,2,1,0:T(8,128)(2,1)S(1)} %get-tuple-element.69.refs_1_), channel_id=1, source_target_pairs={{0,8},{8,0},{16,24},{24,16},{1,9},{9,1},{17,25},{25,17},{2,10},{10... | collective-permute-start | bytes 393224 | tf_op jit(solution)/shard_map/ppermute | solution.py:312
  56.1 12.9 %collective-permute-start.15 = (bf16[2,2,64,256]{3,2,1,0:T(8,128)(2,1)S(1)}, bf16[2,2,64,256]{3,2,1,0:T(8,128)(2,1)S(1)}, u32[]{:S(2)}, u32[]{:S(2)}) collective-permute-start(bf16[2,2,64,256]{3,2,1,0:T(8,128)(2,1)S(1)} %get-tuple-element.70.refs_2_), channel_id=1, source_target_pairs={{0,16},{8,24},{16,0},{24,8},{1,17},{9,25},{17,1},{25,9},{2,18},{10... | collective-permute-start | bytes 393224 | tf_op jit(solution)/shard_map/ppermute | solution.py:312
  59.0 10.0 %collective-permute-start.16 = (bf16[2,2,64,256]{3,2,1,0:T(8,128)(2,1)S(1)}, bf16[2,2,64,256]{3,2,1,0:T(8,128)(2,1)S(1)}, u32[]{:S(2)}, u32[]{:S(2)}) collective-permute-start(bf16[2,2,64,256]{3,2,1,0:T(8,128)(2,1)S(1)} %get-tuple-element.71.refs_3_), channel_id=1, source_target_pairs={{0,24},{8,16},{16,8},{24,0},{1,25},{9,17},{17,9},{25,1},{2,26},{10... | collective-permute-start | bytes 393224 | tf_op jit(solution)/shard_map/ppermute | solution.py:312
  59.2 9.8 %copy-start.6 = (f32[8]{0:T(128)S(1)}, f32[8]{0:T(128)}, u32[]{:S(2)}) copy-start(f32[8]{0:T(128)} %occ.9) | copy-start | bytes 100
  60.8 18.8 %collective-permute-start.20 = (bf16[2,2,64,256]{3,2,1,0:T(8,128)(2,1)S(1)}, bf16[2,2,64,256]{3,2,1,0:T(8,128)(2,1)S(1)}, u32[]{:S(2)}, u32[]{:S(2)}) collective-permute-start(bf16[2,2,64,256]{3,2,1,0:T(8,128)(2,1)S(1)} %get-tuple-element.78.refs_2_), channel_id=1, source_target_pairs={{0,8},{8,0},{16,24},{24,16},{1,9},{9,1},{17,25},{25,17},{2,10},{10... | collective-permute-start | bytes 393224 | tf_op jit(solution)/shard_map/ppermute | solution.py:312
  61.2 20.0 %collective-permute-start.21 = (bf16[2,2,64,256]{3,2,1,0:T(8,128)(2,1)S(1)}, bf16[2,2,64,256]{3,2,1,0:T(8,128)(2,1)S(1)}, u32[]{:S(2)}, u32[]{:S(2)}) collective-permute-start(bf16[2,2,64,256]{3,2,1,0:T(8,128)(2,1)S(1)} %get-tuple-element.79.refs_3_), channel_id=1, source_target_pairs={{0,16},{8,24},{16,0},{24,8},{1,17},{9,25},{17,1},{25,9},{2,18},{10... | collective-permute-start | bytes 393224 | tf_op jit(solution)/shard_map/ppermute | solution.py:312
  65.0 16.2 %collective-permute-start.22 = (bf16[2,2,64,256]{3,2,1,0:T(8,128)(2,1)S(1)}, bf16[2,2,64,256]{3,2,1,0:T(8,128)(2,1)S(1)}, u32[]{:S(2)}, u32[]{:S(2)}) collective-permute-start(bf16[2,2,64,256]{3,2,1,0:T(8,128)(2,1)S(1)} %get-tuple-element.80.refs_4_), channel_id=1, source_target_pairs={{0,24},{8,16},{16,8},{24,0},{1,25},{9,17},{17,9},{25,1},{2,26},{10... | collective-permute-start | bytes 393224 | tf_op jit(solution)/shard_map/ppermute | solution.py:312
  71.5 24.6 %collective-permute-start.26 = (bf16[2,2,64,256]{3,2,1,0:T(8,128)(2,1)S(1)}, bf16[2,2,64,256]{3,2,1,0:T(8,128)(2,1)S(1)}, u32[]{:S(2)}, u32[]{:S(2)}) collective-permute-start(bf16[2,2,64,256]{3,2,1,0:T(8,128)(2,1)S(1)} %get-tuple-element.88), channel_id=1, source_target_pairs={{0,8},{8,0},{16,24},{24,16},{1,9},{9,1},{17,25},{25,17},{2,10},{10... | collective-permute-start | bytes 393224 | tf_op jit(solution)/shard_map/ppermute | solution.py:312
  78.7 18.9 %collective-permute-start.27 = (bf16[2,2,64,256]{3,2,1,0:T(8,128)(2,1)S(1)}, bf16[2,2,64,256]{3,2,1,0:T(8,128)(2,1)S(1)}, u32[]{:S(2)}, u32[]{:S(2)}) collective-permute-start(bf16[2,2,64,256]{3,2,1,0:T(8,128)(2,1)S(1)} %get-tuple-element.89), channel_id=1, source_target_pairs={{0,16},{8,24},{16,0},{24,8},{1,17},{9,25},{17,1},{25,9},{2,18},{10... | collective-permute-start | bytes 393224 | tf_op jit(solution)/shard_map/ppermute | solution.py:312
  79.6 18.0 %collective-permute-start.28 = (bf16[2,2,64,256]{3,2,1,0:T(8,128)(2,1)S(1)}, bf16[2,2,64,256]{3,2,1,0:T(8,128)(2,1)S(1)}, u32[]{:S(2)}, u32[]{:S(2)}) collective-permute-start(bf16[2,2,64,256]{3,2,1,0:T(8,128)(2,1)S(1)} %get-tuple-element.90), channel_id=1, source_target_pairs={{0,24},{8,16},{16,8},{24,0},{1,25},{9,17},{17,9},{25,1},{2,26},{10... | collective-permute-start | bytes 393224 | tf_op jit(solution)/shard_map/ppermute | solution.py:312
  84.9 0.8 copy-start.9
  85.7 14.5 %collective-permute-start.23 = (bf16[2,2,64,256]{3,2,1,0:T(8,128)(2,1)S(1)}, bf16[2,2,64,256]{3,2,1,0:T(8,128)(2,1)S(1)}, u32[]{:S(2)}, u32[]{:S(2)}) collective-permute-start(bf16[2,2,64,256]{3,2,1,0:T(8,128)(2,1)S(1)} %get-tuple-element.84), channel_id=1, source_target_pairs={{0,8},{8,0},{16,24},{24,16},{1,9},{9,1},{17,25},{25,17},{2,10},{10... | collective-permute-start | bytes 393224 | tf_op jit(solution)/shard_map/ppermute | solution.py:312
  90.5 9.7 %collective-permute-start.24 = (bf16[2,2,64,256]{3,2,1,0:T(8,128)(2,1)S(1)}, bf16[2,2,64,256]{3,2,1,0:T(8,128)(2,1)S(1)}, u32[]{:S(2)}, u32[]{:S(2)}) collective-permute-start(bf16[2,2,64,256]{3,2,1,0:T(8,128)(2,1)S(1)} %get-tuple-element.85), channel_id=1, source_target_pairs={{0,16},{8,24},{16,0},{24,8},{1,17},{9,25},{17,1},{25,9},{2,18},{10... | collective-permute-start | bytes 393224 | tf_op jit(solution)/shard_map/ppermute | solution.py:312
  92.5 21.6 %all-to-all-start.1 = ((bf16[8,2,128,256]{3,2,1,0:T(8,128)(2,1)}), bf16[8,2,128,256]{3,2,1,0:T(8,128)(2,1)S(1)}, u32[]{:S(2)}, u32[]{:S(2)}) async-start(bf16[8,2,128,256]{3,2,1,0:T(8,128)(2,1)} %get-tuple-element.81), calls=%async_computation.1 | async-start | bytes 2097152 | tf_op jit(solution)/shard_map/all_to_all | solution.py:299
  96.1 7.7 %collective-permute-start.25 = (bf16[2,2,64,256]{3,2,1,0:T(8,128)(2,1)S(1)}, bf16[2,2,64,256]{3,2,1,0:T(8,128)(2,1)S(1)}, u32[]{:S(2)}, u32[]{:S(2)}) collective-permute-start(bf16[2,2,64,256]{3,2,1,0:T(8,128)(2,1)S(1)} %get-tuple-element.86), channel_id=1, source_target_pairs={{0,24},{8,16},{16,8},{24,0},{1,25},{9,17},{17,9},{25,1},{2,26},{10... | collective-permute-start | bytes 393224 | tf_op jit(solution)/shard_map/ppermute | solution.py:312
  97.6 1.4 %copy-start.7 = (bf16[512,1536]{1,0:T(8,128)(2,1)S(1)}, bf16[512,1536]{1,0:T(8,128)(2,1)}, u32[]{:S(2)}) copy-start(bf16[512,1536]{1,0:T(8,128)(2,1)} %get-tuple-element.82.whole.refs_3_) | copy-start | bytes 4718596
  99.1 4.8 %copy-start.10 = (bf16[2,8,64,256]{3,2,1,0:T(8,128)(2,1)S(1)}, bf16[2,8,64,256]{3,2,1,0:T(8,128)(2,1)}, u32[]{:S(2)}) copy-start(bf16[2,8,64,256]{3,2,1,0:T(8,128)(2,1)} %copy-done.9) | copy-start | bytes 1572868
  103.8 10.3 %copy-start.3 = (f32[512]{0:T(512)S(1)}, f32[512]{0:T(512)}, u32[]{:S(2)}) copy-start(f32[512]{0:T(512)} %param.11) | copy-start | bytes 6148
  105.0 4.2 %collective-permute-start.29 = (bf16[2,128,256]{2,1,0:T(8,128)(2,1)S(1)}, bf16[2,128,256]{2,1,0:T(8,128)(2,1)S(1)}, u32[]{:S(2)}, u32[]{:S(2)}) collective-permute-start(bf16[2,128,256]{2,1,0:T(8,128)(2,1)S(1)} %get-tuple-element.92), channel_id=1, source_target_pairs={{0,1},{1,0},{2,3},{3,2},{4,5},{5,4},{6,7},{7,6},{8,9},{9,8},{10,11... | collective-permute-start | bytes 393224 | tf_op jit(solution)/shard_map/ppermute | solution.py:305
  105.1 8.7 %collective-permute-start.30 = (bf16[2,128,256]{2,1,0:T(8,128)(2,1)S(1)}, bf16[2,128,256]{2,1,0:T(8,128)(2,1)S(1)}, u32[]{:S(2)}, u32[]{:S(2)}) collective-permute-start(bf16[2,128,256]{2,1,0:T(8,128)(2,1)S(1)} %get-tuple-element.93), channel_id=1, source_target_pairs={{0,2},{1,3},{2,0},{3,1},{4,6},{5,7},{6,4},{7,5},{8,10},{9,11},{10,... | collective-permute-start | bytes 393224 | tf_op jit(solution)/shard_map/ppermute | solution.py:305
  106.8 16.7 %collective-permute-start.31 = (bf16[2,128,256]{2,1,0:T(8,128)(2,1)S(1)}, bf16[2,128,256]{2,1,0:T(8,128)(2,1)S(1)}, u32[]{:S(2)}, u32[]{:S(2)}) collective-permute-start(bf16[2,128,256]{2,1,0:T(8,128)(2,1)S(1)} %get-tuple-element.94), channel_id=1, source_target_pairs={{0,3},{1,2},{2,1},{3,0},{4,7},{5,6},{6,5},{7,4},{8,11},{9,10},{10,... | collective-permute-start | bytes 393224 | tf_op jit(solution)/shard_map/ppermute | solution.py:305
  106.9 16.6 %collective-permute-start.32 = (bf16[2,128,256]{2,1,0:T(8,128)(2,1)S(1)}, bf16[2,128,256]{2,1,0:T(8,128)(2,1)S(1)}, u32[]{:S(2)}, u32[]{:S(2)}) collective-permute-start(bf16[2,128,256]{2,1,0:T(8,128)(2,1)S(1)} %get-tuple-element.95), channel_id=1, source_target_pairs={{0,4},{1,5},{2,6},{3,7},{4,0},{5,1},{6,2},{7,3},{8,12},{9,13},{10,... | collective-permute-start | bytes 393224 | tf_op jit(solution)/shard_map/ppermute | solution.py:305
  109.2 14.3 %collective-permute-start.33 = (bf16[2,128,256]{2,1,0:T(8,128)(2,1)S(1)}, bf16[2,128,256]{2,1,0:T(8,128)(2,1)S(1)}, u32[]{:S(2)}, u32[]{:S(2)}) collective-permute-start(bf16[2,128,256]{2,1,0:T(8,128)(2,1)S(1)} %get-tuple-element.96), channel_id=1, source_target_pairs={{0,5},{1,4},{2,7},{3,6},{4,1},{5,0},{6,3},{7,2},{8,13},{9,12},{10,... | collective-permute-start | bytes 393224 | tf_op jit(solution)/shard_map/ppermute | solution.py:305
  109.2 14.3 %collective-permute-start.34 = (bf16[2,128,256]{2,1,0:T(8,128)(2,1)S(1)}, bf16[2,128,256]{2,1,0:T(8,128)(2,1)S(1)}, u32[]{:S(2)}, u32[]{:S(2)}) collective-permute-start(bf16[2,128,256]{2,1,0:T(8,128)(2,1)S(1)} %get-tuple-element.97), channel_id=1, source_target_pairs={{0,6},{1,7},{2,4},{3,5},{4,2},{5,3},{6,0},{7,1},{8,14},{9,15},{10,... | collective-permute-start | bytes 393224 | tf_op jit(solution)/shard_map/ppermute | solution.py:305
  113.8 9.7 %collective-permute-start.35 = (bf16[2,128,256]{2,1,0:T(8,128)(2,1)S(1)}, bf16[2,128,256]{2,1,0:T(8,128)(2,1)S(1)}, u32[]{:S(2)}, u32[]{:S(2)}) collective-permute-start(bf16[2,128,256]{2,1,0:T(8,128)(2,1)S(1)} %get-tuple-element.98), channel_id=1, source_target_pairs={{0,7},{1,6},{2,5},{3,4},{4,3},{5,2},{6,1},{7,0},{8,15},{9,14},{10,... | collective-permute-start | bytes 393224 | tf_op jit(solution)/shard_map/ppermute | solution.py:305
  114.3 1.4 %copy-start.8 = (bf16[512,1536]{1,0:T(8,128)(2,1)S(1)}, bf16[512,1536]{1,0:T(8,128)(2,1)}, u32[]{:S(2)}) copy-start(bf16[512,1536]{1,0:T(8,128)(2,1)} %get-tuple-element.82.whole.refs_3_) | copy-start | bytes 4718596

commit v22 on v14

--- a/solution.py
+++ b/solution.py
@@ -114,13 +114,17 @@
             k += 1
 
 
-def ladder_pair(matrix, whole, inner, total):
+def half_transform(matrix, whole, inner):
     virtual = matrix.shape[0]
     for single in range(whole.shape[1] // virtual):
         at = slice(single * virtual, (single + 1) * virtual)
         inner[at, :] = lax.dot_general(
             matrix, whole[:, at], (((1,), (1,)), ((), ())), preferred_element_type=WIDE
         ).astype(NARROW)
+
+
+def ladder_pair(matrix, whole, inner, total):
+    half_transform(matrix, whole, inner)
     total[...] = jnp.dot(whole[...], inner[...], preferred_element_type=WIDE)
 
 
@@ -137,22 +141,19 @@
         pack_pair(tiles, total, out, pair)
 
 
-def second_ladder_kernel(tiles, first, place, occ, source, blocks, row, column, whole, out, inner, total, matrix):
+def second_ladder_kernel(tiles, first, place, occ, source, blocks, row, column, whole, out, inner, matrix):
     def put(a, b, tile):
         matrix[tiles.span(a), tiles.span(b)] = tile.astype(NARROW)
 
     unpack_pair(tiles, blocks, 0, put)
-    ladder_pair(matrix[...], whole, inner, total)
+    half_transform(matrix[...], whole, inner)
     base = occ[place[0] * first + pl.program_id(0)] + occ[place[1]]
-    strip = math.gcd(64, total.shape[0])
-
-    def finish(step, carry):
-        at = pl.ds(pl.multiple_of(step * strip, strip), strip)
+    half = matrix.shape[0] // 2
+    for start in (0, half):
+        at = slice(start, start + half)
+        total = jnp.dot(whole[at, :], inner[...], preferred_element_type=WIDE)
         own = base - row[at, :1] - column[...]
-        out[0, at, :] = source[0, at, :] + 2.0 * (matrix[at, :].astype(WIDE) + total[at, :] * inverse(own))
-        return carry
-
-    lax.fori_loop(0, total.shape[0] // strip, finish, 0)
+        out[0, at, :] = source[0, at, :] + 2.0 * (matrix[at, :].astype(WIDE) + total * inverse(own))
 
 
 def add_kernel(tiles, place, source, *refs):
@@ -205,11 +206,11 @@
 
     @pl.when(across)
     def _():
-        finish(tiles.mirror_across(x))
+        finish(tiles.mirror_across(x).astype(WIDE))
 
     @pl.when(jnp.logical_not(across))
     def _():
-        finish(tiles.mirror_within(x))
+        finish(tiles.mirror_within(x).astype(WIDE))
 
 
 def update_kernel(tiles, groups, first, chunk, place, fock, occ, sums, *refs):
@@ -231,7 +232,7 @@
                 update[u, s * first + w] = value
                 sent[column, u, here] = value.astype(NARROW)
 
-            with_mirror(tiles, place, other[s][w, u].astype(WIDE), finish)
+            with_mirror(tiles, place, other[s][w, u], finish)
         return carry
 
     lax.fori_loop(0, first * first, one, 0)
@@ -287,7 +288,7 @@
                 value = rest[u, s * first + w].astype(WIDE) + mirrored * inverse(base - sums[here])
                 out[column, u, there] = value.astype(NARROW)
 
-            with_mirror(tiles, place, other[s - 1][w, u].astype(WIDE), finish)
+            with_mirror(tiles, place, other[s - 1][w, u], finish)
         return carry
 
     lax.fori_loop(0, first * first, one, 0)
@@ -434,7 +435,7 @@
             all_pairs(virtual, 128), all_pairs(1, virtual), all_pairs(*whole.shape),
         ],
         out_specs=by_pair(virtual, virtual),
-        scratch_shapes=[inner, square, pltpu.VMEM((virtual, virtual), NARROW)],
+        scratch_shapes=[inner, pltpu.VMEM((virtual, virtual), NARROW)],
         compiler_params=PARAMS,
         cost_estimate=pl.CostEstimate(flops=ladder_flops, bytes_accessed=12 * count, transcendentals=0),
     )(place, occ_energy, current, back, jnp.broadcast_to(vir_energy[:, None], (virtual, 128)),

time: 127 us -> 125 us (0.984)
  Pallas kernels: 31.1 us -> 29.6 us
    pallas_call x1, Pallas kernels: 7.79 us -> 6.04 us  [local(): pl.pallas_call(functools.partial(second_ladder_kernel, tiles, first), gri...]
  transfers between devices with their start and end apart: 38 -> 38, of which waited for: 7 -> 8; matrix products, arithmetic and copies ran while one was open for 2% -> 2% of each run, Pallas kernels for 22% -> 21%
where the time goes in v22:
time: 125 us; the launch traced here: 124 us
  starting transfers between devices  65.7 us (53%)
  Pallas kernels  29.6 us (24%)
  waiting for transfers between devices  20.2 us (16%)
  local copies, waits for them, and re-layouts  6.95 us (6%)
  between operations  1.63 us (1%)
    ppermute x18, starting transfers between devices, across_first(): lax.ppermute(parts[s], 'occi', [(k, k ^ s) for k in range(groups)])  35.1 us
    pallas_call x9, Pallas kernels, call(): pl.pallas_call(body, out_shape=outs, in_specs=specs, out_specs=jax.tree.m...  19.6 us
    ppermute x14, starting transfers between devices, by_distance(): lax.ppermute(parts[k], 'occj', [(d, d ^ k) for d in range(devices)])  15.8 us
    all_to_all x2, starting transfers between devices, exchange(): lax.all_to_all(blocks, 'occj', split_axis=0, concat_axis=0, tiled=True)  10.1 us
    all_to_all x2, waiting for transfers between devices, exchange(): lax.all_to_all(blocks, 'occj', split_axis=0, concat_axis=0, tiled=True)  7.72 us
    ppermute x18, waiting for transfers between devices, across_first(): lax.ppermute(parts[s], 'occi', [(k, k ^ s) for k in range(groups)])  6.94 us
    pallas_call x1, Pallas kernels, local(): pl.pallas_call(functools.partial(second_ladder_kernel, tiles, first), gri...  6.04 us
    unnamed x28, local copies, waits for them, and re-layouts  5.43 us
  transfers between devices with their start and end apart: 38, of which 8 were waited for; matrix products, arithmetic and copies ran while one was open for 2% of the time, Pallas kernels for 21%

profile of v22, /device:TPU:0, one launch (start us, length us, event | category | flops | bytes accessed | tf_op | source)
XLA Modules:
  0.0 124.4 jit_solution(10435723555537299120)
XLA Ops:
  0.0 3.0 %collective-permute-start = (bf16[3,64,512]{2,1,0:T(8,128)(2,1)}, bf16[3,64,512]{2,1,0:T(8,128)(2,1)S(1)}, u32[]{:S(2)}, u32[]{:S(2)}) collective-permute-start(bf16[3,64,512]{2,1,0:T(8,128)(2,1)} %refs_0_.1), channel_id=1, source_target_pairs={{0,2},{1,3},{2,0},{3,1},{4,6},{5,7},{6,4},{7,5},{8,10},{9,11},{10,... | collective-permute-start | bytes 589832 | tf_op jit(solution)/shard_map/ppermute | solution.py:339
  3.0 1.5 %collective-permute-start.1 = (bf16[3,64,512]{2,1,0:T(8,128)(2,1)}, bf16[3,64,512]{2,1,0:T(8,128)(2,1)S(1)}, u32[]{:S(2)}, u32[]{:S(2)}) collective-permute-start(bf16[3,64,512]{2,1,0:T(8,128)(2,1)} %refs_0_.1), channel_id=1, source_target_pairs={{0,4},{1,5},{2,6},{3,7},{4,0},{5,1},{6,2},{7,3},{8,12},{9,13},{10,... | collective-permute-start | bytes 589832 | tf_op jit(solution)/shard_map/ppermute | solution.py:339
  4.6 1.6 %copy-done = f32[2,1,512,512]{3,2,1,0:T(8,128)S(1)} copy-done((f32[2,1,512,512]{3,2,1,0:T(8,128)S(1)}, f32[2,1,512,512]{3,2,1,0:T(8,128)}, u32[]{:S(2)}) %copy-start) | copy-done | bytes 2097176
  6.2 0.9 shard_map.73
  7.1 1.6 %collective-permute-start.10 = (bf16[2,128,256]{2,1,0:T(8,128)(2,1)S(1)}, bf16[2,128,256]{2,1,0:T(8,128)(2,1)S(1)}, u32[]{:S(2)}, u32[]{:S(2)}) collective-permute-start(bf16[2,128,256]{2,1,0:T(8,128)(2,1)S(1)} %get-tuple-element.62), channel_id=1, source_target_pairs={{0,7},{1,6},{2,5},{3,4},{4,3},{5,2},{6,1},{7,0},{8,15},{9,14},{10,... | collective-permute-start | bytes 393224 | tf_op jit(solution)/shard_map/ppermute | solution.py:306
  8.7 1.5 %collective-permute-start.4 = (bf16[2,128,256]{2,1,0:T(8,128)(2,1)S(1)}, bf16[2,128,256]{2,1,0:T(8,128)(2,1)S(1)}, u32[]{:S(2)}, u32[]{:S(2)}) collective-permute-start(bf16[2,128,256]{2,1,0:T(8,128)(2,1)S(1)} %get-tuple-element.56), channel_id=1, source_target_pairs={{0,1},{1,0},{2,3},{3,2},{4,5},{5,4},{6,7},{7,6},{8,9},{9,8},{10,11... | collective-permute-start | bytes 393224 | tf_op jit(solution)/shard_map/ppermute | solution.py:306
  10.2 0.6 dynamic_slice.14
  11.4 0.6 dynamic_slice.12
  12.7 0.6 collective-permute-start.5
  13.3 2.5 %collective-permute-done.1.refs_2_ = bf16[3,64,512]{2,1,0:T(8,128)(2,1)S(1)} collective-permute-done((bf16[3,64,512]{2,1,0:T(8,128)(2,1)}, bf16[3,64,512]{2,1,0:T(8,128)(2,1)S(1)}, u32[]{:S(2)}, u32[]{:S(2)}) %collective-permute-start.1) | collective-permute-done | bytes 196640 | tf_op jit(solution)/shard_map/ppermute | solution.py:339
  15.8 0.1 pad_maximum_fusion
  16.0 0.1 fusion
  16.2 0.1 broadcast_add_fusion.2
  16.3 2.4 %collective-permute-start.7 = (bf16[2,128,256]{2,1,0:T(8,128)(2,1)S(1)}, bf16[2,128,256]{2,1,0:T(8,128)(2,1)S(1)}, u32[]{:S(2)}, u32[]{:S(2)}) collective-permute-start(bf16[2,128,256]{2,1,0:T(8,128)(2,1)S(1)} %get-tuple-element.59), channel_id=1, source_target_pairs={{0,4},{1,5},{2,6},{3,7},{4,0},{5,1},{6,2},{7,3},{8,12},{9,13},{10,... | collective-permute-start | bytes 393224 | tf_op jit(solution)/shard_map/ppermute | solution.py:306
  18.8 0.2 collective-permute-start.8
  18.9 2.9 %collective-permute-start.9 = (bf16[2,128,256]{2,1,0:T(8,128)(2,1)S(1)}, bf16[2,128,256]{2,1,0:T(8,128)(2,1)S(1)}, u32[]{:S(2)}, u32[]{:S(2)}) collective-permute-start(bf16[2,128,256]{2,1,0:T(8,128)(2,1)S(1)} %get-tuple-element.61), channel_id=1, source_target_pairs={{0,6},{1,7},{2,4},{3,5},{4,2},{5,3},{6,0},{7,1},{8,14},{9,15},{10,... | collective-permute-start | bytes 393224 | tf_op jit(solution)/shard_map/ppermute | solution.py:306
  21.8 6.3 %shard_map.74 = (bf16[8,2,128,256]{3,2,1,0:T(8,128)(2,1)}, bf16[512,1536]{1,0:T(8,128)(2,1)}) custom-call(s32[2]{0:T(128)S(1)} %pad_add_fusion.place.source, f32[2,512,512]{2,1,0:T(8,128)} %bitcast.13, bf16[3,64,512]{2,1,0:T(8,128)(2,1)S(1)} %copy-done.1, bf16[3,64,512]{2,1,0:T(8,128)(2,1)S(1)} %collective-permute-done.refs_1_, ...), custom_call_target="tpu_custom_call" | custom-call | flops 3221225472 | bytes 4194304 | tf_op jit(solution)/shard_map/pallas_call | solution.py:42
  28.1 0.2 collective-permute-done.8.refs_5_
  28.3 0.7 shard_map.75
  29.0 1.6 %collective-permute-start.11 = (bf16[2,2,64,256]{3,2,1,0:T(8,128)(2,1)S(1)}, bf16[2,2,64,256]{3,2,1,0:T(8,128)(2,1)S(1)}, u32[]{:S(2)}, u32[]{:S(2)}) collective-permute-start(bf16[2,2,64,256]{3,2,1,0:T(8,128)(2,1)S(1)} %get-tuple-element.64), channel_id=1, source_target_pairs={{0,8},{8,0},{16,24},{24,16},{1,9},{9,1},{17,25},{25,17},{2,10},{10... | collective-permute-start | bytes 393224 | tf_op jit(solution)/shard_map/ppermute | solution.py:313
  30.6 2.6 %collective-permute-start.12 = (bf16[2,2,64,256]{3,2,1,0:T(8,128)(2,1)S(1)}, bf16[2,2,64,256]{3,2,1,0:T(8,128)(2,1)S(1)}, u32[]{:S(2)}, u32[]{:S(2)}) collective-permute-start(bf16[2,2,64,256]{3,2,1,0:T(8,128)(2,1)S(1)} %get-tuple-element.65), channel_id=1, source_target_pairs={{0,16},{8,24},{16,0},{24,8},{1,17},{9,25},{17,1},{25,9},{2,18},{10... | collective-permute-start | bytes 393224 | tf_op jit(solution)/shard_map/ppermute | solution.py:313
  33.2 0.2 collective-permute-start.13
  33.6 3.6 %all-to-all-start = ((bf16[8,2,128,256]{3,2,1,0:T(8,128)(2,1)}), bf16[8,2,128,256]{3,2,1,0:T(8,128)(2,1)S(1)}, u32[]{:S(2)}, u32[]{:S(2)}) async-start(bf16[8,2,128,256]{3,2,1,0:T(8,128)(2,1)} %get-tuple-element.54), calls=%async_computation | async-start | bytes 2097152 | tf_op jit(solution)/shard_map/all_to_all | solution.py:300
  37.2 0.7 collective-permute-start.17
  37.9 3.5 %collective-permute-start.18 = (bf16[2,2,64,256]{3,2,1,0:T(8,128)(2,1)S(1)}, bf16[2,2,64,256]{3,2,1,0:T(8,128)(2,1)S(1)}, u32[]{:S(2)}, u32[]{:S(2)}) collective-permute-start(bf16[2,2,64,256]{3,2,1,0:T(8,128)(2,1)S(1)} %get-tuple-element.75), channel_id=1, source_target_pairs={{0,16},{8,24},{16,0},{24,8},{1,17},{9,25},{17,1},{25,9},{2,18},{10... | collective-permute-start | bytes 393224 | tf_op jit(solution)/shard_map/ppermute | solution.py:313
  41.4 0.2 collective-permute-start.19
  41.6 2.0 %collective-permute-done.12.refs_2_ = bf16[2,2,64,256]{3,2,1,0:T(8,128)(2,1)S(1)} collective-permute-done((bf16[2,2,64,256]{3,2,1,0:T(8,128)(2,1)S(1)}, bf16[2,2,64,256]{3,2,1,0:T(8,128)(2,1)S(1)}, u32[]{:S(2)}, u32[]{:S(2)}) %collective-permute-start.12) | collective-permute-done | bytes 131104 | tf_op jit(solution)/shard_map/ppermute | solution.py:313
  43.6 1.2 shard_map.76.place
  44.8 7.7 %all-to-all-done.ladder = bf16[8,2,128,256]{3,2,1,0:T(8,128)(2,1)S(1)} async-done(((bf16[8,2,128,256]{3,2,1,0:T(8,128)(2,1)}), bf16[8,2,128,256]{3,2,1,0:T(8,128)(2,1)S(1)}, u32[]{:S(2)}, u32[]{:S(2)}) %all-to-all-start) | async-done | bytes 1048608 | tf_op jit(solution)/shard_map/all_to_all | solution.py:300
  52.5 0.6 copy-done.10
  53.1 1.6 %shard_map.77 = (bf16[2,2,64,256]{3,2,1,0:T(8,128)(2,1)S(1)}, bf16[2,2,64,256]{3,2,1,0:T(8,128)(2,1)S(1)}, bf16[2,2,64,256]{3,2,1,0:T(8,128)(2,1)S(1)}, bf16[2,2,64,256]{3,2,1,0:T(8,128)(2,1)S(1)}) custom-call(s32[2]{0:T(128)S(1)} %copy-done.10, f32[8,8]{1,0:T(8,128)S(1)} %convert_element_type.3.fock, bf16[8,2,128,256]{3,2,1,0:T(8,128)(2,1)S(1)} %all-to-all-done.ladder, ...), custom_call_target="tpu_custom_call" | custom-call | flops 30000001024 | bytes 3145728 | tf_op jit(solution)/shard_map/pallas_call | solution.py:42
  54.6 1.3 %collective-permute-start.14 = (bf16[2,2,64,256]{3,2,1,0:T(8,128)(2,1)S(1)}, bf16[2,2,64,256]{3,2,1,0:T(8,128)(2,1)S(1)}, u32[]{:S(2)}, u32[]{:S(2)}) collective-permute-start(bf16[2,2,64,256]{3,2,1,0:T(8,128)(2,1)S(1)} %get-tuple-element.69.refs_1_), channel_id=1, source_target_pairs={{0,8},{8,0},{16,24},{24,16},{1,9},{9,1},{17,25},{25,17},{2,10},{10... | collective-permute-start | bytes 393224 | tf_op jit(solution)/shard_map/ppermute | solution.py:313
  56.0 2.9 %collective-permute-start.15 = (bf16[2,2,64,256]{3,2,1,0:T(8,128)(2,1)S(1)}, bf16[2,2,64,256]{3,2,1,0:T(8,128)(2,1)S(1)}, u32[]{:S(2)}, u32[]{:S(2)}) collective-permute-start(bf16[2,2,64,256]{3,2,1,0:T(8,128)(2,1)S(1)} %get-tuple-element.70.refs_2_), channel_id=1, source_target_pairs={{0,16},{8,24},{16,0},{24,8},{1,17},{9,25},{17,1},{25,9},{2,18},{10... | collective-permute-start | bytes 393224 | tf_op jit(solution)/shard_map/ppermute | solution.py:313
  58.9 0.2 collective-permute-start.16
  59.1 1.6 %shard_map.79 = (bf16[2,2,64,256]{3,2,1,0:T(8,128)(2,1)S(1)}, bf16[2,2,64,256]{3,2,1,0:T(8,128)(2,1)S(1)}, bf16[2,2,64,256]{3,2,1,0:T(8,128)(2,1)S(1)}, bf16[2,2,64,256]{3,2,1,0:T(8,128)(2,1)S(1)}) custom-call(s32[2]{0:T(128)S(1)} %copy-done.5, f32[8,8]{1,0:T(8,128)S(1)} %convert_element_type.3.fock, bf16[8,2,128,256]{3,2,1,0:T(8,128)(2,1)S(1)} %all-to-all-done.ladder, ...), custom_call_target="tpu_custom_call" | custom-call | flops 30000001024 | bytes 3145728 | tf_op jit(solution)/shard_map/pallas_call | solution.py:42
  60.7 0.4 collective-permute-start.20
  61.2 3.8 %collective-permute-start.21 = (bf16[2,2,64,256]{3,2,1,0:T(8,128)(2,1)S(1)}, bf16[2,2,64,256]{3,2,1,0:T(8,128)(2,1)S(1)}, u32[]{:S(2)}, u32[]{:S(2)}) collective-permute-start(bf16[2,2,64,256]{3,2,1,0:T(8,128)(2,1)S(1)} %get-tuple-element.79.refs_3_), channel_id=1, source_target_pairs={{0,16},{8,24},{16,0},{24,8},{1,17},{9,25},{17,1},{25,9},{2,18},{10... | collective-permute-start | bytes 393224 | tf_op jit(solution)/shard_map/ppermute | solution.py:313
  65.0 3.0 %collective-permute-start.22 = (bf16[2,2,64,256]{3,2,1,0:T(8,128)(2,1)S(1)}, bf16[2,2,64,256]{3,2,1,0:T(8,128)(2,1)S(1)}, u32[]{:S(2)}, u32[]{:S(2)}) collective-permute-start(bf16[2,2,64,256]{3,2,1,0:T(8,128)(2,1)S(1)} %get-tuple-element.80.refs_4_), channel_id=1, source_target_pairs={{0,24},{8,16},{16,8},{24,0},{1,25},{9,17},{17,9},{25,1},{2,26},{10... | collective-permute-start | bytes 393224 | tf_op jit(solution)/shard_map/ppermute | solution.py:313
  68.0 0.9 collective-permute-done.15.refs_6_
  68.9 2.6 %shard_map.78 = (bf16[8,2,64,256]{3,2,1,0:T(8,128)(2,1)S(1)}, bf16[2,8,64,256]{3,2,1,0:T(8,128)(2,1)S(1)}, bf16[2,2,64,256]{3,2,1,0:T(8,128)(2,1)S(1)}, bf16[2,2...) custom-call(s32[2]{0:T(128)S(1)} %copy-done.5, f32[8,8]{1,0:T(8,128)S(1)} %convert_element_type.3.fock, ...), custom_call_target="tpu_custom_call" | custom-call | flops 30000001024 | bytes 5242880 | tf_op jit(solution)/shard_map/pallas_call | solution.py:42
  71.5 0.8 copy-done.8
  72.3 7.2 %collective-permute-start.26 = (bf16[2,2,64,256]{3,2,1,0:T(8,128)(2,1)S(1)}, bf16[2,2,64,256]{3,2,1,0:T(8,128)(2,1)S(1)}, u32[]{:S(2)}, u32[]{:S(2)}) collective-permute-start(bf16[2,2,64,256]{3,2,1,0:T(8,128)(2,1)S(1)} %get-tuple-element.88), channel_id=1, source_target_pairs={{0,8},{8,0},{16,24},{24,16},{1,9},{9,1},{17,25},{25,17},{2,10},{10... | collective-permute-start | bytes 393224 | tf_op jit(solution)/shard_map/ppermute | solution.py:313
  79.5 0.8 collective-permute-start.27
  80.2 1.6 %collective-permute-start.28 = (bf16[2,2,64,256]{3,2,1,0:T(8,128)(2,1)S(1)}, bf16[2,2,64,256]{3,2,1,0:T(8,128)(2,1)S(1)}, u32[]{:S(2)}, u32[]{:S(2)}) collective-permute-start(bf16[2,2,64,256]{3,2,1,0:T(8,128)(2,1)S(1)} %get-tuple-element.90), channel_id=1, source_target_pairs={{0,24},{8,16},{16,8},{24,0},{1,25},{9,17},{17,9},{25,1},{2,26},{10... | collective-permute-start | bytes 393224 | tf_op jit(solution)/shard_map/ppermute | solution.py:313
  81.8 3.7 %shard_map.80 = (bf16[8,2,128,256]{3,2,1,0:T(8,128)(2,1)}, bf16[2,8,64,256]{3,2,1,0:T(8,128)(2,1)S(1)}, bf16[2,2,64,256]{3,2,1,0:T(8,128)(2,1)S(1)}, bf16[2,2,64...) custom-call(s32[2]{0:T(128)S(1)} %copy-done.5, f32[8,8]{1,0:T(8,128)S(1)} %convert_element_type.3.fock, ...), custom_call_target="tpu_custom_call" | custom-call | flops 30000001024 | bytes 5242880 | tf_op jit(solution)/shard_map/pallas_call | solution.py:42
  85.5 2.6 %collective-permute-start.23 = (bf16[2,2,64,256]{3,2,1,0:T(8,128)(2,1)S(1)}, bf16[2,2,64,256]{3,2,1,0:T(8,128)(2,1)S(1)}, u32[]{:S(2)}, u32[]{:S(2)}) collective-permute-start(bf16[2,2,64,256]{3,2,1,0:T(8,128)(2,1)S(1)} %get-tuple-element.84), channel_id=1, source_target_pairs={{0,8},{8,0},{16,24},{24,16},{1,9},{9,1},{17,25},{25,17},{2,10},{10... | collective-permute-start | bytes 393224 | tf_op jit(solution)/shard_map/ppermute | solution.py:313
  88.2 0.8 collective-permute-start.24
  88.9 6.6 %all-to-all-start.1 = ((bf16[8,2,128,256]{3,2,1,0:T(8,128)(2,1)}), bf16[8,2,128,256]{3,2,1,0:T(8,128)(2,1)S(1)}, u32[]{:S(2)}, u32[]{:S(2)}) async-start(bf16[8,2,128,256]{3,2,1,0:T(8,128)(2,1)} %get-tuple-element.81), calls=%async_computation.1 | async-start | bytes 2097152 | tf_op jit(solution)/shard_map/all_to_all | solution.py:300
  95.5 1.5 %collective-permute-start.25 = (bf16[2,2,64,256]{3,2,1,0:T(8,128)(2,1)S(1)}, bf16[2,2,64,256]{3,2,1,0:T(8,128)(2,1)S(1)}, u32[]{:S(2)}, u32[]{:S(2)}) collective-permute-start(bf16[2,2,64,256]{3,2,1,0:T(8,128)(2,1)S(1)} %get-tuple-element.86), channel_id=1, source_target_pairs={{0,24},{8,16},{16,8},{24,0},{1,25},{9,17},{17,9},{25,1},{2,26},{10... | collective-permute-start | bytes 393224 | tf_op jit(solution)/shard_map/ppermute | solution.py:313
  97.0 1.0 copy-done.9
  98.1 1.1 shard_map.82.refs_3_
  99.2 4.1 %collective-permute-done.25.refs_2_ = bf16[2,2,64,256]{3,2,1,0:T(8,128)(2,1)S(1)} collective-permute-done((bf16[2,2,64,256]{3,2,1,0:T(8,128)(2,1)S(1)}, bf16[2,2,64,256]{3,2,1,0:T(8,128)(2,1)S(1)}, u32[]{:S(2)}, u32[]{:S(2)}) %collective-permute-start.25) | collective-permute-done | bytes 131104 | tf_op jit(solution)/shard_map/ppermute | solution.py:313
  103.3 1.2 shard_map.83
  104.6 1.7 %collective-permute-start.30 = (bf16[2,128,256]{2,1,0:T(8,128)(2,1)S(1)}, bf16[2,128,256]{2,1,0:T(8,128)(2,1)S(1)}, u32[]{:S(2)}, u32[]{:S(2)}) collective-permute-start(bf16[2,128,256]{2,1,0:T(8,128)(2,1)S(1)} %get-tuple-element.93), channel_id=1, source_target_pairs={{0,2},{1,3},{2,0},{3,1},{4,6},{5,7},{6,4},{7,5},{8,10},{9,11},{10,... | collective-permute-start | bytes 393224 | tf_op jit(solution)/shard_map/ppermute | solution.py:306
  106.3 0.1 collective-permute-start.31
  106.5 1.8 %collective-permute-start.32 = (bf16[2,128,256]{2,1,0:T(8,128)(2,1)S(1)}, bf16[2,128,256]{2,1,0:T(8,128)(2,1)S(1)}, u32[]{:S(2)}, u32[]{:S(2)}) collective-permute-start(bf16[2,128,256]{2,1,0:T(8,128)(2,1)S(1)} %get-tuple-element.95), channel_id=1, source_target_pairs={{0,4},{1,5},{2,6},{3,7},{4,0},{5,1},{6,2},{7,3},{8,12},{9,13},{10,... | collective-permute-start | bytes 393224 | tf_op jit(solution)/shard_map/ppermute | solution.py:306
  108.3 2.9 %collective-permute-start.34 = (bf16[2,128,256]{2,1,0:T(8,128)(2,1)S(1)}, bf16[2,128,256]{2,1,0:T(8,128)(2,1)S(1)}, u32[]{:S(2)}, u32[]{:S(2)}) collective-permute-start(bf16[2,128,256]{2,1,0:T(8,128)(2,1)S(1)} %get-tuple-element.97), channel_id=1, source_target_pairs={{0,6},{1,7},{2,4},{3,5},{4,2},{5,3},{6,0},{7,1},{8,14},{9,15},{10,... | collective-permute-start | bytes 393224 | tf_op jit(solution)/shard_map/ppermute | solution.py:306
  111.2 2.3 %collective-permute-done.30.refs_2_ = bf16[2,128,256]{2,1,0:T(8,128)(2,1)S(1)} collective-permute-done((bf16[2,128,256]{2,1,0:T(8,128)(2,1)S(1)}, bf16[2,128,256]{2,1,0:T(8,128)(2,1)S(1)}, u32[]{:S(2)}, u32[]{:S(2)}) %collective-permute-start.30) | collective-permute-done | bytes 131104 | tf_op jit(solution)/shard_map/ppermute | solution.py:306
  113.5 0.1 collective-permute-start.35
  113.6 0.1 broadcast_in_dim.4.row
  113.7 1.4 %copy-done.7 = bf16[512,1536]{1,0:T(8,128)(2,1)S(1)} copy-done((bf16[512,1536]{1,0:T(8,128)(2,1)S(1)}, bf16[512,1536]{1,0:T(8,128)(2,1)}, u32[]{:S(2)}) %copy-start.7) | copy-done | bytes 1572888
  115.1 6.0 %shard_map.81.source = f32[2,512,512]{2,1,0:T(8,128)} custom-call(s32[2]{0:T(128)S(1)} %copy-done.5, f32[8]{0:T(128)S(1)} %copy-done.6, f32[2,512,512]{2,1,0:T(8,128)} %bitcast.14, bf16[8,2,128,256]{3,2,1,0:T(8,128)(2,1)S(1)} %all-to-all-done.1.blocks, f32[512,128]{1,0:T(8,128)S(1)} %broadcast_in_dim.4.row, f32[1,512]{1,0:T(1,128)S(1)} %bitcast.20, ...), custom_call_target="tpu_custom_call" | custom-call | flops 3221225472 | bytes 6291456 | tf_op jit(solution)/shard_map/pallas_call | solution.py:428
  121.2 0.5 collective-permute-done.35.refs_7_
  121.7 2.8 %shard_map.84 = f32[2,512,512]{2,1,0:T(8,128)} custom-call(s32[2]{0:T(128)S(1)} %copy-done.5, f32[2,512,512]{2,1,0:T(8,128)} %shard_map.81.source, bf16[2,128,256]{2,1,0:T(8,128)(2,1)S(1)} %get-tuple-element.91.refs_0_, bf16[2,128,256]{2,1,0:T(8,128)(2,1)S(1)} %collective-permute-done.29.refs_1_, ...), custom_call_target="tpu_custom_call", output_to_operand_aliasing={{}: (1, {})} | custom-call | flops 524288 | bytes 5242880 | tf_op jit(solution)/shard_map/pallas_call | solution.py:451
  (64 shorter events, 0.6 us)
Async XLA Ops:
  0.0 10.2 %copy-start.13 = (s32[8]{0:T(128)S(1)}, s32[8]{0:T(128)}, u32[]{:S(2)}) copy-start(s32[8]{0:T(128)} %constant.25.clone) | copy-start | bytes 100
  0.0 11.4 %copy-start.12 = (s32[8]{0:T(128)S(1)}, s32[8]{0:T(128)}, u32[]{:S(2)}) copy-start(s32[8]{0:T(128)} %constant.24.clone) | copy-start | bytes 100
  0.0 16.0 %copy-start.2 = (f32[512]{0:T(512)S(1)}, f32[512]{0:T(512)}, u32[]{:S(2)}) copy-start(f32[512]{0:T(512)} %param.11) | copy-start | bytes 6148
  0.0 12.7 %collective-permute-start = (bf16[3,64,512]{2,1,0:T(8,128)(2,1)}, bf16[3,64,512]{2,1,0:T(8,128)(2,1)S(1)}, u32[]{:S(2)}, u32[]{:S(2)}) collective-permute-start(bf16[3,64,512]{2,1,0:T(8,128)(2,1)} %refs_0_.1), channel_id=1, source_target_pairs={{0,2},{1,3},{2,0},{3,1},{4,6},{5,7},{6,4},{7,5},{8,10},{9,11},{10,... | collective-permute-start | bytes 589832 | tf_op jit(solution)/shard_map/ppermute | solution.py:339
  3.0 12.8 %collective-permute-start.1 = (bf16[3,64,512]{2,1,0:T(8,128)(2,1)}, bf16[3,64,512]{2,1,0:T(8,128)(2,1)S(1)}, u32[]{:S(2)}, u32[]{:S(2)}) collective-permute-start(bf16[3,64,512]{2,1,0:T(8,128)(2,1)} %refs_0_.1), channel_id=1, source_target_pairs={{0,4},{1,5},{2,6},{3,7},{4,0},{5,1},{6,2},{7,3},{8,12},{9,13},{10,... | collective-permute-start | bytes 589832 | tf_op jit(solution)/shard_map/ppermute | solution.py:339
  4.5 11.2 %collective-permute-start.2 = (bf16[3,64,512]{2,1,0:T(8,128)(2,1)}, bf16[3,64,512]{2,1,0:T(8,128)(2,1)S(1)}, u32[]{:S(2)}, u32[]{:S(2)}) collective-permute-start(bf16[3,64,512]{2,1,0:T(8,128)(2,1)} %refs_0_.1), channel_id=1, source_target_pairs={{0,6},{1,7},{2,4},{3,5},{4,2},{5,3},{6,0},{7,1},{8,14},{9,15},{10,... | collective-permute-start | bytes 589832 | tf_op jit(solution)/shard_map/ppermute | solution.py:339
  4.6 23.7 %copy-start.4 = (s32[2]{0:T(128)}, s32[2]{0:T(128)S(1)}, u32[]{:S(2)}) copy-start(s32[2]{0:T(128)S(1)} %pad_add_fusion.place.source) | copy-start | bytes 28
  4.6 1.6 %copy-start = (f32[2,1,512,512]{3,2,1,0:T(8,128)S(1)}, f32[2,1,512,512]{3,2,1,0:T(8,128)}, u32[]{:S(2)}) copy-start(f32[2,1,512,512]{3,2,1,0:T(8,128)} %param.7) | copy-start | bytes 6291460
  6.2 9.6 %copy-start.1 = (bf16[3,64,512]{2,1,0:T(8,128)(2,1)S(1)}, bf16[3,64,512]{2,1,0:T(8,128)(2,1)}, u32[]{:S(2)}) copy-start(bf16[3,64,512]{2,1,0:T(8,128)(2,1)} %refs_0_.1) | copy-start | bytes 589828
  7.1 9.2 %collective-permute-start.10 = (bf16[2,128,256]{2,1,0:T(8,128)(2,1)S(1)}, bf16[2,128,256]{2,1,0:T(8,128)(2,1)S(1)}, u32[]{:S(2)}, u32[]{:S(2)}) collective-permute-start(bf16[2,128,256]{2,1,0:T(8,128)(2,1)S(1)} %get-tuple-element.62), channel_id=1, source_target_pairs={{0,7},{1,6},{2,5},{3,4},{4,3},{5,2},{6,1},{7,0},{8,15},{9,14},{10,... | collective-permute-start | bytes 393224 | tf_op jit(solution)/shard_map/ppermute | solution.py:306
  8.7 10.1 %collective-permute-start.4 = (bf16[2,128,256]{2,1,0:T(8,128)(2,1)S(1)}, bf16[2,128,256]{2,1,0:T(8,128)(2,1)S(1)}, u32[]{:S(2)}, u32[]{:S(2)}) collective-permute-start(bf16[2,128,256]{2,1,0:T(8,128)(2,1)S(1)} %get-tuple-element.56), channel_id=1, source_target_pairs={{0,1},{1,0},{2,3},{3,2},{4,5},{5,4},{6,7},{7,6},{8,9},{9,8},{10,11... | collective-permute-start | bytes 393224 | tf_op jit(solution)/shard_map/ppermute | solution.py:306
  12.7 15.4 %collective-permute-start.5 = (bf16[2,128,256]{2,1,0:T(8,128)(2,1)S(1)}, bf16[2,128,256]{2,1,0:T(8,128)(2,1)S(1)}, u32[]{:S(2)}, u32[]{:S(2)}) collective-permute-start(bf16[2,128,256]{2,1,0:T(8,128)(2,1)S(1)} %get-tuple-element.57), channel_id=1, source_target_pairs={{0,2},{1,3},{2,0},{3,1},{4,6},{5,7},{6,4},{7,5},{8,10},{9,11},{10,... | collective-permute-start | bytes 393224 | tf_op jit(solution)/shard_map/ppermute | solution.py:306
  15.8 12.3 %collective-permute-start.6 = (bf16[2,128,256]{2,1,0:T(8,128)(2,1)S(1)}, bf16[2,128,256]{2,1,0:T(8,128)(2,1)S(1)}, u32[]{:S(2)}, u32[]{:S(2)}) collective-permute-start(bf16[2,128,256]{2,1,0:T(8,128)(2,1)S(1)} %get-tuple-element.58), channel_id=1, source_target_pairs={{0,3},{1,2},{2,1},{3,0},{4,7},{5,6},{6,5},{7,4},{8,11},{9,10},{10,... | collective-permute-start | bytes 393224 | tf_op jit(solution)/shard_map/ppermute | solution.py:306
  15.9 3.0 %collective-permute-start.3 = (bf16[4,3,64,512]{3,2,1,0:T(8,128)(2,1)S(1)}, bf16[4,3,64,512]{3,2,1,0:T(8,128)(2,1)S(1)}, u32[]{:S(2)}, u32[]{:S(2)}) collective-permute-start(bf16[4,3,64,512]{3,2,1,0:T(8,128)(2,1)S(1)} %pad_maximum_fusion), channel_id=1, source_target_pairs={{0,1},{1,0},{2,3},{3,2},{4,5},{5,4},{6,7},{7,6},{8,9},{9,8},{10,11... | collective-permute-start | bytes 2359304 | tf_op jit(solution)/shard_map/ppermute | solution.py:339
  16.3 11.7 %collective-permute-start.7 = (bf16[2,128,256]{2,1,0:T(8,128)(2,1)S(1)}, bf16[2,128,256]{2,1,0:T(8,128)(2,1)S(1)}, u32[]{:S(2)}, u32[]{:S(2)}) collective-permute-start(bf16[2,128,256]{2,1,0:T(8,128)(2,1)S(1)} %get-tuple-element.59), channel_id=1, source_target_pairs={{0,4},{1,5},{2,6},{3,7},{4,0},{5,1},{6,2},{7,3},{8,12},{9,13},{10,... | collective-permute-start | bytes 393224 | tf_op jit(solution)/shard_map/ppermute | solution.py:306
  18.8 9.6 %collective-permute-start.8 = (bf16[2,128,256]{2,1,0:T(8,128)(2,1)S(1)}, bf16[2,128,256]{2,1,0:T(8,128)(2,1)S(1)}, u32[]{:S(2)}, u32[]{:S(2)}) collective-permute-start(bf16[2,128,256]{2,1,0:T(8,128)(2,1)S(1)} %get-tuple-element.60), channel_id=1, source_target_pairs={{0,5},{1,4},{2,7},{3,6},{4,1},{5,0},{6,3},{7,2},{8,13},{9,12},{10,... | collective-permute-start | bytes 393224 | tf_op jit(solution)/shard_map/ppermute | solution.py:306
  18.9 14.6 %copy-start.11 = (bf16[8,8]{1,0:T(8,128)(2,1)S(1)}, bf16[8,8]{1,0:T(8,128)(2,1)}, u32[]{:S(2)}) copy-start(bf16[8,8]{1,0:T(8,128)(2,1)} %param.9) | copy-start | bytes 388
  18.9 9.4 %collective-permute-start.9 = (bf16[2,128,256]{2,1,0:T(8,128)(2,1)S(1)}, bf16[2,128,256]{2,1,0:T(8,128)(2,1)S(1)}, u32[]{:S(2)}, u32[]{:S(2)}) collective-permute-start(bf16[2,128,256]{2,1,0:T(8,128)(2,1)S(1)} %get-tuple-element.61), channel_id=1, source_target_pairs={{0,6},{1,7},{2,4},{3,5},{4,2},{5,3},{6,0},{7,1},{8,14},{9,15},{10,... | collective-permute-start | bytes 393224 | tf_op jit(solution)/shard_map/ppermute | solution.py:306
  29.0 12.4 %collective-permute-start.11 = (bf16[2,2,64,256]{3,2,1,0:T(8,128)(2,1)S(1)}, bf16[2,2,64,256]{3,2,1,0:T(8,128)(2,1)S(1)}, u32[]{:S(2)}, u32[]{:S(2)}) collective-permute-start(bf16[2,2,64,256]{3,2,1,0:T(8,128)(2,1)S(1)} %get-tuple-element.64), channel_id=1, source_target_pairs={{0,8},{8,0},{16,24},{24,16},{1,9},{9,1},{17,25},{25,17},{2,10},{10... | collective-permute-start | bytes 393224 | tf_op jit(solution)/shard_map/ppermute | solution.py:313
  30.6 12.9 %collective-permute-start.12 = (bf16[2,2,64,256]{3,2,1,0:T(8,128)(2,1)S(1)}, bf16[2,2,64,256]{3,2,1,0:T(8,128)(2,1)S(1)}, u32[]{:S(2)}, u32[]{:S(2)}) collective-permute-start(bf16[2,2,64,256]{3,2,1,0:T(8,128)(2,1)S(1)} %get-tuple-element.65), channel_id=1, source_target_pairs={{0,16},{8,24},{16,0},{24,8},{1,17},{9,25},{17,1},{25,9},{2,18},{10... | collective-permute-start | bytes 393224 | tf_op jit(solution)/shard_map/ppermute | solution.py:313
  33.2 10.3 %collective-permute-start.13 = (bf16[2,2,64,256]{3,2,1,0:T(8,128)(2,1)S(1)}, bf16[2,2,64,256]{3,2,1,0:T(8,128)(2,1)S(1)}, u32[]{:S(2)}, u32[]{:S(2)}) collective-permute-start(bf16[2,2,64,256]{3,2,1,0:T(8,128)(2,1)S(1)} %get-tuple-element.66), channel_id=1, source_target_pairs={{0,24},{8,16},{16,8},{24,0},{1,25},{9,17},{17,9},{25,1},{2,26},{10... | collective-permute-start | bytes 393224 | tf_op jit(solution)/shard_map/ppermute | solution.py:313
  33.6 18.9 %all-to-all-start = ((bf16[8,2,128,256]{3,2,1,0:T(8,128)(2,1)}), bf16[8,2,128,256]{3,2,1,0:T(8,128)(2,1)S(1)}, u32[]{:S(2)}, u32[]{:S(2)}) async-start(bf16[8,2,128,256]{3,2,1,0:T(8,128)(2,1)} %get-tuple-element.54), calls=%async_computation | async-start | bytes 2097152 | tf_op jit(solution)/shard_map/all_to_all | solution.py:300
  37.2 21.7 %collective-permute-start.17 = (bf16[2,2,64,256]{3,2,1,0:T(8,128)(2,1)S(1)}, bf16[2,2,64,256]{3,2,1,0:T(8,128)(2,1)S(1)}, u32[]{:S(2)}, u32[]{:S(2)}) collective-permute-start(bf16[2,2,64,256]{3,2,1,0:T(8,128)(2,1)S(1)} %get-tuple-element.74), channel_id=1, source_target_pairs={{0,8},{8,0},{16,24},{24,16},{1,9},{9,1},{17,25},{25,17},{2,10},{10... | collective-permute-start | bytes 393224 | tf_op jit(solution)/shard_map/ppermute | solution.py:313
  37.9 21.2 %collective-permute-start.18 = (bf16[2,2,64,256]{3,2,1,0:T(8,128)(2,1)S(1)}, bf16[2,2,64,256]{3,2,1,0:T(8,128)(2,1)S(1)}, u32[]{:S(2)}, u32[]{:S(2)}) collective-permute-start(bf16[2,2,64,256]{3,2,1,0:T(8,128)(2,1)S(1)} %get-tuple-element.75), channel_id=1, source_target_pairs={{0,16},{8,24},{16,0},{24,8},{1,17},{9,25},{17,1},{25,9},{2,18},{10... | collective-permute-start | bytes 393224 | tf_op jit(solution)/shard_map/ppermute | solution.py:313
  41.4 17.7 %collective-permute-start.19 = (bf16[2,2,64,256]{3,2,1,0:T(8,128)(2,1)S(1)}, bf16[2,2,64,256]{3,2,1,0:T(8,128)(2,1)S(1)}, u32[]{:S(2)}, u32[]{:S(2)}) collective-permute-start(bf16[2,2,64,256]{3,2,1,0:T(8,128)(2,1)S(1)} %get-tuple-element.76), channel_id=1, source_target_pairs={{0,24},{8,16},{16,8},{24,0},{1,25},{9,17},{17,9},{25,1},{2,26},{10... | collective-permute-start | bytes 393224 | tf_op jit(solution)/shard_map/ppermute | solution.py:313
  44.8 14.3 %copy-start.5 = (s32[2]{0:T(128)S(1)}, s32[2]{0:T(128)}, u32[]{:S(2)}) copy-start(s32[2]{0:T(128)} %copy-done.4) | copy-start | bytes 28
  52.5 0.6 copy-start.10
  54.6 10.3 %collective-permute-start.14 = (bf16[2,2,64,256]{3,2,1,0:T(8,128)(2,1)S(1)}, bf16[2,2,64,256]{3,2,1,0:T(8,128)(2,1)S(1)}, u32[]{:S(2)}, u32[]{:S(2)}) collective-permute-start(bf16[2,2,64,256]{3,2,1,0:T(8,128)(2,1)S(1)} %get-tuple-element.69.refs_1_), channel_id=1, source_target_pairs={{0,8},{8,0},{16,24},{24,16},{1,9},{9,1},{17,25},{25,17},{2,10},{10... | collective-permute-start | bytes 393224 | tf_op jit(solution)/shard_map/ppermute | solution.py:313
  56.0 12.9 %collective-permute-start.15 = (bf16[2,2,64,256]{3,2,1,0:T(8,128)(2,1)S(1)}, bf16[2,2,64,256]{3,2,1,0:T(8,128)(2,1)S(1)}, u32[]{:S(2)}, u32[]{:S(2)}) collective-permute-start(bf16[2,2,64,256]{3,2,1,0:T(8,128)(2,1)S(1)} %get-tuple-element.70.refs_2_), channel_id=1, source_target_pairs={{0,16},{8,24},{16,0},{24,8},{1,17},{9,25},{17,1},{25,9},{2,18},{10... | collective-permute-start | bytes 393224 | tf_op jit(solution)/shard_map/ppermute | solution.py:313
  58.9 10.0 %collective-permute-start.16 = (bf16[2,2,64,256]{3,2,1,0:T(8,128)(2,1)S(1)}, bf16[2,2,64,256]{3,2,1,0:T(8,128)(2,1)S(1)}, u32[]{:S(2)}, u32[]{:S(2)}) collective-permute-start(bf16[2,2,64,256]{3,2,1,0:T(8,128)(2,1)S(1)} %get-tuple-element.71.refs_3_), channel_id=1, source_target_pairs={{0,24},{8,16},{16,8},{24,0},{1,25},{9,17},{17,9},{25,1},{2,26},{10... | collective-permute-start | bytes 393224 | tf_op jit(solution)/shard_map/ppermute | solution.py:313
  59.1 9.8 %copy-start.6 = (f32[8]{0:T(128)S(1)}, f32[8]{0:T(128)}, u32[]{:S(2)}) copy-start(f32[8]{0:T(128)} %occ.9) | copy-start | bytes 100
  60.7 19.5 %collective-permute-start.20 = (bf16[2,2,64,256]{3,2,1,0:T(8,128)(2,1)S(1)}, bf16[2,2,64,256]{3,2,1,0:T(8,128)(2,1)S(1)}, u32[]{:S(2)}, u32[]{:S(2)}) collective-permute-start(bf16[2,2,64,256]{3,2,1,0:T(8,128)(2,1)S(1)} %get-tuple-element.78.refs_2_), channel_id=1, source_target_pairs={{0,8},{8,0},{16,24},{24,16},{1,9},{9,1},{17,25},{25,17},{2,10},{10... | collective-permute-start | bytes 393224 | tf_op jit(solution)/shard_map/ppermute | solution.py:313
  61.2 20.7 %collective-permute-start.21 = (bf16[2,2,64,256]{3,2,1,0:T(8,128)(2,1)S(1)}, bf16[2,2,64,256]{3,2,1,0:T(8,128)(2,1)S(1)}, u32[]{:S(2)}, u32[]{:S(2)}) collective-permute-start(bf16[2,2,64,256]{3,2,1,0:T(8,128)(2,1)S(1)} %get-tuple-element.79.refs_3_), channel_id=1, source_target_pairs={{0,16},{8,24},{16,0},{24,8},{1,17},{9,25},{17,1},{25,9},{2,18},{10... | collective-permute-start | bytes 393224 | tf_op jit(solution)/shard_map/ppermute | solution.py:313
  65.0 16.9 %collective-permute-start.22 = (bf16[2,2,64,256]{3,2,1,0:T(8,128)(2,1)S(1)}, bf16[2,2,64,256]{3,2,1,0:T(8,128)(2,1)S(1)}, u32[]{:S(2)}, u32[]{:S(2)}) collective-permute-start(bf16[2,2,64,256]{3,2,1,0:T(8,128)(2,1)S(1)} %get-tuple-element.80.refs_4_), channel_id=1, source_target_pairs={{0,24},{8,16},{16,8},{24,0},{1,25},{9,17},{17,9},{25,1},{2,26},{10... | collective-permute-start | bytes 393224 | tf_op jit(solution)/shard_map/ppermute | solution.py:313
  71.5 0.8 copy-start.8
  72.3 23.2 %collective-permute-start.26 = (bf16[2,2,64,256]{3,2,1,0:T(8,128)(2,1)S(1)}, bf16[2,2,64,256]{3,2,1,0:T(8,128)(2,1)S(1)}, u32[]{:S(2)}, u32[]{:S(2)}) collective-permute-start(bf16[2,2,64,256]{3,2,1,0:T(8,128)(2,1)S(1)} %get-tuple-element.88), channel_id=1, source_target_pairs={{0,8},{8,0},{16,24},{24,16},{1,9},{9,1},{17,25},{25,17},{2,10},{10... | collective-permute-start | bytes 393224 | tf_op jit(solution)/shard_map/ppermute | solution.py:313
  79.5 17.6 %collective-permute-start.27 = (bf16[2,2,64,256]{3,2,1,0:T(8,128)(2,1)S(1)}, bf16[2,2,64,256]{3,2,1,0:T(8,128)(2,1)S(1)}, u32[]{:S(2)}, u32[]{:S(2)}) collective-permute-start(bf16[2,2,64,256]{3,2,1,0:T(8,128)(2,1)S(1)} %get-tuple-element.89), channel_id=1, source_target_pairs={{0,16},{8,24},{16,0},{24,8},{1,17},{9,25},{17,1},{25,9},{2,18},{10... | collective-permute-start | bytes 393224 | tf_op jit(solution)/shard_map/ppermute | solution.py:313
  80.2 16.8 %collective-permute-start.28 = (bf16[2,2,64,256]{3,2,1,0:T(8,128)(2,1)S(1)}, bf16[2,2,64,256]{3,2,1,0:T(8,128)(2,1)S(1)}, u32[]{:S(2)}, u32[]{:S(2)}) collective-permute-start(bf16[2,2,64,256]{3,2,1,0:T(8,128)(2,1)S(1)} %get-tuple-element.90), channel_id=1, source_target_pairs={{0,24},{8,16},{16,8},{24,0},{1,25},{9,17},{17,9},{25,1},{2,26},{10... | collective-permute-start | bytes 393224 | tf_op jit(solution)/shard_map/ppermute | solution.py:313
  85.5 13.7 %collective-permute-start.23 = (bf16[2,2,64,256]{3,2,1,0:T(8,128)(2,1)S(1)}, bf16[2,2,64,256]{3,2,1,0:T(8,128)(2,1)S(1)}, u32[]{:S(2)}, u32[]{:S(2)}) collective-permute-start(bf16[2,2,64,256]{3,2,1,0:T(8,128)(2,1)S(1)} %get-tuple-element.84), channel_id=1, source_target_pairs={{0,8},{8,0},{16,24},{24,16},{1,9},{9,1},{17,25},{25,17},{2,10},{10... | collective-permute-start | bytes 393224 | tf_op jit(solution)/shard_map/ppermute | solution.py:313
  88.2 11.1 %collective-permute-start.24 = (bf16[2,2,64,256]{3,2,1,0:T(8,128)(2,1)S(1)}, bf16[2,2,64,256]{3,2,1,0:T(8,128)(2,1)S(1)}, u32[]{:S(2)}, u32[]{:S(2)}) collective-permute-start(bf16[2,2,64,256]{3,2,1,0:T(8,128)(2,1)S(1)} %get-tuple-element.85), channel_id=1, source_target_pairs={{0,16},{8,24},{16,0},{24,8},{1,17},{9,25},{17,1},{25,9},{2,18},{10... | collective-permute-start | bytes 393224 | tf_op jit(solution)/shard_map/ppermute | solution.py:313
  88.9 24.6 %all-to-all-start.1 = ((bf16[8,2,128,256]{3,2,1,0:T(8,128)(2,1)}), bf16[8,2,128,256]{3,2,1,0:T(8,128)(2,1)S(1)}, u32[]{:S(2)}, u32[]{:S(2)}) async-start(bf16[8,2,128,256]{3,2,1,0:T(8,128)(2,1)} %get-tuple-element.81), calls=%async_computation.1 | async-start | bytes 2097152 | tf_op jit(solution)/shard_map/all_to_all | solution.py:300
  95.5 7.8 %collective-permute-start.25 = (bf16[2,2,64,256]{3,2,1,0:T(8,128)(2,1)S(1)}, bf16[2,2,64,256]{3,2,1,0:T(8,128)(2,1)S(1)}, u32[]{:S(2)}, u32[]{:S(2)}) collective-permute-start(bf16[2,2,64,256]{3,2,1,0:T(8,128)(2,1)S(1)} %get-tuple-element.86), channel_id=1, source_target_pairs={{0,24},{8,16},{16,8},{24,0},{1,25},{9,17},{17,9},{25,1},{2,26},{10... | collective-permute-start | bytes 393224 | tf_op jit(solution)/shard_map/ppermute | solution.py:313
  97.0 1.0 copy-start.9
  103.3 10.3 %copy-start.3 = (f32[512]{0:T(512)S(1)}, f32[512]{0:T(512)}, u32[]{:S(2)}) copy-start(f32[512]{0:T(512)} %param.11) | copy-start | bytes 6148
  104.5 3.8 %collective-permute-start.29 = (bf16[2,128,256]{2,1,0:T(8,128)(2,1)S(1)}, bf16[2,128,256]{2,1,0:T(8,128)(2,1)S(1)}, u32[]{:S(2)}, u32[]{:S(2)}) collective-permute-start(bf16[2,128,256]{2,1,0:T(8,128)(2,1)S(1)} %get-tuple-element.92), channel_id=1, source_target_pairs={{0,1},{1,0},{2,3},{3,2},{4,5},{5,4},{6,7},{7,6},{8,9},{9,8},{10,11... | collective-permute-start | bytes 393224 | tf_op jit(solution)/shard_map/ppermute | solution.py:306
  104.6 8.9 %collective-permute-start.30 = (bf16[2,128,256]{2,1,0:T(8,128)(2,1)S(1)}, bf16[2,128,256]{2,1,0:T(8,128)(2,1)S(1)}, u32[]{:S(2)}, u32[]{:S(2)}) collective-permute-start(bf16[2,128,256]{2,1,0:T(8,128)(2,1)S(1)} %get-tuple-element.93), channel_id=1, source_target_pairs={{0,2},{1,3},{2,0},{3,1},{4,6},{5,7},{6,4},{7,5},{8,10},{9,11},{10,... | collective-permute-start | bytes 393224 | tf_op jit(solution)/shard_map/ppermute | solution.py:306
  106.3 14.8 %collective-permute-start.31 = (bf16[2,128,256]{2,1,0:T(8,128)(2,1)S(1)}, bf16[2,128,256]{2,1,0:T(8,128)(2,1)S(1)}, u32[]{:S(2)}, u32[]{:S(2)}) collective-permute-start(bf16[2,128,256]{2,1,0:T(8,128)(2,1)S(1)} %get-tuple-element.94), channel_id=1, source_target_pairs={{0,3},{1,2},{2,1},{3,0},{4,7},{5,6},{6,5},{7,4},{8,11},{9,10},{10,... | collective-permute-start | bytes 393224 | tf_op jit(solution)/shard_map/ppermute | solution.py:306
  106.5 14.7 %collective-permute-start.32 = (bf16[2,128,256]{2,1,0:T(8,128)(2,1)S(1)}, bf16[2,128,256]{2,1,0:T(8,128)(2,1)S(1)}, u32[]{:S(2)}, u32[]{:S(2)}) collective-permute-start(bf16[2,128,256]{2,1,0:T(8,128)(2,1)S(1)} %get-tuple-element.95), channel_id=1, source_target_pairs={{0,4},{1,5},{2,6},{3,7},{4,0},{5,1},{6,2},{7,3},{8,12},{9,13},{10,... | collective-permute-start | bytes 393224 | tf_op jit(solution)/shard_map/ppermute | solution.py:306
  108.3 12.9 %collective-permute-start.33 = (bf16[2,128,256]{2,1,0:T(8,128)(2,1)S(1)}, bf16[2,128,256]{2,1,0:T(8,128)(2,1)S(1)}, u32[]{:S(2)}, u32[]{:S(2)}) collective-permute-start(bf16[2,128,256]{2,1,0:T(8,128)(2,1)S(1)} %get-tuple-element.96), channel_id=1, source_target_pairs={{0,5},{1,4},{2,7},{3,6},{4,1},{5,0},{6,3},{7,2},{8,13},{9,12},{10,... | collective-permute-start | bytes 393224 | tf_op jit(solution)/shard_map/ppermute | solution.py:306
  108.3 12.9 %collective-permute-start.34 = (bf16[2,128,256]{2,1,0:T(8,128)(2,1)S(1)}, bf16[2,128,256]{2,1,0:T(8,128)(2,1)S(1)}, u32[]{:S(2)}, u32[]{:S(2)}) collective-permute-start(bf16[2,128,256]{2,1,0:T(8,128)(2,1)S(1)} %get-tuple-element.97), channel_id=1, source_target_pairs={{0,6},{1,7},{2,4},{3,5},{4,2},{5,3},{6,0},{7,1},{8,14},{9,15},{10,... | collective-permute-start | bytes 393224 | tf_op jit(solution)/shard_map/ppermute | solution.py:306
  113.5 8.2 %collective-permute-start.35 = (bf16[2,128,256]{2,1,0:T(8,128)(2,1)S(1)}, bf16[2,128,256]{2,1,0:T(8,128)(2,1)S(1)}, u32[]{:S(2)}, u32[]{:S(2)}) collective-permute-start(bf16[2,128,256]{2,1,0:T(8,128)(2,1)S(1)} %get-tuple-element.98), channel_id=1, source_target_pairs={{0,7},{1,6},{2,5},{3,4},{4,3},{5,2},{6,1},{7,0},{8,15},{9,14},{10,... | collective-permute-start | bytes 393224 | tf_op jit(solution)/shard_map/ppermute | solution.py:306
  113.7 1.4 %copy-start.7 = (bf16[512,1536]{1,0:T(8,128)(2,1)S(1)}, bf16[512,1536]{1,0:T(8,128)(2,1)}, u32[]{:S(2)}) copy-start(bf16[512,1536]{1,0:T(8,128)(2,1)} %get-tuple-element.82.whole) | copy-start | bytes 4718596

commit v23 on v22

--- a/solution.py
+++ b/solution.py
@@ -55,10 +55,10 @@
     straight, turned = (slice(e, None), slice(0, e)) if mirrored else (slice(0, e), slice(e, None))
     for d, (a, b) in enumerate(tiles.above):
         out[d, pair, :, straight] = source[tiles.span(a), tiles.span(b)].astype(NARROW)
-        out[d, pair, :, turned] = source[tiles.span(b), tiles.span(a)].astype(WIDE).T.astype(NARROW)
+        out[d, pair, :, turned] = source[tiles.span(b), tiles.span(a)].astype(NARROW).T
     for d, c, k in tiles.diagonal:
         tile = source[tiles.span(k), tiles.span(k)]
-        tile = tile.astype(WIDE).T.astype(NARROW) if mirrored else tile.astype(NARROW)
+        tile = tile.astype(NARROW).T if mirrored else tile.astype(NARROW)
         out[d, pair, c * g:(c + 1) * g, :e] = tile[:g]
         out[d, pair, c * g:(c + 1) * g, e:] = tile[g:]
 
@@ -67,7 +67,7 @@
     e, g = tiles.edge, tiles.rows
     for d, (a, b) in enumerate(tiles.above):
         put(a, b, blocks[d, pair, :, :e].astype(WIDE))
-        put(b, a, blocks[d, pair, :, e:].astype(WIDE).T)
+        put(b, a, blocks[d, pair, :, e:].T.astype(WIDE))
     for d, c, k in tiles.diagonal:
         upper = blocks[d, pair, c * g:(c + 1) * g, :e]
         lower = blocks[d, pair, c * g:(c + 1) * g, e:]

time: 125 us -> 125 us (level)
  no operation moved by 1% of the time
where the time goes in v23:
time: 125 us; the launch traced here: 124 us
  starting transfers between devices  65.7 us (53%)
  Pallas kernels  29.5 us (24%)
  waiting for transfers between devices  20.2 us (16%)
  local copies, waits for them, and re-layouts  6.95 us (6%)
  between operations  1.63 us (1%)
    ppermute x18, starting transfers between devices, across_first(): lax.ppermute(parts[s], 'occi', [(k, k ^ s) for k in range(groups)])  35.1 us
    pallas_call x9, Pallas kernels, call(): pl.pallas_call(body, out_shape=outs, in_specs=specs, out_specs=jax.tree.m...  19.6 us
    ppermute x14, starting transfers between devices, by_distance(): lax.ppermute(parts[k], 'occj', [(d, d ^ k) for d in range(devices)])  15.8 us
    all_to_all x2, starting transfers between devices, exchange(): lax.all_to_all(blocks, 'occj', split_axis=0, concat_axis=0, tiled=True)  10.2 us
    all_to_all x2, waiting for transfers between devices, exchange(): lax.all_to_all(blocks, 'occj', split_axis=0, concat_axis=0, tiled=True)  7.72 us
    ppermute x18, waiting for transfers between devices, across_first(): lax.ppermute(parts[s], 'occi', [(k, k ^ s) for k in range(groups)])  6.92 us
    pallas_call x1, Pallas kernels, local(): pl.pallas_call(functools.partial(second_ladder_kernel, tiles, first), gri...  6.03 us
    unnamed x28, local copies, waits for them, and re-layouts  5.43 us
  transfers between devices with their start and end apart: 38, of which 8 were waited for; matrix products, arithmetic and copies ran while one was open for 2% of the time, Pallas kernels for 21%

profile of v23, /device:TPU:0, one launch (start us, length us, event | category | flops | bytes accessed | tf_op | source)
XLA Modules:
  0.0 124.4 jit_solution(13605996424874409409)
XLA Ops:
  0.0 3.0 %collective-permute-start = (bf16[3,64,512]{2,1,0:T(8,128)(2,1)}, bf16[3,64,512]{2,1,0:T(8,128)(2,1)S(1)}, u32[]{:S(2)}, u32[]{:S(2)}) collective-permute-start(bf16[3,64,512]{2,1,0:T(8,128)(2,1)} %refs_0_.1), channel_id=1, source_target_pairs={{0,2},{1,3},{2,0},{3,1},{4,6},{5,7},{6,4},{7,5},{8,10},{9,11},{10,... | collective-permute-start | bytes 589832 | tf_op jit(solution)/shard_map/ppermute | solution.py:339
  3.0 1.5 %collective-permute-start.1 = (bf16[3,64,512]{2,1,0:T(8,128)(2,1)}, bf16[3,64,512]{2,1,0:T(8,128)(2,1)S(1)}, u32[]{:S(2)}, u32[]{:S(2)}) collective-permute-start(bf16[3,64,512]{2,1,0:T(8,128)(2,1)} %refs_0_.1), channel_id=1, source_target_pairs={{0,4},{1,5},{2,6},{3,7},{4,0},{5,1},{6,2},{7,3},{8,12},{9,13},{10,... | collective-permute-start | bytes 589832 | tf_op jit(solution)/shard_map/ppermute | solution.py:339
  4.6 1.6 %copy-done = f32[2,1,512,512]{3,2,1,0:T(8,128)S(1)} copy-done((f32[2,1,512,512]{3,2,1,0:T(8,128)S(1)}, f32[2,1,512,512]{3,2,1,0:T(8,128)}, u32[]{:S(2)}) %copy-start) | copy-done | bytes 2097176
  6.2 0.9 shard_map.73
  7.1 1.6 %collective-permute-start.10 = (bf16[2,128,256]{2,1,0:T(8,128)(2,1)S(1)}, bf16[2,128,256]{2,1,0:T(8,128)(2,1)S(1)}, u32[]{:S(2)}, u32[]{:S(2)}) collective-permute-start(bf16[2,128,256]{2,1,0:T(8,128)(2,1)S(1)} %get-tuple-element.62), channel_id=1, source_target_pairs={{0,7},{1,6},{2,5},{3,4},{4,3},{5,2},{6,1},{7,0},{8,15},{9,14},{10,... | collective-permute-start | bytes 393224 | tf_op jit(solution)/shard_map/ppermute | solution.py:306
  8.7 1.5 %collective-permute-start.4 = (bf16[2,128,256]{2,1,0:T(8,128)(2,1)S(1)}, bf16[2,128,256]{2,1,0:T(8,128)(2,1)S(1)}, u32[]{:S(2)}, u32[]{:S(2)}) collective-permute-start(bf16[2,128,256]{2,1,0:T(8,128)(2,1)S(1)} %get-tuple-element.56), channel_id=1, source_target_pairs={{0,1},{1,0},{2,3},{3,2},{4,5},{5,4},{6,7},{7,6},{8,9},{9,8},{10,11... | collective-permute-start | bytes 393224 | tf_op jit(solution)/shard_map/ppermute | solution.py:306
  10.2 0.6 dynamic_slice.14
  11.4 0.6 dynamic_slice.12
  12.7 0.6 collective-permute-start.5
  13.3 2.5 %collective-permute-done.1.refs_2_ = bf16[3,64,512]{2,1,0:T(8,128)(2,1)S(1)} collective-permute-done((bf16[3,64,512]{2,1,0:T(8,128)(2,1)}, bf16[3,64,512]{2,1,0:T(8,128)(2,1)S(1)}, u32[]{:S(2)}, u32[]{:S(2)}) %collective-permute-start.1) | collective-permute-done | bytes 196640 | tf_op jit(solution)/shard_map/ppermute | solution.py:339
  15.8 0.1 pad_maximum_fusion
  16.0 0.1 fusion
  16.2 0.1 broadcast_add_fusion.2
  16.3 2.4 %collective-permute-start.7 = (bf16[2,128,256]{2,1,0:T(8,128)(2,1)S(1)}, bf16[2,128,256]{2,1,0:T(8,128)(2,1)S(1)}, u32[]{:S(2)}, u32[]{:S(2)}) collective-permute-start(bf16[2,128,256]{2,1,0:T(8,128)(2,1)S(1)} %get-tuple-element.59), channel_id=1, source_target_pairs={{0,4},{1,5},{2,6},{3,7},{4,0},{5,1},{6,2},{7,3},{8,12},{9,13},{10,... | collective-permute-start | bytes 393224 | tf_op jit(solution)/shard_map/ppermute | solution.py:306
  18.8 0.2 collective-permute-start.8
  18.9 2.9 %collective-permute-start.9 = (bf16[2,128,256]{2,1,0:T(8,128)(2,1)S(1)}, bf16[2,128,256]{2,1,0:T(8,128)(2,1)S(1)}, u32[]{:S(2)}, u32[]{:S(2)}) collective-permute-start(bf16[2,128,256]{2,1,0:T(8,128)(2,1)S(1)} %get-tuple-element.61), channel_id=1, source_target_pairs={{0,6},{1,7},{2,4},{3,5},{4,2},{5,3},{6,0},{7,1},{8,14},{9,15},{10,... | collective-permute-start | bytes 393224 | tf_op jit(solution)/shard_map/ppermute | solution.py:306
  21.8 6.3 %shard_map.74 = (bf16[8,2,128,256]{3,2,1,0:T(8,128)(2,1)}, bf16[512,1536]{1,0:T(8,128)(2,1)}) custom-call(s32[2]{0:T(128)S(1)} %pad_add_fusion.place.source, f32[2,512,512]{2,1,0:T(8,128)} %bitcast.13, bf16[3,64,512]{2,1,0:T(8,128)(2,1)S(1)} %copy-done.1, bf16[3,64,512]{2,1,0:T(8,128)(2,1)S(1)} %collective-permute-done.refs_1_, ...), custom_call_target="tpu_custom_call" | custom-call | flops 3221225472 | bytes 4194304 | tf_op jit(solution)/shard_map/pallas_call | solution.py:42
  28.1 0.2 collective-permute-done.8.refs_5_
  28.3 0.7 shard_map.75
  29.0 1.6 %collective-permute-start.11 = (bf16[2,2,64,256]{3,2,1,0:T(8,128)(2,1)S(1)}, bf16[2,2,64,256]{3,2,1,0:T(8,128)(2,1)S(1)}, u32[]{:S(2)}, u32[]{:S(2)}) collective-permute-start(bf16[2,2,64,256]{3,2,1,0:T(8,128)(2,1)S(1)} %get-tuple-element.64), channel_id=1, source_target_pairs={{0,8},{8,0},{16,24},{24,16},{1,9},{9,1},{17,25},{25,17},{2,10},{10... | collective-permute-start | bytes 393224 | tf_op jit(solution)/shard_map/ppermute | solution.py:313
  30.6 2.6 %collective-permute-start.12 = (bf16[2,2,64,256]{3,2,1,0:T(8,128)(2,1)S(1)}, bf16[2,2,64,256]{3,2,1,0:T(8,128)(2,1)S(1)}, u32[]{:S(2)}, u32[]{:S(2)}) collective-permute-start(bf16[2,2,64,256]{3,2,1,0:T(8,128)(2,1)S(1)} %get-tuple-element.65), channel_id=1, source_target_pairs={{0,16},{8,24},{16,0},{24,8},{1,17},{9,25},{17,1},{25,9},{2,18},{10... | collective-permute-start | bytes 393224 | tf_op jit(solution)/shard_map/ppermute | solution.py:313
  33.2 0.2 collective-permute-start.13
  33.6 3.6 %all-to-all-start = ((bf16[8,2,128,256]{3,2,1,0:T(8,128)(2,1)}), bf16[8,2,128,256]{3,2,1,0:T(8,128)(2,1)S(1)}, u32[]{:S(2)}, u32[]{:S(2)}) async-start(bf16[8,2,128,256]{3,2,1,0:T(8,128)(2,1)} %get-tuple-element.54), calls=%async_computation | async-start | bytes 2097152 | tf_op jit(solution)/shard_map/all_to_all | solution.py:300
  37.2 0.7 collective-permute-start.17
  37.9 3.5 %collective-permute-start.18 = (bf16[2,2,64,256]{3,2,1,0:T(8,128)(2,1)S(1)}, bf16[2,2,64,256]{3,2,1,0:T(8,128)(2,1)S(1)}, u32[]{:S(2)}, u32[]{:S(2)}) collective-permute-start(bf16[2,2,64,256]{3,2,1,0:T(8,128)(2,1)S(1)} %get-tuple-element.75), channel_id=1, source_target_pairs={{0,16},{8,24},{16,0},{24,8},{1,17},{9,25},{17,1},{25,9},{2,18},{10... | collective-permute-start | bytes 393224 | tf_op jit(solution)/shard_map/ppermute | solution.py:313
  41.4 0.2 collective-permute-start.19
  41.6 2.0 %collective-permute-done.12.refs_2_ = bf16[2,2,64,256]{3,2,1,0:T(8,128)(2,1)S(1)} collective-permute-done((bf16[2,2,64,256]{3,2,1,0:T(8,128)(2,1)S(1)}, bf16[2,2,64,256]{3,2,1,0:T(8,128)(2,1)S(1)}, u32[]{:S(2)}, u32[]{:S(2)}) %collective-permute-start.12) | collective-permute-done | bytes 131104 | tf_op jit(solution)/shard_map/ppermute | solution.py:313
  43.6 1.2 shard_map.76.place
  44.8 7.7 %all-to-all-done.ladder = bf16[8,2,128,256]{3,2,1,0:T(8,128)(2,1)S(1)} async-done(((bf16[8,2,128,256]{3,2,1,0:T(8,128)(2,1)}), bf16[8,2,128,256]{3,2,1,0:T(8,128)(2,1)S(1)}, u32[]{:S(2)}, u32[]{:S(2)}) %all-to-all-start) | async-done | bytes 1048608 | tf_op jit(solution)/shard_map/all_to_all | solution.py:300
  52.5 0.6 copy-done.10
  53.1 1.6 %shard_map.77 = (bf16[2,2,64,256]{3,2,1,0:T(8,128)(2,1)S(1)}, bf16[2,2,64,256]{3,2,1,0:T(8,128)(2,1)S(1)}, bf16[2,2,64,256]{3,2,1,0:T(8,128)(2,1)S(1)}, bf16[2,2,64,256]{3,2,1,0:T(8,128)(2,1)S(1)}) custom-call(s32[2]{0:T(128)S(1)} %copy-done.10, f32[8,8]{1,0:T(8,128)S(1)} %convert_element_type.3.fock, bf16[8,2,128,256]{3,2,1,0:T(8,128)(2,1)S(1)} %all-to-all-done.ladder, ...), custom_call_target="tpu_custom_call" | custom-call | flops 30000001024 | bytes 3145728 | tf_op jit(solution)/shard_map/pallas_call | solution.py:42
  54.6 1.3 %collective-permute-start.14 = (bf16[2,2,64,256]{3,2,1,0:T(8,128)(2,1)S(1)}, bf16[2,2,64,256]{3,2,1,0:T(8,128)(2,1)S(1)}, u32[]{:S(2)}, u32[]{:S(2)}) collective-permute-start(bf16[2,2,64,256]{3,2,1,0:T(8,128)(2,1)S(1)} %get-tuple-element.69.refs_1_), channel_id=1, source_target_pairs={{0,8},{8,0},{16,24},{24,16},{1,9},{9,1},{17,25},{25,17},{2,10},{10... | collective-permute-start | bytes 393224 | tf_op jit(solution)/shard_map/ppermute | solution.py:313
  56.0 2.9 %collective-permute-start.15 = (bf16[2,2,64,256]{3,2,1,0:T(8,128)(2,1)S(1)}, bf16[2,2,64,256]{3,2,1,0:T(8,128)(2,1)S(1)}, u32[]{:S(2)}, u32[]{:S(2)}) collective-permute-start(bf16[2,2,64,256]{3,2,1,0:T(8,128)(2,1)S(1)} %get-tuple-element.70.refs_2_), channel_id=1, source_target_pairs={{0,16},{8,24},{16,0},{24,8},{1,17},{9,25},{17,1},{25,9},{2,18},{10... | collective-permute-start | bytes 393224 | tf_op jit(solution)/shard_map/ppermute | solution.py:313
  58.9 0.2 collective-permute-start.16
  59.1 1.6 %shard_map.79 = (bf16[2,2,64,256]{3,2,1,0:T(8,128)(2,1)S(1)}, bf16[2,2,64,256]{3,2,1,0:T(8,128)(2,1)S(1)}, bf16[2,2,64,256]{3,2,1,0:T(8,128)(2,1)S(1)}, bf16[2,2,64,256]{3,2,1,0:T(8,128)(2,1)S(1)}) custom-call(s32[2]{0:T(128)S(1)} %copy-done.5, f32[8,8]{1,0:T(8,128)S(1)} %convert_element_type.3.fock, bf16[8,2,128,256]{3,2,1,0:T(8,128)(2,1)S(1)} %all-to-all-done.ladder, ...), custom_call_target="tpu_custom_call" | custom-call | flops 30000001024 | bytes 3145728 | tf_op jit(solution)/shard_map/pallas_call | solution.py:42
  60.7 0.5 collective-permute-start.20
  61.2 3.8 %collective-permute-start.21 = (bf16[2,2,64,256]{3,2,1,0:T(8,128)(2,1)S(1)}, bf16[2,2,64,256]{3,2,1,0:T(8,128)(2,1)S(1)}, u32[]{:S(2)}, u32[]{:S(2)}) collective-permute-start(bf16[2,2,64,256]{3,2,1,0:T(8,128)(2,1)S(1)} %get-tuple-element.79.refs_3_), channel_id=1, source_target_pairs={{0,16},{8,24},{16,0},{24,8},{1,17},{9,25},{17,1},{25,9},{2,18},{10... | collective-permute-start | bytes 393224 | tf_op jit(solution)/shard_map/ppermute | solution.py:313
  65.0 3.1 %collective-permute-start.22 = (bf16[2,2,64,256]{3,2,1,0:T(8,128)(2,1)S(1)}, bf16[2,2,64,256]{3,2,1,0:T(8,128)(2,1)S(1)}, u32[]{:S(2)}, u32[]{:S(2)}) collective-permute-start(bf16[2,2,64,256]{3,2,1,0:T(8,128)(2,1)S(1)} %get-tuple-element.80.refs_4_), channel_id=1, source_target_pairs={{0,24},{8,16},{16,8},{24,0},{1,25},{9,17},{17,9},{25,1},{2,26},{10... | collective-permute-start | bytes 393224 | tf_op jit(solution)/shard_map/ppermute | solution.py:313
  68.0 0.8 collective-permute-done.15.refs_6_
  68.9 2.6 %shard_map.78 = (bf16[8,2,64,256]{3,2,1,0:T(8,128)(2,1)S(1)}, bf16[2,8,64,256]{3,2,1,0:T(8,128)(2,1)S(1)}, bf16[2,2,64,256]{3,2,1,0:T(8,128)(2,1)S(1)}, bf16[2,2...) custom-call(s32[2]{0:T(128)S(1)} %copy-done.5, f32[8,8]{1,0:T(8,128)S(1)} %convert_element_type.3.fock, ...), custom_call_target="tpu_custom_call" | custom-call | flops 30000001024 | bytes 5242880 | tf_op jit(solution)/shard_map/pallas_call | solution.py:42
  71.5 0.8 copy-done.8
  72.3 7.2 %collective-permute-start.26 = (bf16[2,2,64,256]{3,2,1,0:T(8,128)(2,1)S(1)}, bf16[2,2,64,256]{3,2,1,0:T(8,128)(2,1)S(1)}, u32[]{:S(2)}, u32[]{:S(2)}) collective-permute-start(bf16[2,2,64,256]{3,2,1,0:T(8,128)(2,1)S(1)} %get-tuple-element.88), channel_id=1, source_target_pairs={{0,8},{8,0},{16,24},{24,16},{1,9},{9,1},{17,25},{25,17},{2,10},{10... | collective-permute-start | bytes 393224 | tf_op jit(solution)/shard_map/ppermute | solution.py:313
  79.5 0.7 collective-permute-start.27
  80.2 1.6 %collective-permute-start.28 = (bf16[2,2,64,256]{3,2,1,0:T(8,128)(2,1)S(1)}, bf16[2,2,64,256]{3,2,1,0:T(8,128)(2,1)S(1)}, u32[]{:S(2)}, u32[]{:S(2)}) collective-permute-start(bf16[2,2,64,256]{3,2,1,0:T(8,128)(2,1)S(1)} %get-tuple-element.90), channel_id=1, source_target_pairs={{0,24},{8,16},{16,8},{24,0},{1,25},{9,17},{17,9},{25,1},{2,26},{10... | collective-permute-start | bytes 393224 | tf_op jit(solution)/shard_map/ppermute | solution.py:313
  81.9 3.7 %shard_map.80 = (bf16[8,2,128,256]{3,2,1,0:T(8,128)(2,1)}, bf16[2,8,64,256]{3,2,1,0:T(8,128)(2,1)S(1)}, bf16[2,2,64,256]{3,2,1,0:T(8,128)(2,1)S(1)}, bf16[2,2,64...) custom-call(s32[2]{0:T(128)S(1)} %copy-done.5, f32[8,8]{1,0:T(8,128)S(1)} %convert_element_type.3.fock, ...), custom_call_target="tpu_custom_call" | custom-call | flops 30000001024 | bytes 5242880 | tf_op jit(solution)/shard_map/pallas_call | solution.py:42
  85.6 2.6 %collective-permute-start.23 = (bf16[2,2,64,256]{3,2,1,0:T(8,128)(2,1)S(1)}, bf16[2,2,64,256]{3,2,1,0:T(8,128)(2,1)S(1)}, u32[]{:S(2)}, u32[]{:S(2)}) collective-permute-start(bf16[2,2,64,256]{3,2,1,0:T(8,128)(2,1)S(1)} %get-tuple-element.84), channel_id=1, source_target_pairs={{0,8},{8,0},{16,24},{24,16},{1,9},{9,1},{17,25},{25,17},{2,10},{10... | collective-permute-start | bytes 393224 | tf_op jit(solution)/shard_map/ppermute | solution.py:313
  88.2 0.7 collective-permute-start.24
  88.9 6.6 %all-to-all-start.1 = ((bf16[8,2,128,256]{3,2,1,0:T(8,128)(2,1)}), bf16[8,2,128,256]{3,2,1,0:T(8,128)(2,1)S(1)}, u32[]{:S(2)}, u32[]{:S(2)}) async-start(bf16[8,2,128,256]{3,2,1,0:T(8,128)(2,1)} %get-tuple-element.81), calls=%async_computation.1 | async-start | bytes 2097152 | tf_op jit(solution)/shard_map/all_to_all | solution.py:300
  95.5 1.5 %collective-permute-start.25 = (bf16[2,2,64,256]{3,2,1,0:T(8,128)(2,1)S(1)}, bf16[2,2,64,256]{3,2,1,0:T(8,128)(2,1)S(1)}, u32[]{:S(2)}, u32[]{:S(2)}) collective-permute-start(bf16[2,2,64,256]{3,2,1,0:T(8,128)(2,1)S(1)} %get-tuple-element.86), channel_id=1, source_target_pairs={{0,24},{8,16},{16,8},{24,0},{1,25},{9,17},{17,9},{25,1},{2,26},{10... | collective-permute-start | bytes 393224 | tf_op jit(solution)/shard_map/ppermute | solution.py:313
  97.0 1.0 copy-done.9
  98.1 1.1 shard_map.82.refs_3_
  99.2 4.1 %collective-permute-done.25.refs_2_ = bf16[2,2,64,256]{3,2,1,0:T(8,128)(2,1)S(1)} collective-permute-done((bf16[2,2,64,256]{3,2,1,0:T(8,128)(2,1)S(1)}, bf16[2,2,64,256]{3,2,1,0:T(8,128)(2,1)S(1)}, u32[]{:S(2)}, u32[]{:S(2)}) %collective-permute-start.25) | collective-permute-done | bytes 131104 | tf_op jit(solution)/shard_map/ppermute | solution.py:313
  103.3 1.2 shard_map.83
  104.6 1.7 %collective-permute-start.30 = (bf16[2,128,256]{2,1,0:T(8,128)(2,1)S(1)}, bf16[2,128,256]{2,1,0:T(8,128)(2,1)S(1)}, u32[]{:S(2)}, u32[]{:S(2)}) collective-permute-start(bf16[2,128,256]{2,1,0:T(8,128)(2,1)S(1)} %get-tuple-element.93), channel_id=1, source_target_pairs={{0,2},{1,3},{2,0},{3,1},{4,6},{5,7},{6,4},{7,5},{8,10},{9,11},{10,... | collective-permute-start | bytes 393224 | tf_op jit(solution)/shard_map/ppermute | solution.py:306
  106.3 0.1 collective-permute-start.31
  106.5 1.8 %collective-permute-start.32 = (bf16[2,128,256]{2,1,0:T(8,128)(2,1)S(1)}, bf16[2,128,256]{2,1,0:T(8,128)(2,1)S(1)}, u32[]{:S(2)}, u32[]{:S(2)}) collective-permute-start(bf16[2,128,256]{2,1,0:T(8,128)(2,1)S(1)} %get-tuple-element.95), channel_id=1, source_target_pairs={{0,4},{1,5},{2,6},{3,7},{4,0},{5,1},{6,2},{7,3},{8,12},{9,13},{10,... | collective-permute-start | bytes 393224 | tf_op jit(solution)/shard_map/ppermute | solution.py:306
  108.3 2.9 %collective-permute-start.34 = (bf16[2,128,256]{2,1,0:T(8,128)(2,1)S(1)}, bf16[2,128,256]{2,1,0:T(8,128)(2,1)S(1)}, u32[]{:S(2)}, u32[]{:S(2)}) collective-permute-start(bf16[2,128,256]{2,1,0:T(8,128)(2,1)S(1)} %get-tuple-element.97), channel_id=1, source_target_pairs={{0,6},{1,7},{2,4},{3,5},{4,2},{5,3},{6,0},{7,1},{8,14},{9,15},{10,... | collective-permute-start | bytes 393224 | tf_op jit(solution)/shard_map/ppermute | solution.py:306
  111.2 2.3 %collective-permute-done.30.refs_2_ = bf16[2,128,256]{2,1,0:T(8,128)(2,1)S(1)} collective-permute-done((bf16[2,128,256]{2,1,0:T(8,128)(2,1)S(1)}, bf16[2,128,256]{2,1,0:T(8,128)(2,1)S(1)}, u32[]{:S(2)}, u32[]{:S(2)}) %collective-permute-start.30) | collective-permute-done | bytes 131104 | tf_op jit(solution)/shard_map/ppermute | solution.py:306
  113.5 0.1 collective-permute-start.35
  113.6 0.1 broadcast_in_dim.4.row
  113.7 1.4 %copy-done.7 = bf16[512,1536]{1,0:T(8,128)(2,1)S(1)} copy-done((bf16[512,1536]{1,0:T(8,128)(2,1)S(1)}, bf16[512,1536]{1,0:T(8,128)(2,1)}, u32[]{:S(2)}) %copy-start.7) | copy-done | bytes 1572888
  115.1 6.0 %shard_map.81.source = f32[2,512,512]{2,1,0:T(8,128)} custom-call(s32[2]{0:T(128)S(1)} %copy-done.5, f32[8]{0:T(128)S(1)} %copy-done.6, f32[2,512,512]{2,1,0:T(8,128)} %bitcast.14, bf16[8,2,128,256]{3,2,1,0:T(8,128)(2,1)S(1)} %all-to-all-done.1.blocks, f32[512,128]{1,0:T(8,128)S(1)} %broadcast_in_dim.4.row, f32[1,512]{1,0:T(1,128)S(1)} %bitcast.20, ...), custom_call_target="tpu_custom_call" | custom-call | flops 3221225472 | bytes 6291456 | tf_op jit(solution)/shard_map/pallas_call | solution.py:428
  121.2 0.5 collective-permute-done.35.refs_7_
  121.7 2.7 %shard_map.84 = f32[2,512,512]{2,1,0:T(8,128)} custom-call(s32[2]{0:T(128)S(1)} %copy-done.5, f32[2,512,512]{2,1,0:T(8,128)} %shard_map.81.source, bf16[2,128,256]{2,1,0:T(8,128)(2,1)S(1)} %get-tuple-element.91.refs_0_, bf16[2,128,256]{2,1,0:T(8,128)(2,1)S(1)} %collective-permute-done.29.refs_1_, ...), custom_call_target="tpu_custom_call", output_to_operand_aliasing={{}: (1, {})} | custom-call | flops 524288 | bytes 5242880 | tf_op jit(solution)/shard_map/pallas_call | solution.py:451
  (64 shorter events, 0.6 us)
Async XLA Ops:
  0.0 10.2 %copy-start.13 = (s32[8]{0:T(128)S(1)}, s32[8]{0:T(128)}, u32[]{:S(2)}) copy-start(s32[8]{0:T(128)} %constant.25.clone) | copy-start | bytes 100
  0.0 11.4 %copy-start.12 = (s32[8]{0:T(128)S(1)}, s32[8]{0:T(128)}, u32[]{:S(2)}) copy-start(s32[8]{0:T(128)} %constant.24.clone) | copy-start | bytes 100
  0.0 16.0 %copy-start.2 = (f32[512]{0:T(512)S(1)}, f32[512]{0:T(512)}, u32[]{:S(2)}) copy-start(f32[512]{0:T(512)} %param.11) | copy-start | bytes 6148
  0.0 12.7 %collective-permute-start = (bf16[3,64,512]{2,1,0:T(8,128)(2,1)}, bf16[3,64,512]{2,1,0:T(8,128)(2,1)S(1)}, u32[]{:S(2)}, u32[]{:S(2)}) collective-permute-start(bf16[3,64,512]{2,1,0:T(8,128)(2,1)} %refs_0_.1), channel_id=1, source_target_pairs={{0,2},{1,3},{2,0},{3,1},{4,6},{5,7},{6,4},{7,5},{8,10},{9,11},{10,... | collective-permute-start | bytes 589832 | tf_op jit(solution)/shard_map/ppermute | solution.py:339
  3.0 12.8 %collective-permute-start.1 = (bf16[3,64,512]{2,1,0:T(8,128)(2,1)}, bf16[3,64,512]{2,1,0:T(8,128)(2,1)S(1)}, u32[]{:S(2)}, u32[]{:S(2)}) collective-permute-start(bf16[3,64,512]{2,1,0:T(8,128)(2,1)} %refs_0_.1), channel_id=1, source_target_pairs={{0,4},{1,5},{2,6},{3,7},{4,0},{5,1},{6,2},{7,3},{8,12},{9,13},{10,... | collective-permute-start | bytes 589832 | tf_op jit(solution)/shard_map/ppermute | solution.py:339
  4.5 11.2 %collective-permute-start.2 = (bf16[3,64,512]{2,1,0:T(8,128)(2,1)}, bf16[3,64,512]{2,1,0:T(8,128)(2,1)S(1)}, u32[]{:S(2)}, u32[]{:S(2)}) collective-permute-start(bf16[3,64,512]{2,1,0:T(8,128)(2,1)} %refs_0_.1), channel_id=1, source_target_pairs={{0,6},{1,7},{2,4},{3,5},{4,2},{5,3},{6,0},{7,1},{8,14},{9,15},{10,... | collective-permute-start | bytes 589832 | tf_op jit(solution)/shard_map/ppermute | solution.py:339
  4.6 23.7 %copy-start.4 = (s32[2]{0:T(128)}, s32[2]{0:T(128)S(1)}, u32[]{:S(2)}) copy-start(s32[2]{0:T(128)S(1)} %pad_add_fusion.place.source) | copy-start | bytes 28
  4.6 1.6 %copy-start = (f32[2,1,512,512]{3,2,1,0:T(8,128)S(1)}, f32[2,1,512,512]{3,2,1,0:T(8,128)}, u32[]{:S(2)}) copy-start(f32[2,1,512,512]{3,2,1,0:T(8,128)} %param.7) | copy-start | bytes 6291460
  6.2 9.5 %copy-start.1 = (bf16[3,64,512]{2,1,0:T(8,128)(2,1)S(1)}, bf16[3,64,512]{2,1,0:T(8,128)(2,1)}, u32[]{:S(2)}) copy-start(bf16[3,64,512]{2,1,0:T(8,128)(2,1)} %refs_0_.1) | copy-start | bytes 589828
  7.1 9.2 %collective-permute-start.10 = (bf16[2,128,256]{2,1,0:T(8,128)(2,1)S(1)}, bf16[2,128,256]{2,1,0:T(8,128)(2,1)S(1)}, u32[]{:S(2)}, u32[]{:S(2)}) collective-permute-start(bf16[2,128,256]{2,1,0:T(8,128)(2,1)S(1)} %get-tuple-element.62), channel_id=1, source_target_pairs={{0,7},{1,6},{2,5},{3,4},{4,3},{5,2},{6,1},{7,0},{8,15},{9,14},{10,... | collective-permute-start | bytes 393224 | tf_op jit(solution)/shard_map/ppermute | solution.py:306
  8.7 10.1 %collective-permute-start.4 = (bf16[2,128,256]{2,1,0:T(8,128)(2,1)S(1)}, bf16[2,128,256]{2,1,0:T(8,128)(2,1)S(1)}, u32[]{:S(2)}, u32[]{:S(2)}) collective-permute-start(bf16[2,128,256]{2,1,0:T(8,128)(2,1)S(1)} %get-tuple-element.56), channel_id=1, source_target_pairs={{0,1},{1,0},{2,3},{3,2},{4,5},{5,4},{6,7},{7,6},{8,9},{9,8},{10,11... | collective-permute-start | bytes 393224 | tf_op jit(solution)/shard_map/ppermute | solution.py:306
  12.7 15.4 %collective-permute-start.5 = (bf16[2,128,256]{2,1,0:T(8,128)(2,1)S(1)}, bf16[2,128,256]{2,1,0:T(8,128)(2,1)S(1)}, u32[]{:S(2)}, u32[]{:S(2)}) collective-permute-start(bf16[2,128,256]{2,1,0:T(8,128)(2,1)S(1)} %get-tuple-element.57), channel_id=1, source_target_pairs={{0,2},{1,3},{2,0},{3,1},{4,6},{5,7},{6,4},{7,5},{8,10},{9,11},{10,... | collective-permute-start | bytes 393224 | tf_op jit(solution)/shard_map/ppermute | solution.py:306
  15.8 12.3 %collective-permute-start.6 = (bf16[2,128,256]{2,1,0:T(8,128)(2,1)S(1)}, bf16[2,128,256]{2,1,0:T(8,128)(2,1)S(1)}, u32[]{:S(2)}, u32[]{:S(2)}) collective-permute-start(bf16[2,128,256]{2,1,0:T(8,128)(2,1)S(1)} %get-tuple-element.58), channel_id=1, source_target_pairs={{0,3},{1,2},{2,1},{3,0},{4,7},{5,6},{6,5},{7,4},{8,11},{9,10},{10,... | collective-permute-start | bytes 393224 | tf_op jit(solution)/shard_map/ppermute | solution.py:306
  15.9 3.0 %collective-permute-start.3 = (bf16[4,3,64,512]{3,2,1,0:T(8,128)(2,1)S(1)}, bf16[4,3,64,512]{3,2,1,0:T(8,128)(2,1)S(1)}, u32[]{:S(2)}, u32[]{:S(2)}) collective-permute-start(bf16[4,3,64,512]{3,2,1,0:T(8,128)(2,1)S(1)} %pad_maximum_fusion), channel_id=1, source_target_pairs={{0,1},{1,0},{2,3},{3,2},{4,5},{5,4},{6,7},{7,6},{8,9},{9,8},{10,11... | collective-permute-start | bytes 2359304 | tf_op jit(solution)/shard_map/ppermute | solution.py:339
  16.3 11.7 %collective-permute-start.7 = (bf16[2,128,256]{2,1,0:T(8,128)(2,1)S(1)}, bf16[2,128,256]{2,1,0:T(8,128)(2,1)S(1)}, u32[]{:S(2)}, u32[]{:S(2)}) collective-permute-start(bf16[2,128,256]{2,1,0:T(8,128)(2,1)S(1)} %get-tuple-element.59), channel_id=1, source_target_pairs={{0,4},{1,5},{2,6},{3,7},{4,0},{5,1},{6,2},{7,3},{8,12},{9,13},{10,... | collective-permute-start | bytes 393224 | tf_op jit(solution)/shard_map/ppermute | solution.py:306
  18.8 9.6 %collective-permute-start.8 = (bf16[2,128,256]{2,1,0:T(8,128)(2,1)S(1)}, bf16[2,128,256]{2,1,0:T(8,128)(2,1)S(1)}, u32[]{:S(2)}, u32[]{:S(2)}) collective-permute-start(bf16[2,128,256]{2,1,0:T(8,128)(2,1)S(1)} %get-tuple-element.60), channel_id=1, source_target_pairs={{0,5},{1,4},{2,7},{3,6},{4,1},{5,0},{6,3},{7,2},{8,13},{9,12},{10,... | collective-permute-start | bytes 393224 | tf_op jit(solution)/shard_map/ppermute | solution.py:306
  18.9 14.6 %copy-start.11 = (bf16[8,8]{1,0:T(8,128)(2,1)S(1)}, bf16[8,8]{1,0:T(8,128)(2,1)}, u32[]{:S(2)}) copy-start(bf16[8,8]{1,0:T(8,128)(2,1)} %param.9) | copy-start | bytes 388
  18.9 9.4 %collective-permute-start.9 = (bf16[2,128,256]{2,1,0:T(8,128)(2,1)S(1)}, bf16[2,128,256]{2,1,0:T(8,128)(2,1)S(1)}, u32[]{:S(2)}, u32[]{:S(2)}) collective-permute-start(bf16[2,128,256]{2,1,0:T(8,128)(2,1)S(1)} %get-tuple-element.61), channel_id=1, source_target_pairs={{0,6},{1,7},{2,4},{3,5},{4,2},{5,3},{6,0},{7,1},{8,14},{9,15},{10,... | collective-permute-start | bytes 393224 | tf_op jit(solution)/shard_map/ppermute | solution.py:306
  29.0 12.4 %collective-permute-start.11 = (bf16[2,2,64,256]{3,2,1,0:T(8,128)(2,1)S(1)}, bf16[2,2,64,256]{3,2,1,0:T(8,128)(2,1)S(1)}, u32[]{:S(2)}, u32[]{:S(2)}) collective-permute-start(bf16[2,2,64,256]{3,2,1,0:T(8,128)(2,1)S(1)} %get-tuple-element.64), channel_id=1, source_target_pairs={{0,8},{8,0},{16,24},{24,16},{1,9},{9,1},{17,25},{25,17},{2,10},{10... | collective-permute-start | bytes 393224 | tf_op jit(solution)/shard_map/ppermute | solution.py:313
  30.6 12.9 %collective-permute-start.12 = (bf16[2,2,64,256]{3,2,1,0:T(8,128)(2,1)S(1)}, bf16[2,2,64,256]{3,2,1,0:T(8,128)(2,1)S(1)}, u32[]{:S(2)}, u32[]{:S(2)}) collective-permute-start(bf16[2,2,64,256]{3,2,1,0:T(8,128)(2,1)S(1)} %get-tuple-element.65), channel_id=1, source_target_pairs={{0,16},{8,24},{16,0},{24,8},{1,17},{9,25},{17,1},{25,9},{2,18},{10... | collective-permute-start | bytes 393224 | tf_op jit(solution)/shard_map/ppermute | solution.py:313
  33.2 10.4 %collective-permute-start.13 = (bf16[2,2,64,256]{3,2,1,0:T(8,128)(2,1)S(1)}, bf16[2,2,64,256]{3,2,1,0:T(8,128)(2,1)S(1)}, u32[]{:S(2)}, u32[]{:S(2)}) collective-permute-start(bf16[2,2,64,256]{3,2,1,0:T(8,128)(2,1)S(1)} %get-tuple-element.66), channel_id=1, source_target_pairs={{0,24},{8,16},{16,8},{24,0},{1,25},{9,17},{17,9},{25,1},{2,26},{10... | collective-permute-start | bytes 393224 | tf_op jit(solution)/shard_map/ppermute | solution.py:313
  33.6 18.9 %all-to-all-start = ((bf16[8,2,128,256]{3,2,1,0:T(8,128)(2,1)}), bf16[8,2,128,256]{3,2,1,0:T(8,128)(2,1)S(1)}, u32[]{:S(2)}, u32[]{:S(2)}) async-start(bf16[8,2,128,256]{3,2,1,0:T(8,128)(2,1)} %get-tuple-element.54), calls=%async_computation | async-start | bytes 2097152 | tf_op jit(solution)/shard_map/all_to_all | solution.py:300
  37.2 21.7 %collective-permute-start.17 = (bf16[2,2,64,256]{3,2,1,0:T(8,128)(2,1)S(1)}, bf16[2,2,64,256]{3,2,1,0:T(8,128)(2,1)S(1)}, u32[]{:S(2)}, u32[]{:S(2)}) collective-permute-start(bf16[2,2,64,256]{3,2,1,0:T(8,128)(2,1)S(1)} %get-tuple-element.74), channel_id=1, source_target_pairs={{0,8},{8,0},{16,24},{24,16},{1,9},{9,1},{17,25},{25,17},{2,10},{10... | collective-permute-start | bytes 393224 | tf_op jit(solution)/shard_map/ppermute | solution.py:313
  37.9 21.2 %collective-permute-start.18 = (bf16[2,2,64,256]{3,2,1,0:T(8,128)(2,1)S(1)}, bf16[2,2,64,256]{3,2,1,0:T(8,128)(2,1)S(1)}, u32[]{:S(2)}, u32[]{:S(2)}) collective-permute-start(bf16[2,2,64,256]{3,2,1,0:T(8,128)(2,1)S(1)} %get-tuple-element.75), channel_id=1, source_target_pairs={{0,16},{8,24},{16,0},{24,8},{1,17},{9,25},{17,1},{25,9},{2,18},{10... | collective-permute-start | bytes 393224 | tf_op jit(solution)/shard_map/ppermute | solution.py:313
  41.4 17.7 %collective-permute-start.19 = (bf16[2,2,64,256]{3,2,1,0:T(8,128)(2,1)S(1)}, bf16[2,2,64,256]{3,2,1,0:T(8,128)(2,1)S(1)}, u32[]{:S(2)}, u32[]{:S(2)}) collective-permute-start(bf16[2,2,64,256]{3,2,1,0:T(8,128)(2,1)S(1)} %get-tuple-element.76), channel_id=1, source_target_pairs={{0,24},{8,16},{16,8},{24,0},{1,25},{9,17},{17,9},{25,1},{2,26},{10... | collective-permute-start | bytes 393224 | tf_op jit(solution)/shard_map/ppermute | solution.py:313
  44.8 14.3 %copy-start.5 = (s32[2]{0:T(128)S(1)}, s32[2]{0:T(128)}, u32[]{:S(2)}) copy-start(s32[2]{0:T(128)} %copy-done.4) | copy-start | bytes 28
  52.5 0.6 copy-start.10
  54.6 10.3 %collective-permute-start.14 = (bf16[2,2,64,256]{3,2,1,0:T(8,128)(2,1)S(1)}, bf16[2,2,64,256]{3,2,1,0:T(8,128)(2,1)S(1)}, u32[]{:S(2)}, u32[]{:S(2)}) collective-permute-start(bf16[2,2,64,256]{3,2,1,0:T(8,128)(2,1)S(1)} %get-tuple-element.69.refs_1_), channel_id=1, source_target_pairs={{0,8},{8,0},{16,24},{24,16},{1,9},{9,1},{17,25},{25,17},{2,10},{10... | collective-permute-start | bytes 393224 | tf_op jit(solution)/shard_map/ppermute | solution.py:313
  56.0 12.9 %collective-permute-start.15 = (bf16[2,2,64,256]{3,2,1,0:T(8,128)(2,1)S(1)}, bf16[2,2,64,256]{3,2,1,0:T(8,128)(2,1)S(1)}, u32[]{:S(2)}, u32[]{:S(2)}) collective-permute-start(bf16[2,2,64,256]{3,2,1,0:T(8,128)(2,1)S(1)} %get-tuple-element.70.refs_2_), channel_id=1, source_target_pairs={{0,16},{8,24},{16,0},{24,8},{1,17},{9,25},{17,1},{25,9},{2,18},{10... | collective-permute-start | bytes 393224 | tf_op jit(solution)/shard_map/ppermute | solution.py:313
  58.9 10.0 %collective-permute-start.16 = (bf16[2,2,64,256]{3,2,1,0:T(8,128)(2,1)S(1)}, bf16[2,2,64,256]{3,2,1,0:T(8,128)(2,1)S(1)}, u32[]{:S(2)}, u32[]{:S(2)}) collective-permute-start(bf16[2,2,64,256]{3,2,1,0:T(8,128)(2,1)S(1)} %get-tuple-element.71.refs_3_), channel_id=1, source_target_pairs={{0,24},{8,16},{16,8},{24,0},{1,25},{9,17},{17,9},{25,1},{2,26},{10... | collective-permute-start | bytes 393224 | tf_op jit(solution)/shard_map/ppermute | solution.py:313
  59.1 9.8 %copy-start.6 = (f32[8]{0:T(128)S(1)}, f32[8]{0:T(128)}, u32[]{:S(2)}) copy-start(f32[8]{0:T(128)} %occ.9) | copy-start | bytes 100
  60.7 19.5 %collective-permute-start.20 = (bf16[2,2,64,256]{3,2,1,0:T(8,128)(2,1)S(1)}, bf16[2,2,64,256]{3,2,1,0:T(8,128)(2,1)S(1)}, u32[]{:S(2)}, u32[]{:S(2)}) collective-permute-start(bf16[2,2,64,256]{3,2,1,0:T(8,128)(2,1)S(1)} %get-tuple-element.78.refs_2_), channel_id=1, source_target_pairs={{0,8},{8,0},{16,24},{24,16},{1,9},{9,1},{17,25},{25,17},{2,10},{10... | collective-permute-start | bytes 393224 | tf_op jit(solution)/shard_map/ppermute | solution.py:313
  61.2 20.7 %collective-permute-start.21 = (bf16[2,2,64,256]{3,2,1,0:T(8,128)(2,1)S(1)}, bf16[2,2,64,256]{3,2,1,0:T(8,128)(2,1)S(1)}, u32[]{:S(2)}, u32[]{:S(2)}) collective-permute-start(bf16[2,2,64,256]{3,2,1,0:T(8,128)(2,1)S(1)} %get-tuple-element.79.refs_3_), channel_id=1, source_target_pairs={{0,16},{8,24},{16,0},{24,8},{1,17},{9,25},{17,1},{25,9},{2,18},{10... | collective-permute-start | bytes 393224 | tf_op jit(solution)/shard_map/ppermute | solution.py:313
  65.0 16.9 %collective-permute-start.22 = (bf16[2,2,64,256]{3,2,1,0:T(8,128)(2,1)S(1)}, bf16[2,2,64,256]{3,2,1,0:T(8,128)(2,1)S(1)}, u32[]{:S(2)}, u32[]{:S(2)}) collective-permute-start(bf16[2,2,64,256]{3,2,1,0:T(8,128)(2,1)S(1)} %get-tuple-element.80.refs_4_), channel_id=1, source_target_pairs={{0,24},{8,16},{16,8},{24,0},{1,25},{9,17},{17,9},{25,1},{2,26},{10... | collective-permute-start | bytes 393224 | tf_op jit(solution)/shard_map/ppermute | solution.py:313
  71.5 0.8 copy-start.8
  72.3 23.2 %collective-permute-start.26 = (bf16[2,2,64,256]{3,2,1,0:T(8,128)(2,1)S(1)}, bf16[2,2,64,256]{3,2,1,0:T(8,128)(2,1)S(1)}, u32[]{:S(2)}, u32[]{:S(2)}) collective-permute-start(bf16[2,2,64,256]{3,2,1,0:T(8,128)(2,1)S(1)} %get-tuple-element.88), channel_id=1, source_target_pairs={{0,8},{8,0},{16,24},{24,16},{1,9},{9,1},{17,25},{25,17},{2,10},{10... | collective-permute-start | bytes 393224 | tf_op jit(solution)/shard_map/ppermute | solution.py:313
  79.5 17.5 %collective-permute-start.27 = (bf16[2,2,64,256]{3,2,1,0:T(8,128)(2,1)S(1)}, bf16[2,2,64,256]{3,2,1,0:T(8,128)(2,1)S(1)}, u32[]{:S(2)}, u32[]{:S(2)}) collective-permute-start(bf16[2,2,64,256]{3,2,1,0:T(8,128)(2,1)S(1)} %get-tuple-element.89), channel_id=1, source_target_pairs={{0,16},{8,24},{16,0},{24,8},{1,17},{9,25},{17,1},{25,9},{2,18},{10... | collective-permute-start | bytes 393224 | tf_op jit(solution)/shard_map/ppermute | solution.py:313
  80.2 16.8 %collective-permute-start.28 = (bf16[2,2,64,256]{3,2,1,0:T(8,128)(2,1)S(1)}, bf16[2,2,64,256]{3,2,1,0:T(8,128)(2,1)S(1)}, u32[]{:S(2)}, u32[]{:S(2)}) collective-permute-start(bf16[2,2,64,256]{3,2,1,0:T(8,128)(2,1)S(1)} %get-tuple-element.90), channel_id=1, source_target_pairs={{0,24},{8,16},{16,8},{24,0},{1,25},{9,17},{17,9},{25,1},{2,26},{10... | collective-permute-start | bytes 393224 | tf_op jit(solution)/shard_map/ppermute | solution.py:313
  85.6 13.6 %collective-permute-start.23 = (bf16[2,2,64,256]{3,2,1,0:T(8,128)(2,1)S(1)}, bf16[2,2,64,256]{3,2,1,0:T(8,128)(2,1)S(1)}, u32[]{:S(2)}, u32[]{:S(2)}) collective-permute-start(bf16[2,2,64,256]{3,2,1,0:T(8,128)(2,1)S(1)} %get-tuple-element.84), channel_id=1, source_target_pairs={{0,8},{8,0},{16,24},{24,16},{1,9},{9,1},{17,25},{25,17},{2,10},{10... | collective-permute-start | bytes 393224 | tf_op jit(solution)/shard_map/ppermute | solution.py:313
  88.2 11.0 %collective-permute-start.24 = (bf16[2,2,64,256]{3,2,1,0:T(8,128)(2,1)S(1)}, bf16[2,2,64,256]{3,2,1,0:T(8,128)(2,1)S(1)}, u32[]{:S(2)}, u32[]{:S(2)}) collective-permute-start(bf16[2,2,64,256]{3,2,1,0:T(8,128)(2,1)S(1)} %get-tuple-element.85), channel_id=1, source_target_pairs={{0,16},{8,24},{16,0},{24,8},{1,17},{9,25},{17,1},{25,9},{2,18},{10... | collective-permute-start | bytes 393224 | tf_op jit(solution)/shard_map/ppermute | solution.py:313
  88.9 24.7 %all-to-all-start.1 = ((bf16[8,2,128,256]{3,2,1,0:T(8,128)(2,1)}), bf16[8,2,128,256]{3,2,1,0:T(8,128)(2,1)S(1)}, u32[]{:S(2)}, u32[]{:S(2)}) async-start(bf16[8,2,128,256]{3,2,1,0:T(8,128)(2,1)} %get-tuple-element.81), calls=%async_computation.1 | async-start | bytes 2097152 | tf_op jit(solution)/shard_map/all_to_all | solution.py:300
  95.5 7.8 %collective-permute-start.25 = (bf16[2,2,64,256]{3,2,1,0:T(8,128)(2,1)S(1)}, bf16[2,2,64,256]{3,2,1,0:T(8,128)(2,1)S(1)}, u32[]{:S(2)}, u32[]{:S(2)}) collective-permute-start(bf16[2,2,64,256]{3,2,1,0:T(8,128)(2,1)S(1)} %get-tuple-element.86), channel_id=1, source_target_pairs={{0,24},{8,16},{16,8},{24,0},{1,25},{9,17},{17,9},{25,1},{2,26},{10... | collective-permute-start | bytes 393224 | tf_op jit(solution)/shard_map/ppermute | solution.py:313
  97.0 1.0 copy-start.9
  103.3 10.3 %copy-start.3 = (f32[512]{0:T(512)S(1)}, f32[512]{0:T(512)}, u32[]{:S(2)}) copy-start(f32[512]{0:T(512)} %param.11) | copy-start | bytes 6148
  104.5 3.8 %collective-permute-start.29 = (bf16[2,128,256]{2,1,0:T(8,128)(2,1)S(1)}, bf16[2,128,256]{2,1,0:T(8,128)(2,1)S(1)}, u32[]{:S(2)}, u32[]{:S(2)}) collective-permute-start(bf16[2,128,256]{2,1,0:T(8,128)(2,1)S(1)} %get-tuple-element.92), channel_id=1, source_target_pairs={{0,1},{1,0},{2,3},{3,2},{4,5},{5,4},{6,7},{7,6},{8,9},{9,8},{10,11... | collective-permute-start | bytes 393224 | tf_op jit(solution)/shard_map/ppermute | solution.py:306
  104.6 8.9 %collective-permute-start.30 = (bf16[2,128,256]{2,1,0:T(8,128)(2,1)S(1)}, bf16[2,128,256]{2,1,0:T(8,128)(2,1)S(1)}, u32[]{:S(2)}, u32[]{:S(2)}) collective-permute-start(bf16[2,128,256]{2,1,0:T(8,128)(2,1)S(1)} %get-tuple-element.93), channel_id=1, source_target_pairs={{0,2},{1,3},{2,0},{3,1},{4,6},{5,7},{6,4},{7,5},{8,10},{9,11},{10,... | collective-permute-start | bytes 393224 | tf_op jit(solution)/shard_map/ppermute | solution.py:306
  106.3 14.8 %collective-permute-start.31 = (bf16[2,128,256]{2,1,0:T(8,128)(2,1)S(1)}, bf16[2,128,256]{2,1,0:T(8,128)(2,1)S(1)}, u32[]{:S(2)}, u32[]{:S(2)}) collective-permute-start(bf16[2,128,256]{2,1,0:T(8,128)(2,1)S(1)} %get-tuple-element.94), channel_id=1, source_target_pairs={{0,3},{1,2},{2,1},{3,0},{4,7},{5,6},{6,5},{7,4},{8,11},{9,10},{10,... | collective-permute-start | bytes 393224 | tf_op jit(solution)/shard_map/ppermute | solution.py:306
  106.5 14.7 %collective-permute-start.32 = (bf16[2,128,256]{2,1,0:T(8,128)(2,1)S(1)}, bf16[2,128,256]{2,1,0:T(8,128)(2,1)S(1)}, u32[]{:S(2)}, u32[]{:S(2)}) collective-permute-start(bf16[2,128,256]{2,1,0:T(8,128)(2,1)S(1)} %get-tuple-element.95), channel_id=1, source_target_pairs={{0,4},{1,5},{2,6},{3,7},{4,0},{5,1},{6,2},{7,3},{8,12},{9,13},{10,... | collective-permute-start | bytes 393224 | tf_op jit(solution)/shard_map/ppermute | solution.py:306
  108.3 12.9 %collective-permute-start.33 = (bf16[2,128,256]{2,1,0:T(8,128)(2,1)S(1)}, bf16[2,128,256]{2,1,0:T(8,128)(2,1)S(1)}, u32[]{:S(2)}, u32[]{:S(2)}) collective-permute-start(bf16[2,128,256]{2,1,0:T(8,128)(2,1)S(1)} %get-tuple-element.96), channel_id=1, source_target_pairs={{0,5},{1,4},{2,7},{3,6},{4,1},{5,0},{6,3},{7,2},{8,13},{9,12},{10,... | collective-permute-start | bytes 393224 | tf_op jit(solution)/shard_map/ppermute | solution.py:306
  108.3 12.9 %collective-permute-start.34 = (bf16[2,128,256]{2,1,0:T(8,128)(2,1)S(1)}, bf16[2,128,256]{2,1,0:T(8,128)(2,1)S(1)}, u32[]{:S(2)}, u32[]{:S(2)}) collective-permute-start(bf16[2,128,256]{2,1,0:T(8,128)(2,1)S(1)} %get-tuple-element.97), channel_id=1, source_target_pairs={{0,6},{1,7},{2,4},{3,5},{4,2},{5,3},{6,0},{7,1},{8,14},{9,15},{10,... | collective-permute-start | bytes 393224 | tf_op jit(solution)/shard_map/ppermute | solution.py:306
  113.5 8.2 %collective-permute-start.35 = (bf16[2,128,256]{2,1,0:T(8,128)(2,1)S(1)}, bf16[2,128,256]{2,1,0:T(8,128)(2,1)S(1)}, u32[]{:S(2)}, u32[]{:S(2)}) collective-permute-start(bf16[2,128,256]{2,1,0:T(8,128)(2,1)S(1)} %get-tuple-element.98), channel_id=1, source_target_pairs={{0,7},{1,6},{2,5},{3,4},{4,3},{5,2},{6,1},{7,0},{8,15},{9,14},{10,... | collective-permute-start | bytes 393224 | tf_op jit(solution)/shard_map/ppermute | solution.py:306
  113.7 1.4 %copy-start.7 = (bf16[512,1536]{1,0:T(8,128)(2,1)S(1)}, bf16[512,1536]{1,0:T(8,128)(2,1)}, u32[]{:S(2)}) copy-start(bf16[512,1536]{1,0:T(8,128)(2,1)} %get-tuple-element.82.whole) | copy-start | bytes 4718596

commit v24 on v23

--- a/solution.py
+++ b/solution.py
@@ -185,7 +185,7 @@
             store(k // first, u, k % first, column, at, result)
         return carry
 
-    lax.fori_loop(0, first * strips, strip, 0)
+    lax.fori_loop(0, first * strips, strip, 0, unroll=2)
 
 
 def half_kernel(tiles, groups, first, chunk, place, fock, ladder, *refs):

time: 125 us -> 125 us (level)
  no operation moved by 1% of the time
where the time goes in v24:
time: 125 us; the launch traced here: 124 us
  starting transfers between devices  65.8 us (53%)
  Pallas kernels  29.3 us (23%)
  waiting for transfers between devices  20.2 us (16%)
  local copies, waits for them, and re-layouts  6.95 us (6%)
  between operations  1.63 us (1%)
    ppermute x18, starting transfers between devices, across_first(): lax.ppermute(parts[s], 'occi', [(k, k ^ s) for k in range(groups)])  35.2 us
    pallas_call x9, Pallas kernels, call(): pl.pallas_call(body, out_shape=outs, in_specs=specs, out_specs=jax.tree.m...  19.3 us
    ppermute x14, starting transfers between devices, by_distance(): lax.ppermute(parts[k], 'occj', [(d, d ^ k) for d in range(devices)])  15.8 us
    all_to_all x2, starting transfers between devices, exchange(): lax.all_to_all(blocks, 'occj', split_axis=0, concat_axis=0, tiled=True)  10.1 us
    all_to_all x2, waiting for transfers between devices, exchange(): lax.all_to_all(blocks, 'occj', split_axis=0, concat_axis=0, tiled=True)  7.72 us
    ppermute x18, waiting for transfers between devices, across_first(): lax.ppermute(parts[s], 'occi', [(k, k ^ s) for k in range(groups)])  6.92 us
    pallas_call x1, Pallas kernels, local(): pl.pallas_call(functools.partial(second_ladder_kernel, tiles, first), gri...  6.03 us
    unnamed x28, local copies, waits for them, and re-layouts  5.43 us
  transfers between devices with their start and end apart: 38, of which 8 were waited for; matrix products, arithmetic and copies ran while one was open for 2% of the time, Pallas kernels for 21%

profile of v24, /device:TPU:0, one launch (start us, length us, event | category | flops | bytes accessed | tf_op | source)
XLA Modules:
  0.0 124.2 jit_solution(9954452462345122906)
XLA Ops:
  0.0 3.0 %collective-permute-start = (bf16[3,64,512]{2,1,0:T(8,128)(2,1)}, bf16[3,64,512]{2,1,0:T(8,128)(2,1)S(1)}, u32[]{:S(2)}, u32[]{:S(2)}) collective-permute-start(bf16[3,64,512]{2,1,0:T(8,128)(2,1)} %refs_0_.1), channel_id=1, source_target_pairs={{0,2},{1,3},{2,0},{3,1},{4,6},{5,7},{6,4},{7,5},{8,10},{9,11},{10,... | collective-permute-start | bytes 589832 | tf_op jit(solution)/shard_map/ppermute | solution.py:339
  3.0 1.5 %collective-permute-start.1 = (bf16[3,64,512]{2,1,0:T(8,128)(2,1)}, bf16[3,64,512]{2,1,0:T(8,128)(2,1)S(1)}, u32[]{:S(2)}, u32[]{:S(2)}) collective-permute-start(bf16[3,64,512]{2,1,0:T(8,128)(2,1)} %refs_0_.1), channel_id=1, source_target_pairs={{0,4},{1,5},{2,6},{3,7},{4,0},{5,1},{6,2},{7,3},{8,12},{9,13},{10,... | collective-permute-start | bytes 589832 | tf_op jit(solution)/shard_map/ppermute | solution.py:339
  4.6 1.6 %copy-done = f32[2,1,512,512]{3,2,1,0:T(8,128)S(1)} copy-done((f32[2,1,512,512]{3,2,1,0:T(8,128)S(1)}, f32[2,1,512,512]{3,2,1,0:T(8,128)}, u32[]{:S(2)}) %copy-start) | copy-done | bytes 2097176
  6.2 0.9 shard_map.73
  7.1 1.6 %collective-permute-start.10 = (bf16[2,128,256]{2,1,0:T(8,128)(2,1)S(1)}, bf16[2,128,256]{2,1,0:T(8,128)(2,1)S(1)}, u32[]{:S(2)}, u32[]{:S(2)}) collective-permute-start(bf16[2,128,256]{2,1,0:T(8,128)(2,1)S(1)} %get-tuple-element.62), channel_id=1, source_target_pairs={{0,7},{1,6},{2,5},{3,4},{4,3},{5,2},{6,1},{7,0},{8,15},{9,14},{10,... | collective-permute-start | bytes 393224 | tf_op jit(solution)/shard_map/ppermute | solution.py:306
  8.7 1.5 %collective-permute-start.4 = (bf16[2,128,256]{2,1,0:T(8,128)(2,1)S(1)}, bf16[2,128,256]{2,1,0:T(8,128)(2,1)S(1)}, u32[]{:S(2)}, u32[]{:S(2)}) collective-permute-start(bf16[2,128,256]{2,1,0:T(8,128)(2,1)S(1)} %get-tuple-element.56), channel_id=1, source_target_pairs={{0,1},{1,0},{2,3},{3,2},{4,5},{5,4},{6,7},{7,6},{8,9},{9,8},{10,11... | collective-permute-start | bytes 393224 | tf_op jit(solution)/shard_map/ppermute | solution.py:306
  10.2 0.6 dynamic_slice.14
  11.4 0.6 dynamic_slice.12
  12.7 0.6 collective-permute-start.5
  13.3 2.5 %collective-permute-done.1.refs_2_ = bf16[3,64,512]{2,1,0:T(8,128)(2,1)S(1)} collective-permute-done((bf16[3,64,512]{2,1,0:T(8,128)(2,1)}, bf16[3,64,512]{2,1,0:T(8,128)(2,1)S(1)}, u32[]{:S(2)}, u32[]{:S(2)}) %collective-permute-start.1) | collective-permute-done | bytes 196640 | tf_op jit(solution)/shard_map/ppermute | solution.py:339
  15.8 0.1 pad_maximum_fusion
  16.0 0.1 fusion
  16.2 0.1 broadcast_add_fusion.2
  16.3 2.4 %collective-permute-start.7 = (bf16[2,128,256]{2,1,0:T(8,128)(2,1)S(1)}, bf16[2,128,256]{2,1,0:T(8,128)(2,1)S(1)}, u32[]{:S(2)}, u32[]{:S(2)}) collective-permute-start(bf16[2,128,256]{2,1,0:T(8,128)(2,1)S(1)} %get-tuple-element.59), channel_id=1, source_target_pairs={{0,4},{1,5},{2,6},{3,7},{4,0},{5,1},{6,2},{7,3},{8,12},{9,13},{10,... | collective-permute-start | bytes 393224 | tf_op jit(solution)/shard_map/ppermute | solution.py:306
  18.8 0.2 collective-permute-start.8
  18.9 2.9 %collective-permute-start.9 = (bf16[2,128,256]{2,1,0:T(8,128)(2,1)S(1)}, bf16[2,128,256]{2,1,0:T(8,128)(2,1)S(1)}, u32[]{:S(2)}, u32[]{:S(2)}) collective-permute-start(bf16[2,128,256]{2,1,0:T(8,128)(2,1)S(1)} %get-tuple-element.61), channel_id=1, source_target_pairs={{0,6},{1,7},{2,4},{3,5},{4,2},{5,3},{6,0},{7,1},{8,14},{9,15},{10,... | collective-permute-start | bytes 393224 | tf_op jit(solution)/shard_map/ppermute | solution.py:306
  21.8 6.3 %shard_map.74 = (bf16[8,2,128,256]{3,2,1,0:T(8,128)(2,1)}, bf16[512,1536]{1,0:T(8,128)(2,1)}) custom-call(s32[2]{0:T(128)S(1)} %pad_add_fusion.place.source, f32[2,512,512]{2,1,0:T(8,128)} %bitcast.13, bf16[3,64,512]{2,1,0:T(8,128)(2,1)S(1)} %copy-done.1, bf16[3,64,512]{2,1,0:T(8,128)(2,1)S(1)} %collective-permute-done.refs_1_, ...), custom_call_target="tpu_custom_call" | custom-call | flops 3221225472 | bytes 4194304 | tf_op jit(solution)/shard_map/pallas_call | solution.py:42
  28.1 0.2 collective-permute-done.8.refs_5_
  28.3 0.7 shard_map.75
  29.0 1.6 %collective-permute-start.11 = (bf16[2,2,64,256]{3,2,1,0:T(8,128)(2,1)S(1)}, bf16[2,2,64,256]{3,2,1,0:T(8,128)(2,1)S(1)}, u32[]{:S(2)}, u32[]{:S(2)}) collective-permute-start(bf16[2,2,64,256]{3,2,1,0:T(8,128)(2,1)S(1)} %get-tuple-element.64), channel_id=1, source_target_pairs={{0,8},{8,0},{16,24},{24,16},{1,9},{9,1},{17,25},{25,17},{2,10},{10... | collective-permute-start | bytes 393224 | tf_op jit(solution)/shard_map/ppermute | solution.py:313
  30.6 2.6 %collective-permute-start.12 = (bf16[2,2,64,256]{3,2,1,0:T(8,128)(2,1)S(1)}, bf16[2,2,64,256]{3,2,1,0:T(8,128)(2,1)S(1)}, u32[]{:S(2)}, u32[]{:S(2)}) collective-permute-start(bf16[2,2,64,256]{3,2,1,0:T(8,128)(2,1)S(1)} %get-tuple-element.65), channel_id=1, source_target_pairs={{0,16},{8,24},{16,0},{24,8},{1,17},{9,25},{17,1},{25,9},{2,18},{10... | collective-permute-start | bytes 393224 | tf_op jit(solution)/shard_map/ppermute | solution.py:313
  33.2 0.2 collective-permute-start.13
  33.6 3.6 %all-to-all-start = ((bf16[8,2,128,256]{3,2,1,0:T(8,128)(2,1)}), bf16[8,2,128,256]{3,2,1,0:T(8,128)(2,1)S(1)}, u32[]{:S(2)}, u32[]{:S(2)}) async-start(bf16[8,2,128,256]{3,2,1,0:T(8,128)(2,1)} %get-tuple-element.54), calls=%async_computation | async-start | bytes 2097152 | tf_op jit(solution)/shard_map/all_to_all | solution.py:300
  37.2 0.7 collective-permute-start.17
  37.9 3.5 %collective-permute-start.18 = (bf16[2,2,64,256]{3,2,1,0:T(8,128)(2,1)S(1)}, bf16[2,2,64,256]{3,2,1,0:T(8,128)(2,1)S(1)}, u32[]{:S(2)}, u32[]{:S(2)}) collective-permute-start(bf16[2,2,64,256]{3,2,1,0:T(8,128)(2,1)S(1)} %get-tuple-element.75), channel_id=1, source_target_pairs={{0,16},{8,24},{16,0},{24,8},{1,17},{9,25},{17,1},{25,9},{2,18},{10... | collective-permute-start | bytes 393224 | tf_op jit(solution)/shard_map/ppermute | solution.py:313
  41.4 0.2 collective-permute-start.19
  41.6 2.0 %collective-permute-done.12.refs_2_ = bf16[2,2,64,256]{3,2,1,0:T(8,128)(2,1)S(1)} collective-permute-done((bf16[2,2,64,256]{3,2,1,0:T(8,128)(2,1)S(1)}, bf16[2,2,64,256]{3,2,1,0:T(8,128)(2,1)S(1)}, u32[]{:S(2)}, u32[]{:S(2)}) %collective-permute-start.12) | collective-permute-done | bytes 131104 | tf_op jit(solution)/shard_map/ppermute | solution.py:313
  43.6 1.2 shard_map.76.place
  44.8 7.7 %all-to-all-done.ladder = bf16[8,2,128,256]{3,2,1,0:T(8,128)(2,1)S(1)} async-done(((bf16[8,2,128,256]{3,2,1,0:T(8,128)(2,1)}), bf16[8,2,128,256]{3,2,1,0:T(8,128)(2,1)S(1)}, u32[]{:S(2)}, u32[]{:S(2)}) %all-to-all-start) | async-done | bytes 1048608 | tf_op jit(solution)/shard_map/all_to_all | solution.py:300
  52.5 0.6 copy-done.10
  53.1 1.5 %shard_map.77 = (bf16[2,2,64,256]{3,2,1,0:T(8,128)(2,1)S(1)}, bf16[2,2,64,256]{3,2,1,0:T(8,128)(2,1)S(1)}, bf16[2,2,64,256]{3,2,1,0:T(8,128)(2,1)S(1)}, bf16[2,2,64,256]{3,2,1,0:T(8,128)(2,1)S(1)}) custom-call(s32[2]{0:T(128)S(1)} %copy-done.10, f32[8,8]{1,0:T(8,128)S(1)} %convert_element_type.3.fock, bf16[8,2,128,256]{3,2,1,0:T(8,128)(2,1)S(1)} %all-to-all-done.ladder, ...), custom_call_target="tpu_custom_call" | custom-call | flops 30000001024 | bytes 3145728 | tf_op jit(solution)/shard_map/pallas_call | solution.py:42
  54.6 1.3 %collective-permute-start.14 = (bf16[2,2,64,256]{3,2,1,0:T(8,128)(2,1)S(1)}, bf16[2,2,64,256]{3,2,1,0:T(8,128)(2,1)S(1)}, u32[]{:S(2)}, u32[]{:S(2)}) collective-permute-start(bf16[2,2,64,256]{3,2,1,0:T(8,128)(2,1)S(1)} %get-tuple-element.69.refs_1_), channel_id=1, source_target_pairs={{0,8},{8,0},{16,24},{24,16},{1,9},{9,1},{17,25},{25,17},{2,10},{10... | collective-permute-start | bytes 393224 | tf_op jit(solution)/shard_map/ppermute | solution.py:313
  56.0 2.9 %collective-permute-start.15 = (bf16[2,2,64,256]{3,2,1,0:T(8,128)(2,1)S(1)}, bf16[2,2,64,256]{3,2,1,0:T(8,128)(2,1)S(1)}, u32[]{:S(2)}, u32[]{:S(2)}) collective-permute-start(bf16[2,2,64,256]{3,2,1,0:T(8,128)(2,1)S(1)} %get-tuple-element.70.refs_2_), channel_id=1, source_target_pairs={{0,16},{8,24},{16,0},{24,8},{1,17},{9,25},{17,1},{25,9},{2,18},{10... | collective-permute-start | bytes 393224 | tf_op jit(solution)/shard_map/ppermute | solution.py:313
  58.8 0.2 collective-permute-start.16
  59.1 1.5 %shard_map.79 = (bf16[2,2,64,256]{3,2,1,0:T(8,128)(2,1)S(1)}, bf16[2,2,64,256]{3,2,1,0:T(8,128)(2,1)S(1)}, bf16[2,2,64,256]{3,2,1,0:T(8,128)(2,1)S(1)}, bf16[2,2,64,256]{3,2,1,0:T(8,128)(2,1)S(1)}) custom-call(s32[2]{0:T(128)S(1)} %copy-done.5, f32[8,8]{1,0:T(8,128)S(1)} %convert_element_type.3.fock, bf16[8,2,128,256]{3,2,1,0:T(8,128)(2,1)S(1)} %all-to-all-done.ladder, ...), custom_call_target="tpu_custom_call" | custom-call | flops 30000001024 | bytes 3145728 | tf_op jit(solution)/shard_map/pallas_call | solution.py:42
  60.6 0.5 collective-permute-start.20
  61.1 3.8 %collective-permute-start.21 = (bf16[2,2,64,256]{3,2,1,0:T(8,128)(2,1)S(1)}, bf16[2,2,64,256]{3,2,1,0:T(8,128)(2,1)S(1)}, u32[]{:S(2)}, u32[]{:S(2)}) collective-permute-start(bf16[2,2,64,256]{3,2,1,0:T(8,128)(2,1)S(1)} %get-tuple-element.79.refs_3_), channel_id=1, source_target_pairs={{0,16},{8,24},{16,0},{24,8},{1,17},{9,25},{17,1},{25,9},{2,18},{10... | collective-permute-start | bytes 393224 | tf_op jit(solution)/shard_map/ppermute | solution.py:313
  64.9 3.1 %collective-permute-start.22 = (bf16[2,2,64,256]{3,2,1,0:T(8,128)(2,1)S(1)}, bf16[2,2,64,256]{3,2,1,0:T(8,128)(2,1)S(1)}, u32[]{:S(2)}, u32[]{:S(2)}) collective-permute-start(bf16[2,2,64,256]{3,2,1,0:T(8,128)(2,1)S(1)} %get-tuple-element.80.refs_4_), channel_id=1, source_target_pairs={{0,24},{8,16},{16,8},{24,0},{1,25},{9,17},{17,9},{25,1},{2,26},{10... | collective-permute-start | bytes 393224 | tf_op jit(solution)/shard_map/ppermute | solution.py:313
  68.0 0.8 collective-permute-done.15.refs_6_
  68.8 2.5 %shard_map.78 = (bf16[8,2,64,256]{3,2,1,0:T(8,128)(2,1)S(1)}, bf16[2,8,64,256]{3,2,1,0:T(8,128)(2,1)S(1)}, bf16[2,2,64,256]{3,2,1,0:T(8,128)(2,1)S(1)}, bf16[2,2...) custom-call(s32[2]{0:T(128)S(1)} %copy-done.5, f32[8,8]{1,0:T(8,128)S(1)} %convert_element_type.3.fock, ...), custom_call_target="tpu_custom_call" | custom-call | flops 30000001024 | bytes 5242880 | tf_op jit(solution)/shard_map/pallas_call | solution.py:42
  71.4 0.8 copy-done.8
  72.2 7.2 %collective-permute-start.26 = (bf16[2,2,64,256]{3,2,1,0:T(8,128)(2,1)S(1)}, bf16[2,2,64,256]{3,2,1,0:T(8,128)(2,1)S(1)}, u32[]{:S(2)}, u32[]{:S(2)}) collective-permute-start(bf16[2,2,64,256]{3,2,1,0:T(8,128)(2,1)S(1)} %get-tuple-element.88), channel_id=1, source_target_pairs={{0,8},{8,0},{16,24},{24,16},{1,9},{9,1},{17,25},{25,17},{2,10},{10... | collective-permute-start | bytes 393224 | tf_op jit(solution)/shard_map/ppermute | solution.py:313
  79.4 0.7 collective-permute-start.27
  80.1 1.6 %collective-permute-start.28 = (bf16[2,2,64,256]{3,2,1,0:T(8,128)(2,1)S(1)}, bf16[2,2,64,256]{3,2,1,0:T(8,128)(2,1)S(1)}, u32[]{:S(2)}, u32[]{:S(2)}) collective-permute-start(bf16[2,2,64,256]{3,2,1,0:T(8,128)(2,1)S(1)} %get-tuple-element.90), channel_id=1, source_target_pairs={{0,24},{8,16},{16,8},{24,0},{1,25},{9,17},{17,9},{25,1},{2,26},{10... | collective-permute-start | bytes 393224 | tf_op jit(solution)/shard_map/ppermute | solution.py:313
  81.7 3.6 %shard_map.80 = (bf16[8,2,128,256]{3,2,1,0:T(8,128)(2,1)}, bf16[2,8,64,256]{3,2,1,0:T(8,128)(2,1)S(1)}, bf16[2,2,64,256]{3,2,1,0:T(8,128)(2,1)S(1)}, bf16[2,2,64...) custom-call(s32[2]{0:T(128)S(1)} %copy-done.5, f32[8,8]{1,0:T(8,128)S(1)} %convert_element_type.3.fock, ...), custom_call_target="tpu_custom_call" | custom-call | flops 30000001024 | bytes 5242880 | tf_op jit(solution)/shard_map/pallas_call | solution.py:42
  85.3 2.7 %collective-permute-start.23 = (bf16[2,2,64,256]{3,2,1,0:T(8,128)(2,1)S(1)}, bf16[2,2,64,256]{3,2,1,0:T(8,128)(2,1)S(1)}, u32[]{:S(2)}, u32[]{:S(2)}) collective-permute-start(bf16[2,2,64,256]{3,2,1,0:T(8,128)(2,1)S(1)} %get-tuple-element.84), channel_id=1, source_target_pairs={{0,8},{8,0},{16,24},{24,16},{1,9},{9,1},{17,25},{25,17},{2,10},{10... | collective-permute-start | bytes 393224 | tf_op jit(solution)/shard_map/ppermute | solution.py:313
  88.1 0.7 collective-permute-start.24
  88.8 6.5 %all-to-all-start.1 = ((bf16[8,2,128,256]{3,2,1,0:T(8,128)(2,1)}), bf16[8,2,128,256]{3,2,1,0:T(8,128)(2,1)S(1)}, u32[]{:S(2)}, u32[]{:S(2)}) async-start(bf16[8,2,128,256]{3,2,1,0:T(8,128)(2,1)} %get-tuple-element.81), calls=%async_computation.1 | async-start | bytes 2097152 | tf_op jit(solution)/shard_map/all_to_all | solution.py:300
  95.3 1.5 %collective-permute-start.25 = (bf16[2,2,64,256]{3,2,1,0:T(8,128)(2,1)S(1)}, bf16[2,2,64,256]{3,2,1,0:T(8,128)(2,1)S(1)}, u32[]{:S(2)}, u32[]{:S(2)}) collective-permute-start(bf16[2,2,64,256]{3,2,1,0:T(8,128)(2,1)S(1)} %get-tuple-element.86), channel_id=1, source_target_pairs={{0,24},{8,16},{16,8},{24,0},{1,25},{9,17},{17,9},{25,1},{2,26},{10... | collective-permute-start | bytes 393224 | tf_op jit(solution)/shard_map/ppermute | solution.py:313
  96.8 1.0 copy-done.9
  97.9 1.1 shard_map.82.refs_3_
  99.0 4.1 %collective-permute-done.25.refs_2_ = bf16[2,2,64,256]{3,2,1,0:T(8,128)(2,1)S(1)} collective-permute-done((bf16[2,2,64,256]{3,2,1,0:T(8,128)(2,1)S(1)}, bf16[2,2,64,256]{3,2,1,0:T(8,128)(2,1)S(1)}, u32[]{:S(2)}, u32[]{:S(2)}) %collective-permute-start.25) | collective-permute-done | bytes 131104 | tf_op jit(solution)/shard_map/ppermute | solution.py:313
  103.1 1.2 shard_map.83
  104.4 1.7 %collective-permute-start.30 = (bf16[2,128,256]{2,1,0:T(8,128)(2,1)S(1)}, bf16[2,128,256]{2,1,0:T(8,128)(2,1)S(1)}, u32[]{:S(2)}, u32[]{:S(2)}) collective-permute-start(bf16[2,128,256]{2,1,0:T(8,128)(2,1)S(1)} %get-tuple-element.93), channel_id=1, source_target_pairs={{0,2},{1,3},{2,0},{3,1},{4,6},{5,7},{6,4},{7,5},{8,10},{9,11},{10,... | collective-permute-start | bytes 393224 | tf_op jit(solution)/shard_map/ppermute | solution.py:306
  106.1 0.1 collective-permute-start.31
  106.3 1.8 %collective-permute-start.32 = (bf16[2,128,256]{2,1,0:T(8,128)(2,1)S(1)}, bf16[2,128,256]{2,1,0:T(8,128)(2,1)S(1)}, u32[]{:S(2)}, u32[]{:S(2)}) collective-permute-start(bf16[2,128,256]{2,1,0:T(8,128)(2,1)S(1)} %get-tuple-element.95), channel_id=1, source_target_pairs={{0,4},{1,5},{2,6},{3,7},{4,0},{5,1},{6,2},{7,3},{8,12},{9,13},{10,... | collective-permute-start | bytes 393224 | tf_op jit(solution)/shard_map/ppermute | solution.py:306
  108.1 2.9 %collective-permute-start.34 = (bf16[2,128,256]{2,1,0:T(8,128)(2,1)S(1)}, bf16[2,128,256]{2,1,0:T(8,128)(2,1)S(1)}, u32[]{:S(2)}, u32[]{:S(2)}) collective-permute-start(bf16[2,128,256]{2,1,0:T(8,128)(2,1)S(1)} %get-tuple-element.97), channel_id=1, source_target_pairs={{0,6},{1,7},{2,4},{3,5},{4,2},{5,3},{6,0},{7,1},{8,14},{9,15},{10,... | collective-permute-start | bytes 393224 | tf_op jit(solution)/shard_map/ppermute | solution.py:306
  111.0 2.3 %collective-permute-done.30.refs_2_ = bf16[2,128,256]{2,1,0:T(8,128)(2,1)S(1)} collective-permute-done((bf16[2,128,256]{2,1,0:T(8,128)(2,1)S(1)}, bf16[2,128,256]{2,1,0:T(8,128)(2,1)S(1)}, u32[]{:S(2)}, u32[]{:S(2)}) %collective-permute-start.30) | collective-permute-done | bytes 131104 | tf_op jit(solution)/shard_map/ppermute | solution.py:306
  113.3 0.1 collective-permute-start.35
  113.4 0.1 broadcast_in_dim.4.row
  113.5 1.4 %copy-done.7 = bf16[512,1536]{1,0:T(8,128)(2,1)S(1)} copy-done((bf16[512,1536]{1,0:T(8,128)(2,1)S(1)}, bf16[512,1536]{1,0:T(8,128)(2,1)}, u32[]{:S(2)}) %copy-start.7) | copy-done | bytes 1572888
  114.9 6.0 %shard_map.81.source = f32[2,512,512]{2,1,0:T(8,128)} custom-call(s32[2]{0:T(128)S(1)} %copy-done.5, f32[8]{0:T(128)S(1)} %copy-done.6, f32[2,512,512]{2,1,0:T(8,128)} %bitcast.14, bf16[8,2,128,256]{3,2,1,0:T(8,128)(2,1)S(1)} %all-to-all-done.1.blocks, f32[512,128]{1,0:T(8,128)S(1)} %broadcast_in_dim.4.row, f32[1,512]{1,0:T(1,128)S(1)} %bitcast.20, ...), custom_call_target="tpu_custom_call" | custom-call | flops 3221225472 | bytes 6291456 | tf_op jit(solution)/shard_map/pallas_call | solution.py:428
  121.0 0.5 collective-permute-done.35.refs_7_
  121.5 2.7 %shard_map.84 = f32[2,512,512]{2,1,0:T(8,128)} custom-call(s32[2]{0:T(128)S(1)} %copy-done.5, f32[2,512,512]{2,1,0:T(8,128)} %shard_map.81.source, bf16[2,128,256]{2,1,0:T(8,128)(2,1)S(1)} %get-tuple-element.91.refs_0_, bf16[2,128,256]{2,1,0:T(8,128)(2,1)S(1)} %collective-permute-done.29.refs_1_, ...), custom_call_target="tpu_custom_call", output_to_operand_aliasing={{}: (1, {})} | custom-call | flops 524288 | bytes 5242880 | tf_op jit(solution)/shard_map/pallas_call | solution.py:451
  (64 shorter events, 0.6 us)
Async XLA Ops:
  0.0 10.2 %copy-start.13 = (s32[8]{0:T(128)S(1)}, s32[8]{0:T(128)}, u32[]{:S(2)}) copy-start(s32[8]{0:T(128)} %constant.25.clone) | copy-start | bytes 100
  0.0 11.4 %copy-start.12 = (s32[8]{0:T(128)S(1)}, s32[8]{0:T(128)}, u32[]{:S(2)}) copy-start(s32[8]{0:T(128)} %constant.24.clone) | copy-start | bytes 100
  0.0 16.0 %copy-start.2 = (f32[512]{0:T(512)S(1)}, f32[512]{0:T(512)}, u32[]{:S(2)}) copy-start(f32[512]{0:T(512)} %param.11) | copy-start | bytes 6148
  0.0 12.7 %collective-permute-start = (bf16[3,64,512]{2,1,0:T(8,128)(2,1)}, bf16[3,64,512]{2,1,0:T(8,128)(2,1)S(1)}, u32[]{:S(2)}, u32[]{:S(2)}) collective-permute-start(bf16[3,64,512]{2,1,0:T(8,128)(2,1)} %refs_0_.1), channel_id=1, source_target_pairs={{0,2},{1,3},{2,0},{3,1},{4,6},{5,7},{6,4},{7,5},{8,10},{9,11},{10,... | collective-permute-start | bytes 589832 | tf_op jit(solution)/shard_map/ppermute | solution.py:339
  3.0 12.8 %collective-permute-start.1 = (bf16[3,64,512]{2,1,0:T(8,128)(2,1)}, bf16[3,64,512]{2,1,0:T(8,128)(2,1)S(1)}, u32[]{:S(2)}, u32[]{:S(2)}) collective-permute-start(bf16[3,64,512]{2,1,0:T(8,128)(2,1)} %refs_0_.1), channel_id=1, source_target_pairs={{0,4},{1,5},{2,6},{3,7},{4,0},{5,1},{6,2},{7,3},{8,12},{9,13},{10,... | collective-permute-start | bytes 589832 | tf_op jit(solution)/shard_map/ppermute | solution.py:339
  4.5 11.2 %collective-permute-start.2 = (bf16[3,64,512]{2,1,0:T(8,128)(2,1)}, bf16[3,64,512]{2,1,0:T(8,128)(2,1)S(1)}, u32[]{:S(2)}, u32[]{:S(2)}) collective-permute-start(bf16[3,64,512]{2,1,0:T(8,128)(2,1)} %refs_0_.1), channel_id=1, source_target_pairs={{0,6},{1,7},{2,4},{3,5},{4,2},{5,3},{6,0},{7,1},{8,14},{9,15},{10,... | collective-permute-start | bytes 589832 | tf_op jit(solution)/shard_map/ppermute | solution.py:339
  4.6 23.7 %copy-start.4 = (s32[2]{0:T(128)}, s32[2]{0:T(128)S(1)}, u32[]{:S(2)}) copy-start(s32[2]{0:T(128)S(1)} %pad_add_fusion.place.source) | copy-start | bytes 28
  4.6 1.6 %copy-start = (f32[2,1,512,512]{3,2,1,0:T(8,128)S(1)}, f32[2,1,512,512]{3,2,1,0:T(8,128)}, u32[]{:S(2)}) copy-start(f32[2,1,512,512]{3,2,1,0:T(8,128)} %param.7) | copy-start | bytes 6291460
  6.2 9.5 %copy-start.1 = (bf16[3,64,512]{2,1,0:T(8,128)(2,1)S(1)}, bf16[3,64,512]{2,1,0:T(8,128)(2,1)}, u32[]{:S(2)}) copy-start(bf16[3,64,512]{2,1,0:T(8,128)(2,1)} %refs_0_.1) | copy-start | bytes 589828
  7.1 9.2 %collective-permute-start.10 = (bf16[2,128,256]{2,1,0:T(8,128)(2,1)S(1)}, bf16[2,128,256]{2,1,0:T(8,128)(2,1)S(1)}, u32[]{:S(2)}, u32[]{:S(2)}) collective-permute-start(bf16[2,128,256]{2,1,0:T(8,128)(2,1)S(1)} %get-tuple-element.62), channel_id=1, source_target_pairs={{0,7},{1,6},{2,5},{3,4},{4,3},{5,2},{6,1},{7,0},{8,15},{9,14},{10,... | collective-permute-start | bytes 393224 | tf_op jit(solution)/shard_map/ppermute | solution.py:306
  8.7 10.1 %collective-permute-start.4 = (bf16[2,128,256]{2,1,0:T(8,128)(2,1)S(1)}, bf16[2,128,256]{2,1,0:T(8,128)(2,1)S(1)}, u32[]{:S(2)}, u32[]{:S(2)}) collective-permute-start(bf16[2,128,256]{2,1,0:T(8,128)(2,1)S(1)} %get-tuple-element.56), channel_id=1, source_target_pairs={{0,1},{1,0},{2,3},{3,2},{4,5},{5,4},{6,7},{7,6},{8,9},{9,8},{10,11... | collective-permute-start | bytes 393224 | tf_op jit(solution)/shard_map/ppermute | solution.py:306
  12.7 15.4 %collective-permute-start.5 = (bf16[2,128,256]{2,1,0:T(8,128)(2,1)S(1)}, bf16[2,128,256]{2,1,0:T(8,128)(2,1)S(1)}, u32[]{:S(2)}, u32[]{:S(2)}) collective-permute-start(bf16[2,128,256]{2,1,0:T(8,128)(2,1)S(1)} %get-tuple-element.57), channel_id=1, source_target_pairs={{0,2},{1,3},{2,0},{3,1},{4,6},{5,7},{6,4},{7,5},{8,10},{9,11},{10,... | collective-permute-start | bytes 393224 | tf_op jit(solution)/shard_map/ppermute | solution.py:306
  15.8 12.3 %collective-permute-start.6 = (bf16[2,128,256]{2,1,0:T(8,128)(2,1)S(1)}, bf16[2,128,256]{2,1,0:T(8,128)(2,1)S(1)}, u32[]{:S(2)}, u32[]{:S(2)}) collective-permute-start(bf16[2,128,256]{2,1,0:T(8,128)(2,1)S(1)} %get-tuple-element.58), channel_id=1, source_target_pairs={{0,3},{1,2},{2,1},{3,0},{4,7},{5,6},{6,5},{7,4},{8,11},{9,10},{10,... | collective-permute-start | bytes 393224 | tf_op jit(solution)/shard_map/ppermute | solution.py:306
  15.9 3.0 %collective-permute-start.3 = (bf16[4,3,64,512]{3,2,1,0:T(8,128)(2,1)S(1)}, bf16[4,3,64,512]{3,2,1,0:T(8,128)(2,1)S(1)}, u32[]{:S(2)}, u32[]{:S(2)}) collective-permute-start(bf16[4,3,64,512]{3,2,1,0:T(8,128)(2,1)S(1)} %pad_maximum_fusion), channel_id=1, source_target_pairs={{0,1},{1,0},{2,3},{3,2},{4,5},{5,4},{6,7},{7,6},{8,9},{9,8},{10,11... | collective-permute-start | bytes 2359304 | tf_op jit(solution)/shard_map/ppermute | solution.py:339
  16.3 11.7 %collective-permute-start.7 = (bf16[2,128,256]{2,1,0:T(8,128)(2,1)S(1)}, bf16[2,128,256]{2,1,0:T(8,128)(2,1)S(1)}, u32[]{:S(2)}, u32[]{:S(2)}) collective-permute-start(bf16[2,128,256]{2,1,0:T(8,128)(2,1)S(1)} %get-tuple-element.59), channel_id=1, source_target_pairs={{0,4},{1,5},{2,6},{3,7},{4,0},{5,1},{6,2},{7,3},{8,12},{9,13},{10,... | collective-permute-start | bytes 393224 | tf_op jit(solution)/shard_map/ppermute | solution.py:306
  18.8 9.6 %collective-permute-start.8 = (bf16[2,128,256]{2,1,0:T(8,128)(2,1)S(1)}, bf16[2,128,256]{2,1,0:T(8,128)(2,1)S(1)}, u32[]{:S(2)}, u32[]{:S(2)}) collective-permute-start(bf16[2,128,256]{2,1,0:T(8,128)(2,1)S(1)} %get-tuple-element.60), channel_id=1, source_target_pairs={{0,5},{1,4},{2,7},{3,6},{4,1},{5,0},{6,3},{7,2},{8,13},{9,12},{10,... | collective-permute-start | bytes 393224 | tf_op jit(solution)/shard_map/ppermute | solution.py:306
  18.9 14.6 %copy-start.11 = (bf16[8,8]{1,0:T(8,128)(2,1)S(1)}, bf16[8,8]{1,0:T(8,128)(2,1)}, u32[]{:S(2)}) copy-start(bf16[8,8]{1,0:T(8,128)(2,1)} %param.9) | copy-start | bytes 388
  18.9 9.4 %collective-permute-start.9 = (bf16[2,128,256]{2,1,0:T(8,128)(2,1)S(1)}, bf16[2,128,256]{2,1,0:T(8,128)(2,1)S(1)}, u32[]{:S(2)}, u32[]{:S(2)}) collective-permute-start(bf16[2,128,256]{2,1,0:T(8,128)(2,1)S(1)} %get-tuple-element.61), channel_id=1, source_target_pairs={{0,6},{1,7},{2,4},{3,5},{4,2},{5,3},{6,0},{7,1},{8,14},{9,15},{10,... | collective-permute-start | bytes 393224 | tf_op jit(solution)/shard_map/ppermute | solution.py:306
  29.0 12.4 %collective-permute-start.11 = (bf16[2,2,64,256]{3,2,1,0:T(8,128)(2,1)S(1)}, bf16[2,2,64,256]{3,2,1,0:T(8,128)(2,1)S(1)}, u32[]{:S(2)}, u32[]{:S(2)}) collective-permute-start(bf16[2,2,64,256]{3,2,1,0:T(8,128)(2,1)S(1)} %get-tuple-element.64), channel_id=1, source_target_pairs={{0,8},{8,0},{16,24},{24,16},{1,9},{9,1},{17,25},{25,17},{2,10},{10... | collective-permute-start | bytes 393224 | tf_op jit(solution)/shard_map/ppermute | solution.py:313
  30.6 12.9 %collective-permute-start.12 = (bf16[2,2,64,256]{3,2,1,0:T(8,128)(2,1)S(1)}, bf16[2,2,64,256]{3,2,1,0:T(8,128)(2,1)S(1)}, u32[]{:S(2)}, u32[]{:S(2)}) collective-permute-start(bf16[2,2,64,256]{3,2,1,0:T(8,128)(2,1)S(1)} %get-tuple-element.65), channel_id=1, source_target_pairs={{0,16},{8,24},{16,0},{24,8},{1,17},{9,25},{17,1},{25,9},{2,18},{10... | collective-permute-start | bytes 393224 | tf_op jit(solution)/shard_map/ppermute | solution.py:313
  33.2 10.4 %collective-permute-start.13 = (bf16[2,2,64,256]{3,2,1,0:T(8,128)(2,1)S(1)}, bf16[2,2,64,256]{3,2,1,0:T(8,128)(2,1)S(1)}, u32[]{:S(2)}, u32[]{:S(2)}) collective-permute-start(bf16[2,2,64,256]{3,2,1,0:T(8,128)(2,1)S(1)} %get-tuple-element.66), channel_id=1, source_target_pairs={{0,24},{8,16},{16,8},{24,0},{1,25},{9,17},{17,9},{25,1},{2,26},{10... | collective-permute-start | bytes 393224 | tf_op jit(solution)/shard_map/ppermute | solution.py:313
  33.6 18.9 %all-to-all-start = ((bf16[8,2,128,256]{3,2,1,0:T(8,128)(2,1)}), bf16[8,2,128,256]{3,2,1,0:T(8,128)(2,1)S(1)}, u32[]{:S(2)}, u32[]{:S(2)}) async-start(bf16[8,2,128,256]{3,2,1,0:T(8,128)(2,1)} %get-tuple-element.54), calls=%async_computation | async-start | bytes 2097152 | tf_op jit(solution)/shard_map/all_to_all | solution.py:300
  37.2 21.7 %collective-permute-start.17 = (bf16[2,2,64,256]{3,2,1,0:T(8,128)(2,1)S(1)}, bf16[2,2,64,256]{3,2,1,0:T(8,128)(2,1)S(1)}, u32[]{:S(2)}, u32[]{:S(2)}) collective-permute-start(bf16[2,2,64,256]{3,2,1,0:T(8,128)(2,1)S(1)} %get-tuple-element.74), channel_id=1, source_target_pairs={{0,8},{8,0},{16,24},{24,16},{1,9},{9,1},{17,25},{25,17},{2,10},{10... | collective-permute-start | bytes 393224 | tf_op jit(solution)/shard_map/ppermute | solution.py:313
  37.9 21.2 %collective-permute-start.18 = (bf16[2,2,64,256]{3,2,1,0:T(8,128)(2,1)S(1)}, bf16[2,2,64,256]{3,2,1,0:T(8,128)(2,1)S(1)}, u32[]{:S(2)}, u32[]{:S(2)}) collective-permute-start(bf16[2,2,64,256]{3,2,1,0:T(8,128)(2,1)S(1)} %get-tuple-element.75), channel_id=1, source_target_pairs={{0,16},{8,24},{16,0},{24,8},{1,17},{9,25},{17,1},{25,9},{2,18},{10... | collective-permute-start | bytes 393224 | tf_op jit(solution)/shard_map/ppermute | solution.py:313
  41.4 17.7 %collective-permute-start.19 = (bf16[2,2,64,256]{3,2,1,0:T(8,128)(2,1)S(1)}, bf16[2,2,64,256]{3,2,1,0:T(8,128)(2,1)S(1)}, u32[]{:S(2)}, u32[]{:S(2)}) collective-permute-start(bf16[2,2,64,256]{3,2,1,0:T(8,128)(2,1)S(1)} %get-tuple-element.76), channel_id=1, source_target_pairs={{0,24},{8,16},{16,8},{24,0},{1,25},{9,17},{17,9},{25,1},{2,26},{10... | collective-permute-start | bytes 393224 | tf_op jit(solution)/shard_map/ppermute | solution.py:313
  44.8 14.3 %copy-start.5 = (s32[2]{0:T(128)S(1)}, s32[2]{0:T(128)}, u32[]{:S(2)}) copy-start(s32[2]{0:T(128)} %copy-done.4) | copy-start | bytes 28
  52.5 0.6 copy-start.10
  54.6 10.3 %collective-permute-start.14 = (bf16[2,2,64,256]{3,2,1,0:T(8,128)(2,1)S(1)}, bf16[2,2,64,256]{3,2,1,0:T(8,128)(2,1)S(1)}, u32[]{:S(2)}, u32[]{:S(2)}) collective-permute-start(bf16[2,2,64,256]{3,2,1,0:T(8,128)(2,1)S(1)} %get-tuple-element.69.refs_1_), channel_id=1, source_target_pairs={{0,8},{8,0},{16,24},{24,16},{1,9},{9,1},{17,25},{25,17},{2,10},{10... | collective-permute-start | bytes 393224 | tf_op jit(solution)/shard_map/ppermute | solution.py:313
  56.0 12.9 %collective-permute-start.15 = (bf16[2,2,64,256]{3,2,1,0:T(8,128)(2,1)S(1)}, bf16[2,2,64,256]{3,2,1,0:T(8,128)(2,1)S(1)}, u32[]{:S(2)}, u32[]{:S(2)}) collective-permute-start(bf16[2,2,64,256]{3,2,1,0:T(8,128)(2,1)S(1)} %get-tuple-element.70.refs_2_), channel_id=1, source_target_pairs={{0,16},{8,24},{16,0},{24,8},{1,17},{9,25},{17,1},{25,9},{2,18},{10... | collective-permute-start | bytes 393224 | tf_op jit(solution)/shard_map/ppermute | solution.py:313
  58.8 10.0 %collective-permute-start.16 = (bf16[2,2,64,256]{3,2,1,0:T(8,128)(2,1)S(1)}, bf16[2,2,64,256]{3,2,1,0:T(8,128)(2,1)S(1)}, u32[]{:S(2)}, u32[]{:S(2)}) collective-permute-start(bf16[2,2,64,256]{3,2,1,0:T(8,128)(2,1)S(1)} %get-tuple-element.71.refs_3_), channel_id=1, source_target_pairs={{0,24},{8,16},{16,8},{24,0},{1,25},{9,17},{17,9},{25,1},{2,26},{10... | collective-permute-start | bytes 393224 | tf_op jit(solution)/shard_map/ppermute | solution.py:313
  59.1 9.8 %copy-start.6 = (f32[8]{0:T(128)S(1)}, f32[8]{0:T(128)}, u32[]{:S(2)}) copy-start(f32[8]{0:T(128)} %occ.9) | copy-start | bytes 100
  60.6 19.5 %collective-permute-start.20 = (bf16[2,2,64,256]{3,2,1,0:T(8,128)(2,1)S(1)}, bf16[2,2,64,256]{3,2,1,0:T(8,128)(2,1)S(1)}, u32[]{:S(2)}, u32[]{:S(2)}) collective-permute-start(bf16[2,2,64,256]{3,2,1,0:T(8,128)(2,1)S(1)} %get-tuple-element.78.refs_2_), channel_id=1, source_target_pairs={{0,8},{8,0},{16,24},{24,16},{1,9},{9,1},{17,25},{25,17},{2,10},{10... | collective-permute-start | bytes 393224 | tf_op jit(solution)/shard_map/ppermute | solution.py:313
  61.1 20.7 %collective-permute-start.21 = (bf16[2,2,64,256]{3,2,1,0:T(8,128)(2,1)S(1)}, bf16[2,2,64,256]{3,2,1,0:T(8,128)(2,1)S(1)}, u32[]{:S(2)}, u32[]{:S(2)}) collective-permute-start(bf16[2,2,64,256]{3,2,1,0:T(8,128)(2,1)S(1)} %get-tuple-element.79.refs_3_), channel_id=1, source_target_pairs={{0,16},{8,24},{16,0},{24,8},{1,17},{9,25},{17,1},{25,9},{2,18},{10... | collective-permute-start | bytes 393224 | tf_op jit(solution)/shard_map/ppermute | solution.py:313
  64.9 16.9 %collective-permute-start.22 = (bf16[2,2,64,256]{3,2,1,0:T(8,128)(2,1)S(1)}, bf16[2,2,64,256]{3,2,1,0:T(8,128)(2,1)S(1)}, u32[]{:S(2)}, u32[]{:S(2)}) collective-permute-start(bf16[2,2,64,256]{3,2,1,0:T(8,128)(2,1)S(1)} %get-tuple-element.80.refs_4_), channel_id=1, source_target_pairs={{0,24},{8,16},{16,8},{24,0},{1,25},{9,17},{17,9},{25,1},{2,26},{10... | collective-permute-start | bytes 393224 | tf_op jit(solution)/shard_map/ppermute | solution.py:313
  71.4 0.8 copy-start.8
  72.2 23.1 %collective-permute-start.26 = (bf16[2,2,64,256]{3,2,1,0:T(8,128)(2,1)S(1)}, bf16[2,2,64,256]{3,2,1,0:T(8,128)(2,1)S(1)}, u32[]{:S(2)}, u32[]{:S(2)}) collective-permute-start(bf16[2,2,64,256]{3,2,1,0:T(8,128)(2,1)S(1)} %get-tuple-element.88), channel_id=1, source_target_pairs={{0,8},{8,0},{16,24},{24,16},{1,9},{9,1},{17,25},{25,17},{2,10},{10... | collective-permute-start | bytes 393224 | tf_op jit(solution)/shard_map/ppermute | solution.py:313
  79.4 17.5 %collective-permute-start.27 = (bf16[2,2,64,256]{3,2,1,0:T(8,128)(2,1)S(1)}, bf16[2,2,64,256]{3,2,1,0:T(8,128)(2,1)S(1)}, u32[]{:S(2)}, u32[]{:S(2)}) collective-permute-start(bf16[2,2,64,256]{3,2,1,0:T(8,128)(2,1)S(1)} %get-tuple-element.89), channel_id=1, source_target_pairs={{0,16},{8,24},{16,0},{24,8},{1,17},{9,25},{17,1},{25,9},{2,18},{10... | collective-permute-start | bytes 393224 | tf_op jit(solution)/shard_map/ppermute | solution.py:313
  80.1 16.7 %collective-permute-start.28 = (bf16[2,2,64,256]{3,2,1,0:T(8,128)(2,1)S(1)}, bf16[2,2,64,256]{3,2,1,0:T(8,128)(2,1)S(1)}, u32[]{:S(2)}, u32[]{:S(2)}) collective-permute-start(bf16[2,2,64,256]{3,2,1,0:T(8,128)(2,1)S(1)} %get-tuple-element.90), channel_id=1, source_target_pairs={{0,24},{8,16},{16,8},{24,0},{1,25},{9,17},{17,9},{25,1},{2,26},{10... | collective-permute-start | bytes 393224 | tf_op jit(solution)/shard_map/ppermute | solution.py:313
  85.3 13.6 %collective-permute-start.23 = (bf16[2,2,64,256]{3,2,1,0:T(8,128)(2,1)S(1)}, bf16[2,2,64,256]{3,2,1,0:T(8,128)(2,1)S(1)}, u32[]{:S(2)}, u32[]{:S(2)}) collective-permute-start(bf16[2,2,64,256]{3,2,1,0:T(8,128)(2,1)S(1)} %get-tuple-element.84), channel_id=1, source_target_pairs={{0,8},{8,0},{16,24},{24,16},{1,9},{9,1},{17,25},{25,17},{2,10},{10... | collective-permute-start | bytes 393224 | tf_op jit(solution)/shard_map/ppermute | solution.py:313
  88.1 10.9 %collective-permute-start.24 = (bf16[2,2,64,256]{3,2,1,0:T(8,128)(2,1)S(1)}, bf16[2,2,64,256]{3,2,1,0:T(8,128)(2,1)S(1)}, u32[]{:S(2)}, u32[]{:S(2)}) collective-permute-start(bf16[2,2,64,256]{3,2,1,0:T(8,128)(2,1)S(1)} %get-tuple-element.85), channel_id=1, source_target_pairs={{0,16},{8,24},{16,0},{24,8},{1,17},{9,25},{17,1},{25,9},{2,18},{10... | collective-permute-start | bytes 393224 | tf_op jit(solution)/shard_map/ppermute | solution.py:313
  88.8 24.6 %all-to-all-start.1 = ((bf16[8,2,128,256]{3,2,1,0:T(8,128)(2,1)}), bf16[8,2,128,256]{3,2,1,0:T(8,128)(2,1)S(1)}, u32[]{:S(2)}, u32[]{:S(2)}) async-start(bf16[8,2,128,256]{3,2,1,0:T(8,128)(2,1)} %get-tuple-element.81), calls=%async_computation.1 | async-start | bytes 2097152 | tf_op jit(solution)/shard_map/all_to_all | solution.py:300
  95.3 7.8 %collective-permute-start.25 = (bf16[2,2,64,256]{3,2,1,0:T(8,128)(2,1)S(1)}, bf16[2,2,64,256]{3,2,1,0:T(8,128)(2,1)S(1)}, u32[]{:S(2)}, u32[]{:S(2)}) collective-permute-start(bf16[2,2,64,256]{3,2,1,0:T(8,128)(2,1)S(1)} %get-tuple-element.86), channel_id=1, source_target_pairs={{0,24},{8,16},{16,8},{24,0},{1,25},{9,17},{17,9},{25,1},{2,26},{10... | collective-permute-start | bytes 393224 | tf_op jit(solution)/shard_map/ppermute | solution.py:313
  96.8 1.0 copy-start.9
  103.1 10.3 %copy-start.3 = (f32[512]{0:T(512)S(1)}, f32[512]{0:T(512)}, u32[]{:S(2)}) copy-start(f32[512]{0:T(512)} %param.11) | copy-start | bytes 6148
  104.3 3.8 %collective-permute-start.29 = (bf16[2,128,256]{2,1,0:T(8,128)(2,1)S(1)}, bf16[2,128,256]{2,1,0:T(8,128)(2,1)S(1)}, u32[]{:S(2)}, u32[]{:S(2)}) collective-permute-start(bf16[2,128,256]{2,1,0:T(8,128)(2,1)S(1)} %get-tuple-element.92), channel_id=1, source_target_pairs={{0,1},{1,0},{2,3},{3,2},{4,5},{5,4},{6,7},{7,6},{8,9},{9,8},{10,11... | collective-permute-start | bytes 393224 | tf_op jit(solution)/shard_map/ppermute | solution.py:306
  104.4 8.9 %collective-permute-start.30 = (bf16[2,128,256]{2,1,0:T(8,128)(2,1)S(1)}, bf16[2,128,256]{2,1,0:T(8,128)(2,1)S(1)}, u32[]{:S(2)}, u32[]{:S(2)}) collective-permute-start(bf16[2,128,256]{2,1,0:T(8,128)(2,1)S(1)} %get-tuple-element.93), channel_id=1, source_target_pairs={{0,2},{1,3},{2,0},{3,1},{4,6},{5,7},{6,4},{7,5},{8,10},{9,11},{10,... | collective-permute-start | bytes 393224 | tf_op jit(solution)/shard_map/ppermute | solution.py:306
  106.1 14.8 %collective-permute-start.31 = (bf16[2,128,256]{2,1,0:T(8,128)(2,1)S(1)}, bf16[2,128,256]{2,1,0:T(8,128)(2,1)S(1)}, u32[]{:S(2)}, u32[]{:S(2)}) collective-permute-start(bf16[2,128,256]{2,1,0:T(8,128)(2,1)S(1)} %get-tuple-element.94), channel_id=1, source_target_pairs={{0,3},{1,2},{2,1},{3,0},{4,7},{5,6},{6,5},{7,4},{8,11},{9,10},{10,... | collective-permute-start | bytes 393224 | tf_op jit(solution)/shard_map/ppermute | solution.py:306
  106.3 14.7 %collective-permute-start.32 = (bf16[2,128,256]{2,1,0:T(8,128)(2,1)S(1)}, bf16[2,128,256]{2,1,0:T(8,128)(2,1)S(1)}, u32[]{:S(2)}, u32[]{:S(2)}) collective-permute-start(bf16[2,128,256]{2,1,0:T(8,128)(2,1)S(1)} %get-tuple-element.95), channel_id=1, source_target_pairs={{0,4},{1,5},{2,6},{3,7},{4,0},{5,1},{6,2},{7,3},{8,12},{9,13},{10,... | collective-permute-start | bytes 393224 | tf_op jit(solution)/shard_map/ppermute | solution.py:306
  108.1 12.9 %collective-permute-start.33 = (bf16[2,128,256]{2,1,0:T(8,128)(2,1)S(1)}, bf16[2,128,256]{2,1,0:T(8,128)(2,1)S(1)}, u32[]{:S(2)}, u32[]{:S(2)}) collective-permute-start(bf16[2,128,256]{2,1,0:T(8,128)(2,1)S(1)} %get-tuple-element.96), channel_id=1, source_target_pairs={{0,5},{1,4},{2,7},{3,6},{4,1},{5,0},{6,3},{7,2},{8,13},{9,12},{10,... | collective-permute-start | bytes 393224 | tf_op jit(solution)/shard_map/ppermute | solution.py:306
  108.1 12.9 %collective-permute-start.34 = (bf16[2,128,256]{2,1,0:T(8,128)(2,1)S(1)}, bf16[2,128,256]{2,1,0:T(8,128)(2,1)S(1)}, u32[]{:S(2)}, u32[]{:S(2)}) collective-permute-start(bf16[2,128,256]{2,1,0:T(8,128)(2,1)S(1)} %get-tuple-element.97), channel_id=1, source_target_pairs={{0,6},{1,7},{2,4},{3,5},{4,2},{5,3},{6,0},{7,1},{8,14},{9,15},{10,... | collective-permute-start | bytes 393224 | tf_op jit(solution)/shard_map/ppermute | solution.py:306
  113.3 8.2 %collective-permute-start.35 = (bf16[2,128,256]{2,1,0:T(8,128)(2,1)S(1)}, bf16[2,128,256]{2,1,0:T(8,128)(2,1)S(1)}, u32[]{:S(2)}, u32[]{:S(2)}) collective-permute-start(bf16[2,128,256]{2,1,0:T(8,128)(2,1)S(1)} %get-tuple-element.98), channel_id=1, source_target_pairs={{0,7},{1,6},{2,5},{3,4},{4,3},{5,2},{6,1},{7,0},{8,15},{9,14},{10,... | collective-permute-start | bytes 393224 | tf_op jit(solution)/shard_map/ppermute | solution.py:306
  113.5 1.4 %copy-start.7 = (bf16[512,1536]{1,0:T(8,128)(2,1)S(1)}, bf16[512,1536]{1,0:T(8,128)(2,1)}, u32[]{:S(2)}) copy-start(bf16[512,1536]{1,0:T(8,128)(2,1)} %get-tuple-element.82.whole) | copy-start | bytes 4718596
